TPU v7x, 32 devices: a whole 2x2x4 slice. The times are simulated.
32 devices in a mesh: grp: 2 (over x), ex: 16 (over z, y, core).
Axes of the slice: x: 2, y: 2, z: 4, core: 2. Of those that a mesh axis runs over, the one named last changes fastest.
Arguments:
- features: bfloat16 [20480, 8192], P(('grp', 'ex')), parts along dimension 0, may hold values from -6 to 6
- labels: int32 [20480], P(('grp', 'ex')), parts along dimension 0, may hold values from 0 to 31
- pick_index: int32 [6, 32], P('grp'), parts along dimension 0, may hold values from 0 to 10239, as said below
Outputs:
- scores: float32 [3, 20480], P(None, ('grp', 'ex')), parts along dimension 1
- residual: float32 [64, 8192], P('grp'), parts along dimension 0
There are 2 independent parts, one for each index of `grp`. A program takes and returns all parts, laid end to end along the dimension named above; each array names one. Nothing has to cross between parts.
Inputs may be any that keep to these rules, and one draw needn't show every extreme that they name: pick_index[s, c] is an example of class c; the picks of one class differ from step to step; at each step at most 2 picks lie among the 640 examples of one device, and some device holds exactly 2.
All inputs are finite; a program needn't handle non-finite values.
Results may differ from a plain program's by a relative error of at most 0.00105.
Values may be sent and summed in bfloat16 or wider, within the bound.
No kernel may reach another device: no remote copies, remote signals or barrier semaphores. Data moves between devices by JAX's collectives and lax.ppermute only.
A program may use at most 64 MiB of HBM per device.

v0:
```python
import math

import jax
import jax.numpy as jnp
from jax import lax
from jax.sharding import PartitionSpec as P

ridge = 1.0


def solve_small(gram_matrix, right_side):
    factor = jnp.linalg.cholesky(gram_matrix)
    order_size = right_side.shape[1]
    forward = []
    for i in range(order_size):
        partial_value = right_side[:, i]
        for j in range(i):
            partial_value = partial_value - factor[:, i, j] * forward[j]
        forward.append(partial_value / factor[:, i, i])
    backward = [None] * order_size
    for i in reversed(range(order_size)):
        partial_value = forward[i]
        for j in range(i + 1, order_size):
            partial_value = partial_value - factor[:, j, i] * backward[j]
        backward[i] = partial_value / factor[:, i, i]
    return jnp.stack(backward, axis=1)


def project(picked, target, target_low):
    order_size = picked.shape[1]
    gram_matrix = jnp.einsum("ckf,cjf->ckj", picked, picked, preferred_element_type=jnp.float32)
    gram_matrix = gram_matrix + ridge * jnp.eye(order_size, dtype=jnp.float32)[None]
    right_side = jnp.einsum("ckf,cf->ck", picked, target_low, preferred_element_type=jnp.float32)
    weights = solve_small(gram_matrix, right_side)
    result = target
    for k in range(order_size):
        result = result - weights[:, k : k + 1] * picked[:, k, :]
    return result


def correlate(left, features):
    return lax.dot_general(
        left, features, (((1,), (1,)), ((), ())), preferred_element_type=jnp.float32
    )


def fetch_rows(features, picks, device):
    shard_rows = features.shape[0]
    owners = picks // shard_rows
    local_row = picks % shard_rows
    mine = owners == device
    masked = jnp.where(
        mine[:, :, None], features[jnp.where(mine, local_row, 0)].astype(jnp.float32), 0.0
    )
    return lax.psum(masked, "ex").astype(jnp.bfloat16)


def on_device(features, labels, pick_index):
    width_all = features.shape[1]
    class_num = pick_index.shape[1]
    device = lax.axis_index("ex")
    classes = jnp.arange(class_num, dtype=jnp.int32)
    member = (classes[:, None] == labels[None, :]).astype(jnp.bfloat16)
    class_part = jnp.dot(member, features, preferred_element_type=jnp.float32)
    count_part = jnp.sum(member.astype(jnp.float32), axis=1)
    class_total, class_count = lax.psum((class_part, count_part), "ex")
    target = class_total / jnp.sqrt(class_count)[:, None]
    product = correlate(target.astype(jnp.bfloat16), features)
    target_low = target.astype(jnp.bfloat16)
    member_float = member.astype(jnp.float32)
    scale = 1.0 / math.sqrt(width_all)
    current = target
    chosen = []
    score_list = []
    for section in range(pick_index.shape[0]):
        if section > 0:
            product = correlate(current.astype(jnp.bfloat16), features)
        score_list.append(jnp.sum(product * member_float, axis=0) * scale)
        rows_now = fetch_rows(features, pick_index[section : section + 1], device)[0]
        chosen.append(rows_now)
        current = project(jnp.stack(chosen, axis=1), target, target_low)
    return (jnp.stack(score_list), current)


def solution(mesh):
    return jax.shard_map(
        on_device,
        mesh=mesh,
        in_specs=(P(("grp", "ex"), None), P(("grp", "ex")), P("grp", None)),
        out_specs=(P(None, ("grp", "ex")), P("grp", None)),
        check_vma=False,
    )
```

profile of v0, /device:TPU:0, one launch (start us, length us, event | category | flops | bytes accessed | tf_op | source)
XLA Modules:
  0.0 185.2 jit_solution(14100410378717145246)
XLA Ops:
  7.2 6.8 %fusion.32 = f32[32,8192]{1,0:T(8,128)} fusion(bf16[640,8192]{1,0:T(8,128)(2,1)} %param.3, s32[640]{0:T(1024)} %param.4), kind=kOutput, calls=%fused_computation.53 | convolution fusion | flops 335564800 | bytes 11536896 | tf_op jit(solution)/shard_map/dot_general | solution.py:64
  14.1 0.1 convert_reduce_fusion
  14.3 6.7 %gather_fusion.1 = bf16[32,8192]{1,0:T(8,128)(2,1)S(1)} fusion(bf16[640,8192]{1,0:T(8,128)(2,1)} %param.3, s32[1024]{0:T(1024)S(1)} %pad_clamp_fusion.1), kind=kCustom, calls=%fused_computation.1 | custom fusion | bytes 1048704 | tf_op jit(solution)/shard_map/gather | solution.py:53
  21.0 6.8 %gather_fusion = bf16[32,8192]{1,0:T(8,128)(2,1)S(1)} fusion(bf16[640,8192]{1,0:T(8,128)(2,1)} %param.3, s32[1024]{0:T(1024)S(1)} %pad_clamp_fusion.2), kind=kCustom, calls=%fused_computation | custom fusion | bytes 1048704 | tf_op jit(solution)/shard_map/gather | solution.py:53
  27.9 7.5 %gather_fusion.2 = bf16[32,8192]{1,0:T(8,128)(2,1)} fusion(bf16[640,8192]{1,0:T(8,128)(2,1)} %param.3, s32[1024]{0:T(1024)S(1)} %pad_clamp_fusion), kind=kCustom, calls=%fused_computation.2 | custom fusion | bytes 1048704 | tf_op jit(solution)/shard_map/gather | solution.py:53
  35.4 0.1 convert_select_fusion.2
  35.5 2.2 %convert_select_fusion = (f32[1,32,8192]{2,1,0:T(8,128)S(1)}, f32[1,32,8192]{2,1,0:T(8,128)}) fusion(bf16[32,8192]{1,0:T(8,128)(2,1)} %gather_fusion.2, pred[32]{0:T(512)(128)(4,1)S(1)} %get-tuple-element.24, bf16[32,8192]{1,0:T(8,128)(2,1)S(1)} %gather_fusion.1, pred[32]{0:T(512)(128)(4,1)S(1)} %get-tuple-element.34), kind=kLoop, calls=%fused_computation.33 | loop fusion | flops 1048576 | bytes 3145792 | tf_op jit(solution)/shard_map/jit(_where)/select_n | solution.py:52
  37.7 85.7 %all-reduce.5 = (bf16[1,32,8192]{2,1,0:T(8,128)(2,1)S(1)}, bf16[1,32,8192]{2,1,0:T(8,128)(2,1)S(1)}, f32[32]{0:T(128)S(1)}, bf16[1,32,8192]{2,1,0:T(8,128)(2,1)}) all-reduce(f32[1,32,8192]{2,1,0:T(8,128)S(1)} %convert_select_fusion.2, f32[1,32,8192]{2,1,0:T(8,128)} %get-tuple-element.39, ...), channel_id=1, replica_groups=mesh['grp'=2,'ex'=16] {'ex'}, use_global_device_ids=true, to_apply=%region_4.5 | all-reduce | flops 786464 | bytes 4718848 | tf_op jit(solution)/shard_map/psum | solution.py:55
  123.4 0.1 pad_maximum_fusion.1
  123.6 1.0 copy-done.4
  124.5 2.8 %fusion.21 = f32[32,2,2]{2,1,0:T(2,128)S(1)} fusion(bf16[32,2,8192]{2,0,1:T(8,128)(2,1)S(1)} %pad_maximum_fusion.1), kind=kOutput, calls=%fused_computation.40 | convolution fusion | flops 2097152 | bytes 1049088 | tf_op jit(solution)/shard_map/ckf,cjf->ckj/dot_general | solution.py:31
  127.3 0.3 copy.33
  127.7 6.2 %custom-call.8 = f32[32,2,2]{2,1,0:T(2,128)S(1)} custom-call(f32[32,2,2]{2,1,0:T(2,128)S(1)} %fusion.37), custom_call_target="Cholesky" | custom-call | tf_op jit(solution)/shard_map/jit(cholesky)/cholesky | solution.py:12
  134.0 0.1 copy.34
  134.1 0.2 pad_maximum_fusion
  134.3 1.1 copy-done.2
  135.4 3.1 %fusion.2 = f32[32,3,3]{2,1,0:T(4,128)S(1)} fusion(bf16[32,3,8192]{2,0,1:T(8,128)(2,1)S(1)} %pad_maximum_fusion), kind=kOutput, calls=%fused_computation.10 | convolution fusion | flops 4718592 | bytes 1574016 | tf_op jit(solution)/shard_map/ckf,cjf->ckj/dot_general | solution.py:31
  138.5 0.3 copy.38
  138.8 9.3 %custom-call.9 = f32[32,3,3]{2,1,0:T(4,128)S(1)} custom-call(f32[32,3,3]{2,1,0:T(4,128)S(1)} %fusion.34), custom_call_target="Cholesky" | custom-call | tf_op jit(solution)/shard_map/jit(cholesky)/cholesky | solution.py:12
  148.2 0.1 copy.39
  148.3 0.1 select_select_fusion.1
  148.5 0.6 slice_reduce_fusion.5
  149.1 0.1 select_select_fusion
  149.2 0.6 slice_reduce_fusion.1
  149.8 1.5 convert_bitcast_fusion.2
  151.3 3.8 %fusion.18 = f32[32,1,2]{2,1,0:T(1,128)S(1)} fusion(bf16[32,8192,1]{1,0,2:T(8,128)(2,1)S(1)} %convert_bitcast_fusion.2, bf16[32,2,8192]{2,0,1:T(8,128)(2,1)} %copy-done.4), kind=kOutput, calls=%fused_computation.37 | convolution fusion | flops 1048576 | bytes 1573120 | tf_op jit(solution)/shard_map/ckf,cf->ck/dot_general | solution.py:33
  155.1 2.9 %fusion = f32[32,1,3]{2,1,0:T(1,128)S(1)} fusion(bf16[32,3,8192]{2,0,1:T(8,128)(2,1)S(1)} %copy-done.3, bf16[32,8192,1]{1,0,2:T(8,128)(2,1)S(1)} %convert_bitcast_fusion.2), kind=kOutput, calls=%fused_computation.8 | convolution fusion | flops 1572864 | bytes 2097536 | tf_op jit(solution)/shard_map/ckf,cf->ck/dot_general | solution.py:33
  158.1 3.3 %fusion.4 = f32[640]{0:T(1024)S(1)} fusion(bf16[640,8192]{1,0:T(8,128)(2,1)S(1)} %bitcast.155, s32[640]{0:T(1024)S(1)} %copy-done.5, f32[32,8192]{1,0:T(8,128)S(1)} %copy-done, f32[32]{0:T(128)S(1)} %sqrt.7), kind=kOutput, calls=%fused_computation.18 | convolution fusion | flops 336170368 | bytes 11539584 | tf_op jit(solution)/shard_map/dot_general | solution.py:42
  161.5 7.2 %fusion.6 = f32[640]{0:T(1024)S(1)} fusion(bf16[640,8192]{1,0:T(8,128)(2,1)} %param.3, bf16[1,32,8192]{2,1,0:T(8,128)(2,1)S(1)} %get-tuple-element.13, f32[32]{0:T(128)S(1)} %bitcast.164, f32[32]{0:T(128)S(1)} %get-tuple-element.22, s32[640]{0:T(1024)S(1)} %copy-done.5, bf16[1,32,8192]{2,1,0:T(8,128)(2,1)S(1)} %get-tuple-element.14, ...), kind=kOutput, calls=%fused_computation.20 | convolution fusion | flops 337743232 | bytes 12588416 | tf_op jit(solution)/shard_map/dot_general | solution.py:42
  168.9 1.6 fusion.12
  170.5 7.2 %fusion.5 = f32[640]{0:T(1024)S(1)} fusion(bf16[640,8192]{1,0:T(8,128)(2,1)} %param.3, bf16[1,32,8192]{2,1,0:T(8,128)(2,1)S(1)} %get-tuple-element.13, f32[32]{0:T(128)S(1)} %fusion.43, s32[640]{0:T(1024)S(1)} %copy-done.5, f32[32,8192]{1,0:T(8,128)S(1)} %copy-done, f32[32]{0:T(128)S(1)} %sqrt.7), kind=kOutput, calls=%fused_computation.19 | convolution fusion | flops 336956800 | bytes 12064000 | tf_op jit(solution)/shard_map/dot_general | solution.py:42
  177.7 0.6 pad_maximum_fusion.2
  (52 shorter events, 0.7 us)
Async XLA Ops:
  7.2 6.9 %copy-start.5 = (s32[640]{0:T(1024)S(1)}, s32[640]{0:T(1024)}, u32[]{:S(2)}) copy-start(s32[640]{0:T(1024)} %param.4) | copy-start | bytes 7684
  7.2 7.1 %copy-start.6 = (s32[3,32]{1,0:T(4,128)S(1)}, s32[3,32]{1,0:T(4,128)}, u32[]{:S(2)}) copy-start(s32[3,32]{1,0:T(4,128)} %param.5) | copy-start | bytes 1156
  7.2 142.6 %all-reduce.4.cloned.1.call-start = ((), (), s32[]{:S(2)}) async-start(), calls=%async_computation | async-start | bytes 2097152 | tf_op jit(solution)/shard_map/psum | solution.py:66
  123.4 10.7 %copy-start.1 = (bf16[1,32,8192]{2,1,0:T(8,128)(2,1)S(1)}, bf16[1,32,8192]{2,1,0:T(8,128)(2,1)}, u32[]{:S(2)}) copy-start(bf16[1,32,8192]{2,1,0:T(8,128)(2,1)} %get-tuple-element.16) | copy-start | bytes 1572868
  123.5 1.0 copy-start.4
  134.3 1.2 copy-start.2
  149.8 5.3 %copy-start.3 = (bf16[32,3,8192]{2,0,1:T(8,128)(2,1)S(1)}, bf16[32,3,8192]{2,0,1:T(8,128)(2,1)}, u32[]{:S(2)}) copy-start(bf16[32,3,8192]{2,0,1:T(8,128)(2,1)} %copy-done.2) | copy-start | bytes 4718596
  151.3 6.8 %slice-start = ((s8[10485760]{0:T(1024)(128)(4,1)}), s8[4194304]{0:T(1024)(128)(4,1)S(1)}, s32[]{:S(2)}) async-start(s8[10485760]{0:T(1024)(128)(4,1)} %bitcast.154), calls=%async_computation.1 | async-start | bytes 8388608
  151.3 6.7 %slice-start.1 = ((s8[10485760]{0:T(1024)(128)(4,1)}), s8[4194304]{0:T(1024)(128)(4,1)S(1)}, s32[]{:S(2)}) async-start(s8[10485760]{0:T(1024)(128)(4,1)} %bitcast.154), calls=%async_computation.2 | async-start | bytes 8388608
  151.3 6.7 %copy-start = (f32[32,8192]{1,0:T(8,128)S(1)}, f32[32,8192]{1,0:T(8,128)}, u32[]{:S(2)}) copy-start(f32[32,8192]{1,0:T(8,128)} %all-reduce.4.cloned.1.call-done) | copy-start | bytes 3145732
  155.1 2.9 %slice-start.2 = ((s8[10485760]{0:T(1024)(128)(4,1)}), s8[2097152]{0:T(1024)(128)(4,1)S(1)}, s32[]{:S(2)}) async-start(s8[10485760]{0:T(1024)(128)(4,1)} %bitcast.154), calls=%async_computation.3 | async-start | bytes 4194304
Sparse Core Ops, SparseCore 0:
  14.2 100.8 all-reduce.3
where the time goes:
time: 187 us; the launch traced here: 185 us
  blocking collectives  85.7 us (46%)
  matrix products  37.1 us (20%)
  local copies, waits for them, and re-layouts  24.1 us (13%)
  other arithmetic  23.8 us (13%)
  between operations  14.4 us (8%)
    psum x1, blocking collectives, fetch_rows(): return lax.psum(masked, 'ex').astype(jnp.bfloat16)  85.7 us
    gather x3, local copies, waits for them, and re-layouts, fetch_rows(): features[jnp.where(mine, local_row, 0)].astype(jnp.float32)  21 us
    dot_general x3, matrix products, correlate(): lax.dot_general(left, features, (((1,), (1,)), ((), ())), preferred_eleme...  17.7 us
    another operation x8, other arithmetic, solve_small(): factor = jnp.linalg.cholesky(gram_matrix)  15.8 us
    dot_general x1, matrix products, on_device(): class_part = jnp.dot(member, features, preferred_element_type=jnp.float32)  6.79 us
    dot_general x2, matrix products, project(): jnp.einsum('ckf,cf->ck', picked, target_low, preferred_element_type=jnp.f...  6.71 us
    dot_general x2, matrix products, project(): jnp.einsum('ckf,cjf->ckj', picked, picked, preferred_element_type=jnp.flo...  5.85 us
  transfers between devices with their start and end apart: 1, of which 0 were waited for; matrix products, arithmetic and copies ran while one was open for 26% of the time, Pallas kernels for 0%

commit v1 on v0

v1 whole, which is shorter than its diff:
```python
import functools
import math

import jax
import jax.numpy as jnp
from jax import lax
from jax.experimental import pallas as pl
from jax.experimental.pallas import tpu as pltpu
from jax.sharding import PartitionSpec as P

ridge = 1.0
slots = 2
f32 = jnp.float32
bf16 = jnp.bfloat16


def nt_dot(a, b):
    return lax.dot_general(a, b, (((1,), (1,)), ((), ())), preferred_element_type=f32)


def sums_kernel(place, labels_ref, pick_ref, feat_ref, send_ref, keep_ref, rows_ref, left, held, *, classes, steps):
    i = pl.program_id(0)
    half = pl.num_programs(0) // 2
    block = place[1 + i]
    width = feat_ref.shape[1]
    used = steps * slots

    @pl.when(i == 0)
    def _():
        lab = labels_ref[...]
        n = lab.shape[1]
        member = lax.broadcasted_iota(jnp.int32, (classes, n), 0) == lab
        spot = lax.broadcasted_iota(jnp.int32, (8, n), 1) == pick_ref[...]
        left[...] = jnp.concatenate(
            [jnp.where(member, 1.0, 0.0), jnp.where(spot, 1.0, 0.0), jnp.zeros((8, n), f32)], axis=0
        ).astype(bf16)

    both = jnp.dot(left[...], feat_ref[...], preferred_element_type=f32)

    @pl.when(i < half)
    def _():
        send_ref[0] = both[:classes]

    @pl.when(i >= half)
    def _():
        keep_ref[0] = both[:classes]

    held[:, pl.ds(pl.multiple_of(block * width, width), width)] = both[classes : classes + 8]

    @pl.when(i == pl.num_programs(0) - 1)
    def _():
        full = held.shape[1]
        main = full * used // 8
        tail = full - main
        per = main // tail
        lines = [held[0:used, :main]]
        for q in range(used // per):
            lines.append(jnp.concatenate([held[q * per + u : q * per + u + 1, main:] for u in range(per)], axis=1))
        count = jnp.sum(left[0:classes, :].astype(f32), axis=1, keepdims=True)
        high = jnp.floor(count * (1.0 / 128.0))
        low = count - 128.0 * high
        lane = lax.broadcasted_iota(jnp.int32, (8, 128), 1)
        extra = jnp.zeros((8, 128), f32)
        for q in range(classes // 8):
            extra = jnp.where(lane == 2 * q, high[8 * q : 8 * q + 8], extra)
            extra = jnp.where(lane == 2 * q + 1, low[8 * q : 8 * q + 8], extra)
        rows_ref[...] = jnp.concatenate([jnp.concatenate(lines, axis=0), extra], axis=1).astype(bf16)


def picked_kernel(index_ref, rows_ref, feat_ref, x_ref, cross_ref, gram_ref, *, steps):
    i = pl.program_id(0)
    width = feat_ref.shape[1]
    full = width * pl.num_programs(0)
    used = steps * slots
    main = full * used // 8
    per = main // (full - main)
    tail = full - main
    total = x_ref.shape[0]
    lines = rows_ref.shape[0]

    @pl.when(i == 0)
    def _():
        index = index_ref[...]
        line = lax.broadcasted_iota(jnp.int32, (total, lines), 1)
        one = jnp.where(line == index, 1.0, 0.0).astype(bf16)
        x_ref[:, :main] = jnp.dot(one, rows_ref[:, :main], preferred_element_type=f32).astype(bf16)
        slot = index % 8
        rest = jnp.zeros((total, tail), f32)
        home = index - slot + used + slot // per
        for u in range(per):
            here = jnp.where((line == home) & (slot % per == u), 1.0, 0.0).astype(bf16)
            rest = rest + jnp.dot(here, rows_ref[:, u * tail : (u + 1) * tail], preferred_element_type=f32)
        x_ref[:, main:] = rest.astype(bf16)
        cross_ref[...] = jnp.zeros_like(cross_ref)
        gram_ref[...] = jnp.zeros_like(gram_ref)

    x = x_ref[:, pl.ds(pl.multiple_of(i * width, width), width)]
    cross_ref[...] += nt_dot(x, feat_ref[...])
    gram_ref[...] += nt_dot(x, x)


def diagonal(block):
    n = block.shape[0]
    eye = lax.broadcasted_iota(jnp.int32, (n, n), 0) == lax.broadcasted_iota(jnp.int32, (n, n), 1)
    return jnp.sum(jnp.where(eye, block, 0.0), axis=1, keepdims=True)


def solve_all(gram, right):
    order = len(right)
    factor = [[None] * order for _ in range(order)]
    for j in range(order):
        value = gram[j][j]
        for k in range(j):
            value = value - factor[j][k] * factor[j][k]
        factor[j][j] = jnp.sqrt(value)
        for i in range(j + 1, order):
            value = gram[i][j]
            for k in range(j):
                value = value - factor[i][k] * factor[j][k]
            factor[i][j] = value / factor[j][j]
    forward = []
    for i in range(order):
        value = right[i]
        for j in range(i):
            value = value - factor[i][j] * forward[j]
        forward.append(value / factor[i][i])
    result = []
    for size in range(1, order + 1):
        back = [None] * size
        for i in reversed(range(size)):
            value = forward[i]
            for j in range(i + 1, size):
                value = value - factor[j][i] * back[j]
            back[i] = value / factor[i][i]
        result.append(back)
    return result


def final_kernel(
    place, labels_ref, extra_ref, x_ref, cross_ref, gram_ref, own_ref, twin_ref, feat_a, feat_b,
    scores_ref, resid_ref, inv, direct, right, *, steps, scale
):
    i = pl.program_id(0)
    width = feat_a.shape[1]
    classes = direct.shape[0]

    @pl.when(i == 0)
    def _():
        summed = jnp.sum(extra_ref[...].astype(f32), axis=0)
        parts = []
        for q in range(classes // 8):
            parts.append(128.0 * summed[:, 2 * q : 2 * q + 1] + summed[:, 2 * q + 1 : 2 * q + 2])
        inv[...] = jnp.broadcast_to(jnp.sqrt(jnp.concatenate(parts, axis=0)), inv.shape)
        direct[...] = jnp.zeros_like(direct)
        right[...] = jnp.zeros_like(right)

    for block, got, feat in ((place[1 + 2 * i], own_ref, feat_a), (place[2 + 2 * i], twin_ref, feat_b)):
        at = pl.ds(pl.multiple_of(block * width, width), width)
        target = got[0] / inv[:, 0:1]
        resid_ref[:, at] = target
        low = target.astype(bf16)
        direct[...] += nt_dot(low, feat[...])
        right[...] += nt_dot(low, x_ref[:, at])

    @pl.when(i == pl.num_programs(0) - 1)
    def _():
        gram = [
            [
                diagonal(gram_ref[a * classes : (a + 1) * classes, b * classes : (b + 1) * classes])
                + (ridge if a == b else 0.0)
                for b in range(steps)
            ]
            for a in range(steps)
        ]
        rhs = [diagonal(right[:, a * classes : (a + 1) * classes]) for a in range(steps)]
        weights = solve_all(gram, rhs)
        member = lax.broadcasted_iota(jnp.int32, direct.shape, 0) == labels_ref[...]
        for s in range(steps):
            value = direct[...]
            for k in range(s):
                value = value - weights[s - 1][k] * cross_ref[k * classes : (k + 1) * classes]
            scores_ref[s : s + 1, :] = jnp.sum(jnp.where(member, value, 0.0), axis=0, keepdims=True) * scale
        last = weights[steps - 1]
        value = resid_ref[...]
        for k in range(steps):
            value = value - last[k] * x_ref[k * classes : (k + 1) * classes].astype(f32)
        resid_ref[...] = value


def whole(shape):
    return pl.BlockSpec(shape, lambda i, *_: (0,) * len(shape))


def on_device(features, labels, pick_index, *, n_ex):
    rows, full = features.shape
    steps, classes = pick_index.shape
    groups = n_ex // 2
    width = full // n_ex
    device = lax.axis_index("ex")
    core = device % 2
    group = device // 2
    limit = pltpu.CompilerParams(vmem_limit_bytes=48 << 20)

    owner = pick_index // rows
    earlier = jnp.arange(classes)[:, None] > jnp.arange(classes)[None, :]
    rank = jnp.sum((owner[:, :, None] == owner[:, None, :]) & earlier[None], axis=2, dtype=jnp.int32)
    step_id = jnp.arange(steps, dtype=jnp.int32)[:, None]
    index = (owner * 8 + step_id * slots + rank).reshape(steps * classes, 1)
    mine = index - device * 8 == jnp.arange(8, dtype=jnp.int32)[None, :]
    local = (pick_index - device * rows).reshape(steps * classes, 1)
    spot = (jnp.sum(jnp.where(mine, local + 1, 0), axis=0, dtype=jnp.int32) - 1).reshape(8, 1)

    labels_row = labels.reshape(1, rows)
    ids = jnp.arange(groups, dtype=jnp.int32)
    order = jnp.concatenate([ids + (1 - core) * groups, ids + core * groups])
    place = jnp.concatenate([jnp.zeros((1,), jnp.int32), order])

    send, keep, packed = pl.pallas_call(
        functools.partial(sums_kernel, classes=classes, steps=steps),
        grid_spec=pltpu.PrefetchScalarGridSpec(
            num_scalar_prefetch=1,
            grid=(n_ex,),
            in_specs=[
                whole((1, rows)),
                whole((8, 1)),
                pl.BlockSpec((rows, width), lambda i, p: (0, p[1 + i])),
            ],
            out_specs=[
                pl.BlockSpec((1, classes, width), lambda i, p: (jnp.minimum(i, groups - 1), 0, 0)),
                pl.BlockSpec((1, classes, width), lambda i, p: (jnp.maximum(i - groups, 0), 0, 0)),
                whole((8, full * 6 // 8 + 128)),
            ],
            scratch_shapes=[pltpu.VMEM((classes + 16, rows), bf16), pltpu.VMEM((8, full), f32)],
        ),
        out_shape=[
            jax.ShapeDtypeStruct((groups, classes, width), f32),
            jax.ShapeDtypeStruct((groups, classes, width), f32),
            jax.ShapeDtypeStruct((8, full * 6 // 8 + 128), bf16),
        ],
        compiler_params=limit,
        name="class_sums",
    )(place, labels_row, spot, features)

    gathered = lax.all_gather(packed, "ex", axis=0, tiled=True)

    twin_pairs = [(d, d ^ 1) for d in range(n_ex)]
    summed = keep + lax.ppermute(send, "ex", twin_pairs)
    same_core = [[2 * g + c for g in range(groups)] for c in range(2)]
    pieces = lax.all_to_all(summed, "ex", 0, 0, axis_index_groups=same_core, tiled=True)
    mine_sum = jnp.sum(pieces, axis=0)
    own = [mine_sum]
    for k in range(1, groups):
        own.append(lax.ppermute(mine_sum, "ex", [(d, d ^ (2 * k)) for d in range(n_ex)]))
    own = jnp.stack(own)
    twin = lax.ppermute(own, "ex", twin_pairs)

    total = steps * classes
    x, cross, gram = pl.pallas_call(
        functools.partial(picked_kernel, steps=steps),
        grid=(n_ex,),
        in_specs=[
            whole((total, 1)),
            whole(gathered.shape),
            pl.BlockSpec((rows, width), lambda i: (0, i)),
        ],
        out_specs=[whole((total, full)), whole((total, rows)), whole((total, total))],
        out_shape=[
            jax.ShapeDtypeStruct((total, full), bf16),
            jax.ShapeDtypeStruct((total, rows), f32),
            jax.ShapeDtypeStruct((total, total), f32),
        ],
        compiler_params=limit,
        name="picked_products",
    )(index, gathered, features)

    peers = group ^ ids
    pairs = jnp.stack([core * groups + peers, (1 - core) * groups + peers], axis=1).reshape(-1)
    place = jnp.concatenate([jnp.zeros((1,), jnp.int32), pairs])
    extra = gathered[:, full * 6 // 8 :].reshape(n_ex, 8, 128)
    scores, resid = pl.pallas_call(
        functools.partial(final_kernel, steps=steps, scale=1.0 / math.sqrt(full)),
        grid_spec=pltpu.PrefetchScalarGridSpec(
            num_scalar_prefetch=1,
            grid=(groups,),
            in_specs=[
                whole((1, rows)),
                whole((n_ex, 8, 128)),
                whole((total, full)),
                whole((total, rows)),
                whole((total, total)),
                pl.BlockSpec((1, classes, width), lambda i, p: (i, 0, 0)),
                pl.BlockSpec((1, classes, width), lambda i, p: (i, 0, 0)),
                pl.BlockSpec((rows, width), lambda i, p: (0, p[1 + 2 * i])),
                pl.BlockSpec((rows, width), lambda i, p: (0, p[2 + 2 * i])),
            ],
            out_specs=[whole((steps, rows)), whole((classes, full))],
            scratch_shapes=[
                pltpu.VMEM((classes, 128), f32),
                pltpu.VMEM((classes, rows), f32),
                pltpu.VMEM((classes, total), f32),
            ],
        ),
        out_shape=[
            jax.ShapeDtypeStruct((steps, rows), f32),
            jax.ShapeDtypeStruct((classes, full), f32),
        ],
        compiler_params=limit,
        name="pursuit",
    )(place, labels_row, extra, x, cross, gram, own, twin, features, features)
    return scores, resid


def solution(mesh):
    return jax.shard_map(
        functools.partial(on_device, n_ex=mesh.shape["ex"]),
        mesh=mesh,
        in_specs=(P(("grp", "ex"), None), P(("grp", "ex")), P("grp", None)),
        out_specs=(P(None, ("grp", "ex")), P("grp", None)),
        check_vma=False,
    )
```

time: 187 us -> 114 us (0.61)
  blocking collectives: 85.7 us -> 0 us
  waiting for transfers between devices: 0.04 us -> 38.6 us
  matrix products: 37.1 us -> 0 us
  Pallas kernels: 0 us -> 36.5 us
  other arithmetic: 23.8 us -> 2.21 us
  local copies, waits for them, and re-layouts: 24.1 us -> 2.68 us
  starting transfers between devices: 0.04 us -> 19 us
    psum x1 -> x0, blocking collectives: 85.7 us -> none  [fetch_rows(): return lax.psum(masked, 'ex').astype(jnp.bfloat16)]
    dot_general x8 -> x0, matrix products: 37.1 us -> none  [the longest x3 17.7 us: correlate(): lax.dot_general(left, features, (((1,), (1,)), ((), ())), preferred_eleme...]
    pallas_call x0 -> x3, Pallas kernels: none -> 36.5 us  [the longest x1 13.2 us: on_device(): pl.pallas_call(functools.partial(picked_kernel, steps=steps), grid=(n_ex,...]
    gather x3 -> x0, local copies, waits for them, and re-layouts: 21 us -> none  [fetch_rows(): features[jnp.where(mine, local_row, 0)].astype(jnp.float32)]
    all_gather x0 -> x1, waiting for transfers between devices: none -> 16.7 us  [on_device(): gathered = lax.all_gather(packed, 'ex', axis=0, tiled=True)]
    another operation x11 -> x1, other arithmetic: 16.7 us -> 0.01 us  [on_device(): jnp.stack([core * groups + peers, (1 - core) * groups + peers], axis=1)]
    all_to_all x0 -> x1, waiting for transfers between devices: none -> 13.9 us  [on_device(): lax.all_to_all(summed, 'ex', 0, 0, axis_index_groups=same_core, tiled=True)]
    ppermute x0 -> x9, starting transfers between devices: none -> 11.8 us  [the longest x7 11.3 us: on_device(): lax.ppermute(mine_sum, 'ex', [(d, d ^ 2 * k) for d in range(n_ex)])]
  transfers between devices with their start and end apart: 1 -> 11, of which waited for: 0 -> 5; matrix products, arithmetic and copies ran while one was open for 26% -> 0% of each run, Pallas kernels for 0% -> 12%
where the time goes in v1:
time: 114 us; the launch traced here: 113 us
  waiting for transfers between devices  38.6 us (34%)
  Pallas kernels  36.5 us (32%)
  starting transfers between devices  19 us (17%)
  between operations  14.2 us (12%)
  local copies, waits for them, and re-layouts  2.68 us (2%)
  other arithmetic  2.21 us (2%)
    all_gather x1, waiting for transfers between devices, on_device(): gathered = lax.all_gather(packed, 'ex', axis=0, tiled=True)  16.7 us
    all_to_all x1, waiting for transfers between devices, on_device(): lax.all_to_all(summed, 'ex', 0, 0, axis_index_groups=same_core, tiled=True)  13.9 us
    pallas_call x1, Pallas kernels, on_device(): pl.pallas_call(functools.partial(picked_kernel, steps=steps), grid=(n_ex,...  13.2 us
    pallas_call x1, Pallas kernels, on_device(): pl.pallas_call(functools.partial(sums_kernel, classes=classes, steps=step...  12.5 us
    ppermute x7, starting transfers between devices, on_device(): lax.ppermute(mine_sum, 'ex', [(d, d ^ 2 * k) for d in range(n_ex)])  11.3 us
    pallas_call x1, Pallas kernels, on_device(): pl.pallas_call(functools.partial(final_kernel, steps=steps, scale=1.0 / m...  10.8 us
    all_to_all x1, starting transfers between devices, on_device(): lax.all_to_all(summed, 'ex', 0, 0, axis_index_groups=same_core, tiled=True)  7.2 us
    ppermute x7, waiting for transfers between devices, on_device(): lax.ppermute(mine_sum, 'ex', [(d, d ^ 2 * k) for d in range(n_ex)])  5.79 us
  transfers between devices with their start and end apart: 11, of which 5 were waited for; matrix products, arithmetic and copies ran while one was open for 0% of the time, Pallas kernels for 12%

profile of v1, /device:TPU:0, one launch (start us, length us, event | category | flops | bytes accessed | tf_op | source)
XLA Modules:
  0.0 113.3 jit_solution(1691252512057661768)
XLA Ops:
  7.2 0.7 add_select_fusion
  7.9 0.2 convert_reduce_fusion
  8.1 0.1 broadcast_subtract_fusion
  8.2 0.1 sub.44
  8.3 0.1 add.92
  8.4 0.1 select_reduce_fusion
  8.5 0.1 copy.13.pick_ref
  8.6 0.7 reshape.79.labels_ref
  9.3 0.1 fusion.1.place
  9.4 12.5 %class_sums.1 = (f32[8,32,512]{2,1,0:T(8,128)S(1)}, f32[8,32,512]{2,1,0:T(8,128)S(1)}, bf16[8,6272]{1,0:T(8,128)(2,1)}) custom-call(s32[17]{0:T(128)S(1)} %fusion.1.place, s32[1,640]{1,0:T(1,128)S(1)} %reshape.79.labels_ref, s32[8,1]{1,0:T(8,128)S(1)} %copy.13.pick_ref, bf16[640,8192]{1,0:T(8,128)(2,1)} %feat_b.1), custom_call_target="tpu_custom_call" | custom-call | tf_op jit(solution)/shard_map/class_sums/pallas_call | solution.py:218
  21.9 0.5 collective-permute-start
  22.3 1.5 %collective-permute-done = f32[8,32,512]{2,1,0:T(8,128)S(1)} collective-permute-done((f32[8,32,512]{2,1,0:T(8,128)S(1)}, f32[8,32,512]{2,1,0:T(8,128)S(1)}, u32[]{:S(2)}, u32[]{:S(2)}) %collective-permute-start) | collective-permute-done | bytes 524320 | tf_op jit(solution)/shard_map/ppermute | solution.py:247
  23.9 0.9 add.93
  24.7 7.2 %all-to-all-start = ((f32[8,32,512]{2,1,0:T(8,128)}), f32[8,32,512]{2,1,0:T(8,128)S(1)}, u32[]{:S(2)}, u32[]{:S(2)}) async-start(f32[8,32,512]{2,1,0:T(8,128)} %add.93), calls=%async_computation | async-start | bytes 1048576 | tf_op jit(solution)/shard_map/all_to_all | solution.py:249
  32.0 0.7 all-gather.2.cloned.1.call-update
  32.7 0.1 reshape.82.index_ref
  32.8 13.9 %all-to-all-done = f32[8,32,512]{2,1,0:T(8,128)S(1)} async-done(((f32[8,32,512]{2,1,0:T(8,128)}), f32[8,32,512]{2,1,0:T(8,128)S(1)}, u32[]{:S(2)}, u32[]{:S(2)}) %all-to-all-start) | async-done | bytes 524320 | tf_op jit(solution)/shard_map/all_to_all | solution.py:249
  46.8 1.5 %collective-permute-start.1 = (f32[32,512]{1,0:T(8,128)S(1)}, f32[32,512]{1,0:T(8,128)S(1)}, u32[]{:S(2)}, u32[]{:S(2)}) collective-permute-start(f32[32,512]{1,0:T(8,128)S(1)} %reduce_sum.29), channel_id=1, source_target_pairs={{0,2},{1,3},{2,0},{3,1},{4,6},{5,7},{6,4},{7,5},{8,10},{9,11},{10,... | collective-permute-start | bytes 196616 | tf_op jit(solution)/shard_map/ppermute | solution.py:253
  48.3 2.0 %collective-permute-start.3 = (f32[32,512]{1,0:T(8,128)S(1)}, f32[32,512]{1,0:T(8,128)S(1)}, u32[]{:S(2)}, u32[]{:S(2)}) collective-permute-start(f32[32,512]{1,0:T(8,128)S(1)} %reduce_sum.29), channel_id=1, source_target_pairs={{0,6},{1,7},{2,4},{3,5},{4,2},{5,3},{6,0},{7,1},{8,14},{9,15},{10,... | collective-permute-start | bytes 196616 | tf_op jit(solution)/shard_map/ppermute | solution.py:253
  50.3 0.1 collective-permute-start.4
  50.5 3.7 %collective-permute-start.5 = (f32[32,512]{1,0:T(8,128)S(1)}, f32[32,512]{1,0:T(8,128)S(1)}, u32[]{:S(2)}, u32[]{:S(2)}) collective-permute-start(f32[32,512]{1,0:T(8,128)S(1)} %reduce_sum.29), channel_id=1, source_target_pairs={{0,10},{1,11},{2,8},{3,9},{4,14},{5,15},{6,12},{7,13},{8,2},{9,3},... | collective-permute-start | bytes 196616 | tf_op jit(solution)/shard_map/ppermute | solution.py:253
  54.2 1.5 %collective-permute-start.6 = (f32[32,512]{1,0:T(8,128)S(1)}, f32[32,512]{1,0:T(8,128)S(1)}, u32[]{:S(2)}, u32[]{:S(2)}) collective-permute-start(f32[32,512]{1,0:T(8,128)S(1)} %reduce_sum.29), channel_id=1, source_target_pairs={{0,12},{1,13},{2,14},{3,15},{4,8},{5,9},{6,10},{7,11},{8,4},{9,5},... | collective-permute-start | bytes 196616 | tf_op jit(solution)/shard_map/ppermute | solution.py:253
  55.6 2.4 %collective-permute-start.7 = (f32[32,512]{1,0:T(8,128)S(1)}, f32[32,512]{1,0:T(8,128)S(1)}, u32[]{:S(2)}, u32[]{:S(2)}) collective-permute-start(f32[32,512]{1,0:T(8,128)S(1)} %reduce_sum.29), channel_id=1, source_target_pairs={{0,14},{1,15},{2,12},{3,13},{4,10},{5,11},{6,8},{7,9},{8,6},{9,7},... | collective-permute-start | bytes 196616 | tf_op jit(solution)/shard_map/ppermute | solution.py:253
  58.1 4.3 %collective-permute-done.4 = f32[32,512]{1,0:T(8,128)S(1)} collective-permute-done((f32[32,512]{1,0:T(8,128)S(1)}, f32[32,512]{1,0:T(8,128)S(1)}, u32[]{:S(2)}, u32[]{:S(2)}) %collective-permute-start.4) | collective-permute-done | bytes 65568 | tf_op jit(solution)/shard_map/ppermute | solution.py:253
  62.4 1.5 %collective-permute-done.5 = f32[32,512]{1,0:T(8,128)S(1)} collective-permute-done((f32[32,512]{1,0:T(8,128)S(1)}, f32[32,512]{1,0:T(8,128)S(1)}, u32[]{:S(2)}, u32[]{:S(2)}) %collective-permute-start.5) | collective-permute-done | bytes 65568 | tf_op jit(solution)/shard_map/ppermute | solution.py:253
  64.0 0.1 copy.12
  64.1 0.1 reshape.78
  64.2 0.1 pad_add_fusion.2.place
  64.3 16.7 %all-gather.2.cloned.1.call-done.rows_ref = bf16[128,6272]{1,0:T(8,128)(2,1)} async-done(((bf16[8,6272]{1,0:T(8,128)(2,1)}), bf16[128,6272]{1,0:T(8,128)(2,1)}) %all-gather.2.cloned.1.call-update) | async-done | bytes 1605648 | tf_op jit(solution)/shard_map/all_gather | solution.py:244
  81.0 1.4 %copy-done = bf16[128,6272]{1,0:T(8,128)(2,1)S(1)} copy-done((bf16[128,6272]{1,0:T(8,128)(2,1)S(1)}, bf16[128,6272]{1,0:T(8,128)(2,1)}, u32[]{:S(2)}) %copy-start) | copy-done | bytes 1605656
  82.4 13.2 %picked_products.1 = (bf16[96,8192]{1,0:T(8,128)(2,1)S(1)}, f32[96,640]{1,0:T(8,128)S(1)}, f32[96,96]{1,0:T(8,128)S(1)}) custom-call(s32[96,1]{1,0:T(8,128)S(1)} %reshape.82.index_ref, bf16[128,6272]{1,0:T(8,128)(2,1)S(1)} %copy-done, bf16[640,8192]{1,0:T(8,128)(2,1)} %feat_b.1), custom_call_target="tpu_custom_call" | custom-call | tf_op jit(solution)/shard_map/picked_products/pallas_call | solution.py:258
  95.6 10.8 %pursuit.1 = (f32[3,640]{1,0:T(4,128)}, f32[32,8192]{1,0:T(8,128)}) custom-call(s32[17]{0:T(128)S(1)} %pad_add_fusion.2.place, s32[1,640]{1,0:T(1,128)S(1)} %reshape.79.labels_ref, bf16[16,8,128]{2,1,0:T(8,128)(2,1)S(1)} %slice_bitcast_fusion.extra_ref, bf16[96,8192]{1,0:T(8,128)(2,1)S(1)} %get-tuple-element.9.x_ref, ...), custom_call_target="tpu_custom_call" | custom-call | tf_op jit(solution)/shard_map/pursuit/pallas_call | solution.py:280
  (26 shorter events, 0.3 us)
Async XLA Ops:
  21.9 2.0 %collective-permute-start = (f32[8,32,512]{2,1,0:T(8,128)S(1)}, f32[8,32,512]{2,1,0:T(8,128)S(1)}, u32[]{:S(2)}, u32[]{:S(2)}) collective-permute-start(f32[8,32,512]{2,1,0:T(8,128)S(1)} %get-tuple-element.13), channel_id=1, source_target_pairs={{0,1},{1,0},{2,3},{3,2},{4,5},{5,4},{6,7},{7,6},{8,9},{9,8},{10,11... | collective-permute-start | bytes 1572872 | tf_op jit(solution)/shard_map/ppermute | solution.py:247
  24.7 22.0 %all-to-all-start = ((f32[8,32,512]{2,1,0:T(8,128)}), f32[8,32,512]{2,1,0:T(8,128)S(1)}, u32[]{:S(2)}, u32[]{:S(2)}) async-start(f32[8,32,512]{2,1,0:T(8,128)} %add.93), calls=%async_computation | async-start | bytes 1048576 | tf_op jit(solution)/shard_map/all_to_all | solution.py:249
  31.9 49.0 %all-gather.2.cloned.1.call-start = ((), (), s32[]{:S(2)}) async-start(), calls=%async_computation.1 | async-start | bytes 1705984 | tf_op jit(solution)/shard_map/all_gather | solution.py:244
  46.8 7.4 %collective-permute-start.1 = (f32[32,512]{1,0:T(8,128)S(1)}, f32[32,512]{1,0:T(8,128)S(1)}, u32[]{:S(2)}, u32[]{:S(2)}) collective-permute-start(f32[32,512]{1,0:T(8,128)S(1)} %reduce_sum.29), channel_id=1, source_target_pairs={{0,2},{1,3},{2,0},{3,1},{4,6},{5,7},{6,4},{7,5},{8,10},{9,11},{10,... | collective-permute-start | bytes 196616 | tf_op jit(solution)/shard_map/ppermute | solution.py:253
  48.3 7.3 %collective-permute-start.2 = (f32[32,512]{1,0:T(8,128)S(1)}, f32[32,512]{1,0:T(8,128)S(1)}, u32[]{:S(2)}, u32[]{:S(2)}) collective-permute-start(f32[32,512]{1,0:T(8,128)S(1)} %reduce_sum.29), channel_id=1, source_target_pairs={{0,4},{1,5},{2,6},{3,7},{4,0},{5,1},{6,2},{7,3},{8,12},{9,13},{10,... | collective-permute-start | bytes 196616 | tf_op jit(solution)/shard_map/ppermute | solution.py:253
  48.3 9.8 %collective-permute-start.3 = (f32[32,512]{1,0:T(8,128)S(1)}, f32[32,512]{1,0:T(8,128)S(1)}, u32[]{:S(2)}, u32[]{:S(2)}) collective-permute-start(f32[32,512]{1,0:T(8,128)S(1)} %reduce_sum.29), channel_id=1, source_target_pairs={{0,6},{1,7},{2,4},{3,5},{4,2},{5,3},{6,0},{7,1},{8,14},{9,15},{10,... | collective-permute-start | bytes 196616 | tf_op jit(solution)/shard_map/ppermute | solution.py:253
  50.3 12.0 %collective-permute-start.4 = (f32[32,512]{1,0:T(8,128)S(1)}, f32[32,512]{1,0:T(8,128)S(1)}, u32[]{:S(2)}, u32[]{:S(2)}) collective-permute-start(f32[32,512]{1,0:T(8,128)S(1)} %reduce_sum.29), channel_id=1, source_target_pairs={{0,8},{1,9},{2,10},{3,11},{4,12},{5,13},{6,14},{7,15},{8,0},{9,1},... | collective-permute-start | bytes 196616 | tf_op jit(solution)/shard_map/ppermute | solution.py:253
  50.5 13.4 %collective-permute-start.5 = (f32[32,512]{1,0:T(8,128)S(1)}, f32[32,512]{1,0:T(8,128)S(1)}, u32[]{:S(2)}, u32[]{:S(2)}) collective-permute-start(f32[32,512]{1,0:T(8,128)S(1)} %reduce_sum.29), channel_id=1, source_target_pairs={{0,10},{1,11},{2,8},{3,9},{4,14},{5,15},{6,12},{7,13},{8,2},{9,3},... | collective-permute-start | bytes 196616 | tf_op jit(solution)/shard_map/ppermute | solution.py:253
  54.2 9.7 %collective-permute-start.6 = (f32[32,512]{1,0:T(8,128)S(1)}, f32[32,512]{1,0:T(8,128)S(1)}, u32[]{:S(2)}, u32[]{:S(2)}) collective-permute-start(f32[32,512]{1,0:T(8,128)S(1)} %reduce_sum.29), channel_id=1, source_target_pairs={{0,12},{1,13},{2,14},{3,15},{4,8},{5,9},{6,10},{7,11},{8,4},{9,5},... | collective-permute-start | bytes 196616 | tf_op jit(solution)/shard_map/ppermute | solution.py:253
  55.6 8.3 %collective-permute-start.7 = (f32[32,512]{1,0:T(8,128)S(1)}, f32[32,512]{1,0:T(8,128)S(1)}, u32[]{:S(2)}, u32[]{:S(2)}) collective-permute-start(f32[32,512]{1,0:T(8,128)S(1)} %reduce_sum.29), channel_id=1, source_target_pairs={{0,14},{1,15},{2,12},{3,13},{4,10},{5,11},{6,8},{7,9},{8,6},{9,7},... | collective-permute-start | bytes 196616 | tf_op jit(solution)/shard_map/ppermute | solution.py:253
  63.9 31.7 %collective-permute-start.8 = (f32[8,32,512]{2,1,0:T(8,128)S(1)}, f32[8,32,512]{2,1,0:T(8,128)S(1)}, u32[]{:S(2)}, u32[]{:S(2)}) collective-permute-start(f32[8,32,512]{2,1,0:T(8,128)S(1)} %bitcast_dynamic-update-slice_fusion.own_ref), channel_id=1, source_target_pairs={{0,1},{1,0},{2,3},{3,2},{4,5},{5,4},{6,7},{7,6},{8,9},{9,8},{10,11... | collective-permute-start | bytes 1572872 | tf_op jit(solution)/shard_map/ppermute | solution.py:255
  81.0 1.4 %copy-start = (bf16[128,6272]{1,0:T(8,128)(2,1)S(1)}, bf16[128,6272]{1,0:T(8,128)(2,1)}, u32[]{:S(2)}) copy-start(bf16[128,6272]{1,0:T(8,128)(2,1)} %all-gather.2.cloned.1.call-done.rows_ref) | copy-start | bytes 4816900
Sparse Core Ops, SparseCore 0:
  34.9 46.0 all-gather.1

commit v2 on v0

v2 whole, which is shorter than its diff:
```python
import functools
import math

import jax
import jax.numpy as jnp
from jax import lax
from jax.experimental import pallas as pl
from jax.experimental.pallas import tpu as pltpu
from jax.sharding import PartitionSpec as P

ridge = 1.0
slots = 2
f32 = jnp.float32
bf16 = jnp.bfloat16


def nt_dot(a, b):
    return lax.dot_general(a, b, (((1,), (1,)), ((), ())), preferred_element_type=f32)


def encode(x):
    height, width = x.shape
    top = jnp.max(jnp.abs(x), axis=1, keepdims=True)
    power = jnp.ceil(jnp.log2(jnp.maximum(top, 1e-30)) + 0.01)
    whole_x = jnp.round(x * jnp.exp2(15.0 - power))
    lane = lax.broadcasted_iota(jnp.int32, (8, 128), 1)
    mark = jnp.zeros((8, 128), f32)
    for q in range(height // 8):
        mark = jnp.where(lane == q, power[8 * q : 8 * q + 8], mark)
    chunks = [whole_x[:, j * 128 : (j + 1) * 128] for j in range(width // 128)]
    return jnp.concatenate(chunks + [mark], axis=0).astype(jnp.int32).astype(jnp.int16)


def decode(code, height):
    value = code.astype(jnp.int32).astype(f32)
    count = value.shape[0] // height
    mark = value[count * height :]
    power = jnp.concatenate([mark[:, q : q + 1] for q in range(height // 8)], axis=0)
    x = jnp.concatenate([value[j * height : (j + 1) * height] for j in range(count)], axis=1)
    return x * jnp.exp2(power - 15.0)


def sums_kernel(labels_ref, pick_ref, feat_hbm, feat_ref, send_ref, keep_ref, rows_ref, left, held, sems, *, n_ex):
    rows, full = feat_ref.shape
    steps, classes = pick_ref.shape
    width = full // n_ex
    groups = n_ex // 2
    device = lax.axis_index("ex")
    core = device % 2
    columns = []
    copies = []
    for i in range(n_ex):
        block = (1 - core) * groups + i if i < groups else core * groups + i - groups
        at = pl.ds(pl.multiple_of(block * width, width), width)
        columns.append(at)
        copies.append(pltpu.make_async_copy(feat_hbm.at[:, at], feat_ref.at[:, at], sems.at[i]))
        copies[-1].start()

    local = pick_ref[...] - device * rows
    mine = (local >= 0) & (local < rows)
    lane = lax.broadcasted_iota(jnp.int32, local.shape, 1)
    first = jnp.min(jnp.where(mine, lane, classes), axis=1, keepdims=True)
    last = jnp.max(jnp.where(mine, lane, -1), axis=1, keepdims=True)
    spot0 = jnp.max(jnp.where(mine & (lane == first), local, -1), axis=1, keepdims=True)
    spot1 = jnp.max(jnp.where(mine & (lane == last) & (last > first), local, -1), axis=1, keepdims=True)
    member = lax.broadcasted_iota(jnp.int32, (classes, rows), 0) == labels_ref[...].reshape(1, rows)
    line = lax.broadcasted_iota(jnp.int32, (steps, rows), 1)
    left[...] = jnp.concatenate(
        [
            jnp.where(member, 1.0, 0.0),
            jnp.where(line == spot0, 1.0, 0.0),
            jnp.where(line == spot1, 1.0, 0.0),
            jnp.zeros((16 - 2 * steps, rows), f32),
        ],
        axis=0,
    ).astype(bf16)

    for i in range(n_ex):
        copies[i].wait()
        both = jnp.dot(left[...], feat_ref[:, columns[i]], preferred_element_type=f32)
        if i < groups:
            send_ref[i] = both[:classes]
        else:
            keep_ref[i - groups] = both[:classes]
        held[:, columns[i]] = both[classes : classes + 8]

    used = steps * slots
    main = full * used // 8
    tail = full - main
    per = main // tail
    lines = [held[0:used, :main]]
    for q in range(used // per):
        lines.append(jnp.concatenate([held[q * per + u : q * per + u + 1, main:] for u in range(per)], axis=1))
    count = jnp.sum(jnp.where(member, 1.0, 0.0), axis=1, keepdims=True)
    high = jnp.floor(count * (1.0 / 128.0))
    low = count - 128.0 * high
    lane = lax.broadcasted_iota(jnp.int32, (8, 128), 1)
    extra = jnp.zeros((8, 128), f32)
    for q in range(classes // 8):
        extra = jnp.where(lane == 2 * q, high[8 * q : 8 * q + 8], extra)
        extra = jnp.where(lane == 2 * q + 1, low[8 * q : 8 * q + 8], extra)
    rows_ref[...] = jnp.concatenate([jnp.concatenate(lines, axis=0), extra], axis=1).astype(bf16)


def pair_kernel(keep_ref, got_ref, own_ref, *code_refs):
    group = lax.axis_index("ex") // 2
    own_ref[...] = keep_ref[group] + got_ref[group]
    for k, code_ref in enumerate(code_refs):
        block = group ^ (k + 1)
        code_ref[...] = encode(keep_ref[block] + got_ref[block])


def total_kernel(own_ref, *refs):
    value = own_ref[...]
    for code_ref in refs[:-1]:
        value = value + decode(code_ref[...], value.shape[0])
    refs[-1][...] = encode(value)


def picked_kernel(index_ref, feat_ref, *refs, steps):
    parts, (x_ref, cross_ref, gram_ref, rows_ref) = refs[:-4], refs[-4:]
    full = feat_ref.shape[1]
    used = steps * slots
    main = full * used // 8
    per = main // (full - main)
    tail = full - main
    total = x_ref.shape[0]
    lines = rows_ref.shape[0]
    at = 0
    for part in parts:
        rows_ref[at : at + part.shape[0], :] = part[...]
        at += part.shape[0]

    index = index_ref[...]
    line = lax.broadcasted_iota(jnp.int32, (total, lines), 1)
    one = jnp.where(line == index, 1.0, 0.0).astype(bf16)
    x_ref[:, :main] = jnp.dot(one, rows_ref[:, :main], preferred_element_type=f32).astype(bf16)
    slot = index % 8
    rest = jnp.zeros((total, tail), f32)
    home = index - slot + used + slot // per
    for u in range(per):
        here = jnp.where((line == home) & (slot % per == u), 1.0, 0.0).astype(bf16)
        rest = rest + jnp.dot(here, rows_ref[:, u * tail : (u + 1) * tail], preferred_element_type=f32)
    x_ref[:, main:] = rest.astype(bf16)
    x = x_ref[...]
    cross_ref[...] = nt_dot(x, feat_ref[...])
    gram_ref[...] = nt_dot(x, x)


def diagonal(block):
    n = block.shape[0]
    eye = lax.broadcasted_iota(jnp.int32, (n, n), 0) == lax.broadcasted_iota(jnp.int32, (n, n), 1)
    return jnp.sum(jnp.where(eye, block, 0.0), axis=1, keepdims=True)


def solve_all(gram, right):
    order = len(right)
    factor = [[None] * order for _ in range(order)]
    for j in range(order):
        value = gram[j][j]
        for k in range(j):
            value = value - factor[j][k] * factor[j][k]
        factor[j][j] = jnp.sqrt(value)
        for i in range(j + 1, order):
            value = gram[i][j]
            for k in range(j):
                value = value - factor[i][k] * factor[j][k]
            factor[i][j] = value / factor[j][j]
    forward = []
    for i in range(order):
        value = right[i]
        for j in range(i):
            value = value - factor[i][j] * forward[j]
        forward.append(value / factor[i][i])
    result = []
    for size in range(1, order + 1):
        back = [None] * size
        for i in reversed(range(size)):
            value = forward[i]
            for j in range(i + 1, size):
                value = value - factor[j][i] * back[j]
            back[i] = value / factor[i][i]
        result.append(back)
    return result


def pursuit_kernel(
    labels_ref, extra_ref, x_ref, cross_ref, gram_ref, own_ref, twin_ref, feat_ref, scores_ref, resid_ref, low_ref,
    *, steps, scale
):
    classes, full = resid_ref.shape
    groups = own_ref.shape[0]
    width = full // (2 * groups)
    device = lax.axis_index("ex")
    group = device // 2
    core = device % 2

    summed = jnp.sum(extra_ref[...].astype(f32), axis=0)
    count = jnp.concatenate(
        [128.0 * summed[:, 2 * q : 2 * q + 1] + summed[:, 2 * q + 1 : 2 * q + 2] for q in range(classes // 8)], axis=0
    )
    root = jnp.sqrt(count)
    for k in range(groups):
        for side, code_ref in ((core, own_ref), (1 - core, twin_ref)):
            block = side * groups + (group ^ k)
            at = pl.ds(pl.multiple_of(block * width, width), width)
            target = decode(code_ref[k], classes) / root
            resid_ref[:, at] = target
            low_ref[:, at] = target.astype(bf16)

    low = low_ref[...]
    direct = nt_dot(low, feat_ref[...])
    right = nt_dot(low, x_ref[...])
    gram = [
        [
            diagonal(gram_ref[a * classes : (a + 1) * classes, b * classes : (b + 1) * classes])
            + (ridge if a == b else 0.0)
            for b in range(steps)
        ]
        for a in range(steps)
    ]
    rhs = [diagonal(right[:, a * classes : (a + 1) * classes]) for a in range(steps)]
    weights = solve_all(gram, rhs)
    member = lax.broadcasted_iota(jnp.int32, direct.shape, 0) == labels_ref[...].reshape(1, direct.shape[1])
    for s in range(steps):
        value = direct
        for k in range(s):
            value = value - weights[s - 1][k] * cross_ref[k * classes : (k + 1) * classes]
        scores_ref[s : s + 1, :] = jnp.sum(jnp.where(member, value, 0.0), axis=0, keepdims=True) * scale
    last = weights[steps - 1]
    value = resid_ref[...]
    for k in range(steps):
        value = value - last[k] * x_ref[k * classes : (k + 1) * classes].astype(f32)
    resid_ref[...] = value


def on_device(features, labels, pick_index, *, n_ex):
    rows, full = features.shape
    steps, classes = pick_index.shape
    groups = n_ex // 2
    deep = n_ex // 4
    width = full // n_ex
    total = steps * classes
    used = steps * slots
    main = full * used // 8
    device = lax.axis_index("ex")
    limit = pltpu.CompilerParams(vmem_limit_bytes=32 << 20)
    vmem = pl.BlockSpec(memory_space=pltpu.VMEM)
    half = jax.ShapeDtypeStruct((groups, classes, width), f32)
    code = jax.ShapeDtypeStruct((classes * (width // 128) + 8, 128), jnp.int16)

    def swap(x, mask):
        return lax.ppermute(x, "ex", [(d, d ^ mask) for d in range(n_ex)])

    feat, send, keep, packed = pl.pallas_call(
        functools.partial(sums_kernel, n_ex=n_ex),
        in_specs=[vmem, vmem, pl.BlockSpec(memory_space=pltpu.HBM)],
        out_specs=[vmem] * 4,
        out_shape=[
            jax.ShapeDtypeStruct((rows, full), bf16),
            half,
            half,
            jax.ShapeDtypeStruct((8, main + 128), bf16),
        ],
        scratch_shapes=[
            pltpu.VMEM((classes + 16, rows), bf16),
            pltpu.VMEM((8, full), f32),
            pltpu.SemaphoreType.DMA((n_ex,)),
        ],
        compiler_params=limit,
        name="class_sums",
    )(labels, pick_index, features)

    got = swap(send, 1)
    rows_z = jnp.concatenate([packed] + [swap(packed, 4 * k) for k in range(1, deep)], axis=0)

    own, *codes = pl.pallas_call(
        pair_kernel,
        in_specs=[vmem] * 2,
        out_specs=[vmem] * groups,
        out_shape=[jax.ShapeDtypeStruct((classes, width), f32)] + [code] * (groups - 1),
        compiler_params=limit,
        name="pair_sums",
    )(keep, got)
    codes = [swap(codes[k - 1], 2 * k) for k in range(1, groups)]
    summed = pl.pallas_call(
        total_kernel,
        in_specs=[vmem] * groups,
        out_specs=vmem,
        out_shape=code,
        compiler_params=limit,
        name="total_sums",
    )(own, *codes)
    own_half = jnp.stack([summed] + [swap(summed, 2 * k) for k in range(1, groups)])
    twin_half = swap(own_half, 1)

    rows_y = swap(rows_z, 2)
    parts = [rows_z, rows_y, swap(rows_z, 1), swap(rows_y, 1)]

    pick_late, _ = lax.optimization_barrier((pick_index, packed))
    owner = pick_late // rows
    earlier = jnp.arange(classes)[:, None] > jnp.arange(classes)[None, :]
    rank = jnp.sum((owner[:, :, None] == owner[:, None, :]) & earlier[None], axis=2, dtype=jnp.int32)
    step_id = jnp.arange(steps, dtype=jnp.int32)[:, None]
    away = owner ^ device
    spot = ((away & 1) * 2 + ((away >> 1) & 1)) * deep + (away >> 2)
    index = (spot * 8 + rank * steps + step_id).reshape(total, 1)

    x, cross, gram = pl.pallas_call(
        functools.partial(picked_kernel, steps=steps),
        in_specs=[vmem] * 6,
        out_specs=[vmem] * 3,
        out_shape=[
            jax.ShapeDtypeStruct((total, full), bf16),
            jax.ShapeDtypeStruct((total, rows), f32),
            jax.ShapeDtypeStruct((total, total), f32),
        ],
        scratch_shapes=[pltpu.VMEM((n_ex * 8, main + 128), bf16)],
        compiler_params=limit,
        name="picked_products",
    )(index, feat, *parts)

    extra = jnp.concatenate([p[:, main:].reshape(deep, 8, 128) for p in parts], axis=0)
    scores, resid = pl.pallas_call(
        functools.partial(pursuit_kernel, steps=steps, scale=1.0 / math.sqrt(full)),
        in_specs=[vmem] * 8,
        out_specs=[vmem] * 2,
        out_shape=[
            jax.ShapeDtypeStruct((steps, rows), f32),
            jax.ShapeDtypeStruct((classes, full), f32),
        ],
        scratch_shapes=[pltpu.VMEM((classes, full), bf16)],
        compiler_params=limit,
        name="pursuit",
    )(labels, extra, x, cross, gram, own_half, twin_half, feat)
    return scores, resid


def solution(mesh):
    return jax.shard_map(
        functools.partial(on_device, n_ex=mesh.shape["ex"]),
        mesh=mesh,
        in_specs=(P(("grp", "ex"), None), P(("grp", "ex")), P("grp", None)),
        out_specs=(P(None, ("grp", "ex")), P("grp", None)),
        check_vma=False,
    )
```

time: 187 us -> 82.5 us (0.44)
  blocking collectives: 85.7 us -> 0 us
  matrix products: 37.1 us -> 0 us
  starting transfers between devices: 0.04 us -> 30.6 us
  other arithmetic: 23.8 us -> 0.26 us
  waiting for transfers between devices: 0.04 us -> 19.6 us
  Pallas kernels: 0 us -> 17.3 us
  between operations: 14.4 us -> 0.86 us
  local copies, waits for them, and re-layouts: 24.1 us -> 13.6 us
    psum x1 -> x0, blocking collectives: 85.7 us -> none  [fetch_rows(): return lax.psum(masked, 'ex').astype(jnp.bfloat16)]
    dot_general x8 -> x0, matrix products: 37.1 us -> none  [the longest x3 17.7 us: correlate(): lax.dot_general(left, features, (((1,), (1,)), ((), ())), preferred_eleme...]
    ppermute x0 -> x22, starting transfers between devices: none -> 30.6 us  [swap(): return lax.ppermute(x, 'ex', [(d, d ^ mask) for d in range(n_ex)])]
    gather x3 -> x0, local copies, waits for them, and re-layouts: 21 us -> none  [fetch_rows(): features[jnp.where(mine, local_row, 0)].astype(jnp.float32)]
    ppermute x0 -> x22, waiting for transfers between devices: none -> 19.6 us  [swap(): return lax.ppermute(x, 'ex', [(d, d ^ mask) for d in range(n_ex)])]
    pallas_call x0 -> x5, Pallas kernels: none -> 17.3 us  [the longest x1 6.77 us: on_device(): pl.pallas_call(functools.partial(sums_kernel, n_ex=n_ex), in_specs=[vmem,...]
    another operation x11 -> x0, other arithmetic: 16.7 us -> none  [the longest x8 15.8 us: solve_small(): factor = jnp.linalg.cholesky(gram_matrix)]
    unnamed x20 -> x26, local copies, waits for them, and re-layouts: 2.16 us -> 13.5 us
  transfers between devices with their start and end apart: 1 -> 22, of which waited for: 0 -> 7; matrix products, arithmetic and copies ran while one was open for 26% -> 1% of each run, Pallas kernels for 0% -> 6%
where the time goes in v2:
time: 82.5 us; the launch traced here: 82.3 us
  starting transfers between devices  30.6 us (37%)
  waiting for transfers between devices  19.6 us (24%)
  Pallas kernels  17.3 us (21%)
  local copies, waits for them, and re-layouts  13.6 us (16%)
  between operations  0.86 us (1%)
    ppermute x22, starting transfers between devices, swap(): return lax.ppermute(x, 'ex', [(d, d ^ mask) for d in range(n_ex)])  30.6 us
    ppermute x22, waiting for transfers between devices, swap(): return lax.ppermute(x, 'ex', [(d, d ^ mask) for d in range(n_ex)])  19.6 us
    unnamed x26, local copies, waits for them, and re-layouts  13.5 us
    pallas_call x1, Pallas kernels, on_device(): pl.pallas_call(functools.partial(sums_kernel, n_ex=n_ex), in_specs=[vmem,...  6.77 us
    pallas_call x1, Pallas kernels, on_device(): pl.pallas_call(functools.partial(pursuit_kernel, steps=steps, scale=1.0 /...  5.7 us
    pallas_call x1, Pallas kernels, on_device(): pl.pallas_call(functools.partial(picked_kernel, steps=steps), in_specs=[v...  4.4 us
  transfers between devices with their start and end apart: 22, of which 7 were waited for; matrix products, arithmetic and copies ran while one was open for 1% of the time, Pallas kernels for 6%

profile of v2, /device:TPU:0, one launch (start us, length us, event | category | flops | bytes accessed | tf_op | source)
XLA Modules:
  0.0 82.3 jit_solution(11077233624110810605)
XLA Ops:
  0.6 4.0 %copy-done.3 = bf16[640,8192]{1,0:T(8,128)(2,1)S(1)} copy-done((bf16[640,8192]{1,0:T(8,128)(2,1)S(1)}, bf16[640,8192]{1,0:T(8,128)(2,1)}, u32[]{:S(2)}) %copy-start.3) | copy-done | bytes 10485784
  4.6 0.7 copy-done.4
  5.3 0.7 copy-done.6
  6.0 6.8 %class_sums.1 = (bf16[640,8192]{1,0:T(8,128)(2,1)S(1)}, f32[8,32,512]{2,1,0:T(8,128)S(1)}, f32[8,32,512]{2,1,0:T(8,128)S(1)}, bf16[8,6272]{1,0:T(8,128)(2,1)S(1)}) custom-call(s32[640]{0:T(1024)S(1)} %copy-done.6, s32[3,32]{1,0:T(4,128)S(1)} %copy-done.4, bf16[640,8192]{1,0:T(8,128)(2,1)S(1)} %copy-done.3), custom_call_target="tpu_custom_call" | custom-call | tf_op jit(solution)/shard_map/class_sums/pallas_call | solution.py:255
  12.8 4.0 %copy-done = bf16[640,8192]{1,0:T(8,128)(2,1)} copy-done((bf16[640,8192]{1,0:T(8,128)(2,1)}, bf16[640,8192]{1,0:T(8,128)(2,1)S(1)}, u32[]{:S(2)}) %copy-start) | copy-done | bytes 10485784
  16.8 3.0 %collective-permute-start = (bf16[8,6272]{1,0:T(8,128)(2,1)S(1)}, bf16[8,6272]{1,0:T(8,128)(2,1)S(1)}, u32[]{:S(2)}, u32[]{:S(2)}) collective-permute-start(bf16[8,6272]{1,0:T(8,128)(2,1)S(1)} %get-tuple-element.18), channel_id=1, source_target_pairs={{0,4},{1,5},{2,6},{3,7},{4,0},{5,1},{6,2},{7,3},{8,12},{9,13},{10,... | collective-permute-start | bytes 301064 | tf_op jit(solution)/shard_map/ppermute | solution.py:253
  19.8 2.6 %collective-permute-start.1 = (bf16[8,6272]{1,0:T(8,128)(2,1)S(1)}, bf16[8,6272]{1,0:T(8,128)(2,1)S(1)}, u32[]{:S(2)}, u32[]{:S(2)}) collective-permute-start(bf16[8,6272]{1,0:T(8,128)(2,1)S(1)} %get-tuple-element.18), channel_id=1, source_target_pairs={{0,8},{1,9},{2,10},{3,11},{4,12},{5,13},{6,14},{7,15},{8,0},{9,1},... | collective-permute-start | bytes 301064 | tf_op jit(solution)/shard_map/ppermute | solution.py:253
  22.5 0.2 convert_reduce_fusion
  22.7 7.7 %collective-permute-done.1 = bf16[8,6272]{1,0:T(8,128)(2,1)S(1)} collective-permute-done((bf16[8,6272]{1,0:T(8,128)(2,1)S(1)}, bf16[8,6272]{1,0:T(8,128)(2,1)S(1)}, u32[]{:S(2)}, u32[]{:S(2)}) %collective-permute-start.1) | collective-permute-done | bytes 100384 | tf_op jit(solution)/shard_map/ppermute | solution.py:253
  30.4 1.6 %collective-permute-start.3 = (bf16[32,6272]{1,0:T(8,128)(2,1)S(1)}, bf16[32,6272]{1,0:T(8,128)(2,1)S(1)}, u32[]{:S(2)}, u32[]{:S(2)}) collective-permute-start(bf16[32,6272]{1,0:T(8,128)(2,1)S(1)} %constant_dynamic-update-slice_fusion.refs_0_), channel_id=1, source_target_pairs={{0,2},{1,3},{2,0},{3,1},{4,6},{5,7},{6,4},{7,5},{8,10},{9,11},{10,... | collective-permute-start | bytes 1204232 | tf_op jit(solution)/shard_map/ppermute | solution.py:253
  32.5 2.7 %collective-permute-start.10 = (s16[136,128]{1,0:T(8,128)(2,1)S(1)}, s16[136,128]{1,0:T(8,128)(2,1)S(1)}, u32[]{:S(2)}, u32[]{:S(2)}) collective-permute-start(s16[136,128]{1,0:T(8,128)(2,1)S(1)} %get-tuple-element.30), channel_id=1, source_target_pairs={{0,8},{1,9},{2,10},{3,11},{4,12},{5,13},{6,14},{7,15},{8,0},{9,1},... | collective-permute-start | bytes 104456 | tf_op jit(solution)/shard_map/ppermute | solution.py:253
  35.2 0.2 collective-permute-start.11
  35.4 4.3 %collective-permute-done.3.refs_1_ = bf16[32,6272]{1,0:T(8,128)(2,1)S(1)} collective-permute-done((bf16[32,6272]{1,0:T(8,128)(2,1)S(1)}, bf16[32,6272]{1,0:T(8,128)(2,1)S(1)}, u32[]{:S(2)}, u32[]{:S(2)}) %collective-permute-start.3) | collective-permute-done | bytes 401440 | tf_op jit(solution)/shard_map/ppermute | solution.py:253
  39.7 1.2 %collective-permute-start.12 = (s16[136,128]{1,0:T(8,128)(2,1)S(1)}, s16[136,128]{1,0:T(8,128)(2,1)S(1)}, u32[]{:S(2)}, u32[]{:S(2)}) collective-permute-start(s16[136,128]{1,0:T(8,128)(2,1)S(1)} %get-tuple-element.32), channel_id=1, source_target_pairs={{0,12},{1,13},{2,14},{3,15},{4,8},{5,9},{6,10},{7,11},{8,4},{9,5},... | collective-permute-start | bytes 104456 | tf_op jit(solution)/shard_map/ppermute | solution.py:253
  40.9 4.4 %collective-permute-start.13 = (s16[136,128]{1,0:T(8,128)(2,1)S(1)}, s16[136,128]{1,0:T(8,128)(2,1)S(1)}, u32[]{:S(2)}, u32[]{:S(2)}) collective-permute-start(s16[136,128]{1,0:T(8,128)(2,1)S(1)} %get-tuple-element.33), channel_id=1, source_target_pairs={{0,14},{1,15},{2,12},{3,13},{4,10},{5,11},{6,8},{7,9},{8,6},{9,7},... | collective-permute-start | bytes 104456 | tf_op jit(solution)/shard_map/ppermute | solution.py:253
  45.2 1.0 %collective-permute-start.8 = (s16[136,128]{1,0:T(8,128)(2,1)S(1)}, s16[136,128]{1,0:T(8,128)(2,1)S(1)}, u32[]{:S(2)}, u32[]{:S(2)}) collective-permute-start(s16[136,128]{1,0:T(8,128)(2,1)S(1)} %get-tuple-element.28), channel_id=1, source_target_pairs={{0,4},{1,5},{2,6},{3,7},{4,0},{5,1},{6,2},{7,3},{8,12},{9,13},{10,... | collective-permute-start | bytes 104456 | tf_op jit(solution)/shard_map/ppermute | solution.py:253
  46.2 2.5 %collective-permute-start.9 = (s16[136,128]{1,0:T(8,128)(2,1)S(1)}, s16[136,128]{1,0:T(8,128)(2,1)S(1)}, u32[]{:S(2)}, u32[]{:S(2)}) collective-permute-start(s16[136,128]{1,0:T(8,128)(2,1)S(1)} %get-tuple-element.29), channel_id=1, source_target_pairs={{0,6},{1,7},{2,4},{3,5},{4,2},{5,3},{6,0},{7,1},{8,14},{9,15},{10,... | collective-permute-start | bytes 104456 | tf_op jit(solution)/shard_map/ppermute | solution.py:253
  48.7 0.4 collective-permute-done.7.refs_0_
  49.2 1.8 %collective-permute-done.9.refs_2_ = s16[136,128]{1,0:T(8,128)(2,1)S(1)} collective-permute-done((s16[136,128]{1,0:T(8,128)(2,1)S(1)}, s16[136,128]{1,0:T(8,128)(2,1)S(1)}, u32[]{:S(2)}, u32[]{:S(2)}) %collective-permute-start.9) | collective-permute-done | bytes 34848 | tf_op jit(solution)/shard_map/ppermute | solution.py:253
  51.0 0.3 total_sums.1
  51.3 1.6 %collective-permute-start.14 = (s16[136,128]{1,0:T(8,128)(2,1)S(1)}, s16[136,128]{1,0:T(8,128)(2,1)S(1)}, u32[]{:S(2)}, u32[]{:S(2)}) collective-permute-start(s16[136,128]{1,0:T(8,128)(2,1)S(1)} %total_sums.1), channel_id=1, source_target_pairs={{0,2},{1,3},{2,0},{3,1},{4,6},{5,7},{6,4},{7,5},{8,10},{9,11},{10,... | collective-permute-start | bytes 104456 | tf_op jit(solution)/shard_map/ppermute | solution.py:253
  52.9 1.6 %collective-permute-start.15 = (s16[136,128]{1,0:T(8,128)(2,1)S(1)}, s16[136,128]{1,0:T(8,128)(2,1)S(1)}, u32[]{:S(2)}, u32[]{:S(2)}) collective-permute-start(s16[136,128]{1,0:T(8,128)(2,1)S(1)} %total_sums.1), channel_id=1, source_target_pairs={{0,4},{1,5},{2,6},{3,7},{4,0},{5,1},{6,2},{7,3},{8,12},{9,13},{10,... | collective-permute-start | bytes 104456 | tf_op jit(solution)/shard_map/ppermute | solution.py:253
  54.5 0.4 collective-permute-start.16
  54.9 1.4 %collective-permute-start.17 = (s16[136,128]{1,0:T(8,128)(2,1)S(1)}, s16[136,128]{1,0:T(8,128)(2,1)S(1)}, u32[]{:S(2)}, u32[]{:S(2)}) collective-permute-start(s16[136,128]{1,0:T(8,128)(2,1)S(1)} %total_sums.1), channel_id=1, source_target_pairs={{0,8},{1,9},{2,10},{3,11},{4,12},{5,13},{6,14},{7,15},{8,0},{9,1},... | collective-permute-start | bytes 104456 | tf_op jit(solution)/shard_map/ppermute | solution.py:253
  56.3 2.4 %collective-permute-start.18 = (s16[136,128]{1,0:T(8,128)(2,1)S(1)}, s16[136,128]{1,0:T(8,128)(2,1)S(1)}, u32[]{:S(2)}, u32[]{:S(2)}) collective-permute-start(s16[136,128]{1,0:T(8,128)(2,1)S(1)} %total_sums.1), channel_id=1, source_target_pairs={{0,10},{1,11},{2,8},{3,9},{4,14},{5,15},{6,12},{7,13},{8,2},{9,3},... | collective-permute-start | bytes 104456 | tf_op jit(solution)/shard_map/ppermute | solution.py:253
  58.8 2.5 %collective-permute-start.19 = (s16[136,128]{1,0:T(8,128)(2,1)S(1)}, s16[136,128]{1,0:T(8,128)(2,1)S(1)}, u32[]{:S(2)}, u32[]{:S(2)}) collective-permute-start(s16[136,128]{1,0:T(8,128)(2,1)S(1)} %total_sums.1), channel_id=1, source_target_pairs={{0,12},{1,13},{2,14},{3,15},{4,8},{5,9},{6,10},{7,11},{8,4},{9,5},... | collective-permute-start | bytes 104456 | tf_op jit(solution)/shard_map/ppermute | solution.py:253
  61.3 1.3 %collective-permute-start.20 = (s16[136,128]{1,0:T(8,128)(2,1)S(1)}, s16[136,128]{1,0:T(8,128)(2,1)S(1)}, u32[]{:S(2)}, u32[]{:S(2)}) collective-permute-start(s16[136,128]{1,0:T(8,128)(2,1)S(1)} %total_sums.1), channel_id=1, source_target_pairs={{0,14},{1,15},{2,12},{3,13},{4,10},{5,11},{6,8},{7,9},{8,6},{9,7},... | collective-permute-start | bytes 104456 | tf_op jit(solution)/shard_map/ppermute | solution.py:253
  62.7 1.9 %collective-permute-done.19 = s16[136,128]{1,0:T(8,128)(2,1)S(1)} collective-permute-done((s16[136,128]{1,0:T(8,128)(2,1)S(1)}, s16[136,128]{1,0:T(8,128)(2,1)S(1)}, u32[]{:S(2)}, u32[]{:S(2)}) %collective-permute-start.19) | collective-permute-done | bytes 34848 | tf_op jit(solution)/shard_map/ppermute | solution.py:253
  64.6 3.4 %collective-permute-done.20 = s16[136,128]{1,0:T(8,128)(2,1)S(1)} collective-permute-done((s16[136,128]{1,0:T(8,128)(2,1)S(1)}, s16[136,128]{1,0:T(8,128)(2,1)S(1)}, u32[]{:S(2)}, u32[]{:S(2)}) %collective-permute-start.20) | collective-permute-done | bytes 34848 | tf_op jit(solution)/shard_map/ppermute | solution.py:253
  68.1 4.0 %copy-done.1 = bf16[640,8192]{1,0:T(8,128)(2,1)S(1)} copy-done((bf16[640,8192]{1,0:T(8,128)(2,1)S(1)}, bf16[640,8192]{1,0:T(8,128)(2,1)}, u32[]{:S(2)}) %copy-start.1) | copy-done | bytes 10485784
  72.1 4.4 %picked_products.1 = (bf16[96,8192]{1,0:T(8,128)(2,1)S(1)}, f32[96,640]{1,0:T(8,128)S(1)}, f32[96,96]{1,0:T(8,128)S(1)}) custom-call(s32[96,1]{1,0:T(8,128)S(1)} %reshape.38.index_ref, bf16[640,8192]{1,0:T(8,128)(2,1)S(1)} %copy-done.1, bf16[32,6272]{1,0:T(8,128)(2,1)S(1)} %constant_dynamic-update-slice_fusion.refs_0_, ...), custom_call_target="tpu_custom_call" | custom-call | tf_op jit(solution)/shard_map/picked_products/pallas_call | solution.py:309
  76.6 5.7 %pursuit.1 = (f32[3,640]{1,0:T(4,128)}, f32[32,8192]{1,0:T(8,128)}) custom-call(s32[640]{0:T(1024)S(1)} %copy-done.7, bf16[16,8,128]{2,1,0:T(8,128)(2,1)S(1)} %pad_maximum_fusion.extra_ref, bf16[96,8192]{1,0:T(8,128)(2,1)S(1)} %get-tuple-element.21.x_ref, f32[96,640]{1,0:T(8,128)S(1)} %get-tuple-element.22.cross_ref, ...), custom_call_target="tpu_custom_call" | custom-call | tf_op jit(solution)/shard_map/pursuit/pallas_call | solution.py:324
  (55 shorter events, 0.8 us)
Async XLA Ops:
  0.6 4.0 %copy-start.3 = (bf16[640,8192]{1,0:T(8,128)(2,1)S(1)}, bf16[640,8192]{1,0:T(8,128)(2,1)}, u32[]{:S(2)}) copy-start(bf16[640,8192]{1,0:T(8,128)(2,1)} %feat_hbm.1) | copy-start | bytes 31457284
  4.6 0.7 copy-start.4
  5.3 0.7 copy-start.6
  6.0 26.0 %copy-start.5 = (s32[3,32]{1,0:T(4,128)S(1)}, s32[3,32]{1,0:T(4,128)}, u32[]{:S(2)}) copy-start(s32[3,32]{1,0:T(4,128)} %pick_ref.1) | copy-start | bytes 1156
  6.0 70.6 %copy-start.7 = (s32[640]{0:T(1024)S(1)}, s32[640]{0:T(1024)}, u32[]{:S(2)}) copy-start(s32[640]{0:T(1024)} %labels_ref.3) | copy-start | bytes 7684
  12.8 4.0 %copy-start = (bf16[640,8192]{1,0:T(8,128)(2,1)}, bf16[640,8192]{1,0:T(8,128)(2,1)S(1)}, u32[]{:S(2)}) copy-start(bf16[640,8192]{1,0:T(8,128)(2,1)S(1)} %get-tuple-element.20.feat_ref) | copy-start | bytes 31457284
  16.8 5.9 %collective-permute-start = (bf16[8,6272]{1,0:T(8,128)(2,1)S(1)}, bf16[8,6272]{1,0:T(8,128)(2,1)S(1)}, u32[]{:S(2)}, u32[]{:S(2)}) collective-permute-start(bf16[8,6272]{1,0:T(8,128)(2,1)S(1)} %get-tuple-element.18), channel_id=1, source_target_pairs={{0,4},{1,5},{2,6},{3,7},{4,0},{5,1},{6,2},{7,3},{8,12},{9,13},{10,... | collective-permute-start | bytes 301064 | tf_op jit(solution)/shard_map/ppermute | solution.py:253
  19.8 10.6 %collective-permute-start.1 = (bf16[8,6272]{1,0:T(8,128)(2,1)S(1)}, bf16[8,6272]{1,0:T(8,128)(2,1)S(1)}, u32[]{:S(2)}, u32[]{:S(2)}) collective-permute-start(bf16[8,6272]{1,0:T(8,128)(2,1)S(1)} %get-tuple-element.18), channel_id=1, source_target_pairs={{0,8},{1,9},{2,10},{3,11},{4,12},{5,13},{6,14},{7,15},{8,0},{9,1},... | collective-permute-start | bytes 301064 | tf_op jit(solution)/shard_map/ppermute | solution.py:253
  22.4 8.0 %collective-permute-start.2 = (bf16[8,6272]{1,0:T(8,128)(2,1)S(1)}, bf16[8,6272]{1,0:T(8,128)(2,1)S(1)}, u32[]{:S(2)}, u32[]{:S(2)}) collective-permute-start(bf16[8,6272]{1,0:T(8,128)(2,1)S(1)} %get-tuple-element.18), channel_id=1, source_target_pairs={{0,12},{1,13},{2,14},{3,15},{4,8},{5,9},{6,10},{7,11},{8,4},{9,5},... | collective-permute-start | bytes 301064 | tf_op jit(solution)/shard_map/ppermute | solution.py:253
  22.4 9.8 %collective-permute-start.6 = (f32[8,32,512]{2,1,0:T(8,128)S(1)}, f32[8,32,512]{2,1,0:T(8,128)S(1)}, u32[]{:S(2)}, u32[]{:S(2)}) collective-permute-start(f32[8,32,512]{2,1,0:T(8,128)S(1)} %get-tuple-element.25), channel_id=1, source_target_pairs={{0,1},{1,0},{2,3},{3,2},{4,5},{5,4},{6,7},{7,6},{8,9},{9,8},{10,11... | collective-permute-start | bytes 1572872 | tf_op jit(solution)/shard_map/ppermute | solution.py:253
  30.4 9.2 %collective-permute-start.3 = (bf16[32,6272]{1,0:T(8,128)(2,1)S(1)}, bf16[32,6272]{1,0:T(8,128)(2,1)S(1)}, u32[]{:S(2)}, u32[]{:S(2)}) collective-permute-start(bf16[32,6272]{1,0:T(8,128)(2,1)S(1)} %constant_dynamic-update-slice_fusion.refs_0_), channel_id=1, source_target_pairs={{0,2},{1,3},{2,0},{3,1},{4,6},{5,7},{6,4},{7,5},{8,10},{9,11},{10,... | collective-permute-start | bytes 1204232 | tf_op jit(solution)/shard_map/ppermute | solution.py:253
  32.2 13.1 %collective-permute-start.4 = (bf16[32,6272]{1,0:T(8,128)(2,1)S(1)}, bf16[32,6272]{1,0:T(8,128)(2,1)S(1)}, u32[]{:S(2)}, u32[]{:S(2)}) collective-permute-start(bf16[32,6272]{1,0:T(8,128)(2,1)S(1)} %constant_dynamic-update-slice_fusion.refs_0_), channel_id=1, source_target_pairs={{0,1},{1,0},{2,3},{3,2},{4,5},{5,4},{6,7},{7,6},{8,9},{9,8},{10,11... | collective-permute-start | bytes 1204232 | tf_op jit(solution)/shard_map/ppermute | solution.py:253
  32.5 12.8 %collective-permute-start.10 = (s16[136,128]{1,0:T(8,128)(2,1)S(1)}, s16[136,128]{1,0:T(8,128)(2,1)S(1)}, u32[]{:S(2)}, u32[]{:S(2)}) collective-permute-start(s16[136,128]{1,0:T(8,128)(2,1)S(1)} %get-tuple-element.30), channel_id=1, source_target_pairs={{0,8},{1,9},{2,10},{3,11},{4,12},{5,13},{6,14},{7,15},{8,0},{9,1},... | collective-permute-start | bytes 104456 | tf_op jit(solution)/shard_map/ppermute | solution.py:253
  35.2 11.0 %collective-permute-start.11 = (s16[136,128]{1,0:T(8,128)(2,1)S(1)}, s16[136,128]{1,0:T(8,128)(2,1)S(1)}, u32[]{:S(2)}, u32[]{:S(2)}) collective-permute-start(s16[136,128]{1,0:T(8,128)(2,1)S(1)} %get-tuple-element.31), channel_id=1, source_target_pairs={{0,10},{1,11},{2,8},{3,9},{4,14},{5,15},{6,12},{7,13},{8,2},{9,3},... | collective-permute-start | bytes 104456 | tf_op jit(solution)/shard_map/ppermute | solution.py:253
  39.7 9.0 %collective-permute-start.12 = (s16[136,128]{1,0:T(8,128)(2,1)S(1)}, s16[136,128]{1,0:T(8,128)(2,1)S(1)}, u32[]{:S(2)}, u32[]{:S(2)}) collective-permute-start(s16[136,128]{1,0:T(8,128)(2,1)S(1)} %get-tuple-element.32), channel_id=1, source_target_pairs={{0,12},{1,13},{2,14},{3,15},{4,8},{5,9},{6,10},{7,11},{8,4},{9,5},... | collective-permute-start | bytes 104456 | tf_op jit(solution)/shard_map/ppermute | solution.py:253
  40.9 7.9 %collective-permute-start.13 = (s16[136,128]{1,0:T(8,128)(2,1)S(1)}, s16[136,128]{1,0:T(8,128)(2,1)S(1)}, u32[]{:S(2)}, u32[]{:S(2)}) collective-permute-start(s16[136,128]{1,0:T(8,128)(2,1)S(1)} %get-tuple-element.33), channel_id=1, source_target_pairs={{0,14},{1,15},{2,12},{3,13},{4,10},{5,11},{6,8},{7,9},{8,6},{9,7},... | collective-permute-start | bytes 104456 | tf_op jit(solution)/shard_map/ppermute | solution.py:253
  45.2 3.9 %collective-permute-start.7 = (s16[136,128]{1,0:T(8,128)(2,1)S(1)}, s16[136,128]{1,0:T(8,128)(2,1)S(1)}, u32[]{:S(2)}, u32[]{:S(2)}) collective-permute-start(s16[136,128]{1,0:T(8,128)(2,1)S(1)} %get-tuple-element.27), channel_id=1, source_target_pairs={{0,2},{1,3},{2,0},{3,1},{4,6},{5,7},{6,4},{7,5},{8,10},{9,11},{10,... | collective-permute-start | bytes 104456 | tf_op jit(solution)/shard_map/ppermute | solution.py:253
  45.2 4.0 %collective-permute-start.8 = (s16[136,128]{1,0:T(8,128)(2,1)S(1)}, s16[136,128]{1,0:T(8,128)(2,1)S(1)}, u32[]{:S(2)}, u32[]{:S(2)}) collective-permute-start(s16[136,128]{1,0:T(8,128)(2,1)S(1)} %get-tuple-element.28), channel_id=1, source_target_pairs={{0,4},{1,5},{2,6},{3,7},{4,0},{5,1},{6,2},{7,3},{8,12},{9,13},{10,... | collective-permute-start | bytes 104456 | tf_op jit(solution)/shard_map/ppermute | solution.py:253
  46.2 4.8 %collective-permute-start.9 = (s16[136,128]{1,0:T(8,128)(2,1)S(1)}, s16[136,128]{1,0:T(8,128)(2,1)S(1)}, u32[]{:S(2)}, u32[]{:S(2)}) collective-permute-start(s16[136,128]{1,0:T(8,128)(2,1)S(1)} %get-tuple-element.29), channel_id=1, source_target_pairs={{0,6},{1,7},{2,4},{3,5},{4,2},{5,3},{6,0},{7,1},{8,14},{9,15},{10,... | collective-permute-start | bytes 104456 | tf_op jit(solution)/shard_map/ppermute | solution.py:253
  48.7 19.4 %collective-permute-start.5 = (bf16[32,6272]{1,0:T(8,128)(2,1)S(1)}, bf16[32,6272]{1,0:T(8,128)(2,1)S(1)}, u32[]{:S(2)}, u32[]{:S(2)}) collective-permute-start(bf16[32,6272]{1,0:T(8,128)(2,1)S(1)} %collective-permute-done.3.refs_1_), channel_id=1, source_target_pairs={{0,1},{1,0},{2,3},{3,2},{4,5},{5,4},{6,7},{7,6},{8,9},{9,8},{10,11... | collective-permute-start | bytes 1204232 | tf_op jit(solution)/shard_map/ppermute | solution.py:253
  51.3 5.0 %collective-permute-start.14 = (s16[136,128]{1,0:T(8,128)(2,1)S(1)}, s16[136,128]{1,0:T(8,128)(2,1)S(1)}, u32[]{:S(2)}, u32[]{:S(2)}) collective-permute-start(s16[136,128]{1,0:T(8,128)(2,1)S(1)} %total_sums.1), channel_id=1, source_target_pairs={{0,2},{1,3},{2,0},{3,1},{4,6},{5,7},{6,4},{7,5},{8,10},{9,11},{10,... | collective-permute-start | bytes 104456 | tf_op jit(solution)/shard_map/ppermute | solution.py:253
  52.9 5.9 %collective-permute-start.15 = (s16[136,128]{1,0:T(8,128)(2,1)S(1)}, s16[136,128]{1,0:T(8,128)(2,1)S(1)}, u32[]{:S(2)}, u32[]{:S(2)}) collective-permute-start(s16[136,128]{1,0:T(8,128)(2,1)S(1)} %total_sums.1), channel_id=1, source_target_pairs={{0,4},{1,5},{2,6},{3,7},{4,0},{5,1},{6,2},{7,3},{8,12},{9,13},{10,... | collective-permute-start | bytes 104456 | tf_op jit(solution)/shard_map/ppermute | solution.py:253
  54.5 6.9 %collective-permute-start.16 = (s16[136,128]{1,0:T(8,128)(2,1)S(1)}, s16[136,128]{1,0:T(8,128)(2,1)S(1)}, u32[]{:S(2)}, u32[]{:S(2)}) collective-permute-start(s16[136,128]{1,0:T(8,128)(2,1)S(1)} %total_sums.1), channel_id=1, source_target_pairs={{0,6},{1,7},{2,4},{3,5},{4,2},{5,3},{6,0},{7,1},{8,14},{9,15},{10,... | collective-permute-start | bytes 104456 | tf_op jit(solution)/shard_map/ppermute | solution.py:253
  54.9 7.8 %collective-permute-start.17 = (s16[136,128]{1,0:T(8,128)(2,1)S(1)}, s16[136,128]{1,0:T(8,128)(2,1)S(1)}, u32[]{:S(2)}, u32[]{:S(2)}) collective-permute-start(s16[136,128]{1,0:T(8,128)(2,1)S(1)} %total_sums.1), channel_id=1, source_target_pairs={{0,8},{1,9},{2,10},{3,11},{4,12},{5,13},{6,14},{7,15},{8,0},{9,1},... | collective-permute-start | bytes 104456 | tf_op jit(solution)/shard_map/ppermute | solution.py:253
  56.3 6.4 %collective-permute-start.18 = (s16[136,128]{1,0:T(8,128)(2,1)S(1)}, s16[136,128]{1,0:T(8,128)(2,1)S(1)}, u32[]{:S(2)}, u32[]{:S(2)}) collective-permute-start(s16[136,128]{1,0:T(8,128)(2,1)S(1)} %total_sums.1), channel_id=1, source_target_pairs={{0,10},{1,11},{2,8},{3,9},{4,14},{5,15},{6,12},{7,13},{8,2},{9,3},... | collective-permute-start | bytes 104456 | tf_op jit(solution)/shard_map/ppermute | solution.py:253
  58.8 5.8 %collective-permute-start.19 = (s16[136,128]{1,0:T(8,128)(2,1)S(1)}, s16[136,128]{1,0:T(8,128)(2,1)S(1)}, u32[]{:S(2)}, u32[]{:S(2)}) collective-permute-start(s16[136,128]{1,0:T(8,128)(2,1)S(1)} %total_sums.1), channel_id=1, source_target_pairs={{0,12},{1,13},{2,14},{3,15},{4,8},{5,9},{6,10},{7,11},{8,4},{9,5},... | collective-permute-start | bytes 104456 | tf_op jit(solution)/shard_map/ppermute | solution.py:253
  61.3 6.7 %collective-permute-start.20 = (s16[136,128]{1,0:T(8,128)(2,1)S(1)}, s16[136,128]{1,0:T(8,128)(2,1)S(1)}, u32[]{:S(2)}, u32[]{:S(2)}) collective-permute-start(s16[136,128]{1,0:T(8,128)(2,1)S(1)} %total_sums.1), channel_id=1, source_target_pairs={{0,14},{1,15},{2,12},{3,13},{4,10},{5,11},{6,8},{7,9},{8,6},{9,7},... | collective-permute-start | bytes 104456 | tf_op jit(solution)/shard_map/ppermute | solution.py:253
  68.0 8.5 %collective-permute-start.21 = (s16[8,136,128]{2,1,0:T(8,128)(2,1)S(1)}, s16[8,136,128]{2,1,0:T(8,128)(2,1)S(1)}, u32[]{:S(2)}, u32[]{:S(2)}) collective-permute-start(s16[8,136,128]{2,1,0:T(8,128)(2,1)S(1)} %bitcast_dynamic-update-slice_fusion.own_ref), channel_id=1, source_target_pairs={{0,1},{1,0},{2,3},{3,2},{4,5},{5,4},{6,7},{7,6},{8,9},{9,8},{10,11... | collective-permute-start | bytes 835592 | tf_op jit(solution)/shard_map/ppermute | solution.py:253
  68.1 4.0 %copy-start.1 = (bf16[640,8192]{1,0:T(8,128)(2,1)S(1)}, bf16[640,8192]{1,0:T(8,128)(2,1)}, u32[]{:S(2)}) copy-start(bf16[640,8192]{1,0:T(8,128)(2,1)} %copy-done) | copy-start | bytes 31457284
  72.1 4.5 %copy-start.2 = (bf16[640,8192]{1,0:T(8,128)(2,1)S(1)}, bf16[640,8192]{1,0:T(8,128)(2,1)}, u32[]{:S(2)}) copy-start(bf16[640,8192]{1,0:T(8,128)(2,1)} %copy-done) | copy-start | bytes 31457284

commit v3 on v2

--- a/solution.py
+++ b/solution.py
@@ -40,13 +40,21 @@
     return x * jnp.exp2(power - 15.0)
 
 
-def sums_kernel(labels_ref, pick_ref, feat_hbm, feat_ref, send_ref, keep_ref, rows_ref, left, held, sems, *, n_ex):
+def sums_kernel(
+    labels_hbm, pick_hbm, feat_hbm, feat_ref, send_ref, keep_ref, rows_ref, labels_ref, pick_ref, left, held, sems, *, n_ex
+):
     rows, full = feat_ref.shape
     steps, classes = pick_ref.shape
     width = full // n_ex
     groups = n_ex // 2
     device = lax.axis_index("ex")
     core = device % 2
+    small = [
+        pltpu.make_async_copy(pick_hbm, pick_ref, sems.at[n_ex]),
+        pltpu.make_async_copy(labels_hbm, labels_ref, sems.at[n_ex + 1]),
+    ]
+    for copy in small:
+        copy.start()
     columns = []
     copies = []
     for i in range(n_ex):
@@ -56,6 +64,8 @@
         copies.append(pltpu.make_async_copy(feat_hbm.at[:, at], feat_ref.at[:, at], sems.at[i]))
         copies[-1].start()
 
+    for copy in small:
+        copy.wait()
     local = pick_ref[...] - device * rows
     mine = (local >= 0) & (local < rows)
     lane = lax.broadcasted_iota(jnp.int32, local.shape, 1)
@@ -102,19 +112,18 @@
     rows_ref[...] = jnp.concatenate([jnp.concatenate(lines, axis=0), extra], axis=1).astype(bf16)
 
 
-def pair_kernel(keep_ref, got_ref, own_ref, *code_refs):
-    group = lax.axis_index("ex") // 2
-    own_ref[...] = keep_ref[group] + got_ref[group]
-    for k, code_ref in enumerate(code_refs):
-        block = group ^ (k + 1)
-        code_ref[...] = encode(keep_ref[block] + got_ref[block])
-
-
-def total_kernel(own_ref, *refs):
-    value = own_ref[...]
-    for code_ref in refs[:-1]:
-        value = value + decode(code_ref[...], value.shape[0])
-    refs[-1][...] = encode(value)
+def pair_kernel(keep_ref, got_ref, code_ref):
+    for k in range(keep_ref.shape[0]):
+        code_ref[k] = encode(keep_ref[k] + got_ref[k])
+
+
+def total_kernel(got_ref, code_ref, *, classes):
+    value = decode(got_ref[0], classes)
+    for k in range(1, got_ref.shape[0]):
+        value = value + decode(got_ref[k], classes)
+    code = encode(value)
+    for k in range(code_ref.shape[0]):
+        code_ref[k] = code
 
 
 def picked_kernel(index_ref, feat_ref, *refs, steps):
@@ -192,7 +201,6 @@
     groups = own_ref.shape[0]
     width = full // (2 * groups)
     device = lax.axis_index("ex")
-    group = device // 2
     core = device % 2
 
     summed = jnp.sum(extra_ref[...].astype(f32), axis=0)
@@ -202,7 +210,7 @@
     root = jnp.sqrt(count)
     for k in range(groups):
         for side, code_ref in ((core, own_ref), (1 - core, twin_ref)):
-            block = side * groups + (group ^ k)
+            block = side * groups + k
             at = pl.ds(pl.multiple_of(block * width, width), width)
             target = decode(code_ref[k], classes) / root
             resid_ref[:, at] = target
@@ -244,54 +252,60 @@
     used = steps * slots
     main = full * used // 8
     device = lax.axis_index("ex")
-    limit = pltpu.CompilerParams(vmem_limit_bytes=32 << 20)
+    limit = pltpu.CompilerParams(vmem_limit_bytes=12 << 20)
     vmem = pl.BlockSpec(memory_space=pltpu.VMEM)
+    hbm = pl.BlockSpec(memory_space=pltpu.HBM)
     half = jax.ShapeDtypeStruct((groups, classes, width), f32)
-    code = jax.ShapeDtypeStruct((classes * (width // 128) + 8, 128), jnp.int16)
+    codes = jax.ShapeDtypeStruct((groups, classes * (width // 128) + 8, 128), jnp.int16)
 
     def swap(x, mask):
         return lax.ppermute(x, "ex", [(d, d ^ mask) for d in range(n_ex)])
 
+    def trade(x, stride):
+        teams = [[s + stride * k for k in range(n_ex // stride)] for s in range(stride)]
+        return lax.all_to_all(x, "ex", 0, 0, axis_index_groups=teams, tiled=True)
+
     feat, send, keep, packed = pl.pallas_call(
         functools.partial(sums_kernel, n_ex=n_ex),
-        in_specs=[vmem, vmem, pl.BlockSpec(memory_space=pltpu.HBM)],
+        in_specs=[hbm] * 3,
         out_specs=[vmem] * 4,
         out_shape=[
-            jax.ShapeDtypeStruct((rows, full), bf16),
+            pltpu.VMEM((rows, full), bf16),
             half,
             half,
             jax.ShapeDtypeStruct((8, main + 128), bf16),
         ],
         scratch_shapes=[
+            pltpu.VMEM(labels.shape, jnp.int32),
+            pltpu.VMEM(pick_index.shape, jnp.int32),
             pltpu.VMEM((classes + 16, rows), bf16),
             pltpu.VMEM((8, full), f32),
-            pltpu.SemaphoreType.DMA((n_ex,)),
+            pltpu.SemaphoreType.DMA((n_ex + 2,)),
         ],
         compiler_params=limit,
         name="class_sums",
-    )(labels, pick_index, features)
+    )(*[pltpu.with_memory_space_constraint(a, pltpu.HBM) for a in (labels, pick_index, features)])
 
     got = swap(send, 1)
-    rows_z = jnp.concatenate([packed] + [swap(packed, 4 * k) for k in range(1, deep)], axis=0)
-
-    own, *codes = pl.pallas_call(
+    rows_z = trade(jnp.broadcast_to(packed[None], (deep,) + packed.shape), 4).reshape(deep * 8, main + 128)
+
+    codes_out = pl.pallas_call(
         pair_kernel,
         in_specs=[vmem] * 2,
-        out_specs=[vmem] * groups,
-        out_shape=[jax.ShapeDtypeStruct((classes, width), f32)] + [code] * (groups - 1),
+        out_specs=vmem,
+        out_shape=codes,
         compiler_params=limit,
         name="pair_sums",
     )(keep, got)
-    codes = [swap(codes[k - 1], 2 * k) for k in range(1, groups)]
-    summed = pl.pallas_call(
-        total_kernel,
-        in_specs=[vmem] * groups,
+    own_half = pl.pallas_call(
+        functools.partial(total_kernel, classes=classes),
+        in_specs=[vmem],
         out_specs=vmem,
-        out_shape=code,
+        out_shape=codes,
         compiler_params=limit,
         name="total_sums",
-    )(own, *codes)
-    own_half = jnp.stack([summed] + [swap(summed, 2 * k) for k in range(1, groups)])
+    )(trade(codes_out, 2))
+    own_half = trade(own_half, 2)
     twin_half = swap(own_half, 1)
 
     rows_y = swap(rows_z, 2)
@@ -303,7 +317,7 @@
     rank = jnp.sum((owner[:, :, None] == owner[:, None, :]) & earlier[None], axis=2, dtype=jnp.int32)
     step_id = jnp.arange(steps, dtype=jnp.int32)[:, None]
     away = owner ^ device
-    spot = ((away & 1) * 2 + ((away >> 1) & 1)) * deep + (away >> 2)
+    spot = ((away & 1) * 2 + ((away >> 1) & 1)) * deep + (owner >> 2)
     index = (spot * 8 + rank * steps + step_id).reshape(total, 1)
 
     x, cross, gram = pl.pallas_call(

time: 82.5 us -> 69.9 us (0.85)
  starting transfers between devices: 30.6 us -> 15.8 us
  local copies, waits for them, and re-layouts: 13.6 us -> 17 us
  waiting for transfers between devices: 19.6 us -> 18.2 us
    ppermute x22 -> x5, starting transfers between devices: 30.6 us -> 2.3 us  [swap(): return lax.ppermute(x, 'ex', [(d, d ^ mask) for d in range(n_ex)])]
    ppermute x22 -> x5, waiting for transfers between devices: 19.6 us -> 3.12 us  [swap(): return lax.ppermute(x, 'ex', [(d, d ^ mask) for d in range(n_ex)])]
    all_to_all x0 -> x3, waiting for transfers between devices: none -> 15 us  [trade(): return lax.all_to_all(x, 'ex', 0, 0, axis_index_groups=teams, tiled=True)]
    all_to_all x0 -> x3, starting transfers between devices: none -> 13.5 us  [trade(): return lax.all_to_all(x, 'ex', 0, 0, axis_index_groups=teams, tiled=True)]
    reshape x4, local copies, waits for them, and re-layouts: 0.01 us -> 1.79 us  [on_device(): p[:, main:].reshape(deep, 8, 128)]
    unnamed x26 -> x14, local copies, waits for them, and re-layouts: 13.5 us -> 14.3 us
  transfers between devices with their start and end apart: 22 -> 8, of which waited for: 7 -> 5; matrix products, arithmetic and copies ran while one was open for 1% -> 4% of each run, Pallas kernels for 6% -> 9%
where the time goes in v3:
time: 69.9 us; the launch traced here: 69.3 us
  waiting for transfers between devices  18.2 us (26%)
  local copies, waits for them, and re-layouts  17 us (24%)
  Pallas kernels  16.7 us (24%)
  starting transfers between devices  15.8 us (23%)
  other arithmetic  0.99 us (1%)
  between operations  0.72 us (1%)
    all_to_all x3, waiting for transfers between devices, trade(): return lax.all_to_all(x, 'ex', 0, 0, axis_index_groups=teams, tiled=True)  15 us
    unnamed x14, local copies, waits for them, and re-layouts  14.3 us
    all_to_all x3, starting transfers between devices, trade(): return lax.all_to_all(x, 'ex', 0, 0, axis_index_groups=teams, tiled=True)  13.5 us
    pallas_call x1, Pallas kernels, on_device(): pl.pallas_call(functools.partial(pursuit_kernel, steps=steps, scale=1.0 /...  5.39 us
    pallas_call x1, Pallas kernels, on_device(): pl.pallas_call(functools.partial(sums_kernel, n_ex=n_ex), in_specs=[hbm]...  5.06 us
    pallas_call x1, Pallas kernels, on_device(): pl.pallas_call(functools.partial(picked_kernel, steps=steps), in_specs=[v...  4.39 us
    ppermute x5, waiting for transfers between devices, swap(): return lax.ppermute(x, 'ex', [(d, d ^ mask) for d in range(n_ex)])  3.12 us
    ppermute x5, starting transfers between devices, swap(): return lax.ppermute(x, 'ex', [(d, d ^ mask) for d in range(n_ex)])  2.3 us
  transfers between devices with their start and end apart: 8, of which 5 were waited for; matrix products, arithmetic and copies ran while one was open for 4% of the time, Pallas kernels for 9%

profile of v3, /device:TPU:0, one launch (start us, length us, event | category | flops | bytes accessed | tf_op | source)
XLA Modules:
  0.0 69.3 jit_solution(11141257926228538824)
XLA Ops:
  0.6 5.1 %class_sums.1 = (bf16[640,8192]{1,0:T(8,128)(2,1)S(1)}, f32[8,32,512]{2,1,0:T(8,128)S(1)}, f32[8,32,512]{2,1,0:T(8,128)S(1)}, bf16[8,6272]{1,0:T(8,128)(2,1)S(1)}) custom-call(s32[640]{0:T(1024)} %labels_ref.1, s32[3,32]{1,0:T(4,128)} %pick_hbm.1, bf16[640,8192]{1,0:T(8,128)(2,1)} %feat_hbm.1), custom_call_target="tpu_custom_call" | custom-call | tf_op jit(solution)/shard_map/class_sums/pallas_call | solution.py:268
  5.7 4.0 %copy-done = bf16[640,8192]{1,0:T(8,128)(2,1)} copy-done((bf16[640,8192]{1,0:T(8,128)(2,1)}, bf16[640,8192]{1,0:T(8,128)(2,1)S(1)}, u32[]{:S(2)}) %copy-start) | copy-done | bytes 10485784
  9.7 0.8 %broadcast_in_dim.2 = bf16[4,8,6272]{2,1,0:T(8,128)(2,1)} broadcast(bf16[8,6272]{1,0:T(8,128)(2,1)S(1)} %get-tuple-element.10), dimensions={1,2} | broadcast | bytes 501760 | tf_op jit(solution)/shard_map/broadcast_in_dim | solution.py:290
  10.5 6.3 %all-to-all-start = ((bf16[4,8,6272]{2,1,0:T(8,128)(2,1)}), bf16[4,8,6272]{2,1,0:T(8,128)(2,1)S(1)}, u32[]{:S(2)}, u32[]{:S(2)}) async-start(bf16[4,8,6272]{2,1,0:T(8,128)(2,1)} %broadcast_in_dim.2), calls=%async_computation | async-start | bytes 802816 | tf_op jit(solution)/shard_map/all_to_all | solution.py:266
  16.8 1.9 %collective-permute-done.3.got_ref = f32[8,32,512]{2,1,0:T(8,128)S(1)} collective-permute-done((f32[8,32,512]{2,1,0:T(8,128)S(1)}, f32[8,32,512]{2,1,0:T(8,128)S(1)}, u32[]{:S(2)}, u32[]{:S(2)}) %collective-permute-start.3) | collective-permute-done | bytes 524320 | tf_op jit(solution)/shard_map/ppermute | solution.py:262
  18.7 0.9 %pair_sums.1 = s16[8,136,128]{2,1,0:T(8,128)(2,1)} custom-call(f32[8,32,512]{2,1,0:T(8,128)S(1)} %get-tuple-element.16.keep_ref, f32[8,32,512]{2,1,0:T(8,128)S(1)} %collective-permute-done.3.got_ref), custom_call_target="tpu_custom_call" | custom-call | tf_op jit(solution)/shard_map/pair_sums/pallas_call | solution.py:292
  19.6 9.1 %all-to-all-done = bf16[4,8,6272]{2,1,0:T(8,128)(2,1)S(1)} async-done(((bf16[4,8,6272]{2,1,0:T(8,128)(2,1)}), bf16[4,8,6272]{2,1,0:T(8,128)(2,1)S(1)}, u32[]{:S(2)}, u32[]{:S(2)}) %all-to-all-start) | async-done | bytes 401440 | tf_op jit(solution)/shard_map/all_to_all | solution.py:266
  28.7 3.7 %all-to-all-start.1 = ((s16[8,136,128]{2,1,0:T(8,128)(2,1)}), s16[8,136,128]{2,1,0:T(8,128)(2,1)S(1)}, u32[]{:S(2)}, u32[]{:S(2)}) async-start(s16[8,136,128]{2,1,0:T(8,128)(2,1)} %pair_sums.1), calls=%async_computation.1 | async-start | bytes 557056 | tf_op jit(solution)/shard_map/all_to_all | solution.py:266
  32.4 0.2 convert_reduce_fusion
  32.6 2.1 %collective-permute-start = (bf16[32,6272]{1,0:T(8,128)(2,1)S(1)}, bf16[32,6272]{1,0:T(8,128)(2,1)S(1)}, u32[]{:S(2)}, u32[]{:S(2)}) collective-permute-start(bf16[32,6272]{1,0:T(8,128)(2,1)S(1)} %bitcast.9), channel_id=1, source_target_pairs={{0,2},{1,3},{2,0},{3,1},{4,6},{5,7},{6,4},{7,5},{8,10},{9,11},{10,... | collective-permute-start | bytes 1204232 | tf_op jit(solution)/shard_map/ppermute | solution.py:262
  34.7 0.1 reshape.43.index_ref
  34.8 0.1 collective-permute-start.1
  34.9 6.0 %all-to-all-done.1.got_ref = s16[8,136,128]{2,1,0:T(8,128)(2,1)S(1)} async-done(((s16[8,136,128]{2,1,0:T(8,128)(2,1)}), s16[8,136,128]{2,1,0:T(8,128)(2,1)S(1)}, u32[]{:S(2)}, u32[]{:S(2)}) %all-to-all-start.1) | async-done | bytes 278560 | tf_op jit(solution)/shard_map/all_to_all | solution.py:266
  40.9 1.0 %total_sums.1 = s16[8,136,128]{2,1,0:T(8,128)(2,1)} custom-call(s16[8,136,128]{2,1,0:T(8,128)(2,1)S(1)} %all-to-all-done.1.got_ref), custom_call_target="tpu_custom_call" | custom-call | tf_op jit(solution)/shard_map/total_sums/pallas_call | solution.py:300
  41.9 3.5 %all-to-all-start.2 = ((s16[8,136,128]{2,1,0:T(8,128)(2,1)}), s16[8,136,128]{2,1,0:T(8,128)(2,1)S(1)}, u32[]{:S(2)}, u32[]{:S(2)}) async-start(s16[8,136,128]{2,1,0:T(8,128)(2,1)} %total_sums.1), calls=%async_computation.2 | async-start | bytes 557056 | tf_op jit(solution)/shard_map/all_to_all | solution.py:266
  45.3 0.6 slice_bitcast_fusion.3
  45.9 0.0 collective-permute-start.2
  45.9 0.6 slice_bitcast_fusion.2
  46.5 0.0 collective-permute-done.1.refs_2_
  46.5 0.6 slice_bitcast_fusion.1
  47.1 0.5 collective-permute-done.2.refs_3_
  47.7 4.0 %copy-done.1 = bf16[640,8192]{1,0:T(8,128)(2,1)S(1)} copy-done((bf16[640,8192]{1,0:T(8,128)(2,1)S(1)}, bf16[640,8192]{1,0:T(8,128)(2,1)}, u32[]{:S(2)}) %copy-start.1) | copy-done | bytes 10485784
  51.7 4.4 %picked_products.1 = (bf16[96,8192]{1,0:T(8,128)(2,1)S(1)}, f32[96,640]{1,0:T(8,128)S(1)}, f32[96,96]{1,0:T(8,128)S(1)}) custom-call(s32[96,1]{1,0:T(8,128)S(1)} %reshape.43.index_ref, bf16[640,8192]{1,0:T(8,128)(2,1)S(1)} %copy-done.1, bf16[32,6272]{1,0:T(8,128)(2,1)S(1)} %bitcast.12, bf16[32,6272]{1,0:T(8,128)(2,1)S(1)} %collective-permute-done.refs_1_, ...), custom_call_target="tpu_custom_call" | custom-call | tf_op jit(solution)/shard_map/picked_products/pallas_call | solution.py:323
  56.1 0.7 %copy-done.3 = f32[96,640]{1,0:T(8,128)} copy-done((f32[96,640]{1,0:T(8,128)}, f32[96,640]{1,0:T(8,128)S(1)}, u32[]{:S(2)}) %copy-start.3) | copy-done | bytes 245784
  56.8 0.0 all-to-all-done.2.own_ref
  56.8 0.1 collective-permute-start.4
  56.9 0.7 %pad_maximum_fusion.extra_ref = bf16[16,8,128]{2,1,0:T(8,128)(2,1)S(1)} fusion(bf16[4,8,128]{2,1,0:T(8,128)(2,1)S(1)} %slice_bitcast_fusion, bf16[4,8,128]{2,1,0:T(8,128)(2,1)} %slice_bitcast_fusion.1, bf16[4,8,128]{2,1,0:T(8,128)(2,1)} %slice_bitcast_fusion.2, bf16[4,8,128]{2,1,0:T(8,128)(2,1)} %slice_bitcast_fusion.3), kind=kLoop, calls=%fused_computation.1 | loop fusion | flops 49152 | bytes 65536 | tf_op jit(solution)/shard_map/concatenate | solution.py:337
  57.7 0.7 collective-permute-done.4.twin_ref
  58.3 4.0 %copy-done.2 = bf16[640,8192]{1,0:T(8,128)(2,1)S(1)} copy-done((bf16[640,8192]{1,0:T(8,128)(2,1)S(1)}, bf16[640,8192]{1,0:T(8,128)(2,1)}, u32[]{:S(2)}) %copy-start.2) | copy-done | bytes 10485784
  62.3 0.9 %copy-done.4 = f32[96,640]{1,0:T(8,128)S(1)} copy-done((f32[96,640]{1,0:T(8,128)S(1)}, f32[96,640]{1,0:T(8,128)}, u32[]{:S(2)}) %copy-start.4) | copy-done | bytes 245784
  63.3 0.7 copy-done.5
  63.9 5.4 %pursuit.1 = (f32[3,640]{1,0:T(4,128)}, f32[32,8192]{1,0:T(8,128)}) custom-call(s32[640]{0:T(1024)S(1)} %copy-done.5, bf16[16,8,128]{2,1,0:T(8,128)(2,1)S(1)} %pad_maximum_fusion.extra_ref, bf16[96,8192]{1,0:T(8,128)(2,1)S(1)} %get-tuple-element.13.x_ref, f32[96,640]{1,0:T(8,128)S(1)} %copy-done.4, f32[96,96]{1,0:T(8,128)S(1)} %get-tuple-element.15.gram_ref, ...), custom_call_target="tpu_custom_call" | custom-call | tf_op jit(solution)/shard_map/pursuit/pallas_call | solution.py:338
  (14 shorter events, 0.1 us)
Async XLA Ops:
  0.6 31.7 %copy-start.6 = (s32[3,32]{1,0:T(4,128)S(1)}, s32[3,32]{1,0:T(4,128)}, u32[]{:S(2)}) copy-start(s32[3,32]{1,0:T(4,128)} %pick_hbm.1) | copy-start | bytes 1156
  5.7 4.0 %copy-start = (bf16[640,8192]{1,0:T(8,128)(2,1)}, bf16[640,8192]{1,0:T(8,128)(2,1)S(1)}, u32[]{:S(2)}) copy-start(bf16[640,8192]{1,0:T(8,128)(2,1)S(1)} %get-tuple-element.12.feat_ref) | copy-start | bytes 31457284
  10.5 18.2 %all-to-all-start = ((bf16[4,8,6272]{2,1,0:T(8,128)(2,1)}), bf16[4,8,6272]{2,1,0:T(8,128)(2,1)S(1)}, u32[]{:S(2)}, u32[]{:S(2)}) async-start(bf16[4,8,6272]{2,1,0:T(8,128)(2,1)} %broadcast_in_dim.2), calls=%async_computation | async-start | bytes 802816 | tf_op jit(solution)/shard_map/all_to_all | solution.py:266
  16.8 1.9 %collective-permute-start.3 = (f32[8,32,512]{2,1,0:T(8,128)S(1)}, f32[8,32,512]{2,1,0:T(8,128)S(1)}, u32[]{:S(2)}, u32[]{:S(2)}) collective-permute-start(f32[8,32,512]{2,1,0:T(8,128)S(1)} %get-tuple-element.17), channel_id=1, source_target_pairs={{0,1},{1,0},{2,3},{3,2},{4,5},{5,4},{6,7},{7,6},{8,9},{9,8},{10,11... | collective-permute-start | bytes 1572872 | tf_op jit(solution)/shard_map/ppermute | solution.py:262
  28.7 12.2 %all-to-all-start.1 = ((s16[8,136,128]{2,1,0:T(8,128)(2,1)}), s16[8,136,128]{2,1,0:T(8,128)(2,1)S(1)}, u32[]{:S(2)}, u32[]{:S(2)}) async-start(s16[8,136,128]{2,1,0:T(8,128)(2,1)} %pair_sums.1), calls=%async_computation.1 | async-start | bytes 557056 | tf_op jit(solution)/shard_map/all_to_all | solution.py:266
  32.6 13.3 %collective-permute-start = (bf16[32,6272]{1,0:T(8,128)(2,1)S(1)}, bf16[32,6272]{1,0:T(8,128)(2,1)S(1)}, u32[]{:S(2)}, u32[]{:S(2)}) collective-permute-start(bf16[32,6272]{1,0:T(8,128)(2,1)S(1)} %bitcast.9), channel_id=1, source_target_pairs={{0,2},{1,3},{2,0},{3,1},{4,6},{5,7},{6,4},{7,5},{8,10},{9,11},{10,... | collective-permute-start | bytes 1204232 | tf_op jit(solution)/shard_map/ppermute | solution.py:262
  34.8 11.7 %collective-permute-start.1 = (bf16[32,6272]{1,0:T(8,128)(2,1)S(1)}, bf16[32,6272]{1,0:T(8,128)(2,1)S(1)}, u32[]{:S(2)}, u32[]{:S(2)}) collective-permute-start(bf16[32,6272]{1,0:T(8,128)(2,1)S(1)} %bitcast.10), channel_id=1, source_target_pairs={{0,1},{1,0},{2,3},{3,2},{4,5},{5,4},{6,7},{7,6},{8,9},{9,8},{10,11... | collective-permute-start | bytes 1204232 | tf_op jit(solution)/shard_map/ppermute | solution.py:262
  41.9 14.9 %all-to-all-start.2 = ((s16[8,136,128]{2,1,0:T(8,128)(2,1)}), s16[8,136,128]{2,1,0:T(8,128)(2,1)S(1)}, u32[]{:S(2)}, u32[]{:S(2)}) async-start(s16[8,136,128]{2,1,0:T(8,128)(2,1)} %total_sums.1), calls=%async_computation.2 | async-start | bytes 557056 | tf_op jit(solution)/shard_map/all_to_all | solution.py:266
  45.9 1.7 %collective-permute-start.2 = (bf16[32,6272]{1,0:T(8,128)(2,1)S(1)}, bf16[32,6272]{1,0:T(8,128)(2,1)S(1)}, u32[]{:S(2)}, u32[]{:S(2)}) collective-permute-start(bf16[32,6272]{1,0:T(8,128)(2,1)S(1)} %collective-permute-done.refs_1_), channel_id=1, source_target_pairs={{0,1},{1,0},{2,3},{3,2},{4,5},{5,4},{6,7},{7,6},{8,9},{9,8},{10,11... | collective-permute-start | bytes 1204232 | tf_op jit(solution)/shard_map/ppermute | solution.py:262
  47.7 4.0 %copy-start.1 = (bf16[640,8192]{1,0:T(8,128)(2,1)S(1)}, bf16[640,8192]{1,0:T(8,128)(2,1)}, u32[]{:S(2)}) copy-start(bf16[640,8192]{1,0:T(8,128)(2,1)} %copy-done) | copy-start | bytes 31457284
  56.0 0.7 %copy-start.3 = (f32[96,640]{1,0:T(8,128)}, f32[96,640]{1,0:T(8,128)S(1)}, u32[]{:S(2)}) copy-start(f32[96,640]{1,0:T(8,128)S(1)} %get-tuple-element.14.cross_ref) | copy-start | bytes 737284
  56.8 1.6 %collective-permute-start.4 = (s16[8,136,128]{2,1,0:T(8,128)(2,1)S(1)}, s16[8,136,128]{2,1,0:T(8,128)(2,1)S(1)}, u32[]{:S(2)}, u32[]{:S(2)}) collective-permute-start(s16[8,136,128]{2,1,0:T(8,128)(2,1)S(1)} %all-to-all-done.2.own_ref), channel_id=1, source_target_pairs={{0,1},{1,0},{2,3},{3,2},{4,5},{5,4},{6,7},{7,6},{8,9},{9,8},{10,11... | collective-permute-start | bytes 835592 | tf_op jit(solution)/shard_map/ppermute | solution.py:262
  58.3 4.0 %copy-start.2 = (bf16[640,8192]{1,0:T(8,128)(2,1)S(1)}, bf16[640,8192]{1,0:T(8,128)(2,1)}, u32[]{:S(2)}) copy-start(bf16[640,8192]{1,0:T(8,128)(2,1)} %copy-done) | copy-start | bytes 31457284
  62.3 0.9 %copy-start.4 = (f32[96,640]{1,0:T(8,128)S(1)}, f32[96,640]{1,0:T(8,128)}, u32[]{:S(2)}) copy-start(f32[96,640]{1,0:T(8,128)} %copy-done.3) | copy-start | bytes 737284
  63.3 0.7 copy-start.5

commit v4 on v3

v4 whole, which is shorter than its diff:
```python
import functools
import math

import jax
import jax.numpy as jnp
from jax import lax
from jax.experimental import pallas as pl
from jax.experimental.pallas import tpu as pltpu
from jax.sharding import PartitionSpec as P

ridge = 1.0
slots = 2
f32 = jnp.float32
bf16 = jnp.bfloat16


def nt_dot(a, b):
    return lax.dot_general(a, b, (((1,), (1,)), ((), ())), preferred_element_type=f32)


def column(tile, height, start=0):
    return jnp.concatenate([tile[:, start + q : start + q + 1] for q in range(height // 8)], axis=0)


def spread(values, start=0):
    lane = lax.broadcasted_iota(jnp.int32, (8, 128), 1)
    tile = jnp.zeros((8, 128), f32)
    for q in range(values.shape[0] // 8):
        tile = jnp.where(lane == start + q, values[8 * q : 8 * q + 8], tile)
    return tile


def encode(x, count_tile=None):
    height, width = x.shape
    top = jnp.max(jnp.abs(x), axis=1, keepdims=True)
    power = jnp.ceil(jnp.log2(jnp.maximum(top, 1e-30)) + 0.01)
    whole_x = jnp.round(x * jnp.exp2(15.0 - power))
    mark = spread(power)
    if count_tile is not None:
        mark = mark + count_tile
    chunks = [whole_x[:, j * 128 : (j + 1) * 128] for j in range(width // 128)]
    return jnp.concatenate(chunks + [mark], axis=0).astype(jnp.int32).astype(jnp.int16)


def decode(code, height):
    value = code.astype(jnp.int32).astype(f32)
    count = value.shape[0] // height
    mark = value[count * height :]
    x = jnp.concatenate([value[j * height : (j + 1) * height] for j in range(count)], axis=1)
    return x * jnp.exp2(column(mark, height) - 15.0), mark


def sums_kernel(
    labels_hbm, pick_hbm, feat_hbm, send_ref, keep_ref, rows_ref, labels_ref, pick_ref, feat_ref, left, held, sems, *, n_ex
):
    rows, full = feat_ref.shape
    steps, classes = pick_ref.shape
    width = full // n_ex
    groups = n_ex // 2
    device = lax.axis_index("ex")
    core = device % 2
    small = [
        pltpu.make_async_copy(pick_hbm, pick_ref, sems.at[n_ex]),
        pltpu.make_async_copy(labels_hbm, labels_ref, sems.at[n_ex + 1]),
    ]
    for copy in small:
        copy.start()
    columns = []
    copies = []
    for i in range(n_ex):
        block = (1 - core) * groups + i if i < groups else core * groups + i - groups
        at = pl.ds(pl.multiple_of(block * width, width), width)
        columns.append(at)
        copies.append(pltpu.make_async_copy(feat_hbm.at[:, at], feat_ref.at[:, at], sems.at[i]))
        copies[-1].start()

    for copy in small:
        copy.wait()
    local = pick_ref[...] - device * rows
    mine = (local >= 0) & (local < rows)
    lane = lax.broadcasted_iota(jnp.int32, local.shape, 1)
    first = jnp.min(jnp.where(mine, lane, classes), axis=1, keepdims=True)
    last = jnp.max(jnp.where(mine, lane, -1), axis=1, keepdims=True)
    spot0 = jnp.max(jnp.where(mine & (lane == first), local, -1), axis=1, keepdims=True)
    spot1 = jnp.max(jnp.where(mine & (lane == last) & (last > first), local, -1), axis=1, keepdims=True)
    member = lax.broadcasted_iota(jnp.int32, (classes, rows), 0) == labels_ref[...].reshape(1, rows)
    line = lax.broadcasted_iota(jnp.int32, (steps, rows), 1)
    left[...] = jnp.concatenate(
        [
            jnp.where(member, 1.0, 0.0),
            jnp.where(line == spot0, 1.0, 0.0),
            jnp.where(line == spot1, 1.0, 0.0),
            jnp.zeros((16 - 2 * steps, rows), f32),
        ],
        axis=0,
    ).astype(bf16)
    count = jnp.sum(jnp.where(member, 1.0, 0.0), axis=1, keepdims=True)
    tile = spread(count, classes // 8)
    for ref in (send_ref, keep_ref):
        ref[groups * classes :, :128] = tile
        if width > 128:
            ref[groups * classes :, 128:] = jnp.zeros((8, width - 128), f32)

    for i in range(n_ex):
        copies[i].wait()
        both = jnp.dot(left[...], feat_ref[:, columns[i]], preferred_element_type=f32)
        k = i % groups
        ref = send_ref if i < groups else keep_ref
        ref[k * classes : (k + 1) * classes, :] = both[:classes]
        held[:, columns[i]] = both[classes : classes + 8]

    used = steps * slots
    main = full * used // 8
    tail = full - main
    lines = [held[0:used, :main]]
    for q in range(slots):
        lines.append(jnp.concatenate([held[q * steps + u : q * steps + u + 1, main:] for u in range(steps)], axis=1))
    rows_ref[...] = jnp.concatenate(lines, axis=0).astype(bf16)


def pair_kernel(keep_ref, got_ref, code_ref, *, classes):
    groups = code_ref.shape[0]
    base = groups * classes
    tile = keep_ref[base : base + 8, :128] + got_ref[base : base + 8, :128]
    for k in range(groups):
        at = slice(k * classes, (k + 1) * classes)
        code_ref[k] = encode(keep_ref[at, :] + got_ref[at, :], tile)


def total_kernel(got_ref, code_ref, *, classes):
    value, mark = decode(got_ref[0], classes)
    for k in range(1, got_ref.shape[0]):
        more, more_mark = decode(got_ref[k], classes)
        value = value + more
        mark = mark + more_mark
    code = encode(value / jnp.sqrt(column(mark, classes, classes // 8)))
    for k in range(code_ref.shape[0]):
        code_ref[k] = code


def diagonal(block):
    n = block.shape[0]
    eye = lax.broadcasted_iota(jnp.int32, (n, n), 0) == lax.broadcasted_iota(jnp.int32, (n, n), 1)
    return jnp.sum(jnp.where(eye, block, 0.0), axis=1, keepdims=True)


def factor_all(gram):
    order = len(gram)
    factor = [[None] * order for _ in range(order)]
    for j in range(order):
        value = gram[j][j]
        for k in range(j):
            value = value - factor[j][k] * factor[j][k]
        root = jnp.sqrt(value)
        factor[j][j] = 1.0 / root
        for i in range(j + 1, order):
            value = gram[i][j]
            for k in range(j):
                value = value - factor[i][k] * factor[j][k]
            factor[i][j] = value * factor[j][j]
    return factor


def solve_all(factor, right):
    order = len(right)
    forward = []
    for i in range(order):
        value = right[i]
        for j in range(i):
            value = value - factor[i][j] * forward[j]
        forward.append(value * factor[i][i])
    result = []
    for size in range(1, order + 1):
        back = [None] * size
        for i in reversed(range(size)):
            value = forward[i]
            for j in range(i + 1, size):
                value = value - factor[j][i] * back[j]
            back[i] = value * factor[i][i]
        result.append(back)
    return result


def picked_kernel(pick_hbm, feat_hbm, *refs, n_ex):
    parts = refs[:-9]
    x_ref, cross_ref, factor_ref, pick_ref, rows_ref, feat_ref, feat_sems, part_sems, pick_sem = refs[-9:]
    rows, full = feat_ref.shape
    steps, classes = pick_ref.shape
    lines, main = rows_ref.shape
    tail = full - main
    width = full // n_ex
    device = lax.axis_index("ex")

    pick_copy = pltpu.make_async_copy(pick_hbm, pick_ref, pick_sem)
    pick_copy.start()
    part_copies = []
    at = 0
    for i, part in enumerate(parts):
        part_copies.append(pltpu.make_async_copy(part, rows_ref.at[at : at + part.shape[0]], part_sems.at[i]))
        part_copies[-1].start()
        at += part.shape[0]
    copies = []
    for i in range(n_ex):
        col = slice(i * width, (i + 1) * width)
        copies.append(pltpu.make_async_copy(feat_hbm.at[:, col], feat_ref.at[:, col], feat_sems.at[i]))
        copies[-1].start()

    pick_copy.wait()
    pick = pick_ref[...]
    lane = lax.broadcasted_iota(jnp.int32, pick.shape, 1)
    owner = jnp.zeros_like(pick)
    rank = jnp.zeros_like(pick)
    for d in range(n_ex):
        here = (pick >= d * rows) & (pick < (d + 1) * rows)
        first = jnp.min(jnp.where(here, lane, classes), axis=1, keepdims=True)
        owner = jnp.where(here, d, owner)
        rank = jnp.where(here & (lane > first), 1, rank)
    away = owner ^ device
    spot = jnp.zeros_like(pick)
    bits = n_ex.bit_length() - 1
    for b in range(1, bits):
        spot = spot + (((away >> b) & 1) << (bits - 1 - b))
    spot = spot + ((away & 1) << (bits - 1))
    step = lax.broadcasted_iota(jnp.int32, pick.shape, 0)
    index = spot * 8 + rank * steps + step
    home = spot * 8 + slots * steps + rank
    line = lax.broadcasted_iota(jnp.int32, (lines, classes), 0)

    def choose(where):
        hits = [jnp.where(line == where[s : s + 1, :], 1.0, 0.0) for s in range(steps)]
        pad = jnp.zeros((lines, 128 - steps * classes), f32)
        return jnp.transpose(jnp.concatenate(hits + [pad], axis=1))[: steps * classes].astype(bf16)

    one = choose(index)
    rest = choose(home)
    for copy in part_copies:
        copy.wait()
    x_ref[:, :main] = jnp.dot(one, rows_ref[...], preferred_element_type=f32).astype(bf16)
    for s in range(steps):
        at = slice(s * classes, (s + 1) * classes)
        x_ref[at, main:] = jnp.dot(rest[at], rows_ref[:, s * tail : (s + 1) * tail], preferred_element_type=f32).astype(bf16)

    x = x_ref[...]
    full_gram = nt_dot(x, x)
    gram = [
        [
            diagonal(full_gram[a * classes : (a + 1) * classes, b * classes : (b + 1) * classes])
            + (ridge if a == b else 0.0)
            for b in range(a + 1)
        ]
        for a in range(steps)
    ]
    factor = factor_all(gram)
    lane = lax.broadcasted_iota(jnp.int32, (classes, 128), 1)
    packed = jnp.zeros((classes, 128), f32)
    for i in range(steps):
        for j in range(i + 1):
            packed = jnp.where(lane == i * steps + j, factor[i][j], packed)
    factor_ref[...] = packed

    for i in range(n_ex):
        col = slice(i * width, (i + 1) * width)
        copies[i].wait()
        part = nt_dot(x_ref[:, col], feat_ref[:, col])
        cross_ref[...] = part if i == 0 else cross_ref[...] + part


def start_half(feat_hbm, feat_ref, sems, side, groups):
    half = feat_ref.shape[1]
    width = half // groups
    copies = []
    for k in range(groups):
        src = pl.ds(pl.multiple_of(side * half + k * width, width), width)
        dst = slice(k * width, (k + 1) * width)
        copies.append(pltpu.make_async_copy(feat_hbm.at[:, src], feat_ref.at[:, dst], sems.at[k]))
        copies[-1].start()
    return copies


def half_kernel(feat_hbm, code_ref, direct_ref, feat_ref, sems, *, classes):
    groups = code_ref.shape[0]
    width = feat_ref.shape[1] // groups
    copies = start_half(feat_hbm, feat_ref, sems, lax.axis_index("ex") % 2, groups)
    for k in range(groups):
        low = decode(code_ref[k], classes)[0].astype(bf16)
        copies[k].wait()
        part = nt_dot(low, feat_ref[:, k * width : (k + 1) * width])
        direct_ref[...] = part if k == 0 else direct_ref[...] + part


def pursuit_kernel(
    feat_hbm, labels_ref, x_ref, cross_ref, factor_ref, start_ref, own_ref, twin_ref,
    scores_ref, resid_ref, low_ref, feat_ref, sems, *, steps, scale
):
    classes, full = resid_ref.shape
    groups = own_ref.shape[0]
    half = full // 2
    width = half // groups
    core = lax.axis_index("ex") % 2
    copies = start_half(feat_hbm, feat_ref, sems, 1 - core, groups)
    direct = start_ref[...]
    for side, code_ref in ((core, own_ref), (1 - core, twin_ref)):
        for k in range(groups):
            at = pl.ds(pl.multiple_of(side * half + k * width, width), width)
            target = decode(code_ref[k], classes)[0]
            resid_ref[:, at] = target
            low = target.astype(bf16)
            low_ref[:, at] = low

    right = nt_dot(low_ref[...], x_ref[...])
    for k in range(groups):
        at = pl.ds(pl.multiple_of((1 - core) * half + k * width, width), width)
        copies[k].wait()
        direct = direct + nt_dot(low_ref[:, at], feat_ref[:, k * width : (k + 1) * width])

    rhs = [diagonal(right[:, a * classes : (a + 1) * classes]) for a in range(steps)]
    factor = [[factor_ref[:, i * steps + j : i * steps + j + 1] for j in range(i + 1)] for i in range(steps)]
    weights = solve_all(factor, rhs)
    member = lax.broadcasted_iota(jnp.int32, direct.shape, 0) == labels_ref[...].reshape(1, direct.shape[1])
    for s in range(steps):
        value = direct
        for k in range(s):
            value = value - weights[s - 1][k] * cross_ref[k * classes : (k + 1) * classes]
        scores_ref[s : s + 1, :] = jnp.sum(jnp.where(member, value, 0.0), axis=0, keepdims=True) * scale
    last = weights[steps - 1]
    value = resid_ref[...]
    for k in range(steps):
        value = value - last[k] * x_ref[k * classes : (k + 1) * classes].astype(f32)
    resid_ref[...] = value


def on_device(features, labels, pick_index, *, n_ex):
    rows, full = features.shape
    steps, classes = pick_index.shape
    groups = n_ex // 2
    width = full // n_ex
    total = steps * classes
    main = full * steps * slots // 8
    limit = pltpu.CompilerParams(vmem_limit_bytes=24 << 20)
    vmem = pl.BlockSpec(memory_space=pltpu.VMEM)
    hbm = pl.BlockSpec(memory_space=pltpu.HBM)
    anywhere = pl.BlockSpec(memory_space=pl.ANY)
    half = jax.ShapeDtypeStruct((groups * classes + 8, width), f32)
    codes = jax.ShapeDtypeStruct((groups, classes * (width // 128) + 8, 128), jnp.int16)
    features, picks, labels_in = [
        pltpu.with_memory_space_constraint(a, pltpu.HBM) for a in (features, pick_index, labels)
    ]

    def swap(x, mask):
        return lax.ppermute(x, "ex", [(d, d ^ mask) for d in range(n_ex)])

    def trade(x):
        teams = [[s + 2 * k for k in range(groups)] for s in range(2)]
        return lax.all_to_all(x, "ex", 0, 0, axis_index_groups=teams, tiled=True)

    send, keep, packed = pl.pallas_call(
        functools.partial(sums_kernel, n_ex=n_ex),
        in_specs=[hbm] * 3,
        out_specs=[vmem] * 3,
        out_shape=[half, half, jax.ShapeDtypeStruct((8, main), bf16)],
        scratch_shapes=[
            pltpu.VMEM(labels.shape, jnp.int32),
            pltpu.VMEM(pick_index.shape, jnp.int32),
            pltpu.VMEM((rows, full), bf16),
            pltpu.VMEM((classes + 16, rows), bf16),
            pltpu.VMEM((8, full), f32),
            pltpu.SemaphoreType.DMA((n_ex + 2,)),
        ],
        compiler_params=limit,
        name="class_sums",
    )(labels_in, picks, features)

    got = swap(send, 1)
    near = packed
    mask = n_ex // 2
    while mask > 4:
        near = jnp.concatenate([near, swap(near, mask)], axis=0)
        mask //= 2
    by_z = swap(near, 4)
    by_y = swap(near, 2)
    cut = near.shape[0] // 2
    last = jnp.concatenate([swap(by_y[:cut], 4), swap(by_z[cut:], 2)], axis=0)
    parts = [near, by_z, by_y, last]
    parts = parts + [swap(p, 1) for p in parts]

    codes_out = pl.pallas_call(
        functools.partial(pair_kernel, classes=classes),
        in_specs=[vmem] * 2,
        out_specs=vmem,
        out_shape=codes,
        compiler_params=limit,
        name="pair_sums",
    )(keep, got)
    own_half = trade(
        pl.pallas_call(
            functools.partial(total_kernel, classes=classes),
            in_specs=[vmem],
            out_specs=vmem,
            out_shape=codes,
            compiler_params=limit,
            name="total_sums",
        )(trade(codes_out))
    )
    twin_half = swap(own_half, 1)

    feat_half = pltpu.VMEM((rows, full // 2), bf16)
    direct = pl.pallas_call(
        functools.partial(half_kernel, classes=classes),
        in_specs=[hbm, vmem],
        out_specs=vmem,
        out_shape=jax.ShapeDtypeStruct((classes, rows), f32),
        scratch_shapes=[feat_half, pltpu.SemaphoreType.DMA((groups,))],
        compiler_params=limit,
        name="own_half_products",
    )(features, own_half)

    x, cross, factor = pl.pallas_call(
        functools.partial(picked_kernel, n_ex=n_ex),
        in_specs=[hbm, hbm] + [anywhere] * len(parts),
        out_specs=[vmem] * 3,
        out_shape=[
            jax.ShapeDtypeStruct((total, full), bf16),
            jax.ShapeDtypeStruct((total, rows), f32),
            jax.ShapeDtypeStruct((classes, 128), f32),
        ],
        scratch_shapes=[
            pltpu.VMEM(pick_index.shape, jnp.int32),
            pltpu.VMEM((n_ex * 8, main), bf16),
            pltpu.VMEM((rows, full), bf16),
            pltpu.SemaphoreType.DMA((n_ex,)),
            pltpu.SemaphoreType.DMA((len(parts),)),
            pltpu.SemaphoreType.DMA(()),
        ],
        compiler_params=limit,
        name="picked_products",
    )(picks, features, *parts)

    scores, resid = pl.pallas_call(
        functools.partial(pursuit_kernel, steps=steps, scale=1.0 / math.sqrt(full)),
        in_specs=[hbm] + [vmem] * 7,
        out_specs=[vmem] * 2,
        out_shape=[
            jax.ShapeDtypeStruct((steps, rows), f32),
            jax.ShapeDtypeStruct((classes, full), f32),
        ],
        scratch_shapes=[
            pltpu.VMEM((classes, full), bf16),
            feat_half,
            pltpu.SemaphoreType.DMA((groups,)),
        ],
        compiler_params=limit,
        name="pursuit",
    )(features, labels, x, cross, factor, direct, own_half, twin_half)
    return scores, resid


def solution(mesh):
    return jax.shard_map(
        functools.partial(on_device, n_ex=mesh.shape["ex"]),
        mesh=mesh,
        in_specs=(P(("grp", "ex"), None), P(("grp", "ex")), P("grp", None)),
        out_specs=(P(None, ("grp", "ex")), P("grp", None)),
        check_vma=False,
    )
```

time: 69.9 us -> 65.8 us (0.941)
  local copies, waits for them, and re-layouts: 17 us -> 0.05 us
  Pallas kernels: 16.7 us -> 26.4 us
  starting transfers between devices: 15.8 us -> 18.9 us
  waiting for transfers between devices: 18.2 us -> 19.4 us
  other arithmetic: 0.99 us -> 0 us
    unnamed x14 -> x4, local copies, waits for them, and re-layouts: 14.3 us -> 0.02 us
    ppermute x5 -> x11, starting transfers between devices: 2.3 us -> 11.4 us  [swap(): return lax.ppermute(x, 'ex', [(d, d ^ mask) for d in range(n_ex)])]
    pallas_call x2 -> x3, Pallas kernels: 5.28 us -> 14 us  [the longest x1 9.9 us: on_device(): pl.pallas_call(functools.partial(picked_kernel, n_ex=n_ex), in_specs=[hbm...]
    ppermute x5 -> x11, waiting for transfers between devices: 3.12 us -> 9.8 us  [swap(): return lax.ppermute(x, 'ex', [(d, d ^ mask) for d in range(n_ex)])]
    all_to_all x3 -> x2, starting transfers between devices: 13.5 us -> 7.46 us  [trade(): return lax.all_to_all(x, 'ex', 0, 0, axis_index_groups=teams, tiled=True)]
    all_to_all x3 -> x2, waiting for transfers between devices: 15 us -> 9.59 us  [trade(): return lax.all_to_all(x, 'ex', 0, 0, axis_index_groups=teams, tiled=True)]
    reshape x5 -> x0, local copies, waits for them, and re-layouts: 1.9 us -> none  [the longest x4 1.79 us: on_device(): p[:, main:].reshape(deep, 8, 128)]
    pallas_call x1, Pallas kernels: 5.39 us -> 6.34 us  [on_device(): pl.pallas_call(functools.partial(pursuit_kernel, steps=steps, scale=1.0 /...]
  transfers between devices with their start and end apart: 8 -> 13, of which waited for: 5 -> 5; matrix products, arithmetic and copies ran while one was open for 4% -> 0% of each run, Pallas kernels for 9% -> 23%
where the time goes in v4:
time: 65.8 us; the launch traced here: 65.4 us
  Pallas kernels  26.4 us (40%)
  waiting for transfers between devices  19.4 us (29%)
  starting transfers between devices  18.9 us (29%)
  between operations  0.73 us (1%)
    ppermute x11, starting transfers between devices, swap(): return lax.ppermute(x, 'ex', [(d, d ^ mask) for d in range(n_ex)])  11.4 us
    pallas_call x1, Pallas kernels, on_device(): pl.pallas_call(functools.partial(picked_kernel, n_ex=n_ex), in_specs=[hbm...  9.9 us
    ppermute x11, waiting for transfers between devices, swap(): return lax.ppermute(x, 'ex', [(d, d ^ mask) for d in range(n_ex)])  9.8 us
    all_to_all x2, waiting for transfers between devices, trade(): return lax.all_to_all(x, 'ex', 0, 0, axis_index_groups=teams, tiled=True)  9.59 us
    all_to_all x2, starting transfers between devices, trade(): return lax.all_to_all(x, 'ex', 0, 0, axis_index_groups=teams, tiled=True)  7.46 us
    pallas_call x1, Pallas kernels, on_device(): pl.pallas_call(functools.partial(pursuit_kernel, steps=steps, scale=1.0 /...  6.34 us
    pallas_call x1, Pallas kernels, on_device(): pl.pallas_call(functools.partial(sums_kernel, n_ex=n_ex), in_specs=[hbm]...  5.05 us
    pallas_call x1, Pallas kernels, on_device(): pl.pallas_call(functools.partial(half_kernel, classes=classes), in_specs=...  3.18 us
  transfers between devices with their start and end apart: 13, of which 5 were waited for; matrix products, arithmetic and copies ran while one was open for 0% of the time, Pallas kernels for 23%

profile of v4, /device:TPU:0, one launch (start us, length us, event | category | flops | bytes accessed | tf_op | source)
XLA Modules:
  0.0 65.4 jit_solution(4372148147175980318)
XLA Ops:
  0.6 5.0 %class_sums.1 = (f32[264,512]{1,0:T(8,128)S(1)}, f32[264,512]{1,0:T(8,128)S(1)}, bf16[8,6144]{1,0:T(8,128)(2,1)S(1)}) custom-call(s32[640]{0:T(1024)} %labels_ref.1, s32[3,32]{1,0:T(4,128)} %pick_hbm.3, bf16[640,8192]{1,0:T(8,128)(2,1)} %feat_hbm.7), custom_call_target="tpu_custom_call" | custom-call | tf_op jit(solution)/shard_map/class_sums/pallas_call | solution.py:356
  5.7 4.1 %collective-permute-start = (bf16[8,6144]{1,0:T(8,128)(2,1)S(1)}, bf16[8,6144]{1,0:T(8,128)(2,1)S(1)}, u32[]{:S(2)}, u32[]{:S(2)}) collective-permute-start(bf16[8,6144]{1,0:T(8,128)(2,1)S(1)} %get-tuple-element.8), channel_id=1, source_target_pairs={{0,8},{1,9},{2,10},{3,11},{4,12},{5,13},{6,14},{7,15},{8,0},{9,1},... | collective-permute-start | bytes 294920 | tf_op jit(solution)/shard_map/ppermute | solution.py:350
  9.8 0.0 collective-permute-start.9
  9.8 1.9 %collective-permute-done.9.got_ref = f32[264,512]{1,0:T(8,128)S(1)} collective-permute-done((f32[264,512]{1,0:T(8,128)S(1)}, f32[264,512]{1,0:T(8,128)S(1)}, u32[]{:S(2)}, u32[]{:S(2)}) %collective-permute-start.9) | collective-permute-done | bytes 540704 | tf_op jit(solution)/shard_map/ppermute | solution.py:350
  11.7 0.9 %pair_sums.1 = s16[8,136,128]{2,1,0:T(8,128)(2,1)} custom-call(f32[264,512]{1,0:T(8,128)S(1)} %get-tuple-element.12.keep_ref, f32[264,512]{1,0:T(8,128)S(1)} %collective-permute-done.9.got_ref), custom_call_target="tpu_custom_call" | custom-call | tf_op jit(solution)/shard_map/pair_sums/pallas_call | solution.py:386
  12.6 3.8 %all-to-all-start = ((s16[8,136,128]{2,1,0:T(8,128)(2,1)}), s16[8,136,128]{2,1,0:T(8,128)(2,1)S(1)}, u32[]{:S(2)}, u32[]{:S(2)}) async-start(s16[8,136,128]{2,1,0:T(8,128)(2,1)} %pair_sums.1), calls=%async_computation | async-start | bytes 557056 | tf_op jit(solution)/shard_map/all_to_all | solution.py:354
  16.4 0.0 collective-permute-done
  16.4 2.1 %collective-permute-start.2 = (bf16[16,6144]{1,0:T(8,128)(2,1)S(1)}, bf16[16,6144]{1,0:T(8,128)(2,1)S(1)}, u32[]{:S(2)}, u32[]{:S(2)}) collective-permute-start(bf16[16,6144]{1,0:T(8,128)(2,1)S(1)} %constant_dynamic-update-slice_fusion.refs_0_), channel_id=1, source_target_pairs={{0,2},{1,3},{2,0},{3,1},{4,6},{5,7},{6,4},{7,5},{8,10},{9,11},{10,... | collective-permute-start | bytes 589832 | tf_op jit(solution)/shard_map/ppermute | solution.py:350
  18.5 1.5 %collective-permute-start.1 = (bf16[16,6144]{1,0:T(8,128)(2,1)S(1)}, bf16[16,6144]{1,0:T(8,128)(2,1)S(1)}, u32[]{:S(2)}, u32[]{:S(2)}) collective-permute-start(bf16[16,6144]{1,0:T(8,128)(2,1)S(1)} %constant_dynamic-update-slice_fusion.refs_0_), channel_id=1, source_target_pairs={{0,4},{1,5},{2,6},{3,7},{4,0},{5,1},{6,2},{7,3},{8,12},{9,13},{10,... | collective-permute-start | bytes 589832 | tf_op jit(solution)/shard_map/ppermute | solution.py:350
  20.0 5.9 %collective-permute-done.2.refs_2_ = bf16[16,6144]{1,0:T(8,128)(2,1)S(1)} collective-permute-done((bf16[16,6144]{1,0:T(8,128)(2,1)S(1)}, bf16[16,6144]{1,0:T(8,128)(2,1)S(1)}, u32[]{:S(2)}, u32[]{:S(2)}) %collective-permute-start.2) | collective-permute-done | bytes 196640 | tf_op jit(solution)/shard_map/ppermute | solution.py:350
  25.9 1.9 %collective-permute-start.3 = (bf16[8,6144]{1,0:T(8,128)(2,1)S(1)}, bf16[8,6144]{1,0:T(8,128)(2,1)S(1)}, u32[]{:S(2)}, u32[]{:S(2)}) collective-permute-start(bf16[8,6144]{1,0:T(8,128)(2,1)S(1)} %slice.8), channel_id=1, source_target_pairs={{0,4},{1,5},{2,6},{3,7},{4,0},{5,1},{6,2},{7,3},{8,12},{9,13},{10,... | collective-permute-start | bytes 294920 | tf_op jit(solution)/shard_map/ppermute | solution.py:350
  27.8 0.0 collective-permute-start.5
  27.8 0.7 %collective-permute-done.1.refs_1_ = bf16[16,6144]{1,0:T(8,128)(2,1)S(1)} collective-permute-done((bf16[16,6144]{1,0:T(8,128)(2,1)S(1)}, bf16[16,6144]{1,0:T(8,128)(2,1)S(1)}, u32[]{:S(2)}, u32[]{:S(2)}) %collective-permute-start.1) | collective-permute-done | bytes 196640 | tf_op jit(solution)/shard_map/ppermute | solution.py:350
  28.6 0.8 %collective-permute-start.4 = (bf16[8,6144]{1,0:T(8,128)(2,1)S(1)}, bf16[8,6144]{1,0:T(8,128)(2,1)S(1)}, u32[]{:S(2)}, u32[]{:S(2)}) collective-permute-start(bf16[8,6144]{1,0:T(8,128)(2,1)S(1)} %slice.9), channel_id=1, source_target_pairs={{0,2},{1,3},{2,0},{3,1},{4,6},{5,7},{6,4},{7,5},{8,10},{9,11},{10,... | collective-permute-start | bytes 294920 | tf_op jit(solution)/shard_map/ppermute | solution.py:350
  29.4 0.0 collective-permute-start.7
  29.4 0.5 collective-permute-start.6
  29.9 0.0 all-to-all-done.got_ref
  29.9 1.0 %total_sums.1 = s16[8,136,128]{2,1,0:T(8,128)(2,1)} custom-call(s16[8,136,128]{2,1,0:T(8,128)(2,1)S(1)} %all-to-all-done.got_ref), custom_call_target="tpu_custom_call" | custom-call | tf_op jit(solution)/shard_map/total_sums/pallas_call | solution.py:395
  30.9 3.6 %all-to-all-start.1 = ((s16[8,136,128]{2,1,0:T(8,128)(2,1)}), s16[8,136,128]{2,1,0:T(8,128)(2,1)S(1)}, u32[]{:S(2)}, u32[]{:S(2)}) async-start(s16[8,136,128]{2,1,0:T(8,128)(2,1)} %total_sums.1), calls=%async_computation.1 | async-start | bytes 557056 | tf_op jit(solution)/shard_map/all_to_all | solution.py:354
  34.5 0.0 collective-permute-done.3
  34.6 9.6 %all-to-all-done.1.code_ref.own_ref = s16[8,136,128]{2,1,0:T(8,128)(2,1)S(1)} async-done(((s16[8,136,128]{2,1,0:T(8,128)(2,1)}), s16[8,136,128]{2,1,0:T(8,128)(2,1)S(1)}, u32[]{:S(2)}, u32[]{:S(2)}) %all-to-all-start.1) | async-done | bytes 278560 | tf_op jit(solution)/shard_map/all_to_all | solution.py:354
  44.1 0.0 collective-permute-start.10
  44.2 0.0 copy-start
  44.2 0.6 collective-permute-start.8
  44.7 0.0 collective-permute-done.5.refs_4_
  44.7 0.0 collective-permute-done.7.refs_6_
  44.8 0.0 collective-permute-done.6.refs_5_
  44.8 1.2 %collective-permute-done.8.refs_7_ = bf16[16,6144]{1,0:T(8,128)(2,1)S(1)} collective-permute-done((bf16[16,6144]{1,0:T(8,128)(2,1)S(1)}, bf16[16,6144]{1,0:T(8,128)(2,1)S(1)}, u32[]{:S(2)}, u32[]{:S(2)}) %collective-permute-start.8) | collective-permute-done | bytes 196640 | tf_op jit(solution)/shard_map/ppermute | solution.py:350
  46.0 9.9 %picked_products.1 = (bf16[96,8192]{1,0:T(8,128)(2,1)S(1)}, f32[96,640]{1,0:T(8,128)S(1)}, f32[32,128]{1,0:T(8,128)S(1)}) custom-call(s32[3,32]{1,0:T(4,128)} %pick_hbm.3, bf16[640,8192]{1,0:T(8,128)(2,1)} %feat_hbm.7, bf16[16,6144]{1,0:T(8,128)(2,1)S(1)} %constant_dynamic-update-slice_fusion.refs_0_, bf16[16,6144]{1,0:T(8,128)(2,1)S(1)} %collective-permute-done.1.refs_1_, ...), custom_call_target="tpu_custom_call" | custom-call | tf_op jit(solution)/shard_map/picked_products/pallas_call | solution.py:417
  55.9 3.2 %own_half_products.1.start_ref = f32[32,640]{1,0:T(8,128)S(1)} custom-call(bf16[640,8192]{1,0:T(8,128)(2,1)} %feat_hbm.7, s16[8,136,128]{2,1,0:T(8,128)(2,1)S(1)} %all-to-all-done.1.code_ref.own_ref), custom_call_target="tpu_custom_call" | custom-call | tf_op jit(solution)/shard_map/own_half_products/pallas_call | solution.py:407
  59.1 0.0 collective-permute-done.10.twin_ref
  59.1 6.3 %pursuit.1 = (f32[3,640]{1,0:T(4,128)}, f32[32,8192]{1,0:T(8,128)}) custom-call(bf16[640,8192]{1,0:T(8,128)(2,1)} %feat_hbm.7, s32[640]{0:T(1024)S(1)} %copy-done, bf16[96,8192]{1,0:T(8,128)(2,1)S(1)} %get-tuple-element.9.x_ref, f32[96,640]{1,0:T(8,128)S(1)} %get-tuple-element.10.cross_ref, f32[32,128]{1,0:T(8,128)S(1)} %get-tuple-element.11.factor_ref, ...), custom_call_target="tpu_custom_call" | custom-call | tf_op jit(solution)/shard_map/pursuit/pallas_call | solution.py:438
  (8 shorter events, 0.1 us)
Async XLA Ops:
  5.7 10.7 %collective-permute-start = (bf16[8,6144]{1,0:T(8,128)(2,1)S(1)}, bf16[8,6144]{1,0:T(8,128)(2,1)S(1)}, u32[]{:S(2)}, u32[]{:S(2)}) collective-permute-start(bf16[8,6144]{1,0:T(8,128)(2,1)S(1)} %get-tuple-element.8), channel_id=1, source_target_pairs={{0,8},{1,9},{2,10},{3,11},{4,12},{5,13},{6,14},{7,15},{8,0},{9,1},... | collective-permute-start | bytes 294920 | tf_op jit(solution)/shard_map/ppermute | solution.py:350
  9.8 1.9 %collective-permute-start.9 = (f32[264,512]{1,0:T(8,128)S(1)}, f32[264,512]{1,0:T(8,128)S(1)}, u32[]{:S(2)}, u32[]{:S(2)}) collective-permute-start(f32[264,512]{1,0:T(8,128)S(1)} %get-tuple-element.13), channel_id=1, source_target_pairs={{0,1},{1,0},{2,3},{3,2},{4,5},{5,4},{6,7},{7,6},{8,9},{9,8},{10,11... | collective-permute-start | bytes 1622024 | tf_op jit(solution)/shard_map/ppermute | solution.py:350
  12.6 17.2 %all-to-all-start = ((s16[8,136,128]{2,1,0:T(8,128)(2,1)}), s16[8,136,128]{2,1,0:T(8,128)(2,1)S(1)}, u32[]{:S(2)}, u32[]{:S(2)}) async-start(s16[8,136,128]{2,1,0:T(8,128)(2,1)} %pair_sums.1), calls=%async_computation | async-start | bytes 557056 | tf_op jit(solution)/shard_map/all_to_all | solution.py:354
  16.4 9.5 %collective-permute-start.2 = (bf16[16,6144]{1,0:T(8,128)(2,1)S(1)}, bf16[16,6144]{1,0:T(8,128)(2,1)S(1)}, u32[]{:S(2)}, u32[]{:S(2)}) collective-permute-start(bf16[16,6144]{1,0:T(8,128)(2,1)S(1)} %constant_dynamic-update-slice_fusion.refs_0_), channel_id=1, source_target_pairs={{0,2},{1,3},{2,0},{3,1},{4,6},{5,7},{6,4},{7,5},{8,10},{9,11},{10,... | collective-permute-start | bytes 589832 | tf_op jit(solution)/shard_map/ppermute | solution.py:350
  18.5 10.0 %collective-permute-start.1 = (bf16[16,6144]{1,0:T(8,128)(2,1)S(1)}, bf16[16,6144]{1,0:T(8,128)(2,1)S(1)}, u32[]{:S(2)}, u32[]{:S(2)}) collective-permute-start(bf16[16,6144]{1,0:T(8,128)(2,1)S(1)} %constant_dynamic-update-slice_fusion.refs_0_), channel_id=1, source_target_pairs={{0,4},{1,5},{2,6},{3,7},{4,0},{5,1},{6,2},{7,3},{8,12},{9,13},{10,... | collective-permute-start | bytes 589832 | tf_op jit(solution)/shard_map/ppermute | solution.py:350
  25.9 8.6 %collective-permute-start.3 = (bf16[8,6144]{1,0:T(8,128)(2,1)S(1)}, bf16[8,6144]{1,0:T(8,128)(2,1)S(1)}, u32[]{:S(2)}, u32[]{:S(2)}) collective-permute-start(bf16[8,6144]{1,0:T(8,128)(2,1)S(1)} %slice.8), channel_id=1, source_target_pairs={{0,4},{1,5},{2,6},{3,7},{4,0},{5,1},{6,2},{7,3},{8,12},{9,13},{10,... | collective-permute-start | bytes 294920 | tf_op jit(solution)/shard_map/ppermute | solution.py:350
  27.8 16.9 %collective-permute-start.5 = (bf16[16,6144]{1,0:T(8,128)(2,1)S(1)}, bf16[16,6144]{1,0:T(8,128)(2,1)S(1)}, u32[]{:S(2)}, u32[]{:S(2)}) collective-permute-start(bf16[16,6144]{1,0:T(8,128)(2,1)S(1)} %constant_dynamic-update-slice_fusion.refs_0_), channel_id=1, source_target_pairs={{0,1},{1,0},{2,3},{3,2},{4,5},{5,4},{6,7},{7,6},{8,9},{9,8},{10,11... | collective-permute-start | bytes 589832 | tf_op jit(solution)/shard_map/ppermute | solution.py:350
  28.6 15.6 %collective-permute-start.4 = (bf16[8,6144]{1,0:T(8,128)(2,1)S(1)}, bf16[8,6144]{1,0:T(8,128)(2,1)S(1)}, u32[]{:S(2)}, u32[]{:S(2)}) collective-permute-start(bf16[8,6144]{1,0:T(8,128)(2,1)S(1)} %slice.9), channel_id=1, source_target_pairs={{0,2},{1,3},{2,0},{3,1},{4,6},{5,7},{6,4},{7,5},{8,10},{9,11},{10,... | collective-permute-start | bytes 294920 | tf_op jit(solution)/shard_map/ppermute | solution.py:350
  29.4 15.4 %collective-permute-start.7 = (bf16[16,6144]{1,0:T(8,128)(2,1)S(1)}, bf16[16,6144]{1,0:T(8,128)(2,1)S(1)}, u32[]{:S(2)}, u32[]{:S(2)}) collective-permute-start(bf16[16,6144]{1,0:T(8,128)(2,1)S(1)} %collective-permute-done.2.refs_2_), channel_id=1, source_target_pairs={{0,1},{1,0},{2,3},{3,2},{4,5},{5,4},{6,7},{7,6},{8,9},{9,8},{10,11... | collective-permute-start | bytes 589832 | tf_op jit(solution)/shard_map/ppermute | solution.py:350
  29.4 15.4 %collective-permute-start.6 = (bf16[16,6144]{1,0:T(8,128)(2,1)S(1)}, bf16[16,6144]{1,0:T(8,128)(2,1)S(1)}, u32[]{:S(2)}, u32[]{:S(2)}) collective-permute-start(bf16[16,6144]{1,0:T(8,128)(2,1)S(1)} %collective-permute-done.1.refs_1_), channel_id=1, source_target_pairs={{0,1},{1,0},{2,3},{3,2},{4,5},{5,4},{6,7},{7,6},{8,9},{9,8},{10,11... | collective-permute-start | bytes 589832 | tf_op jit(solution)/shard_map/ppermute | solution.py:350
  30.9 13.3 %all-to-all-start.1 = ((s16[8,136,128]{2,1,0:T(8,128)(2,1)}), s16[8,136,128]{2,1,0:T(8,128)(2,1)S(1)}, u32[]{:S(2)}, u32[]{:S(2)}) async-start(s16[8,136,128]{2,1,0:T(8,128)(2,1)} %total_sums.1), calls=%async_computation.1 | async-start | bytes 557056 | tf_op jit(solution)/shard_map/all_to_all | solution.py:354
  44.1 14.9 %collective-permute-start.10 = (s16[8,136,128]{2,1,0:T(8,128)(2,1)S(1)}, s16[8,136,128]{2,1,0:T(8,128)(2,1)S(1)}, u32[]{:S(2)}, u32[]{:S(2)}) collective-permute-start(s16[8,136,128]{2,1,0:T(8,128)(2,1)S(1)} %all-to-all-done.1.code_ref.own_ref), channel_id=1, source_target_pairs={{0,1},{1,0},{2,3},{3,2},{4,5},{5,4},{6,7},{7,6},{8,9},{9,8},{10,11... | collective-permute-start | bytes 835592 | tf_op jit(solution)/shard_map/ppermute | solution.py:350
  44.2 14.9 %copy-start = (s32[640]{0:T(1024)S(1)}, s32[640]{0:T(1024)}, u32[]{:S(2)}) copy-start(s32[640]{0:T(1024)} %labels_ref.1) | copy-start | bytes 7684
  44.2 1.8 %collective-permute-start.8 = (bf16[16,6144]{1,0:T(8,128)(2,1)S(1)}, bf16[16,6144]{1,0:T(8,128)(2,1)S(1)}, u32[]{:S(2)}, u32[]{:S(2)}) collective-permute-start(bf16[16,6144]{1,0:T(8,128)(2,1)S(1)} %constant_dynamic-update-slice_fusion.2.refs_3_), channel_id=1, source_target_pairs={{0,1},{1,0},{2,3},{3,2},{4,5},{5,4},{6,7},{7,6},{8,9},{9,8},{10,11... | collective-permute-start | bytes 589832 | tf_op jit(solution)/shard_map/ppermute | solution.py:350

commit v5 on v4

--- a/solution.py
+++ b/solution.py
@@ -204,6 +204,7 @@
         col = slice(i * width, (i + 1) * width)
         copies.append(pltpu.make_async_copy(feat_hbm.at[:, col], feat_ref.at[:, col], feat_sems.at[i]))
         copies[-1].start()
+    span = full // 4
 
     pick_copy.wait()
     pick = pick_ref[...]
@@ -258,75 +259,80 @@
             packed = jnp.where(lane == i * steps + j, factor[i][j], packed)
     factor_ref[...] = packed
 
-    for i in range(n_ex):
-        col = slice(i * width, (i + 1) * width)
-        copies[i].wait()
-        part = nt_dot(x_ref[:, col], feat_ref[:, col])
+    for i in range(4):
+        for copy in copies[i * n_ex // 4 : (i + 1) * n_ex // 4]:
+            copy.wait()
+        col = slice(i * span, (i + 1) * span)
+        part = nt_dot(x_ref[: cross_ref.shape[0], col], feat_ref[:, col])
         cross_ref[...] = part if i == 0 else cross_ref[...] + part
 
 
-def start_half(feat_hbm, feat_ref, sems, side, groups):
+def half_kernel(feat_hbm, code_ref, x_ref, direct_ref, right_ref, target_ref, other_ref, low_ref, feat_ref, sems, *, classes):
+    groups = code_ref.shape[0]
     half = feat_ref.shape[1]
     width = half // groups
+    core = lax.axis_index("ex") % 2
     copies = []
+    for side, ref in ((core, feat_ref), (1 - core, other_ref)):
+        for k in range(groups):
+            src = pl.ds(pl.multiple_of(side * half + k * width, width), width)
+            dst = slice(k * width, (k + 1) * width)
+            copies.append(pltpu.make_async_copy(feat_hbm.at[:, src], ref.at[:, dst], sems.at[len(copies)]))
+            copies[-1].start()
     for k in range(groups):
-        src = pl.ds(pl.multiple_of(side * half + k * width, width), width)
-        dst = slice(k * width, (k + 1) * width)
-        copies.append(pltpu.make_async_copy(feat_hbm.at[:, src], feat_ref.at[:, dst], sems.at[k]))
-        copies[-1].start()
-    return copies
-
-
-def half_kernel(feat_hbm, code_ref, direct_ref, feat_ref, sems, *, classes):
-    groups = code_ref.shape[0]
-    width = feat_ref.shape[1] // groups
-    copies = start_half(feat_hbm, feat_ref, sems, lax.axis_index("ex") % 2, groups)
-    for k in range(groups):
-        low = decode(code_ref[k], classes)[0].astype(bf16)
-        copies[k].wait()
-        part = nt_dot(low, feat_ref[:, k * width : (k + 1) * width])
-        direct_ref[...] = part if k == 0 else direct_ref[...] + part
+        target = decode(code_ref[k], classes)[0]
+        target_ref[:, k * width : (k + 1) * width] = target
+        low_ref[:, k * width : (k + 1) * width] = target.astype(bf16)
+    right_ref[...] = nt_dot(low_ref[...], x_ref[:, pl.ds(pl.multiple_of(core * half, half), half)])
+    for copy in copies[:groups]:
+        copy.wait()
+    direct_ref[...] = nt_dot(low_ref[...], feat_ref[...])
+    for copy in copies[groups:]:
+        copy.wait()
 
 
 def pursuit_kernel(
-    feat_hbm, labels_ref, x_ref, cross_ref, factor_ref, start_ref, own_ref, twin_ref,
-    scores_ref, resid_ref, low_ref, feat_ref, sems, *, steps, scale
+    labels_ref, x_ref, cross_ref, factor_ref, direct_own, right_own, target_own, feat_ref, code_ref,
+    scores_ref, resid_hbm, resid_ref, low_ref, sems, *, steps, scale
 ):
     classes, full = resid_ref.shape
-    groups = own_ref.shape[0]
+    groups = code_ref.shape[0]
     half = full // 2
     width = half // groups
     core = lax.axis_index("ex") % 2
-    copies = start_half(feat_hbm, feat_ref, sems, 1 - core, groups)
-    direct = start_ref[...]
-    for side, code_ref in ((core, own_ref), (1 - core, twin_ref)):
-        for k in range(groups):
-            at = pl.ds(pl.multiple_of(side * half + k * width, width), width)
-            target = decode(code_ref[k], classes)[0]
-            resid_ref[:, at] = target
-            low = target.astype(bf16)
-            low_ref[:, at] = low
-
-    right = nt_dot(low_ref[...], x_ref[...])
+    mine = pl.ds(pl.multiple_of(core * half, half), half)
+    rest = pl.ds(pl.multiple_of((1 - core) * half, half), half)
     for k in range(groups):
         at = pl.ds(pl.multiple_of((1 - core) * half + k * width, width), width)
-        copies[k].wait()
-        direct = direct + nt_dot(low_ref[:, at], feat_ref[:, k * width : (k + 1) * width])
-
+        target = decode(code_ref[k], classes)[0]
+        resid_ref[:, at] = target
+        low_ref[:, k * width : (k + 1) * width] = target.astype(bf16)
+    right = right_own[...] + nt_dot(low_ref[...], x_ref[:, rest])
     rhs = [diagonal(right[:, a * classes : (a + 1) * classes]) for a in range(steps)]
     factor = [[factor_ref[:, i * steps + j : i * steps + j + 1] for j in range(i + 1)] for i in range(steps)]
     weights = solve_all(factor, rhs)
+    last = weights[steps - 1]
+    copies = []
+    for source, side, at in ((target_own, core, mine), (resid_ref, 1 - core, rest)):
+        for q in range(2):
+            span = half // 2
+            here = pl.ds(pl.multiple_of(side * half + q * span, span), span)
+            value = source[:, q * span : (q + 1) * span] if source is target_own else source[:, here]
+            for k in range(steps):
+                value = value - last[k] * x_ref[k * classes : (k + 1) * classes, here].astype(f32)
+            resid_ref[:, here] = value
+            copies.append(pltpu.make_async_copy(resid_ref.at[:, here], resid_hbm.at[:, here], sems.at[len(copies)]))
+            copies[-1].start()
+
+    direct = direct_own[...] + nt_dot(low_ref[...], feat_ref[...])
     member = lax.broadcasted_iota(jnp.int32, direct.shape, 0) == labels_ref[...].reshape(1, direct.shape[1])
     for s in range(steps):
         value = direct
         for k in range(s):
             value = value - weights[s - 1][k] * cross_ref[k * classes : (k + 1) * classes]
         scores_ref[s : s + 1, :] = jnp.sum(jnp.where(member, value, 0.0), axis=0, keepdims=True) * scale
-    last = weights[steps - 1]
-    value = resid_ref[...]
-    for k in range(steps):
-        value = value - last[k] * x_ref[k * classes : (k + 1) * classes].astype(f32)
-    resid_ref[...] = value
+    for copy in copies:
+        copy.wait()
 
 
 def on_device(features, labels, pick_index, *, n_ex):
@@ -376,12 +382,7 @@
     while mask > 4:
         near = jnp.concatenate([near, swap(near, mask)], axis=0)
         mask //= 2
-    by_z = swap(near, 4)
-    by_y = swap(near, 2)
-    cut = near.shape[0] // 2
-    last = jnp.concatenate([swap(by_y[:cut], 4), swap(by_z[cut:], 2)], axis=0)
-    parts = [near, by_z, by_y, last]
-    parts = parts + [swap(p, 1) for p in parts]
+    parts = [near, swap(near, 4), swap(near, 2), swap(near, 6)]
 
     codes_out = pl.pallas_call(
         functools.partial(pair_kernel, classes=classes),
@@ -391,28 +392,17 @@
         compiler_params=limit,
         name="pair_sums",
     )(keep, got)
-    own_half = trade(
-        pl.pallas_call(
-            functools.partial(total_kernel, classes=classes),
-            in_specs=[vmem],
-            out_specs=vmem,
-            out_shape=codes,
-            compiler_params=limit,
-            name="total_sums",
-        )(trade(codes_out))
-    )
-    twin_half = swap(own_half, 1)
-
-    feat_half = pltpu.VMEM((rows, full // 2), bf16)
-    direct = pl.pallas_call(
-        functools.partial(half_kernel, classes=classes),
-        in_specs=[hbm, vmem],
+    summed = pl.pallas_call(
+        functools.partial(total_kernel, classes=classes),
+        in_specs=[vmem],
         out_specs=vmem,
-        out_shape=jax.ShapeDtypeStruct((classes, rows), f32),
-        scratch_shapes=[feat_half, pltpu.SemaphoreType.DMA((groups,))],
-        compiler_params=limit,
-        name="own_half_products",
-    )(features, own_half)
+        out_shape=codes,
+        compiler_params=limit,
+        name="total_sums",
+    )(trade(codes_out))
+    parts, summed = lax.optimization_barrier((parts, summed))
+    parts = parts + [swap(p, 1) for p in parts]
+    own_half = trade(summed)
 
     x, cross, factor = pl.pallas_call(
         functools.partial(picked_kernel, n_ex=n_ex),
@@ -420,7 +410,7 @@
         out_specs=[vmem] * 3,
         out_shape=[
             jax.ShapeDtypeStruct((total, full), bf16),
-            jax.ShapeDtypeStruct((total, rows), f32),
+            jax.ShapeDtypeStruct((total - classes, rows), f32),
             jax.ShapeDtypeStruct((classes, 128), f32),
         ],
         scratch_shapes=[
@@ -435,22 +425,44 @@
         name="picked_products",
     )(picks, features, *parts)
 
+    own_half, x = lax.optimization_barrier((own_half, x))
+    twin_half = swap(own_half, 1)
+    feat_half = pltpu.VMEM((rows, full // 2), bf16)
+    direct, right, target, feat_rest = pl.pallas_call(
+        functools.partial(half_kernel, classes=classes),
+        in_specs=[hbm, vmem, vmem],
+        out_specs=[vmem] * 4,
+        out_shape=[
+            jax.ShapeDtypeStruct((classes, rows), f32),
+            jax.ShapeDtypeStruct((classes, total), f32),
+            jax.ShapeDtypeStruct((classes, full // 2), f32),
+            feat_half,
+        ],
+        scratch_shapes=[
+            pltpu.VMEM((classes, full // 2), bf16),
+            feat_half,
+            pltpu.SemaphoreType.DMA((n_ex,)),
+        ],
+        compiler_params=limit,
+        name="own_half_products",
+    )(features, own_half, x)
+
     scores, resid = pl.pallas_call(
         functools.partial(pursuit_kernel, steps=steps, scale=1.0 / math.sqrt(full)),
-        in_specs=[hbm] + [vmem] * 7,
-        out_specs=[vmem] * 2,
+        in_specs=[vmem] * 9,
+        out_specs=[vmem, anywhere],
         out_shape=[
             jax.ShapeDtypeStruct((steps, rows), f32),
             jax.ShapeDtypeStruct((classes, full), f32),
         ],
         scratch_shapes=[
-            pltpu.VMEM((classes, full), bf16),
-            feat_half,
-            pltpu.SemaphoreType.DMA((groups,)),
+            pltpu.VMEM((classes, full), f32),
+            pltpu.VMEM((classes, full // 2), bf16),
+            pltpu.SemaphoreType.DMA((4,)),
         ],
         compiler_params=limit,
         name="pursuit",
-    )(features, labels, x, cross, factor, direct, own_half, twin_half)
+    )(labels, x, cross, factor, direct, right, target, feat_rest, twin_half)
     return scores, resid
 
 

time: 65.8 us -> 57.4 us (0.87)
  waiting for transfers between devices: 19.4 us -> 14.4 us
  starting transfers between devices: 18.9 us -> 17.1 us
  Pallas kernels: 26.4 us -> 24.9 us
    all_to_all x2, waiting for transfers between devices: 9.59 us -> 6.59 us  [trade(): return lax.all_to_all(x, 'ex', 0, 0, axis_index_groups=teams, tiled=True)]
    pallas_call x1, Pallas kernels: 6.34 us -> 3.79 us  [on_device(): pl.pallas_call(functools.partial(pursuit_kernel, steps=steps, scale=1.0 /...]
    ppermute x11 -> x10, starting transfers between devices: 11.4 us -> 9.05 us  [swap(): return lax.ppermute(x, 'ex', [(d, d ^ mask) for d in range(n_ex)])]
    ppermute x11 -> x10, waiting for transfers between devices: 9.8 us -> 7.8 us  [swap(): return lax.ppermute(x, 'ex', [(d, d ^ mask) for d in range(n_ex)])]
    pallas_call x1, Pallas kernels: 3.18 us -> 4.97 us  [on_device(): pl.pallas_call(functools.partial(half_kernel, classes=classes), in_specs=...]
    pallas_call x1, Pallas kernels: 9.9 us -> 9.15 us  [on_device(): pl.pallas_call(functools.partial(picked_kernel, n_ex=n_ex), in_specs=[hbm...]
  transfers between devices with their start and end apart: 13 -> 12, of which waited for: 5 -> 9; matrix products, arithmetic and copies ran while one was open for 0% -> 0% of each run, Pallas kernels for 23% -> 28%
where the time goes in v5:
time: 57.4 us; the launch traced here: 57.1 us
  Pallas kernels  24.9 us (43%)
  starting transfers between devices  17.1 us (30%)
  waiting for transfers between devices  14.4 us (25%)
  between operations  0.72 us (1%)
    pallas_call x1, Pallas kernels, on_device(): pl.pallas_call(functools.partial(picked_kernel, n_ex=n_ex), in_specs=[hbm...  9.15 us
    ppermute x10, starting transfers between devices, swap(): return lax.ppermute(x, 'ex', [(d, d ^ mask) for d in range(n_ex)])  9.05 us
    all_to_all x2, starting transfers between devices, trade(): return lax.all_to_all(x, 'ex', 0, 0, axis_index_groups=teams, tiled=True)  8.04 us
    ppermute x10, waiting for transfers between devices, swap(): return lax.ppermute(x, 'ex', [(d, d ^ mask) for d in range(n_ex)])  7.8 us
    all_to_all x2, waiting for transfers between devices, trade(): return lax.all_to_all(x, 'ex', 0, 0, axis_index_groups=teams, tiled=True)  6.59 us
    pallas_call x1, Pallas kernels, on_device(): pl.pallas_call(functools.partial(sums_kernel, n_ex=n_ex), in_specs=[hbm]...  5.05 us
    pallas_call x1, Pallas kernels, on_device(): pl.pallas_call(functools.partial(half_kernel, classes=classes), in_specs=...  4.97 us
    pallas_call x1, Pallas kernels, on_device(): pl.pallas_call(functools.partial(pursuit_kernel, steps=steps, scale=1.0 /...  3.79 us
  transfers between devices with their start and end apart: 12, of which 9 were waited for; matrix products, arithmetic and copies ran while one was open for 0% of the time, Pallas kernels for 28%

profile of v5, /device:TPU:0, one launch (start us, length us, event | category | flops | bytes accessed | tf_op | source)
XLA Modules:
  0.0 57.1 jit_solution(5141115302622589872)
XLA Ops:
  0.6 5.0 %class_sums.1 = (f32[264,512]{1,0:T(8,128)S(1)}, f32[264,512]{1,0:T(8,128)S(1)}, bf16[8,6144]{1,0:T(8,128)(2,1)S(1)}) custom-call(s32[640]{0:T(1024)} %labels_ref.1, s32[3,32]{1,0:T(4,128)} %pick_hbm.3, bf16[640,8192]{1,0:T(8,128)(2,1)} %feat_hbm.5), custom_call_target="tpu_custom_call" | custom-call | tf_op jit(solution)/shard_map/class_sums/pallas_call | solution.py:362
  5.7 4.1 %collective-permute-start = (bf16[8,6144]{1,0:T(8,128)(2,1)S(1)}, bf16[8,6144]{1,0:T(8,128)(2,1)S(1)}, u32[]{:S(2)}, u32[]{:S(2)}) collective-permute-start(bf16[8,6144]{1,0:T(8,128)(2,1)S(1)} %get-tuple-element.19), channel_id=1, source_target_pairs={{0,8},{1,9},{2,10},{3,11},{4,12},{5,13},{6,14},{7,15},{8,0},{9,1},... | collective-permute-start | bytes 294920 | tf_op jit(solution)/shard_map/ppermute | solution.py:356
  9.8 0.0 collective-permute-start.4
  9.8 1.9 %collective-permute-done.4.got_ref = f32[264,512]{1,0:T(8,128)S(1)} collective-permute-done((f32[264,512]{1,0:T(8,128)S(1)}, f32[264,512]{1,0:T(8,128)S(1)}, u32[]{:S(2)}, u32[]{:S(2)}) %collective-permute-start.4) | collective-permute-done | bytes 540704 | tf_op jit(solution)/shard_map/ppermute | solution.py:356
  11.7 0.9 %pair_sums.1 = s16[8,136,128]{2,1,0:T(8,128)(2,1)} custom-call(f32[264,512]{1,0:T(8,128)S(1)} %get-tuple-element.20.keep_ref, f32[264,512]{1,0:T(8,128)S(1)} %collective-permute-done.4.got_ref), custom_call_target="tpu_custom_call" | custom-call | tf_op jit(solution)/shard_map/pair_sums/pallas_call | solution.py:387
  12.6 3.8 %all-to-all-start = ((s16[8,136,128]{2,1,0:T(8,128)(2,1)}), s16[8,136,128]{2,1,0:T(8,128)(2,1)S(1)}, u32[]{:S(2)}, u32[]{:S(2)}) async-start(s16[8,136,128]{2,1,0:T(8,128)(2,1)} %pair_sums.1), calls=%async_computation | async-start | bytes 557056 | tf_op jit(solution)/shard_map/all_to_all | solution.py:360
  16.4 0.0 collective-permute-done
  16.4 3.0 %collective-permute-start.3 = (bf16[16,6144]{1,0:T(8,128)(2,1)S(1)}, bf16[16,6144]{1,0:T(8,128)(2,1)S(1)}, u32[]{:S(2)}, u32[]{:S(2)}) collective-permute-start(bf16[16,6144]{1,0:T(8,128)(2,1)S(1)} %constant_dynamic-update-slice_fusion.refs_0_), channel_id=1, source_target_pairs={{0,6},{1,7},{2,4},{3,5},{4,2},{5,3},{6,0},{7,1},{8,14},{9,15},{10,... | collective-permute-start | bytes 589832 | tf_op jit(solution)/shard_map/ppermute | solution.py:356
  19.4 0.6 collective-permute-start.2
  20.0 0.1 collective-permute-start.1
  20.1 6.6 %all-to-all-done.got_ref = s16[8,136,128]{2,1,0:T(8,128)(2,1)S(1)} async-done(((s16[8,136,128]{2,1,0:T(8,128)(2,1)}), s16[8,136,128]{2,1,0:T(8,128)(2,1)S(1)}, u32[]{:S(2)}, u32[]{:S(2)}) %all-to-all-start) | async-done | bytes 278560 | tf_op jit(solution)/shard_map/all_to_all | solution.py:360
  26.7 1.0 %total_sums.1 = s16[8,136,128]{2,1,0:T(8,128)(2,1)} custom-call(s16[8,136,128]{2,1,0:T(8,128)(2,1)S(1)} %all-to-all-done.got_ref), custom_call_target="tpu_custom_call" | custom-call | tf_op jit(solution)/shard_map/total_sums/pallas_call | solution.py:395
  27.7 2.0 %collective-permute-done.3.refs_3_ = bf16[16,6144]{1,0:T(8,128)(2,1)S(1)} collective-permute-done((bf16[16,6144]{1,0:T(8,128)(2,1)S(1)}, bf16[16,6144]{1,0:T(8,128)(2,1)S(1)}, u32[]{:S(2)}, u32[]{:S(2)}) %collective-permute-start.3) | collective-permute-done | bytes 196640 | tf_op jit(solution)/shard_map/ppermute | solution.py:356
  29.7 1.5 %collective-permute-done.2.refs_2_ = bf16[16,6144]{1,0:T(8,128)(2,1)S(1)} collective-permute-done((bf16[16,6144]{1,0:T(8,128)(2,1)S(1)}, bf16[16,6144]{1,0:T(8,128)(2,1)S(1)}, u32[]{:S(2)}, u32[]{:S(2)}) %collective-permute-start.2) | collective-permute-done | bytes 196640 | tf_op jit(solution)/shard_map/ppermute | solution.py:356
  31.2 1.1 %collective-permute-done.1.refs_1_ = bf16[16,6144]{1,0:T(8,128)(2,1)S(1)} collective-permute-done((bf16[16,6144]{1,0:T(8,128)(2,1)S(1)}, bf16[16,6144]{1,0:T(8,128)(2,1)S(1)}, u32[]{:S(2)}, u32[]{:S(2)}) %collective-permute-start.1) | collective-permute-done | bytes 196640 | tf_op jit(solution)/shard_map/ppermute | solution.py:356
  32.3 4.2 %all-to-all-start.1 = ((s16[8,136,128]{2,1,0:T(8,128)(2,1)}), s16[8,136,128]{2,1,0:T(8,128)(2,1)S(1)}, u32[]{:S(2)}, u32[]{:S(2)}) async-start(s16[8,136,128]{2,1,0:T(8,128)(2,1)} %total_sums.1), calls=%async_computation.1 | async-start | bytes 557056 | tf_op jit(solution)/shard_map/all_to_all | solution.py:360
  36.5 0.0 collective-permute-start.5
  36.5 0.5 collective-permute-start.6
  37.0 0.1 collective-permute-start.7
  37.1 0.4 collective-permute-start.8
  37.5 0.4 collective-permute-done.5.refs_4_
  38.0 0.3 collective-permute-done.6.refs_5_
  38.2 0.3 collective-permute-done.7.refs_6_
  38.5 0.3 collective-permute-done.8.refs_7_
  38.8 9.1 %picked_products.1 = (bf16[96,8192]{1,0:T(8,128)(2,1)S(1)}, f32[64,640]{1,0:T(8,128)S(1)}, f32[32,128]{1,0:T(8,128)S(1)}) custom-call(s32[3,32]{1,0:T(4,128)} %pick_hbm.3, bf16[640,8192]{1,0:T(8,128)(2,1)} %feat_hbm.5, bf16[16,6144]{1,0:T(8,128)(2,1)S(1)} %constant_dynamic-update-slice_fusion.refs_0_, bf16[16,6144]{1,0:T(8,128)(2,1)S(1)} %collective-permute-done.1.refs_1_, ...), custom_call_target="tpu_custom_call" | custom-call | tf_op jit(solution)/shard_map/picked_products/pallas_call | solution.py:407
  48.0 0.0 all-to-all-done.1.code_ref
  48.0 0.0 copy-start
  48.0 0.3 collective-permute-start.9
  48.3 5.0 %own_half_products.1 = (f32[32,640]{1,0:T(8,128)S(1)}, f32[32,96]{1,0:T(8,128)S(1)}, f32[32,4096]{1,0:T(8,128)S(1)}, bf16[640,4096]{1,0:T(8,128)(2,1)S(1)}) custom-call(bf16[640,8192]{1,0:T(8,128)(2,1)} %feat_hbm.5, s16[8,136,128]{2,1,0:T(8,128)(2,1)S(1)} %all-to-all-done.1.code_ref, bf16[96,8192]{1,0:T(8,128)(2,1)S(1)} %get-tuple-element.28.x_ref), custom_call_target="tpu_custom_call" | custom-call | tf_op jit(solution)/shard_map/own_half_products/pallas_call | solution.py:431
  53.3 0.0 collective-permute-done.9.code_ref
  53.3 0.0 copy-done
  53.3 3.8 %pursuit.1 = (f32[3,640]{1,0:T(4,128)}, f32[32,8192]{1,0:T(8,128)}) custom-call(s32[640]{0:T(1024)S(1)} %copy-done, bf16[96,8192]{1,0:T(8,128)(2,1)S(1)} %get-tuple-element.28.x_ref, f32[64,640]{1,0:T(8,128)S(1)} %get-tuple-element.29.cross_ref, f32[32,128]{1,0:T(8,128)S(1)} %get-tuple-element.30.factor_ref, f32[32,640]{1,0:T(8,128)S(1)} %get-tuple-element.32.direct_own, ...), custom_call_target="tpu_custom_call" | custom-call | tf_op jit(solution)/shard_map/pursuit/pallas_call | solution.py:450
  (2 shorter events, 0.0 us)
Async XLA Ops:
  5.7 10.7 %collective-permute-start = (bf16[8,6144]{1,0:T(8,128)(2,1)S(1)}, bf16[8,6144]{1,0:T(8,128)(2,1)S(1)}, u32[]{:S(2)}, u32[]{:S(2)}) collective-permute-start(bf16[8,6144]{1,0:T(8,128)(2,1)S(1)} %get-tuple-element.19), channel_id=1, source_target_pairs={{0,8},{1,9},{2,10},{3,11},{4,12},{5,13},{6,14},{7,15},{8,0},{9,1},... | collective-permute-start | bytes 294920 | tf_op jit(solution)/shard_map/ppermute | solution.py:356
  9.8 1.9 %collective-permute-start.4 = (f32[264,512]{1,0:T(8,128)S(1)}, f32[264,512]{1,0:T(8,128)S(1)}, u32[]{:S(2)}, u32[]{:S(2)}) collective-permute-start(f32[264,512]{1,0:T(8,128)S(1)} %get-tuple-element.21), channel_id=1, source_target_pairs={{0,1},{1,0},{2,3},{3,2},{4,5},{5,4},{6,7},{7,6},{8,9},{9,8},{10,11... | collective-permute-start | bytes 1622024 | tf_op jit(solution)/shard_map/ppermute | solution.py:356
  12.6 14.0 %all-to-all-start = ((s16[8,136,128]{2,1,0:T(8,128)(2,1)}), s16[8,136,128]{2,1,0:T(8,128)(2,1)S(1)}, u32[]{:S(2)}, u32[]{:S(2)}) async-start(s16[8,136,128]{2,1,0:T(8,128)(2,1)} %pair_sums.1), calls=%async_computation | async-start | bytes 557056 | tf_op jit(solution)/shard_map/all_to_all | solution.py:360
  16.4 13.3 %collective-permute-start.3 = (bf16[16,6144]{1,0:T(8,128)(2,1)S(1)}, bf16[16,6144]{1,0:T(8,128)(2,1)S(1)}, u32[]{:S(2)}, u32[]{:S(2)}) collective-permute-start(bf16[16,6144]{1,0:T(8,128)(2,1)S(1)} %constant_dynamic-update-slice_fusion.refs_0_), channel_id=1, source_target_pairs={{0,6},{1,7},{2,4},{3,5},{4,2},{5,3},{6,0},{7,1},{8,14},{9,15},{10,... | collective-permute-start | bytes 589832 | tf_op jit(solution)/shard_map/ppermute | solution.py:356
  19.4 11.8 %collective-permute-start.2 = (bf16[16,6144]{1,0:T(8,128)(2,1)S(1)}, bf16[16,6144]{1,0:T(8,128)(2,1)S(1)}, u32[]{:S(2)}, u32[]{:S(2)}) collective-permute-start(bf16[16,6144]{1,0:T(8,128)(2,1)S(1)} %constant_dynamic-update-slice_fusion.refs_0_), channel_id=1, source_target_pairs={{0,2},{1,3},{2,0},{3,1},{4,6},{5,7},{6,4},{7,5},{8,10},{9,11},{10,... | collective-permute-start | bytes 589832 | tf_op jit(solution)/shard_map/ppermute | solution.py:356
  20.0 12.3 %collective-permute-start.1 = (bf16[16,6144]{1,0:T(8,128)(2,1)S(1)}, bf16[16,6144]{1,0:T(8,128)(2,1)S(1)}, u32[]{:S(2)}, u32[]{:S(2)}) collective-permute-start(bf16[16,6144]{1,0:T(8,128)(2,1)S(1)} %constant_dynamic-update-slice_fusion.refs_0_), channel_id=1, source_target_pairs={{0,4},{1,5},{2,6},{3,7},{4,0},{5,1},{6,2},{7,3},{8,12},{9,13},{10,... | collective-permute-start | bytes 589832 | tf_op jit(solution)/shard_map/ppermute | solution.py:356
  32.3 15.7 %all-to-all-start.1 = ((s16[8,136,128]{2,1,0:T(8,128)(2,1)}), s16[8,136,128]{2,1,0:T(8,128)(2,1)S(1)}, u32[]{:S(2)}, u32[]{:S(2)}) async-start(s16[8,136,128]{2,1,0:T(8,128)(2,1)} %total_sums.1), calls=%async_computation.1 | async-start | bytes 557056 | tf_op jit(solution)/shard_map/all_to_all | solution.py:360
  36.5 1.4 %collective-permute-start.5 = (bf16[16,6144]{1,0:T(8,128)(2,1)S(1)}, bf16[16,6144]{1,0:T(8,128)(2,1)S(1)}, u32[]{:S(2)}, u32[]{:S(2)}) collective-permute-start(bf16[16,6144]{1,0:T(8,128)(2,1)S(1)} %constant_dynamic-update-slice_fusion.refs_0_), channel_id=1, source_target_pairs={{0,1},{1,0},{2,3},{3,2},{4,5},{5,4},{6,7},{7,6},{8,9},{9,8},{10,11... | collective-permute-start | bytes 589832 | tf_op jit(solution)/shard_map/ppermute | solution.py:356
  36.5 1.7 %collective-permute-start.6 = (bf16[16,6144]{1,0:T(8,128)(2,1)S(1)}, bf16[16,6144]{1,0:T(8,128)(2,1)S(1)}, u32[]{:S(2)}, u32[]{:S(2)}) collective-permute-start(bf16[16,6144]{1,0:T(8,128)(2,1)S(1)} %collective-permute-done.1.refs_1_), channel_id=1, source_target_pairs={{0,1},{1,0},{2,3},{3,2},{4,5},{5,4},{6,7},{7,6},{8,9},{9,8},{10,11... | collective-permute-start | bytes 589832 | tf_op jit(solution)/shard_map/ppermute | solution.py:356
  37.0 1.5 %collective-permute-start.7 = (bf16[16,6144]{1,0:T(8,128)(2,1)S(1)}, bf16[16,6144]{1,0:T(8,128)(2,1)S(1)}, u32[]{:S(2)}, u32[]{:S(2)}) collective-permute-start(bf16[16,6144]{1,0:T(8,128)(2,1)S(1)} %collective-permute-done.2.refs_2_), channel_id=1, source_target_pairs={{0,1},{1,0},{2,3},{3,2},{4,5},{5,4},{6,7},{7,6},{8,9},{9,8},{10,11... | collective-permute-start | bytes 589832 | tf_op jit(solution)/shard_map/ppermute | solution.py:356
  37.1 1.7 %collective-permute-start.8 = (bf16[16,6144]{1,0:T(8,128)(2,1)S(1)}, bf16[16,6144]{1,0:T(8,128)(2,1)S(1)}, u32[]{:S(2)}, u32[]{:S(2)}) collective-permute-start(bf16[16,6144]{1,0:T(8,128)(2,1)S(1)} %collective-permute-done.3.refs_3_), channel_id=1, source_target_pairs={{0,1},{1,0},{2,3},{3,2},{4,5},{5,4},{6,7},{7,6},{8,9},{9,8},{10,11... | collective-permute-start | bytes 589832 | tf_op jit(solution)/shard_map/ppermute | solution.py:356
  48.0 5.3 %copy-start = (s32[640]{0:T(1024)S(1)}, s32[640]{0:T(1024)}, u32[]{:S(2)}) copy-start(s32[640]{0:T(1024)} %labels_ref.1) | copy-start | bytes 7684
  48.0 5.3 %collective-permute-start.9 = (s16[8,136,128]{2,1,0:T(8,128)(2,1)S(1)}, s16[8,136,128]{2,1,0:T(8,128)(2,1)S(1)}, u32[]{:S(2)}, u32[]{:S(2)}) collective-permute-start(s16[8,136,128]{2,1,0:T(8,128)(2,1)S(1)} %all-to-all-done.1.code_ref), channel_id=1, source_target_pairs={{0,1},{1,0},{2,3},{3,2},{4,5},{5,4},{6,7},{7,6},{8,9},{9,8},{10,11... | collective-permute-start | bytes 835592 | tf_op jit(solution)/shard_map/ppermute | solution.py:356

commit v6 on v5

--- a/solution.py
+++ b/solution.py
@@ -133,9 +133,7 @@
         more, more_mark = decode(got_ref[k], classes)
         value = value + more
         mark = mark + more_mark
-    code = encode(value / jnp.sqrt(column(mark, classes, classes // 8)))
-    for k in range(code_ref.shape[0]):
-        code_ref[k] = code
+    code_ref[0] = encode(value / jnp.sqrt(column(mark, classes, classes // 8)))
 
 
 def diagonal(block):
@@ -181,32 +179,10 @@
     return result
 
 
-def picked_kernel(pick_hbm, feat_hbm, *refs, n_ex):
-    parts = refs[:-9]
-    x_ref, cross_ref, factor_ref, pick_ref, rows_ref, feat_ref, feat_sems, part_sems, pick_sem = refs[-9:]
-    rows, full = feat_ref.shape
+def select_kernel(pick_ref, one_ref, rest_ref, *, n_ex, rows):
     steps, classes = pick_ref.shape
-    lines, main = rows_ref.shape
-    tail = full - main
-    width = full // n_ex
+    lines = one_ref.shape[1]
     device = lax.axis_index("ex")
-
-    pick_copy = pltpu.make_async_copy(pick_hbm, pick_ref, pick_sem)
-    pick_copy.start()
-    part_copies = []
-    at = 0
-    for i, part in enumerate(parts):
-        part_copies.append(pltpu.make_async_copy(part, rows_ref.at[at : at + part.shape[0]], part_sems.at[i]))
-        part_copies[-1].start()
-        at += part.shape[0]
-    copies = []
-    for i in range(n_ex):
-        col = slice(i * width, (i + 1) * width)
-        copies.append(pltpu.make_async_copy(feat_hbm.at[:, col], feat_ref.at[:, col], feat_sems.at[i]))
-        copies[-1].start()
-    span = full // 4
-
-    pick_copy.wait()
     pick = pick_ref[...]
     lane = lax.broadcasted_iota(jnp.int32, pick.shape, 1)
     owner = jnp.zeros_like(pick)
@@ -223,23 +199,38 @@
         spot = spot + (((away >> b) & 1) << (bits - 1 - b))
     spot = spot + ((away & 1) << (bits - 1))
     step = lax.broadcasted_iota(jnp.int32, pick.shape, 0)
-    index = spot * 8 + rank * steps + step
-    home = spot * 8 + slots * steps + rank
     line = lax.broadcasted_iota(jnp.int32, (lines, classes), 0)
-
-    def choose(where):
+    for ref, where in ((one_ref, spot * 8 + rank * steps + step), (rest_ref, spot * 8 + slots * steps + rank)):
         hits = [jnp.where(line == where[s : s + 1, :], 1.0, 0.0) for s in range(steps)]
         pad = jnp.zeros((lines, 128 - steps * classes), f32)
-        return jnp.transpose(jnp.concatenate(hits + [pad], axis=1))[: steps * classes].astype(bf16)
-
-    one = choose(index)
-    rest = choose(home)
-    for copy in part_copies:
+        ref[...] = jnp.transpose(jnp.concatenate(hits + [pad], axis=1))[: steps * classes].astype(bf16)
+
+
+def picked_kernel(feat_hbm, one_ref, rest_ref, *refs, steps):
+    parts, (x_ref, factor_ref, feat_ref, rows_ref, sems, feat_sems) = refs[:-6], refs[-6:]
+    total, full = x_ref.shape
+    loads = feat_sems.shape[0]
+    classes = total // steps
+    main = rows_ref.shape[1]
+    tail = full - main
+    copies = []
+    at = 0
+    for i, part in enumerate(parts):
+        copies.append(pltpu.make_async_copy(part, rows_ref.at[at : at + part.shape[0]], sems.at[i]))
+        copies[-1].start()
+        at += part.shape[0]
+    feat_copies = []
+    for i in range(loads):
+        col = slice(i * full // loads, (i + 1) * full // loads)
+        feat_copies.append(pltpu.make_async_copy(feat_hbm.at[:, col], feat_ref.at[:, col], feat_sems.at[i]))
+        feat_copies[-1].start()
+    for copy in copies:
         copy.wait()
-    x_ref[:, :main] = jnp.dot(one, rows_ref[...], preferred_element_type=f32).astype(bf16)
+    x_ref[:, :main] = jnp.dot(one_ref[...], rows_ref[...], preferred_element_type=f32).astype(bf16)
     for s in range(steps):
         at = slice(s * classes, (s + 1) * classes)
-        x_ref[at, main:] = jnp.dot(rest[at], rows_ref[:, s * tail : (s + 1) * tail], preferred_element_type=f32).astype(bf16)
+        rest = jnp.dot(rest_ref[at, :], rows_ref[:, s * tail : (s + 1) * tail], preferred_element_type=f32)
+        x_ref[at, main:] = rest.astype(bf16)
 
     x = x_ref[...]
     full_gram = nt_dot(x, x)
@@ -258,64 +249,61 @@
         for j in range(i + 1):
             packed = jnp.where(lane == i * steps + j, factor[i][j], packed)
     factor_ref[...] = packed
-
-    for i in range(4):
-        for copy in copies[i * n_ex // 4 : (i + 1) * n_ex // 4]:
-            copy.wait()
-        col = slice(i * span, (i + 1) * span)
-        part = nt_dot(x_ref[: cross_ref.shape[0], col], feat_ref[:, col])
-        cross_ref[...] = part if i == 0 else cross_ref[...] + part
-
-
-def half_kernel(feat_hbm, code_ref, x_ref, direct_ref, right_ref, target_ref, other_ref, low_ref, feat_ref, sems, *, classes):
-    groups = code_ref.shape[0]
-    half = feat_ref.shape[1]
-    width = half // groups
+    for copy in feat_copies:
+        copy.wait()
+
+
+def masks_of(n_ex):
+    masks = [0]
+    mask = n_ex // 2
+    while mask > 4:
+        masks = masks + [m ^ mask for m in masks]
+        mask //= 2
+    return masks + [m ^ 4 for m in masks] + [m ^ 2 for m in masks] + [m ^ 6 for m in masks]
+
+
+def half_products(side, code_ref, x_ref, feat_ref, target_ref, target_at, left_ref, *, n_ex, classes):
+    half = left_ref.shape[1]
+    width = half // code_ref.shape[0]
+    used = left_ref.shape[0] - classes
+    group = lax.axis_index("ex") // 2
+    here = pl.ds(pl.multiple_of(side * half, half), half)
+    for k, mask in enumerate(masks_of(n_ex)):
+        block = group ^ (mask // 2)
+        target = decode(code_ref[k], classes)[0]
+        target_ref[:, pl.ds(pl.multiple_of(target_at + block * width, width), width)] = target
+        left_ref[:classes, pl.ds(pl.multiple_of(block * width, width), width)] = target.astype(bf16)
+    left_ref[classes:, :] = x_ref[:used, here]
+    right = nt_dot(left_ref[:classes, :], x_ref[:, here])
+    return right, nt_dot(left_ref[...], feat_ref[:, here])
+
+
+def half_kernel(feat_ref, code_ref, x_ref, direct_ref, right_ref, target_ref, left_ref, *, n_ex, classes):
     core = lax.axis_index("ex") % 2
-    copies = []
-    for side, ref in ((core, feat_ref), (1 - core, other_ref)):
-        for k in range(groups):
-            src = pl.ds(pl.multiple_of(side * half + k * width, width), width)
-            dst = slice(k * width, (k + 1) * width)
-            copies.append(pltpu.make_async_copy(feat_hbm.at[:, src], ref.at[:, dst], sems.at[len(copies)]))
-            copies[-1].start()
-    for k in range(groups):
-        target = decode(code_ref[k], classes)[0]
-        target_ref[:, k * width : (k + 1) * width] = target
-        low_ref[:, k * width : (k + 1) * width] = target.astype(bf16)
-    right_ref[...] = nt_dot(low_ref[...], x_ref[:, pl.ds(pl.multiple_of(core * half, half), half)])
-    for copy in copies[:groups]:
-        copy.wait()
-    direct_ref[...] = nt_dot(low_ref[...], feat_ref[...])
-    for copy in copies[groups:]:
-        copy.wait()
+    right_ref[...], direct_ref[...] = half_products(
+        core, code_ref, x_ref, feat_ref, target_ref, 0, left_ref, n_ex=n_ex, classes=classes
+    )
 
 
 def pursuit_kernel(
-    labels_ref, x_ref, cross_ref, factor_ref, direct_own, right_own, target_own, feat_ref, code_ref,
-    scores_ref, resid_hbm, resid_ref, low_ref, sems, *, steps, scale
+    labels_ref, feat_ref, x_ref, factor_ref, direct_own, right_own, target_own, code_ref,
+    scores_ref, resid_hbm, resid_ref, left_ref, sems, *, n_ex, steps, scale
 ):
     classes, full = resid_ref.shape
-    groups = code_ref.shape[0]
     half = full // 2
-    width = half // groups
     core = lax.axis_index("ex") % 2
-    mine = pl.ds(pl.multiple_of(core * half, half), half)
-    rest = pl.ds(pl.multiple_of((1 - core) * half, half), half)
-    for k in range(groups):
-        at = pl.ds(pl.multiple_of((1 - core) * half + k * width, width), width)
-        target = decode(code_ref[k], classes)[0]
-        resid_ref[:, at] = target
-        low_ref[:, k * width : (k + 1) * width] = target.astype(bf16)
-    right = right_own[...] + nt_dot(low_ref[...], x_ref[:, rest])
+    right, direct = half_products(
+        1 - core, code_ref, x_ref, feat_ref, resid_ref, (1 - core) * half, left_ref, n_ex=n_ex, classes=classes
+    )
+    right = right + right_own[...]
     rhs = [diagonal(right[:, a * classes : (a + 1) * classes]) for a in range(steps)]
     factor = [[factor_ref[:, i * steps + j : i * steps + j + 1] for j in range(i + 1)] for i in range(steps)]
     weights = solve_all(factor, rhs)
     last = weights[steps - 1]
     copies = []
-    for source, side, at in ((target_own, core, mine), (resid_ref, 1 - core, rest)):
+    span = half // 2
+    for source, side in ((target_own, core), (resid_ref, 1 - core)):
         for q in range(2):
-            span = half // 2
             here = pl.ds(pl.multiple_of(side * half + q * span, span), span)
             value = source[:, q * span : (q + 1) * span] if source is target_own else source[:, here]
             for k in range(steps):
@@ -324,12 +312,12 @@
             copies.append(pltpu.make_async_copy(resid_ref.at[:, here], resid_hbm.at[:, here], sems.at[len(copies)]))
             copies[-1].start()
 
-    direct = direct_own[...] + nt_dot(low_ref[...], feat_ref[...])
-    member = lax.broadcasted_iota(jnp.int32, direct.shape, 0) == labels_ref[...].reshape(1, direct.shape[1])
+    direct = direct + direct_own[...]
+    member = lax.broadcasted_iota(jnp.int32, (classes, direct.shape[1]), 0) == labels_ref[...].reshape(1, direct.shape[1])
     for s in range(steps):
-        value = direct
+        value = direct[:classes]
         for k in range(s):
-            value = value - weights[s - 1][k] * cross_ref[k * classes : (k + 1) * classes]
+            value = value - weights[s - 1][k] * direct[(k + 1) * classes : (k + 2) * classes]
         scores_ref[s : s + 1, :] = jnp.sum(jnp.where(member, value, 0.0), axis=0, keepdims=True) * scale
     for copy in copies:
         copy.wait()
@@ -377,13 +365,6 @@
     )(labels_in, picks, features)
 
     got = swap(send, 1)
-    near = packed
-    mask = n_ex // 2
-    while mask > 4:
-        near = jnp.concatenate([near, swap(near, mask)], axis=0)
-        mask //= 2
-    parts = [near, swap(near, 4), swap(near, 2), swap(near, 6)]
-
     codes_out = pl.pallas_call(
         functools.partial(pair_kernel, classes=classes),
         in_specs=[vmem] * 2,
@@ -392,77 +373,88 @@
         compiler_params=limit,
         name="pair_sums",
     )(keep, got)
+    pick_late, packed, _ = lax.optimization_barrier((pick_index, packed, codes_out))
+
+    def along_z(x):
+        mask = n_ex // 2
+        while mask > 4:
+            x = jnp.concatenate([x, swap(x, mask)], axis=0)
+            mask //= 2
+        return x
+
+    near = along_z(packed)
+    parts = [near, swap(near, 4), swap(near, 2), swap(near, 6)]
+    one, rest = pl.pallas_call(
+        functools.partial(select_kernel, n_ex=n_ex, rows=rows),
+        in_specs=[vmem],
+        out_specs=[vmem] * 2,
+        out_shape=[jax.ShapeDtypeStruct((total, n_ex * 8), bf16)] * 2,
+        compiler_params=limit,
+        name="selectors",
+    )(pick_late)
+
+    traded, _ = lax.optimization_barrier((trade(codes_out), parts[0]))
     summed = pl.pallas_call(
         functools.partial(total_kernel, classes=classes),
         in_specs=[vmem],
         out_specs=vmem,
-        out_shape=codes,
+        out_shape=jax.ShapeDtypeStruct((1,) + codes.shape[1:], codes.dtype),
         compiler_params=limit,
         name="total_sums",
-    )(trade(codes_out))
-    parts, summed = lax.optimization_barrier((parts, summed))
+    )(traded)
+    near = along_z(summed)
+    parts, _ = lax.optimization_barrier((parts, near))
+    own_parts = [near, swap(near, 4), swap(near, 2), swap(near, 6)]
     parts = parts + [swap(p, 1) for p in parts]
-    own_half = trade(summed)
-
-    x, cross, factor = pl.pallas_call(
-        functools.partial(picked_kernel, n_ex=n_ex),
-        in_specs=[hbm, hbm] + [anywhere] * len(parts),
+
+    x, factor, features_in = pl.pallas_call(
+        functools.partial(picked_kernel, steps=steps),
+        in_specs=[hbm] + [vmem] * 2 + [anywhere] * len(parts),
         out_specs=[vmem] * 3,
         out_shape=[
             jax.ShapeDtypeStruct((total, full), bf16),
-            jax.ShapeDtypeStruct((total - classes, rows), f32),
             jax.ShapeDtypeStruct((classes, 128), f32),
+            pltpu.VMEM((rows, full), bf16),
         ],
         scratch_shapes=[
-            pltpu.VMEM(pick_index.shape, jnp.int32),
             pltpu.VMEM((n_ex * 8, main), bf16),
-            pltpu.VMEM((rows, full), bf16),
+            pltpu.SemaphoreType.DMA((len(parts),)),
             pltpu.SemaphoreType.DMA((n_ex,)),
-            pltpu.SemaphoreType.DMA((len(parts),)),
-            pltpu.SemaphoreType.DMA(()),
-        ],
-        compiler_params=limit,
-        name="picked_products",
-    )(picks, features, *parts)
-
-    own_half, x = lax.optimization_barrier((own_half, x))
+        ],
+        compiler_params=limit,
+        name="picked_rows",
+    )(features, one, rest, *parts)
+
+    own_parts, x = lax.optimization_barrier((own_parts, x))
+    own_half = jnp.concatenate(own_parts, axis=0)
     twin_half = swap(own_half, 1)
-    feat_half = pltpu.VMEM((rows, full // 2), bf16)
-    direct, right, target, feat_rest = pl.pallas_call(
-        functools.partial(half_kernel, classes=classes),
-        in_specs=[hbm, vmem, vmem],
-        out_specs=[vmem] * 4,
+    left = pltpu.VMEM((total, full // 2), bf16)
+    direct, right, target = pl.pallas_call(
+        functools.partial(half_kernel, n_ex=n_ex, classes=classes),
+        in_specs=[vmem] * 3,
+        out_specs=[vmem] * 3,
         out_shape=[
-            jax.ShapeDtypeStruct((classes, rows), f32),
+            jax.ShapeDtypeStruct((total, rows), f32),
             jax.ShapeDtypeStruct((classes, total), f32),
             jax.ShapeDtypeStruct((classes, full // 2), f32),
-            feat_half,
-        ],
-        scratch_shapes=[
-            pltpu.VMEM((classes, full // 2), bf16),
-            feat_half,
-            pltpu.SemaphoreType.DMA((n_ex,)),
-        ],
+        ],
+        scratch_shapes=[left],
         compiler_params=limit,
         name="own_half_products",
-    )(features, own_half, x)
+    )(features_in, own_half, x)
 
     scores, resid = pl.pallas_call(
-        functools.partial(pursuit_kernel, steps=steps, scale=1.0 / math.sqrt(full)),
-        in_specs=[vmem] * 9,
+        functools.partial(pursuit_kernel, n_ex=n_ex, steps=steps, scale=1.0 / math.sqrt(full)),
+        in_specs=[vmem] * 8,
         out_specs=[vmem, anywhere],
         out_shape=[
             jax.ShapeDtypeStruct((steps, rows), f32),
             jax.ShapeDtypeStruct((classes, full), f32),
         ],
-        scratch_shapes=[
-            pltpu.VMEM((classes, full), f32),
-            pltpu.VMEM((classes, full // 2), bf16),
-            pltpu.SemaphoreType.DMA((4,)),
-        ],
+        scratch_shapes=[pltpu.VMEM((classes, full), f32), left, pltpu.SemaphoreType.DMA((4,))],
         compiler_params=limit,
         name="pursuit",
-    )(labels, x, cross, factor, direct, right, target, feat_rest, twin_half)
+    )(labels, features_in, x, factor, direct, right, target, twin_half)
     return scores, resid
 
 

time: 57.4 us -> 58.6 us (1.021)
  Pallas kernels: 24.9 us -> 18.2 us
  waiting for transfers between devices: 14.4 us -> 20.3 us
  starting transfers between devices: 17.1 us -> 18.9 us
    ppermute x10 -> x14, waiting for transfers between devices: 7.8 us -> 20.3 us  [swap(): return lax.ppermute(x, 'ex', [(d, d ^ mask) for d in range(n_ex)])]
    all_to_all x2 -> x1, waiting for transfers between devices: 6.59 us -> 0.01 us  [trade(): return lax.all_to_all(x, 'ex', 0, 0, axis_index_groups=teams, tiled=True)]
    pallas_call x3 -> x4, Pallas kernels: 17.9 us -> 12 us  [the longest x1 6.29 us: on_device(): pl.pallas_call(functools.partial(picked_kernel, steps=steps), in_specs=[h...]
    ppermute x10 -> x14, starting transfers between devices: 9.05 us -> 11.7 us  [swap(): return lax.ppermute(x, 'ex', [(d, d ^ mask) for d in range(n_ex)])]
    all_to_all x2 -> x1, starting transfers between devices: 8.04 us -> 7.2 us  [trade(): return lax.all_to_all(x, 'ex', 0, 0, axis_index_groups=teams, tiled=True)]
    pallas_call x1, Pallas kernels: 1.01 us -> 0.28 us  [on_device(): pl.pallas_call(functools.partial(total_kernel, classes=classes), in_specs...]
  transfers between devices with their start and end apart: 12 -> 15, of which waited for: 9 -> 6; matrix products, arithmetic and copies ran while one was open for 0% -> 0% of each run, Pallas kernels for 28% -> 15%
where the time goes in v6:
time: 58.6 us; the launch traced here: 58.3 us
  waiting for transfers between devices  20.3 us (35%)
  starting transfers between devices  18.9 us (32%)
  Pallas kernels  18.2 us (31%)
  between operations  0.79 us (1%)
    ppermute x14, waiting for transfers between devices, swap(): return lax.ppermute(x, 'ex', [(d, d ^ mask) for d in range(n_ex)])  20.3 us
    ppermute x14, starting transfers between devices, swap(): return lax.ppermute(x, 'ex', [(d, d ^ mask) for d in range(n_ex)])  11.7 us
    all_to_all x1, starting transfers between devices, trade(): return lax.all_to_all(x, 'ex', 0, 0, axis_index_groups=teams, tiled=True)  7.2 us
    pallas_call x1, Pallas kernels, on_device(): pl.pallas_call(functools.partial(picked_kernel, steps=steps), in_specs=[h...  6.29 us
    pallas_call x1, Pallas kernels, on_device(): pl.pallas_call(functools.partial(sums_kernel, n_ex=n_ex), in_specs=[hbm]...  5.05 us
    pallas_call x1, Pallas kernels, on_device(): pl.pallas_call(functools.partial(pursuit_kernel, n_ex=n_ex, steps=steps,...  3.33 us
    pallas_call x1, Pallas kernels, on_device(): pl.pallas_call(functools.partial(half_kernel, n_ex=n_ex, classes=classes)...  2.02 us
  transfers between devices with their start and end apart: 15, of which 6 were waited for; matrix products, arithmetic and copies ran while one was open for 0% of the time, Pallas kernels for 15%

profile of v6, /device:TPU:0, one launch (start us, length us, event | category | flops | bytes accessed | tf_op | source)
XLA Modules:
  0.0 58.3 jit_solution(4791577108524971631)
XLA Ops:
  0.6 5.1 %class_sums.1 = (f32[264,512]{1,0:T(8,128)S(1)}, f32[264,512]{1,0:T(8,128)S(1)}, bf16[8,6144]{1,0:T(8,128)(2,1)S(1)}) custom-call(s32[640]{0:T(1024)} %labels_ref.1, s32[3,32]{1,0:T(4,128)} %pick_ref, bf16[640,8192]{1,0:T(8,128)(2,1)} %feat_hbm.3), custom_call_target="tpu_custom_call" | custom-call | tf_op jit(solution)/shard_map/class_sums/pallas_call | solution.py:350
  5.7 0.5 collective-permute-start
  6.2 1.6 %collective-permute-done.got_ref = f32[264,512]{1,0:T(8,128)S(1)} collective-permute-done((f32[264,512]{1,0:T(8,128)S(1)}, f32[264,512]{1,0:T(8,128)S(1)}, u32[]{:S(2)}, u32[]{:S(2)}) %collective-permute-start) | collective-permute-done | bytes 540704 | tf_op jit(solution)/shard_map/ppermute | solution.py:344
  7.8 0.9 %pair_sums.1 = s16[8,136,128]{2,1,0:T(8,128)(2,1)} custom-call(f32[264,512]{1,0:T(8,128)S(1)} %get-tuple-element.26.keep_ref, f32[264,512]{1,0:T(8,128)S(1)} %collective-permute-done.got_ref), custom_call_target="tpu_custom_call" | custom-call | tf_op jit(solution)/shard_map/pair_sums/pallas_call | solution.py:368
  8.7 7.2 %all-to-all-start = ((s16[8,136,128]{2,1,0:T(8,128)(2,1)}), s16[8,136,128]{2,1,0:T(8,128)(2,1)S(1)}, u32[]{:S(2)}, u32[]{:S(2)}) async-start(s16[8,136,128]{2,1,0:T(8,128)(2,1)} %pair_sums.1), calls=%async_computation | async-start | bytes 557056 | tf_op jit(solution)/shard_map/all_to_all | solution.py:348
  15.9 2.9 %collective-permute-start.1 = (bf16[8,6144]{1,0:T(8,128)(2,1)S(1)}, bf16[8,6144]{1,0:T(8,128)(2,1)S(1)}, u32[]{:S(2)}, u32[]{:S(2)}) collective-permute-start(bf16[8,6144]{1,0:T(8,128)(2,1)S(1)} %get-tuple-element.31), channel_id=1, source_target_pairs={{0,8},{1,9},{2,10},{3,11},{4,12},{5,13},{6,14},{7,15},{8,0},{9,1},... | collective-permute-start | bytes 294920 | tf_op jit(solution)/shard_map/ppermute | solution.py:344
  18.8 10.8 %collective-permute-done.1 = bf16[8,6144]{1,0:T(8,128)(2,1)S(1)} collective-permute-done((bf16[8,6144]{1,0:T(8,128)(2,1)S(1)}, bf16[8,6144]{1,0:T(8,128)(2,1)S(1)}, u32[]{:S(2)}, u32[]{:S(2)}) %collective-permute-start.1) | collective-permute-done | bytes 98336 | tf_op jit(solution)/shard_map/ppermute | solution.py:344
  29.6 0.1 collective-permute-start.4
  29.7 1.5 %collective-permute-start.3 = (bf16[16,6144]{1,0:T(8,128)(2,1)S(1)}, bf16[16,6144]{1,0:T(8,128)(2,1)S(1)}, u32[]{:S(2)}, u32[]{:S(2)}) collective-permute-start(bf16[16,6144]{1,0:T(8,128)(2,1)S(1)} %constant_dynamic-update-slice_fusion.refs_0_), channel_id=1, source_target_pairs={{0,2},{1,3},{2,0},{3,1},{4,6},{5,7},{6,4},{7,5},{8,10},{9,11},{10,... | collective-permute-start | bytes 589832 | tf_op jit(solution)/shard_map/ppermute | solution.py:344
  31.2 1.9 %collective-permute-start.2 = (bf16[16,6144]{1,0:T(8,128)(2,1)S(1)}, bf16[16,6144]{1,0:T(8,128)(2,1)S(1)}, u32[]{:S(2)}, u32[]{:S(2)}) collective-permute-start(bf16[16,6144]{1,0:T(8,128)(2,1)S(1)} %constant_dynamic-update-slice_fusion.refs_0_), channel_id=1, source_target_pairs={{0,4},{1,5},{2,6},{3,7},{4,0},{5,1},{6,2},{7,3},{8,12},{9,13},{10,... | collective-permute-start | bytes 589832 | tf_op jit(solution)/shard_map/ppermute | solution.py:344
  33.2 0.0 all-to-all-done.got_ref
  33.2 0.3 total_sums.1
  33.5 0.1 collective-permute-start.5
  33.6 4.9 %collective-permute-done.5 = s16[1,136,128]{2,1,0:T(8,128)(2,1)S(1)} collective-permute-done((s16[1,136,128]{2,1,0:T(8,128)(2,1)S(1)}, s16[1,136,128]{2,1,0:T(8,128)(2,1)S(1)}, u32[]{:S(2)}, u32[]{:S(2)}) %collective-permute-start.5) | collective-permute-done | bytes 34848 | tf_op jit(solution)/shard_map/ppermute | solution.py:344
  38.5 0.3 collective-permute-done.4.refs_3_
  38.8 1.0 %collective-permute-done.3.refs_2_ = bf16[16,6144]{1,0:T(8,128)(2,1)S(1)} collective-permute-done((bf16[16,6144]{1,0:T(8,128)(2,1)S(1)}, bf16[16,6144]{1,0:T(8,128)(2,1)S(1)}, u32[]{:S(2)}, u32[]{:S(2)}) %collective-permute-start.3) | collective-permute-done | bytes 196640 | tf_op jit(solution)/shard_map/ppermute | solution.py:344
  39.8 1.7 %collective-permute-done.2.refs_1_ = bf16[16,6144]{1,0:T(8,128)(2,1)S(1)} collective-permute-done((bf16[16,6144]{1,0:T(8,128)(2,1)S(1)}, bf16[16,6144]{1,0:T(8,128)(2,1)S(1)}, u32[]{:S(2)}, u32[]{:S(2)}) %collective-permute-start.2) | collective-permute-done | bytes 196640 | tf_op jit(solution)/shard_map/ppermute | solution.py:344
  41.5 0.0 collective-permute-start.6
  41.5 0.5 collective-permute-start.7
  42.0 0.0 collective-permute-start.8
  42.0 0.5 collective-permute-start.9
  42.5 1.0 %collective-permute-start.12 = (s16[2,136,128]{2,1,0:T(8,128)(2,1)S(1)}, s16[2,136,128]{2,1,0:T(8,128)(2,1)S(1)}, u32[]{:S(2)}, u32[]{:S(2)}) collective-permute-start(s16[2,136,128]{2,1,0:T(8,128)(2,1)S(1)} %pad_add_fusion), channel_id=1, source_target_pairs={{0,6},{1,7},{2,4},{3,5},{4,2},{5,3},{6,0},{7,1},{8,14},{9,15},{10,... | collective-permute-start | bytes 208904 | tf_op jit(solution)/shard_map/ppermute | solution.py:344
  43.5 0.0 collective-permute-done.6.refs_4_
  43.5 0.2 collective-permute-start.11
  43.7 2.3 %collective-permute-start.10 = (s16[2,136,128]{2,1,0:T(8,128)(2,1)S(1)}, s16[2,136,128]{2,1,0:T(8,128)(2,1)S(1)}, u32[]{:S(2)}, u32[]{:S(2)}) collective-permute-start(s16[2,136,128]{2,1,0:T(8,128)(2,1)S(1)} %pad_add_fusion), channel_id=1, source_target_pairs={{0,4},{1,5},{2,6},{3,7},{4,0},{5,1},{6,2},{7,3},{8,12},{9,13},{10,... | collective-permute-start | bytes 208904 | tf_op jit(solution)/shard_map/ppermute | solution.py:344
  46.0 0.4 selectors.1
  46.4 0.0 collective-permute-done.8.refs_6_
  46.4 0.0 copy-start
  46.4 6.3 %picked_rows.1 = (bf16[96,8192]{1,0:T(8,128)(2,1)S(1)}, f32[32,128]{1,0:T(8,128)S(1)}, bf16[640,8192]{1,0:T(8,128)(2,1)S(1)}) custom-call(bf16[640,8192]{1,0:T(8,128)(2,1)} %feat_hbm.3, bf16[96,128]{1,0:T(8,128)(2,1)S(1)} %get-tuple-element.29.one_ref, bf16[96,128]{1,0:T(8,128)(2,1)S(1)} %get-tuple-element.30.rest_ref, ...), custom_call_target="tpu_custom_call" | custom-call | tf_op jit(solution)/shard_map/picked_rows/pallas_call | solution.py:410
  52.8 0.1 collective-permute-start.13
  52.9 2.0 %own_half_products.1 = (f32[96,640]{1,0:T(8,128)S(1)}, f32[32,96]{1,0:T(8,128)S(1)}, f32[32,4096]{1,0:T(8,128)S(1)}) custom-call(bf16[640,8192]{1,0:T(8,128)(2,1)S(1)} %get-tuple-element.37.feat_ref, s16[8,136,128]{2,1,0:T(8,128)(2,1)S(1)} %constant_dynamic-update-slice_fusion.2.code_ref, bf16[96,8192]{1,0:T(8,128)(2,1)S(1)} %get-tuple-element.39.x_ref), custom_call_target="tpu_custom_call" | custom-call | tf_op jit(solution)/shard_map/own_half_products/pallas_call | solution.py:432
  55.0 3.3 %pursuit.1 = (f32[3,640]{1,0:T(4,128)}, f32[32,8192]{1,0:T(8,128)}) custom-call(s32[640]{0:T(1024)S(1)} %copy-done, bf16[640,8192]{1,0:T(8,128)(2,1)S(1)} %get-tuple-element.37.feat_ref, bf16[96,8192]{1,0:T(8,128)(2,1)S(1)} %get-tuple-element.39.x_ref, f32[32,128]{1,0:T(8,128)S(1)} %get-tuple-element.40.factor_ref, ...), custom_call_target="tpu_custom_call" | custom-call | tf_op jit(solution)/shard_map/pursuit/pallas_call | solution.py:446
  (16 shorter events, 0.1 us)
Async XLA Ops:
  0.6 45.4 %copy-start.1 = (s32[3,32]{1,0:T(4,128)S(1)}, s32[3,32]{1,0:T(4,128)}, u32[]{:S(2)}) copy-start(s32[3,32]{1,0:T(4,128)} %pick_ref) | copy-start | bytes 1156
  5.7 2.1 %collective-permute-start = (f32[264,512]{1,0:T(8,128)S(1)}, f32[264,512]{1,0:T(8,128)S(1)}, u32[]{:S(2)}, u32[]{:S(2)}) collective-permute-start(f32[264,512]{1,0:T(8,128)S(1)} %get-tuple-element.27), channel_id=1, source_target_pairs={{0,1},{1,0},{2,3},{3,2},{4,5},{5,4},{6,7},{7,6},{8,9},{9,8},{10,11... | collective-permute-start | bytes 1622024 | tf_op jit(solution)/shard_map/ppermute | solution.py:344
  8.7 24.5 %all-to-all-start = ((s16[8,136,128]{2,1,0:T(8,128)(2,1)}), s16[8,136,128]{2,1,0:T(8,128)(2,1)S(1)}, u32[]{:S(2)}, u32[]{:S(2)}) async-start(s16[8,136,128]{2,1,0:T(8,128)(2,1)} %pair_sums.1), calls=%async_computation | async-start | bytes 557056 | tf_op jit(solution)/shard_map/all_to_all | solution.py:348
  15.9 13.7 %collective-permute-start.1 = (bf16[8,6144]{1,0:T(8,128)(2,1)S(1)}, bf16[8,6144]{1,0:T(8,128)(2,1)S(1)}, u32[]{:S(2)}, u32[]{:S(2)}) collective-permute-start(bf16[8,6144]{1,0:T(8,128)(2,1)S(1)} %get-tuple-element.31), channel_id=1, source_target_pairs={{0,8},{1,9},{2,10},{3,11},{4,12},{5,13},{6,14},{7,15},{8,0},{9,1},... | collective-permute-start | bytes 294920 | tf_op jit(solution)/shard_map/ppermute | solution.py:344
  29.6 9.2 %collective-permute-start.4 = (bf16[16,6144]{1,0:T(8,128)(2,1)S(1)}, bf16[16,6144]{1,0:T(8,128)(2,1)S(1)}, u32[]{:S(2)}, u32[]{:S(2)}) collective-permute-start(bf16[16,6144]{1,0:T(8,128)(2,1)S(1)} %constant_dynamic-update-slice_fusion.refs_0_), channel_id=1, source_target_pairs={{0,6},{1,7},{2,4},{3,5},{4,2},{5,3},{6,0},{7,1},{8,14},{9,15},{10,... | collective-permute-start | bytes 589832 | tf_op jit(solution)/shard_map/ppermute | solution.py:344
  29.7 10.1 %collective-permute-start.3 = (bf16[16,6144]{1,0:T(8,128)(2,1)S(1)}, bf16[16,6144]{1,0:T(8,128)(2,1)S(1)}, u32[]{:S(2)}, u32[]{:S(2)}) collective-permute-start(bf16[16,6144]{1,0:T(8,128)(2,1)S(1)} %constant_dynamic-update-slice_fusion.refs_0_), channel_id=1, source_target_pairs={{0,2},{1,3},{2,0},{3,1},{4,6},{5,7},{6,4},{7,5},{8,10},{9,11},{10,... | collective-permute-start | bytes 589832 | tf_op jit(solution)/shard_map/ppermute | solution.py:344
  31.2 10.3 %collective-permute-start.2 = (bf16[16,6144]{1,0:T(8,128)(2,1)S(1)}, bf16[16,6144]{1,0:T(8,128)(2,1)S(1)}, u32[]{:S(2)}, u32[]{:S(2)}) collective-permute-start(bf16[16,6144]{1,0:T(8,128)(2,1)S(1)} %constant_dynamic-update-slice_fusion.refs_0_), channel_id=1, source_target_pairs={{0,4},{1,5},{2,6},{3,7},{4,0},{5,1},{6,2},{7,3},{8,12},{9,13},{10,... | collective-permute-start | bytes 589832 | tf_op jit(solution)/shard_map/ppermute | solution.py:344
  33.5 5.0 %collective-permute-start.5 = (s16[1,136,128]{2,1,0:T(8,128)(2,1)S(1)}, s16[1,136,128]{2,1,0:T(8,128)(2,1)S(1)}, u32[]{:S(2)}, u32[]{:S(2)}) collective-permute-start(s16[1,136,128]{2,1,0:T(8,128)(2,1)S(1)} %total_sums.1), channel_id=1, source_target_pairs={{0,8},{1,9},{2,10},{3,11},{4,12},{5,13},{6,14},{7,15},{8,0},{9,1},... | collective-permute-start | bytes 104456 | tf_op jit(solution)/shard_map/ppermute | solution.py:344
  41.5 2.0 %collective-permute-start.6 = (bf16[16,6144]{1,0:T(8,128)(2,1)S(1)}, bf16[16,6144]{1,0:T(8,128)(2,1)S(1)}, u32[]{:S(2)}, u32[]{:S(2)}) collective-permute-start(bf16[16,6144]{1,0:T(8,128)(2,1)S(1)} %constant_dynamic-update-slice_fusion.refs_0_), channel_id=1, source_target_pairs={{0,1},{1,0},{2,3},{3,2},{4,5},{5,4},{6,7},{7,6},{8,9},{9,8},{10,11... | collective-permute-start | bytes 589832 | tf_op jit(solution)/shard_map/ppermute | solution.py:344
  41.5 2.2 %collective-permute-start.7 = (bf16[16,6144]{1,0:T(8,128)(2,1)S(1)}, bf16[16,6144]{1,0:T(8,128)(2,1)S(1)}, u32[]{:S(2)}, u32[]{:S(2)}) collective-permute-start(bf16[16,6144]{1,0:T(8,128)(2,1)S(1)} %collective-permute-done.2.refs_1_), channel_id=1, source_target_pairs={{0,1},{1,0},{2,3},{3,2},{4,5},{5,4},{6,7},{7,6},{8,9},{9,8},{10,11... | collective-permute-start | bytes 589832 | tf_op jit(solution)/shard_map/ppermute | solution.py:344
  42.0 4.4 %collective-permute-start.8 = (bf16[16,6144]{1,0:T(8,128)(2,1)S(1)}, bf16[16,6144]{1,0:T(8,128)(2,1)S(1)}, u32[]{:S(2)}, u32[]{:S(2)}) collective-permute-start(bf16[16,6144]{1,0:T(8,128)(2,1)S(1)} %collective-permute-done.3.refs_2_), channel_id=1, source_target_pairs={{0,1},{1,0},{2,3},{3,2},{4,5},{5,4},{6,7},{7,6},{8,9},{9,8},{10,11... | collective-permute-start | bytes 589832 | tf_op jit(solution)/shard_map/ppermute | solution.py:344
  42.0 4.4 %collective-permute-start.9 = (bf16[16,6144]{1,0:T(8,128)(2,1)S(1)}, bf16[16,6144]{1,0:T(8,128)(2,1)S(1)}, u32[]{:S(2)}, u32[]{:S(2)}) collective-permute-start(bf16[16,6144]{1,0:T(8,128)(2,1)S(1)} %collective-permute-done.4.refs_3_), channel_id=1, source_target_pairs={{0,1},{1,0},{2,3},{3,2},{4,5},{5,4},{6,7},{7,6},{8,9},{9,8},{10,11... | collective-permute-start | bytes 589832 | tf_op jit(solution)/shard_map/ppermute | solution.py:344
  42.5 10.2 %collective-permute-start.12 = (s16[2,136,128]{2,1,0:T(8,128)(2,1)S(1)}, s16[2,136,128]{2,1,0:T(8,128)(2,1)S(1)}, u32[]{:S(2)}, u32[]{:S(2)}) collective-permute-start(s16[2,136,128]{2,1,0:T(8,128)(2,1)S(1)} %pad_add_fusion), channel_id=1, source_target_pairs={{0,6},{1,7},{2,4},{3,5},{4,2},{5,3},{6,0},{7,1},{8,14},{9,15},{10,... | collective-permute-start | bytes 208904 | tf_op jit(solution)/shard_map/ppermute | solution.py:344
  43.5 9.2 %collective-permute-start.11 = (s16[2,136,128]{2,1,0:T(8,128)(2,1)S(1)}, s16[2,136,128]{2,1,0:T(8,128)(2,1)S(1)}, u32[]{:S(2)}, u32[]{:S(2)}) collective-permute-start(s16[2,136,128]{2,1,0:T(8,128)(2,1)S(1)} %pad_add_fusion), channel_id=1, source_target_pairs={{0,2},{1,3},{2,0},{3,1},{4,6},{5,7},{6,4},{7,5},{8,10},{9,11},{10,... | collective-permute-start | bytes 208904 | tf_op jit(solution)/shard_map/ppermute | solution.py:344
  43.7 9.0 %collective-permute-start.10 = (s16[2,136,128]{2,1,0:T(8,128)(2,1)S(1)}, s16[2,136,128]{2,1,0:T(8,128)(2,1)S(1)}, u32[]{:S(2)}, u32[]{:S(2)}) collective-permute-start(s16[2,136,128]{2,1,0:T(8,128)(2,1)S(1)} %pad_add_fusion), channel_id=1, source_target_pairs={{0,4},{1,5},{2,6},{3,7},{4,0},{5,1},{6,2},{7,3},{8,12},{9,13},{10,... | collective-permute-start | bytes 208904 | tf_op jit(solution)/shard_map/ppermute | solution.py:344
  46.4 8.5 %copy-start = (s32[640]{0:T(1024)S(1)}, s32[640]{0:T(1024)}, u32[]{:S(2)}) copy-start(s32[640]{0:T(1024)} %labels_ref.1) | copy-start | bytes 7684
  52.8 2.1 %collective-permute-start.13 = (s16[8,136,128]{2,1,0:T(8,128)(2,1)S(1)}, s16[8,136,128]{2,1,0:T(8,128)(2,1)S(1)}, u32[]{:S(2)}, u32[]{:S(2)}) collective-permute-start(s16[8,136,128]{2,1,0:T(8,128)(2,1)S(1)} %constant_dynamic-update-slice_fusion.2.code_ref), channel_id=1, source_target_pairs={{0,1},{1,0},{2,3},{3,2},{4,5},{5,4},{6,7},{7,6},{8,9},{9,8},{10,11... | collective-permute-start | bytes 835592 | tf_op jit(solution)/shard_map/ppermute | solution.py:344

commit v7 on v6

--- a/solution.py
+++ b/solution.py
@@ -51,7 +51,7 @@
 
 
 def sums_kernel(
-    labels_hbm, pick_hbm, feat_hbm, send_ref, keep_ref, rows_ref, labels_ref, pick_ref, feat_ref, left, held, sems, *, n_ex
+    labels_hbm, pick_hbm, feat_hbm, feat_ref, send_ref, keep_ref, rows_ref, labels_ref, pick_ref, left, held, sems, *, n_ex
 ):
     rows, full = feat_ref.shape
     steps, classes = pick_ref.shape
@@ -118,22 +118,33 @@
     rows_ref[...] = jnp.concatenate(lines, axis=0).astype(bf16)
 
 
-def pair_kernel(keep_ref, got_ref, code_ref, *, classes):
-    groups = code_ref.shape[0]
-    base = groups * classes
+def near_id(mask):
+    return (lax.axis_index("ex") // 2 % 4) ^ (mask // 2)
+
+
+def pair_kernel(keep_ref, got_ref, *code_refs, classes):
+    far = code_refs[0].shape[0]
+    base = 4 * far * classes
     tile = keep_ref[base : base + 8, :128] + got_ref[base : base + 8, :128]
-    for k in range(groups):
-        at = slice(k * classes, (k + 1) * classes)
-        code_ref[k] = encode(keep_ref[at, :] + got_ref[at, :], tile)
-
-
-def total_kernel(got_ref, code_ref, *, classes):
-    value, mark = decode(got_ref[0], classes)
-    for k in range(1, got_ref.shape[0]):
-        more, more_mark = decode(got_ref[k], classes)
-        value = value + more
-        mark = mark + more_mark
-    code_ref[0] = encode(value / jnp.sqrt(column(mark, classes, classes // 8)))
+    for mask, code_ref in zip((0, 4, 2, 6), code_refs):
+        for j in range(far):
+            at = pl.ds(pl.multiple_of((j * 4 + near_id(mask)) * classes, classes), classes)
+            code_ref[j] = encode(keep_ref[at, :] + got_ref[at, :], tile)
+
+
+def add_kernel(*refs, classes, last):
+    code_ref = refs[-1]
+    for j in range(code_ref.shape[0]):
+        value, mark = decode(refs[0][j], classes)
+        for ref in refs[1:-1]:
+            more, more_mark = decode(ref[j], classes)
+            value = value + more
+            mark = mark + more_mark
+        if last:
+            code_ref[j] = encode(value / jnp.sqrt(column(mark, classes, classes // 8)))
+        else:
+            lane = lax.broadcasted_iota(jnp.int32, mark.shape, 1)
+            code_ref[j] = encode(value, jnp.where(lane < classes // 8, 0.0, mark))
 
 
 def diagonal(block):
@@ -206,26 +217,16 @@
         ref[...] = jnp.transpose(jnp.concatenate(hits + [pad], axis=1))[: steps * classes].astype(bf16)
 
 
-def picked_kernel(feat_hbm, one_ref, rest_ref, *refs, steps):
-    parts, (x_ref, factor_ref, feat_ref, rows_ref, sems, feat_sems) = refs[:-6], refs[-6:]
+def picked_kernel(one_ref, rest_ref, *refs, steps):
+    parts, (x_ref, factor_ref, rows_ref) = refs[:-3], refs[-3:]
     total, full = x_ref.shape
-    loads = feat_sems.shape[0]
     classes = total // steps
     main = rows_ref.shape[1]
     tail = full - main
-    copies = []
     at = 0
-    for i, part in enumerate(parts):
-        copies.append(pltpu.make_async_copy(part, rows_ref.at[at : at + part.shape[0]], sems.at[i]))
-        copies[-1].start()
+    for part in parts:
+        rows_ref[at : at + part.shape[0], :] = part[...]
         at += part.shape[0]
-    feat_copies = []
-    for i in range(loads):
-        col = slice(i * full // loads, (i + 1) * full // loads)
-        feat_copies.append(pltpu.make_async_copy(feat_hbm.at[:, col], feat_ref.at[:, col], feat_sems.at[i]))
-        feat_copies[-1].start()
-    for copy in copies:
-        copy.wait()
     x_ref[:, :main] = jnp.dot(one_ref[...], rows_ref[...], preferred_element_type=f32).astype(bf16)
     for s in range(steps):
         at = slice(s * classes, (s + 1) * classes)
@@ -249,27 +250,16 @@
         for j in range(i + 1):
             packed = jnp.where(lane == i * steps + j, factor[i][j], packed)
     factor_ref[...] = packed
-    for copy in feat_copies:
-        copy.wait()
-
-
-def masks_of(n_ex):
-    masks = [0]
-    mask = n_ex // 2
-    while mask > 4:
-        masks = masks + [m ^ mask for m in masks]
-        mask //= 2
-    return masks + [m ^ 4 for m in masks] + [m ^ 2 for m in masks] + [m ^ 6 for m in masks]
-
-
-def half_products(side, code_ref, x_ref, feat_ref, target_ref, target_at, left_ref, *, n_ex, classes):
+
+
+def half_products(side, code_ref, x_ref, feat_ref, target_ref, target_at, left_ref, *, classes):
     half = left_ref.shape[1]
+    far = code_ref.shape[0] // 4
     width = half // code_ref.shape[0]
     used = left_ref.shape[0] - classes
-    group = lax.axis_index("ex") // 2
     here = pl.ds(pl.multiple_of(side * half, half), half)
-    for k, mask in enumerate(masks_of(n_ex)):
-        block = group ^ (mask // 2)
+    for k in range(4 * far):
+        block = k % far * 4 + near_id((0, 4, 2, 6)[k // far])
         target = decode(code_ref[k], classes)[0]
         target_ref[:, pl.ds(pl.multiple_of(target_at + block * width, width), width)] = target
         left_ref[:classes, pl.ds(pl.multiple_of(block * width, width), width)] = target.astype(bf16)
@@ -278,22 +268,22 @@
     return right, nt_dot(left_ref[...], feat_ref[:, here])
 
 
-def half_kernel(feat_ref, code_ref, x_ref, direct_ref, right_ref, target_ref, left_ref, *, n_ex, classes):
+def half_kernel(feat_ref, code_ref, x_ref, direct_ref, right_ref, target_ref, left_ref, *, classes):
     core = lax.axis_index("ex") % 2
     right_ref[...], direct_ref[...] = half_products(
-        core, code_ref, x_ref, feat_ref, target_ref, 0, left_ref, n_ex=n_ex, classes=classes
+        core, code_ref, x_ref, feat_ref, target_ref, 0, left_ref, classes=classes
     )
 
 
 def pursuit_kernel(
     labels_ref, feat_ref, x_ref, factor_ref, direct_own, right_own, target_own, code_ref,
-    scores_ref, resid_hbm, resid_ref, left_ref, sems, *, n_ex, steps, scale
+    scores_ref, resid_hbm, resid_ref, left_ref, sems, *, steps, scale
 ):
     classes, full = resid_ref.shape
     half = full // 2
     core = lax.axis_index("ex") % 2
     right, direct = half_products(
-        1 - core, code_ref, x_ref, feat_ref, resid_ref, (1 - core) * half, left_ref, n_ex=n_ex, classes=classes
+        1 - core, code_ref, x_ref, feat_ref, resid_ref, (1 - core) * half, left_ref, classes=classes
     )
     right = right + right_own[...]
     rhs = [diagonal(right[:, a * classes : (a + 1) * classes]) for a in range(steps)]
@@ -330,60 +320,60 @@
     width = full // n_ex
     total = steps * classes
     main = full * steps * slots // 8
-    limit = pltpu.CompilerParams(vmem_limit_bytes=24 << 20)
+    limit = pltpu.CompilerParams(vmem_limit_bytes=16 << 20)
     vmem = pl.BlockSpec(memory_space=pltpu.VMEM)
     hbm = pl.BlockSpec(memory_space=pltpu.HBM)
     anywhere = pl.BlockSpec(memory_space=pl.ANY)
     half = jax.ShapeDtypeStruct((groups * classes + 8, width), f32)
-    codes = jax.ShapeDtypeStruct((groups, classes * (width // 128) + 8, 128), jnp.int16)
-    features, picks, labels_in = [
-        pltpu.with_memory_space_constraint(a, pltpu.HBM) for a in (features, pick_index, labels)
-    ]
+    code = jax.ShapeDtypeStruct((groups // 4, classes * (width // 128) + 8, 128), jnp.int16)
 
     def swap(x, mask):
         return lax.ppermute(x, "ex", [(d, d ^ mask) for d in range(n_ex)])
 
-    def trade(x):
-        teams = [[s + 2 * k for k in range(groups)] for s in range(2)]
-        return lax.all_to_all(x, "ex", 0, 0, axis_index_groups=teams, tiled=True)
-
-    send, keep, packed = pl.pallas_call(
+    def after(x, *others):
+        return lax.optimization_barrier((x,) + others)[0]
+
+    feat, send, keep, packed = pl.pallas_call(
         functools.partial(sums_kernel, n_ex=n_ex),
         in_specs=[hbm] * 3,
-        out_specs=[vmem] * 3,
-        out_shape=[half, half, jax.ShapeDtypeStruct((8, main), bf16)],
+        out_specs=[vmem] * 4,
+        out_shape=[pltpu.VMEM((rows, full), bf16), half, half, jax.ShapeDtypeStruct((8, main), bf16)],
         scratch_shapes=[
             pltpu.VMEM(labels.shape, jnp.int32),
             pltpu.VMEM(pick_index.shape, jnp.int32),
-            pltpu.VMEM((rows, full), bf16),
             pltpu.VMEM((classes + 16, rows), bf16),
             pltpu.VMEM((8, full), f32),
             pltpu.SemaphoreType.DMA((n_ex + 2,)),
         ],
         compiler_params=limit,
         name="class_sums",
-    )(labels_in, picks, features)
-
-    got = swap(send, 1)
-    codes_out = pl.pallas_call(
+    )(*[pltpu.with_memory_space_constraint(a, pltpu.HBM) for a in (labels, pick_index, features)])
+
+    def add(codes, last):
+        return pl.pallas_call(
+            functools.partial(add_kernel, classes=classes, last=last),
+            in_specs=[vmem] * len(codes),
+            out_specs=vmem,
+            out_shape=code,
+            compiler_params=limit,
+            name="add_sums",
+        )(*codes)
+
+    far_masks = [8 << b for b in range(n_ex.bit_length() - 4)]
+    codes = pl.pallas_call(
         functools.partial(pair_kernel, classes=classes),
         in_specs=[vmem] * 2,
-        out_specs=vmem,
-        out_shape=codes,
+        out_specs=[vmem] * 4,
+        out_shape=[code] * 4,
         compiler_params=limit,
         name="pair_sums",
-    )(keep, got)
-    pick_late, packed, _ = lax.optimization_barrier((pick_index, packed, codes_out))
-
-    def along_z(x):
-        mask = n_ex // 2
-        while mask > 4:
-            x = jnp.concatenate([x, swap(x, mask)], axis=0)
-            mask //= 2
-        return x
-
-    near = along_z(packed)
+    )(keep, swap(send, 1))
+    near = packed
+    for mask in reversed(far_masks):
+        near = jnp.concatenate([near, after(swap(near, mask), codes[0])], axis=0)
     parts = [near, swap(near, 4), swap(near, 2), swap(near, 6)]
+
+    part_sum = add([codes[0], swap(codes[1], 4), swap(codes[2], 2), swap(codes[3], 6)], False)
     one, rest = pl.pallas_call(
         functools.partial(select_kernel, n_ex=n_ex, rows=rows),
         in_specs=[vmem],
@@ -391,46 +381,32 @@
         out_shape=[jax.ShapeDtypeStruct((total, n_ex * 8), bf16)] * 2,
         compiler_params=limit,
         name="selectors",
-    )(pick_late)
-
-    traded, _ = lax.optimization_barrier((trade(codes_out), parts[0]))
-    summed = pl.pallas_call(
-        functools.partial(total_kernel, classes=classes),
-        in_specs=[vmem],
-        out_specs=vmem,
-        out_shape=jax.ShapeDtypeStruct((1,) + codes.shape[1:], codes.dtype),
-        compiler_params=limit,
-        name="total_sums",
-    )(traded)
-    near = along_z(summed)
-    parts, _ = lax.optimization_barrier((parts, near))
-    own_parts = [near, swap(near, 4), swap(near, 2), swap(near, 6)]
+    )(after(pick_index, part_sum))
+    for mask in far_masks:
+        part_sum = add([part_sum, after(swap(part_sum, mask), one)], mask == far_masks[-1])
+    own_parts = [part_sum, swap(part_sum, 4), swap(part_sum, 2), swap(part_sum, 6)]
+    parts = [after(p, part_sum) for p in parts]
     parts = parts + [swap(p, 1) for p in parts]
 
-    x, factor, features_in = pl.pallas_call(
+    x, factor = pl.pallas_call(
         functools.partial(picked_kernel, steps=steps),
-        in_specs=[hbm] + [vmem] * 2 + [anywhere] * len(parts),
-        out_specs=[vmem] * 3,
+        in_specs=[vmem] * (2 + len(parts)),
+        out_specs=[vmem] * 2,
         out_shape=[
             jax.ShapeDtypeStruct((total, full), bf16),
             jax.ShapeDtypeStruct((classes, 128), f32),
-            pltpu.VMEM((rows, full), bf16),
         ],
-        scratch_shapes=[
-            pltpu.VMEM((n_ex * 8, main), bf16),
-            pltpu.SemaphoreType.DMA((len(parts),)),
-            pltpu.SemaphoreType.DMA((n_ex,)),
-        ],
+        scratch_shapes=[pltpu.VMEM((n_ex * 8, main), bf16)],
         compiler_params=limit,
         name="picked_rows",
-    )(features, one, rest, *parts)
+    )(one, rest, *parts)
 
     own_parts, x = lax.optimization_barrier((own_parts, x))
     own_half = jnp.concatenate(own_parts, axis=0)
     twin_half = swap(own_half, 1)
     left = pltpu.VMEM((total, full // 2), bf16)
     direct, right, target = pl.pallas_call(
-        functools.partial(half_kernel, n_ex=n_ex, classes=classes),
+        functools.partial(half_kernel, classes=classes),
         in_specs=[vmem] * 3,
         out_specs=[vmem] * 3,
         out_shape=[
@@ -441,10 +417,10 @@
         scratch_shapes=[left],
         compiler_params=limit,
         name="own_half_products",
-    )(features_in, own_half, x)
+    )(feat, own_half, x)
 
     scores, resid = pl.pallas_call(
-        functools.partial(pursuit_kernel, n_ex=n_ex, steps=steps, scale=1.0 / math.sqrt(full)),
+        functools.partial(pursuit_kernel, steps=steps, scale=1.0 / math.sqrt(full)),
         in_specs=[vmem] * 8,
         out_specs=[vmem, anywhere],
         out_shape=[
@@ -454,7 +430,7 @@
         scratch_shapes=[pltpu.VMEM((classes, full), f32), left, pltpu.SemaphoreType.DMA((4,))],
         compiler_params=limit,
         name="pursuit",
-    )(labels, features_in, x, factor, direct, right, target, twin_half)
+    )(labels, feat, x, factor, direct, right, target, twin_half)
     return scores, resid
 
 

time: 58.6 us -> 46.8 us (0.80)
  waiting for transfers between devices: 20.3 us -> 14.3 us
  Pallas kernels: 18.2 us -> 12.9 us
    all_to_all x1 -> x0, starting transfers between devices: 7.2 us -> none  [trade(): return lax.all_to_all(x, 'ex', 0, 0, axis_index_groups=teams, tiled=True)]
    ppermute x14 -> x17, starting transfers between devices: 11.7 us -> 18.6 us  [swap(): return lax.ppermute(x, 'ex', [(d, d ^ mask) for d in range(n_ex)])]
    ppermute x14 -> x17, waiting for transfers between devices: 20.3 us -> 14.3 us  [swap(): return lax.ppermute(x, 'ex', [(d, d ^ mask) for d in range(n_ex)])]
    pallas_call x4 -> x5, Pallas kernels: 11.9 us -> 7.29 us  [the longest x1 3.33 us: on_device(): pl.pallas_call(functools.partial(pursuit_kernel, steps=steps, scale=1.0 /...]
    pallas_call x1, Pallas kernels: 0.89 us -> 0.18 us  [on_device(): pl.pallas_call(functools.partial(pair_kernel, classes=classes), in_specs=...]
  transfers between devices with their start and end apart: 15 -> 17, of which waited for: 6 -> 7; matrix products, arithmetic and copies ran while one was open for 0% -> 0% of each run, Pallas kernels for 15% -> 10%
where the time goes in v7:
time: 46.8 us; the launch traced here: 46.7 us
  starting transfers between devices  18.6 us (40%)
  waiting for transfers between devices  14.3 us (31%)
  Pallas kernels  12.9 us (28%)
  between operations  0.76 us (2%)
    ppermute x17, starting transfers between devices, swap(): return lax.ppermute(x, 'ex', [(d, d ^ mask) for d in range(n_ex)])  18.6 us
    ppermute x17, waiting for transfers between devices, swap(): return lax.ppermute(x, 'ex', [(d, d ^ mask) for d in range(n_ex)])  14.3 us
    pallas_call x1, Pallas kernels, on_device(): pl.pallas_call(functools.partial(sums_kernel, n_ex=n_ex), in_specs=[hbm]...  5.06 us
    pallas_call x1, Pallas kernels, on_device(): pl.pallas_call(functools.partial(pursuit_kernel, steps=steps, scale=1.0 /...  3.33 us
    pallas_call x1, Pallas kernels, on_device(): pl.pallas_call(functools.partial(half_kernel, classes=classes), in_specs=...  2.02 us
    pallas_call x1, Pallas kernels, on_device(): pl.pallas_call(functools.partial(picked_kernel, steps=steps), in_specs=[v...  1.39 us
  transfers between devices with their start and end apart: 17, of which 7 were waited for; matrix products, arithmetic and copies ran while one was open for 0% of the time, Pallas kernels for 10%

profile of v7, /device:TPU:0, one launch (start us, length us, event | category | flops | bytes accessed | tf_op | source)
XLA Modules:
  0.0 46.7 jit_solution(2574919769006900847)
XLA Ops:
  0.6 5.1 %class_sums.1 = (bf16[640,8192]{1,0:T(8,128)(2,1)S(1)}, f32[264,512]{1,0:T(8,128)S(1)}, f32[264,512]{1,0:T(8,128)S(1)}, bf16[8,6144]{1,0:T(8,128)(2,1)S(1)}) custom-call(s32[640]{0:T(1024)} %labels_ref.1, s32[3,32]{1,0:T(4,128)} %pick_ref, bf16[640,8192]{1,0:T(8,128)(2,1)} %feat_hbm.1), custom_call_target="tpu_custom_call" | custom-call | tf_op jit(solution)/shard_map/class_sums/pallas_call | solution.py:336
  5.7 0.0 copy-start
  5.7 4.1 %collective-permute-start.8 = (bf16[8,6144]{1,0:T(8,128)(2,1)S(1)}, bf16[8,6144]{1,0:T(8,128)(2,1)S(1)}, u32[]{:S(2)}, u32[]{:S(2)}) collective-permute-start(bf16[8,6144]{1,0:T(8,128)(2,1)S(1)} %get-tuple-element.40), channel_id=1, source_target_pairs={{0,8},{1,9},{2,10},{3,11},{4,12},{5,13},{6,14},{7,15},{8,0},{9,1},... | collective-permute-start | bytes 294920 | tf_op jit(solution)/shard_map/ppermute | solution.py:331
  9.8 1.9 %collective-permute-done.got_ref = f32[264,512]{1,0:T(8,128)S(1)} collective-permute-done((f32[264,512]{1,0:T(8,128)S(1)}, f32[264,512]{1,0:T(8,128)S(1)}, u32[]{:S(2)}, u32[]{:S(2)}) %collective-permute-start) | collective-permute-done | bytes 540704 | tf_op jit(solution)/shard_map/ppermute | solution.py:331
  11.8 0.2 pair_sums.1
  11.9 2.8 %collective-permute-done.8 = bf16[8,6144]{1,0:T(8,128)(2,1)S(1)} collective-permute-done((bf16[8,6144]{1,0:T(8,128)(2,1)S(1)}, bf16[8,6144]{1,0:T(8,128)(2,1)S(1)}, u32[]{:S(2)}, u32[]{:S(2)}) %collective-permute-start.8) | collective-permute-done | bytes 98336 | tf_op jit(solution)/shard_map/ppermute | solution.py:331
  14.7 0.7 %collective-permute-start.1 = (s16[2,136,128]{2,1,0:T(8,128)(2,1)S(1)}, s16[2,136,128]{2,1,0:T(8,128)(2,1)S(1)}, u32[]{:S(2)}, u32[]{:S(2)}) collective-permute-start(s16[2,136,128]{2,1,0:T(8,128)(2,1)S(1)} %get-tuple-element.33), channel_id=1, source_target_pairs={{0,4},{1,5},{2,6},{3,7},{4,0},{5,1},{6,2},{7,3},{8,12},{9,13},{10,... | collective-permute-start | bytes 208904 | tf_op jit(solution)/shard_map/ppermute | solution.py:331
  15.5 2.4 %collective-permute-start.11 = (bf16[16,6144]{1,0:T(8,128)(2,1)S(1)}, bf16[16,6144]{1,0:T(8,128)(2,1)S(1)}, u32[]{:S(2)}, u32[]{:S(2)}) collective-permute-start(bf16[16,6144]{1,0:T(8,128)(2,1)S(1)} %constant_dynamic-update-slice_fusion.refs_0_), channel_id=1, source_target_pairs={{0,6},{1,7},{2,4},{3,5},{4,2},{5,3},{6,0},{7,1},{8,14},{9,15},{10,... | collective-permute-start | bytes 589832 | tf_op jit(solution)/shard_map/ppermute | solution.py:331
  17.8 0.5 collective-permute-start.2
  18.3 1.7 %collective-permute-start.3 = (s16[2,136,128]{2,1,0:T(8,128)(2,1)S(1)}, s16[2,136,128]{2,1,0:T(8,128)(2,1)S(1)}, u32[]{:S(2)}, u32[]{:S(2)}) collective-permute-start(s16[2,136,128]{2,1,0:T(8,128)(2,1)S(1)} %get-tuple-element.35), channel_id=1, source_target_pairs={{0,6},{1,7},{2,4},{3,5},{4,2},{5,3},{6,0},{7,1},{8,14},{9,15},{10,... | collective-permute-start | bytes 208904 | tf_op jit(solution)/shard_map/ppermute | solution.py:331
  20.0 0.5 %collective-permute-start.10 = (bf16[16,6144]{1,0:T(8,128)(2,1)S(1)}, bf16[16,6144]{1,0:T(8,128)(2,1)S(1)}, u32[]{:S(2)}, u32[]{:S(2)}) collective-permute-start(bf16[16,6144]{1,0:T(8,128)(2,1)S(1)} %constant_dynamic-update-slice_fusion.refs_0_), channel_id=1, source_target_pairs={{0,2},{1,3},{2,0},{3,1},{4,6},{5,7},{6,4},{7,5},{8,10},{9,11},{10,... | collective-permute-start | bytes 589832 | tf_op jit(solution)/shard_map/ppermute | solution.py:331
  20.5 1.3 %collective-permute-start.9 = (bf16[16,6144]{1,0:T(8,128)(2,1)S(1)}, bf16[16,6144]{1,0:T(8,128)(2,1)S(1)}, u32[]{:S(2)}, u32[]{:S(2)}) collective-permute-start(bf16[16,6144]{1,0:T(8,128)(2,1)S(1)} %constant_dynamic-update-slice_fusion.refs_0_), channel_id=1, source_target_pairs={{0,4},{1,5},{2,6},{3,7},{4,0},{5,1},{6,2},{7,3},{8,12},{9,13},{10,... | collective-permute-start | bytes 589832 | tf_op jit(solution)/shard_map/ppermute | solution.py:331
  21.8 4.9 %collective-permute-done.2.refs_2_ = s16[2,136,128]{2,1,0:T(8,128)(2,1)S(1)} collective-permute-done((s16[2,136,128]{2,1,0:T(8,128)(2,1)S(1)}, s16[2,136,128]{2,1,0:T(8,128)(2,1)S(1)}, u32[]{:S(2)}, u32[]{:S(2)}) %collective-permute-start.2) | collective-permute-done | bytes 69664 | tf_op jit(solution)/shard_map/ppermute | solution.py:331
  26.7 0.3 add_sums.2.refs_0_
  27.0 2.8 %collective-permute-start.4 = (s16[2,136,128]{2,1,0:T(8,128)(2,1)S(1)}, s16[2,136,128]{2,1,0:T(8,128)(2,1)S(1)}, u32[]{:S(2)}, u32[]{:S(2)}) collective-permute-start(s16[2,136,128]{2,1,0:T(8,128)(2,1)S(1)} %add_sums.2.refs_0_), channel_id=1, source_target_pairs={{0,8},{1,9},{2,10},{3,11},{4,12},{5,13},{6,14},{7,15},{8,0},{9,1},... | collective-permute-start | bytes 208904 | tf_op jit(solution)/shard_map/ppermute | solution.py:331
  29.8 0.4 selectors.1
  30.2 2.5 %collective-permute-done.4.refs_1_ = s16[2,136,128]{2,1,0:T(8,128)(2,1)S(1)} collective-permute-done((s16[2,136,128]{2,1,0:T(8,128)(2,1)S(1)}, s16[2,136,128]{2,1,0:T(8,128)(2,1)S(1)}, u32[]{:S(2)}, u32[]{:S(2)}) %collective-permute-start.4) | collective-permute-done | bytes 69664 | tf_op jit(solution)/shard_map/ppermute | solution.py:331
  32.7 0.3 add_sums.3
  33.0 0.1 collective-permute-start.12
  33.1 0.5 %collective-permute-start.15 = (bf16[16,6144]{1,0:T(8,128)(2,1)S(1)}, bf16[16,6144]{1,0:T(8,128)(2,1)S(1)}, u32[]{:S(2)}, u32[]{:S(2)}) collective-permute-start(bf16[16,6144]{1,0:T(8,128)(2,1)S(1)} %collective-permute-done.11.refs_3_), channel_id=1, source_target_pairs={{0,1},{1,0},{2,3},{3,2},{4,5},{5,4},{6,7},{7,6},{8,9},{9,8},{10,11... | collective-permute-start | bytes 589832 | tf_op jit(solution)/shard_map/ppermute | solution.py:331
  33.6 0.1 collective-permute-start.14
  33.6 0.4 collective-permute-start.13
  34.1 1.7 %collective-permute-start.7 = (s16[2,136,128]{2,1,0:T(8,128)(2,1)S(1)}, s16[2,136,128]{2,1,0:T(8,128)(2,1)S(1)}, u32[]{:S(2)}, u32[]{:S(2)}) collective-permute-start(s16[2,136,128]{2,1,0:T(8,128)(2,1)S(1)} %add_sums.3), channel_id=1, source_target_pairs={{0,6},{1,7},{2,4},{3,5},{4,2},{5,3},{6,0},{7,1},{8,14},{9,15},{10,... | collective-permute-start | bytes 208904 | tf_op jit(solution)/shard_map/ppermute | solution.py:331
  35.7 1.1 %collective-permute-start.6 = (s16[2,136,128]{2,1,0:T(8,128)(2,1)S(1)}, s16[2,136,128]{2,1,0:T(8,128)(2,1)S(1)}, u32[]{:S(2)}, u32[]{:S(2)}) collective-permute-start(s16[2,136,128]{2,1,0:T(8,128)(2,1)S(1)} %add_sums.3), channel_id=1, source_target_pairs={{0,2},{1,3},{2,0},{3,1},{4,6},{5,7},{6,4},{7,5},{8,10},{9,11},{10,... | collective-permute-start | bytes 208904 | tf_op jit(solution)/shard_map/ppermute | solution.py:331
  36.8 0.7 %collective-permute-start.5 = (s16[2,136,128]{2,1,0:T(8,128)(2,1)S(1)}, s16[2,136,128]{2,1,0:T(8,128)(2,1)S(1)}, u32[]{:S(2)}, u32[]{:S(2)}) collective-permute-start(s16[2,136,128]{2,1,0:T(8,128)(2,1)S(1)} %add_sums.3), channel_id=1, source_target_pairs={{0,4},{1,5},{2,6},{3,7},{4,0},{5,1},{6,2},{7,3},{8,12},{9,13},{10,... | collective-permute-start | bytes 208904 | tf_op jit(solution)/shard_map/ppermute | solution.py:331
  37.6 1.4 %picked_rows.1 = (bf16[96,8192]{1,0:T(8,128)(2,1)S(1)}, f32[32,128]{1,0:T(8,128)S(1)}) custom-call(bf16[96,128]{1,0:T(8,128)(2,1)S(1)} %get-tuple-element.37.one_ref, bf16[96,128]{1,0:T(8,128)(2,1)S(1)} %get-tuple-element.39.rest_ref, bf16[16,6144]{1,0:T(8,128)(2,1)S(1)} %constant_dynamic-update-slice_fusion.refs_0_, ...), custom_call_target="tpu_custom_call" | custom-call | tf_op jit(solution)/shard_map/picked_rows/pallas_call | solution.py:391
  39.0 0.4 collective-permute-done.7
  39.3 1.3 %collective-permute-done.6 = s16[2,136,128]{2,1,0:T(8,128)(2,1)S(1)} collective-permute-done((s16[2,136,128]{2,1,0:T(8,128)(2,1)S(1)}, s16[2,136,128]{2,1,0:T(8,128)(2,1)S(1)}, u32[]{:S(2)}, u32[]{:S(2)}) %collective-permute-start.6) | collective-permute-done | bytes 69664 | tf_op jit(solution)/shard_map/ppermute | solution.py:331
  40.6 0.5 %collective-permute-done.5 = s16[2,136,128]{2,1,0:T(8,128)(2,1)S(1)} collective-permute-done((s16[2,136,128]{2,1,0:T(8,128)(2,1)S(1)}, s16[2,136,128]{2,1,0:T(8,128)(2,1)S(1)}, u32[]{:S(2)}, u32[]{:S(2)}) %collective-permute-start.5) | collective-permute-done | bytes 69664 | tf_op jit(solution)/shard_map/ppermute | solution.py:331
  41.2 0.1 collective-permute-start.16
  41.3 2.0 %own_half_products.1 = (f32[96,640]{1,0:T(8,128)S(1)}, f32[32,96]{1,0:T(8,128)S(1)}, f32[32,4096]{1,0:T(8,128)S(1)}) custom-call(bf16[640,8192]{1,0:T(8,128)(2,1)S(1)} %get-tuple-element.29.feat_ref, s16[8,136,128]{2,1,0:T(8,128)(2,1)S(1)} %constant_dynamic-update-slice_fusion.2.code_ref, bf16[96,8192]{1,0:T(8,128)(2,1)S(1)} %get-tuple-element.47.x_ref), custom_call_target="tpu_custom_call" | custom-call | tf_op jit(solution)/shard_map/own_half_products/pallas_call | solution.py:408
  43.3 3.3 %pursuit.1 = (f32[3,640]{1,0:T(4,128)}, f32[32,8192]{1,0:T(8,128)}) custom-call(s32[640]{0:T(1024)S(1)} %copy-done, bf16[640,8192]{1,0:T(8,128)(2,1)S(1)} %get-tuple-element.29.feat_ref, bf16[96,8192]{1,0:T(8,128)(2,1)S(1)} %get-tuple-element.47.x_ref, f32[32,128]{1,0:T(8,128)S(1)} %get-tuple-element.48.factor_ref, ...), custom_call_target="tpu_custom_call" | custom-call | tf_op jit(solution)/shard_map/pursuit/pallas_call | solution.py:422
  (20 shorter events, 0.1 us)
Async XLA Ops:
  0.6 29.2 %copy-start.1 = (s32[3,32]{1,0:T(4,128)S(1)}, s32[3,32]{1,0:T(4,128)}, u32[]{:S(2)}) copy-start(s32[3,32]{1,0:T(4,128)} %pick_ref) | copy-start | bytes 1156
  5.7 37.6 %copy-start = (s32[640]{0:T(1024)S(1)}, s32[640]{0:T(1024)}, u32[]{:S(2)}) copy-start(s32[640]{0:T(1024)} %labels_ref.1) | copy-start | bytes 7684
  5.7 9.0 %collective-permute-start.8 = (bf16[8,6144]{1,0:T(8,128)(2,1)S(1)}, bf16[8,6144]{1,0:T(8,128)(2,1)S(1)}, u32[]{:S(2)}, u32[]{:S(2)}) collective-permute-start(bf16[8,6144]{1,0:T(8,128)(2,1)S(1)} %get-tuple-element.40), channel_id=1, source_target_pairs={{0,8},{1,9},{2,10},{3,11},{4,12},{5,13},{6,14},{7,15},{8,0},{9,1},... | collective-permute-start | bytes 294920 | tf_op jit(solution)/shard_map/ppermute | solution.py:331
  9.8 1.9 %collective-permute-start = (f32[264,512]{1,0:T(8,128)S(1)}, f32[264,512]{1,0:T(8,128)S(1)}, u32[]{:S(2)}, u32[]{:S(2)}) collective-permute-start(f32[264,512]{1,0:T(8,128)S(1)} %get-tuple-element.31), channel_id=1, source_target_pairs={{0,1},{1,0},{2,3},{3,2},{4,5},{5,4},{6,7},{7,6},{8,9},{9,8},{10,11... | collective-permute-start | bytes 1622024 | tf_op jit(solution)/shard_map/ppermute | solution.py:331
  14.7 5.7 %collective-permute-start.1 = (s16[2,136,128]{2,1,0:T(8,128)(2,1)S(1)}, s16[2,136,128]{2,1,0:T(8,128)(2,1)S(1)}, u32[]{:S(2)}, u32[]{:S(2)}) collective-permute-start(s16[2,136,128]{2,1,0:T(8,128)(2,1)S(1)} %get-tuple-element.33), channel_id=1, source_target_pairs={{0,4},{1,5},{2,6},{3,7},{4,0},{5,1},{6,2},{7,3},{8,12},{9,13},{10,... | collective-permute-start | bytes 208904 | tf_op jit(solution)/shard_map/ppermute | solution.py:331
  15.5 17.6 %collective-permute-start.11 = (bf16[16,6144]{1,0:T(8,128)(2,1)S(1)}, bf16[16,6144]{1,0:T(8,128)(2,1)S(1)}, u32[]{:S(2)}, u32[]{:S(2)}) collective-permute-start(bf16[16,6144]{1,0:T(8,128)(2,1)S(1)} %constant_dynamic-update-slice_fusion.refs_0_), channel_id=1, source_target_pairs={{0,6},{1,7},{2,4},{3,5},{4,2},{5,3},{6,0},{7,1},{8,14},{9,15},{10,... | collective-permute-start | bytes 589832 | tf_op jit(solution)/shard_map/ppermute | solution.py:331
  17.8 8.9 %collective-permute-start.2 = (s16[2,136,128]{2,1,0:T(8,128)(2,1)S(1)}, s16[2,136,128]{2,1,0:T(8,128)(2,1)S(1)}, u32[]{:S(2)}, u32[]{:S(2)}) collective-permute-start(s16[2,136,128]{2,1,0:T(8,128)(2,1)S(1)} %get-tuple-element.34), channel_id=1, source_target_pairs={{0,2},{1,3},{2,0},{3,1},{4,6},{5,7},{6,4},{7,5},{8,10},{9,11},{10,... | collective-permute-start | bytes 208904 | tf_op jit(solution)/shard_map/ppermute | solution.py:331
  18.3 8.4 %collective-permute-start.3 = (s16[2,136,128]{2,1,0:T(8,128)(2,1)S(1)}, s16[2,136,128]{2,1,0:T(8,128)(2,1)S(1)}, u32[]{:S(2)}, u32[]{:S(2)}) collective-permute-start(s16[2,136,128]{2,1,0:T(8,128)(2,1)S(1)} %get-tuple-element.35), channel_id=1, source_target_pairs={{0,6},{1,7},{2,4},{3,5},{4,2},{5,3},{6,0},{7,1},{8,14},{9,15},{10,... | collective-permute-start | bytes 208904 | tf_op jit(solution)/shard_map/ppermute | solution.py:331
  20.0 13.6 %collective-permute-start.10 = (bf16[16,6144]{1,0:T(8,128)(2,1)S(1)}, bf16[16,6144]{1,0:T(8,128)(2,1)S(1)}, u32[]{:S(2)}, u32[]{:S(2)}) collective-permute-start(bf16[16,6144]{1,0:T(8,128)(2,1)S(1)} %constant_dynamic-update-slice_fusion.refs_0_), channel_id=1, source_target_pairs={{0,2},{1,3},{2,0},{3,1},{4,6},{5,7},{6,4},{7,5},{8,10},{9,11},{10,... | collective-permute-start | bytes 589832 | tf_op jit(solution)/shard_map/ppermute | solution.py:331
  20.5 13.2 %collective-permute-start.9 = (bf16[16,6144]{1,0:T(8,128)(2,1)S(1)}, bf16[16,6144]{1,0:T(8,128)(2,1)S(1)}, u32[]{:S(2)}, u32[]{:S(2)}) collective-permute-start(bf16[16,6144]{1,0:T(8,128)(2,1)S(1)} %constant_dynamic-update-slice_fusion.refs_0_), channel_id=1, source_target_pairs={{0,4},{1,5},{2,6},{3,7},{4,0},{5,1},{6,2},{7,3},{8,12},{9,13},{10,... | collective-permute-start | bytes 589832 | tf_op jit(solution)/shard_map/ppermute | solution.py:331
  27.0 5.7 %collective-permute-start.4 = (s16[2,136,128]{2,1,0:T(8,128)(2,1)S(1)}, s16[2,136,128]{2,1,0:T(8,128)(2,1)S(1)}, u32[]{:S(2)}, u32[]{:S(2)}) collective-permute-start(s16[2,136,128]{2,1,0:T(8,128)(2,1)S(1)} %add_sums.2.refs_0_), channel_id=1, source_target_pairs={{0,8},{1,9},{2,10},{3,11},{4,12},{5,13},{6,14},{7,15},{8,0},{9,1},... | collective-permute-start | bytes 208904 | tf_op jit(solution)/shard_map/ppermute | solution.py:331
  33.0 2.8 %collective-permute-start.12 = (bf16[16,6144]{1,0:T(8,128)(2,1)S(1)}, bf16[16,6144]{1,0:T(8,128)(2,1)S(1)}, u32[]{:S(2)}, u32[]{:S(2)}) collective-permute-start(bf16[16,6144]{1,0:T(8,128)(2,1)S(1)} %constant_dynamic-update-slice_fusion.refs_0_), channel_id=1, source_target_pairs={{0,1},{1,0},{2,3},{3,2},{4,5},{5,4},{6,7},{7,6},{8,9},{9,8},{10,11... | collective-permute-start | bytes 589832 | tf_op jit(solution)/shard_map/ppermute | solution.py:331
  33.1 3.8 %collective-permute-start.15 = (bf16[16,6144]{1,0:T(8,128)(2,1)S(1)}, bf16[16,6144]{1,0:T(8,128)(2,1)S(1)}, u32[]{:S(2)}, u32[]{:S(2)}) collective-permute-start(bf16[16,6144]{1,0:T(8,128)(2,1)S(1)} %collective-permute-done.11.refs_3_), channel_id=1, source_target_pairs={{0,1},{1,0},{2,3},{3,2},{4,5},{5,4},{6,7},{7,6},{8,9},{9,8},{10,11... | collective-permute-start | bytes 589832 | tf_op jit(solution)/shard_map/ppermute | solution.py:331
  33.6 4.0 %collective-permute-start.14 = (bf16[16,6144]{1,0:T(8,128)(2,1)S(1)}, bf16[16,6144]{1,0:T(8,128)(2,1)S(1)}, u32[]{:S(2)}, u32[]{:S(2)}) collective-permute-start(bf16[16,6144]{1,0:T(8,128)(2,1)S(1)} %collective-permute-done.10.refs_2_), channel_id=1, source_target_pairs={{0,1},{1,0},{2,3},{3,2},{4,5},{5,4},{6,7},{7,6},{8,9},{9,8},{10,11... | collective-permute-start | bytes 589832 | tf_op jit(solution)/shard_map/ppermute | solution.py:331
  33.6 3.9 %collective-permute-start.13 = (bf16[16,6144]{1,0:T(8,128)(2,1)S(1)}, bf16[16,6144]{1,0:T(8,128)(2,1)S(1)}, u32[]{:S(2)}, u32[]{:S(2)}) collective-permute-start(bf16[16,6144]{1,0:T(8,128)(2,1)S(1)} %collective-permute-done.9.refs_1_), channel_id=1, source_target_pairs={{0,1},{1,0},{2,3},{3,2},{4,5},{5,4},{6,7},{7,6},{8,9},{9,8},{10,11... | collective-permute-start | bytes 589832 | tf_op jit(solution)/shard_map/ppermute | solution.py:331
  34.1 5.3 %collective-permute-start.7 = (s16[2,136,128]{2,1,0:T(8,128)(2,1)S(1)}, s16[2,136,128]{2,1,0:T(8,128)(2,1)S(1)}, u32[]{:S(2)}, u32[]{:S(2)}) collective-permute-start(s16[2,136,128]{2,1,0:T(8,128)(2,1)S(1)} %add_sums.3), channel_id=1, source_target_pairs={{0,6},{1,7},{2,4},{3,5},{4,2},{5,3},{6,0},{7,1},{8,14},{9,15},{10,... | collective-permute-start | bytes 208904 | tf_op jit(solution)/shard_map/ppermute | solution.py:331
  35.7 4.9 %collective-permute-start.6 = (s16[2,136,128]{2,1,0:T(8,128)(2,1)S(1)}, s16[2,136,128]{2,1,0:T(8,128)(2,1)S(1)}, u32[]{:S(2)}, u32[]{:S(2)}) collective-permute-start(s16[2,136,128]{2,1,0:T(8,128)(2,1)S(1)} %add_sums.3), channel_id=1, source_target_pairs={{0,2},{1,3},{2,0},{3,1},{4,6},{5,7},{6,4},{7,5},{8,10},{9,11},{10,... | collective-permute-start | bytes 208904 | tf_op jit(solution)/shard_map/ppermute | solution.py:331
  36.8 4.3 %collective-permute-start.5 = (s16[2,136,128]{2,1,0:T(8,128)(2,1)S(1)}, s16[2,136,128]{2,1,0:T(8,128)(2,1)S(1)}, u32[]{:S(2)}, u32[]{:S(2)}) collective-permute-start(s16[2,136,128]{2,1,0:T(8,128)(2,1)S(1)} %add_sums.3), channel_id=1, source_target_pairs={{0,4},{1,5},{2,6},{3,7},{4,0},{5,1},{6,2},{7,3},{8,12},{9,13},{10,... | collective-permute-start | bytes 208904 | tf_op jit(solution)/shard_map/ppermute | solution.py:331
  41.2 2.1 %collective-permute-start.16 = (s16[8,136,128]{2,1,0:T(8,128)(2,1)S(1)}, s16[8,136,128]{2,1,0:T(8,128)(2,1)S(1)}, u32[]{:S(2)}, u32[]{:S(2)}) collective-permute-start(s16[8,136,128]{2,1,0:T(8,128)(2,1)S(1)} %constant_dynamic-update-slice_fusion.2.code_ref), channel_id=1, source_target_pairs={{0,1},{1,0},{2,3},{3,2},{4,5},{5,4},{6,7},{7,6},{8,9},{9,8},{10,11... | collective-permute-start | bytes 835592 | tf_op jit(solution)/shard_map/ppermute | solution.py:331

commit v8 on v7

--- a/solution.py
+++ b/solution.py
@@ -51,7 +51,7 @@
 
 
 def sums_kernel(
-    labels_hbm, pick_hbm, feat_hbm, feat_ref, send_ref, keep_ref, rows_ref, labels_ref, pick_ref, left, held, sems, *, n_ex
+    labels_hbm, pick_hbm, feat_hbm, feat_ref, send_ref, keep_ref, held, labels_ref, pick_ref, left, sems, *, n_ex
 ):
     rows, full = feat_ref.shape
     steps, classes = pick_ref.shape
@@ -109,9 +109,10 @@
         ref[k * classes : (k + 1) * classes, :] = both[:classes]
         held[:, columns[i]] = both[classes : classes + 8]
 
+
+def pack_kernel(held, rows_ref, *, steps):
     used = steps * slots
-    main = full * used // 8
-    tail = full - main
+    main = rows_ref.shape[1]
     lines = [held[0:used, :main]]
     for q in range(slots):
         lines.append(jnp.concatenate([held[q * steps + u : q * steps + u + 1, main:] for u in range(steps)], axis=1))
@@ -190,7 +191,7 @@
     return result
 
 
-def select_kernel(pick_ref, one_ref, rest_ref, *, n_ex, rows):
+def select_kernel(pick_ref, one_ref, *, n_ex, rows, tail):
     steps, classes = pick_ref.shape
     lines = one_ref.shape[1]
     device = lax.axis_index("ex")
@@ -211,10 +212,10 @@
     spot = spot + ((away & 1) << (bits - 1))
     step = lax.broadcasted_iota(jnp.int32, pick.shape, 0)
     line = lax.broadcasted_iota(jnp.int32, (lines, classes), 0)
-    for ref, where in ((one_ref, spot * 8 + rank * steps + step), (rest_ref, spot * 8 + slots * steps + rank)):
-        hits = [jnp.where(line == where[s : s + 1, :], 1.0, 0.0) for s in range(steps)]
-        pad = jnp.zeros((lines, 128 - steps * classes), f32)
-        ref[...] = jnp.transpose(jnp.concatenate(hits + [pad], axis=1))[: steps * classes].astype(bf16)
+    where = spot * 8 + (slots * steps + rank if tail else rank * steps + step)
+    hits = [jnp.where(line == where[s : s + 1, :], 1.0, 0.0) for s in range(steps)]
+    pad = jnp.zeros((lines, 128 - steps * classes), f32)
+    one_ref[...] = jnp.transpose(jnp.concatenate(hits + [pad], axis=1))[: steps * classes].astype(bf16)
 
 
 def picked_kernel(one_ref, rest_ref, *refs, steps):
@@ -252,7 +253,7 @@
     factor_ref[...] = packed
 
 
-def half_products(side, code_ref, x_ref, feat_ref, target_ref, target_at, left_ref, *, classes):
+def half_target(side, code_ref, x_ref, target_ref, target_at, left_ref, *, classes):
     half = left_ref.shape[1]
     far = code_ref.shape[0] // 4
     width = half // code_ref.shape[0]
@@ -264,15 +265,13 @@
         target_ref[:, pl.ds(pl.multiple_of(target_at + block * width, width), width)] = target
         left_ref[:classes, pl.ds(pl.multiple_of(block * width, width), width)] = target.astype(bf16)
     left_ref[classes:, :] = x_ref[:used, here]
-    right = nt_dot(left_ref[:classes, :], x_ref[:, here])
-    return right, nt_dot(left_ref[...], feat_ref[:, here])
+    return nt_dot(left_ref[:classes, :], x_ref[:, here]), here
 
 
 def half_kernel(feat_ref, code_ref, x_ref, direct_ref, right_ref, target_ref, left_ref, *, classes):
     core = lax.axis_index("ex") % 2
-    right_ref[...], direct_ref[...] = half_products(
-        core, code_ref, x_ref, feat_ref, target_ref, 0, left_ref, classes=classes
-    )
+    right_ref[...], here = half_target(core, code_ref, x_ref, target_ref, 0, left_ref, classes=classes)
+    direct_ref[...] = nt_dot(left_ref[...], feat_ref[:, here])
 
 
 def pursuit_kernel(
@@ -282,9 +281,7 @@
     classes, full = resid_ref.shape
     half = full // 2
     core = lax.axis_index("ex") % 2
-    right, direct = half_products(
-        1 - core, code_ref, x_ref, feat_ref, resid_ref, (1 - core) * half, left_ref, classes=classes
-    )
+    right, other = half_target(1 - core, code_ref, x_ref, resid_ref, (1 - core) * half, left_ref, classes=classes)
     right = right + right_own[...]
     rhs = [diagonal(right[:, a * classes : (a + 1) * classes]) for a in range(steps)]
     factor = [[factor_ref[:, i * steps + j : i * steps + j + 1] for j in range(i + 1)] for i in range(steps)]
@@ -302,7 +299,7 @@
             copies.append(pltpu.make_async_copy(resid_ref.at[:, here], resid_hbm.at[:, here], sems.at[len(copies)]))
             copies[-1].start()
 
-    direct = direct + direct_own[...]
+    direct = direct_own[...] + nt_dot(left_ref[...], feat_ref[:, other])
     member = lax.broadcasted_iota(jnp.int32, (classes, direct.shape[1]), 0) == labels_ref[...].reshape(1, direct.shape[1])
     for s in range(steps):
         value = direct[:classes]
@@ -333,16 +330,15 @@
     def after(x, *others):
         return lax.optimization_barrier((x,) + others)[0]
 
-    feat, send, keep, packed = pl.pallas_call(
+    feat, send, keep, held = pl.pallas_call(
         functools.partial(sums_kernel, n_ex=n_ex),
         in_specs=[hbm] * 3,
         out_specs=[vmem] * 4,
-        out_shape=[pltpu.VMEM((rows, full), bf16), half, half, jax.ShapeDtypeStruct((8, main), bf16)],
+        out_shape=[pltpu.VMEM((rows, full), bf16), half, half, jax.ShapeDtypeStruct((8, full), f32)],
         scratch_shapes=[
             pltpu.VMEM(labels.shape, jnp.int32),
             pltpu.VMEM(pick_index.shape, jnp.int32),
             pltpu.VMEM((classes + 16, rows), bf16),
-            pltpu.VMEM((8, full), f32),
             pltpu.SemaphoreType.DMA((n_ex + 2,)),
         ],
         compiler_params=limit,
@@ -368,24 +364,38 @@
         compiler_params=limit,
         name="pair_sums",
     )(keep, swap(send, 1))
-    near = packed
+    near = pl.pallas_call(
+        functools.partial(pack_kernel, steps=steps),
+        in_specs=[vmem],
+        out_specs=vmem,
+        out_shape=jax.ShapeDtypeStruct((8, main), bf16),
+        compiler_params=limit,
+        name="pack_rows",
+    )(held)
     for mask in reversed(far_masks):
-        near = jnp.concatenate([near, after(swap(near, mask), codes[0])], axis=0)
+        near = jnp.concatenate([near, swap(near, mask)], axis=0)
+    got = [swap(codes[1], 4), swap(codes[2], 2), swap(codes[3], 6)]
+    near = after(near, got[0])
     parts = [near, swap(near, 4), swap(near, 2), swap(near, 6)]
-
-    part_sum = add([codes[0], swap(codes[1], 4), swap(codes[2], 2), swap(codes[3], 6)], False)
-    one, rest = pl.pallas_call(
-        functools.partial(select_kernel, n_ex=n_ex, rows=rows),
-        in_specs=[vmem],
-        out_specs=[vmem] * 2,
-        out_shape=[jax.ShapeDtypeStruct((total, n_ex * 8), bf16)] * 2,
-        compiler_params=limit,
-        name="selectors",
-    )(after(pick_index, part_sum))
+    part_sum = add([codes[0]] + got, False)
+
+
+    def select(tail, *others):
+        return pl.pallas_call(
+            functools.partial(select_kernel, n_ex=n_ex, rows=rows, tail=tail),
+            in_specs=[vmem],
+            out_specs=vmem,
+            out_shape=jax.ShapeDtypeStruct((total, n_ex * 8), bf16),
+            compiler_params=limit,
+            name="select_tails" if tail else "select_rows",
+        )(after(pick_index, *others))
+
+    one = select(False, part_sum)
+    rest = select(True, part_sum)
     for mask in far_masks:
-        part_sum = add([part_sum, after(swap(part_sum, mask), one)], mask == far_masks[-1])
+        part_sum = add([part_sum, after(swap(part_sum, mask), one, rest)], mask == far_masks[-1])
     own_parts = [part_sum, swap(part_sum, 4), swap(part_sum, 2), swap(part_sum, 6)]
-    parts = [after(p, part_sum) for p in parts]
+    parts = [after(p, own_parts[2], own_parts[3]) for p in parts]
     parts = parts + [swap(p, 1) for p in parts]
 
     x, factor = pl.pallas_call(

time: 46.8 us -> 47.5 us (1.015)
  waiting for transfers between devices: 14.3 us -> 13.1 us
  starting transfers between devices: 18.6 us -> 19.8 us
  Pallas kernels: 12.9 us -> 13.5 us
    ppermute x17, starting transfers between devices: 18.6 us -> 19.8 us  [swap(): return lax.ppermute(x, 'ex', [(d, d ^ mask) for d in range(n_ex)])]
    ppermute x17, waiting for transfers between devices: 14.3 us -> 13.1 us  [swap(): return lax.ppermute(x, 'ex', [(d, d ^ mask) for d in range(n_ex)])]
  transfers between devices with their start and end apart: 17 -> 17, of which waited for: 7 -> 9; matrix products, arithmetic and copies ran while one was open for 0% -> 0% of each run, Pallas kernels for 10% -> 10%
where the time goes in v8:
time: 47.5 us; the launch traced here: 47.4 us
  starting transfers between devices  19.8 us (42%)
  Pallas kernels  13.5 us (28%)
  waiting for transfers between devices  13.1 us (28%)
  between operations  0.76 us (2%)
    ppermute x17, starting transfers between devices, swap(): return lax.ppermute(x, 'ex', [(d, d ^ mask) for d in range(n_ex)])  19.8 us
    ppermute x17, waiting for transfers between devices, swap(): return lax.ppermute(x, 'ex', [(d, d ^ mask) for d in range(n_ex)])  13.1 us
    pallas_call x1, Pallas kernels, on_device(): pl.pallas_call(functools.partial(sums_kernel, n_ex=n_ex), in_specs=[hbm]...  5.02 us
    pallas_call x1, Pallas kernels, on_device(): pl.pallas_call(functools.partial(pursuit_kernel, steps=steps, scale=1.0 /...  3.65 us
    pallas_call x1, Pallas kernels, on_device(): pl.pallas_call(functools.partial(half_kernel, classes=classes), in_specs=...  2.02 us
    pallas_call x1, Pallas kernels, on_device(): pl.pallas_call(functools.partial(picked_kernel, steps=steps), in_specs=[v...  1.39 us
  transfers between devices with their start and end apart: 17, of which 9 were waited for; matrix products, arithmetic and copies ran while one was open for 0% of the time, Pallas kernels for 10%

profile of v8, /device:TPU:0, one launch (start us, length us, event | category | flops | bytes accessed | tf_op | source)
XLA Modules:
  0.0 47.4 jit_solution(6921970183842105025)
XLA Ops:
  0.6 5.0 %class_sums.1 = (bf16[640,8192]{1,0:T(8,128)(2,1)S(1)}, f32[264,512]{1,0:T(8,128)S(1)}, f32[264,512]{1,0:T(8,128)S(1)}, f32[8,8192]{1,0:T(8,128)S(1)}) custom-call(s32[640]{0:T(1024)} %labels_ref.1, s32[3,32]{1,0:T(4,128)} %pick_ref.1, bf16[640,8192]{1,0:T(8,128)(2,1)} %feat_hbm.1), custom_call_target="tpu_custom_call" | custom-call | tf_op jit(solution)/shard_map/class_sums/pallas_call | solution.py:333
  5.7 0.5 %collective-permute-start = (f32[264,512]{1,0:T(8,128)S(1)}, f32[264,512]{1,0:T(8,128)S(1)}, u32[]{:S(2)}, u32[]{:S(2)}) collective-permute-start(f32[264,512]{1,0:T(8,128)S(1)} %get-tuple-element.29), channel_id=1, source_target_pairs={{0,1},{1,0},{2,3},{3,2},{4,5},{5,4},{6,7},{7,6},{8,9},{9,8},{10,11... | collective-permute-start | bytes 1622024 | tf_op jit(solution)/shard_map/ppermute | solution.py:328
  6.3 3.7 %collective-permute-start.8 = (bf16[8,6144]{1,0:T(8,128)(2,1)S(1)}, bf16[8,6144]{1,0:T(8,128)(2,1)S(1)}, u32[]{:S(2)}, u32[]{:S(2)}) collective-permute-start(bf16[8,6144]{1,0:T(8,128)(2,1)S(1)} %pack_rows.1), channel_id=1, source_target_pairs={{0,8},{1,9},{2,10},{3,11},{4,12},{5,13},{6,14},{7,15},{8,0},{9,1},... | collective-permute-start | bytes 294920 | tf_op jit(solution)/shard_map/ppermute | solution.py:328
  9.9 0.2 pair_sums.1
  10.1 1.6 %collective-permute-start.1 = (s16[2,136,128]{2,1,0:T(8,128)(2,1)S(1)}, s16[2,136,128]{2,1,0:T(8,128)(2,1)S(1)}, u32[]{:S(2)}, u32[]{:S(2)}) collective-permute-start(s16[2,136,128]{2,1,0:T(8,128)(2,1)S(1)} %get-tuple-element.31), channel_id=1, source_target_pairs={{0,4},{1,5},{2,6},{3,7},{4,0},{5,1},{6,2},{7,3},{8,12},{9,13},{10,... | collective-permute-start | bytes 208904 | tf_op jit(solution)/shard_map/ppermute | solution.py:328
  11.8 1.5 %collective-permute-start.2 = (s16[2,136,128]{2,1,0:T(8,128)(2,1)S(1)}, s16[2,136,128]{2,1,0:T(8,128)(2,1)S(1)}, u32[]{:S(2)}, u32[]{:S(2)}) collective-permute-start(s16[2,136,128]{2,1,0:T(8,128)(2,1)S(1)} %get-tuple-element.32), channel_id=1, source_target_pairs={{0,2},{1,3},{2,0},{3,1},{4,6},{5,7},{6,4},{7,5},{8,10},{9,11},{10,... | collective-permute-start | bytes 208904 | tf_op jit(solution)/shard_map/ppermute | solution.py:328
  13.3 0.4 collective-permute-start.3
  13.7 1.8 %collective-permute-done.8 = bf16[8,6144]{1,0:T(8,128)(2,1)S(1)} collective-permute-done((bf16[8,6144]{1,0:T(8,128)(2,1)S(1)}, bf16[8,6144]{1,0:T(8,128)(2,1)S(1)}, u32[]{:S(2)}, u32[]{:S(2)}) %collective-permute-start.8) | collective-permute-done | bytes 98336 | tf_op jit(solution)/shard_map/ppermute | solution.py:328
  15.5 2.5 %collective-permute-start.11 = (bf16[16,6144]{1,0:T(8,128)(2,1)S(1)}, bf16[16,6144]{1,0:T(8,128)(2,1)S(1)}, u32[]{:S(2)}, u32[]{:S(2)}) collective-permute-start(bf16[16,6144]{1,0:T(8,128)(2,1)S(1)} %pad_maximum_fusion.refs_0_), channel_id=1, source_target_pairs={{0,6},{1,7},{2,4},{3,5},{4,2},{5,3},{6,0},{7,1},{8,14},{9,15},{10,... | collective-permute-start | bytes 589832 | tf_op jit(solution)/shard_map/ppermute | solution.py:328
  18.0 0.5 %collective-permute-start.10 = (bf16[16,6144]{1,0:T(8,128)(2,1)S(1)}, bf16[16,6144]{1,0:T(8,128)(2,1)S(1)}, u32[]{:S(2)}, u32[]{:S(2)}) collective-permute-start(bf16[16,6144]{1,0:T(8,128)(2,1)S(1)} %pad_maximum_fusion.refs_0_), channel_id=1, source_target_pairs={{0,2},{1,3},{2,0},{3,1},{4,6},{5,7},{6,4},{7,5},{8,10},{9,11},{10,... | collective-permute-start | bytes 589832 | tf_op jit(solution)/shard_map/ppermute | solution.py:328
  18.5 0.6 %collective-permute-start.9 = (bf16[16,6144]{1,0:T(8,128)(2,1)S(1)}, bf16[16,6144]{1,0:T(8,128)(2,1)S(1)}, u32[]{:S(2)}, u32[]{:S(2)}) collective-permute-start(bf16[16,6144]{1,0:T(8,128)(2,1)S(1)} %pad_maximum_fusion.refs_0_), channel_id=1, source_target_pairs={{0,4},{1,5},{2,6},{3,7},{4,0},{5,1},{6,2},{7,3},{8,12},{9,13},{10,... | collective-permute-start | bytes 589832 | tf_op jit(solution)/shard_map/ppermute | solution.py:328
  19.1 0.3 add_sums.2.refs_0_
  19.4 2.8 %collective-permute-start.4 = (s16[2,136,128]{2,1,0:T(8,128)(2,1)S(1)}, s16[2,136,128]{2,1,0:T(8,128)(2,1)S(1)}, u32[]{:S(2)}, u32[]{:S(2)}) collective-permute-start(s16[2,136,128]{2,1,0:T(8,128)(2,1)S(1)} %add_sums.2.refs_0_), channel_id=1, source_target_pairs={{0,8},{1,9},{2,10},{3,11},{4,12},{5,13},{6,14},{7,15},{8,0},{9,1},... | collective-permute-start | bytes 208904 | tf_op jit(solution)/shard_map/ppermute | solution.py:328
  22.2 0.3 select_tails.1.rest_ref
  22.5 0.3 select_rows.1.one_ref
  22.8 4.6 %collective-permute-done.4.refs_1_ = s16[2,136,128]{2,1,0:T(8,128)(2,1)S(1)} collective-permute-done((s16[2,136,128]{2,1,0:T(8,128)(2,1)S(1)}, s16[2,136,128]{2,1,0:T(8,128)(2,1)S(1)}, u32[]{:S(2)}, u32[]{:S(2)}) %collective-permute-start.4) | collective-permute-done | bytes 69664 | tf_op jit(solution)/shard_map/ppermute | solution.py:328
  27.4 0.3 add_sums.3
  27.7 4.1 %collective-permute-start.7 = (s16[2,136,128]{2,1,0:T(8,128)(2,1)S(1)}, s16[2,136,128]{2,1,0:T(8,128)(2,1)S(1)}, u32[]{:S(2)}, u32[]{:S(2)}) collective-permute-start(s16[2,136,128]{2,1,0:T(8,128)(2,1)S(1)} %add_sums.3), channel_id=1, source_target_pairs={{0,6},{1,7},{2,4},{3,5},{4,2},{5,3},{6,0},{7,1},{8,14},{9,15},{10,... | collective-permute-start | bytes 208904 | tf_op jit(solution)/shard_map/ppermute | solution.py:328
  31.9 0.5 %collective-permute-start.6 = (s16[2,136,128]{2,1,0:T(8,128)(2,1)S(1)}, s16[2,136,128]{2,1,0:T(8,128)(2,1)S(1)}, u32[]{:S(2)}, u32[]{:S(2)}) collective-permute-start(s16[2,136,128]{2,1,0:T(8,128)(2,1)S(1)} %add_sums.3), channel_id=1, source_target_pairs={{0,2},{1,3},{2,0},{3,1},{4,6},{5,7},{6,4},{7,5},{8,10},{9,11},{10,... | collective-permute-start | bytes 208904 | tf_op jit(solution)/shard_map/ppermute | solution.py:328
  32.4 1.9 %collective-permute-done.7 = s16[2,136,128]{2,1,0:T(8,128)(2,1)S(1)} collective-permute-done((s16[2,136,128]{2,1,0:T(8,128)(2,1)S(1)}, s16[2,136,128]{2,1,0:T(8,128)(2,1)S(1)}, u32[]{:S(2)}, u32[]{:S(2)}) %collective-permute-start.7) | collective-permute-done | bytes 69664 | tf_op jit(solution)/shard_map/ppermute | solution.py:328
  34.3 1.9 %collective-permute-done.6 = s16[2,136,128]{2,1,0:T(8,128)(2,1)S(1)} collective-permute-done((s16[2,136,128]{2,1,0:T(8,128)(2,1)S(1)}, s16[2,136,128]{2,1,0:T(8,128)(2,1)S(1)}, u32[]{:S(2)}, u32[]{:S(2)}) %collective-permute-start.6) | collective-permute-done | bytes 69664 | tf_op jit(solution)/shard_map/ppermute | solution.py:328
  36.2 0.5 %collective-permute-start.15 = (bf16[16,6144]{1,0:T(8,128)(2,1)S(1)}, bf16[16,6144]{1,0:T(8,128)(2,1)S(1)}, u32[]{:S(2)}, u32[]{:S(2)}) collective-permute-start(bf16[16,6144]{1,0:T(8,128)(2,1)S(1)} %collective-permute-done.11.refs_3_), channel_id=1, source_target_pairs={{0,1},{1,0},{2,3},{3,2},{4,5},{5,4},{6,7},{7,6},{8,9},{9,8},{10,11... | collective-permute-start | bytes 589832 | tf_op jit(solution)/shard_map/ppermute | solution.py:328
  36.8 0.4 collective-permute-start.13
  37.2 0.4 collective-permute-done.12.refs_4_
  37.6 0.3 collective-permute-done.15.refs_7_
  37.9 0.3 collective-permute-done.14.refs_6_
  38.2 0.3 collective-permute-done.13.refs_5_
  38.5 1.4 %picked_rows.1 = (bf16[96,8192]{1,0:T(8,128)(2,1)S(1)}, f32[32,128]{1,0:T(8,128)S(1)}) custom-call(bf16[96,128]{1,0:T(8,128)(2,1)S(1)} %select_rows.1.one_ref, bf16[96,128]{1,0:T(8,128)(2,1)S(1)} %select_tails.1.rest_ref, bf16[16,6144]{1,0:T(8,128)(2,1)S(1)} %pad_maximum_fusion.refs_0_, bf16[16,6144]{1,0:T(8,128)(2,1)S(1)} %collective-permute-done.9.refs_1_, ...), custom_call_target="tpu_custom_call" | custom-call | tf_op jit(solution)/shard_map/picked_rows/pallas_call | solution.py:401
  39.9 1.7 %collective-permute-done.5 = s16[2,136,128]{2,1,0:T(8,128)(2,1)S(1)} collective-permute-done((s16[2,136,128]{2,1,0:T(8,128)(2,1)S(1)}, s16[2,136,128]{2,1,0:T(8,128)(2,1)S(1)}, u32[]{:S(2)}, u32[]{:S(2)}) %collective-permute-start.5) | collective-permute-done | bytes 69664 | tf_op jit(solution)/shard_map/ppermute | solution.py:328
  41.6 0.1 collective-permute-start.16
  41.7 2.0 %own_half_products.1 = (f32[96,640]{1,0:T(8,128)S(1)}, f32[32,96]{1,0:T(8,128)S(1)}, f32[32,4096]{1,0:T(8,128)S(1)}) custom-call(bf16[640,8192]{1,0:T(8,128)(2,1)S(1)} %get-tuple-element.27.feat_ref, s16[8,136,128]{2,1,0:T(8,128)(2,1)S(1)} %constant_dynamic-update-slice_fusion.code_ref, bf16[96,8192]{1,0:T(8,128)(2,1)S(1)} %get-tuple-element.43.x_ref), custom_call_target="tpu_custom_call" | custom-call | tf_op jit(solution)/shard_map/own_half_products/pallas_call | solution.py:418
  43.7 3.7 %pursuit.1 = (f32[3,640]{1,0:T(4,128)}, f32[32,8192]{1,0:T(8,128)}) custom-call(s32[640]{0:T(1024)S(1)} %copy-done.1, bf16[640,8192]{1,0:T(8,128)(2,1)S(1)} %get-tuple-element.27.feat_ref, bf16[96,8192]{1,0:T(8,128)(2,1)S(1)} %get-tuple-element.43.x_ref, f32[32,128]{1,0:T(8,128)S(1)} %get-tuple-element.44.factor_ref, ...), custom_call_target="tpu_custom_call" | custom-call | tf_op jit(solution)/shard_map/pursuit/pallas_call | solution.py:432
  (21 shorter events, 0.2 us)
Async XLA Ops:
  0.6 21.5 %copy-start = (s32[3,32]{1,0:T(4,128)S(1)}, s32[3,32]{1,0:T(4,128)}, u32[]{:S(2)}) copy-start(s32[3,32]{1,0:T(4,128)} %pick_ref.1) | copy-start | bytes 1156
  5.7 38.0 %copy-start.1 = (s32[640]{0:T(1024)S(1)}, s32[640]{0:T(1024)}, u32[]{:S(2)}) copy-start(s32[640]{0:T(1024)} %labels_ref.1) | copy-start | bytes 7684
  5.7 4.2 %collective-permute-start = (f32[264,512]{1,0:T(8,128)S(1)}, f32[264,512]{1,0:T(8,128)S(1)}, u32[]{:S(2)}, u32[]{:S(2)}) collective-permute-start(f32[264,512]{1,0:T(8,128)S(1)} %get-tuple-element.29), channel_id=1, source_target_pairs={{0,1},{1,0},{2,3},{3,2},{4,5},{5,4},{6,7},{7,6},{8,9},{9,8},{10,11... | collective-permute-start | bytes 1622024 | tf_op jit(solution)/shard_map/ppermute | solution.py:328
  6.3 9.2 %collective-permute-start.8 = (bf16[8,6144]{1,0:T(8,128)(2,1)S(1)}, bf16[8,6144]{1,0:T(8,128)(2,1)S(1)}, u32[]{:S(2)}, u32[]{:S(2)}) collective-permute-start(bf16[8,6144]{1,0:T(8,128)(2,1)S(1)} %pack_rows.1), channel_id=1, source_target_pairs={{0,8},{1,9},{2,10},{3,11},{4,12},{5,13},{6,14},{7,15},{8,0},{9,1},... | collective-permute-start | bytes 294920 | tf_op jit(solution)/shard_map/ppermute | solution.py:328
  10.1 5.4 %collective-permute-start.1 = (s16[2,136,128]{2,1,0:T(8,128)(2,1)S(1)}, s16[2,136,128]{2,1,0:T(8,128)(2,1)S(1)}, u32[]{:S(2)}, u32[]{:S(2)}) collective-permute-start(s16[2,136,128]{2,1,0:T(8,128)(2,1)S(1)} %get-tuple-element.31), channel_id=1, source_target_pairs={{0,4},{1,5},{2,6},{3,7},{4,0},{5,1},{6,2},{7,3},{8,12},{9,13},{10,... | collective-permute-start | bytes 208904 | tf_op jit(solution)/shard_map/ppermute | solution.py:328
  11.8 7.3 %collective-permute-start.2 = (s16[2,136,128]{2,1,0:T(8,128)(2,1)S(1)}, s16[2,136,128]{2,1,0:T(8,128)(2,1)S(1)}, u32[]{:S(2)}, u32[]{:S(2)}) collective-permute-start(s16[2,136,128]{2,1,0:T(8,128)(2,1)S(1)} %get-tuple-element.32), channel_id=1, source_target_pairs={{0,2},{1,3},{2,0},{3,1},{4,6},{5,7},{6,4},{7,5},{8,10},{9,11},{10,... | collective-permute-start | bytes 208904 | tf_op jit(solution)/shard_map/ppermute | solution.py:328
  13.3 5.8 %collective-permute-start.3 = (s16[2,136,128]{2,1,0:T(8,128)(2,1)S(1)}, s16[2,136,128]{2,1,0:T(8,128)(2,1)S(1)}, u32[]{:S(2)}, u32[]{:S(2)}) collective-permute-start(s16[2,136,128]{2,1,0:T(8,128)(2,1)S(1)} %get-tuple-element.33), channel_id=1, source_target_pairs={{0,6},{1,7},{2,4},{3,5},{4,2},{5,3},{6,0},{7,1},{8,14},{9,15},{10,... | collective-permute-start | bytes 208904 | tf_op jit(solution)/shard_map/ppermute | solution.py:328
  15.5 20.7 %collective-permute-start.11 = (bf16[16,6144]{1,0:T(8,128)(2,1)S(1)}, bf16[16,6144]{1,0:T(8,128)(2,1)S(1)}, u32[]{:S(2)}, u32[]{:S(2)}) collective-permute-start(bf16[16,6144]{1,0:T(8,128)(2,1)S(1)} %pad_maximum_fusion.refs_0_), channel_id=1, source_target_pairs={{0,6},{1,7},{2,4},{3,5},{4,2},{5,3},{6,0},{7,1},{8,14},{9,15},{10,... | collective-permute-start | bytes 589832 | tf_op jit(solution)/shard_map/ppermute | solution.py:328
  18.0 18.7 %collective-permute-start.10 = (bf16[16,6144]{1,0:T(8,128)(2,1)S(1)}, bf16[16,6144]{1,0:T(8,128)(2,1)S(1)}, u32[]{:S(2)}, u32[]{:S(2)}) collective-permute-start(bf16[16,6144]{1,0:T(8,128)(2,1)S(1)} %pad_maximum_fusion.refs_0_), channel_id=1, source_target_pairs={{0,2},{1,3},{2,0},{3,1},{4,6},{5,7},{6,4},{7,5},{8,10},{9,11},{10,... | collective-permute-start | bytes 589832 | tf_op jit(solution)/shard_map/ppermute | solution.py:328
  18.5 18.3 %collective-permute-start.9 = (bf16[16,6144]{1,0:T(8,128)(2,1)S(1)}, bf16[16,6144]{1,0:T(8,128)(2,1)S(1)}, u32[]{:S(2)}, u32[]{:S(2)}) collective-permute-start(bf16[16,6144]{1,0:T(8,128)(2,1)S(1)} %pad_maximum_fusion.refs_0_), channel_id=1, source_target_pairs={{0,4},{1,5},{2,6},{3,7},{4,0},{5,1},{6,2},{7,3},{8,12},{9,13},{10,... | collective-permute-start | bytes 589832 | tf_op jit(solution)/shard_map/ppermute | solution.py:328
  19.4 8.1 %collective-permute-start.4 = (s16[2,136,128]{2,1,0:T(8,128)(2,1)S(1)}, s16[2,136,128]{2,1,0:T(8,128)(2,1)S(1)}, u32[]{:S(2)}, u32[]{:S(2)}) collective-permute-start(s16[2,136,128]{2,1,0:T(8,128)(2,1)S(1)} %add_sums.2.refs_0_), channel_id=1, source_target_pairs={{0,8},{1,9},{2,10},{3,11},{4,12},{5,13},{6,14},{7,15},{8,0},{9,1},... | collective-permute-start | bytes 208904 | tf_op jit(solution)/shard_map/ppermute | solution.py:328
  27.7 6.5 %collective-permute-start.7 = (s16[2,136,128]{2,1,0:T(8,128)(2,1)S(1)}, s16[2,136,128]{2,1,0:T(8,128)(2,1)S(1)}, u32[]{:S(2)}, u32[]{:S(2)}) collective-permute-start(s16[2,136,128]{2,1,0:T(8,128)(2,1)S(1)} %add_sums.3), channel_id=1, source_target_pairs={{0,6},{1,7},{2,4},{3,5},{4,2},{5,3},{6,0},{7,1},{8,14},{9,15},{10,... | collective-permute-start | bytes 208904 | tf_op jit(solution)/shard_map/ppermute | solution.py:328
  31.9 4.3 %collective-permute-start.6 = (s16[2,136,128]{2,1,0:T(8,128)(2,1)S(1)}, s16[2,136,128]{2,1,0:T(8,128)(2,1)S(1)}, u32[]{:S(2)}, u32[]{:S(2)}) collective-permute-start(s16[2,136,128]{2,1,0:T(8,128)(2,1)S(1)} %add_sums.3), channel_id=1, source_target_pairs={{0,2},{1,3},{2,0},{3,1},{4,6},{5,7},{6,4},{7,5},{8,10},{9,11},{10,... | collective-permute-start | bytes 208904 | tf_op jit(solution)/shard_map/ppermute | solution.py:328
  36.2 1.4 %collective-permute-start.12 = (bf16[16,6144]{1,0:T(8,128)(2,1)S(1)}, bf16[16,6144]{1,0:T(8,128)(2,1)S(1)}, u32[]{:S(2)}, u32[]{:S(2)}) collective-permute-start(bf16[16,6144]{1,0:T(8,128)(2,1)S(1)} %pad_maximum_fusion.refs_0_), channel_id=1, source_target_pairs={{0,1},{1,0},{2,3},{3,2},{4,5},{5,4},{6,7},{7,6},{8,9},{9,8},{10,11... | collective-permute-start | bytes 589832 | tf_op jit(solution)/shard_map/ppermute | solution.py:328
  36.2 1.7 %collective-permute-start.15 = (bf16[16,6144]{1,0:T(8,128)(2,1)S(1)}, bf16[16,6144]{1,0:T(8,128)(2,1)S(1)}, u32[]{:S(2)}, u32[]{:S(2)}) collective-permute-start(bf16[16,6144]{1,0:T(8,128)(2,1)S(1)} %collective-permute-done.11.refs_3_), channel_id=1, source_target_pairs={{0,1},{1,0},{2,3},{3,2},{4,5},{5,4},{6,7},{7,6},{8,9},{9,8},{10,11... | collective-permute-start | bytes 589832 | tf_op jit(solution)/shard_map/ppermute | solution.py:328
  36.7 1.5 %collective-permute-start.14 = (bf16[16,6144]{1,0:T(8,128)(2,1)S(1)}, bf16[16,6144]{1,0:T(8,128)(2,1)S(1)}, u32[]{:S(2)}, u32[]{:S(2)}) collective-permute-start(bf16[16,6144]{1,0:T(8,128)(2,1)S(1)} %collective-permute-done.10.refs_2_), channel_id=1, source_target_pairs={{0,1},{1,0},{2,3},{3,2},{4,5},{5,4},{6,7},{7,6},{8,9},{9,8},{10,11... | collective-permute-start | bytes 589832 | tf_op jit(solution)/shard_map/ppermute | solution.py:328
  36.8 1.7 %collective-permute-start.13 = (bf16[16,6144]{1,0:T(8,128)(2,1)S(1)}, bf16[16,6144]{1,0:T(8,128)(2,1)S(1)}, u32[]{:S(2)}, u32[]{:S(2)}) collective-permute-start(bf16[16,6144]{1,0:T(8,128)(2,1)S(1)} %collective-permute-done.9.refs_1_), channel_id=1, source_target_pairs={{0,1},{1,0},{2,3},{3,2},{4,5},{5,4},{6,7},{7,6},{8,9},{9,8},{10,11... | collective-permute-start | bytes 589832 | tf_op jit(solution)/shard_map/ppermute | solution.py:328
  37.2 4.3 %collective-permute-start.5 = (s16[2,136,128]{2,1,0:T(8,128)(2,1)S(1)}, s16[2,136,128]{2,1,0:T(8,128)(2,1)S(1)}, u32[]{:S(2)}, u32[]{:S(2)}) collective-permute-start(s16[2,136,128]{2,1,0:T(8,128)(2,1)S(1)} %add_sums.3), channel_id=1, source_target_pairs={{0,4},{1,5},{2,6},{3,7},{4,0},{5,1},{6,2},{7,3},{8,12},{9,13},{10,... | collective-permute-start | bytes 208904 | tf_op jit(solution)/shard_map/ppermute | solution.py:328
  41.6 2.1 %collective-permute-start.16 = (s16[8,136,128]{2,1,0:T(8,128)(2,1)S(1)}, s16[8,136,128]{2,1,0:T(8,128)(2,1)S(1)}, u32[]{:S(2)}, u32[]{:S(2)}) collective-permute-start(s16[8,136,128]{2,1,0:T(8,128)(2,1)S(1)} %constant_dynamic-update-slice_fusion.code_ref), channel_id=1, source_target_pairs={{0,1},{1,0},{2,3},{3,2},{4,5},{5,4},{6,7},{7,6},{8,9},{9,8},{10,11... | collective-permute-start | bytes 835592 | tf_op jit(solution)/shard_map/ppermute | solution.py:328

commit v9 on v8

v9 whole, which is shorter than its diff:
```python
import functools
import math

import jax
import jax.numpy as jnp
from jax import lax
from jax.experimental import pallas as pl
from jax.experimental.pallas import tpu as pltpu
from jax.sharding import PartitionSpec as P

ridge = 1.0
slots = 2
near_masks = (0, 4, 2, 6)
f32 = jnp.float32
bf16 = jnp.bfloat16


def nt_dot(a, b):
    return lax.dot_general(a, b, (((1,), (1,)), ((), ())), preferred_element_type=f32)


def column(tile, height, start=0):
    return jnp.concatenate([tile[:, start + q : start + q + 1] for q in range(height // 8)], axis=0)


def spread(values, start=0):
    lane = lax.broadcasted_iota(jnp.int32, (8, 128), 1)
    tile = jnp.zeros((8, 128), f32)
    for q in range(values.shape[0] // 8):
        tile = jnp.where(lane == start + q, values[8 * q : 8 * q + 8], tile)
    return tile


def encode(x, count_tile=None):
    height, width = x.shape
    top = jnp.max(jnp.abs(x), axis=1, keepdims=True)
    power = jnp.ceil(jnp.log2(jnp.maximum(top, 1e-30)) + 0.01)
    whole_x = jnp.round(x * jnp.exp2(15.0 - power))
    mark = spread(power)
    if count_tile is not None:
        mark = mark + count_tile
    chunks = [whole_x[:, j * 128 : (j + 1) * 128] for j in range(width // 128)]
    return jnp.concatenate(chunks + [mark], axis=0).astype(jnp.int32).astype(jnp.int16)


def decode(code, height):
    value = code.astype(jnp.int32).astype(f32)
    count = value.shape[0] // height
    mark = value[count * height :]
    x = jnp.concatenate([value[j * height : (j + 1) * height] for j in range(count)], axis=1)
    return x * jnp.exp2(column(mark, height) - 15.0), mark


def sums_kernel(
    labels_hbm, pick_hbm, feat_hbm, feat_ref, sums_ref, tile_ref, code_ref, held, labels_ref, pick_ref, left, sems
):
    rows, full = feat_ref.shape
    steps, classes = pick_ref.shape
    blocks, _, width = sums_ref.shape
    device = lax.axis_index("ex")
    small = [
        pltpu.make_async_copy(pick_hbm, pick_ref, sems.at[blocks]),
        pltpu.make_async_copy(labels_hbm, labels_ref, sems.at[blocks + 1]),
    ]
    for copy in small:
        copy.start()
    copies = []
    for i in range(blocks):
        at = slice(i * width, (i + 1) * width)
        copies.append(pltpu.make_async_copy(feat_hbm.at[:, at], feat_ref.at[:, at], sems.at[i]))
        copies[-1].start()

    for copy in small:
        copy.wait()
    local = pick_ref[...] - device * rows
    mine = (local >= 0) & (local < rows)
    lane = lax.broadcasted_iota(jnp.int32, local.shape, 1)
    first = jnp.min(jnp.where(mine, lane, classes), axis=1, keepdims=True)
    last = jnp.max(jnp.where(mine, lane, -1), axis=1, keepdims=True)
    spot0 = jnp.max(jnp.where(mine & (lane == first), local, -1), axis=1, keepdims=True)
    spot1 = jnp.max(jnp.where(mine & (lane == last) & (last > first), local, -1), axis=1, keepdims=True)
    member = lax.broadcasted_iota(jnp.int32, (classes, rows), 0) == labels_ref[...].reshape(1, rows)
    line = lax.broadcasted_iota(jnp.int32, (steps, rows), 1)
    left[...] = jnp.concatenate(
        [
            jnp.where(member, 1.0, 0.0),
            jnp.where(line == spot0, 1.0, 0.0),
            jnp.where(line == spot1, 1.0, 0.0),
            jnp.zeros((16 - 2 * steps, rows), f32),
        ],
        axis=0,
    ).astype(bf16)
    count = jnp.sum(jnp.where(member, 1.0, 0.0), axis=1, keepdims=True)
    tile = spread(count, classes // 8)
    tile_ref[...] = tile

    for i in range(blocks):
        at = slice(i * width, (i + 1) * width)
        copies[i].wait()
        both = jnp.dot(left[...], feat_ref[:, at], preferred_element_type=f32)
        sums_ref[i] = both[:classes]
        code_ref[i] = encode(both[:classes], tile)
        held[:, at] = both[classes : classes + 8]


def pack_kernel(held, rows_ref, *, steps):
    used = steps * slots
    main = rows_ref.shape[1]
    lines = [held[0:used, :main]]
    for q in range(slots):
        lines.append(jnp.concatenate([held[q * steps + u : q * steps + u + 1, main:] for u in range(steps)], axis=1))
    rows_ref[...] = jnp.concatenate(lines, axis=0).astype(bf16)


def near_id(mask):
    return (lax.axis_index("ex") // 2 % 4) ^ (mask // 2)


def pair_kernel(sums_ref, tile_ref, got_ref, *code_refs, classes):
    lane = lax.broadcasted_iota(jnp.int32, (8, 128), 1)
    for mask, code_ref in zip(near_masks, code_refs):
        for j in range(code_ref.shape[0]):
            block = near_id(mask) * code_ref.shape[0] + j
            more, mark = decode(got_ref[block], classes)
            mark = jnp.where(lane < classes // 8, 0.0, mark) + tile_ref[...]
            code_ref[j] = encode(sums_ref[block] + more, mark)


def add_kernel(*refs, classes, last):
    code_ref = refs[-1]
    for j in range(code_ref.shape[0]):
        value, mark = decode(refs[0][j], classes)
        for ref in refs[1:-1]:
            more, more_mark = decode(ref[j], classes)
            value = value + more
            mark = mark + more_mark
        if last:
            code_ref[j] = encode(value / jnp.sqrt(column(mark, classes, classes // 8)))
        else:
            lane = lax.broadcasted_iota(jnp.int32, mark.shape, 1)
            code_ref[j] = encode(value, jnp.where(lane < classes // 8, 0.0, mark))


def diagonal(block):
    n = block.shape[0]
    eye = lax.broadcasted_iota(jnp.int32, (n, n), 0) == lax.broadcasted_iota(jnp.int32, (n, n), 1)
    return jnp.sum(jnp.where(eye, block, 0.0), axis=1, keepdims=True)


def factor_all(gram):
    order = len(gram)
    factor = [[None] * order for _ in range(order)]
    for j in range(order):
        value = gram[j][j]
        for k in range(j):
            value = value - factor[j][k] * factor[j][k]
        root = jnp.sqrt(value)
        factor[j][j] = 1.0 / root
        for i in range(j + 1, order):
            value = gram[i][j]
            for k in range(j):
                value = value - factor[i][k] * factor[j][k]
            factor[i][j] = value * factor[j][j]
    return factor


def solve_all(factor, right):
    order = len(right)
    forward = []
    for i in range(order):
        value = right[i]
        for j in range(i):
            value = value - factor[i][j] * forward[j]
        forward.append(value * factor[i][i])
    result = []
    for size in range(1, order + 1):
        back = [None] * size
        for i in reversed(range(size)):
            value = forward[i]
            for j in range(i + 1, size):
                value = value - factor[j][i] * back[j]
            back[i] = value * factor[i][i]
        result.append(back)
    return result


def select_kernel(pick_ref, one_ref, *, n_ex, rows, tail):
    steps, classes = pick_ref.shape
    lines = one_ref.shape[1]
    device = lax.axis_index("ex")
    pick = pick_ref[...]
    lane = lax.broadcasted_iota(jnp.int32, pick.shape, 1)
    owner = jnp.zeros_like(pick)
    rank = jnp.zeros_like(pick)
    for d in range(n_ex):
        here = (pick >= d * rows) & (pick < (d + 1) * rows)
        first = jnp.min(jnp.where(here, lane, classes), axis=1, keepdims=True)
        owner = jnp.where(here, d, owner)
        rank = jnp.where(here & (lane > first), 1, rank)
    away = owner ^ device
    spot = jnp.zeros_like(pick)
    bits = n_ex.bit_length() - 1
    for b in range(1, bits):
        spot = spot + (((away >> b) & 1) << (bits - 1 - b))
    spot = 2 * spot + 1 - (owner & 1)
    step = lax.broadcasted_iota(jnp.int32, pick.shape, 0)
    line = lax.broadcasted_iota(jnp.int32, (lines, classes), 0)
    where = spot * 8 + (slots * steps + rank if tail else rank * steps + step)
    hits = [jnp.where(line == where[s : s + 1, :], 1.0, 0.0) for s in range(steps)]
    pad = jnp.zeros((lines, 128 - steps * classes), f32)
    one_ref[...] = jnp.transpose(jnp.concatenate(hits + [pad], axis=1))[: steps * classes].astype(bf16)


def picked_kernel(one_ref, rest_ref, *refs, steps):
    (x_ref, factor_ref, rows_ref), count = refs[-3:], (len(refs) - 3) // 2
    odd = lax.axis_index("ex") % 2 == 1
    total, full = x_ref.shape
    classes = total // steps
    main = rows_ref.shape[1]
    tail = full - main
    at = 0
    for mine, got in zip(refs[:count], refs[count : 2 * count]):
        here = slice(at, at + mine.shape[0])

        @pl.when(odd)
        def _():
            rows_ref[here, :] = mine[...]

        @pl.when(jnp.logical_not(odd))
        def _():
            rows_ref[here, :] = got[...]

        at += mine.shape[0]
    x_ref[:, :main] = jnp.dot(one_ref[...], rows_ref[...], preferred_element_type=f32).astype(bf16)
    for s in range(steps):
        at = slice(s * classes, (s + 1) * classes)
        rest = jnp.dot(rest_ref[at, :], rows_ref[:, s * tail : (s + 1) * tail], preferred_element_type=f32)
        x_ref[at, main:] = rest.astype(bf16)

    x = x_ref[...]
    full_gram = nt_dot(x, x)
    gram = [
        [
            diagonal(full_gram[a * classes : (a + 1) * classes, b * classes : (b + 1) * classes])
            + (ridge if a == b else 0.0)
            for b in range(a + 1)
        ]
        for a in range(steps)
    ]
    factor = factor_all(gram)
    lane = lax.broadcasted_iota(jnp.int32, (classes, 128), 1)
    packed = jnp.zeros((classes, 128), f32)
    for i in range(steps):
        for j in range(i + 1):
            packed = jnp.where(lane == i * steps + j, factor[i][j], packed)
    factor_ref[...] = packed


def quarter_target(mask, own_ref, got_ref, x_ref, target_ref, left_ref, *, classes):
    count = own_ref.shape[0]
    span = left_ref.shape[1]
    width = span // count
    used = left_ref.shape[0] - classes
    even = lax.axis_index("ex") % 2 == 0
    quarter = near_id(mask)
    here = pl.ds(pl.multiple_of(quarter * span, span), span)
    for j in range(count):
        target = decode(jnp.where(even, own_ref[j].astype(jnp.int32), got_ref[j].astype(jnp.int32)), classes)[0]
        at = slice(j * width, (j + 1) * width)
        target_ref[:, at] = target
        left_ref[:classes, at] = target.astype(bf16)
    left_ref[classes:, :] = x_ref[:used, here]
    return nt_dot(left_ref[:classes, :], x_ref[:, here]), here


def first_kernel(feat_ref, own_ref, got_ref, x_ref, direct_ref, right_ref, target_ref, left_ref, *, classes):
    right_ref[...], here = quarter_target(0, own_ref, got_ref, x_ref, target_ref, left_ref, classes=classes)
    direct_ref[...] = nt_dot(left_ref[...], feat_ref[:, here])


def pursuit_kernel(
    labels_ref, feat_ref, x_ref, factor_ref, direct_first, right_first, target_first, *refs, steps, scale
):
    owns, gots, (scores_ref, resid_hbm, target_ref, left_ref, sems) = refs[:3], refs[3:6], refs[6:]
    classes = target_first.shape[0]
    right = right_first[...]
    places = []
    for k, mask in enumerate(near_masks[1:]):
        more, here = quarter_target(
            mask, owns[k], gots[k], x_ref, target_ref.at[k + 1], left_ref.at[k], classes=classes
        )
        right = right + more
        places.append(here)
    span = target_first.shape[1]
    target_ref[0] = target_first[...]
    places.insert(0, pl.ds(pl.multiple_of(near_id(0) * span, span), span))
    rhs = [diagonal(right[:, a * classes : (a + 1) * classes]) for a in range(steps)]
    factor = [[factor_ref[:, i * steps + j : i * steps + j + 1] for j in range(i + 1)] for i in range(steps)]
    weights = solve_all(factor, rhs)
    last = weights[steps - 1]
    copies = []
    for q, here in enumerate(places):
        value = target_ref[q]
        for k in range(steps):
            value = value - last[k] * x_ref[k * classes : (k + 1) * classes, here].astype(f32)
        target_ref[q] = value
        copies.append(pltpu.make_async_copy(target_ref.at[q], resid_hbm.at[:, here], sems.at[q]))
        copies[-1].start()

    direct = direct_first[...]
    for k, here in enumerate(places[1:]):
        direct = direct + nt_dot(left_ref[k], feat_ref[:, here])
    member = lax.broadcasted_iota(jnp.int32, (classes, direct.shape[1]), 0) == labels_ref[...].reshape(1, direct.shape[1])
    for s in range(steps):
        value = direct[:classes]
        for k in range(s):
            value = value - weights[s - 1][k] * direct[(k + 1) * classes : (k + 2) * classes]
        scores_ref[s : s + 1, :] = jnp.sum(jnp.where(member, value, 0.0), axis=0, keepdims=True) * scale
    for copy in copies:
        copy.wait()


def on_device(features, labels, pick_index, *, n_ex):
    rows, full = features.shape
    steps, classes = pick_index.shape
    total = steps * classes
    main = full * steps * slots // 8
    blocks = 16
    width = full // blocks
    limit = pltpu.CompilerParams(vmem_limit_bytes=16 << 20)
    vmem = pl.BlockSpec(memory_space=pltpu.VMEM)
    hbm = pl.BlockSpec(memory_space=pltpu.HBM)
    anywhere = pl.BlockSpec(memory_space=pl.ANY)
    code = jax.ShapeDtypeStruct((blocks // 4, classes * (width // 128) + 8, 128), jnp.int16)

    def after(x, *others):
        return lax.optimization_barrier((x,) + others)[0]

    def move(x, side, mask):
        return lax.ppermute(x, "ex", [(d, d ^ mask) for d in range(side, n_ex, 2)])

    feat, sums, tile, sum_codes, held = pl.pallas_call(
        sums_kernel,
        in_specs=[hbm] * 3,
        out_specs=[vmem] * 5,
        out_shape=[
            pltpu.VMEM((rows, full), bf16),
            jax.ShapeDtypeStruct((blocks, classes, width), f32),
            jax.ShapeDtypeStruct((8, 128), f32),
            jax.ShapeDtypeStruct((blocks,) + code.shape[1:], jnp.int16),
            jax.ShapeDtypeStruct((8, full), f32),
        ],
        scratch_shapes=[
            pltpu.VMEM(labels.shape, jnp.int32),
            pltpu.VMEM(pick_index.shape, jnp.int32),
            pltpu.VMEM((classes + 16, rows), bf16),
            pltpu.SemaphoreType.DMA((blocks + 2,)),
        ],
        compiler_params=limit,
        name="class_sums",
    )(*[pltpu.with_memory_space_constraint(a, pltpu.HBM) for a in (labels, pick_index, features)])

    packed = pl.pallas_call(
        functools.partial(pack_kernel, steps=steps),
        in_specs=[vmem],
        out_specs=vmem,
        out_shape=jax.ShapeDtypeStruct((8, main), bf16),
        compiler_params=limit,
        name="pack_rows",
    )(held)

    far_masks = [8 << b for b in range(n_ex.bit_length() - 4)]
    twin_codes = move(sum_codes, 1, 1)
    codes = pl.pallas_call(
        functools.partial(pair_kernel, classes=classes),
        in_specs=[vmem] * 3,
        out_specs=[vmem] * 4,
        out_shape=[code] * 4,
        compiler_params=limit,
        name="pair_sums",
    )(sums, tile, twin_codes)

    def add(parts, last):
        return pl.pallas_call(
            functools.partial(add_kernel, classes=classes, last=last),
            in_specs=[vmem] * len(parts),
            out_specs=vmem,
            out_shape=code,
            compiler_params=limit,
            name="add_sums",
        )(*parts)

    near_codes = [move(c, 0, m) for c, m in zip(codes[1:], near_masks[1:])]
    part_sum = add([codes[0]] + near_codes, False)
    for mask in far_masks:
        part_sum = add([part_sum, move(part_sum, 0, mask)], mask == far_masks[-1])

    near = after(jnp.concatenate([packed, move(packed, 0, 1)], axis=0), twin_codes)
    for mask in reversed(far_masks):
        near = jnp.concatenate([near, move(near, 1, mask)], axis=0)
    near = after(near, near_codes[0])
    own_rows = [near] + [move(near, 1, m) for m in near_masks[1:]]

    own = [part_sum] + [move(part_sum, 0, m) for m in near_masks[1:3]]
    own.append(move(after(part_sum, own_rows[1]), 0, near_masks[3]))
    got = [move(after(c, own[1]), 0, 1) for c in own]
    got_rows = [move(near, 1, 1)] + [move(after(p, *own[1:]), 1, 1) for p in own_rows[1:]]

    def select(tail):
        return pl.pallas_call(
            functools.partial(select_kernel, n_ex=n_ex, rows=rows, tail=tail),
            in_specs=[vmem],
            out_specs=vmem,
            out_shape=jax.ShapeDtypeStruct((total, n_ex * 8), bf16),
            compiler_params=limit,
            name="select_tails" if tail else "select_rows",
        )(after(pick_index, packed))

    x, factor = pl.pallas_call(
        functools.partial(picked_kernel, steps=steps),
        in_specs=[vmem] * 10,
        out_specs=[vmem] * 2,
        out_shape=[
            jax.ShapeDtypeStruct((total, full), bf16),
            jax.ShapeDtypeStruct((classes, 128), f32),
        ],
        scratch_shapes=[pltpu.VMEM((n_ex * 8, main), bf16)],
        compiler_params=limit,
        name="picked_rows",
    )(select(False), select(True), *own_rows, *got_rows)

    span = full // 4
    direct, right, target = pl.pallas_call(
        functools.partial(first_kernel, classes=classes),
        in_specs=[vmem] * 4,
        out_specs=[vmem] * 3,
        out_shape=[
            jax.ShapeDtypeStruct((total, rows), f32),
            jax.ShapeDtypeStruct((classes, total), f32),
            jax.ShapeDtypeStruct((classes, span), f32),
        ],
        scratch_shapes=[pltpu.VMEM((total, span), bf16)],
        compiler_params=limit,
        name="first_products",
    )(feat, own[0], got[0], x)

    scores, resid = pl.pallas_call(
        functools.partial(pursuit_kernel, steps=steps, scale=1.0 / math.sqrt(full)),
        in_specs=[vmem] * 13,
        out_specs=[vmem, anywhere],
        out_shape=[
            jax.ShapeDtypeStruct((steps, rows), f32),
            jax.ShapeDtypeStruct((classes, full), f32),
        ],
        scratch_shapes=[
            pltpu.VMEM((4, classes, span), f32),
            pltpu.VMEM((3, total, span), bf16),
            pltpu.SemaphoreType.DMA((4,)),
        ],
        compiler_params=limit,
        name="pursuit",
    )(labels, feat, x, factor, direct, right, target, *own[1:], *got[1:])
    return scores, resid


def solution(mesh):
    return jax.shard_map(
        functools.partial(on_device, n_ex=mesh.shape["ex"]),
        mesh=mesh,
        in_specs=(P(("grp", "ex"), None), P(("grp", "ex")), P("grp", None)),
        out_specs=(P(None, ("grp", "ex")), P("grp", None)),
        check_vma=False,
    )
```

time: 47.5 us -> 79.3 us (1.67)
  starting transfers between devices: 19.8 us -> 43.3 us
  waiting for transfers between devices: 13.1 us -> 17.7 us
  Pallas kernels: 13.5 us -> 16.6 us
    ppermute x17 -> x21, starting transfers between devices: 19.8 us -> 43.3 us  [move(): return lax.ppermute(x, 'ex', [(d, d ^ mask) for d in range(side, n_ex, 2)])]
    ppermute x17 -> x21, waiting for transfers between devices: 13.1 us -> 17.7 us  [move(): return lax.ppermute(x, 'ex', [(d, d ^ mask) for d in range(side, n_ex, 2)])]
    pallas_call x1, Pallas kernels: 0.18 us -> 1.73 us  [on_device(): pl.pallas_call(functools.partial(pair_kernel, classes=classes), in_specs=...]
  transfers between devices with their start and end apart: 17 -> 21, of which waited for: 9 -> 6; matrix products, arithmetic and copies ran while one was open for 0% -> 0% of each run, Pallas kernels for 10% -> 7%
where the time goes in v9:
time: 79.3 us; the launch traced here: 78.7 us
  starting transfers between devices  43.3 us (55%)
  waiting for transfers between devices  17.7 us (22%)
  Pallas kernels  16.6 us (21%)
  between operations  1.02 us (1%)
    ppermute x21, starting transfers between devices, move(): return lax.ppermute(x, 'ex', [(d, d ^ mask) for d in range(side, n_ex, 2)])  43.3 us
    ppermute x21, waiting for transfers between devices, move(): return lax.ppermute(x, 'ex', [(d, d ^ mask) for d in range(side, n_ex, 2)])  17.7 us
    pallas_call x1, Pallas kernels, on_device(): pl.pallas_call(sums_kernel, in_specs=[hbm] * 3, out_specs=[vmem] * 5, out...  6.55 us
    pallas_call x1, Pallas kernels, on_device(): pl.pallas_call(functools.partial(pursuit_kernel, steps=steps, scale=1.0 /...  4.14 us
    pallas_call x1, Pallas kernels, on_device(): pl.pallas_call(functools.partial(pair_kernel, classes=classes), in_specs=...  1.73 us
  transfers between devices with their start and end apart: 21, of which 6 were waited for; matrix products, arithmetic and copies ran while one was open for 0% of the time, Pallas kernels for 7%

profile of v9, /device:TPU:0, one launch (start us, length us, event | category | flops | bytes accessed | tf_op | source)
XLA Modules:
  0.0 78.7 jit_solution(8776500706839126657)
XLA Ops:
  0.6 6.6 %class_sums.1 = (bf16[640,8192]{1,0:T(8,128)(2,1)S(1)}, f32[16,32,512]{2,1,0:T(8,128)S(1)}, f32[8,128]{1,0:T(8,128)S(1)}, s16[16,136,128]{2,1,0:T(8,128)(2,1)S(1)}, f32[8,8192]{1,0:T(8,128)S(1)}) custom-call(s32[640]{0:T(1024)} %labels_ref.1, s32[3,32]{1,0:T(4,128)} %pick_ref.1, bf16[640,8192]{1,0:T(8,128)(2,1)} %feat_hbm.1), custom_call_target="tpu_custom_call" | custom-call | tf_op jit(solution)/shard_map/class_sums/pallas_call | solution.py:342
  7.3 2.4 %collective-permute-start = (bf16[8,6144]{1,0:T(8,128)(2,1)S(1)}, bf16[8,6144]{1,0:T(8,128)(2,1)S(1)}, u32[]{:S(2)}, u32[]{:S(2)}) collective-permute-start(bf16[8,6144]{1,0:T(8,128)(2,1)S(1)} %pack_rows.1), channel_id=1, source_target_pairs={{0,1},{2,3},{4,5},{6,7},{8,9},{10,11},{12,13},{14,15},{16,17},{18,... | collective-permute-start | bytes 294920 | tf_op jit(solution)/shard_map/ppermute | solution.py:340
  9.6 1.3 %collective-permute-start.1 = (s16[16,136,128]{2,1,0:T(8,128)(2,1)S(1)}, s16[16,136,128]{2,1,0:T(8,128)(2,1)S(1)}, u32[]{:S(2)}, u32[]{:S(2)}) collective-permute-start(s16[16,136,128]{2,1,0:T(8,128)(2,1)S(1)} %get-tuple-element.30), channel_id=1, source_target_pairs={{1,0},{3,2},{5,4},{7,6},{9,8},{11,10},{13,12},{15,14},{17,16},{19,... | collective-permute-start | bytes 1671176 | tf_op jit(solution)/shard_map/ppermute | solution.py:340
  11.0 2.5 %collective-permute-done.1.got_ref = s16[16,136,128]{2,1,0:T(8,128)(2,1)S(1)} collective-permute-done((s16[16,136,128]{2,1,0:T(8,128)(2,1)S(1)}, s16[16,136,128]{2,1,0:T(8,128)(2,1)S(1)}, u32[]{:S(2)}, u32[]{:S(2)}) %collective-permute-start.1) | collective-permute-done | bytes 557088 | tf_op jit(solution)/shard_map/ppermute | solution.py:340
  13.5 0.7 collective-permute-start.2
  14.2 1.7 %pair_sums.1 = (s16[4,136,128]{2,1,0:T(8,128)(2,1)S(1)}, s16[4,136,128]{2,1,0:T(8,128)(2,1)S(1)}, s16[4,136,128]{2,1,0:T(8,128)(2,1)S(1)}, s16[4,136,128]{2,1,0:T(8,128)(2,1)S(1)}) custom-call(f32[16,32,512]{2,1,0:T(8,128)S(1)} %get-tuple-element.32.sums_ref, f32[8,128]{1,0:T(8,128)S(1)} %get-tuple-element.33.tile_ref, ...), custom_call_target="tpu_custom_call" | custom-call | tf_op jit(solution)/shard_map/pair_sums/pallas_call | solution.py:374
  15.9 4.3 %collective-permute-start.3 = (s16[4,136,128]{2,1,0:T(8,128)(2,1)S(1)}, s16[4,136,128]{2,1,0:T(8,128)(2,1)S(1)}, u32[]{:S(2)}, u32[]{:S(2)}) collective-permute-start(s16[4,136,128]{2,1,0:T(8,128)(2,1)S(1)} %get-tuple-element.34), channel_id=1, source_target_pairs={{0,4},{2,6},{4,0},{6,2},{8,12},{10,14},{12,8},{14,10},{16,20},{18,... | collective-permute-start | bytes 417800 | tf_op jit(solution)/shard_map/ppermute | solution.py:340
  20.3 3.9 %collective-permute-done.3.refs_1_ = s16[4,136,128]{2,1,0:T(8,128)(2,1)S(1)} collective-permute-done((s16[4,136,128]{2,1,0:T(8,128)(2,1)S(1)}, s16[4,136,128]{2,1,0:T(8,128)(2,1)S(1)}, u32[]{:S(2)}, u32[]{:S(2)}) %collective-permute-start.3) | collective-permute-done | bytes 139296 | tf_op jit(solution)/shard_map/ppermute | solution.py:340
  24.2 0.7 collective-permute-start.4
  24.9 3.9 %collective-permute-start.8 = (s16[4,136,128]{2,1,0:T(8,128)(2,1)S(1)}, s16[4,136,128]{2,1,0:T(8,128)(2,1)S(1)}, u32[]{:S(2)}, u32[]{:S(2)}) collective-permute-start(s16[4,136,128]{2,1,0:T(8,128)(2,1)S(1)} %get-tuple-element.37), channel_id=1, source_target_pairs={{0,2},{2,0},{4,6},{6,4},{8,10},{10,8},{12,14},{14,12},{16,18},{18,... | collective-permute-start | bytes 417800 | tf_op jit(solution)/shard_map/ppermute | solution.py:340
  28.8 2.4 %collective-permute-start.9 = (s16[4,136,128]{2,1,0:T(8,128)(2,1)S(1)}, s16[4,136,128]{2,1,0:T(8,128)(2,1)S(1)}, u32[]{:S(2)}, u32[]{:S(2)}) collective-permute-start(s16[4,136,128]{2,1,0:T(8,128)(2,1)S(1)} %get-tuple-element.38), channel_id=1, source_target_pairs={{0,6},{2,4},{4,2},{6,0},{8,14},{10,12},{12,10},{14,8},{16,22},{18,... | collective-permute-start | bytes 417800 | tf_op jit(solution)/shard_map/ppermute | solution.py:340
  31.2 0.7 collective-permute-start.5
  31.9 4.8 %collective-permute-done.9.refs_3_ = s16[4,136,128]{2,1,0:T(8,128)(2,1)S(1)} collective-permute-done((s16[4,136,128]{2,1,0:T(8,128)(2,1)S(1)}, s16[4,136,128]{2,1,0:T(8,128)(2,1)S(1)}, u32[]{:S(2)}, u32[]{:S(2)}) %collective-permute-start.9) | collective-permute-done | bytes 139296 | tf_op jit(solution)/shard_map/ppermute | solution.py:340
  36.7 0.5 add_sums.2.refs_0_
  37.2 4.3 %collective-permute-start.10 = (s16[4,136,128]{2,1,0:T(8,128)(2,1)S(1)}, s16[4,136,128]{2,1,0:T(8,128)(2,1)S(1)}, u32[]{:S(2)}, u32[]{:S(2)}) collective-permute-start(s16[4,136,128]{2,1,0:T(8,128)(2,1)S(1)} %add_sums.2.refs_0_), channel_id=1, source_target_pairs={{0,8},{2,10},{4,12},{6,14},{8,0},{10,2},{12,4},{14,6},{16,24},{18,... | collective-permute-start | bytes 417800 | tf_op jit(solution)/shard_map/ppermute | solution.py:340
  41.6 0.7 collective-permute-start.6
  42.3 2.8 %collective-permute-done.10.refs_1_ = s16[4,136,128]{2,1,0:T(8,128)(2,1)S(1)} collective-permute-done((s16[4,136,128]{2,1,0:T(8,128)(2,1)S(1)}, s16[4,136,128]{2,1,0:T(8,128)(2,1)S(1)}, u32[]{:S(2)}, u32[]{:S(2)}) %collective-permute-start.10) | collective-permute-done | bytes 139296 | tf_op jit(solution)/shard_map/ppermute | solution.py:340
  45.4 4.4 %collective-permute-start.11 = (s16[4,136,128]{2,1,0:T(8,128)(2,1)S(1)}, s16[4,136,128]{2,1,0:T(8,128)(2,1)S(1)}, u32[]{:S(2)}, u32[]{:S(2)}) collective-permute-start(s16[4,136,128]{2,1,0:T(8,128)(2,1)S(1)} %add_sums.3.own_ref), channel_id=1, source_target_pairs={{0,4},{2,6},{4,0},{6,2},{8,12},{10,14},{12,8},{14,10},{16,20},{18,... | collective-permute-start | bytes 417800 | tf_op jit(solution)/shard_map/ppermute | solution.py:340
  49.9 2.4 %collective-permute-start.12 = (s16[4,136,128]{2,1,0:T(8,128)(2,1)S(1)}, s16[4,136,128]{2,1,0:T(8,128)(2,1)S(1)}, u32[]{:S(2)}, u32[]{:S(2)}) collective-permute-start(s16[4,136,128]{2,1,0:T(8,128)(2,1)S(1)} %add_sums.3.own_ref), channel_id=1, source_target_pairs={{0,2},{2,0},{4,6},{6,4},{8,10},{10,8},{12,14},{14,12},{16,18},{18,... | collective-permute-start | bytes 417800 | tf_op jit(solution)/shard_map/ppermute | solution.py:340
  52.3 2.9 %collective-permute-start.13 = (s16[4,136,128]{2,1,0:T(8,128)(2,1)S(1)}, s16[4,136,128]{2,1,0:T(8,128)(2,1)S(1)}, u32[]{:S(2)}, u32[]{:S(2)}) collective-permute-start(s16[4,136,128]{2,1,0:T(8,128)(2,1)S(1)} %add_sums.3.own_ref), channel_id=1, source_target_pairs={{0,6},{2,4},{4,2},{6,0},{8,14},{10,12},{12,10},{14,8},{16,22},{18,... | collective-permute-start | bytes 417800 | tf_op jit(solution)/shard_map/ppermute | solution.py:340
  55.2 1.3 %collective-permute-start.7 = (bf16[32,6144]{1,0:T(8,128)(2,1)S(1)}, bf16[32,6144]{1,0:T(8,128)(2,1)S(1)}, u32[]{:S(2)}, u32[]{:S(2)}) collective-permute-start(bf16[32,6144]{1,0:T(8,128)(2,1)S(1)} %pad_maximum_fusion.refs_0_), channel_id=1, source_target_pairs={{1,0},{3,2},{5,4},{7,6},{9,8},{11,10},{13,12},{15,14},{17,16},{19,... | collective-permute-start | bytes 1179656 | tf_op jit(solution)/shard_map/ppermute | solution.py:340
  56.8 3.3 %collective-permute-done.13.refs_2_ = s16[4,136,128]{2,1,0:T(8,128)(2,1)S(1)} collective-permute-done((s16[4,136,128]{2,1,0:T(8,128)(2,1)S(1)}, s16[4,136,128]{2,1,0:T(8,128)(2,1)S(1)}, u32[]{:S(2)}, u32[]{:S(2)}) %collective-permute-start.13) | collective-permute-done | bytes 139296 | tf_op jit(solution)/shard_map/ppermute | solution.py:340
  60.2 1.3 %collective-permute-start.14 = (bf16[32,6144]{1,0:T(8,128)(2,1)S(1)}, bf16[32,6144]{1,0:T(8,128)(2,1)S(1)}, u32[]{:S(2)}, u32[]{:S(2)}) collective-permute-start(bf16[32,6144]{1,0:T(8,128)(2,1)S(1)} %collective-permute-done.4.refs_1_), channel_id=1, source_target_pairs={{1,0},{3,2},{5,4},{7,6},{9,8},{11,10},{13,12},{15,14},{17,16},{19,... | collective-permute-start | bytes 1179656 | tf_op jit(solution)/shard_map/ppermute | solution.py:340
  61.5 1.3 %collective-permute-start.15 = (bf16[32,6144]{1,0:T(8,128)(2,1)S(1)}, bf16[32,6144]{1,0:T(8,128)(2,1)S(1)}, u32[]{:S(2)}, u32[]{:S(2)}) collective-permute-start(bf16[32,6144]{1,0:T(8,128)(2,1)S(1)} %collective-permute-done.5.refs_2_), channel_id=1, source_target_pairs={{1,0},{3,2},{5,4},{7,6},{9,8},{11,10},{13,12},{15,14},{17,16},{19,... | collective-permute-start | bytes 1179656 | tf_op jit(solution)/shard_map/ppermute | solution.py:340
  62.8 1.3 %collective-permute-start.16 = (bf16[32,6144]{1,0:T(8,128)(2,1)S(1)}, bf16[32,6144]{1,0:T(8,128)(2,1)S(1)}, u32[]{:S(2)}, u32[]{:S(2)}) collective-permute-start(bf16[32,6144]{1,0:T(8,128)(2,1)S(1)} %collective-permute-done.6.refs_3_), channel_id=1, source_target_pairs={{1,0},{3,2},{5,4},{7,6},{9,8},{11,10},{13,12},{15,14},{17,16},{19,... | collective-permute-start | bytes 1179656 | tf_op jit(solution)/shard_map/ppermute | solution.py:340
  64.1 3.1 %collective-permute-start.17 = (s16[4,136,128]{2,1,0:T(8,128)(2,1)S(1)}, s16[4,136,128]{2,1,0:T(8,128)(2,1)S(1)}, u32[]{:S(2)}, u32[]{:S(2)}) collective-permute-start(s16[4,136,128]{2,1,0:T(8,128)(2,1)S(1)} %add_sums.3.own_ref), channel_id=1, source_target_pairs={{0,1},{2,3},{4,5},{6,7},{8,9},{10,11},{12,13},{14,15},{16,17},{18,... | collective-permute-start | bytes 417800 | tf_op jit(solution)/shard_map/ppermute | solution.py:340
  67.2 1.3 %collective-permute-start.18 = (s16[4,136,128]{2,1,0:T(8,128)(2,1)S(1)}, s16[4,136,128]{2,1,0:T(8,128)(2,1)S(1)}, u32[]{:S(2)}, u32[]{:S(2)}) collective-permute-start(s16[4,136,128]{2,1,0:T(8,128)(2,1)S(1)} %collective-permute-done.11.refs_0_), channel_id=1, source_target_pairs={{0,1},{2,3},{4,5},{6,7},{8,9},{10,11},{12,13},{14,15},{16,17},{18,... | collective-permute-start | bytes 417800 | tf_op jit(solution)/shard_map/ppermute | solution.py:340
  68.5 1.3 %collective-permute-start.19 = (s16[4,136,128]{2,1,0:T(8,128)(2,1)S(1)}, s16[4,136,128]{2,1,0:T(8,128)(2,1)S(1)}, u32[]{:S(2)}, u32[]{:S(2)}) collective-permute-start(s16[4,136,128]{2,1,0:T(8,128)(2,1)S(1)} %collective-permute-done.12.refs_1_), channel_id=1, source_target_pairs={{0,1},{2,3},{4,5},{6,7},{8,9},{10,11},{12,13},{14,15},{16,17},{18,... | collective-permute-start | bytes 417800 | tf_op jit(solution)/shard_map/ppermute | solution.py:340
  69.8 1.3 %collective-permute-start.20 = (s16[4,136,128]{2,1,0:T(8,128)(2,1)S(1)}, s16[4,136,128]{2,1,0:T(8,128)(2,1)S(1)}, u32[]{:S(2)}, u32[]{:S(2)}) collective-permute-start(s16[4,136,128]{2,1,0:T(8,128)(2,1)S(1)} %collective-permute-done.13.refs_2_), channel_id=1, source_target_pairs={{0,1},{2,3},{4,5},{6,7},{8,9},{10,11},{12,13},{14,15},{16,17},{18,... | collective-permute-start | bytes 417800 | tf_op jit(solution)/shard_map/ppermute | solution.py:340
  71.8 1.5 %picked_rows.1 = (bf16[96,8192]{1,0:T(8,128)(2,1)S(1)}, f32[32,128]{1,0:T(8,128)S(1)}) custom-call(bf16[96,128]{1,0:T(8,128)(2,1)S(1)} %select_rows.1.one_ref, bf16[96,128]{1,0:T(8,128)(2,1)S(1)} %select_tails.1.rest_ref, bf16[32,6144]{1,0:T(8,128)(2,1)S(1)} %pad_maximum_fusion.refs_0_, bf16[32,6144]{1,0:T(8,128)(2,1)S(1)} %collective-permute-done.4.refs_1_, ...), custom_call_target="tpu_custom_call" | custom-call | tf_op jit(solution)/shard_map/picked_rows/pallas_call | solution.py:419
  73.4 1.2 %first_products.1 = (f32[96,640]{1,0:T(8,128)S(1)}, f32[32,96]{1,0:T(8,128)S(1)}, f32[32,2048]{1,0:T(8,128)S(1)}) custom-call(bf16[640,8192]{1,0:T(8,128)(2,1)S(1)} %get-tuple-element.27.feat_ref, s16[4,136,128]{2,1,0:T(8,128)(2,1)S(1)} %add_sums.3.own_ref, s16[4,136,128]{2,1,0:T(8,128)(2,1)S(1)} %collective-permute-done.17.got_ref, ...), custom_call_target="tpu_custom_call" | custom-call | tf_op jit(solution)/shard_map/first_products/pallas_call | solution.py:433
  74.6 4.1 %pursuit.1 = (f32[3,640]{1,0:T(4,128)}, f32[32,8192]{1,0:T(8,128)}) custom-call(s32[640]{0:T(1024)S(1)} %copy-done.1, bf16[640,8192]{1,0:T(8,128)(2,1)S(1)} %get-tuple-element.27.feat_ref, bf16[96,8192]{1,0:T(8,128)(2,1)S(1)} %get-tuple-element.43.x_ref, f32[32,128]{1,0:T(8,128)S(1)} %get-tuple-element.44.factor_ref, ...), custom_call_target="tpu_custom_call" | custom-call | tf_op jit(solution)/shard_map/pursuit/pallas_call | solution.py:447
  (26 shorter events, 1.5 us)
Async XLA Ops:
  0.6 70.5 %copy-start = (s32[3,32]{1,0:T(4,128)S(1)}, s32[3,32]{1,0:T(4,128)}, u32[]{:S(2)}) copy-start(s32[3,32]{1,0:T(4,128)} %pick_ref.1) | copy-start | bytes 1156
  7.2 67.4 %copy-start.1 = (s32[640]{0:T(1024)S(1)}, s32[640]{0:T(1024)}, u32[]{:S(2)}) copy-start(s32[640]{0:T(1024)} %labels_ref.1) | copy-start | bytes 7684
  7.3 3.7 %collective-permute-start = (bf16[8,6144]{1,0:T(8,128)(2,1)S(1)}, bf16[8,6144]{1,0:T(8,128)(2,1)S(1)}, u32[]{:S(2)}, u32[]{:S(2)}) collective-permute-start(bf16[8,6144]{1,0:T(8,128)(2,1)S(1)} %pack_rows.1), channel_id=1, source_target_pairs={{0,1},{2,3},{4,5},{6,7},{8,9},{10,11},{12,13},{14,15},{16,17},{18,... | collective-permute-start | bytes 294920 | tf_op jit(solution)/shard_map/ppermute | solution.py:340
  9.6 3.9 %collective-permute-start.1 = (s16[16,136,128]{2,1,0:T(8,128)(2,1)S(1)}, s16[16,136,128]{2,1,0:T(8,128)(2,1)S(1)}, u32[]{:S(2)}, u32[]{:S(2)}) collective-permute-start(s16[16,136,128]{2,1,0:T(8,128)(2,1)S(1)} %get-tuple-element.30), channel_id=1, source_target_pairs={{1,0},{3,2},{5,4},{7,6},{9,8},{11,10},{13,12},{15,14},{17,16},{19,... | collective-permute-start | bytes 1671176 | tf_op jit(solution)/shard_map/ppermute | solution.py:340
  13.5 6.7 %collective-permute-start.2 = (bf16[16,6144]{1,0:T(8,128)(2,1)S(1)}, bf16[16,6144]{1,0:T(8,128)(2,1)S(1)}, u32[]{:S(2)}, u32[]{:S(2)}) collective-permute-start(bf16[16,6144]{1,0:T(8,128)(2,1)S(1)} %pad_maximum_fusion.1), channel_id=1, source_target_pairs={{1,9},{3,11},{5,13},{7,15},{9,1},{11,3},{13,5},{15,7},{17,25},{19,... | collective-permute-start | bytes 589832 | tf_op jit(solution)/shard_map/ppermute | solution.py:340
  15.9 8.3 %collective-permute-start.3 = (s16[4,136,128]{2,1,0:T(8,128)(2,1)S(1)}, s16[4,136,128]{2,1,0:T(8,128)(2,1)S(1)}, u32[]{:S(2)}, u32[]{:S(2)}) collective-permute-start(s16[4,136,128]{2,1,0:T(8,128)(2,1)S(1)} %get-tuple-element.34), channel_id=1, source_target_pairs={{0,4},{2,6},{4,0},{6,2},{8,12},{10,14},{12,8},{14,10},{16,20},{18,... | collective-permute-start | bytes 417800 | tf_op jit(solution)/shard_map/ppermute | solution.py:340
  24.2 28.1 %collective-permute-start.4 = (bf16[32,6144]{1,0:T(8,128)(2,1)S(1)}, bf16[32,6144]{1,0:T(8,128)(2,1)S(1)}, u32[]{:S(2)}, u32[]{:S(2)}) collective-permute-start(bf16[32,6144]{1,0:T(8,128)(2,1)S(1)} %pad_maximum_fusion.refs_0_), channel_id=1, source_target_pairs={{1,5},{3,7},{5,1},{7,3},{9,13},{11,15},{13,9},{15,11},{17,21},{19,... | collective-permute-start | bytes 1179656 | tf_op jit(solution)/shard_map/ppermute | solution.py:340
  24.9 7.1 %collective-permute-start.8 = (s16[4,136,128]{2,1,0:T(8,128)(2,1)S(1)}, s16[4,136,128]{2,1,0:T(8,128)(2,1)S(1)}, u32[]{:S(2)}, u32[]{:S(2)}) collective-permute-start(s16[4,136,128]{2,1,0:T(8,128)(2,1)S(1)} %get-tuple-element.37), channel_id=1, source_target_pairs={{0,2},{2,0},{4,6},{6,4},{8,10},{10,8},{12,14},{14,12},{16,18},{18,... | collective-permute-start | bytes 417800 | tf_op jit(solution)/shard_map/ppermute | solution.py:340
  28.8 8.0 %collective-permute-start.9 = (s16[4,136,128]{2,1,0:T(8,128)(2,1)S(1)}, s16[4,136,128]{2,1,0:T(8,128)(2,1)S(1)}, u32[]{:S(2)}, u32[]{:S(2)}) collective-permute-start(s16[4,136,128]{2,1,0:T(8,128)(2,1)S(1)} %get-tuple-element.38), channel_id=1, source_target_pairs={{0,6},{2,4},{4,2},{6,0},{8,14},{10,12},{12,10},{14,8},{16,22},{18,... | collective-permute-start | bytes 417800 | tf_op jit(solution)/shard_map/ppermute | solution.py:340
  31.2 30.2 %collective-permute-start.5 = (bf16[32,6144]{1,0:T(8,128)(2,1)S(1)}, bf16[32,6144]{1,0:T(8,128)(2,1)S(1)}, u32[]{:S(2)}, u32[]{:S(2)}) collective-permute-start(bf16[32,6144]{1,0:T(8,128)(2,1)S(1)} %pad_maximum_fusion.refs_0_), channel_id=1, source_target_pairs={{1,3},{3,1},{5,7},{7,5},{9,11},{11,9},{13,15},{15,13},{17,19},{19,... | collective-permute-start | bytes 1179656 | tf_op jit(solution)/shard_map/ppermute | solution.py:340
  37.2 7.8 %collective-permute-start.10 = (s16[4,136,128]{2,1,0:T(8,128)(2,1)S(1)}, s16[4,136,128]{2,1,0:T(8,128)(2,1)S(1)}, u32[]{:S(2)}, u32[]{:S(2)}) collective-permute-start(s16[4,136,128]{2,1,0:T(8,128)(2,1)S(1)} %add_sums.2.refs_0_), channel_id=1, source_target_pairs={{0,8},{2,10},{4,12},{6,14},{8,0},{10,2},{12,4},{14,6},{16,24},{18,... | collective-permute-start | bytes 417800 | tf_op jit(solution)/shard_map/ppermute | solution.py:340
  41.6 21.2 %collective-permute-start.6 = (bf16[32,6144]{1,0:T(8,128)(2,1)S(1)}, bf16[32,6144]{1,0:T(8,128)(2,1)S(1)}, u32[]{:S(2)}, u32[]{:S(2)}) collective-permute-start(bf16[32,6144]{1,0:T(8,128)(2,1)S(1)} %pad_maximum_fusion.refs_0_), channel_id=1, source_target_pairs={{1,7},{3,5},{5,3},{7,1},{9,15},{11,13},{13,11},{15,9},{17,23},{19,... | collective-permute-start | bytes 1179656 | tf_op jit(solution)/shard_map/ppermute | solution.py:340
  45.4 9.8 %collective-permute-start.11 = (s16[4,136,128]{2,1,0:T(8,128)(2,1)S(1)}, s16[4,136,128]{2,1,0:T(8,128)(2,1)S(1)}, u32[]{:S(2)}, u32[]{:S(2)}) collective-permute-start(s16[4,136,128]{2,1,0:T(8,128)(2,1)S(1)} %add_sums.3.own_ref), channel_id=1, source_target_pairs={{0,4},{2,6},{4,0},{6,2},{8,12},{10,14},{12,8},{14,10},{16,20},{18,... | collective-permute-start | bytes 417800 | tf_op jit(solution)/shard_map/ppermute | solution.py:340
  49.9 6.9 %collective-permute-start.12 = (s16[4,136,128]{2,1,0:T(8,128)(2,1)S(1)}, s16[4,136,128]{2,1,0:T(8,128)(2,1)S(1)}, u32[]{:S(2)}, u32[]{:S(2)}) collective-permute-start(s16[4,136,128]{2,1,0:T(8,128)(2,1)S(1)} %add_sums.3.own_ref), channel_id=1, source_target_pairs={{0,2},{2,0},{4,6},{6,4},{8,10},{10,8},{12,14},{14,12},{16,18},{18,... | collective-permute-start | bytes 417800 | tf_op jit(solution)/shard_map/ppermute | solution.py:340
  52.3 7.8 %collective-permute-start.13 = (s16[4,136,128]{2,1,0:T(8,128)(2,1)S(1)}, s16[4,136,128]{2,1,0:T(8,128)(2,1)S(1)}, u32[]{:S(2)}, u32[]{:S(2)}) collective-permute-start(s16[4,136,128]{2,1,0:T(8,128)(2,1)S(1)} %add_sums.3.own_ref), channel_id=1, source_target_pairs={{0,6},{2,4},{4,2},{6,0},{8,14},{10,12},{12,10},{14,8},{16,22},{18,... | collective-permute-start | bytes 417800 | tf_op jit(solution)/shard_map/ppermute | solution.py:340
  55.2 12.0 %collective-permute-start.7 = (bf16[32,6144]{1,0:T(8,128)(2,1)S(1)}, bf16[32,6144]{1,0:T(8,128)(2,1)S(1)}, u32[]{:S(2)}, u32[]{:S(2)}) collective-permute-start(bf16[32,6144]{1,0:T(8,128)(2,1)S(1)} %pad_maximum_fusion.refs_0_), channel_id=1, source_target_pairs={{1,0},{3,2},{5,4},{7,6},{9,8},{11,10},{13,12},{15,14},{17,16},{19,... | collective-permute-start | bytes 1179656 | tf_op jit(solution)/shard_map/ppermute | solution.py:340
  60.2 8.3 %collective-permute-start.14 = (bf16[32,6144]{1,0:T(8,128)(2,1)S(1)}, bf16[32,6144]{1,0:T(8,128)(2,1)S(1)}, u32[]{:S(2)}, u32[]{:S(2)}) collective-permute-start(bf16[32,6144]{1,0:T(8,128)(2,1)S(1)} %collective-permute-done.4.refs_1_), channel_id=1, source_target_pairs={{1,0},{3,2},{5,4},{7,6},{9,8},{11,10},{13,12},{15,14},{17,16},{19,... | collective-permute-start | bytes 1179656 | tf_op jit(solution)/shard_map/ppermute | solution.py:340
  61.5 8.4 %collective-permute-start.15 = (bf16[32,6144]{1,0:T(8,128)(2,1)S(1)}, bf16[32,6144]{1,0:T(8,128)(2,1)S(1)}, u32[]{:S(2)}, u32[]{:S(2)}) collective-permute-start(bf16[32,6144]{1,0:T(8,128)(2,1)S(1)} %collective-permute-done.5.refs_2_), channel_id=1, source_target_pairs={{1,0},{3,2},{5,4},{7,6},{9,8},{11,10},{13,12},{15,14},{17,16},{19,... | collective-permute-start | bytes 1179656 | tf_op jit(solution)/shard_map/ppermute | solution.py:340
  62.8 9.1 %collective-permute-start.16 = (bf16[32,6144]{1,0:T(8,128)(2,1)S(1)}, bf16[32,6144]{1,0:T(8,128)(2,1)S(1)}, u32[]{:S(2)}, u32[]{:S(2)}) collective-permute-start(bf16[32,6144]{1,0:T(8,128)(2,1)S(1)} %collective-permute-done.6.refs_3_), channel_id=1, source_target_pairs={{1,0},{3,2},{5,4},{7,6},{9,8},{11,10},{13,12},{15,14},{17,16},{19,... | collective-permute-start | bytes 1179656 | tf_op jit(solution)/shard_map/ppermute | solution.py:340
  64.1 9.3 %collective-permute-start.17 = (s16[4,136,128]{2,1,0:T(8,128)(2,1)S(1)}, s16[4,136,128]{2,1,0:T(8,128)(2,1)S(1)}, u32[]{:S(2)}, u32[]{:S(2)}) collective-permute-start(s16[4,136,128]{2,1,0:T(8,128)(2,1)S(1)} %add_sums.3.own_ref), channel_id=1, source_target_pairs={{0,1},{2,3},{4,5},{6,7},{8,9},{10,11},{12,13},{14,15},{16,17},{18,... | collective-permute-start | bytes 417800 | tf_op jit(solution)/shard_map/ppermute | solution.py:340
  67.2 7.4 %collective-permute-start.18 = (s16[4,136,128]{2,1,0:T(8,128)(2,1)S(1)}, s16[4,136,128]{2,1,0:T(8,128)(2,1)S(1)}, u32[]{:S(2)}, u32[]{:S(2)}) collective-permute-start(s16[4,136,128]{2,1,0:T(8,128)(2,1)S(1)} %collective-permute-done.11.refs_0_), channel_id=1, source_target_pairs={{0,1},{2,3},{4,5},{6,7},{8,9},{10,11},{12,13},{14,15},{16,17},{18,... | collective-permute-start | bytes 417800 | tf_op jit(solution)/shard_map/ppermute | solution.py:340
  68.5 6.1 %collective-permute-start.19 = (s16[4,136,128]{2,1,0:T(8,128)(2,1)S(1)}, s16[4,136,128]{2,1,0:T(8,128)(2,1)S(1)}, u32[]{:S(2)}, u32[]{:S(2)}) collective-permute-start(s16[4,136,128]{2,1,0:T(8,128)(2,1)S(1)} %collective-permute-done.12.refs_1_), channel_id=1, source_target_pairs={{0,1},{2,3},{4,5},{6,7},{8,9},{10,11},{12,13},{14,15},{16,17},{18,... | collective-permute-start | bytes 417800 | tf_op jit(solution)/shard_map/ppermute | solution.py:340
  69.8 4.8 %collective-permute-start.20 = (s16[4,136,128]{2,1,0:T(8,128)(2,1)S(1)}, s16[4,136,128]{2,1,0:T(8,128)(2,1)S(1)}, u32[]{:S(2)}, u32[]{:S(2)}) collective-permute-start(s16[4,136,128]{2,1,0:T(8,128)(2,1)S(1)} %collective-permute-done.13.refs_2_), channel_id=1, source_target_pairs={{0,1},{2,3},{4,5},{6,7},{8,9},{10,11},{12,13},{14,15},{16,17},{18,... | collective-permute-start | bytes 417800 | tf_op jit(solution)/shard_map/ppermute | solution.py:340

commit v10 on v8

--- a/solution.py
+++ b/solution.py
@@ -10,6 +10,7 @@
 
 ridge = 1.0
 slots = 2
+near_masks = (0, 4, 2, 6)
 f32 = jnp.float32
 bf16 = jnp.bfloat16
 
@@ -51,7 +52,7 @@
 
 
 def sums_kernel(
-    labels_hbm, pick_hbm, feat_hbm, feat_ref, send_ref, keep_ref, held, labels_ref, pick_ref, left, sems, *, n_ex
+    labels_hbm, pick_hbm, feat_hbm, feat_ref, send_ref, keep_ref, labels_ref, pick_ref, left, sems, *, n_ex
 ):
     rows, full = feat_ref.shape
     steps, classes = pick_ref.shape
@@ -96,10 +97,11 @@
     ).astype(bf16)
     count = jnp.sum(jnp.where(member, 1.0, 0.0), axis=1, keepdims=True)
     tile = spread(count, classes // 8)
+    base = groups * classes
     for ref in (send_ref, keep_ref):
-        ref[groups * classes :, :128] = tile
+        ref[base : base + 8, :128] = tile
         if width > 128:
-            ref[groups * classes :, 128:] = jnp.zeros((8, width - 128), f32)
+            ref[base : base + 8, 128:] = jnp.zeros((8, width - 128), f32)
 
     for i in range(n_ex):
         copies[i].wait()
@@ -107,16 +109,21 @@
         k = i % groups
         ref = send_ref if i < groups else keep_ref
         ref[k * classes : (k + 1) * classes, :] = both[:classes]
-        held[:, columns[i]] = both[classes : classes + 8]
-
-
-def pack_kernel(held, rows_ref, *, steps):
+        ref[base + 8 + 8 * k : base + 16 + 8 * k, :] = both[classes : classes + 8]
+
+
+def pack_kernel(keep_ref, got_ref, rows_ref, *, steps, start):
+    lines, main = rows_ref.shape
     used = steps * slots
-    main = rows_ref.shape[1]
-    lines = [held[0:used, :main]]
-    for q in range(slots):
-        lines.append(jnp.concatenate([held[q * steps + u : q * steps + u + 1, main:] for u in range(steps)], axis=1))
-    rows_ref[...] = jnp.concatenate(lines, axis=0).astype(bf16)
+    count = (keep_ref.shape[0] - start) // 8
+    halves = []
+    for ref in (keep_ref, got_ref):
+        halves.append(jnp.concatenate([ref[start + 8 * k : start + 8 * k + 8, :] for k in range(count)], axis=1))
+    out = [h[:used, :main] for h in halves]
+    for h in halves:
+        for q in range(slots):
+            out.append(jnp.concatenate([h[q * steps + u : q * steps + u + 1, main:] for u in range(steps)], axis=1))
+    rows_ref[...] = jnp.concatenate(out, axis=0).astype(bf16)
 
 
 def near_id(mask):
@@ -127,7 +134,7 @@
     far = code_refs[0].shape[0]
     base = 4 * far * classes
     tile = keep_ref[base : base + 8, :128] + got_ref[base : base + 8, :128]
-    for mask, code_ref in zip((0, 4, 2, 6), code_refs):
+    for mask, code_ref in zip(near_masks, code_refs):
         for j in range(far):
             at = pl.ds(pl.multiple_of((j * 4 + near_id(mask)) * classes, classes), classes)
             code_ref[j] = encode(keep_ref[at, :] + got_ref[at, :], tile)
@@ -209,21 +216,25 @@
     bits = n_ex.bit_length() - 1
     for b in range(1, bits):
         spot = spot + (((away >> b) & 1) << (bits - 1 - b))
-    spot = spot + ((away & 1) << (bits - 1))
+    other = away & 1
+    used = steps * slots
     step = lax.broadcasted_iota(jnp.int32, pick.shape, 0)
     line = lax.broadcasted_iota(jnp.int32, (lines, classes), 0)
-    where = spot * 8 + (slots * steps + rank if tail else rank * steps + step)
+    if tail:
+        where = spot * 16 + 2 * used + other * slots + rank
+    else:
+        where = spot * 16 + other * used + rank * steps + step
     hits = [jnp.where(line == where[s : s + 1, :], 1.0, 0.0) for s in range(steps)]
     pad = jnp.zeros((lines, 128 - steps * classes), f32)
     one_ref[...] = jnp.transpose(jnp.concatenate(hits + [pad], axis=1))[: steps * classes].astype(bf16)
 
 
 def picked_kernel(one_ref, rest_ref, *refs, steps):
-    parts, (x_ref, factor_ref, rows_ref) = refs[:-3], refs[-3:]
-    total, full = x_ref.shape
+    parts, (x_ref, rows_ref) = refs[:-2], refs[-2:]
+    total, half = x_ref.shape
     classes = total // steps
     main = rows_ref.shape[1]
-    tail = full - main
+    tail = half - main
     at = 0
     for part in parts:
         rows_ref[at : at + part.shape[0], :] = part[...]
@@ -234,72 +245,61 @@
         rest = jnp.dot(rest_ref[at, :], rows_ref[:, s * tail : (s + 1) * tail], preferred_element_type=f32)
         x_ref[at, main:] = rest.astype(bf16)
 
-    x = x_ref[...]
-    full_gram = nt_dot(x, x)
-    gram = [
+
+def half_target(side, code_ref, x_ref, target_ref, target_at, left_ref, *, classes):
+    half = left_ref.shape[1]
+    far = code_ref.shape[0] // 4
+    width = half // code_ref.shape[0]
+    here = pl.ds(pl.multiple_of(side * half, half), half)
+    for k in range(4 * far):
+        block = k % far * 4 + near_id(near_masks[k // far])
+        target = decode(code_ref[k], classes)[0]
+        target_ref[:, pl.ds(pl.multiple_of(target_at + block * width, width), width)] = target
+        left_ref[:classes, pl.ds(pl.multiple_of(block * width, width), width)] = target.astype(bf16)
+    left_ref[classes:, :] = x_ref[...]
+    return nt_dot(left_ref[...], x_ref[...]), here
+
+
+def half_kernel(feat_ref, code_ref, x_ref, direct_ref, gram_ref, target_ref, left_ref, *, classes):
+    core = lax.axis_index("ex") % 2
+    gram_ref[...], here = half_target(core, code_ref, x_ref, target_ref, 0, left_ref, classes=classes)
+    direct_ref[...] = nt_dot(left_ref[: direct_ref.shape[0], :], feat_ref[:, here])
+
+
+def pursuit_kernel(
+    labels_ref, feat_ref, x_own, x_twin, direct_own, gram_own, target_own, code_ref,
+    scores_ref, resid_hbm, resid_ref, left_ref, sems, *, steps, scale
+):
+    classes, full = resid_ref.shape
+    half = full // 2
+    core = lax.axis_index("ex") % 2
+    gram, other = half_target(1 - core, code_ref, x_twin, resid_ref, (1 - core) * half, left_ref, classes=classes)
+    gram = gram + gram_own[...]
+    blocks = [
         [
-            diagonal(full_gram[a * classes : (a + 1) * classes, b * classes : (b + 1) * classes])
+            diagonal(gram[(a + 1) * classes : (a + 2) * classes, b * classes : (b + 1) * classes])
             + (ridge if a == b else 0.0)
             for b in range(a + 1)
         ]
         for a in range(steps)
     ]
-    factor = factor_all(gram)
-    lane = lax.broadcasted_iota(jnp.int32, (classes, 128), 1)
-    packed = jnp.zeros((classes, 128), f32)
-    for i in range(steps):
-        for j in range(i + 1):
-            packed = jnp.where(lane == i * steps + j, factor[i][j], packed)
-    factor_ref[...] = packed
-
-
-def half_target(side, code_ref, x_ref, target_ref, target_at, left_ref, *, classes):
-    half = left_ref.shape[1]
-    far = code_ref.shape[0] // 4
-    width = half // code_ref.shape[0]
-    used = left_ref.shape[0] - classes
-    here = pl.ds(pl.multiple_of(side * half, half), half)
-    for k in range(4 * far):
-        block = k % far * 4 + near_id((0, 4, 2, 6)[k // far])
-        target = decode(code_ref[k], classes)[0]
-        target_ref[:, pl.ds(pl.multiple_of(target_at + block * width, width), width)] = target
-        left_ref[:classes, pl.ds(pl.multiple_of(block * width, width), width)] = target.astype(bf16)
-    left_ref[classes:, :] = x_ref[:used, here]
-    return nt_dot(left_ref[:classes, :], x_ref[:, here]), here
-
-
-def half_kernel(feat_ref, code_ref, x_ref, direct_ref, right_ref, target_ref, left_ref, *, classes):
-    core = lax.axis_index("ex") % 2
-    right_ref[...], here = half_target(core, code_ref, x_ref, target_ref, 0, left_ref, classes=classes)
-    direct_ref[...] = nt_dot(left_ref[...], feat_ref[:, here])
-
-
-def pursuit_kernel(
-    labels_ref, feat_ref, x_ref, factor_ref, direct_own, right_own, target_own, code_ref,
-    scores_ref, resid_hbm, resid_ref, left_ref, sems, *, steps, scale
-):
-    classes, full = resid_ref.shape
-    half = full // 2
-    core = lax.axis_index("ex") % 2
-    right, other = half_target(1 - core, code_ref, x_ref, resid_ref, (1 - core) * half, left_ref, classes=classes)
-    right = right + right_own[...]
-    rhs = [diagonal(right[:, a * classes : (a + 1) * classes]) for a in range(steps)]
-    factor = [[factor_ref[:, i * steps + j : i * steps + j + 1] for j in range(i + 1)] for i in range(steps)]
-    weights = solve_all(factor, rhs)
+    rhs = [diagonal(gram[:classes, a * classes : (a + 1) * classes]) for a in range(steps)]
+    weights = solve_all(factor_all(blocks), rhs)
     last = weights[steps - 1]
     copies = []
     span = half // 2
-    for source, side in ((target_own, core), (resid_ref, 1 - core)):
+    for x_ref, side in ((x_own, core), (x_twin, 1 - core)):
         for q in range(2):
+            there = slice(q * span, (q + 1) * span)
             here = pl.ds(pl.multiple_of(side * half + q * span, span), span)
-            value = source[:, q * span : (q + 1) * span] if source is target_own else source[:, here]
+            value = target_own[:, there] if x_ref is x_own else resid_ref[:, here]
             for k in range(steps):
-                value = value - last[k] * x_ref[k * classes : (k + 1) * classes, here].astype(f32)
+                value = value - last[k] * x_ref[k * classes : (k + 1) * classes, there].astype(f32)
             resid_ref[:, here] = value
             copies.append(pltpu.make_async_copy(resid_ref.at[:, here], resid_hbm.at[:, here], sems.at[len(copies)]))
             copies[-1].start()
 
-    direct = direct_own[...] + nt_dot(left_ref[...], feat_ref[:, other])
+    direct = direct_own[...] + nt_dot(left_ref[: direct_own.shape[0], :], feat_ref[:, other])
     member = lax.broadcasted_iota(jnp.int32, (classes, direct.shape[1]), 0) == labels_ref[...].reshape(1, direct.shape[1])
     for s in range(steps):
         value = direct[:classes]
@@ -316,12 +316,12 @@
     groups = n_ex // 2
     width = full // n_ex
     total = steps * classes
-    main = full * steps * slots // 8
+    main = full // 2 * steps * slots // 8
     limit = pltpu.CompilerParams(vmem_limit_bytes=16 << 20)
     vmem = pl.BlockSpec(memory_space=pltpu.VMEM)
     hbm = pl.BlockSpec(memory_space=pltpu.HBM)
     anywhere = pl.BlockSpec(memory_space=pl.ANY)
-    half = jax.ShapeDtypeStruct((groups * classes + 8, width), f32)
+    half = jax.ShapeDtypeStruct((groups * (classes + 8) + 8, width), f32)
     code = jax.ShapeDtypeStruct((groups // 4, classes * (width // 128) + 8, 128), jnp.int16)
 
     def swap(x, mask):
@@ -330,11 +330,11 @@
     def after(x, *others):
         return lax.optimization_barrier((x,) + others)[0]
 
-    feat, send, keep, held = pl.pallas_call(
+    feat, send, keep = pl.pallas_call(
         functools.partial(sums_kernel, n_ex=n_ex),
         in_specs=[hbm] * 3,
-        out_specs=[vmem] * 4,
-        out_shape=[pltpu.VMEM((rows, full), bf16), half, half, jax.ShapeDtypeStruct((8, full), f32)],
+        out_specs=[vmem] * 3,
+        out_shape=[pltpu.VMEM((rows, full), bf16), half, half],
         scratch_shapes=[
             pltpu.VMEM(labels.shape, jnp.int32),
             pltpu.VMEM(pick_index.shape, jnp.int32),
@@ -356,6 +356,7 @@
         )(*codes)
 
     far_masks = [8 << b for b in range(n_ex.bit_length() - 4)]
+    got = swap(send, 1)
     codes = pl.pallas_call(
         functools.partial(pair_kernel, classes=classes),
         in_specs=[vmem] * 2,
@@ -363,22 +364,22 @@
         out_shape=[code] * 4,
         compiler_params=limit,
         name="pair_sums",
-    )(keep, swap(send, 1))
+    )(keep, got)
     near = pl.pallas_call(
-        functools.partial(pack_kernel, steps=steps),
-        in_specs=[vmem],
+        functools.partial(pack_kernel, steps=steps, start=groups * classes + 8),
+        in_specs=[vmem] * 2,
         out_specs=vmem,
-        out_shape=jax.ShapeDtypeStruct((8, main), bf16),
+        out_shape=jax.ShapeDtypeStruct((16, main), bf16),
         compiler_params=limit,
         name="pack_rows",
-    )(held)
+    )(keep, got)
     for mask in reversed(far_masks):
         near = jnp.concatenate([near, swap(near, mask)], axis=0)
-    got = [swap(codes[1], 4), swap(codes[2], 2), swap(codes[3], 6)]
-    near = after(near, got[0])
-    parts = [near, swap(near, 4), swap(near, 2), swap(near, 6)]
-    part_sum = add([codes[0]] + got, False)
-
+
+    near_codes = [swap(c, m) for c, m in zip(codes[1:], near_masks[1:])]
+    near = after(near, near_codes[0])
+    part_sum = add([codes[0]] + near_codes, False)
+    parts = [near] + [swap(near, m) for m in near_masks[1:]]
 
     def select(tail, *others):
         return pl.pallas_call(
@@ -394,34 +395,30 @@
     rest = select(True, part_sum)
     for mask in far_masks:
         part_sum = add([part_sum, after(swap(part_sum, mask), one, rest)], mask == far_masks[-1])
-    own_parts = [part_sum, swap(part_sum, 4), swap(part_sum, 2), swap(part_sum, 6)]
-    parts = [after(p, own_parts[2], own_parts[3]) for p in parts]
-    parts = parts + [swap(p, 1) for p in parts]
-
-    x, factor = pl.pallas_call(
+    own_parts = [part_sum] + [swap(part_sum, m) for m in near_masks[1:3]]
+    own_parts.append(swap(after(part_sum, parts[1]), near_masks[3]))
+
+    x = pl.pallas_call(
         functools.partial(picked_kernel, steps=steps),
-        in_specs=[vmem] * (2 + len(parts)),
-        out_specs=[vmem] * 2,
-        out_shape=[
-            jax.ShapeDtypeStruct((total, full), bf16),
-            jax.ShapeDtypeStruct((classes, 128), f32),
-        ],
+        in_specs=[vmem] * 6,
+        out_specs=vmem,
+        out_shape=jax.ShapeDtypeStruct((total, full // 2), bf16),
         scratch_shapes=[pltpu.VMEM((n_ex * 8, main), bf16)],
         compiler_params=limit,
         name="picked_rows",
     )(one, rest, *parts)
 
-    own_parts, x = lax.optimization_barrier((own_parts, x))
-    own_half = jnp.concatenate(own_parts, axis=0)
+    x_twin = swap(x, 1)
+    own_half = jnp.concatenate(after(own_parts, x), axis=0)
     twin_half = swap(own_half, 1)
-    left = pltpu.VMEM((total, full // 2), bf16)
-    direct, right, target = pl.pallas_call(
+    left = pltpu.VMEM((total + classes, full // 2), bf16)
+    direct, gram, target = pl.pallas_call(
         functools.partial(half_kernel, classes=classes),
         in_specs=[vmem] * 3,
         out_specs=[vmem] * 3,
         out_shape=[
             jax.ShapeDtypeStruct((total, rows), f32),
-            jax.ShapeDtypeStruct((classes, total), f32),
+            jax.ShapeDtypeStruct((total + classes, total), f32),
             jax.ShapeDtypeStruct((classes, full // 2), f32),
         ],
         scratch_shapes=[left],
@@ -440,7 +437,7 @@
         scratch_shapes=[pltpu.VMEM((classes, full), f32), left, pltpu.SemaphoreType.DMA((4,))],
         compiler_params=limit,
         name="pursuit",
-    )(labels, feat, x, factor, direct, right, target, twin_half)
+    )(labels, feat, x, x_twin, direct, gram, target, twin_half)
     return scores, resid
 
 

time: 47.5 us -> 52.3 us (1.10)
  waiting for transfers between devices: 13.1 us -> 19.9 us
  Pallas kernels: 13.5 us -> 12.1 us
    ppermute x17 -> x14, waiting for transfers between devices: 13.1 us -> 19.9 us  [swap(): return lax.ppermute(x, 'ex', [(d, d ^ mask) for d in range(n_ex)])]
    pallas_call x1, Pallas kernels: 1.39 us -> 0.41 us  [on_device(): pl.pallas_call(functools.partial(picked_kernel, steps=steps), in_specs=[v...]
    ppermute x17 -> x14, starting transfers between devices: 19.8 us -> 19.3 us  [swap(): return lax.ppermute(x, 'ex', [(d, d ^ mask) for d in range(n_ex)])]
  transfers between devices with their start and end apart: 17 -> 14, of which waited for: 9 -> 7; matrix products, arithmetic and copies ran while one was open for 0% -> 0% of each run, Pallas kernels for 10% -> 7%
where the time goes in v10:
time: 52.3 us; the launch traced here: 52.1 us
  waiting for transfers between devices  19.9 us (38%)
  starting transfers between devices  19.3 us (37%)
  Pallas kernels  12.1 us (23%)
  between operations  0.77 us (1%)
    ppermute x14, waiting for transfers between devices, swap(): return lax.ppermute(x, 'ex', [(d, d ^ mask) for d in range(n_ex)])  19.9 us
    ppermute x14, starting transfers between devices, swap(): return lax.ppermute(x, 'ex', [(d, d ^ mask) for d in range(n_ex)])  19.3 us
    pallas_call x1, Pallas kernels, on_device(): pl.pallas_call(functools.partial(sums_kernel, n_ex=n_ex), in_specs=[hbm]...  5.02 us
    pallas_call x1, Pallas kernels, on_device(): pl.pallas_call(functools.partial(pursuit_kernel, steps=steps, scale=1.0 /...  3.19 us
    pallas_call x1, Pallas kernels, on_device(): pl.pallas_call(functools.partial(half_kernel, classes=classes), in_specs=...  2.06 us
  transfers between devices with their start and end apart: 14, of which 7 were waited for; matrix products, arithmetic and copies ran while one was open for 0% of the time, Pallas kernels for 7%

profile of v10, /device:TPU:0, one launch (start us, length us, event | category | flops | bytes accessed | tf_op | source)
XLA Modules:
  0.0 52.1 jit_solution(9469932241003601776)
XLA Ops:
  0.6 5.0 %class_sums.1 = (bf16[640,8192]{1,0:T(8,128)(2,1)S(1)}, f32[328,512]{1,0:T(8,128)S(1)}, f32[328,512]{1,0:T(8,128)S(1)}) custom-call(s32[640]{0:T(1024)} %labels_ref.1, s32[3,32]{1,0:T(4,128)} %pick_ref.1, bf16[640,8192]{1,0:T(8,128)(2,1)} %feat_hbm.1), custom_call_target="tpu_custom_call" | custom-call | tf_op jit(solution)/shard_map/class_sums/pallas_call | solution.py:333
  5.7 0.0 copy-start.1
  5.7 0.5 collective-permute-start
  6.2 1.7 %collective-permute-done.got_ref = f32[328,512]{1,0:T(8,128)S(1)} collective-permute-done((f32[328,512]{1,0:T(8,128)S(1)}, f32[328,512]{1,0:T(8,128)S(1)}, u32[]{:S(2)}, u32[]{:S(2)}) %collective-permute-start) | collective-permute-done | bytes 671776 | tf_op jit(solution)/shard_map/ppermute | solution.py:328
  8.0 4.0 %collective-permute-start.4 = (bf16[16,3072]{1,0:T(8,128)(2,1)S(1)}, bf16[16,3072]{1,0:T(8,128)(2,1)S(1)}, u32[]{:S(2)}, u32[]{:S(2)}) collective-permute-start(bf16[16,3072]{1,0:T(8,128)(2,1)S(1)} %pack_rows.1), channel_id=1, source_target_pairs={{0,8},{1,9},{2,10},{3,11},{4,12},{5,13},{6,14},{7,15},{8,0},{9,1},... | collective-permute-start | bytes 294920 | tf_op jit(solution)/shard_map/ppermute | solution.py:328
  12.0 0.2 pair_sums.1
  12.2 1.6 %collective-permute-start.1 = (s16[2,136,128]{2,1,0:T(8,128)(2,1)S(1)}, s16[2,136,128]{2,1,0:T(8,128)(2,1)S(1)}, u32[]{:S(2)}, u32[]{:S(2)}) collective-permute-start(s16[2,136,128]{2,1,0:T(8,128)(2,1)S(1)} %get-tuple-element.24), channel_id=1, source_target_pairs={{0,4},{1,5},{2,6},{3,7},{4,0},{5,1},{6,2},{7,3},{8,12},{9,13},{10,... | collective-permute-start | bytes 208904 | tf_op jit(solution)/shard_map/ppermute | solution.py:328
  13.8 3.5 %collective-permute-done.4 = bf16[16,3072]{1,0:T(8,128)(2,1)S(1)} collective-permute-done((bf16[16,3072]{1,0:T(8,128)(2,1)S(1)}, bf16[16,3072]{1,0:T(8,128)(2,1)S(1)}, u32[]{:S(2)}, u32[]{:S(2)}) %collective-permute-start.4) | collective-permute-done | bytes 98336 | tf_op jit(solution)/shard_map/ppermute | solution.py:328
  17.3 0.0 collective-permute-done.1.refs_1_
  17.4 1.0 %collective-permute-start.5 = (bf16[32,3072]{1,0:T(8,128)(2,1)S(1)}, bf16[32,3072]{1,0:T(8,128)(2,1)S(1)}, u32[]{:S(2)}, u32[]{:S(2)}) collective-permute-start(bf16[32,3072]{1,0:T(8,128)(2,1)S(1)} %pad_maximum_fusion.refs_0_), channel_id=1, source_target_pairs={{0,4},{1,5},{2,6},{3,7},{4,0},{5,1},{6,2},{7,3},{8,12},{9,13},{10,... | collective-permute-start | bytes 589832 | tf_op jit(solution)/shard_map/ppermute | solution.py:328
  18.3 2.1 %collective-permute-start.7 = (bf16[32,3072]{1,0:T(8,128)(2,1)S(1)}, bf16[32,3072]{1,0:T(8,128)(2,1)S(1)}, u32[]{:S(2)}, u32[]{:S(2)}) collective-permute-start(bf16[32,3072]{1,0:T(8,128)(2,1)S(1)} %pad_maximum_fusion.refs_0_), channel_id=1, source_target_pairs={{0,6},{1,7},{2,4},{3,5},{4,2},{5,3},{6,0},{7,1},{8,14},{9,15},{10,... | collective-permute-start | bytes 589832 | tf_op jit(solution)/shard_map/ppermute | solution.py:328
  20.5 0.5 collective-permute-start.6
  20.9 1.6 %collective-permute-start.2 = (s16[2,136,128]{2,1,0:T(8,128)(2,1)S(1)}, s16[2,136,128]{2,1,0:T(8,128)(2,1)S(1)}, u32[]{:S(2)}, u32[]{:S(2)}) collective-permute-start(s16[2,136,128]{2,1,0:T(8,128)(2,1)S(1)} %get-tuple-element.25), channel_id=1, source_target_pairs={{0,2},{1,3},{2,0},{3,1},{4,6},{5,7},{6,4},{7,5},{8,10},{9,11},{10,... | collective-permute-start | bytes 208904 | tf_op jit(solution)/shard_map/ppermute | solution.py:328
  22.5 0.8 %collective-permute-start.3 = (s16[2,136,128]{2,1,0:T(8,128)(2,1)S(1)}, s16[2,136,128]{2,1,0:T(8,128)(2,1)S(1)}, u32[]{:S(2)}, u32[]{:S(2)}) collective-permute-start(s16[2,136,128]{2,1,0:T(8,128)(2,1)S(1)} %get-tuple-element.26), channel_id=1, source_target_pairs={{0,6},{1,7},{2,4},{3,5},{4,2},{5,3},{6,0},{7,1},{8,14},{9,15},{10,... | collective-permute-start | bytes 208904 | tf_op jit(solution)/shard_map/ppermute | solution.py:328
  23.3 9.5 %collective-permute-done.2.refs_2_ = s16[2,136,128]{2,1,0:T(8,128)(2,1)S(1)} collective-permute-done((s16[2,136,128]{2,1,0:T(8,128)(2,1)S(1)}, s16[2,136,128]{2,1,0:T(8,128)(2,1)S(1)}, u32[]{:S(2)}, u32[]{:S(2)}) %collective-permute-start.2) | collective-permute-done | bytes 69664 | tf_op jit(solution)/shard_map/ppermute | solution.py:328
  32.8 0.3 add_sums.2.refs_0_
  33.1 3.4 %collective-permute-start.9 = (s16[2,136,128]{2,1,0:T(8,128)(2,1)S(1)}, s16[2,136,128]{2,1,0:T(8,128)(2,1)S(1)}, u32[]{:S(2)}, u32[]{:S(2)}) collective-permute-start(s16[2,136,128]{2,1,0:T(8,128)(2,1)S(1)} %add_sums.2.refs_0_), channel_id=1, source_target_pairs={{0,8},{1,9},{2,10},{3,11},{4,12},{5,13},{6,14},{7,15},{8,0},{9,1},... | collective-permute-start | bytes 208904 | tf_op jit(solution)/shard_map/ppermute | solution.py:328
  36.6 0.3 select_tails.1.rest_ref
  36.9 0.3 select_rows.1.one_ref
  37.2 1.6 %collective-permute-done.9.refs_1_ = s16[2,136,128]{2,1,0:T(8,128)(2,1)S(1)} collective-permute-done((s16[2,136,128]{2,1,0:T(8,128)(2,1)S(1)}, s16[2,136,128]{2,1,0:T(8,128)(2,1)S(1)}, u32[]{:S(2)}, u32[]{:S(2)}) %collective-permute-start.9) | collective-permute-done | bytes 69664 | tf_op jit(solution)/shard_map/ppermute | solution.py:328
  38.8 0.3 add_sums.3
  39.1 0.6 %collective-permute-start.11 = (s16[2,136,128]{2,1,0:T(8,128)(2,1)S(1)}, s16[2,136,128]{2,1,0:T(8,128)(2,1)S(1)}, u32[]{:S(2)}, u32[]{:S(2)}) collective-permute-start(s16[2,136,128]{2,1,0:T(8,128)(2,1)S(1)} %add_sums.3), channel_id=1, source_target_pairs={{0,2},{1,3},{2,0},{3,1},{4,6},{5,7},{6,4},{7,5},{8,10},{9,11},{10,... | collective-permute-start | bytes 208904 | tf_op jit(solution)/shard_map/ppermute | solution.py:328
  39.7 1.7 %collective-permute-start.10 = (s16[2,136,128]{2,1,0:T(8,128)(2,1)S(1)}, s16[2,136,128]{2,1,0:T(8,128)(2,1)S(1)}, u32[]{:S(2)}, u32[]{:S(2)}) collective-permute-start(s16[2,136,128]{2,1,0:T(8,128)(2,1)S(1)} %add_sums.3), channel_id=1, source_target_pairs={{0,4},{1,5},{2,6},{3,7},{4,0},{5,1},{6,2},{7,3},{8,12},{9,13},{10,... | collective-permute-start | bytes 208904 | tf_op jit(solution)/shard_map/ppermute | solution.py:328
  41.5 1.2 %collective-permute-start.12 = (s16[2,136,128]{2,1,0:T(8,128)(2,1)S(1)}, s16[2,136,128]{2,1,0:T(8,128)(2,1)S(1)}, u32[]{:S(2)}, u32[]{:S(2)}) collective-permute-start(s16[2,136,128]{2,1,0:T(8,128)(2,1)S(1)} %add_sums.3), channel_id=1, source_target_pairs={{0,6},{1,7},{2,4},{3,5},{4,2},{5,3},{6,0},{7,1},{8,14},{9,15},{10,... | collective-permute-start | bytes 208904 | tf_op jit(solution)/shard_map/ppermute | solution.py:328
  42.7 0.4 picked_rows.1.x_ref.x_own
  43.1 0.1 collective-permute-start.8
  43.2 0.6 %collective-permute-done.11 = s16[2,136,128]{2,1,0:T(8,128)(2,1)S(1)} collective-permute-done((s16[2,136,128]{2,1,0:T(8,128)(2,1)S(1)}, s16[2,136,128]{2,1,0:T(8,128)(2,1)S(1)}, u32[]{:S(2)}, u32[]{:S(2)}) %collective-permute-start.11) | collective-permute-done | bytes 69664 | tf_op jit(solution)/shard_map/ppermute | solution.py:328
  43.8 0.2 collective-permute-done.10
  44.0 2.6 %collective-permute-done.12 = s16[2,136,128]{2,1,0:T(8,128)(2,1)S(1)} collective-permute-done((s16[2,136,128]{2,1,0:T(8,128)(2,1)S(1)}, s16[2,136,128]{2,1,0:T(8,128)(2,1)S(1)}, u32[]{:S(2)}, u32[]{:S(2)}) %collective-permute-start.12) | collective-permute-done | bytes 69664 | tf_op jit(solution)/shard_map/ppermute | solution.py:328
  46.7 0.1 collective-permute-start.13
  46.8 2.1 %own_half_products.1 = (f32[96,640]{1,0:T(8,128)S(1)}, f32[128,96]{1,0:T(8,128)S(1)}, f32[32,4096]{1,0:T(8,128)S(1)}) custom-call(bf16[640,8192]{1,0:T(8,128)(2,1)S(1)} %get-tuple-element.20.feat_ref, s16[8,136,128]{2,1,0:T(8,128)(2,1)S(1)} %constant_dynamic-update-slice_fusion.code_ref, bf16[96,4096]{1,0:T(8,128)(2,1)S(1)} %picked_rows.1.x_ref.x_own), custom_call_target="tpu_custom_call" | custom-call | tf_op jit(solution)/shard_map/own_half_products/pallas_call | solution.py:415
  48.9 3.2 %pursuit.1 = (f32[3,640]{1,0:T(4,128)}, f32[32,8192]{1,0:T(8,128)}) custom-call(s32[640]{0:T(1024)S(1)} %copy-done.1, bf16[640,8192]{1,0:T(8,128)(2,1)S(1)} %get-tuple-element.20.feat_ref, bf16[96,4096]{1,0:T(8,128)(2,1)S(1)} %picked_rows.1.x_ref.x_own, bf16[96,4096]{1,0:T(8,128)(2,1)S(1)} %collective-permute-done.8.x_twin, ...), custom_call_target="tpu_custom_call" | custom-call | tf_op jit(solution)/shard_map/pursuit/pallas_call | solution.py:429
  (15 shorter events, 0.1 us)
Async XLA Ops:
  0.6 35.9 %copy-start = (s32[3,32]{1,0:T(4,128)S(1)}, s32[3,32]{1,0:T(4,128)}, u32[]{:S(2)}) copy-start(s32[3,32]{1,0:T(4,128)} %pick_ref.1) | copy-start | bytes 1156
  5.7 43.2 %copy-start.1 = (s32[640]{0:T(1024)S(1)}, s32[640]{0:T(1024)}, u32[]{:S(2)}) copy-start(s32[640]{0:T(1024)} %labels_ref.1) | copy-start | bytes 7684
  5.7 2.3 %collective-permute-start = (f32[328,512]{1,0:T(8,128)S(1)}, f32[328,512]{1,0:T(8,128)S(1)}, u32[]{:S(2)}, u32[]{:S(2)}) collective-permute-start(f32[328,512]{1,0:T(8,128)S(1)} %get-tuple-element.22), channel_id=1, source_target_pairs={{0,1},{1,0},{2,3},{3,2},{4,5},{5,4},{6,7},{7,6},{8,9},{9,8},{10,11... | collective-permute-start | bytes 2015240 | tf_op jit(solution)/shard_map/ppermute | solution.py:328
  8.0 9.3 %collective-permute-start.4 = (bf16[16,3072]{1,0:T(8,128)(2,1)S(1)}, bf16[16,3072]{1,0:T(8,128)(2,1)S(1)}, u32[]{:S(2)}, u32[]{:S(2)}) collective-permute-start(bf16[16,3072]{1,0:T(8,128)(2,1)S(1)} %pack_rows.1), channel_id=1, source_target_pairs={{0,8},{1,9},{2,10},{3,11},{4,12},{5,13},{6,14},{7,15},{8,0},{9,1},... | collective-permute-start | bytes 294920 | tf_op jit(solution)/shard_map/ppermute | solution.py:328
  12.2 5.2 %collective-permute-start.1 = (s16[2,136,128]{2,1,0:T(8,128)(2,1)S(1)}, s16[2,136,128]{2,1,0:T(8,128)(2,1)S(1)}, u32[]{:S(2)}, u32[]{:S(2)}) collective-permute-start(s16[2,136,128]{2,1,0:T(8,128)(2,1)S(1)} %get-tuple-element.24), channel_id=1, source_target_pairs={{0,4},{1,5},{2,6},{3,7},{4,0},{5,1},{6,2},{7,3},{8,12},{9,13},{10,... | collective-permute-start | bytes 208904 | tf_op jit(solution)/shard_map/ppermute | solution.py:328
  17.4 24.1 %collective-permute-start.5 = (bf16[32,3072]{1,0:T(8,128)(2,1)S(1)}, bf16[32,3072]{1,0:T(8,128)(2,1)S(1)}, u32[]{:S(2)}, u32[]{:S(2)}) collective-permute-start(bf16[32,3072]{1,0:T(8,128)(2,1)S(1)} %pad_maximum_fusion.refs_0_), channel_id=1, source_target_pairs={{0,4},{1,5},{2,6},{3,7},{4,0},{5,1},{6,2},{7,3},{8,12},{9,13},{10,... | collective-permute-start | bytes 589832 | tf_op jit(solution)/shard_map/ppermute | solution.py:328
  18.3 24.3 %collective-permute-start.7 = (bf16[32,3072]{1,0:T(8,128)(2,1)S(1)}, bf16[32,3072]{1,0:T(8,128)(2,1)S(1)}, u32[]{:S(2)}, u32[]{:S(2)}) collective-permute-start(bf16[32,3072]{1,0:T(8,128)(2,1)S(1)} %pad_maximum_fusion.refs_0_), channel_id=1, source_target_pairs={{0,6},{1,7},{2,4},{3,5},{4,2},{5,3},{6,0},{7,1},{8,14},{9,15},{10,... | collective-permute-start | bytes 589832 | tf_op jit(solution)/shard_map/ppermute | solution.py:328
  20.5 22.2 %collective-permute-start.6 = (bf16[32,3072]{1,0:T(8,128)(2,1)S(1)}, bf16[32,3072]{1,0:T(8,128)(2,1)S(1)}, u32[]{:S(2)}, u32[]{:S(2)}) collective-permute-start(bf16[32,3072]{1,0:T(8,128)(2,1)S(1)} %pad_maximum_fusion.refs_0_), channel_id=1, source_target_pairs={{0,2},{1,3},{2,0},{3,1},{4,6},{5,7},{6,4},{7,5},{8,10},{9,11},{10,... | collective-permute-start | bytes 589832 | tf_op jit(solution)/shard_map/ppermute | solution.py:328
  20.9 11.9 %collective-permute-start.2 = (s16[2,136,128]{2,1,0:T(8,128)(2,1)S(1)}, s16[2,136,128]{2,1,0:T(8,128)(2,1)S(1)}, u32[]{:S(2)}, u32[]{:S(2)}) collective-permute-start(s16[2,136,128]{2,1,0:T(8,128)(2,1)S(1)} %get-tuple-element.25), channel_id=1, source_target_pairs={{0,2},{1,3},{2,0},{3,1},{4,6},{5,7},{6,4},{7,5},{8,10},{9,11},{10,... | collective-permute-start | bytes 208904 | tf_op jit(solution)/shard_map/ppermute | solution.py:328
  22.5 10.4 %collective-permute-start.3 = (s16[2,136,128]{2,1,0:T(8,128)(2,1)S(1)}, s16[2,136,128]{2,1,0:T(8,128)(2,1)S(1)}, u32[]{:S(2)}, u32[]{:S(2)}) collective-permute-start(s16[2,136,128]{2,1,0:T(8,128)(2,1)S(1)} %get-tuple-element.26), channel_id=1, source_target_pairs={{0,6},{1,7},{2,4},{3,5},{4,2},{5,3},{6,0},{7,1},{8,14},{9,15},{10,... | collective-permute-start | bytes 208904 | tf_op jit(solution)/shard_map/ppermute | solution.py:328
  33.1 5.7 %collective-permute-start.9 = (s16[2,136,128]{2,1,0:T(8,128)(2,1)S(1)}, s16[2,136,128]{2,1,0:T(8,128)(2,1)S(1)}, u32[]{:S(2)}, u32[]{:S(2)}) collective-permute-start(s16[2,136,128]{2,1,0:T(8,128)(2,1)S(1)} %add_sums.2.refs_0_), channel_id=1, source_target_pairs={{0,8},{1,9},{2,10},{3,11},{4,12},{5,13},{6,14},{7,15},{8,0},{9,1},... | collective-permute-start | bytes 208904 | tf_op jit(solution)/shard_map/ppermute | solution.py:328
  39.1 4.7 %collective-permute-start.11 = (s16[2,136,128]{2,1,0:T(8,128)(2,1)S(1)}, s16[2,136,128]{2,1,0:T(8,128)(2,1)S(1)}, u32[]{:S(2)}, u32[]{:S(2)}) collective-permute-start(s16[2,136,128]{2,1,0:T(8,128)(2,1)S(1)} %add_sums.3), channel_id=1, source_target_pairs={{0,2},{1,3},{2,0},{3,1},{4,6},{5,7},{6,4},{7,5},{8,10},{9,11},{10,... | collective-permute-start | bytes 208904 | tf_op jit(solution)/shard_map/ppermute | solution.py:328
  39.7 4.3 %collective-permute-start.10 = (s16[2,136,128]{2,1,0:T(8,128)(2,1)S(1)}, s16[2,136,128]{2,1,0:T(8,128)(2,1)S(1)}, u32[]{:S(2)}, u32[]{:S(2)}) collective-permute-start(s16[2,136,128]{2,1,0:T(8,128)(2,1)S(1)} %add_sums.3), channel_id=1, source_target_pairs={{0,4},{1,5},{2,6},{3,7},{4,0},{5,1},{6,2},{7,3},{8,12},{9,13},{10,... | collective-permute-start | bytes 208904 | tf_op jit(solution)/shard_map/ppermute | solution.py:328
  41.5 5.2 %collective-permute-start.12 = (s16[2,136,128]{2,1,0:T(8,128)(2,1)S(1)}, s16[2,136,128]{2,1,0:T(8,128)(2,1)S(1)}, u32[]{:S(2)}, u32[]{:S(2)}) collective-permute-start(s16[2,136,128]{2,1,0:T(8,128)(2,1)S(1)} %add_sums.3), channel_id=1, source_target_pairs={{0,6},{1,7},{2,4},{3,5},{4,2},{5,3},{6,0},{7,1},{8,14},{9,15},{10,... | collective-permute-start | bytes 208904 | tf_op jit(solution)/shard_map/ppermute | solution.py:328
  43.1 5.8 %collective-permute-start.8 = (bf16[96,4096]{1,0:T(8,128)(2,1)S(1)}, bf16[96,4096]{1,0:T(8,128)(2,1)S(1)}, u32[]{:S(2)}, u32[]{:S(2)}) collective-permute-start(bf16[96,4096]{1,0:T(8,128)(2,1)S(1)} %picked_rows.1.x_ref.x_own), channel_id=1, source_target_pairs={{0,1},{1,0},{2,3},{3,2},{4,5},{5,4},{6,7},{7,6},{8,9},{9,8},{10,11... | collective-permute-start | bytes 2359304 | tf_op jit(solution)/shard_map/ppermute | solution.py:328
  46.7 2.1 %collective-permute-start.13 = (s16[8,136,128]{2,1,0:T(8,128)(2,1)S(1)}, s16[8,136,128]{2,1,0:T(8,128)(2,1)S(1)}, u32[]{:S(2)}, u32[]{:S(2)}) collective-permute-start(s16[8,136,128]{2,1,0:T(8,128)(2,1)S(1)} %constant_dynamic-update-slice_fusion.code_ref), channel_id=1, source_target_pairs={{0,1},{1,0},{2,3},{3,2},{4,5},{5,4},{6,7},{7,6},{8,9},{9,8},{10,11... | collective-permute-start | bytes 835592 | tf_op jit(solution)/shard_map/ppermute | solution.py:328

commit v11 on v10

--- a/solution.py
+++ b/solution.py
@@ -373,14 +373,8 @@
         compiler_params=limit,
         name="pack_rows",
     )(keep, got)
-    for mask in reversed(far_masks):
-        near = jnp.concatenate([near, swap(near, mask)], axis=0)
-
     near_codes = [swap(c, m) for c, m in zip(codes[1:], near_masks[1:])]
-    near = after(near, near_codes[0])
     part_sum = add([codes[0]] + near_codes, False)
-    parts = [near] + [swap(near, m) for m in near_masks[1:]]
-
     def select(tail, *others):
         return pl.pallas_call(
             functools.partial(select_kernel, n_ex=n_ex, rows=rows, tail=tail),
@@ -391,10 +385,14 @@
             name="select_tails" if tail else "select_rows",
         )(after(pick_index, *others))
 
-    one = select(False, part_sum)
-    rest = select(True, part_sum)
-    for mask in far_masks:
-        part_sum = add([part_sum, after(swap(part_sum, mask), one, rest)], mask == far_masks[-1])
+    one = select(False, codes[0])
+    rest = select(True, codes[0])
+    for far, mask in zip(reversed(far_masks), far_masks):
+        far_rows = swap(near, far)
+        more = swap(after(part_sum, far_rows, one, rest), mask)
+        near = jnp.concatenate([after(near, more), far_rows], axis=0)
+        part_sum = add([part_sum, more], mask == far_masks[-1])
+    parts = [near] + [swap(near, m) for m in near_masks[1:]]
     own_parts = [part_sum] + [swap(part_sum, m) for m in near_masks[1:3]]
     own_parts.append(swap(after(part_sum, parts[1]), near_masks[3]))
 

time: 52.3 us -> 45.5 us (0.87)
  starting transfers between devices: 19.3 us -> 12.8 us
    ppermute x14, starting transfers between devices: 19.3 us -> 12.8 us  [swap(): return lax.ppermute(x, 'ex', [(d, d ^ mask) for d in range(n_ex)])]
  transfers between devices with their start and end apart: 14 -> 14, of which waited for: 7 -> 10; matrix products, arithmetic and copies ran while one was open for 0% -> 0% of each run, Pallas kernels for 7% -> 9%
where the time goes in v11:
time: 45.5 us; the launch traced here: 45.3 us
  waiting for transfers between devices  19.4 us (43%)
  starting transfers between devices  12.8 us (28%)
  Pallas kernels  12.1 us (27%)
  between operations  0.79 us (2%)
    ppermute x14, waiting for transfers between devices, swap(): return lax.ppermute(x, 'ex', [(d, d ^ mask) for d in range(n_ex)])  19.4 us
    ppermute x14, starting transfers between devices, swap(): return lax.ppermute(x, 'ex', [(d, d ^ mask) for d in range(n_ex)])  12.8 us
    pallas_call x1, Pallas kernels, on_device(): pl.pallas_call(functools.partial(sums_kernel, n_ex=n_ex), in_specs=[hbm]...  5.02 us
    pallas_call x1, Pallas kernels, on_device(): pl.pallas_call(functools.partial(pursuit_kernel, steps=steps, scale=1.0 /...  3.19 us
    pallas_call x1, Pallas kernels, on_device(): pl.pallas_call(functools.partial(half_kernel, classes=classes), in_specs=...  2.06 us
  transfers between devices with their start and end apart: 14, of which 10 were waited for; matrix products, arithmetic and copies ran while one was open for 0% of the time, Pallas kernels for 9%

profile of v11, /device:TPU:0, one launch (start us, length us, event | category | flops | bytes accessed | tf_op | source)
XLA Modules:
  0.0 45.3 jit_solution(10031512243946359975)
XLA Ops:
  0.6 5.0 %class_sums.1 = (bf16[640,8192]{1,0:T(8,128)(2,1)S(1)}, f32[328,512]{1,0:T(8,128)S(1)}, f32[328,512]{1,0:T(8,128)S(1)}) custom-call(s32[640]{0:T(1024)} %labels_ref.1, s32[3,32]{1,0:T(4,128)} %pick_ref.1, bf16[640,8192]{1,0:T(8,128)(2,1)} %feat_hbm.1), custom_call_target="tpu_custom_call" | custom-call | tf_op jit(solution)/shard_map/class_sums/pallas_call | solution.py:333
  5.7 0.5 %collective-permute-start = (f32[328,512]{1,0:T(8,128)S(1)}, f32[328,512]{1,0:T(8,128)S(1)}, u32[]{:S(2)}, u32[]{:S(2)}) collective-permute-start(f32[328,512]{1,0:T(8,128)S(1)} %get-tuple-element.22), channel_id=1, source_target_pairs={{0,1},{1,0},{2,3},{3,2},{4,5},{5,4},{6,7},{7,6},{8,9},{9,8},{10,11... | collective-permute-start | bytes 2015240 | tf_op jit(solution)/shard_map/ppermute | solution.py:328
  6.2 1.7 %collective-permute-done.got_ref = f32[328,512]{1,0:T(8,128)S(1)} collective-permute-done((f32[328,512]{1,0:T(8,128)S(1)}, f32[328,512]{1,0:T(8,128)S(1)}, u32[]{:S(2)}, u32[]{:S(2)}) %collective-permute-start) | collective-permute-done | bytes 671776 | tf_op jit(solution)/shard_map/ppermute | solution.py:328
  8.0 4.0 %collective-permute-start.4 = (bf16[16,3072]{1,0:T(8,128)(2,1)S(1)}, bf16[16,3072]{1,0:T(8,128)(2,1)S(1)}, u32[]{:S(2)}, u32[]{:S(2)}) collective-permute-start(bf16[16,3072]{1,0:T(8,128)(2,1)S(1)} %pack_rows.1), channel_id=1, source_target_pairs={{0,8},{1,9},{2,10},{3,11},{4,12},{5,13},{6,14},{7,15},{8,0},{9,1},... | collective-permute-start | bytes 294920 | tf_op jit(solution)/shard_map/ppermute | solution.py:328
  12.0 0.2 pair_sums.1
  12.2 1.6 %collective-permute-start.1 = (s16[2,136,128]{2,1,0:T(8,128)(2,1)S(1)}, s16[2,136,128]{2,1,0:T(8,128)(2,1)S(1)}, u32[]{:S(2)}, u32[]{:S(2)}) collective-permute-start(s16[2,136,128]{2,1,0:T(8,128)(2,1)S(1)} %get-tuple-element.25), channel_id=1, source_target_pairs={{0,4},{1,5},{2,6},{3,7},{4,0},{5,1},{6,2},{7,3},{8,12},{9,13},{10,... | collective-permute-start | bytes 208904 | tf_op jit(solution)/shard_map/ppermute | solution.py:328
  13.8 1.5 %collective-permute-start.2 = (s16[2,136,128]{2,1,0:T(8,128)(2,1)S(1)}, s16[2,136,128]{2,1,0:T(8,128)(2,1)S(1)}, u32[]{:S(2)}, u32[]{:S(2)}) collective-permute-start(s16[2,136,128]{2,1,0:T(8,128)(2,1)S(1)} %get-tuple-element.26), channel_id=1, source_target_pairs={{0,2},{1,3},{2,0},{3,1},{4,6},{5,7},{6,4},{7,5},{8,10},{9,11},{10,... | collective-permute-start | bytes 208904 | tf_op jit(solution)/shard_map/ppermute | solution.py:328
  15.4 0.4 collective-permute-start.3
  15.8 0.3 select_tails.1.rest_ref
  16.1 0.3 select_rows.1.one_ref
  16.4 0.9 %collective-permute-done.1.refs_1_ = s16[2,136,128]{2,1,0:T(8,128)(2,1)S(1)} collective-permute-done((s16[2,136,128]{2,1,0:T(8,128)(2,1)S(1)}, s16[2,136,128]{2,1,0:T(8,128)(2,1)S(1)}, u32[]{:S(2)}, u32[]{:S(2)}) %collective-permute-start.1) | collective-permute-done | bytes 69664 | tf_op jit(solution)/shard_map/ppermute | solution.py:328
  17.4 0.8 %collective-permute-done.2.refs_2_ = s16[2,136,128]{2,1,0:T(8,128)(2,1)S(1)} collective-permute-done((s16[2,136,128]{2,1,0:T(8,128)(2,1)S(1)}, s16[2,136,128]{2,1,0:T(8,128)(2,1)S(1)}, u32[]{:S(2)}, u32[]{:S(2)}) %collective-permute-start.2) | collective-permute-done | bytes 69664 | tf_op jit(solution)/shard_map/ppermute | solution.py:328
  18.2 2.4 %collective-permute-done.3.refs_3_ = s16[2,136,128]{2,1,0:T(8,128)(2,1)S(1)} collective-permute-done((s16[2,136,128]{2,1,0:T(8,128)(2,1)S(1)}, s16[2,136,128]{2,1,0:T(8,128)(2,1)S(1)}, u32[]{:S(2)}, u32[]{:S(2)}) %collective-permute-start.3) | collective-permute-done | bytes 69664 | tf_op jit(solution)/shard_map/ppermute | solution.py:328
  20.6 0.3 add_sums.2.refs_0_
  20.9 0.4 collective-permute-start.5
  21.3 5.5 %collective-permute-done.5.refs_1_ = s16[2,136,128]{2,1,0:T(8,128)(2,1)S(1)} collective-permute-done((s16[2,136,128]{2,1,0:T(8,128)(2,1)S(1)}, s16[2,136,128]{2,1,0:T(8,128)(2,1)S(1)}, u32[]{:S(2)}, u32[]{:S(2)}) %collective-permute-start.5) | collective-permute-done | bytes 69664 | tf_op jit(solution)/shard_map/ppermute | solution.py:328
  26.8 0.1 collective-permute-start.6
  26.9 2.0 %collective-permute-start.8 = (bf16[32,3072]{1,0:T(8,128)(2,1)S(1)}, bf16[32,3072]{1,0:T(8,128)(2,1)S(1)}, u32[]{:S(2)}, u32[]{:S(2)}) collective-permute-start(bf16[32,3072]{1,0:T(8,128)(2,1)S(1)} %constant_dynamic-update-slice_fusion.refs_0_), channel_id=1, source_target_pairs={{0,6},{1,7},{2,4},{3,5},{4,2},{5,3},{6,0},{7,1},{8,14},{9,15},{10,... | collective-permute-start | bytes 589832 | tf_op jit(solution)/shard_map/ppermute | solution.py:328
  28.8 1.5 %collective-permute-start.7 = (bf16[32,3072]{1,0:T(8,128)(2,1)S(1)}, bf16[32,3072]{1,0:T(8,128)(2,1)S(1)}, u32[]{:S(2)}, u32[]{:S(2)}) collective-permute-start(bf16[32,3072]{1,0:T(8,128)(2,1)S(1)} %constant_dynamic-update-slice_fusion.refs_0_), channel_id=1, source_target_pairs={{0,2},{1,3},{2,0},{3,1},{4,6},{5,7},{6,4},{7,5},{8,10},{9,11},{10,... | collective-permute-start | bytes 589832 | tf_op jit(solution)/shard_map/ppermute | solution.py:328
  30.4 0.3 add_sums.3
  30.6 0.6 %collective-permute-start.11 = (s16[2,136,128]{2,1,0:T(8,128)(2,1)S(1)}, s16[2,136,128]{2,1,0:T(8,128)(2,1)S(1)}, u32[]{:S(2)}, u32[]{:S(2)}) collective-permute-start(s16[2,136,128]{2,1,0:T(8,128)(2,1)S(1)} %add_sums.3), channel_id=1, source_target_pairs={{0,2},{1,3},{2,0},{3,1},{4,6},{5,7},{6,4},{7,5},{8,10},{9,11},{10,... | collective-permute-start | bytes 208904 | tf_op jit(solution)/shard_map/ppermute | solution.py:328
  31.2 0.1 collective-permute-start.10
  31.3 3.4 %collective-permute-done.6.refs_1_ = bf16[32,3072]{1,0:T(8,128)(2,1)S(1)} collective-permute-done((bf16[32,3072]{1,0:T(8,128)(2,1)S(1)}, bf16[32,3072]{1,0:T(8,128)(2,1)S(1)}, u32[]{:S(2)}, u32[]{:S(2)}) %collective-permute-start.6) | collective-permute-done | bytes 196640 | tf_op jit(solution)/shard_map/ppermute | solution.py:328
  34.7 2.2 %collective-permute-done.8.refs_3_ = bf16[32,3072]{1,0:T(8,128)(2,1)S(1)} collective-permute-done((bf16[32,3072]{1,0:T(8,128)(2,1)S(1)}, bf16[32,3072]{1,0:T(8,128)(2,1)S(1)}, u32[]{:S(2)}, u32[]{:S(2)}) %collective-permute-start.8) | collective-permute-done | bytes 196640 | tf_op jit(solution)/shard_map/ppermute | solution.py:328
  36.8 1.3 %collective-permute-done.7.refs_2_ = bf16[32,3072]{1,0:T(8,128)(2,1)S(1)} collective-permute-done((bf16[32,3072]{1,0:T(8,128)(2,1)S(1)}, bf16[32,3072]{1,0:T(8,128)(2,1)S(1)}, u32[]{:S(2)}, u32[]{:S(2)}) %collective-permute-start.7) | collective-permute-done | bytes 196640 | tf_op jit(solution)/shard_map/ppermute | solution.py:328
  38.1 0.4 picked_rows.1.x_ref.x_own
  38.6 0.1 collective-permute-start.9
  38.6 0.2 collective-permute-done.11
  38.9 1.0 %collective-permute-done.12 = s16[2,136,128]{2,1,0:T(8,128)(2,1)S(1)} collective-permute-done((s16[2,136,128]{2,1,0:T(8,128)(2,1)S(1)}, s16[2,136,128]{2,1,0:T(8,128)(2,1)S(1)}, u32[]{:S(2)}, u32[]{:S(2)}) %collective-permute-start.12) | collective-permute-done | bytes 69664 | tf_op jit(solution)/shard_map/ppermute | solution.py:328
  39.9 0.1 collective-permute-start.13
  40.0 2.1 %own_half_products.1 = (f32[96,640]{1,0:T(8,128)S(1)}, f32[128,96]{1,0:T(8,128)S(1)}, f32[32,4096]{1,0:T(8,128)S(1)}) custom-call(bf16[640,8192]{1,0:T(8,128)(2,1)S(1)} %get-tuple-element.20.feat_ref, s16[8,136,128]{2,1,0:T(8,128)(2,1)S(1)} %constant_dynamic-update-slice_fusion.2.code_ref, bf16[96,4096]{1,0:T(8,128)(2,1)S(1)} %picked_rows.1.x_ref.x_own), custom_call_target="tpu_custom_call" | custom-call | tf_op jit(solution)/shard_map/own_half_products/pallas_call | solution.py:413
  42.1 3.2 %pursuit.1 = (f32[3,640]{1,0:T(4,128)}, f32[32,8192]{1,0:T(8,128)}) custom-call(s32[640]{0:T(1024)S(1)} %copy-done.1, bf16[640,8192]{1,0:T(8,128)(2,1)S(1)} %get-tuple-element.20.feat_ref, bf16[96,4096]{1,0:T(8,128)(2,1)S(1)} %picked_rows.1.x_ref.x_own, bf16[96,4096]{1,0:T(8,128)(2,1)S(1)} %collective-permute-done.9.x_twin, ...), custom_call_target="tpu_custom_call" | custom-call | tf_op jit(solution)/shard_map/pursuit/pallas_call | solution.py:427
  (16 shorter events, 0.1 us)
Async XLA Ops:
  0.6 15.1 %copy-start = (s32[3,32]{1,0:T(4,128)S(1)}, s32[3,32]{1,0:T(4,128)}, u32[]{:S(2)}) copy-start(s32[3,32]{1,0:T(4,128)} %pick_ref.1) | copy-start | bytes 1156
  5.7 36.4 %copy-start.1 = (s32[640]{0:T(1024)S(1)}, s32[640]{0:T(1024)}, u32[]{:S(2)}) copy-start(s32[640]{0:T(1024)} %labels_ref.1) | copy-start | bytes 7684
  5.7 2.3 %collective-permute-start = (f32[328,512]{1,0:T(8,128)S(1)}, f32[328,512]{1,0:T(8,128)S(1)}, u32[]{:S(2)}, u32[]{:S(2)}) collective-permute-start(f32[328,512]{1,0:T(8,128)S(1)} %get-tuple-element.22), channel_id=1, source_target_pairs={{0,1},{1,0},{2,3},{3,2},{4,5},{5,4},{6,7},{7,6},{8,9},{9,8},{10,11... | collective-permute-start | bytes 2015240 | tf_op jit(solution)/shard_map/ppermute | solution.py:328
  8.0 12.9 %collective-permute-start.4 = (bf16[16,3072]{1,0:T(8,128)(2,1)S(1)}, bf16[16,3072]{1,0:T(8,128)(2,1)S(1)}, u32[]{:S(2)}, u32[]{:S(2)}) collective-permute-start(bf16[16,3072]{1,0:T(8,128)(2,1)S(1)} %pack_rows.1), channel_id=1, source_target_pairs={{0,8},{1,9},{2,10},{3,11},{4,12},{5,13},{6,14},{7,15},{8,0},{9,1},... | collective-permute-start | bytes 294920 | tf_op jit(solution)/shard_map/ppermute | solution.py:328
  12.2 5.2 %collective-permute-start.1 = (s16[2,136,128]{2,1,0:T(8,128)(2,1)S(1)}, s16[2,136,128]{2,1,0:T(8,128)(2,1)S(1)}, u32[]{:S(2)}, u32[]{:S(2)}) collective-permute-start(s16[2,136,128]{2,1,0:T(8,128)(2,1)S(1)} %get-tuple-element.25), channel_id=1, source_target_pairs={{0,4},{1,5},{2,6},{3,7},{4,0},{5,1},{6,2},{7,3},{8,12},{9,13},{10,... | collective-permute-start | bytes 208904 | tf_op jit(solution)/shard_map/ppermute | solution.py:328
  13.8 4.3 %collective-permute-start.2 = (s16[2,136,128]{2,1,0:T(8,128)(2,1)S(1)}, s16[2,136,128]{2,1,0:T(8,128)(2,1)S(1)}, u32[]{:S(2)}, u32[]{:S(2)}) collective-permute-start(s16[2,136,128]{2,1,0:T(8,128)(2,1)S(1)} %get-tuple-element.26), channel_id=1, source_target_pairs={{0,2},{1,3},{2,0},{3,1},{4,6},{5,7},{6,4},{7,5},{8,10},{9,11},{10,... | collective-permute-start | bytes 208904 | tf_op jit(solution)/shard_map/ppermute | solution.py:328
  15.4 5.2 %collective-permute-start.3 = (s16[2,136,128]{2,1,0:T(8,128)(2,1)S(1)}, s16[2,136,128]{2,1,0:T(8,128)(2,1)S(1)}, u32[]{:S(2)}, u32[]{:S(2)}) collective-permute-start(s16[2,136,128]{2,1,0:T(8,128)(2,1)S(1)} %get-tuple-element.27), channel_id=1, source_target_pairs={{0,6},{1,7},{2,4},{3,5},{4,2},{5,3},{6,0},{7,1},{8,14},{9,15},{10,... | collective-permute-start | bytes 208904 | tf_op jit(solution)/shard_map/ppermute | solution.py:328
  20.9 5.9 %collective-permute-start.5 = (s16[2,136,128]{2,1,0:T(8,128)(2,1)S(1)}, s16[2,136,128]{2,1,0:T(8,128)(2,1)S(1)}, u32[]{:S(2)}, u32[]{:S(2)}) collective-permute-start(s16[2,136,128]{2,1,0:T(8,128)(2,1)S(1)} %add_sums.2.refs_0_), channel_id=1, source_target_pairs={{0,8},{1,9},{2,10},{3,11},{4,12},{5,13},{6,14},{7,15},{8,0},{9,1},... | collective-permute-start | bytes 208904 | tf_op jit(solution)/shard_map/ppermute | solution.py:328
  26.8 7.8 %collective-permute-start.6 = (bf16[32,3072]{1,0:T(8,128)(2,1)S(1)}, bf16[32,3072]{1,0:T(8,128)(2,1)S(1)}, u32[]{:S(2)}, u32[]{:S(2)}) collective-permute-start(bf16[32,3072]{1,0:T(8,128)(2,1)S(1)} %constant_dynamic-update-slice_fusion.refs_0_), channel_id=1, source_target_pairs={{0,4},{1,5},{2,6},{3,7},{4,0},{5,1},{6,2},{7,3},{8,12},{9,13},{10,... | collective-permute-start | bytes 589832 | tf_op jit(solution)/shard_map/ppermute | solution.py:328
  26.9 9.9 %collective-permute-start.8 = (bf16[32,3072]{1,0:T(8,128)(2,1)S(1)}, bf16[32,3072]{1,0:T(8,128)(2,1)S(1)}, u32[]{:S(2)}, u32[]{:S(2)}) collective-permute-start(bf16[32,3072]{1,0:T(8,128)(2,1)S(1)} %constant_dynamic-update-slice_fusion.refs_0_), channel_id=1, source_target_pairs={{0,6},{1,7},{2,4},{3,5},{4,2},{5,3},{6,0},{7,1},{8,14},{9,15},{10,... | collective-permute-start | bytes 589832 | tf_op jit(solution)/shard_map/ppermute | solution.py:328
  28.8 9.3 %collective-permute-start.7 = (bf16[32,3072]{1,0:T(8,128)(2,1)S(1)}, bf16[32,3072]{1,0:T(8,128)(2,1)S(1)}, u32[]{:S(2)}, u32[]{:S(2)}) collective-permute-start(bf16[32,3072]{1,0:T(8,128)(2,1)S(1)} %constant_dynamic-update-slice_fusion.refs_0_), channel_id=1, source_target_pairs={{0,2},{1,3},{2,0},{3,1},{4,6},{5,7},{6,4},{7,5},{8,10},{9,11},{10,... | collective-permute-start | bytes 589832 | tf_op jit(solution)/shard_map/ppermute | solution.py:328
  30.6 8.2 %collective-permute-start.11 = (s16[2,136,128]{2,1,0:T(8,128)(2,1)S(1)}, s16[2,136,128]{2,1,0:T(8,128)(2,1)S(1)}, u32[]{:S(2)}, u32[]{:S(2)}) collective-permute-start(s16[2,136,128]{2,1,0:T(8,128)(2,1)S(1)} %add_sums.3), channel_id=1, source_target_pairs={{0,2},{1,3},{2,0},{3,1},{4,6},{5,7},{6,4},{7,5},{8,10},{9,11},{10,... | collective-permute-start | bytes 208904 | tf_op jit(solution)/shard_map/ppermute | solution.py:328
  31.2 7.7 %collective-permute-start.10 = (s16[2,136,128]{2,1,0:T(8,128)(2,1)S(1)}, s16[2,136,128]{2,1,0:T(8,128)(2,1)S(1)}, u32[]{:S(2)}, u32[]{:S(2)}) collective-permute-start(s16[2,136,128]{2,1,0:T(8,128)(2,1)S(1)} %add_sums.3), channel_id=1, source_target_pairs={{0,4},{1,5},{2,6},{3,7},{4,0},{5,1},{6,2},{7,3},{8,12},{9,13},{10,... | collective-permute-start | bytes 208904 | tf_op jit(solution)/shard_map/ppermute | solution.py:328
  34.6 5.2 %collective-permute-start.12 = (s16[2,136,128]{2,1,0:T(8,128)(2,1)S(1)}, s16[2,136,128]{2,1,0:T(8,128)(2,1)S(1)}, u32[]{:S(2)}, u32[]{:S(2)}) collective-permute-start(s16[2,136,128]{2,1,0:T(8,128)(2,1)S(1)} %add_sums.3), channel_id=1, source_target_pairs={{0,6},{1,7},{2,4},{3,5},{4,2},{5,3},{6,0},{7,1},{8,14},{9,15},{10,... | collective-permute-start | bytes 208904 | tf_op jit(solution)/shard_map/ppermute | solution.py:328
  38.6 3.5 %collective-permute-start.9 = (bf16[96,4096]{1,0:T(8,128)(2,1)S(1)}, bf16[96,4096]{1,0:T(8,128)(2,1)S(1)}, u32[]{:S(2)}, u32[]{:S(2)}) collective-permute-start(bf16[96,4096]{1,0:T(8,128)(2,1)S(1)} %picked_rows.1.x_ref.x_own), channel_id=1, source_target_pairs={{0,1},{1,0},{2,3},{3,2},{4,5},{5,4},{6,7},{7,6},{8,9},{9,8},{10,11... | collective-permute-start | bytes 2359304 | tf_op jit(solution)/shard_map/ppermute | solution.py:328
  39.9 2.1 %collective-permute-start.13 = (s16[8,136,128]{2,1,0:T(8,128)(2,1)S(1)}, s16[8,136,128]{2,1,0:T(8,128)(2,1)S(1)}, u32[]{:S(2)}, u32[]{:S(2)}) collective-permute-start(s16[8,136,128]{2,1,0:T(8,128)(2,1)S(1)} %constant_dynamic-update-slice_fusion.2.code_ref), channel_id=1, source_target_pairs={{0,1},{1,0},{2,3},{3,2},{4,5},{5,4},{6,7},{7,6},{8,9},{9,8},{10,11... | collective-permute-start | bytes 835592 | tf_op jit(solution)/shard_map/ppermute | solution.py:328

commit v12 on v11

--- a/solution.py
+++ b/solution.py
@@ -52,7 +52,7 @@
 
 
 def sums_kernel(
-    labels_hbm, pick_hbm, feat_hbm, feat_ref, send_ref, keep_ref, labels_ref, pick_ref, left, sems, *, n_ex
+    labels_hbm, pick_hbm, feat_hbm, feat_ref, send_ref, keep_ref, held, labels_ref, pick_ref, left, sems, *, n_ex
 ):
     rows, full = feat_ref.shape
     steps, classes = pick_ref.shape
@@ -109,21 +109,20 @@
         k = i % groups
         ref = send_ref if i < groups else keep_ref
         ref[k * classes : (k + 1) * classes, :] = both[:classes]
-        ref[base + 8 + 8 * k : base + 16 + 8 * k, :] = both[classes : classes + 8]
-
-
-def pack_kernel(keep_ref, got_ref, rows_ref, *, steps, start):
-    lines, main = rows_ref.shape
+        held[:, columns[i]] = both[classes : classes + 8]
+
+
+def pack_kernel(held, rows_ref, *, steps):
+    half = held.shape[1] // 2
     used = steps * slots
-    count = (keep_ref.shape[0] - start) // 8
-    halves = []
-    for ref in (keep_ref, got_ref):
-        halves.append(jnp.concatenate([ref[start + 8 * k : start + 8 * k + 8, :] for k in range(count)], axis=1))
-    out = [h[:used, :main] for h in halves]
-    for h in halves:
+    main = rows_ref.shape[2]
+    core = lax.axis_index("ex") % 2
+    for part, side in ((0, core), (1, 1 - core)):
+        h = held[:, pl.ds(pl.multiple_of(side * half, half), half)]
+        lines = [h[:used, :main]]
         for q in range(slots):
-            out.append(jnp.concatenate([h[q * steps + u : q * steps + u + 1, main:] for u in range(steps)], axis=1))
-    rows_ref[...] = jnp.concatenate(out, axis=0).astype(bf16)
+            lines.append(jnp.concatenate([h[q * steps + u : q * steps + u + 1, main:] for u in range(steps)], axis=1))
+        rows_ref[part] = jnp.concatenate(lines, axis=0).astype(bf16)
 
 
 def near_id(mask):
@@ -212,18 +211,15 @@
         owner = jnp.where(here, d, owner)
         rank = jnp.where(here & (lane > first), 1, rank)
     away = owner ^ device
-    spot = jnp.zeros_like(pick)
     bits = n_ex.bit_length() - 1
-    for b in range(1, bits):
-        spot = spot + (((away >> b) & 1) << (bits - 1 - b))
-    other = away & 1
-    used = steps * slots
+    far = jnp.zeros_like(pick)
+    for b in range(3, bits):
+        far = far + (((away >> b) & 1) << (bits - 1 - b))
+    near = ((away >> 2) & 1) + 2 * ((away >> 1) & 1)
+    spot = (2 * near + (away & 1)) * (n_ex // 8) + far
     step = lax.broadcasted_iota(jnp.int32, pick.shape, 0)
     line = lax.broadcasted_iota(jnp.int32, (lines, classes), 0)
-    if tail:
-        where = spot * 16 + 2 * used + other * slots + rank
-    else:
-        where = spot * 16 + other * used + rank * steps + step
+    where = spot * 8 + (slots * steps + rank if tail else rank * steps + step)
     hits = [jnp.where(line == where[s : s + 1, :], 1.0, 0.0) for s in range(steps)]
     pad = jnp.zeros((lines, 128 - steps * classes), f32)
     one_ref[...] = jnp.transpose(jnp.concatenate(hits + [pad], axis=1))[: steps * classes].astype(bf16)
@@ -321,7 +317,7 @@
     vmem = pl.BlockSpec(memory_space=pltpu.VMEM)
     hbm = pl.BlockSpec(memory_space=pltpu.HBM)
     anywhere = pl.BlockSpec(memory_space=pl.ANY)
-    half = jax.ShapeDtypeStruct((groups * (classes + 8) + 8, width), f32)
+    half = jax.ShapeDtypeStruct((groups * classes + 8, width), f32)
     code = jax.ShapeDtypeStruct((groups // 4, classes * (width // 128) + 8, 128), jnp.int16)
 
     def swap(x, mask):
@@ -330,11 +326,11 @@
     def after(x, *others):
         return lax.optimization_barrier((x,) + others)[0]
 
-    feat, send, keep = pl.pallas_call(
+    feat, send, keep, held = pl.pallas_call(
         functools.partial(sums_kernel, n_ex=n_ex),
         in_specs=[hbm] * 3,
-        out_specs=[vmem] * 3,
-        out_shape=[pltpu.VMEM((rows, full), bf16), half, half],
+        out_specs=[vmem] * 4,
+        out_shape=[pltpu.VMEM((rows, full), bf16), half, half, jax.ShapeDtypeStruct((8, full), f32)],
         scratch_shapes=[
             pltpu.VMEM(labels.shape, jnp.int32),
             pltpu.VMEM(pick_index.shape, jnp.int32),
@@ -365,16 +361,20 @@
         compiler_params=limit,
         name="pair_sums",
     )(keep, got)
-    near = pl.pallas_call(
-        functools.partial(pack_kernel, steps=steps, start=groups * classes + 8),
-        in_specs=[vmem] * 2,
+    packed = pl.pallas_call(
+        functools.partial(pack_kernel, steps=steps),
+        in_specs=[vmem],
         out_specs=vmem,
-        out_shape=jax.ShapeDtypeStruct((16, main), bf16),
+        out_shape=jax.ShapeDtypeStruct((2, 8, main), bf16),
         compiler_params=limit,
         name="pack_rows",
-    )(keep, got)
+    )(held)
+    for mask in reversed(far_masks):
+        packed = jnp.concatenate([packed, swap(packed, mask)], axis=1)
+
     near_codes = [swap(c, m) for c, m in zip(codes[1:], near_masks[1:])]
-    part_sum = add([codes[0]] + near_codes, False)
+    part_sum = add([codes[0], after(near_codes[0], packed)] + near_codes[1:], False)
+
     def select(tail, *others):
         return pl.pallas_call(
             functools.partial(select_kernel, n_ex=n_ex, rows=rows, tail=tail),
@@ -387,11 +387,12 @@
 
     one = select(False, codes[0])
     rest = select(True, codes[0])
-    for far, mask in zip(reversed(far_masks), far_masks):
-        far_rows = swap(near, far)
-        more = swap(after(part_sum, far_rows, one, rest), mask)
-        near = jnp.concatenate([after(near, more), far_rows], axis=0)
+    given = swap(after(packed[1], part_sum), 1)
+    part_sum = after(part_sum, one, rest)
+    for mask in far_masks:
+        more = swap(part_sum, mask)
         part_sum = add([part_sum, more], mask == far_masks[-1])
+    near = jnp.concatenate([after(packed[0], more), given], axis=0)
     parts = [near] + [swap(near, m) for m in near_masks[1:]]
     own_parts = [part_sum] + [swap(part_sum, m) for m in near_masks[1:3]]
     own_parts.append(swap(after(part_sum, parts[1]), near_masks[3]))

time: 45.5 us -> 43.6 us (0.958)
  waiting for transfers between devices: 19.4 us -> 16.2 us
  starting transfers between devices: 12.8 us -> 14.3 us
    ppermute x14 -> x15, waiting for transfers between devices: 19.4 us -> 16.2 us  [swap(): return lax.ppermute(x, 'ex', [(d, d ^ mask) for d in range(n_ex)])]
    ppermute x14 -> x15, starting transfers between devices: 12.8 us -> 14.3 us  [swap(): return lax.ppermute(x, 'ex', [(d, d ^ mask) for d in range(n_ex)])]
  transfers between devices with their start and end apart: 14 -> 15, of which waited for: 10 -> 9; matrix products, arithmetic and copies ran while one was open for 0% -> 0% of each run, Pallas kernels for 9% -> 9%
where the time goes in v12:
time: 43.6 us; the launch traced here: 43.4 us
  waiting for transfers between devices  16.2 us (37%)
  starting transfers between devices  14.3 us (33%)
  Pallas kernels  12.1 us (28%)
  between operations  0.79 us (2%)
    ppermute x15, waiting for transfers between devices, swap(): return lax.ppermute(x, 'ex', [(d, d ^ mask) for d in range(n_ex)])  16.2 us
    ppermute x15, starting transfers between devices, swap(): return lax.ppermute(x, 'ex', [(d, d ^ mask) for d in range(n_ex)])  14.3 us
    pallas_call x1, Pallas kernels, on_device(): pl.pallas_call(functools.partial(sums_kernel, n_ex=n_ex), in_specs=[hbm]...  5.02 us
    pallas_call x1, Pallas kernels, on_device(): pl.pallas_call(functools.partial(pursuit_kernel, steps=steps, scale=1.0 /...  3.19 us
    pallas_call x1, Pallas kernels, on_device(): pl.pallas_call(functools.partial(half_kernel, classes=classes), in_specs=...  2.06 us
  transfers between devices with their start and end apart: 15, of which 9 were waited for; matrix products, arithmetic and copies ran while one was open for 0% of the time, Pallas kernels for 9%

profile of v12, /device:TPU:0, one launch (start us, length us, event | category | flops | bytes accessed | tf_op | source)
XLA Modules:
  0.0 43.4 jit_solution(10010612938895056040)
XLA Ops:
  0.6 5.0 %class_sums.1 = (bf16[640,8192]{1,0:T(8,128)(2,1)S(1)}, f32[264,512]{1,0:T(8,128)S(1)}, f32[264,512]{1,0:T(8,128)S(1)}, f32[8,8192]{1,0:T(8,128)S(1)}) custom-call(s32[640]{0:T(1024)} %labels_ref.1, s32[3,32]{1,0:T(4,128)} %pick_ref.1, bf16[640,8192]{1,0:T(8,128)(2,1)} %feat_hbm.1), custom_call_target="tpu_custom_call" | custom-call | tf_op jit(solution)/shard_map/class_sums/pallas_call | solution.py:329
  5.7 0.5 %collective-permute-start = (f32[264,512]{1,0:T(8,128)S(1)}, f32[264,512]{1,0:T(8,128)S(1)}, u32[]{:S(2)}, u32[]{:S(2)}) collective-permute-start(f32[264,512]{1,0:T(8,128)S(1)} %get-tuple-element.25), channel_id=1, source_target_pairs={{0,1},{1,0},{2,3},{3,2},{4,5},{5,4},{6,7},{7,6},{8,9},{9,8},{10,11... | collective-permute-start | bytes 1622024 | tf_op jit(solution)/shard_map/ppermute | solution.py:324
  6.2 3.7 %collective-permute-start.1 = (bf16[2,8,3072]{2,1,0:T(8,128)(2,1)S(1)}, bf16[2,8,3072]{2,1,0:T(8,128)(2,1)S(1)}, u32[]{:S(2)}, u32[]{:S(2)}) collective-permute-start(bf16[2,8,3072]{2,1,0:T(8,128)(2,1)S(1)} %pack_rows.1), channel_id=1, source_target_pairs={{0,8},{1,9},{2,10},{3,11},{4,12},{5,13},{6,14},{7,15},{8,0},{9,1},... | collective-permute-start | bytes 294920 | tf_op jit(solution)/shard_map/ppermute | solution.py:324
  9.9 0.2 pair_sums.1
  10.1 1.6 %collective-permute-start.2 = (s16[2,136,128]{2,1,0:T(8,128)(2,1)S(1)}, s16[2,136,128]{2,1,0:T(8,128)(2,1)S(1)}, u32[]{:S(2)}, u32[]{:S(2)}) collective-permute-start(s16[2,136,128]{2,1,0:T(8,128)(2,1)S(1)} %get-tuple-element.29), channel_id=1, source_target_pairs={{0,4},{1,5},{2,6},{3,7},{4,0},{5,1},{6,2},{7,3},{8,12},{9,13},{10,... | collective-permute-start | bytes 208904 | tf_op jit(solution)/shard_map/ppermute | solution.py:324
  11.8 1.5 %collective-permute-start.3 = (s16[2,136,128]{2,1,0:T(8,128)(2,1)S(1)}, s16[2,136,128]{2,1,0:T(8,128)(2,1)S(1)}, u32[]{:S(2)}, u32[]{:S(2)}) collective-permute-start(s16[2,136,128]{2,1,0:T(8,128)(2,1)S(1)} %get-tuple-element.31), channel_id=1, source_target_pairs={{0,2},{1,3},{2,0},{3,1},{4,6},{5,7},{6,4},{7,5},{8,10},{9,11},{10,... | collective-permute-start | bytes 208904 | tf_op jit(solution)/shard_map/ppermute | solution.py:324
  13.3 0.4 collective-permute-start.4
  13.7 0.3 select_tails.1.rest_ref
  14.0 0.3 select_rows.1.one_ref
  14.4 0.3 collective-permute-done.2.refs_1_
  14.7 1.4 %collective-permute-done.3.refs_2_ = s16[2,136,128]{2,1,0:T(8,128)(2,1)S(1)} collective-permute-done((s16[2,136,128]{2,1,0:T(8,128)(2,1)S(1)}, s16[2,136,128]{2,1,0:T(8,128)(2,1)S(1)}, u32[]{:S(2)}, u32[]{:S(2)}) %collective-permute-start.3) | collective-permute-done | bytes 69664 | tf_op jit(solution)/shard_map/ppermute | solution.py:324
  16.1 2.4 %collective-permute-done.4.refs_3_ = s16[2,136,128]{2,1,0:T(8,128)(2,1)S(1)} collective-permute-done((s16[2,136,128]{2,1,0:T(8,128)(2,1)S(1)}, s16[2,136,128]{2,1,0:T(8,128)(2,1)S(1)}, u32[]{:S(2)}, u32[]{:S(2)}) %collective-permute-start.4) | collective-permute-done | bytes 69664 | tf_op jit(solution)/shard_map/ppermute | solution.py:324
  18.5 0.3 add_sums.2.refs_0_
  18.8 1.9 %collective-permute-start.5 = (s16[2,136,128]{2,1,0:T(8,128)(2,1)S(1)}, s16[2,136,128]{2,1,0:T(8,128)(2,1)S(1)}, u32[]{:S(2)}, u32[]{:S(2)}) collective-permute-start(s16[2,136,128]{2,1,0:T(8,128)(2,1)S(1)} %add_sums.2.refs_0_), channel_id=1, source_target_pairs={{0,8},{1,9},{2,10},{3,11},{4,12},{5,13},{6,14},{7,15},{8,0},{9,1},... | collective-permute-start | bytes 208904 | tf_op jit(solution)/shard_map/ppermute | solution.py:324
  20.6 0.1 collective-permute-start.6
  20.7 4.1 %collective-permute-done.5.refs_1_ = s16[2,136,128]{2,1,0:T(8,128)(2,1)S(1)} collective-permute-done((s16[2,136,128]{2,1,0:T(8,128)(2,1)S(1)}, s16[2,136,128]{2,1,0:T(8,128)(2,1)S(1)}, u32[]{:S(2)}, u32[]{:S(2)}) %collective-permute-start.5) | collective-permute-done | bytes 69664 | tf_op jit(solution)/shard_map/ppermute | solution.py:324
  24.9 0.1 collective-permute-start.7
  25.1 1.9 %collective-permute-start.9 = (bf16[32,3072]{1,0:T(8,128)(2,1)S(1)}, bf16[32,3072]{1,0:T(8,128)(2,1)S(1)}, u32[]{:S(2)}, u32[]{:S(2)}) collective-permute-start(bf16[32,3072]{1,0:T(8,128)(2,1)S(1)} %constant_dynamic-update-slice_fusion.refs_0_), channel_id=1, source_target_pairs={{0,6},{1,7},{2,4},{3,5},{4,2},{5,3},{6,0},{7,1},{8,14},{9,15},{10,... | collective-permute-start | bytes 589832 | tf_op jit(solution)/shard_map/ppermute | solution.py:324
  26.9 1.5 %collective-permute-start.8 = (bf16[32,3072]{1,0:T(8,128)(2,1)S(1)}, bf16[32,3072]{1,0:T(8,128)(2,1)S(1)}, u32[]{:S(2)}, u32[]{:S(2)}) collective-permute-start(bf16[32,3072]{1,0:T(8,128)(2,1)S(1)} %constant_dynamic-update-slice_fusion.refs_0_), channel_id=1, source_target_pairs={{0,2},{1,3},{2,0},{3,1},{4,6},{5,7},{6,4},{7,5},{8,10},{9,11},{10,... | collective-permute-start | bytes 589832 | tf_op jit(solution)/shard_map/ppermute | solution.py:324
  28.5 0.3 add_sums.3
  28.7 0.6 %collective-permute-start.12 = (s16[2,136,128]{2,1,0:T(8,128)(2,1)S(1)}, s16[2,136,128]{2,1,0:T(8,128)(2,1)S(1)}, u32[]{:S(2)}, u32[]{:S(2)}) collective-permute-start(s16[2,136,128]{2,1,0:T(8,128)(2,1)S(1)} %add_sums.3), channel_id=1, source_target_pairs={{0,2},{1,3},{2,0},{3,1},{4,6},{5,7},{6,4},{7,5},{8,10},{9,11},{10,... | collective-permute-start | bytes 208904 | tf_op jit(solution)/shard_map/ppermute | solution.py:324
  29.3 0.2 collective-permute-start.11
  29.5 3.3 %collective-permute-done.7.refs_1_ = bf16[32,3072]{1,0:T(8,128)(2,1)S(1)} collective-permute-done((bf16[32,3072]{1,0:T(8,128)(2,1)S(1)}, bf16[32,3072]{1,0:T(8,128)(2,1)S(1)}, u32[]{:S(2)}, u32[]{:S(2)}) %collective-permute-start.7) | collective-permute-done | bytes 196640 | tf_op jit(solution)/shard_map/ppermute | solution.py:324
  32.8 0.1 collective-permute-start.13
  32.9 2.5 %collective-permute-done.9.refs_3_ = bf16[32,3072]{1,0:T(8,128)(2,1)S(1)} collective-permute-done((bf16[32,3072]{1,0:T(8,128)(2,1)S(1)}, bf16[32,3072]{1,0:T(8,128)(2,1)S(1)}, u32[]{:S(2)}, u32[]{:S(2)}) %collective-permute-start.9) | collective-permute-done | bytes 196640 | tf_op jit(solution)/shard_map/ppermute | solution.py:324
  35.4 1.1 %collective-permute-done.8.refs_2_ = bf16[32,3072]{1,0:T(8,128)(2,1)S(1)} collective-permute-done((bf16[32,3072]{1,0:T(8,128)(2,1)S(1)}, bf16[32,3072]{1,0:T(8,128)(2,1)S(1)}, u32[]{:S(2)}, u32[]{:S(2)}) %collective-permute-start.8) | collective-permute-done | bytes 196640 | tf_op jit(solution)/shard_map/ppermute | solution.py:324
  36.5 0.4 picked_rows.1.x_ref.x_own
  36.9 0.1 collective-permute-start.10
  37.0 0.3 collective-permute-done.12
  37.2 0.8 %collective-permute-done.13 = s16[2,136,128]{2,1,0:T(8,128)(2,1)S(1)} collective-permute-done((s16[2,136,128]{2,1,0:T(8,128)(2,1)S(1)}, s16[2,136,128]{2,1,0:T(8,128)(2,1)S(1)}, u32[]{:S(2)}, u32[]{:S(2)}) %collective-permute-start.13) | collective-permute-done | bytes 69664 | tf_op jit(solution)/shard_map/ppermute | solution.py:324
  38.2 2.1 %own_half_products.1 = (f32[96,640]{1,0:T(8,128)S(1)}, f32[128,96]{1,0:T(8,128)S(1)}, f32[32,4096]{1,0:T(8,128)S(1)}) custom-call(bf16[640,8192]{1,0:T(8,128)(2,1)S(1)} %get-tuple-element.23.feat_ref, s16[8,136,128]{2,1,0:T(8,128)(2,1)S(1)} %constant_dynamic-update-slice_fusion.2.code_ref, bf16[96,4096]{1,0:T(8,128)(2,1)S(1)} %picked_rows.1.x_ref.x_own), custom_call_target="tpu_custom_call" | custom-call | tf_op jit(solution)/shard_map/own_half_products/pallas_call | solution.py:414
  40.3 3.2 %pursuit.1 = (f32[3,640]{1,0:T(4,128)}, f32[32,8192]{1,0:T(8,128)}) custom-call(s32[640]{0:T(1024)S(1)} %copy-done.1, bf16[640,8192]{1,0:T(8,128)(2,1)S(1)} %get-tuple-element.23.feat_ref, bf16[96,4096]{1,0:T(8,128)(2,1)S(1)} %picked_rows.1.x_ref.x_own, bf16[96,4096]{1,0:T(8,128)(2,1)S(1)} %collective-permute-done.10.x_twin, ...), custom_call_target="tpu_custom_call" | custom-call | tf_op jit(solution)/shard_map/pursuit/pallas_call | solution.py:428
  (19 shorter events, 0.2 us)
Async XLA Ops:
  0.6 13.0 %copy-start = (s32[3,32]{1,0:T(4,128)S(1)}, s32[3,32]{1,0:T(4,128)}, u32[]{:S(2)}) copy-start(s32[3,32]{1,0:T(4,128)} %pick_ref.1) | copy-start | bytes 1156
  5.7 34.6 %copy-start.1 = (s32[640]{0:T(1024)S(1)}, s32[640]{0:T(1024)}, u32[]{:S(2)}) copy-start(s32[640]{0:T(1024)} %labels_ref.1) | copy-start | bytes 7684
  5.7 4.2 %collective-permute-start = (f32[264,512]{1,0:T(8,128)S(1)}, f32[264,512]{1,0:T(8,128)S(1)}, u32[]{:S(2)}, u32[]{:S(2)}) collective-permute-start(f32[264,512]{1,0:T(8,128)S(1)} %get-tuple-element.25), channel_id=1, source_target_pairs={{0,1},{1,0},{2,3},{3,2},{4,5},{5,4},{6,7},{7,6},{8,9},{9,8},{10,11... | collective-permute-start | bytes 1622024 | tf_op jit(solution)/shard_map/ppermute | solution.py:324
  6.2 14.4 %collective-permute-start.1 = (bf16[2,8,3072]{2,1,0:T(8,128)(2,1)S(1)}, bf16[2,8,3072]{2,1,0:T(8,128)(2,1)S(1)}, u32[]{:S(2)}, u32[]{:S(2)}) collective-permute-start(bf16[2,8,3072]{2,1,0:T(8,128)(2,1)S(1)} %pack_rows.1), channel_id=1, source_target_pairs={{0,8},{1,9},{2,10},{3,11},{4,12},{5,13},{6,14},{7,15},{8,0},{9,1},... | collective-permute-start | bytes 294920 | tf_op jit(solution)/shard_map/ppermute | solution.py:324
  10.1 4.6 %collective-permute-start.2 = (s16[2,136,128]{2,1,0:T(8,128)(2,1)S(1)}, s16[2,136,128]{2,1,0:T(8,128)(2,1)S(1)}, u32[]{:S(2)}, u32[]{:S(2)}) collective-permute-start(s16[2,136,128]{2,1,0:T(8,128)(2,1)S(1)} %get-tuple-element.29), channel_id=1, source_target_pairs={{0,4},{1,5},{2,6},{3,7},{4,0},{5,1},{6,2},{7,3},{8,12},{9,13},{10,... | collective-permute-start | bytes 208904 | tf_op jit(solution)/shard_map/ppermute | solution.py:324
  11.8 4.3 %collective-permute-start.3 = (s16[2,136,128]{2,1,0:T(8,128)(2,1)S(1)}, s16[2,136,128]{2,1,0:T(8,128)(2,1)S(1)}, u32[]{:S(2)}, u32[]{:S(2)}) collective-permute-start(s16[2,136,128]{2,1,0:T(8,128)(2,1)S(1)} %get-tuple-element.31), channel_id=1, source_target_pairs={{0,2},{1,3},{2,0},{3,1},{4,6},{5,7},{6,4},{7,5},{8,10},{9,11},{10,... | collective-permute-start | bytes 208904 | tf_op jit(solution)/shard_map/ppermute | solution.py:324
  13.3 5.2 %collective-permute-start.4 = (s16[2,136,128]{2,1,0:T(8,128)(2,1)S(1)}, s16[2,136,128]{2,1,0:T(8,128)(2,1)S(1)}, u32[]{:S(2)}, u32[]{:S(2)}) collective-permute-start(s16[2,136,128]{2,1,0:T(8,128)(2,1)S(1)} %get-tuple-element.32), channel_id=1, source_target_pairs={{0,6},{1,7},{2,4},{3,5},{4,2},{5,3},{6,0},{7,1},{8,14},{9,15},{10,... | collective-permute-start | bytes 208904 | tf_op jit(solution)/shard_map/ppermute | solution.py:324
  18.8 6.1 %collective-permute-start.5 = (s16[2,136,128]{2,1,0:T(8,128)(2,1)S(1)}, s16[2,136,128]{2,1,0:T(8,128)(2,1)S(1)}, u32[]{:S(2)}, u32[]{:S(2)}) collective-permute-start(s16[2,136,128]{2,1,0:T(8,128)(2,1)S(1)} %add_sums.2.refs_0_), channel_id=1, source_target_pairs={{0,8},{1,9},{2,10},{3,11},{4,12},{5,13},{6,14},{7,15},{8,0},{9,1},... | collective-permute-start | bytes 208904 | tf_op jit(solution)/shard_map/ppermute | solution.py:324
  20.6 4.2 %collective-permute-start.6 = (bf16[16,3072]{1,0:T(8,128)(2,1)S(1)}, bf16[16,3072]{1,0:T(8,128)(2,1)S(1)}, u32[]{:S(2)}, u32[]{:S(2)}) collective-permute-start(bf16[16,3072]{1,0:T(8,128)(2,1)S(1)} %get-tuple-element.35), channel_id=1, source_target_pairs={{0,1},{1,0},{2,3},{3,2},{4,5},{5,4},{6,7},{7,6},{8,9},{9,8},{10,11... | collective-permute-start | bytes 294920 | tf_op jit(solution)/shard_map/ppermute | solution.py:324
  24.9 7.9 %collective-permute-start.7 = (bf16[32,3072]{1,0:T(8,128)(2,1)S(1)}, bf16[32,3072]{1,0:T(8,128)(2,1)S(1)}, u32[]{:S(2)}, u32[]{:S(2)}) collective-permute-start(bf16[32,3072]{1,0:T(8,128)(2,1)S(1)} %constant_dynamic-update-slice_fusion.refs_0_), channel_id=1, source_target_pairs={{0,4},{1,5},{2,6},{3,7},{4,0},{5,1},{6,2},{7,3},{8,12},{9,13},{10,... | collective-permute-start | bytes 589832 | tf_op jit(solution)/shard_map/ppermute | solution.py:324
  25.1 10.4 %collective-permute-start.9 = (bf16[32,3072]{1,0:T(8,128)(2,1)S(1)}, bf16[32,3072]{1,0:T(8,128)(2,1)S(1)}, u32[]{:S(2)}, u32[]{:S(2)}) collective-permute-start(bf16[32,3072]{1,0:T(8,128)(2,1)S(1)} %constant_dynamic-update-slice_fusion.refs_0_), channel_id=1, source_target_pairs={{0,6},{1,7},{2,4},{3,5},{4,2},{5,3},{6,0},{7,1},{8,14},{9,15},{10,... | collective-permute-start | bytes 589832 | tf_op jit(solution)/shard_map/ppermute | solution.py:324
  26.9 9.5 %collective-permute-start.8 = (bf16[32,3072]{1,0:T(8,128)(2,1)S(1)}, bf16[32,3072]{1,0:T(8,128)(2,1)S(1)}, u32[]{:S(2)}, u32[]{:S(2)}) collective-permute-start(bf16[32,3072]{1,0:T(8,128)(2,1)S(1)} %constant_dynamic-update-slice_fusion.refs_0_), channel_id=1, source_target_pairs={{0,2},{1,3},{2,0},{3,1},{4,6},{5,7},{6,4},{7,5},{8,10},{9,11},{10,... | collective-permute-start | bytes 589832 | tf_op jit(solution)/shard_map/ppermute | solution.py:324
  28.7 8.5 %collective-permute-start.12 = (s16[2,136,128]{2,1,0:T(8,128)(2,1)S(1)}, s16[2,136,128]{2,1,0:T(8,128)(2,1)S(1)}, u32[]{:S(2)}, u32[]{:S(2)}) collective-permute-start(s16[2,136,128]{2,1,0:T(8,128)(2,1)S(1)} %add_sums.3), channel_id=1, source_target_pairs={{0,2},{1,3},{2,0},{3,1},{4,6},{5,7},{6,4},{7,5},{8,10},{9,11},{10,... | collective-permute-start | bytes 208904 | tf_op jit(solution)/shard_map/ppermute | solution.py:324
  29.3 7.9 %collective-permute-start.11 = (s16[2,136,128]{2,1,0:T(8,128)(2,1)S(1)}, s16[2,136,128]{2,1,0:T(8,128)(2,1)S(1)}, u32[]{:S(2)}, u32[]{:S(2)}) collective-permute-start(s16[2,136,128]{2,1,0:T(8,128)(2,1)S(1)} %add_sums.3), channel_id=1, source_target_pairs={{0,4},{1,5},{2,6},{3,7},{4,0},{5,1},{6,2},{7,3},{8,12},{9,13},{10,... | collective-permute-start | bytes 208904 | tf_op jit(solution)/shard_map/ppermute | solution.py:324
  32.8 5.2 %collective-permute-start.13 = (s16[2,136,128]{2,1,0:T(8,128)(2,1)S(1)}, s16[2,136,128]{2,1,0:T(8,128)(2,1)S(1)}, u32[]{:S(2)}, u32[]{:S(2)}) collective-permute-start(s16[2,136,128]{2,1,0:T(8,128)(2,1)S(1)} %add_sums.3), channel_id=1, source_target_pairs={{0,6},{1,7},{2,4},{3,5},{4,2},{5,3},{6,0},{7,1},{8,14},{9,15},{10,... | collective-permute-start | bytes 208904 | tf_op jit(solution)/shard_map/ppermute | solution.py:324
  36.9 3.3 %collective-permute-start.10 = (bf16[96,4096]{1,0:T(8,128)(2,1)S(1)}, bf16[96,4096]{1,0:T(8,128)(2,1)S(1)}, u32[]{:S(2)}, u32[]{:S(2)}) collective-permute-start(bf16[96,4096]{1,0:T(8,128)(2,1)S(1)} %picked_rows.1.x_ref.x_own), channel_id=1, source_target_pairs={{0,1},{1,0},{2,3},{3,2},{4,5},{5,4},{6,7},{7,6},{8,9},{9,8},{10,11... | collective-permute-start | bytes 2359304 | tf_op jit(solution)/shard_map/ppermute | solution.py:324
  38.1 2.1 %collective-permute-start.14 = (s16[8,136,128]{2,1,0:T(8,128)(2,1)S(1)}, s16[8,136,128]{2,1,0:T(8,128)(2,1)S(1)}, u32[]{:S(2)}, u32[]{:S(2)}) collective-permute-start(s16[8,136,128]{2,1,0:T(8,128)(2,1)S(1)} %constant_dynamic-update-slice_fusion.2.code_ref), channel_id=1, source_target_pairs={{0,1},{1,0},{2,3},{3,2},{4,5},{5,4},{6,7},{7,6},{8,9},{9,8},{10,11... | collective-permute-start | bytes 835592 | tf_op jit(solution)/shard_map/ppermute | solution.py:324

commit v13 on v12

--- a/solution.py
+++ b/solution.py
@@ -348,6 +348,7 @@
             out_specs=vmem,
             out_shape=code,
             compiler_params=limit,
+            cost_estimate=pl.CostEstimate(flops=0, bytes_accessed=10**8, transcendentals=0) if last else None,
             name="add_sums",
         )(*codes)
 
@@ -385,14 +386,15 @@
             name="select_tails" if tail else "select_rows",
         )(after(pick_index, *others))
 
-    one = select(False, codes[0])
     rest = select(True, codes[0])
-    given = swap(after(packed[1], part_sum), 1)
-    part_sum = after(part_sum, one, rest)
-    for mask in far_masks:
-        more = swap(part_sum, mask)
-        part_sum = add([part_sum, more], mask == far_masks[-1])
-    near = jnp.concatenate([after(packed[0], more), given], axis=0)
+    near_sum = after(part_sum, rest)
+    more = swap(near_sum, far_masks[0])
+    one = select(False, near_sum)
+    part_sum = add([near_sum, more], len(far_masks) == 1)
+    for mask in far_masks[1:]:
+        part_sum = add([part_sum, swap(part_sum, mask)], mask == far_masks[-1])
+    given = swap(after(packed[1], one), 1)
+    near = jnp.concatenate([packed[0], given], axis=0)
     parts = [near] + [swap(near, m) for m in near_masks[1:]]
     own_parts = [part_sum] + [swap(part_sum, m) for m in near_masks[1:3]]
     own_parts.append(swap(after(part_sum, parts[1]), near_masks[3]))

time: 43.6 us -> 47 us (1.078)
  starting transfers between devices: 14.3 us -> 18.9 us
  waiting for transfers between devices: 16.2 us -> 14.9 us
    ppermute x15, starting transfers between devices: 14.3 us -> 18.9 us  [swap(): return lax.ppermute(x, 'ex', [(d, d ^ mask) for d in range(n_ex)])]
    ppermute x15, waiting for transfers between devices: 16.2 us -> 14.9 us  [swap(): return lax.ppermute(x, 'ex', [(d, d ^ mask) for d in range(n_ex)])]
  transfers between devices with their start and end apart: 15 -> 15, of which waited for: 9 -> 7; matrix products, arithmetic and copies ran while one was open for 0% -> 0% of each run, Pallas kernels for 9% -> 7%
where the time goes in v13:
time: 47 us; the launch traced here: 46.9 us
  starting transfers between devices  18.9 us (40%)
  waiting for transfers between devices  14.9 us (32%)
  Pallas kernels  12.1 us (26%)
  between operations  0.8 us (2%)
    ppermute x15, starting transfers between devices, swap(): return lax.ppermute(x, 'ex', [(d, d ^ mask) for d in range(n_ex)])  18.9 us
    ppermute x15, waiting for transfers between devices, swap(): return lax.ppermute(x, 'ex', [(d, d ^ mask) for d in range(n_ex)])  14.9 us
    pallas_call x1, Pallas kernels, on_device(): pl.pallas_call(functools.partial(sums_kernel, n_ex=n_ex), in_specs=[hbm]...  5.02 us
    pallas_call x1, Pallas kernels, on_device(): pl.pallas_call(functools.partial(pursuit_kernel, steps=steps, scale=1.0 /...  3.19 us
    pallas_call x1, Pallas kernels, on_device(): pl.pallas_call(functools.partial(half_kernel, classes=classes), in_specs=...  2.06 us
  transfers between devices with their start and end apart: 15, of which 7 were waited for; matrix products, arithmetic and copies ran while one was open for 0% of the time, Pallas kernels for 7%

profile of v13, /device:TPU:0, one launch (start us, length us, event | category | flops | bytes accessed | tf_op | source)
XLA Modules:
  0.0 46.9 jit_solution(18205047814341957965)
XLA Ops:
  0.6 5.0 %class_sums.1 = (bf16[640,8192]{1,0:T(8,128)(2,1)S(1)}, f32[264,512]{1,0:T(8,128)S(1)}, f32[264,512]{1,0:T(8,128)S(1)}, f32[8,8192]{1,0:T(8,128)S(1)}) custom-call(s32[640]{0:T(1024)} %labels_ref.1, s32[3,32]{1,0:T(4,128)} %pick_ref.1, bf16[640,8192]{1,0:T(8,128)(2,1)} %feat_hbm.1), custom_call_target="tpu_custom_call" | custom-call | tf_op jit(solution)/shard_map/class_sums/pallas_call | solution.py:329
  5.7 0.0 copy-start.1
  5.7 0.5 %collective-permute-start = (f32[264,512]{1,0:T(8,128)S(1)}, f32[264,512]{1,0:T(8,128)S(1)}, u32[]{:S(2)}, u32[]{:S(2)}) collective-permute-start(f32[264,512]{1,0:T(8,128)S(1)} %get-tuple-element.25), channel_id=1, source_target_pairs={{0,1},{1,0},{2,3},{3,2},{4,5},{5,4},{6,7},{7,6},{8,9},{9,8},{10,11... | collective-permute-start | bytes 1622024 | tf_op jit(solution)/shard_map/ppermute | solution.py:324
  6.2 3.7 %collective-permute-start.2 = (bf16[2,8,3072]{2,1,0:T(8,128)(2,1)S(1)}, bf16[2,8,3072]{2,1,0:T(8,128)(2,1)S(1)}, u32[]{:S(2)}, u32[]{:S(2)}) collective-permute-start(bf16[2,8,3072]{2,1,0:T(8,128)(2,1)S(1)} %pack_rows.1), channel_id=1, source_target_pairs={{0,8},{1,9},{2,10},{3,11},{4,12},{5,13},{6,14},{7,15},{8,0},{9,1},... | collective-permute-start | bytes 294920 | tf_op jit(solution)/shard_map/ppermute | solution.py:324
  9.9 0.2 pair_sums.1
  10.1 1.6 %collective-permute-start.1 = (s16[2,136,128]{2,1,0:T(8,128)(2,1)S(1)}, s16[2,136,128]{2,1,0:T(8,128)(2,1)S(1)}, u32[]{:S(2)}, u32[]{:S(2)}) collective-permute-start(s16[2,136,128]{2,1,0:T(8,128)(2,1)S(1)} %get-tuple-element.27), channel_id=1, source_target_pairs={{0,4},{1,5},{2,6},{3,7},{4,0},{5,1},{6,2},{7,3},{8,12},{9,13},{10,... | collective-permute-start | bytes 208904 | tf_op jit(solution)/shard_map/ppermute | solution.py:324
  11.8 1.5 %collective-permute-start.3 = (s16[2,136,128]{2,1,0:T(8,128)(2,1)S(1)}, s16[2,136,128]{2,1,0:T(8,128)(2,1)S(1)}, u32[]{:S(2)}, u32[]{:S(2)}) collective-permute-start(s16[2,136,128]{2,1,0:T(8,128)(2,1)S(1)} %get-tuple-element.30), channel_id=1, source_target_pairs={{0,2},{1,3},{2,0},{3,1},{4,6},{5,7},{6,4},{7,5},{8,10},{9,11},{10,... | collective-permute-start | bytes 208904 | tf_op jit(solution)/shard_map/ppermute | solution.py:324
  13.3 0.4 collective-permute-start.4
  13.7 1.8 %collective-permute-done.2 = bf16[2,8,3072]{2,1,0:T(8,128)(2,1)S(1)} collective-permute-done((bf16[2,8,3072]{2,1,0:T(8,128)(2,1)S(1)}, bf16[2,8,3072]{2,1,0:T(8,128)(2,1)S(1)}, u32[]{:S(2)}, u32[]{:S(2)}) %collective-permute-start.2) | collective-permute-done | bytes 98336 | tf_op jit(solution)/shard_map/ppermute | solution.py:324
  15.5 0.3 select_tails.1.rest_ref
  15.8 0.2 collective-permute-done.3.refs_2_
  16.1 2.4 %collective-permute-done.4.refs_3_ = s16[2,136,128]{2,1,0:T(8,128)(2,1)S(1)} collective-permute-done((s16[2,136,128]{2,1,0:T(8,128)(2,1)S(1)}, s16[2,136,128]{2,1,0:T(8,128)(2,1)S(1)}, u32[]{:S(2)}, u32[]{:S(2)}) %collective-permute-start.4) | collective-permute-done | bytes 69664 | tf_op jit(solution)/shard_map/ppermute | solution.py:324
  18.5 0.3 add_sums.2.refs_0_
  18.8 0.3 select_rows.1.one_ref
  19.1 0.1 collective-permute-start.5
  19.2 1.3 %collective-permute-done.5 = bf16[16,3072]{1,0:T(8,128)(2,1)S(1)} collective-permute-done((bf16[16,3072]{1,0:T(8,128)(2,1)S(1)}, bf16[16,3072]{1,0:T(8,128)(2,1)S(1)}, u32[]{:S(2)}, u32[]{:S(2)}) %collective-permute-start.5) | collective-permute-done | bytes 98336 | tf_op jit(solution)/shard_map/ppermute | solution.py:324
  20.5 0.6 %collective-permute-start.6 = (bf16[32,3072]{1,0:T(8,128)(2,1)S(1)}, bf16[32,3072]{1,0:T(8,128)(2,1)S(1)}, u32[]{:S(2)}, u32[]{:S(2)}) collective-permute-start(bf16[32,3072]{1,0:T(8,128)(2,1)S(1)} %pad_maximum_fusion.1.refs_0_), channel_id=1, source_target_pairs={{0,4},{1,5},{2,6},{3,7},{4,0},{5,1},{6,2},{7,3},{8,12},{9,13},{10,... | collective-permute-start | bytes 589832 | tf_op jit(solution)/shard_map/ppermute | solution.py:324
  21.1 1.5 %collective-permute-start.8 = (bf16[32,3072]{1,0:T(8,128)(2,1)S(1)}, bf16[32,3072]{1,0:T(8,128)(2,1)S(1)}, u32[]{:S(2)}, u32[]{:S(2)}) collective-permute-start(bf16[32,3072]{1,0:T(8,128)(2,1)S(1)} %pad_maximum_fusion.1.refs_0_), channel_id=1, source_target_pairs={{0,6},{1,7},{2,4},{3,5},{4,2},{5,3},{6,0},{7,1},{8,14},{9,15},{10,... | collective-permute-start | bytes 589832 | tf_op jit(solution)/shard_map/ppermute | solution.py:324
  22.6 1.4 %collective-permute-start.7 = (bf16[32,3072]{1,0:T(8,128)(2,1)S(1)}, bf16[32,3072]{1,0:T(8,128)(2,1)S(1)}, u32[]{:S(2)}, u32[]{:S(2)}) collective-permute-start(bf16[32,3072]{1,0:T(8,128)(2,1)S(1)} %pad_maximum_fusion.1.refs_0_), channel_id=1, source_target_pairs={{0,2},{1,3},{2,0},{3,1},{4,6},{5,7},{6,4},{7,5},{8,10},{9,11},{10,... | collective-permute-start | bytes 589832 | tf_op jit(solution)/shard_map/ppermute | solution.py:324
  24.0 1.9 %collective-permute-start.10 = (s16[2,136,128]{2,1,0:T(8,128)(2,1)S(1)}, s16[2,136,128]{2,1,0:T(8,128)(2,1)S(1)}, u32[]{:S(2)}, u32[]{:S(2)}) collective-permute-start(s16[2,136,128]{2,1,0:T(8,128)(2,1)S(1)} %add_sums.2.refs_0_), channel_id=1, source_target_pairs={{0,8},{1,9},{2,10},{3,11},{4,12},{5,13},{6,14},{7,15},{8,0},{9,1},... | collective-permute-start | bytes 208904 | tf_op jit(solution)/shard_map/ppermute | solution.py:324
  25.9 5.4 %collective-permute-done.10.refs_1_ = s16[2,136,128]{2,1,0:T(8,128)(2,1)S(1)} collective-permute-done((s16[2,136,128]{2,1,0:T(8,128)(2,1)S(1)}, s16[2,136,128]{2,1,0:T(8,128)(2,1)S(1)}, u32[]{:S(2)}, u32[]{:S(2)}) %collective-permute-start.10) | collective-permute-done | bytes 69664 | tf_op jit(solution)/shard_map/ppermute | solution.py:324
  31.4 0.3 add_sums.3
  31.6 0.6 %collective-permute-start.12 = (s16[2,136,128]{2,1,0:T(8,128)(2,1)S(1)}, s16[2,136,128]{2,1,0:T(8,128)(2,1)S(1)}, u32[]{:S(2)}, u32[]{:S(2)}) collective-permute-start(s16[2,136,128]{2,1,0:T(8,128)(2,1)S(1)} %add_sums.3), channel_id=1, source_target_pairs={{0,2},{1,3},{2,0},{3,1},{4,6},{5,7},{6,4},{7,5},{8,10},{9,11},{10,... | collective-permute-start | bytes 208904 | tf_op jit(solution)/shard_map/ppermute | solution.py:324
  32.2 4.0 %collective-permute-start.11 = (s16[2,136,128]{2,1,0:T(8,128)(2,1)S(1)}, s16[2,136,128]{2,1,0:T(8,128)(2,1)S(1)}, u32[]{:S(2)}, u32[]{:S(2)}) collective-permute-start(s16[2,136,128]{2,1,0:T(8,128)(2,1)S(1)} %add_sums.3), channel_id=1, source_target_pairs={{0,4},{1,5},{2,6},{3,7},{4,0},{5,1},{6,2},{7,3},{8,12},{9,13},{10,... | collective-permute-start | bytes 208904 | tf_op jit(solution)/shard_map/ppermute | solution.py:324
  36.2 1.0 %collective-permute-start.13 = (s16[2,136,128]{2,1,0:T(8,128)(2,1)S(1)}, s16[2,136,128]{2,1,0:T(8,128)(2,1)S(1)}, u32[]{:S(2)}, u32[]{:S(2)}) collective-permute-start(s16[2,136,128]{2,1,0:T(8,128)(2,1)S(1)} %add_sums.3), channel_id=1, source_target_pairs={{0,6},{1,7},{2,4},{3,5},{4,2},{5,3},{6,0},{7,1},{8,14},{9,15},{10,... | collective-permute-start | bytes 208904 | tf_op jit(solution)/shard_map/ppermute | solution.py:324
  37.2 0.4 picked_rows.1.x_ref.x_own
  37.6 0.1 collective-permute-start.9
  37.7 0.8 %collective-permute-done.11 = s16[2,136,128]{2,1,0:T(8,128)(2,1)S(1)} collective-permute-done((s16[2,136,128]{2,1,0:T(8,128)(2,1)S(1)}, s16[2,136,128]{2,1,0:T(8,128)(2,1)S(1)}, u32[]{:S(2)}, u32[]{:S(2)}) %collective-permute-start.11) | collective-permute-done | bytes 69664 | tf_op jit(solution)/shard_map/ppermute | solution.py:324
  38.5 2.9 %collective-permute-done.13 = s16[2,136,128]{2,1,0:T(8,128)(2,1)S(1)} collective-permute-done((s16[2,136,128]{2,1,0:T(8,128)(2,1)S(1)}, s16[2,136,128]{2,1,0:T(8,128)(2,1)S(1)}, u32[]{:S(2)}, u32[]{:S(2)}) %collective-permute-start.13) | collective-permute-done | bytes 69664 | tf_op jit(solution)/shard_map/ppermute | solution.py:324
  41.5 0.1 collective-permute-start.14
  41.6 2.1 %own_half_products.1 = (f32[96,640]{1,0:T(8,128)S(1)}, f32[128,96]{1,0:T(8,128)S(1)}, f32[32,4096]{1,0:T(8,128)S(1)}) custom-call(bf16[640,8192]{1,0:T(8,128)(2,1)S(1)} %get-tuple-element.23.feat_ref, s16[8,136,128]{2,1,0:T(8,128)(2,1)S(1)} %constant_dynamic-update-slice_fusion.code_ref, bf16[96,4096]{1,0:T(8,128)(2,1)S(1)} %picked_rows.1.x_ref.x_own), custom_call_target="tpu_custom_call" | custom-call | tf_op jit(solution)/shard_map/own_half_products/pallas_call | solution.py:416
  43.7 3.2 %pursuit.1 = (f32[3,640]{1,0:T(4,128)}, f32[32,8192]{1,0:T(8,128)}) custom-call(s32[640]{0:T(1024)S(1)} %copy-done.1, bf16[640,8192]{1,0:T(8,128)(2,1)S(1)} %get-tuple-element.23.feat_ref, bf16[96,4096]{1,0:T(8,128)(2,1)S(1)} %picked_rows.1.x_ref.x_own, bf16[96,4096]{1,0:T(8,128)(2,1)S(1)} %collective-permute-done.9.x_twin, ...), custom_call_target="tpu_custom_call" | custom-call | tf_op jit(solution)/shard_map/pursuit/pallas_call | solution.py:430
  (18 shorter events, 0.1 us)
Async XLA Ops:
  0.6 14.9 %copy-start = (s32[3,32]{1,0:T(4,128)S(1)}, s32[3,32]{1,0:T(4,128)}, u32[]{:S(2)}) copy-start(s32[3,32]{1,0:T(4,128)} %pick_ref.1) | copy-start | bytes 1156
  5.7 38.0 %copy-start.1 = (s32[640]{0:T(1024)S(1)}, s32[640]{0:T(1024)}, u32[]{:S(2)}) copy-start(s32[640]{0:T(1024)} %labels_ref.1) | copy-start | bytes 7684
  5.7 4.2 %collective-permute-start = (f32[264,512]{1,0:T(8,128)S(1)}, f32[264,512]{1,0:T(8,128)S(1)}, u32[]{:S(2)}, u32[]{:S(2)}) collective-permute-start(f32[264,512]{1,0:T(8,128)S(1)} %get-tuple-element.25), channel_id=1, source_target_pairs={{0,1},{1,0},{2,3},{3,2},{4,5},{5,4},{6,7},{7,6},{8,9},{9,8},{10,11... | collective-permute-start | bytes 1622024 | tf_op jit(solution)/shard_map/ppermute | solution.py:324
  6.2 9.2 %collective-permute-start.2 = (bf16[2,8,3072]{2,1,0:T(8,128)(2,1)S(1)}, bf16[2,8,3072]{2,1,0:T(8,128)(2,1)S(1)}, u32[]{:S(2)}, u32[]{:S(2)}) collective-permute-start(bf16[2,8,3072]{2,1,0:T(8,128)(2,1)S(1)} %pack_rows.1), channel_id=1, source_target_pairs={{0,8},{1,9},{2,10},{3,11},{4,12},{5,13},{6,14},{7,15},{8,0},{9,1},... | collective-permute-start | bytes 294920 | tf_op jit(solution)/shard_map/ppermute | solution.py:324
  10.1 5.7 %collective-permute-start.1 = (s16[2,136,128]{2,1,0:T(8,128)(2,1)S(1)}, s16[2,136,128]{2,1,0:T(8,128)(2,1)S(1)}, u32[]{:S(2)}, u32[]{:S(2)}) collective-permute-start(s16[2,136,128]{2,1,0:T(8,128)(2,1)S(1)} %get-tuple-element.27), channel_id=1, source_target_pairs={{0,4},{1,5},{2,6},{3,7},{4,0},{5,1},{6,2},{7,3},{8,12},{9,13},{10,... | collective-permute-start | bytes 208904 | tf_op jit(solution)/shard_map/ppermute | solution.py:324
  11.8 4.3 %collective-permute-start.3 = (s16[2,136,128]{2,1,0:T(8,128)(2,1)S(1)}, s16[2,136,128]{2,1,0:T(8,128)(2,1)S(1)}, u32[]{:S(2)}, u32[]{:S(2)}) collective-permute-start(s16[2,136,128]{2,1,0:T(8,128)(2,1)S(1)} %get-tuple-element.30), channel_id=1, source_target_pairs={{0,2},{1,3},{2,0},{3,1},{4,6},{5,7},{6,4},{7,5},{8,10},{9,11},{10,... | collective-permute-start | bytes 208904 | tf_op jit(solution)/shard_map/ppermute | solution.py:324
  13.3 5.2 %collective-permute-start.4 = (s16[2,136,128]{2,1,0:T(8,128)(2,1)S(1)}, s16[2,136,128]{2,1,0:T(8,128)(2,1)S(1)}, u32[]{:S(2)}, u32[]{:S(2)}) collective-permute-start(s16[2,136,128]{2,1,0:T(8,128)(2,1)S(1)} %get-tuple-element.31), channel_id=1, source_target_pairs={{0,6},{1,7},{2,4},{3,5},{4,2},{5,3},{6,0},{7,1},{8,14},{9,15},{10,... | collective-permute-start | bytes 208904 | tf_op jit(solution)/shard_map/ppermute | solution.py:324
  19.1 1.4 %collective-permute-start.5 = (bf16[16,3072]{1,0:T(8,128)(2,1)S(1)}, bf16[16,3072]{1,0:T(8,128)(2,1)S(1)}, u32[]{:S(2)}, u32[]{:S(2)}) collective-permute-start(bf16[16,3072]{1,0:T(8,128)(2,1)S(1)} %get-tuple-element.35), channel_id=1, source_target_pairs={{0,1},{1,0},{2,3},{3,2},{4,5},{5,4},{6,7},{7,6},{8,9},{9,8},{10,11... | collective-permute-start | bytes 294920 | tf_op jit(solution)/shard_map/ppermute | solution.py:324
  20.5 15.7 %collective-permute-start.6 = (bf16[32,3072]{1,0:T(8,128)(2,1)S(1)}, bf16[32,3072]{1,0:T(8,128)(2,1)S(1)}, u32[]{:S(2)}, u32[]{:S(2)}) collective-permute-start(bf16[32,3072]{1,0:T(8,128)(2,1)S(1)} %pad_maximum_fusion.1.refs_0_), channel_id=1, source_target_pairs={{0,4},{1,5},{2,6},{3,7},{4,0},{5,1},{6,2},{7,3},{8,12},{9,13},{10,... | collective-permute-start | bytes 589832 | tf_op jit(solution)/shard_map/ppermute | solution.py:324
  21.1 16.1 %collective-permute-start.8 = (bf16[32,3072]{1,0:T(8,128)(2,1)S(1)}, bf16[32,3072]{1,0:T(8,128)(2,1)S(1)}, u32[]{:S(2)}, u32[]{:S(2)}) collective-permute-start(bf16[32,3072]{1,0:T(8,128)(2,1)S(1)} %pad_maximum_fusion.1.refs_0_), channel_id=1, source_target_pairs={{0,6},{1,7},{2,4},{3,5},{4,2},{5,3},{6,0},{7,1},{8,14},{9,15},{10,... | collective-permute-start | bytes 589832 | tf_op jit(solution)/shard_map/ppermute | solution.py:324
  22.6 14.6 %collective-permute-start.7 = (bf16[32,3072]{1,0:T(8,128)(2,1)S(1)}, bf16[32,3072]{1,0:T(8,128)(2,1)S(1)}, u32[]{:S(2)}, u32[]{:S(2)}) collective-permute-start(bf16[32,3072]{1,0:T(8,128)(2,1)S(1)} %pad_maximum_fusion.1.refs_0_), channel_id=1, source_target_pairs={{0,2},{1,3},{2,0},{3,1},{4,6},{5,7},{6,4},{7,5},{8,10},{9,11},{10,... | collective-permute-start | bytes 589832 | tf_op jit(solution)/shard_map/ppermute | solution.py:324
  24.0 7.3 %collective-permute-start.10 = (s16[2,136,128]{2,1,0:T(8,128)(2,1)S(1)}, s16[2,136,128]{2,1,0:T(8,128)(2,1)S(1)}, u32[]{:S(2)}, u32[]{:S(2)}) collective-permute-start(s16[2,136,128]{2,1,0:T(8,128)(2,1)S(1)} %add_sums.2.refs_0_), channel_id=1, source_target_pairs={{0,8},{1,9},{2,10},{3,11},{4,12},{5,13},{6,14},{7,15},{8,0},{9,1},... | collective-permute-start | bytes 208904 | tf_op jit(solution)/shard_map/ppermute | solution.py:324
  31.6 6.0 %collective-permute-start.12 = (s16[2,136,128]{2,1,0:T(8,128)(2,1)S(1)}, s16[2,136,128]{2,1,0:T(8,128)(2,1)S(1)}, u32[]{:S(2)}, u32[]{:S(2)}) collective-permute-start(s16[2,136,128]{2,1,0:T(8,128)(2,1)S(1)} %add_sums.3), channel_id=1, source_target_pairs={{0,2},{1,3},{2,0},{3,1},{4,6},{5,7},{6,4},{7,5},{8,10},{9,11},{10,... | collective-permute-start | bytes 208904 | tf_op jit(solution)/shard_map/ppermute | solution.py:324
  32.2 6.3 %collective-permute-start.11 = (s16[2,136,128]{2,1,0:T(8,128)(2,1)S(1)}, s16[2,136,128]{2,1,0:T(8,128)(2,1)S(1)}, u32[]{:S(2)}, u32[]{:S(2)}) collective-permute-start(s16[2,136,128]{2,1,0:T(8,128)(2,1)S(1)} %add_sums.3), channel_id=1, source_target_pairs={{0,4},{1,5},{2,6},{3,7},{4,0},{5,1},{6,2},{7,3},{8,12},{9,13},{10,... | collective-permute-start | bytes 208904 | tf_op jit(solution)/shard_map/ppermute | solution.py:324
  36.2 5.2 %collective-permute-start.13 = (s16[2,136,128]{2,1,0:T(8,128)(2,1)S(1)}, s16[2,136,128]{2,1,0:T(8,128)(2,1)S(1)}, u32[]{:S(2)}, u32[]{:S(2)}) collective-permute-start(s16[2,136,128]{2,1,0:T(8,128)(2,1)S(1)} %add_sums.3), channel_id=1, source_target_pairs={{0,6},{1,7},{2,4},{3,5},{4,2},{5,3},{6,0},{7,1},{8,14},{9,15},{10,... | collective-permute-start | bytes 208904 | tf_op jit(solution)/shard_map/ppermute | solution.py:324
  37.6 6.0 %collective-permute-start.9 = (bf16[96,4096]{1,0:T(8,128)(2,1)S(1)}, bf16[96,4096]{1,0:T(8,128)(2,1)S(1)}, u32[]{:S(2)}, u32[]{:S(2)}) collective-permute-start(bf16[96,4096]{1,0:T(8,128)(2,1)S(1)} %picked_rows.1.x_ref.x_own), channel_id=1, source_target_pairs={{0,1},{1,0},{2,3},{3,2},{4,5},{5,4},{6,7},{7,6},{8,9},{9,8},{10,11... | collective-permute-start | bytes 2359304 | tf_op jit(solution)/shard_map/ppermute | solution.py:324
  41.5 2.1 %collective-permute-start.14 = (s16[8,136,128]{2,1,0:T(8,128)(2,1)S(1)}, s16[8,136,128]{2,1,0:T(8,128)(2,1)S(1)}, u32[]{:S(2)}, u32[]{:S(2)}) collective-permute-start(s16[8,136,128]{2,1,0:T(8,128)(2,1)S(1)} %constant_dynamic-update-slice_fusion.code_ref), channel_id=1, source_target_pairs={{0,1},{1,0},{2,3},{3,2},{4,5},{5,4},{6,7},{7,6},{8,9},{9,8},{10,11... | collective-permute-start | bytes 835592 | tf_op jit(solution)/shard_map/ppermute | solution.py:324

commit v14 on v13

--- a/solution.py
+++ b/solution.py
@@ -348,7 +348,7 @@
             out_specs=vmem,
             out_shape=code,
             compiler_params=limit,
-            cost_estimate=pl.CostEstimate(flops=0, bytes_accessed=10**8, transcendentals=0) if last else None,
+            cost_estimate=pl.CostEstimate(flops=10**10, bytes_accessed=10**8, transcendentals=0) if last else None,
             name="add_sums",
         )(*codes)
 
@@ -393,8 +393,8 @@
     part_sum = add([near_sum, more], len(far_masks) == 1)
     for mask in far_masks[1:]:
         part_sum = add([part_sum, swap(part_sum, mask)], mask == far_masks[-1])
-    given = swap(after(packed[1], one), 1)
-    near = jnp.concatenate([packed[0], given], axis=0)
+    given = swap(after(packed[1], near_sum), 1)
+    near = jnp.concatenate([after(packed[0], one), given], axis=0)
     parts = [near] + [swap(near, m) for m in near_masks[1:]]
     own_parts = [part_sum] + [swap(part_sum, m) for m in near_masks[1:3]]
     own_parts.append(swap(after(part_sum, parts[1]), near_masks[3]))

time: 47 us -> 45.2 us (0.962)
  waiting for transfers between devices: 14.9 us -> 13.2 us
    ppermute x15, waiting for transfers between devices: 14.9 us -> 13.2 us  [swap(): return lax.ppermute(x, 'ex', [(d, d ^ mask) for d in range(n_ex)])]
  transfers between devices with their start and end apart: 15 -> 15, of which waited for: 7 -> 6; matrix products, arithmetic and copies ran while one was open for 0% -> 0% of each run, Pallas kernels for 7% -> 8%
where the time goes in v14:
time: 45.2 us; the launch traced here: 45 us
  starting transfers between devices  18.8 us (42%)
  waiting for transfers between devices  13.2 us (29%)
  Pallas kernels  12.1 us (27%)
  between operations  0.82 us (2%)
    ppermute x15, starting transfers between devices, swap(): return lax.ppermute(x, 'ex', [(d, d ^ mask) for d in range(n_ex)])  18.8 us
    ppermute x15, waiting for transfers between devices, swap(): return lax.ppermute(x, 'ex', [(d, d ^ mask) for d in range(n_ex)])  13.2 us
    pallas_call x1, Pallas kernels, on_device(): pl.pallas_call(functools.partial(sums_kernel, n_ex=n_ex), in_specs=[hbm]...  5.02 us
    pallas_call x1, Pallas kernels, on_device(): pl.pallas_call(functools.partial(pursuit_kernel, steps=steps, scale=1.0 /...  3.19 us
    pallas_call x1, Pallas kernels, on_device(): pl.pallas_call(functools.partial(half_kernel, classes=classes), in_specs=...  2.06 us
  transfers between devices with their start and end apart: 15, of which 6 were waited for; matrix products, arithmetic and copies ran while one was open for 0% of the time, Pallas kernels for 8%

profile of v14, /device:TPU:0, one launch (start us, length us, event | category | flops | bytes accessed | tf_op | source)
XLA Modules:
  0.0 45.0 jit_solution(8507813891752351234)
XLA Ops:
  0.6 5.0 %class_sums.1 = (bf16[640,8192]{1,0:T(8,128)(2,1)S(1)}, f32[264,512]{1,0:T(8,128)S(1)}, f32[264,512]{1,0:T(8,128)S(1)}, f32[8,8192]{1,0:T(8,128)S(1)}) custom-call(s32[640]{0:T(1024)} %labels_ref.1, s32[3,32]{1,0:T(4,128)} %pick_ref.1, bf16[640,8192]{1,0:T(8,128)(2,1)} %feat_hbm.1), custom_call_target="tpu_custom_call" | custom-call | tf_op jit(solution)/shard_map/class_sums/pallas_call | solution.py:329
  5.7 0.5 %collective-permute-start = (f32[264,512]{1,0:T(8,128)S(1)}, f32[264,512]{1,0:T(8,128)S(1)}, u32[]{:S(2)}, u32[]{:S(2)}) collective-permute-start(f32[264,512]{1,0:T(8,128)S(1)} %get-tuple-element.26), channel_id=1, source_target_pairs={{0,1},{1,0},{2,3},{3,2},{4,5},{5,4},{6,7},{7,6},{8,9},{9,8},{10,11... | collective-permute-start | bytes 1622024 | tf_op jit(solution)/shard_map/ppermute | solution.py:324
  6.2 3.7 %collective-permute-start.2 = (bf16[2,8,3072]{2,1,0:T(8,128)(2,1)S(1)}, bf16[2,8,3072]{2,1,0:T(8,128)(2,1)S(1)}, u32[]{:S(2)}, u32[]{:S(2)}) collective-permute-start(bf16[2,8,3072]{2,1,0:T(8,128)(2,1)S(1)} %pack_rows.1), channel_id=1, source_target_pairs={{0,8},{1,9},{2,10},{3,11},{4,12},{5,13},{6,14},{7,15},{8,0},{9,1},... | collective-permute-start | bytes 294920 | tf_op jit(solution)/shard_map/ppermute | solution.py:324
  9.9 0.0 collective-permute-done.got_ref
  9.9 0.2 pair_sums.1
  10.1 1.6 %collective-permute-start.1 = (s16[2,136,128]{2,1,0:T(8,128)(2,1)S(1)}, s16[2,136,128]{2,1,0:T(8,128)(2,1)S(1)}, u32[]{:S(2)}, u32[]{:S(2)}) collective-permute-start(s16[2,136,128]{2,1,0:T(8,128)(2,1)S(1)} %get-tuple-element.28), channel_id=1, source_target_pairs={{0,4},{1,5},{2,6},{3,7},{4,0},{5,1},{6,2},{7,3},{8,12},{9,13},{10,... | collective-permute-start | bytes 208904 | tf_op jit(solution)/shard_map/ppermute | solution.py:324
  11.7 1.5 %collective-permute-start.3 = (s16[2,136,128]{2,1,0:T(8,128)(2,1)S(1)}, s16[2,136,128]{2,1,0:T(8,128)(2,1)S(1)}, u32[]{:S(2)}, u32[]{:S(2)}) collective-permute-start(s16[2,136,128]{2,1,0:T(8,128)(2,1)S(1)} %get-tuple-element.31), channel_id=1, source_target_pairs={{0,2},{1,3},{2,0},{3,1},{4,6},{5,7},{6,4},{7,5},{8,10},{9,11},{10,... | collective-permute-start | bytes 208904 | tf_op jit(solution)/shard_map/ppermute | solution.py:324
  13.3 0.4 collective-permute-start.4
  13.7 1.8 %collective-permute-done.2 = bf16[2,8,3072]{2,1,0:T(8,128)(2,1)S(1)} collective-permute-done((bf16[2,8,3072]{2,1,0:T(8,128)(2,1)S(1)}, bf16[2,8,3072]{2,1,0:T(8,128)(2,1)S(1)}, u32[]{:S(2)}, u32[]{:S(2)}) %collective-permute-start.2) | collective-permute-done | bytes 98336 | tf_op jit(solution)/shard_map/ppermute | solution.py:324
  15.5 0.3 select_tails.1.rest_ref
  15.8 0.0 collective-permute-done.1.refs_1_
  15.8 0.2 collective-permute-done.3.refs_2_
  16.1 2.4 %collective-permute-done.4.refs_3_ = s16[2,136,128]{2,1,0:T(8,128)(2,1)S(1)} collective-permute-done((s16[2,136,128]{2,1,0:T(8,128)(2,1)S(1)}, s16[2,136,128]{2,1,0:T(8,128)(2,1)S(1)}, u32[]{:S(2)}, u32[]{:S(2)}) %collective-permute-start.4) | collective-permute-done | bytes 69664 | tf_op jit(solution)/shard_map/ppermute | solution.py:324
  18.5 0.3 add_sums.2.refs_0_
  18.8 1.9 %collective-permute-start.10 = (s16[2,136,128]{2,1,0:T(8,128)(2,1)S(1)}, s16[2,136,128]{2,1,0:T(8,128)(2,1)S(1)}, u32[]{:S(2)}, u32[]{:S(2)}) collective-permute-start(s16[2,136,128]{2,1,0:T(8,128)(2,1)S(1)} %add_sums.2.refs_0_), channel_id=1, source_target_pairs={{0,8},{1,9},{2,10},{3,11},{4,12},{5,13},{6,14},{7,15},{8,0},{9,1},... | collective-permute-start | bytes 208904 | tf_op jit(solution)/shard_map/ppermute | solution.py:324
  20.6 0.3 select_rows.1.one_ref
  21.0 0.1 collective-permute-start.5
  21.0 1.3 %collective-permute-done.5 = bf16[16,3072]{1,0:T(8,128)(2,1)S(1)} collective-permute-done((bf16[16,3072]{1,0:T(8,128)(2,1)S(1)}, bf16[16,3072]{1,0:T(8,128)(2,1)S(1)}, u32[]{:S(2)}, u32[]{:S(2)}) %collective-permute-start.5) | collective-permute-done | bytes 98336 | tf_op jit(solution)/shard_map/ppermute | solution.py:324
  22.3 2.0 %collective-permute-start.8 = (bf16[32,3072]{1,0:T(8,128)(2,1)S(1)}, bf16[32,3072]{1,0:T(8,128)(2,1)S(1)}, u32[]{:S(2)}, u32[]{:S(2)}) collective-permute-start(bf16[32,3072]{1,0:T(8,128)(2,1)S(1)} %constant_dynamic-update-slice_fusion.refs_0_), channel_id=1, source_target_pairs={{0,6},{1,7},{2,4},{3,5},{4,2},{5,3},{6,0},{7,1},{8,14},{9,15},{10,... | collective-permute-start | bytes 589832 | tf_op jit(solution)/shard_map/ppermute | solution.py:324
  24.4 1.5 %collective-permute-start.7 = (bf16[32,3072]{1,0:T(8,128)(2,1)S(1)}, bf16[32,3072]{1,0:T(8,128)(2,1)S(1)}, u32[]{:S(2)}, u32[]{:S(2)}) collective-permute-start(bf16[32,3072]{1,0:T(8,128)(2,1)S(1)} %constant_dynamic-update-slice_fusion.refs_0_), channel_id=1, source_target_pairs={{0,2},{1,3},{2,0},{3,1},{4,6},{5,7},{6,4},{7,5},{8,10},{9,11},{10,... | collective-permute-start | bytes 589832 | tf_op jit(solution)/shard_map/ppermute | solution.py:324
  25.9 0.3 add_sums.3
  26.2 0.0 copy-start.1
  26.2 0.7 %collective-permute-start.12 = (s16[2,136,128]{2,1,0:T(8,128)(2,1)S(1)}, s16[2,136,128]{2,1,0:T(8,128)(2,1)S(1)}, u32[]{:S(2)}, u32[]{:S(2)}) collective-permute-start(s16[2,136,128]{2,1,0:T(8,128)(2,1)S(1)} %add_sums.3), channel_id=1, source_target_pairs={{0,2},{1,3},{2,0},{3,1},{4,6},{5,7},{6,4},{7,5},{8,10},{9,11},{10,... | collective-permute-start | bytes 208904 | tf_op jit(solution)/shard_map/ppermute | solution.py:324
  26.9 1.9 %collective-permute-start.11 = (s16[2,136,128]{2,1,0:T(8,128)(2,1)S(1)}, s16[2,136,128]{2,1,0:T(8,128)(2,1)S(1)}, u32[]{:S(2)}, u32[]{:S(2)}) collective-permute-start(s16[2,136,128]{2,1,0:T(8,128)(2,1)S(1)} %add_sums.3), channel_id=1, source_target_pairs={{0,4},{1,5},{2,6},{3,7},{4,0},{5,1},{6,2},{7,3},{8,12},{9,13},{10,... | collective-permute-start | bytes 208904 | tf_op jit(solution)/shard_map/ppermute | solution.py:324
  28.8 5.6 %collective-permute-done.6.refs_1_ = bf16[32,3072]{1,0:T(8,128)(2,1)S(1)} collective-permute-done((bf16[32,3072]{1,0:T(8,128)(2,1)S(1)}, bf16[32,3072]{1,0:T(8,128)(2,1)S(1)}, u32[]{:S(2)}, u32[]{:S(2)}) %collective-permute-start.6) | collective-permute-done | bytes 196640 | tf_op jit(solution)/shard_map/ppermute | solution.py:324
  34.4 2.9 %collective-permute-start.13 = (s16[2,136,128]{2,1,0:T(8,128)(2,1)S(1)}, s16[2,136,128]{2,1,0:T(8,128)(2,1)S(1)}, u32[]{:S(2)}, u32[]{:S(2)}) collective-permute-start(s16[2,136,128]{2,1,0:T(8,128)(2,1)S(1)} %add_sums.3), channel_id=1, source_target_pairs={{0,6},{1,7},{2,4},{3,5},{4,2},{5,3},{6,0},{7,1},{8,14},{9,15},{10,... | collective-permute-start | bytes 208904 | tf_op jit(solution)/shard_map/ppermute | solution.py:324
  37.3 0.4 picked_rows.1.x_ref.x_own
  37.7 0.1 collective-permute-start.9
  37.8 1.8 %collective-permute-done.13 = s16[2,136,128]{2,1,0:T(8,128)(2,1)S(1)} collective-permute-done((s16[2,136,128]{2,1,0:T(8,128)(2,1)S(1)}, s16[2,136,128]{2,1,0:T(8,128)(2,1)S(1)}, u32[]{:S(2)}, u32[]{:S(2)}) %collective-permute-start.13) | collective-permute-done | bytes 69664 | tf_op jit(solution)/shard_map/ppermute | solution.py:324
  39.7 0.1 collective-permute-start.14
  39.7 2.1 %own_half_products.1 = (f32[96,640]{1,0:T(8,128)S(1)}, f32[128,96]{1,0:T(8,128)S(1)}, f32[32,4096]{1,0:T(8,128)S(1)}) custom-call(bf16[640,8192]{1,0:T(8,128)(2,1)S(1)} %get-tuple-element.24.feat_ref, s16[8,136,128]{2,1,0:T(8,128)(2,1)S(1)} %constant_dynamic-update-slice_fusion.2.code_ref, bf16[96,4096]{1,0:T(8,128)(2,1)S(1)} %picked_rows.1.x_ref.x_own), custom_call_target="tpu_custom_call" | custom-call | tf_op jit(solution)/shard_map/own_half_products/pallas_call | solution.py:416
  41.8 3.2 %pursuit.1 = (f32[3,640]{1,0:T(4,128)}, f32[32,8192]{1,0:T(8,128)}) custom-call(s32[640]{0:T(1024)S(1)} %copy-done.1, bf16[640,8192]{1,0:T(8,128)(2,1)S(1)} %get-tuple-element.24.feat_ref, bf16[96,4096]{1,0:T(8,128)(2,1)S(1)} %picked_rows.1.x_ref.x_own, bf16[96,4096]{1,0:T(8,128)(2,1)S(1)} %collective-permute-done.9.x_twin, ...), custom_call_target="tpu_custom_call" | custom-call | tf_op jit(solution)/shard_map/pursuit/pallas_call | solution.py:430
  (19 shorter events, 0.1 us)
Async XLA Ops:
  0.6 14.8 %copy-start = (s32[3,32]{1,0:T(4,128)S(1)}, s32[3,32]{1,0:T(4,128)}, u32[]{:S(2)}) copy-start(s32[3,32]{1,0:T(4,128)} %pick_ref.1) | copy-start | bytes 1156
  5.7 4.2 %collective-permute-start = (f32[264,512]{1,0:T(8,128)S(1)}, f32[264,512]{1,0:T(8,128)S(1)}, u32[]{:S(2)}, u32[]{:S(2)}) collective-permute-start(f32[264,512]{1,0:T(8,128)S(1)} %get-tuple-element.26), channel_id=1, source_target_pairs={{0,1},{1,0},{2,3},{3,2},{4,5},{5,4},{6,7},{7,6},{8,9},{9,8},{10,11... | collective-permute-start | bytes 1622024 | tf_op jit(solution)/shard_map/ppermute | solution.py:324
  6.2 9.2 %collective-permute-start.2 = (bf16[2,8,3072]{2,1,0:T(8,128)(2,1)S(1)}, bf16[2,8,3072]{2,1,0:T(8,128)(2,1)S(1)}, u32[]{:S(2)}, u32[]{:S(2)}) collective-permute-start(bf16[2,8,3072]{2,1,0:T(8,128)(2,1)S(1)} %pack_rows.1), channel_id=1, source_target_pairs={{0,8},{1,9},{2,10},{3,11},{4,12},{5,13},{6,14},{7,15},{8,0},{9,1},... | collective-permute-start | bytes 294920 | tf_op jit(solution)/shard_map/ppermute | solution.py:324
  10.1 5.7 %collective-permute-start.1 = (s16[2,136,128]{2,1,0:T(8,128)(2,1)S(1)}, s16[2,136,128]{2,1,0:T(8,128)(2,1)S(1)}, u32[]{:S(2)}, u32[]{:S(2)}) collective-permute-start(s16[2,136,128]{2,1,0:T(8,128)(2,1)S(1)} %get-tuple-element.28), channel_id=1, source_target_pairs={{0,4},{1,5},{2,6},{3,7},{4,0},{5,1},{6,2},{7,3},{8,12},{9,13},{10,... | collective-permute-start | bytes 208904 | tf_op jit(solution)/shard_map/ppermute | solution.py:324
  11.7 4.3 %collective-permute-start.3 = (s16[2,136,128]{2,1,0:T(8,128)(2,1)S(1)}, s16[2,136,128]{2,1,0:T(8,128)(2,1)S(1)}, u32[]{:S(2)}, u32[]{:S(2)}) collective-permute-start(s16[2,136,128]{2,1,0:T(8,128)(2,1)S(1)} %get-tuple-element.31), channel_id=1, source_target_pairs={{0,2},{1,3},{2,0},{3,1},{4,6},{5,7},{6,4},{7,5},{8,10},{9,11},{10,... | collective-permute-start | bytes 208904 | tf_op jit(solution)/shard_map/ppermute | solution.py:324
  13.3 5.2 %collective-permute-start.4 = (s16[2,136,128]{2,1,0:T(8,128)(2,1)S(1)}, s16[2,136,128]{2,1,0:T(8,128)(2,1)S(1)}, u32[]{:S(2)}, u32[]{:S(2)}) collective-permute-start(s16[2,136,128]{2,1,0:T(8,128)(2,1)S(1)} %get-tuple-element.32), channel_id=1, source_target_pairs={{0,6},{1,7},{2,4},{3,5},{4,2},{5,3},{6,0},{7,1},{8,14},{9,15},{10,... | collective-permute-start | bytes 208904 | tf_op jit(solution)/shard_map/ppermute | solution.py:324
  18.8 7.2 %collective-permute-start.10 = (s16[2,136,128]{2,1,0:T(8,128)(2,1)S(1)}, s16[2,136,128]{2,1,0:T(8,128)(2,1)S(1)}, u32[]{:S(2)}, u32[]{:S(2)}) collective-permute-start(s16[2,136,128]{2,1,0:T(8,128)(2,1)S(1)} %add_sums.2.refs_0_), channel_id=1, source_target_pairs={{0,8},{1,9},{2,10},{3,11},{4,12},{5,13},{6,14},{7,15},{8,0},{9,1},... | collective-permute-start | bytes 208904 | tf_op jit(solution)/shard_map/ppermute | solution.py:324
  21.0 1.4 %collective-permute-start.5 = (bf16[16,3072]{1,0:T(8,128)(2,1)S(1)}, bf16[16,3072]{1,0:T(8,128)(2,1)S(1)}, u32[]{:S(2)}, u32[]{:S(2)}) collective-permute-start(bf16[16,3072]{1,0:T(8,128)(2,1)S(1)} %get-tuple-element.37), channel_id=1, source_target_pairs={{0,1},{1,0},{2,3},{3,2},{4,5},{5,4},{6,7},{7,6},{8,9},{9,8},{10,11... | collective-permute-start | bytes 294920 | tf_op jit(solution)/shard_map/ppermute | solution.py:324
  22.3 14.9 %collective-permute-start.8 = (bf16[32,3072]{1,0:T(8,128)(2,1)S(1)}, bf16[32,3072]{1,0:T(8,128)(2,1)S(1)}, u32[]{:S(2)}, u32[]{:S(2)}) collective-permute-start(bf16[32,3072]{1,0:T(8,128)(2,1)S(1)} %constant_dynamic-update-slice_fusion.refs_0_), channel_id=1, source_target_pairs={{0,6},{1,7},{2,4},{3,5},{4,2},{5,3},{6,0},{7,1},{8,14},{9,15},{10,... | collective-permute-start | bytes 589832 | tf_op jit(solution)/shard_map/ppermute | solution.py:324
  24.4 12.9 %collective-permute-start.7 = (bf16[32,3072]{1,0:T(8,128)(2,1)S(1)}, bf16[32,3072]{1,0:T(8,128)(2,1)S(1)}, u32[]{:S(2)}, u32[]{:S(2)}) collective-permute-start(bf16[32,3072]{1,0:T(8,128)(2,1)S(1)} %constant_dynamic-update-slice_fusion.refs_0_), channel_id=1, source_target_pairs={{0,2},{1,3},{2,0},{3,1},{4,6},{5,7},{6,4},{7,5},{8,10},{9,11},{10,... | collective-permute-start | bytes 589832 | tf_op jit(solution)/shard_map/ppermute | solution.py:324
  25.9 8.5 %collective-permute-start.6 = (bf16[32,3072]{1,0:T(8,128)(2,1)S(1)}, bf16[32,3072]{1,0:T(8,128)(2,1)S(1)}, u32[]{:S(2)}, u32[]{:S(2)}) collective-permute-start(bf16[32,3072]{1,0:T(8,128)(2,1)S(1)} %constant_dynamic-update-slice_fusion.refs_0_), channel_id=1, source_target_pairs={{0,4},{1,5},{2,6},{3,7},{4,0},{5,1},{6,2},{7,3},{8,12},{9,13},{10,... | collective-permute-start | bytes 589832 | tf_op jit(solution)/shard_map/ppermute | solution.py:324
  26.2 15.6 %copy-start.1 = (s32[640]{0:T(1024)S(1)}, s32[640]{0:T(1024)}, u32[]{:S(2)}) copy-start(s32[640]{0:T(1024)} %labels_ref.1) | copy-start | bytes 7684
  26.2 11.6 %collective-permute-start.12 = (s16[2,136,128]{2,1,0:T(8,128)(2,1)S(1)}, s16[2,136,128]{2,1,0:T(8,128)(2,1)S(1)}, u32[]{:S(2)}, u32[]{:S(2)}) collective-permute-start(s16[2,136,128]{2,1,0:T(8,128)(2,1)S(1)} %add_sums.3), channel_id=1, source_target_pairs={{0,2},{1,3},{2,0},{3,1},{4,6},{5,7},{6,4},{7,5},{8,10},{9,11},{10,... | collective-permute-start | bytes 208904 | tf_op jit(solution)/shard_map/ppermute | solution.py:324
  26.9 10.9 %collective-permute-start.11 = (s16[2,136,128]{2,1,0:T(8,128)(2,1)S(1)}, s16[2,136,128]{2,1,0:T(8,128)(2,1)S(1)}, u32[]{:S(2)}, u32[]{:S(2)}) collective-permute-start(s16[2,136,128]{2,1,0:T(8,128)(2,1)S(1)} %add_sums.3), channel_id=1, source_target_pairs={{0,4},{1,5},{2,6},{3,7},{4,0},{5,1},{6,2},{7,3},{8,12},{9,13},{10,... | collective-permute-start | bytes 208904 | tf_op jit(solution)/shard_map/ppermute | solution.py:324
  34.4 5.2 %collective-permute-start.13 = (s16[2,136,128]{2,1,0:T(8,128)(2,1)S(1)}, s16[2,136,128]{2,1,0:T(8,128)(2,1)S(1)}, u32[]{:S(2)}, u32[]{:S(2)}) collective-permute-start(s16[2,136,128]{2,1,0:T(8,128)(2,1)S(1)} %add_sums.3), channel_id=1, source_target_pairs={{0,6},{1,7},{2,4},{3,5},{4,2},{5,3},{6,0},{7,1},{8,14},{9,15},{10,... | collective-permute-start | bytes 208904 | tf_op jit(solution)/shard_map/ppermute | solution.py:324
  37.7 4.2 %collective-permute-start.9 = (bf16[96,4096]{1,0:T(8,128)(2,1)S(1)}, bf16[96,4096]{1,0:T(8,128)(2,1)S(1)}, u32[]{:S(2)}, u32[]{:S(2)}) collective-permute-start(bf16[96,4096]{1,0:T(8,128)(2,1)S(1)} %picked_rows.1.x_ref.x_own), channel_id=1, source_target_pairs={{0,1},{1,0},{2,3},{3,2},{4,5},{5,4},{6,7},{7,6},{8,9},{9,8},{10,11... | collective-permute-start | bytes 2359304 | tf_op jit(solution)/shard_map/ppermute | solution.py:324
  39.7 2.1 %collective-permute-start.14 = (s16[8,136,128]{2,1,0:T(8,128)(2,1)S(1)}, s16[8,136,128]{2,1,0:T(8,128)(2,1)S(1)}, u32[]{:S(2)}, u32[]{:S(2)}) collective-permute-start(s16[8,136,128]{2,1,0:T(8,128)(2,1)S(1)} %constant_dynamic-update-slice_fusion.2.code_ref), channel_id=1, source_target_pairs={{0,1},{1,0},{2,3},{3,2},{4,5},{5,4},{6,7},{7,6},{8,9},{9,8},{10,11... | collective-permute-start | bytes 835592 | tf_op jit(solution)/shard_map/ppermute | solution.py:324

commit v15 on v14

--- a/solution.py
+++ b/solution.py
@@ -395,13 +395,15 @@
         part_sum = add([part_sum, swap(part_sum, mask)], mask == far_masks[-1])
     given = swap(after(packed[1], near_sum), 1)
     near = jnp.concatenate([after(packed[0], one), given], axis=0)
-    parts = [near] + [swap(near, m) for m in near_masks[1:]]
-    own_parts = [part_sum] + [swap(part_sum, m) for m in near_masks[1:3]]
-    own_parts.append(swap(after(part_sum, parts[1]), near_masks[3]))
+    by_z, by_y = swap(near, 4), swap(near, 2)
+    own_parts = [part_sum] + [swap(part_sum, m) for m in near_masks[1:]]
+    by_z, by_y = after(by_z, own_parts[1]), after(by_y, own_parts[1])
+    cut = near.shape[0] // 2
+    parts = [near, by_z, by_y, swap(by_y[:cut], 4), swap(by_z[cut:], 2)]
 
     x = pl.pallas_call(
         functools.partial(picked_kernel, steps=steps),
-        in_specs=[vmem] * 6,
+        in_specs=[vmem] * 7,
         out_specs=vmem,
         out_shape=jax.ShapeDtypeStruct((total, full // 2), bf16),
         scratch_shapes=[pltpu.VMEM((n_ex * 8, main), bf16)],

time: 45.2 us -> 45.7 us (1.011)
  waiting for transfers between devices: 13.2 us -> 14.7 us
  starting transfers between devices: 18.8 us -> 17.7 us
    ppermute x15 -> x16, waiting for transfers between devices: 13.2 us -> 14.7 us  [swap(): return lax.ppermute(x, 'ex', [(d, d ^ mask) for d in range(n_ex)])]
    ppermute x15 -> x16, starting transfers between devices: 18.8 us -> 17.7 us  [swap(): return lax.ppermute(x, 'ex', [(d, d ^ mask) for d in range(n_ex)])]
  transfers between devices with their start and end apart: 15 -> 16, of which waited for: 6 -> 7; matrix products, arithmetic and copies ran while one was open for 0% -> 0% of each run, Pallas kernels for 8% -> 8%
where the time goes in v15:
time: 45.7 us; the launch traced here: 45.5 us
  starting transfers between devices  17.7 us (39%)
  waiting for transfers between devices  14.7 us (32%)
  Pallas kernels  12.1 us (26%)
  between operations  0.82 us (2%)
    ppermute x16, starting transfers between devices, swap(): return lax.ppermute(x, 'ex', [(d, d ^ mask) for d in range(n_ex)])  17.7 us
    ppermute x16, waiting for transfers between devices, swap(): return lax.ppermute(x, 'ex', [(d, d ^ mask) for d in range(n_ex)])  14.7 us
    pallas_call x1, Pallas kernels, on_device(): pl.pallas_call(functools.partial(sums_kernel, n_ex=n_ex), in_specs=[hbm]...  5.02 us
    pallas_call x1, Pallas kernels, on_device(): pl.pallas_call(functools.partial(pursuit_kernel, steps=steps, scale=1.0 /...  3.19 us
    pallas_call x1, Pallas kernels, on_device(): pl.pallas_call(functools.partial(half_kernel, classes=classes), in_specs=...  2.06 us
  transfers between devices with their start and end apart: 16, of which 7 were waited for; matrix products, arithmetic and copies ran while one was open for 0% of the time, Pallas kernels for 8%

profile of v15, /device:TPU:0, one launch (start us, length us, event | category | flops | bytes accessed | tf_op | source)
XLA Modules:
  0.0 45.5 jit_solution(14855246552160226665)
XLA Ops:
  0.6 5.0 %class_sums.1 = (bf16[640,8192]{1,0:T(8,128)(2,1)S(1)}, f32[264,512]{1,0:T(8,128)S(1)}, f32[264,512]{1,0:T(8,128)S(1)}, f32[8,8192]{1,0:T(8,128)S(1)}) custom-call(s32[640]{0:T(1024)} %labels_ref.1, s32[3,32]{1,0:T(4,128)} %pick_ref.1, bf16[640,8192]{1,0:T(8,128)(2,1)} %feat_hbm.1), custom_call_target="tpu_custom_call" | custom-call | tf_op jit(solution)/shard_map/class_sums/pallas_call | solution.py:329
  5.7 0.5 %collective-permute-start = (f32[264,512]{1,0:T(8,128)S(1)}, f32[264,512]{1,0:T(8,128)S(1)}, u32[]{:S(2)}, u32[]{:S(2)}) collective-permute-start(f32[264,512]{1,0:T(8,128)S(1)} %get-tuple-element.27), channel_id=1, source_target_pairs={{0,1},{1,0},{2,3},{3,2},{4,5},{5,4},{6,7},{7,6},{8,9},{9,8},{10,11... | collective-permute-start | bytes 1622024 | tf_op jit(solution)/shard_map/ppermute | solution.py:324
  6.2 3.7 %collective-permute-start.2 = (bf16[2,8,3072]{2,1,0:T(8,128)(2,1)S(1)}, bf16[2,8,3072]{2,1,0:T(8,128)(2,1)S(1)}, u32[]{:S(2)}, u32[]{:S(2)}) collective-permute-start(bf16[2,8,3072]{2,1,0:T(8,128)(2,1)S(1)} %pack_rows.1), channel_id=1, source_target_pairs={{0,8},{1,9},{2,10},{3,11},{4,12},{5,13},{6,14},{7,15},{8,0},{9,1},... | collective-permute-start | bytes 294920 | tf_op jit(solution)/shard_map/ppermute | solution.py:324
  9.9 0.2 pair_sums.1
  10.1 1.6 %collective-permute-start.1 = (s16[2,136,128]{2,1,0:T(8,128)(2,1)S(1)}, s16[2,136,128]{2,1,0:T(8,128)(2,1)S(1)}, u32[]{:S(2)}, u32[]{:S(2)}) collective-permute-start(s16[2,136,128]{2,1,0:T(8,128)(2,1)S(1)} %get-tuple-element.29), channel_id=1, source_target_pairs={{0,4},{1,5},{2,6},{3,7},{4,0},{5,1},{6,2},{7,3},{8,12},{9,13},{10,... | collective-permute-start | bytes 208904 | tf_op jit(solution)/shard_map/ppermute | solution.py:324
  11.7 1.5 %collective-permute-start.3 = (s16[2,136,128]{2,1,0:T(8,128)(2,1)S(1)}, s16[2,136,128]{2,1,0:T(8,128)(2,1)S(1)}, u32[]{:S(2)}, u32[]{:S(2)}) collective-permute-start(s16[2,136,128]{2,1,0:T(8,128)(2,1)S(1)} %get-tuple-element.32), channel_id=1, source_target_pairs={{0,2},{1,3},{2,0},{3,1},{4,6},{5,7},{6,4},{7,5},{8,10},{9,11},{10,... | collective-permute-start | bytes 208904 | tf_op jit(solution)/shard_map/ppermute | solution.py:324
  13.3 0.4 collective-permute-start.4
  13.7 1.8 %collective-permute-done.2 = bf16[2,8,3072]{2,1,0:T(8,128)(2,1)S(1)} collective-permute-done((bf16[2,8,3072]{2,1,0:T(8,128)(2,1)S(1)}, bf16[2,8,3072]{2,1,0:T(8,128)(2,1)S(1)}, u32[]{:S(2)}, u32[]{:S(2)}) %collective-permute-start.2) | collective-permute-done | bytes 98336 | tf_op jit(solution)/shard_map/ppermute | solution.py:324
  15.5 0.3 select_tails.1.rest_ref
  15.8 0.2 collective-permute-done.3.refs_2_
  16.1 2.4 %collective-permute-done.4.refs_3_ = s16[2,136,128]{2,1,0:T(8,128)(2,1)S(1)} collective-permute-done((s16[2,136,128]{2,1,0:T(8,128)(2,1)S(1)}, s16[2,136,128]{2,1,0:T(8,128)(2,1)S(1)}, u32[]{:S(2)}, u32[]{:S(2)}) %collective-permute-start.4) | collective-permute-done | bytes 69664 | tf_op jit(solution)/shard_map/ppermute | solution.py:324
  18.5 0.3 add_sums.2.refs_0_
  18.8 1.9 %collective-permute-start.7 = (s16[2,136,128]{2,1,0:T(8,128)(2,1)S(1)}, s16[2,136,128]{2,1,0:T(8,128)(2,1)S(1)}, u32[]{:S(2)}, u32[]{:S(2)}) collective-permute-start(s16[2,136,128]{2,1,0:T(8,128)(2,1)S(1)} %add_sums.2.refs_0_), channel_id=1, source_target_pairs={{0,8},{1,9},{2,10},{3,11},{4,12},{5,13},{6,14},{7,15},{8,0},{9,1},... | collective-permute-start | bytes 208904 | tf_op jit(solution)/shard_map/ppermute | solution.py:324
  20.6 0.3 select_rows.1.one_ref
  21.0 0.1 collective-permute-start.5
  21.0 1.3 %collective-permute-done.5 = bf16[16,3072]{1,0:T(8,128)(2,1)S(1)} collective-permute-done((bf16[16,3072]{1,0:T(8,128)(2,1)S(1)}, bf16[16,3072]{1,0:T(8,128)(2,1)S(1)}, u32[]{:S(2)}, u32[]{:S(2)}) %collective-permute-start.5) | collective-permute-done | bytes 98336 | tf_op jit(solution)/shard_map/ppermute | solution.py:324
  22.3 0.7 %collective-permute-start.9 = (bf16[32,3072]{1,0:T(8,128)(2,1)S(1)}, bf16[32,3072]{1,0:T(8,128)(2,1)S(1)}, u32[]{:S(2)}, u32[]{:S(2)}) collective-permute-start(bf16[32,3072]{1,0:T(8,128)(2,1)S(1)} %constant_dynamic-update-slice_fusion.refs_0_), channel_id=1, source_target_pairs={{0,2},{1,3},{2,0},{3,1},{4,6},{5,7},{6,4},{7,5},{8,10},{9,11},{10,... | collective-permute-start | bytes 589832 | tf_op jit(solution)/shard_map/ppermute | solution.py:324
  23.0 1.9 %collective-permute-start.6 = (bf16[32,3072]{1,0:T(8,128)(2,1)S(1)}, bf16[32,3072]{1,0:T(8,128)(2,1)S(1)}, u32[]{:S(2)}, u32[]{:S(2)}) collective-permute-start(bf16[32,3072]{1,0:T(8,128)(2,1)S(1)} %constant_dynamic-update-slice_fusion.refs_0_), channel_id=1, source_target_pairs={{0,4},{1,5},{2,6},{3,7},{4,0},{5,1},{6,2},{7,3},{8,12},{9,13},{10,... | collective-permute-start | bytes 589832 | tf_op jit(solution)/shard_map/ppermute | solution.py:324
  24.9 0.3 add_sums.3
  25.2 0.1 collective-permute-start.8
  25.4 5.9 %collective-permute-done.8 = s16[2,136,128]{2,1,0:T(8,128)(2,1)S(1)} collective-permute-done((s16[2,136,128]{2,1,0:T(8,128)(2,1)S(1)}, s16[2,136,128]{2,1,0:T(8,128)(2,1)S(1)}, u32[]{:S(2)}, u32[]{:S(2)}) %collective-permute-start.8) | collective-permute-done | bytes 69664 | tf_op jit(solution)/shard_map/ppermute | solution.py:324
  31.3 1.8 %collective-permute-start.10 = (bf16[16,3072]{1,0:T(8,128)(2,1)S(1)}, bf16[16,3072]{1,0:T(8,128)(2,1)S(1)}, u32[]{:S(2)}, u32[]{:S(2)}) collective-permute-start(bf16[16,3072]{1,0:T(8,128)(2,1)S(1)} %slice.14), channel_id=1, source_target_pairs={{0,4},{1,5},{2,6},{3,7},{4,0},{5,1},{6,2},{7,3},{8,12},{9,13},{10,... | collective-permute-start | bytes 294920 | tf_op jit(solution)/shard_map/ppermute | solution.py:324
  33.2 1.6 %collective-permute-start.11 = (bf16[16,3072]{1,0:T(8,128)(2,1)S(1)}, bf16[16,3072]{1,0:T(8,128)(2,1)S(1)}, u32[]{:S(2)}, u32[]{:S(2)}) collective-permute-start(bf16[16,3072]{1,0:T(8,128)(2,1)S(1)} %slice.15), channel_id=1, source_target_pairs={{0,2},{1,3},{2,0},{3,1},{4,6},{5,7},{6,4},{7,5},{8,10},{9,11},{10,... | collective-permute-start | bytes 294920 | tf_op jit(solution)/shard_map/ppermute | solution.py:324
  34.7 0.2 collective-permute-start.14
  35.0 1.5 %collective-permute-start.13 = (s16[2,136,128]{2,1,0:T(8,128)(2,1)S(1)}, s16[2,136,128]{2,1,0:T(8,128)(2,1)S(1)}, u32[]{:S(2)}, u32[]{:S(2)}) collective-permute-start(s16[2,136,128]{2,1,0:T(8,128)(2,1)S(1)} %add_sums.3), channel_id=1, source_target_pairs={{0,2},{1,3},{2,0},{3,1},{4,6},{5,7},{6,4},{7,5},{8,10},{9,11},{10,... | collective-permute-start | bytes 208904 | tf_op jit(solution)/shard_map/ppermute | solution.py:324
  36.5 2.0 %collective-permute-done.11.refs_4_ = bf16[16,3072]{1,0:T(8,128)(2,1)S(1)} collective-permute-done((bf16[16,3072]{1,0:T(8,128)(2,1)S(1)}, bf16[16,3072]{1,0:T(8,128)(2,1)S(1)}, u32[]{:S(2)}, u32[]{:S(2)}) %collective-permute-start.11) | collective-permute-done | bytes 98336 | tf_op jit(solution)/shard_map/ppermute | solution.py:324
  38.5 0.4 picked_rows.1.x_ref.x_own
  38.9 0.1 collective-permute-start.12
  39.0 1.0 %collective-permute-done.14 = s16[2,136,128]{2,1,0:T(8,128)(2,1)S(1)} collective-permute-done((s16[2,136,128]{2,1,0:T(8,128)(2,1)S(1)}, s16[2,136,128]{2,1,0:T(8,128)(2,1)S(1)}, u32[]{:S(2)}, u32[]{:S(2)}) %collective-permute-start.14) | collective-permute-done | bytes 69664 | tf_op jit(solution)/shard_map/ppermute | solution.py:324
  40.1 0.1 collective-permute-start.15
  40.2 2.1 %own_half_products.1 = (f32[96,640]{1,0:T(8,128)S(1)}, f32[128,96]{1,0:T(8,128)S(1)}, f32[32,4096]{1,0:T(8,128)S(1)}) custom-call(bf16[640,8192]{1,0:T(8,128)(2,1)S(1)} %get-tuple-element.25.feat_ref, s16[8,136,128]{2,1,0:T(8,128)(2,1)S(1)} %constant_dynamic-update-slice_fusion.2.code_ref, bf16[96,4096]{1,0:T(8,128)(2,1)S(1)} %picked_rows.1.x_ref.x_own), custom_call_target="tpu_custom_call" | custom-call | tf_op jit(solution)/shard_map/own_half_products/pallas_call | solution.py:418
  42.3 3.2 %pursuit.1 = (f32[3,640]{1,0:T(4,128)}, f32[32,8192]{1,0:T(8,128)}) custom-call(s32[640]{0:T(1024)S(1)} %copy-done.1, bf16[640,8192]{1,0:T(8,128)(2,1)S(1)} %get-tuple-element.25.feat_ref, bf16[96,4096]{1,0:T(8,128)(2,1)S(1)} %picked_rows.1.x_ref.x_own, bf16[96,4096]{1,0:T(8,128)(2,1)S(1)} %collective-permute-done.12.x_twin, ...), custom_call_target="tpu_custom_call" | custom-call | tf_op jit(solution)/shard_map/pursuit/pallas_call | solution.py:432
  (23 shorter events, 0.2 us)
Async XLA Ops:
  0.6 14.8 %copy-start = (s32[3,32]{1,0:T(4,128)S(1)}, s32[3,32]{1,0:T(4,128)}, u32[]{:S(2)}) copy-start(s32[3,32]{1,0:T(4,128)} %pick_ref.1) | copy-start | bytes 1156
  5.7 4.2 %collective-permute-start = (f32[264,512]{1,0:T(8,128)S(1)}, f32[264,512]{1,0:T(8,128)S(1)}, u32[]{:S(2)}, u32[]{:S(2)}) collective-permute-start(f32[264,512]{1,0:T(8,128)S(1)} %get-tuple-element.27), channel_id=1, source_target_pairs={{0,1},{1,0},{2,3},{3,2},{4,5},{5,4},{6,7},{7,6},{8,9},{9,8},{10,11... | collective-permute-start | bytes 1622024 | tf_op jit(solution)/shard_map/ppermute | solution.py:324
  6.2 9.2 %collective-permute-start.2 = (bf16[2,8,3072]{2,1,0:T(8,128)(2,1)S(1)}, bf16[2,8,3072]{2,1,0:T(8,128)(2,1)S(1)}, u32[]{:S(2)}, u32[]{:S(2)}) collective-permute-start(bf16[2,8,3072]{2,1,0:T(8,128)(2,1)S(1)} %pack_rows.1), channel_id=1, source_target_pairs={{0,8},{1,9},{2,10},{3,11},{4,12},{5,13},{6,14},{7,15},{8,0},{9,1},... | collective-permute-start | bytes 294920 | tf_op jit(solution)/shard_map/ppermute | solution.py:324
  10.1 5.7 %collective-permute-start.1 = (s16[2,136,128]{2,1,0:T(8,128)(2,1)S(1)}, s16[2,136,128]{2,1,0:T(8,128)(2,1)S(1)}, u32[]{:S(2)}, u32[]{:S(2)}) collective-permute-start(s16[2,136,128]{2,1,0:T(8,128)(2,1)S(1)} %get-tuple-element.29), channel_id=1, source_target_pairs={{0,4},{1,5},{2,6},{3,7},{4,0},{5,1},{6,2},{7,3},{8,12},{9,13},{10,... | collective-permute-start | bytes 208904 | tf_op jit(solution)/shard_map/ppermute | solution.py:324
  11.7 4.3 %collective-permute-start.3 = (s16[2,136,128]{2,1,0:T(8,128)(2,1)S(1)}, s16[2,136,128]{2,1,0:T(8,128)(2,1)S(1)}, u32[]{:S(2)}, u32[]{:S(2)}) collective-permute-start(s16[2,136,128]{2,1,0:T(8,128)(2,1)S(1)} %get-tuple-element.32), channel_id=1, source_target_pairs={{0,2},{1,3},{2,0},{3,1},{4,6},{5,7},{6,4},{7,5},{8,10},{9,11},{10,... | collective-permute-start | bytes 208904 | tf_op jit(solution)/shard_map/ppermute | solution.py:324
  13.3 5.2 %collective-permute-start.4 = (s16[2,136,128]{2,1,0:T(8,128)(2,1)S(1)}, s16[2,136,128]{2,1,0:T(8,128)(2,1)S(1)}, u32[]{:S(2)}, u32[]{:S(2)}) collective-permute-start(s16[2,136,128]{2,1,0:T(8,128)(2,1)S(1)} %get-tuple-element.33), channel_id=1, source_target_pairs={{0,6},{1,7},{2,4},{3,5},{4,2},{5,3},{6,0},{7,1},{8,14},{9,15},{10,... | collective-permute-start | bytes 208904 | tf_op jit(solution)/shard_map/ppermute | solution.py:324
  18.8 6.2 %collective-permute-start.7 = (s16[2,136,128]{2,1,0:T(8,128)(2,1)S(1)}, s16[2,136,128]{2,1,0:T(8,128)(2,1)S(1)}, u32[]{:S(2)}, u32[]{:S(2)}) collective-permute-start(s16[2,136,128]{2,1,0:T(8,128)(2,1)S(1)} %add_sums.2.refs_0_), channel_id=1, source_target_pairs={{0,8},{1,9},{2,10},{3,11},{4,12},{5,13},{6,14},{7,15},{8,0},{9,1},... | collective-permute-start | bytes 208904 | tf_op jit(solution)/shard_map/ppermute | solution.py:324
  21.0 1.4 %collective-permute-start.5 = (bf16[16,3072]{1,0:T(8,128)(2,1)S(1)}, bf16[16,3072]{1,0:T(8,128)(2,1)S(1)}, u32[]{:S(2)}, u32[]{:S(2)}) collective-permute-start(bf16[16,3072]{1,0:T(8,128)(2,1)S(1)} %get-tuple-element.38), channel_id=1, source_target_pairs={{0,1},{1,0},{2,3},{3,2},{4,5},{5,4},{6,7},{7,6},{8,9},{9,8},{10,11... | collective-permute-start | bytes 294920 | tf_op jit(solution)/shard_map/ppermute | solution.py:324
  22.3 9.0 %collective-permute-start.9 = (bf16[32,3072]{1,0:T(8,128)(2,1)S(1)}, bf16[32,3072]{1,0:T(8,128)(2,1)S(1)}, u32[]{:S(2)}, u32[]{:S(2)}) collective-permute-start(bf16[32,3072]{1,0:T(8,128)(2,1)S(1)} %constant_dynamic-update-slice_fusion.refs_0_), channel_id=1, source_target_pairs={{0,2},{1,3},{2,0},{3,1},{4,6},{5,7},{6,4},{7,5},{8,10},{9,11},{10,... | collective-permute-start | bytes 589832 | tf_op jit(solution)/shard_map/ppermute | solution.py:324
  23.0 10.2 %collective-permute-start.6 = (bf16[32,3072]{1,0:T(8,128)(2,1)S(1)}, bf16[32,3072]{1,0:T(8,128)(2,1)S(1)}, u32[]{:S(2)}, u32[]{:S(2)}) collective-permute-start(bf16[32,3072]{1,0:T(8,128)(2,1)S(1)} %constant_dynamic-update-slice_fusion.refs_0_), channel_id=1, source_target_pairs={{0,4},{1,5},{2,6},{3,7},{4,0},{5,1},{6,2},{7,3},{8,12},{9,13},{10,... | collective-permute-start | bytes 589832 | tf_op jit(solution)/shard_map/ppermute | solution.py:324
  25.2 17.0 %copy-start.1 = (s32[640]{0:T(1024)S(1)}, s32[640]{0:T(1024)}, u32[]{:S(2)}) copy-start(s32[640]{0:T(1024)} %labels_ref.1) | copy-start | bytes 7684
  25.2 6.1 %collective-permute-start.8 = (s16[2,136,128]{2,1,0:T(8,128)(2,1)S(1)}, s16[2,136,128]{2,1,0:T(8,128)(2,1)S(1)}, u32[]{:S(2)}, u32[]{:S(2)}) collective-permute-start(s16[2,136,128]{2,1,0:T(8,128)(2,1)S(1)} %add_sums.3), channel_id=1, source_target_pairs={{0,4},{1,5},{2,6},{3,7},{4,0},{5,1},{6,2},{7,3},{8,12},{9,13},{10,... | collective-permute-start | bytes 208904 | tf_op jit(solution)/shard_map/ppermute | solution.py:324
  31.3 5.2 %collective-permute-start.10 = (bf16[16,3072]{1,0:T(8,128)(2,1)S(1)}, bf16[16,3072]{1,0:T(8,128)(2,1)S(1)}, u32[]{:S(2)}, u32[]{:S(2)}) collective-permute-start(bf16[16,3072]{1,0:T(8,128)(2,1)S(1)} %slice.14), channel_id=1, source_target_pairs={{0,4},{1,5},{2,6},{3,7},{4,0},{5,1},{6,2},{7,3},{8,12},{9,13},{10,... | collective-permute-start | bytes 294920 | tf_op jit(solution)/shard_map/ppermute | solution.py:324
  33.2 5.3 %collective-permute-start.11 = (bf16[16,3072]{1,0:T(8,128)(2,1)S(1)}, bf16[16,3072]{1,0:T(8,128)(2,1)S(1)}, u32[]{:S(2)}, u32[]{:S(2)}) collective-permute-start(bf16[16,3072]{1,0:T(8,128)(2,1)S(1)} %slice.15), channel_id=1, source_target_pairs={{0,2},{1,3},{2,0},{3,1},{4,6},{5,7},{6,4},{7,5},{8,10},{9,11},{10,... | collective-permute-start | bytes 294920 | tf_op jit(solution)/shard_map/ppermute | solution.py:324
  34.7 5.3 %collective-permute-start.14 = (s16[2,136,128]{2,1,0:T(8,128)(2,1)S(1)}, s16[2,136,128]{2,1,0:T(8,128)(2,1)S(1)}, u32[]{:S(2)}, u32[]{:S(2)}) collective-permute-start(s16[2,136,128]{2,1,0:T(8,128)(2,1)S(1)} %add_sums.3), channel_id=1, source_target_pairs={{0,6},{1,7},{2,4},{3,5},{4,2},{5,3},{6,0},{7,1},{8,14},{9,15},{10,... | collective-permute-start | bytes 208904 | tf_op jit(solution)/shard_map/ppermute | solution.py:324
  35.0 5.1 %collective-permute-start.13 = (s16[2,136,128]{2,1,0:T(8,128)(2,1)S(1)}, s16[2,136,128]{2,1,0:T(8,128)(2,1)S(1)}, u32[]{:S(2)}, u32[]{:S(2)}) collective-permute-start(s16[2,136,128]{2,1,0:T(8,128)(2,1)S(1)} %add_sums.3), channel_id=1, source_target_pairs={{0,2},{1,3},{2,0},{3,1},{4,6},{5,7},{6,4},{7,5},{8,10},{9,11},{10,... | collective-permute-start | bytes 208904 | tf_op jit(solution)/shard_map/ppermute | solution.py:324
  38.9 3.4 %collective-permute-start.12 = (bf16[96,4096]{1,0:T(8,128)(2,1)S(1)}, bf16[96,4096]{1,0:T(8,128)(2,1)S(1)}, u32[]{:S(2)}, u32[]{:S(2)}) collective-permute-start(bf16[96,4096]{1,0:T(8,128)(2,1)S(1)} %picked_rows.1.x_ref.x_own), channel_id=1, source_target_pairs={{0,1},{1,0},{2,3},{3,2},{4,5},{5,4},{6,7},{7,6},{8,9},{9,8},{10,11... | collective-permute-start | bytes 2359304 | tf_op jit(solution)/shard_map/ppermute | solution.py:324
  40.1 2.1 %collective-permute-start.15 = (s16[8,136,128]{2,1,0:T(8,128)(2,1)S(1)}, s16[8,136,128]{2,1,0:T(8,128)(2,1)S(1)}, u32[]{:S(2)}, u32[]{:S(2)}) collective-permute-start(s16[8,136,128]{2,1,0:T(8,128)(2,1)S(1)} %constant_dynamic-update-slice_fusion.2.code_ref), channel_id=1, source_target_pairs={{0,1},{1,0},{2,3},{3,2},{4,5},{5,4},{6,7},{7,6},{8,9},{9,8},{10,11... | collective-permute-start | bytes 835592 | tf_op jit(solution)/shard_map/ppermute | solution.py:324

commit v16 on v15

--- a/solution.py
+++ b/solution.py
@@ -216,7 +216,9 @@
     for b in range(3, bits):
         far = far + (((away >> b) & 1) << (bits - 1 - b))
     near = ((away >> 2) & 1) + 2 * ((away >> 1) & 1)
-    spot = (2 * near + (away & 1)) * (n_ex // 8) + far
+    side = away & 1
+    others = n_ex // 8 - 1
+    spot = 2 * near * (others + 1) + jnp.where(far == 0, side, 1 + side * others + far)
     step = lax.broadcasted_iota(jnp.int32, pick.shape, 0)
     line = lax.broadcasted_iota(jnp.int32, (lines, classes), 0)
     where = spot * 8 + (slots * steps + rank if tail else rank * steps + step)
@@ -348,7 +350,7 @@
             out_specs=vmem,
             out_shape=code,
             compiler_params=limit,
-            cost_estimate=pl.CostEstimate(flops=10**10, bytes_accessed=10**8, transcendentals=0) if last else None,
+            cost_estimate=pl.CostEstimate(flops=10**10, bytes_accessed=10**8, transcendentals=0),
             name="add_sums",
         )(*codes)
 
@@ -374,7 +376,8 @@
         packed = jnp.concatenate([packed, swap(packed, mask)], axis=1)
 
     near_codes = [swap(c, m) for c, m in zip(codes[1:], near_masks[1:])]
-    part_sum = add([codes[0], after(near_codes[0], packed)] + near_codes[1:], False)
+    given = swap(after(packed[1], *near_codes), 1)
+    part_sum = add([codes[0]] + near_codes, False)
 
     def select(tail, *others):
         return pl.pallas_call(
@@ -387,23 +390,22 @@
         )(after(pick_index, *others))
 
     rest = select(True, codes[0])
-    near_sum = after(part_sum, rest)
+    near_sum = after(part_sum, rest, given)
     more = swap(near_sum, far_masks[0])
     one = select(False, near_sum)
+    here = jnp.concatenate([packed[0][:8], after(given, near_sum)[:8]], axis=0)
+    there = jnp.concatenate([packed[0][8:], after(given, more)[8:]], axis=0)
     part_sum = add([near_sum, more], len(far_masks) == 1)
     for mask in far_masks[1:]:
         part_sum = add([part_sum, swap(part_sum, mask)], mask == far_masks[-1])
-    given = swap(after(packed[1], near_sum), 1)
-    near = jnp.concatenate([after(packed[0], one), given], axis=0)
-    by_z, by_y = swap(near, 4), swap(near, 2)
+    parts = [here, there]
+    for m in near_masks[1:]:
+        parts += [swap(here, m), swap(there, m)]
     own_parts = [part_sum] + [swap(part_sum, m) for m in near_masks[1:]]
-    by_z, by_y = after(by_z, own_parts[1]), after(by_y, own_parts[1])
-    cut = near.shape[0] // 2
-    parts = [near, by_z, by_y, swap(by_y[:cut], 4), swap(by_z[cut:], 2)]
 
     x = pl.pallas_call(
         functools.partial(picked_kernel, steps=steps),
-        in_specs=[vmem] * 7,
+        in_specs=[vmem] * (2 + len(parts)),
         out_specs=vmem,
         out_shape=jax.ShapeDtypeStruct((total, full // 2), bf16),
         scratch_shapes=[pltpu.VMEM((n_ex * 8, main), bf16)],

time: 45.7 us -> 48 us (1.050)
  starting transfers between devices: 17.7 us -> 20 us
    ppermute x16 -> x18, starting transfers between devices: 17.7 us -> 20 us  [swap(): return lax.ppermute(x, 'ex', [(d, d ^ mask) for d in range(n_ex)])]
    ppermute x16 -> x18, waiting for transfers between devices: 14.7 us -> 14.7 us  [swap(): return lax.ppermute(x, 'ex', [(d, d ^ mask) for d in range(n_ex)])]
  transfers between devices with their start and end apart: 16 -> 18, of which waited for: 7 -> 12; matrix products, arithmetic and copies ran while one was open for 0% -> 0% of each run, Pallas kernels for 8% -> 8%
where the time goes in v16:
time: 48 us; the launch traced here: 47.8 us
  starting transfers between devices  20 us (42%)
  waiting for transfers between devices  14.7 us (31%)
  Pallas kernels  12.1 us (25%)
  between operations  0.81 us (2%)
    ppermute x18, starting transfers between devices, swap(): return lax.ppermute(x, 'ex', [(d, d ^ mask) for d in range(n_ex)])  20 us
    ppermute x18, waiting for transfers between devices, swap(): return lax.ppermute(x, 'ex', [(d, d ^ mask) for d in range(n_ex)])  14.7 us
    pallas_call x1, Pallas kernels, on_device(): pl.pallas_call(functools.partial(sums_kernel, n_ex=n_ex), in_specs=[hbm]...  5.02 us
    pallas_call x1, Pallas kernels, on_device(): pl.pallas_call(functools.partial(pursuit_kernel, steps=steps, scale=1.0 /...  3.19 us
    pallas_call x1, Pallas kernels, on_device(): pl.pallas_call(functools.partial(half_kernel, classes=classes), in_specs=...  2.06 us
  transfers between devices with their start and end apart: 18, of which 12 were waited for; matrix products, arithmetic and copies ran while one was open for 0% of the time, Pallas kernels for 8%

profile of v16, /device:TPU:0, one launch (start us, length us, event | category | flops | bytes accessed | tf_op | source)
XLA Modules:
  0.0 47.8 jit_solution(7096164714705106049)
XLA Ops:
  0.6 5.0 %class_sums.1 = (bf16[640,8192]{1,0:T(8,128)(2,1)S(1)}, f32[264,512]{1,0:T(8,128)S(1)}, f32[264,512]{1,0:T(8,128)S(1)}, f32[8,8192]{1,0:T(8,128)S(1)}) custom-call(s32[640]{0:T(1024)} %labels_ref.1, s32[3,32]{1,0:T(4,128)} %pick_ref.1, bf16[640,8192]{1,0:T(8,128)(2,1)} %feat_hbm.1), custom_call_target="tpu_custom_call" | custom-call | tf_op jit(solution)/shard_map/class_sums/pallas_call | solution.py:331
  5.7 4.1 %collective-permute-start.4 = (bf16[2,8,3072]{2,1,0:T(8,128)(2,1)S(1)}, bf16[2,8,3072]{2,1,0:T(8,128)(2,1)S(1)}, u32[]{:S(2)}, u32[]{:S(2)}) collective-permute-start(bf16[2,8,3072]{2,1,0:T(8,128)(2,1)S(1)} %pack_rows.1), channel_id=1, source_target_pairs={{0,8},{1,9},{2,10},{3,11},{4,12},{5,13},{6,14},{7,15},{8,0},{9,1},... | collective-permute-start | bytes 294920 | tf_op jit(solution)/shard_map/ppermute | solution.py:326
  9.8 4.9 %collective-permute-done.4 = bf16[2,8,3072]{2,1,0:T(8,128)(2,1)S(1)} collective-permute-done((bf16[2,8,3072]{2,1,0:T(8,128)(2,1)S(1)}, bf16[2,8,3072]{2,1,0:T(8,128)(2,1)S(1)}, u32[]{:S(2)}, u32[]{:S(2)}) %collective-permute-start.4) | collective-permute-done | bytes 98336 | tf_op jit(solution)/shard_map/ppermute | solution.py:326
  14.9 0.8 %collective-permute-start.1 = (s16[2,136,128]{2,1,0:T(8,128)(2,1)S(1)}, s16[2,136,128]{2,1,0:T(8,128)(2,1)S(1)}, u32[]{:S(2)}, u32[]{:S(2)}) collective-permute-start(s16[2,136,128]{2,1,0:T(8,128)(2,1)S(1)} %get-tuple-element.27), channel_id=1, source_target_pairs={{0,4},{1,5},{2,6},{3,7},{4,0},{5,1},{6,2},{7,3},{8,12},{9,13},{10,... | collective-permute-start | bytes 208904 | tf_op jit(solution)/shard_map/ppermute | solution.py:326
  15.7 1.5 %collective-permute-start.2 = (s16[2,136,128]{2,1,0:T(8,128)(2,1)S(1)}, s16[2,136,128]{2,1,0:T(8,128)(2,1)S(1)}, u32[]{:S(2)}, u32[]{:S(2)}) collective-permute-start(s16[2,136,128]{2,1,0:T(8,128)(2,1)S(1)} %get-tuple-element.28), channel_id=1, source_target_pairs={{0,2},{1,3},{2,0},{3,1},{4,6},{5,7},{6,4},{7,5},{8,10},{9,11},{10,... | collective-permute-start | bytes 208904 | tf_op jit(solution)/shard_map/ppermute | solution.py:326
  17.2 1.3 %collective-permute-start.3 = (s16[2,136,128]{2,1,0:T(8,128)(2,1)S(1)}, s16[2,136,128]{2,1,0:T(8,128)(2,1)S(1)}, u32[]{:S(2)}, u32[]{:S(2)}) collective-permute-start(s16[2,136,128]{2,1,0:T(8,128)(2,1)S(1)} %get-tuple-element.29), channel_id=1, source_target_pairs={{0,6},{1,7},{2,4},{3,5},{4,2},{5,3},{6,0},{7,1},{8,14},{9,15},{10,... | collective-permute-start | bytes 208904 | tf_op jit(solution)/shard_map/ppermute | solution.py:326
  18.5 0.3 select_tails.1.rest_ref
  18.9 0.6 %collective-permute-done.1.refs_1_ = s16[2,136,128]{2,1,0:T(8,128)(2,1)S(1)} collective-permute-done((s16[2,136,128]{2,1,0:T(8,128)(2,1)S(1)}, s16[2,136,128]{2,1,0:T(8,128)(2,1)S(1)}, u32[]{:S(2)}, u32[]{:S(2)}) %collective-permute-start.1) | collective-permute-done | bytes 69664 | tf_op jit(solution)/shard_map/ppermute | solution.py:326
  19.5 0.6 %collective-permute-done.2.refs_2_ = s16[2,136,128]{2,1,0:T(8,128)(2,1)S(1)} collective-permute-done((s16[2,136,128]{2,1,0:T(8,128)(2,1)S(1)}, s16[2,136,128]{2,1,0:T(8,128)(2,1)S(1)}, u32[]{:S(2)}, u32[]{:S(2)}) %collective-permute-start.2) | collective-permute-done | bytes 69664 | tf_op jit(solution)/shard_map/ppermute | solution.py:326
  20.0 2.4 %collective-permute-done.3.refs_3_ = s16[2,136,128]{2,1,0:T(8,128)(2,1)S(1)} collective-permute-done((s16[2,136,128]{2,1,0:T(8,128)(2,1)S(1)}, s16[2,136,128]{2,1,0:T(8,128)(2,1)S(1)}, u32[]{:S(2)}, u32[]{:S(2)}) %collective-permute-start.3) | collective-permute-done | bytes 69664 | tf_op jit(solution)/shard_map/ppermute | solution.py:326
  22.4 0.3 add_sums.2.refs_0_
  22.7 1.0 %collective-permute-done.5 = bf16[16,3072]{1,0:T(8,128)(2,1)S(1)} collective-permute-done((bf16[16,3072]{1,0:T(8,128)(2,1)S(1)}, bf16[16,3072]{1,0:T(8,128)(2,1)S(1)}, u32[]{:S(2)}, u32[]{:S(2)}) %collective-permute-start.5) | collective-permute-done | bytes 98336 | tf_op jit(solution)/shard_map/ppermute | solution.py:326
  23.7 3.4 %collective-permute-start.6 = (s16[2,136,128]{2,1,0:T(8,128)(2,1)S(1)}, s16[2,136,128]{2,1,0:T(8,128)(2,1)S(1)}, u32[]{:S(2)}, u32[]{:S(2)}) collective-permute-start(s16[2,136,128]{2,1,0:T(8,128)(2,1)S(1)} %add_sums.2.refs_0_), channel_id=1, source_target_pairs={{0,8},{1,9},{2,10},{3,11},{4,12},{5,13},{6,14},{7,15},{8,0},{9,1},... | collective-permute-start | bytes 208904 | tf_op jit(solution)/shard_map/ppermute | solution.py:326
  27.3 1.4 %collective-permute-start.9 = (bf16[16,3072]{1,0:T(8,128)(2,1)S(1)}, bf16[16,3072]{1,0:T(8,128)(2,1)S(1)}, u32[]{:S(2)}, u32[]{:S(2)}) collective-permute-start(bf16[16,3072]{1,0:T(8,128)(2,1)S(1)} %pad_maximum_fusion.1.refs_0_), channel_id=1, source_target_pairs={{0,2},{1,3},{2,0},{3,1},{4,6},{5,7},{6,4},{7,5},{8,10},{9,11},{10,... | collective-permute-start | bytes 294920 | tf_op jit(solution)/shard_map/ppermute | solution.py:326
  28.8 1.9 %collective-permute-start.7 = (bf16[16,3072]{1,0:T(8,128)(2,1)S(1)}, bf16[16,3072]{1,0:T(8,128)(2,1)S(1)}, u32[]{:S(2)}, u32[]{:S(2)}) collective-permute-start(bf16[16,3072]{1,0:T(8,128)(2,1)S(1)} %pad_maximum_fusion.1.refs_0_), channel_id=1, source_target_pairs={{0,4},{1,5},{2,6},{3,7},{4,0},{5,1},{6,2},{7,3},{8,12},{9,13},{10,... | collective-permute-start | bytes 294920 | tf_op jit(solution)/shard_map/ppermute | solution.py:326
  30.7 0.5 %collective-permute-done.6.refs_1_ = s16[2,136,128]{2,1,0:T(8,128)(2,1)S(1)} collective-permute-done((s16[2,136,128]{2,1,0:T(8,128)(2,1)S(1)}, s16[2,136,128]{2,1,0:T(8,128)(2,1)S(1)}, u32[]{:S(2)}, u32[]{:S(2)}) %collective-permute-start.6) | collective-permute-done | bytes 69664 | tf_op jit(solution)/shard_map/ppermute | solution.py:326
  31.3 1.0 %collective-permute-start.10 = (bf16[16,3072]{1,0:T(8,128)(2,1)S(1)}, bf16[16,3072]{1,0:T(8,128)(2,1)S(1)}, u32[]{:S(2)}, u32[]{:S(2)}) collective-permute-start(bf16[16,3072]{1,0:T(8,128)(2,1)S(1)} %pad_maximum_fusion.2.refs_1_), channel_id=1, source_target_pairs={{0,2},{1,3},{2,0},{3,1},{4,6},{5,7},{6,4},{7,5},{8,10},{9,11},{10,... | collective-permute-start | bytes 294920 | tf_op jit(solution)/shard_map/ppermute | solution.py:326
  32.3 1.5 %collective-permute-done.11.refs_6_ = bf16[16,3072]{1,0:T(8,128)(2,1)S(1)} collective-permute-done((bf16[16,3072]{1,0:T(8,128)(2,1)S(1)}, bf16[16,3072]{1,0:T(8,128)(2,1)S(1)}, u32[]{:S(2)}, u32[]{:S(2)}) %collective-permute-start.11) | collective-permute-done | bytes 98336 | tf_op jit(solution)/shard_map/ppermute | solution.py:326
  33.9 1.0 %collective-permute-start.8 = (bf16[16,3072]{1,0:T(8,128)(2,1)S(1)}, bf16[16,3072]{1,0:T(8,128)(2,1)S(1)}, u32[]{:S(2)}, u32[]{:S(2)}) collective-permute-start(bf16[16,3072]{1,0:T(8,128)(2,1)S(1)} %pad_maximum_fusion.2.refs_1_), channel_id=1, source_target_pairs={{0,4},{1,5},{2,6},{3,7},{4,0},{5,1},{6,2},{7,3},{8,12},{9,13},{10,... | collective-permute-start | bytes 294920 | tf_op jit(solution)/shard_map/ppermute | solution.py:326
  34.8 0.3 add_sums.3
  35.1 1.6 %collective-permute-start.16 = (s16[2,136,128]{2,1,0:T(8,128)(2,1)S(1)}, s16[2,136,128]{2,1,0:T(8,128)(2,1)S(1)}, u32[]{:S(2)}, u32[]{:S(2)}) collective-permute-start(s16[2,136,128]{2,1,0:T(8,128)(2,1)S(1)} %add_sums.3), channel_id=1, source_target_pairs={{0,6},{1,7},{2,4},{3,5},{4,2},{5,3},{6,0},{7,1},{8,14},{9,15},{10,... | collective-permute-start | bytes 208904 | tf_op jit(solution)/shard_map/ppermute | solution.py:326
  36.7 1.0 %collective-permute-start.15 = (s16[2,136,128]{2,1,0:T(8,128)(2,1)S(1)}, s16[2,136,128]{2,1,0:T(8,128)(2,1)S(1)}, u32[]{:S(2)}, u32[]{:S(2)}) collective-permute-start(s16[2,136,128]{2,1,0:T(8,128)(2,1)S(1)} %add_sums.3), channel_id=1, source_target_pairs={{0,2},{1,3},{2,0},{3,1},{4,6},{5,7},{6,4},{7,5},{8,10},{9,11},{10,... | collective-permute-start | bytes 208904 | tf_op jit(solution)/shard_map/ppermute | solution.py:326
  37.7 0.3 collective-permute-done.12.refs_7_
  38.1 0.6 %collective-permute-start.14 = (s16[2,136,128]{2,1,0:T(8,128)(2,1)S(1)}, s16[2,136,128]{2,1,0:T(8,128)(2,1)S(1)}, u32[]{:S(2)}, u32[]{:S(2)}) collective-permute-start(s16[2,136,128]{2,1,0:T(8,128)(2,1)S(1)} %add_sums.3), channel_id=1, source_target_pairs={{0,4},{1,5},{2,6},{3,7},{4,0},{5,1},{6,2},{7,3},{8,12},{9,13},{10,... | collective-permute-start | bytes 208904 | tf_op jit(solution)/shard_map/ppermute | solution.py:326
  38.7 0.3 select_rows.1.one_ref
  39.0 0.7 %collective-permute-done.8.refs_3_ = bf16[16,3072]{1,0:T(8,128)(2,1)S(1)} collective-permute-done((bf16[16,3072]{1,0:T(8,128)(2,1)S(1)}, bf16[16,3072]{1,0:T(8,128)(2,1)S(1)}, u32[]{:S(2)}, u32[]{:S(2)}) %collective-permute-start.8) | collective-permute-done | bytes 98336 | tf_op jit(solution)/shard_map/ppermute | solution.py:326
  39.8 0.4 picked_rows.1.x_ref.x_own
  40.2 1.3 %collective-permute-done.16 = s16[2,136,128]{2,1,0:T(8,128)(2,1)S(1)} collective-permute-done((s16[2,136,128]{2,1,0:T(8,128)(2,1)S(1)}, s16[2,136,128]{2,1,0:T(8,128)(2,1)S(1)}, u32[]{:S(2)}, u32[]{:S(2)}) %collective-permute-start.16) | collective-permute-done | bytes 69664 | tf_op jit(solution)/shard_map/ppermute | solution.py:326
  41.5 0.3 collective-permute-done.15
  41.8 0.6 %collective-permute-done.14 = s16[2,136,128]{2,1,0:T(8,128)(2,1)S(1)} collective-permute-done((s16[2,136,128]{2,1,0:T(8,128)(2,1)S(1)}, s16[2,136,128]{2,1,0:T(8,128)(2,1)S(1)}, u32[]{:S(2)}, u32[]{:S(2)}) %collective-permute-start.14) | collective-permute-done | bytes 69664 | tf_op jit(solution)/shard_map/ppermute | solution.py:326
  42.5 2.1 %own_half_products.1 = (f32[96,640]{1,0:T(8,128)S(1)}, f32[128,96]{1,0:T(8,128)S(1)}, f32[32,4096]{1,0:T(8,128)S(1)}) custom-call(bf16[640,8192]{1,0:T(8,128)(2,1)S(1)} %get-tuple-element.23.feat_ref, s16[8,136,128]{2,1,0:T(8,128)(2,1)S(1)} %constant_dynamic-update-slice_fusion.code_ref, bf16[96,4096]{1,0:T(8,128)(2,1)S(1)} %picked_rows.1.x_ref.x_own), custom_call_target="tpu_custom_call" | custom-call | tf_op jit(solution)/shard_map/own_half_products/pallas_call | solution.py:420
  44.6 3.2 %pursuit.1 = (f32[3,640]{1,0:T(4,128)}, f32[32,8192]{1,0:T(8,128)}) custom-call(s32[640]{0:T(1024)S(1)} %copy-done.1, bf16[640,8192]{1,0:T(8,128)(2,1)S(1)} %get-tuple-element.23.feat_ref, bf16[96,4096]{1,0:T(8,128)(2,1)S(1)} %picked_rows.1.x_ref.x_own, bf16[96,4096]{1,0:T(8,128)(2,1)S(1)} %collective-permute-done.13.x_twin, ...), custom_call_target="tpu_custom_call" | custom-call | tf_op jit(solution)/shard_map/pursuit/pallas_call | solution.py:434
  (29 shorter events, 0.8 us)
Async XLA Ops:
  0.6 17.9 %copy-start = (s32[3,32]{1,0:T(4,128)S(1)}, s32[3,32]{1,0:T(4,128)}, u32[]{:S(2)}) copy-start(s32[3,32]{1,0:T(4,128)} %pick_ref.1) | copy-start | bytes 1156
  5.7 9.0 %collective-permute-start.4 = (bf16[2,8,3072]{2,1,0:T(8,128)(2,1)S(1)}, bf16[2,8,3072]{2,1,0:T(8,128)(2,1)S(1)}, u32[]{:S(2)}, u32[]{:S(2)}) collective-permute-start(bf16[2,8,3072]{2,1,0:T(8,128)(2,1)S(1)} %pack_rows.1), channel_id=1, source_target_pairs={{0,8},{1,9},{2,10},{3,11},{4,12},{5,13},{6,14},{7,15},{8,0},{9,1},... | collective-permute-start | bytes 294920 | tf_op jit(solution)/shard_map/ppermute | solution.py:326
  9.8 4.9 %collective-permute-start = (f32[264,512]{1,0:T(8,128)S(1)}, f32[264,512]{1,0:T(8,128)S(1)}, u32[]{:S(2)}, u32[]{:S(2)}) collective-permute-start(f32[264,512]{1,0:T(8,128)S(1)} %get-tuple-element.25), channel_id=1, source_target_pairs={{0,1},{1,0},{2,3},{3,2},{4,5},{5,4},{6,7},{7,6},{8,9},{9,8},{10,11... | collective-permute-start | bytes 1622024 | tf_op jit(solution)/shard_map/ppermute | solution.py:326
  14.9 4.5 %collective-permute-start.1 = (s16[2,136,128]{2,1,0:T(8,128)(2,1)S(1)}, s16[2,136,128]{2,1,0:T(8,128)(2,1)S(1)}, u32[]{:S(2)}, u32[]{:S(2)}) collective-permute-start(s16[2,136,128]{2,1,0:T(8,128)(2,1)S(1)} %get-tuple-element.27), channel_id=1, source_target_pairs={{0,4},{1,5},{2,6},{3,7},{4,0},{5,1},{6,2},{7,3},{8,12},{9,13},{10,... | collective-permute-start | bytes 208904 | tf_op jit(solution)/shard_map/ppermute | solution.py:326
  15.7 4.3 %collective-permute-start.2 = (s16[2,136,128]{2,1,0:T(8,128)(2,1)S(1)}, s16[2,136,128]{2,1,0:T(8,128)(2,1)S(1)}, u32[]{:S(2)}, u32[]{:S(2)}) collective-permute-start(s16[2,136,128]{2,1,0:T(8,128)(2,1)S(1)} %get-tuple-element.28), channel_id=1, source_target_pairs={{0,2},{1,3},{2,0},{3,1},{4,6},{5,7},{6,4},{7,5},{8,10},{9,11},{10,... | collective-permute-start | bytes 208904 | tf_op jit(solution)/shard_map/ppermute | solution.py:326
  17.2 5.2 %collective-permute-start.3 = (s16[2,136,128]{2,1,0:T(8,128)(2,1)S(1)}, s16[2,136,128]{2,1,0:T(8,128)(2,1)S(1)}, u32[]{:S(2)}, u32[]{:S(2)}) collective-permute-start(s16[2,136,128]{2,1,0:T(8,128)(2,1)S(1)} %get-tuple-element.29), channel_id=1, source_target_pairs={{0,6},{1,7},{2,4},{3,5},{4,2},{5,3},{6,0},{7,1},{8,14},{9,15},{10,... | collective-permute-start | bytes 208904 | tf_op jit(solution)/shard_map/ppermute | solution.py:326
  22.4 1.3 %collective-permute-start.5 = (bf16[16,3072]{1,0:T(8,128)(2,1)S(1)}, bf16[16,3072]{1,0:T(8,128)(2,1)S(1)}, u32[]{:S(2)}, u32[]{:S(2)}) collective-permute-start(bf16[16,3072]{1,0:T(8,128)(2,1)S(1)} %fusion), channel_id=1, source_target_pairs={{0,1},{1,0},{2,3},{3,2},{4,5},{5,4},{6,7},{7,6},{8,9},{9,8},{10,11... | collective-permute-start | bytes 294920 | tf_op jit(solution)/shard_map/ppermute | solution.py:326
  23.7 7.5 %collective-permute-start.6 = (s16[2,136,128]{2,1,0:T(8,128)(2,1)S(1)}, s16[2,136,128]{2,1,0:T(8,128)(2,1)S(1)}, u32[]{:S(2)}, u32[]{:S(2)}) collective-permute-start(s16[2,136,128]{2,1,0:T(8,128)(2,1)S(1)} %add_sums.2.refs_0_), channel_id=1, source_target_pairs={{0,8},{1,9},{2,10},{3,11},{4,12},{5,13},{6,14},{7,15},{8,0},{9,1},... | collective-permute-start | bytes 208904 | tf_op jit(solution)/shard_map/ppermute | solution.py:326
  27.2 6.7 %collective-permute-start.11 = (bf16[16,3072]{1,0:T(8,128)(2,1)S(1)}, bf16[16,3072]{1,0:T(8,128)(2,1)S(1)}, u32[]{:S(2)}, u32[]{:S(2)}) collective-permute-start(bf16[16,3072]{1,0:T(8,128)(2,1)S(1)} %pad_maximum_fusion.1.refs_0_), channel_id=1, source_target_pairs={{0,6},{1,7},{2,4},{3,5},{4,2},{5,3},{6,0},{7,1},{8,14},{9,15},{10,... | collective-permute-start | bytes 294920 | tf_op jit(solution)/shard_map/ppermute | solution.py:326
  27.3 7.8 %collective-permute-start.9 = (bf16[16,3072]{1,0:T(8,128)(2,1)S(1)}, bf16[16,3072]{1,0:T(8,128)(2,1)S(1)}, u32[]{:S(2)}, u32[]{:S(2)}) collective-permute-start(bf16[16,3072]{1,0:T(8,128)(2,1)S(1)} %pad_maximum_fusion.1.refs_0_), channel_id=1, source_target_pairs={{0,2},{1,3},{2,0},{3,1},{4,6},{5,7},{6,4},{7,5},{8,10},{9,11},{10,... | collective-permute-start | bytes 294920 | tf_op jit(solution)/shard_map/ppermute | solution.py:326
  28.8 7.9 %collective-permute-start.7 = (bf16[16,3072]{1,0:T(8,128)(2,1)S(1)}, bf16[16,3072]{1,0:T(8,128)(2,1)S(1)}, u32[]{:S(2)}, u32[]{:S(2)}) collective-permute-start(bf16[16,3072]{1,0:T(8,128)(2,1)S(1)} %pad_maximum_fusion.1.refs_0_), channel_id=1, source_target_pairs={{0,4},{1,5},{2,6},{3,7},{4,0},{5,1},{6,2},{7,3},{8,12},{9,13},{10,... | collective-permute-start | bytes 294920 | tf_op jit(solution)/shard_map/ppermute | solution.py:326
  31.3 6.8 %collective-permute-start.12 = (bf16[16,3072]{1,0:T(8,128)(2,1)S(1)}, bf16[16,3072]{1,0:T(8,128)(2,1)S(1)}, u32[]{:S(2)}, u32[]{:S(2)}) collective-permute-start(bf16[16,3072]{1,0:T(8,128)(2,1)S(1)} %pad_maximum_fusion.2.refs_1_), channel_id=1, source_target_pairs={{0,6},{1,7},{2,4},{3,5},{4,2},{5,3},{6,0},{7,1},{8,14},{9,15},{10,... | collective-permute-start | bytes 294920 | tf_op jit(solution)/shard_map/ppermute | solution.py:326
  31.3 7.7 %collective-permute-start.10 = (bf16[16,3072]{1,0:T(8,128)(2,1)S(1)}, bf16[16,3072]{1,0:T(8,128)(2,1)S(1)}, u32[]{:S(2)}, u32[]{:S(2)}) collective-permute-start(bf16[16,3072]{1,0:T(8,128)(2,1)S(1)} %pad_maximum_fusion.2.refs_1_), channel_id=1, source_target_pairs={{0,2},{1,3},{2,0},{3,1},{4,6},{5,7},{6,4},{7,5},{8,10},{9,11},{10,... | collective-permute-start | bytes 294920 | tf_op jit(solution)/shard_map/ppermute | solution.py:326
  33.9 5.9 %collective-permute-start.8 = (bf16[16,3072]{1,0:T(8,128)(2,1)S(1)}, bf16[16,3072]{1,0:T(8,128)(2,1)S(1)}, u32[]{:S(2)}, u32[]{:S(2)}) collective-permute-start(bf16[16,3072]{1,0:T(8,128)(2,1)S(1)} %pad_maximum_fusion.2.refs_1_), channel_id=1, source_target_pairs={{0,4},{1,5},{2,6},{3,7},{4,0},{5,1},{6,2},{7,3},{8,12},{9,13},{10,... | collective-permute-start | bytes 294920 | tf_op jit(solution)/shard_map/ppermute | solution.py:326
  35.1 9.5 %copy-start.1 = (s32[640]{0:T(1024)S(1)}, s32[640]{0:T(1024)}, u32[]{:S(2)}) copy-start(s32[640]{0:T(1024)} %labels_ref.1) | copy-start | bytes 7684
  35.1 6.4 %collective-permute-start.16 = (s16[2,136,128]{2,1,0:T(8,128)(2,1)S(1)}, s16[2,136,128]{2,1,0:T(8,128)(2,1)S(1)}, u32[]{:S(2)}, u32[]{:S(2)}) collective-permute-start(s16[2,136,128]{2,1,0:T(8,128)(2,1)S(1)} %add_sums.3), channel_id=1, source_target_pairs={{0,6},{1,7},{2,4},{3,5},{4,2},{5,3},{6,0},{7,1},{8,14},{9,15},{10,... | collective-permute-start | bytes 208904 | tf_op jit(solution)/shard_map/ppermute | solution.py:326
  36.7 5.1 %collective-permute-start.15 = (s16[2,136,128]{2,1,0:T(8,128)(2,1)S(1)}, s16[2,136,128]{2,1,0:T(8,128)(2,1)S(1)}, u32[]{:S(2)}, u32[]{:S(2)}) collective-permute-start(s16[2,136,128]{2,1,0:T(8,128)(2,1)S(1)} %add_sums.3), channel_id=1, source_target_pairs={{0,2},{1,3},{2,0},{3,1},{4,6},{5,7},{6,4},{7,5},{8,10},{9,11},{10,... | collective-permute-start | bytes 208904 | tf_op jit(solution)/shard_map/ppermute | solution.py:326
  38.1 4.3 %collective-permute-start.14 = (s16[2,136,128]{2,1,0:T(8,128)(2,1)S(1)}, s16[2,136,128]{2,1,0:T(8,128)(2,1)S(1)}, u32[]{:S(2)}, u32[]{:S(2)}) collective-permute-start(s16[2,136,128]{2,1,0:T(8,128)(2,1)S(1)} %add_sums.3), channel_id=1, source_target_pairs={{0,4},{1,5},{2,6},{3,7},{4,0},{5,1},{6,2},{7,3},{8,12},{9,13},{10,... | collective-permute-start | bytes 208904 | tf_op jit(solution)/shard_map/ppermute | solution.py:326
  40.2 4.4 %collective-permute-start.13 = (bf16[96,4096]{1,0:T(8,128)(2,1)S(1)}, bf16[96,4096]{1,0:T(8,128)(2,1)S(1)}, u32[]{:S(2)}, u32[]{:S(2)}) collective-permute-start(bf16[96,4096]{1,0:T(8,128)(2,1)S(1)} %picked_rows.1.x_ref.x_own), channel_id=1, source_target_pairs={{0,1},{1,0},{2,3},{3,2},{4,5},{5,4},{6,7},{7,6},{8,9},{9,8},{10,11... | collective-permute-start | bytes 2359304 | tf_op jit(solution)/shard_map/ppermute | solution.py:326
  42.4 2.1 %collective-permute-start.17 = (s16[8,136,128]{2,1,0:T(8,128)(2,1)S(1)}, s16[8,136,128]{2,1,0:T(8,128)(2,1)S(1)}, u32[]{:S(2)}, u32[]{:S(2)}) collective-permute-start(s16[8,136,128]{2,1,0:T(8,128)(2,1)S(1)} %constant_dynamic-update-slice_fusion.code_ref), channel_id=1, source_target_pairs={{0,1},{1,0},{2,3},{3,2},{4,5},{5,4},{6,7},{7,6},{8,9},{9,8},{10,11... | collective-permute-start | bytes 835592 | tf_op jit(solution)/shard_map/ppermute | solution.py:326

commit v17 on v15

--- a/solution.py
+++ b/solution.py
@@ -397,7 +397,7 @@
     near = jnp.concatenate([after(packed[0], one), given], axis=0)
     by_z, by_y = swap(near, 4), swap(near, 2)
     own_parts = [part_sum] + [swap(part_sum, m) for m in near_masks[1:]]
-    by_z, by_y = after(by_z, own_parts[1]), after(by_y, own_parts[1])
+    by_z, by_y = after(by_z, part_sum), after(by_y, part_sum)
     cut = near.shape[0] // 2
     parts = [near, by_z, by_y, swap(by_y[:cut], 4), swap(by_z[cut:], 2)]
 

time: 45.7 us -> 44.6 us (0.976)
  waiting for transfers between devices: 14.7 us -> 12.7 us
  starting transfers between devices: 17.7 us -> 18.6 us
    ppermute x16, waiting for transfers between devices: 14.7 us -> 12.7 us  [swap(): return lax.ppermute(x, 'ex', [(d, d ^ mask) for d in range(n_ex)])]
    ppermute x16, starting transfers between devices: 17.7 us -> 18.6 us  [swap(): return lax.ppermute(x, 'ex', [(d, d ^ mask) for d in range(n_ex)])]
  transfers between devices with their start and end apart: 16 -> 16, of which waited for: 7 -> 8; matrix products, arithmetic and copies ran while one was open for 0% -> 0% of each run, Pallas kernels for 8% -> 8%
where the time goes in v17:
time: 44.6 us; the launch traced here: 44.4 us
  starting transfers between devices  18.6 us (42%)
  waiting for transfers between devices  12.7 us (28%)
  Pallas kernels  12.1 us (27%)
  between operations  0.82 us (2%)
    ppermute x16, starting transfers between devices, swap(): return lax.ppermute(x, 'ex', [(d, d ^ mask) for d in range(n_ex)])  18.6 us
    ppermute x16, waiting for transfers between devices, swap(): return lax.ppermute(x, 'ex', [(d, d ^ mask) for d in range(n_ex)])  12.7 us
    pallas_call x1, Pallas kernels, on_device(): pl.pallas_call(functools.partial(sums_kernel, n_ex=n_ex), in_specs=[hbm]...  5.02 us
    pallas_call x1, Pallas kernels, on_device(): pl.pallas_call(functools.partial(pursuit_kernel, steps=steps, scale=1.0 /...  3.19 us
    pallas_call x1, Pallas kernels, on_device(): pl.pallas_call(functools.partial(half_kernel, classes=classes), in_specs=...  2.06 us
  transfers between devices with their start and end apart: 16, of which 8 were waited for; matrix products, arithmetic and copies ran while one was open for 0% of the time, Pallas kernels for 8%

profile of v17, /device:TPU:0, one launch (start us, length us, event | category | flops | bytes accessed | tf_op | source)
XLA Modules:
  0.0 44.4 jit_solution(4105533063114195174)
XLA Ops:
  0.6 5.0 %class_sums.1 = (bf16[640,8192]{1,0:T(8,128)(2,1)S(1)}, f32[264,512]{1,0:T(8,128)S(1)}, f32[264,512]{1,0:T(8,128)S(1)}, f32[8,8192]{1,0:T(8,128)S(1)}) custom-call(s32[640]{0:T(1024)} %labels_ref.1, s32[3,32]{1,0:T(4,128)} %pick_ref.1, bf16[640,8192]{1,0:T(8,128)(2,1)} %feat_hbm.1), custom_call_target="tpu_custom_call" | custom-call | tf_op jit(solution)/shard_map/class_sums/pallas_call | solution.py:329
  5.7 0.5 %collective-permute-start = (f32[264,512]{1,0:T(8,128)S(1)}, f32[264,512]{1,0:T(8,128)S(1)}, u32[]{:S(2)}, u32[]{:S(2)}) collective-permute-start(f32[264,512]{1,0:T(8,128)S(1)} %get-tuple-element.27), channel_id=1, source_target_pairs={{0,1},{1,0},{2,3},{3,2},{4,5},{5,4},{6,7},{7,6},{8,9},{9,8},{10,11... | collective-permute-start | bytes 1622024 | tf_op jit(solution)/shard_map/ppermute | solution.py:324
  6.2 3.7 %collective-permute-start.2 = (bf16[2,8,3072]{2,1,0:T(8,128)(2,1)S(1)}, bf16[2,8,3072]{2,1,0:T(8,128)(2,1)S(1)}, u32[]{:S(2)}, u32[]{:S(2)}) collective-permute-start(bf16[2,8,3072]{2,1,0:T(8,128)(2,1)S(1)} %pack_rows.1), channel_id=1, source_target_pairs={{0,8},{1,9},{2,10},{3,11},{4,12},{5,13},{6,14},{7,15},{8,0},{9,1},... | collective-permute-start | bytes 294920 | tf_op jit(solution)/shard_map/ppermute | solution.py:324
  9.9 0.2 pair_sums.1
  10.1 1.6 %collective-permute-start.1 = (s16[2,136,128]{2,1,0:T(8,128)(2,1)S(1)}, s16[2,136,128]{2,1,0:T(8,128)(2,1)S(1)}, u32[]{:S(2)}, u32[]{:S(2)}) collective-permute-start(s16[2,136,128]{2,1,0:T(8,128)(2,1)S(1)} %get-tuple-element.29), channel_id=1, source_target_pairs={{0,4},{1,5},{2,6},{3,7},{4,0},{5,1},{6,2},{7,3},{8,12},{9,13},{10,... | collective-permute-start | bytes 208904 | tf_op jit(solution)/shard_map/ppermute | solution.py:324
  11.7 1.5 %collective-permute-start.3 = (s16[2,136,128]{2,1,0:T(8,128)(2,1)S(1)}, s16[2,136,128]{2,1,0:T(8,128)(2,1)S(1)}, u32[]{:S(2)}, u32[]{:S(2)}) collective-permute-start(s16[2,136,128]{2,1,0:T(8,128)(2,1)S(1)} %get-tuple-element.32), channel_id=1, source_target_pairs={{0,2},{1,3},{2,0},{3,1},{4,6},{5,7},{6,4},{7,5},{8,10},{9,11},{10,... | collective-permute-start | bytes 208904 | tf_op jit(solution)/shard_map/ppermute | solution.py:324
  13.3 0.4 collective-permute-start.4
  13.7 1.8 %collective-permute-done.2 = bf16[2,8,3072]{2,1,0:T(8,128)(2,1)S(1)} collective-permute-done((bf16[2,8,3072]{2,1,0:T(8,128)(2,1)S(1)}, bf16[2,8,3072]{2,1,0:T(8,128)(2,1)S(1)}, u32[]{:S(2)}, u32[]{:S(2)}) %collective-permute-start.2) | collective-permute-done | bytes 98336 | tf_op jit(solution)/shard_map/ppermute | solution.py:324
  15.5 0.3 select_tails.1.rest_ref
  15.8 0.2 collective-permute-done.3.refs_2_
  16.1 2.4 %collective-permute-done.4.refs_3_ = s16[2,136,128]{2,1,0:T(8,128)(2,1)S(1)} collective-permute-done((s16[2,136,128]{2,1,0:T(8,128)(2,1)S(1)}, s16[2,136,128]{2,1,0:T(8,128)(2,1)S(1)}, u32[]{:S(2)}, u32[]{:S(2)}) %collective-permute-start.4) | collective-permute-done | bytes 69664 | tf_op jit(solution)/shard_map/ppermute | solution.py:324
  18.5 0.3 add_sums.2.refs_0_
  18.8 1.9 %collective-permute-start.7 = (s16[2,136,128]{2,1,0:T(8,128)(2,1)S(1)}, s16[2,136,128]{2,1,0:T(8,128)(2,1)S(1)}, u32[]{:S(2)}, u32[]{:S(2)}) collective-permute-start(s16[2,136,128]{2,1,0:T(8,128)(2,1)S(1)} %add_sums.2.refs_0_), channel_id=1, source_target_pairs={{0,8},{1,9},{2,10},{3,11},{4,12},{5,13},{6,14},{7,15},{8,0},{9,1},... | collective-permute-start | bytes 208904 | tf_op jit(solution)/shard_map/ppermute | solution.py:324
  20.6 0.3 select_rows.1.one_ref
  21.0 0.1 collective-permute-start.5
  21.0 1.3 %collective-permute-done.5 = bf16[16,3072]{1,0:T(8,128)(2,1)S(1)} collective-permute-done((bf16[16,3072]{1,0:T(8,128)(2,1)S(1)}, bf16[16,3072]{1,0:T(8,128)(2,1)S(1)}, u32[]{:S(2)}, u32[]{:S(2)}) %collective-permute-start.5) | collective-permute-done | bytes 98336 | tf_op jit(solution)/shard_map/ppermute | solution.py:324
  22.3 0.7 %collective-permute-start.8 = (bf16[32,3072]{1,0:T(8,128)(2,1)S(1)}, bf16[32,3072]{1,0:T(8,128)(2,1)S(1)}, u32[]{:S(2)}, u32[]{:S(2)}) collective-permute-start(bf16[32,3072]{1,0:T(8,128)(2,1)S(1)} %constant_dynamic-update-slice_fusion.refs_0_), channel_id=1, source_target_pairs={{0,2},{1,3},{2,0},{3,1},{4,6},{5,7},{6,4},{7,5},{8,10},{9,11},{10,... | collective-permute-start | bytes 589832 | tf_op jit(solution)/shard_map/ppermute | solution.py:324
  23.0 1.9 %collective-permute-start.6 = (bf16[32,3072]{1,0:T(8,128)(2,1)S(1)}, bf16[32,3072]{1,0:T(8,128)(2,1)S(1)}, u32[]{:S(2)}, u32[]{:S(2)}) collective-permute-start(bf16[32,3072]{1,0:T(8,128)(2,1)S(1)} %constant_dynamic-update-slice_fusion.refs_0_), channel_id=1, source_target_pairs={{0,4},{1,5},{2,6},{3,7},{4,0},{5,1},{6,2},{7,3},{8,12},{9,13},{10,... | collective-permute-start | bytes 589832 | tf_op jit(solution)/shard_map/ppermute | solution.py:324
  24.9 0.3 add_sums.3
  25.2 4.1 %collective-permute-done.8.refs_2_ = bf16[32,3072]{1,0:T(8,128)(2,1)S(1)} collective-permute-done((bf16[32,3072]{1,0:T(8,128)(2,1)S(1)}, bf16[32,3072]{1,0:T(8,128)(2,1)S(1)}, u32[]{:S(2)}, u32[]{:S(2)}) %collective-permute-start.8) | collective-permute-done | bytes 196640 | tf_op jit(solution)/shard_map/ppermute | solution.py:324
  29.3 2.1 %collective-permute-start.9 = (bf16[16,3072]{1,0:T(8,128)(2,1)S(1)}, bf16[16,3072]{1,0:T(8,128)(2,1)S(1)}, u32[]{:S(2)}, u32[]{:S(2)}) collective-permute-start(bf16[16,3072]{1,0:T(8,128)(2,1)S(1)} %slice.14), channel_id=1, source_target_pairs={{0,4},{1,5},{2,6},{3,7},{4,0},{5,1},{6,2},{7,3},{8,12},{9,13},{10,... | collective-permute-start | bytes 294920 | tf_op jit(solution)/shard_map/ppermute | solution.py:324
  31.4 0.6 %collective-permute-start.10 = (bf16[16,3072]{1,0:T(8,128)(2,1)S(1)}, bf16[16,3072]{1,0:T(8,128)(2,1)S(1)}, u32[]{:S(2)}, u32[]{:S(2)}) collective-permute-start(bf16[16,3072]{1,0:T(8,128)(2,1)S(1)} %slice.15), channel_id=1, source_target_pairs={{0,2},{1,3},{2,0},{3,1},{4,6},{5,7},{6,4},{7,5},{8,10},{9,11},{10,... | collective-permute-start | bytes 294920 | tf_op jit(solution)/shard_map/ppermute | solution.py:324
  32.0 1.1 %collective-permute-start.14 = (s16[2,136,128]{2,1,0:T(8,128)(2,1)S(1)}, s16[2,136,128]{2,1,0:T(8,128)(2,1)S(1)}, u32[]{:S(2)}, u32[]{:S(2)}) collective-permute-start(s16[2,136,128]{2,1,0:T(8,128)(2,1)S(1)} %add_sums.3), channel_id=1, source_target_pairs={{0,6},{1,7},{2,4},{3,5},{4,2},{5,3},{6,0},{7,1},{8,14},{9,15},{10,... | collective-permute-start | bytes 208904 | tf_op jit(solution)/shard_map/ppermute | solution.py:324
  33.1 1.5 %collective-permute-start.13 = (s16[2,136,128]{2,1,0:T(8,128)(2,1)S(1)}, s16[2,136,128]{2,1,0:T(8,128)(2,1)S(1)}, u32[]{:S(2)}, u32[]{:S(2)}) collective-permute-start(s16[2,136,128]{2,1,0:T(8,128)(2,1)S(1)} %add_sums.3), channel_id=1, source_target_pairs={{0,2},{1,3},{2,0},{3,1},{4,6},{5,7},{6,4},{7,5},{8,10},{9,11},{10,... | collective-permute-start | bytes 208904 | tf_op jit(solution)/shard_map/ppermute | solution.py:324
  34.6 0.9 %collective-permute-start.12 = (s16[2,136,128]{2,1,0:T(8,128)(2,1)S(1)}, s16[2,136,128]{2,1,0:T(8,128)(2,1)S(1)}, u32[]{:S(2)}, u32[]{:S(2)}) collective-permute-start(s16[2,136,128]{2,1,0:T(8,128)(2,1)S(1)} %add_sums.3), channel_id=1, source_target_pairs={{0,4},{1,5},{2,6},{3,7},{4,0},{5,1},{6,2},{7,3},{8,12},{9,13},{10,... | collective-permute-start | bytes 208904 | tf_op jit(solution)/shard_map/ppermute | solution.py:324
  35.5 2.0 %collective-permute-done.10.refs_4_ = bf16[16,3072]{1,0:T(8,128)(2,1)S(1)} collective-permute-done((bf16[16,3072]{1,0:T(8,128)(2,1)S(1)}, bf16[16,3072]{1,0:T(8,128)(2,1)S(1)}, u32[]{:S(2)}, u32[]{:S(2)}) %collective-permute-start.10) | collective-permute-done | bytes 98336 | tf_op jit(solution)/shard_map/ppermute | solution.py:324
  37.5 0.4 picked_rows.1.x_ref.x_own
  38.0 0.2 collective-permute-done.13
  38.3 0.7 %collective-permute-done.12 = s16[2,136,128]{2,1,0:T(8,128)(2,1)S(1)} collective-permute-done((s16[2,136,128]{2,1,0:T(8,128)(2,1)S(1)}, s16[2,136,128]{2,1,0:T(8,128)(2,1)S(1)}, u32[]{:S(2)}, u32[]{:S(2)}) %collective-permute-start.12) | collective-permute-done | bytes 69664 | tf_op jit(solution)/shard_map/ppermute | solution.py:324
  39.0 0.1 collective-permute-start.15
  39.1 2.1 %own_half_products.1 = (f32[96,640]{1,0:T(8,128)S(1)}, f32[128,96]{1,0:T(8,128)S(1)}, f32[32,4096]{1,0:T(8,128)S(1)}) custom-call(bf16[640,8192]{1,0:T(8,128)(2,1)S(1)} %get-tuple-element.25.feat_ref, s16[8,136,128]{2,1,0:T(8,128)(2,1)S(1)} %constant_dynamic-update-slice_fusion.2.code_ref, bf16[96,4096]{1,0:T(8,128)(2,1)S(1)} %picked_rows.1.x_ref.x_own), custom_call_target="tpu_custom_call" | custom-call | tf_op jit(solution)/shard_map/own_half_products/pallas_call | solution.py:418
  41.2 3.2 %pursuit.1 = (f32[3,640]{1,0:T(4,128)}, f32[32,8192]{1,0:T(8,128)}) custom-call(s32[640]{0:T(1024)S(1)} %copy-done.1, bf16[640,8192]{1,0:T(8,128)(2,1)S(1)} %get-tuple-element.25.feat_ref, bf16[96,4096]{1,0:T(8,128)(2,1)S(1)} %picked_rows.1.x_ref.x_own, bf16[96,4096]{1,0:T(8,128)(2,1)S(1)} %collective-permute-done.11.x_twin, ...), custom_call_target="tpu_custom_call" | custom-call | tf_op jit(solution)/shard_map/pursuit/pallas_call | solution.py:432
  (23 shorter events, 0.2 us)
Async XLA Ops:
  0.6 14.8 %copy-start = (s32[3,32]{1,0:T(4,128)S(1)}, s32[3,32]{1,0:T(4,128)}, u32[]{:S(2)}) copy-start(s32[3,32]{1,0:T(4,128)} %pick_ref.1) | copy-start | bytes 1156
  5.7 4.2 %collective-permute-start = (f32[264,512]{1,0:T(8,128)S(1)}, f32[264,512]{1,0:T(8,128)S(1)}, u32[]{:S(2)}, u32[]{:S(2)}) collective-permute-start(f32[264,512]{1,0:T(8,128)S(1)} %get-tuple-element.27), channel_id=1, source_target_pairs={{0,1},{1,0},{2,3},{3,2},{4,5},{5,4},{6,7},{7,6},{8,9},{9,8},{10,11... | collective-permute-start | bytes 1622024 | tf_op jit(solution)/shard_map/ppermute | solution.py:324
  6.2 9.2 %collective-permute-start.2 = (bf16[2,8,3072]{2,1,0:T(8,128)(2,1)S(1)}, bf16[2,8,3072]{2,1,0:T(8,128)(2,1)S(1)}, u32[]{:S(2)}, u32[]{:S(2)}) collective-permute-start(bf16[2,8,3072]{2,1,0:T(8,128)(2,1)S(1)} %pack_rows.1), channel_id=1, source_target_pairs={{0,8},{1,9},{2,10},{3,11},{4,12},{5,13},{6,14},{7,15},{8,0},{9,1},... | collective-permute-start | bytes 294920 | tf_op jit(solution)/shard_map/ppermute | solution.py:324
  10.1 5.7 %collective-permute-start.1 = (s16[2,136,128]{2,1,0:T(8,128)(2,1)S(1)}, s16[2,136,128]{2,1,0:T(8,128)(2,1)S(1)}, u32[]{:S(2)}, u32[]{:S(2)}) collective-permute-start(s16[2,136,128]{2,1,0:T(8,128)(2,1)S(1)} %get-tuple-element.29), channel_id=1, source_target_pairs={{0,4},{1,5},{2,6},{3,7},{4,0},{5,1},{6,2},{7,3},{8,12},{9,13},{10,... | collective-permute-start | bytes 208904 | tf_op jit(solution)/shard_map/ppermute | solution.py:324
  11.7 4.3 %collective-permute-start.3 = (s16[2,136,128]{2,1,0:T(8,128)(2,1)S(1)}, s16[2,136,128]{2,1,0:T(8,128)(2,1)S(1)}, u32[]{:S(2)}, u32[]{:S(2)}) collective-permute-start(s16[2,136,128]{2,1,0:T(8,128)(2,1)S(1)} %get-tuple-element.32), channel_id=1, source_target_pairs={{0,2},{1,3},{2,0},{3,1},{4,6},{5,7},{6,4},{7,5},{8,10},{9,11},{10,... | collective-permute-start | bytes 208904 | tf_op jit(solution)/shard_map/ppermute | solution.py:324
  13.3 5.2 %collective-permute-start.4 = (s16[2,136,128]{2,1,0:T(8,128)(2,1)S(1)}, s16[2,136,128]{2,1,0:T(8,128)(2,1)S(1)}, u32[]{:S(2)}, u32[]{:S(2)}) collective-permute-start(s16[2,136,128]{2,1,0:T(8,128)(2,1)S(1)} %get-tuple-element.33), channel_id=1, source_target_pairs={{0,6},{1,7},{2,4},{3,5},{4,2},{5,3},{6,0},{7,1},{8,14},{9,15},{10,... | collective-permute-start | bytes 208904 | tf_op jit(solution)/shard_map/ppermute | solution.py:324
  18.8 6.2 %collective-permute-start.7 = (s16[2,136,128]{2,1,0:T(8,128)(2,1)S(1)}, s16[2,136,128]{2,1,0:T(8,128)(2,1)S(1)}, u32[]{:S(2)}, u32[]{:S(2)}) collective-permute-start(s16[2,136,128]{2,1,0:T(8,128)(2,1)S(1)} %add_sums.2.refs_0_), channel_id=1, source_target_pairs={{0,8},{1,9},{2,10},{3,11},{4,12},{5,13},{6,14},{7,15},{8,0},{9,1},... | collective-permute-start | bytes 208904 | tf_op jit(solution)/shard_map/ppermute | solution.py:324
  21.0 1.4 %collective-permute-start.5 = (bf16[16,3072]{1,0:T(8,128)(2,1)S(1)}, bf16[16,3072]{1,0:T(8,128)(2,1)S(1)}, u32[]{:S(2)}, u32[]{:S(2)}) collective-permute-start(bf16[16,3072]{1,0:T(8,128)(2,1)S(1)} %get-tuple-element.38), channel_id=1, source_target_pairs={{0,1},{1,0},{2,3},{3,2},{4,5},{5,4},{6,7},{7,6},{8,9},{9,8},{10,11... | collective-permute-start | bytes 294920 | tf_op jit(solution)/shard_map/ppermute | solution.py:324
  22.3 7.0 %collective-permute-start.8 = (bf16[32,3072]{1,0:T(8,128)(2,1)S(1)}, bf16[32,3072]{1,0:T(8,128)(2,1)S(1)}, u32[]{:S(2)}, u32[]{:S(2)}) collective-permute-start(bf16[32,3072]{1,0:T(8,128)(2,1)S(1)} %constant_dynamic-update-slice_fusion.refs_0_), channel_id=1, source_target_pairs={{0,2},{1,3},{2,0},{3,1},{4,6},{5,7},{6,4},{7,5},{8,10},{9,11},{10,... | collective-permute-start | bytes 589832 | tf_op jit(solution)/shard_map/ppermute | solution.py:324
  23.0 8.4 %collective-permute-start.6 = (bf16[32,3072]{1,0:T(8,128)(2,1)S(1)}, bf16[32,3072]{1,0:T(8,128)(2,1)S(1)}, u32[]{:S(2)}, u32[]{:S(2)}) collective-permute-start(bf16[32,3072]{1,0:T(8,128)(2,1)S(1)} %constant_dynamic-update-slice_fusion.refs_0_), channel_id=1, source_target_pairs={{0,4},{1,5},{2,6},{3,7},{4,0},{5,1},{6,2},{7,3},{8,12},{9,13},{10,... | collective-permute-start | bytes 589832 | tf_op jit(solution)/shard_map/ppermute | solution.py:324
  25.2 15.9 %copy-start.1 = (s32[640]{0:T(1024)S(1)}, s32[640]{0:T(1024)}, u32[]{:S(2)}) copy-start(s32[640]{0:T(1024)} %labels_ref.1) | copy-start | bytes 7684
  29.3 6.2 %collective-permute-start.9 = (bf16[16,3072]{1,0:T(8,128)(2,1)S(1)}, bf16[16,3072]{1,0:T(8,128)(2,1)S(1)}, u32[]{:S(2)}, u32[]{:S(2)}) collective-permute-start(bf16[16,3072]{1,0:T(8,128)(2,1)S(1)} %slice.14), channel_id=1, source_target_pairs={{0,4},{1,5},{2,6},{3,7},{4,0},{5,1},{6,2},{7,3},{8,12},{9,13},{10,... | collective-permute-start | bytes 294920 | tf_op jit(solution)/shard_map/ppermute | solution.py:324
  31.4 6.1 %collective-permute-start.10 = (bf16[16,3072]{1,0:T(8,128)(2,1)S(1)}, bf16[16,3072]{1,0:T(8,128)(2,1)S(1)}, u32[]{:S(2)}, u32[]{:S(2)}) collective-permute-start(bf16[16,3072]{1,0:T(8,128)(2,1)S(1)} %slice.15), channel_id=1, source_target_pairs={{0,2},{1,3},{2,0},{3,1},{4,6},{5,7},{6,4},{7,5},{8,10},{9,11},{10,... | collective-permute-start | bytes 294920 | tf_op jit(solution)/shard_map/ppermute | solution.py:324
  32.0 6.0 %collective-permute-start.14 = (s16[2,136,128]{2,1,0:T(8,128)(2,1)S(1)}, s16[2,136,128]{2,1,0:T(8,128)(2,1)S(1)}, u32[]{:S(2)}, u32[]{:S(2)}) collective-permute-start(s16[2,136,128]{2,1,0:T(8,128)(2,1)S(1)} %add_sums.3), channel_id=1, source_target_pairs={{0,6},{1,7},{2,4},{3,5},{4,2},{5,3},{6,0},{7,1},{8,14},{9,15},{10,... | collective-permute-start | bytes 208904 | tf_op jit(solution)/shard_map/ppermute | solution.py:324
  33.1 5.1 %collective-permute-start.13 = (s16[2,136,128]{2,1,0:T(8,128)(2,1)S(1)}, s16[2,136,128]{2,1,0:T(8,128)(2,1)S(1)}, u32[]{:S(2)}, u32[]{:S(2)}) collective-permute-start(s16[2,136,128]{2,1,0:T(8,128)(2,1)S(1)} %add_sums.3), channel_id=1, source_target_pairs={{0,2},{1,3},{2,0},{3,1},{4,6},{5,7},{6,4},{7,5},{8,10},{9,11},{10,... | collective-permute-start | bytes 208904 | tf_op jit(solution)/shard_map/ppermute | solution.py:324
  34.6 4.3 %collective-permute-start.12 = (s16[2,136,128]{2,1,0:T(8,128)(2,1)S(1)}, s16[2,136,128]{2,1,0:T(8,128)(2,1)S(1)}, u32[]{:S(2)}, u32[]{:S(2)}) collective-permute-start(s16[2,136,128]{2,1,0:T(8,128)(2,1)S(1)} %add_sums.3), channel_id=1, source_target_pairs={{0,4},{1,5},{2,6},{3,7},{4,0},{5,1},{6,2},{7,3},{8,12},{9,13},{10,... | collective-permute-start | bytes 208904 | tf_op jit(solution)/shard_map/ppermute | solution.py:324
  37.9 3.2 %collective-permute-start.11 = (bf16[96,4096]{1,0:T(8,128)(2,1)S(1)}, bf16[96,4096]{1,0:T(8,128)(2,1)S(1)}, u32[]{:S(2)}, u32[]{:S(2)}) collective-permute-start(bf16[96,4096]{1,0:T(8,128)(2,1)S(1)} %picked_rows.1.x_ref.x_own), channel_id=1, source_target_pairs={{0,1},{1,0},{2,3},{3,2},{4,5},{5,4},{6,7},{7,6},{8,9},{9,8},{10,11... | collective-permute-start | bytes 2359304 | tf_op jit(solution)/shard_map/ppermute | solution.py:324
  39.0 2.1 %collective-permute-start.15 = (s16[8,136,128]{2,1,0:T(8,128)(2,1)S(1)}, s16[8,136,128]{2,1,0:T(8,128)(2,1)S(1)}, u32[]{:S(2)}, u32[]{:S(2)}) collective-permute-start(s16[8,136,128]{2,1,0:T(8,128)(2,1)S(1)} %constant_dynamic-update-slice_fusion.2.code_ref), channel_id=1, source_target_pairs={{0,1},{1,0},{2,3},{3,2},{4,5},{5,4},{6,7},{7,6},{8,9},{9,8},{10,11... | collective-permute-start | bytes 835592 | tf_op jit(solution)/shard_map/ppermute | solution.py:324

commit v18 on v14

--- a/solution.py
+++ b/solution.py
@@ -10,7 +10,6 @@
 
 ridge = 1.0
 slots = 2
-near_masks = (0, 4, 2, 6)
 f32 = jnp.float32
 bf16 = jnp.bfloat16
 
@@ -125,18 +124,48 @@
         rows_ref[part] = jnp.concatenate(lines, axis=0).astype(bf16)
 
 
-def near_id(mask):
-    return (lax.axis_index("ex") // 2 % 4) ^ (mask // 2)
-
-
-def pair_kernel(keep_ref, got_ref, *code_refs, classes):
-    far = code_refs[0].shape[0]
+def near_id(step, parity):
+    first = 1 + parity
+    flip = (step % 2) * first + (step // 2) * (3 - first)
+    return (lax.axis_index("ex") // 2 % 4) ^ flip
+
+
+def counts_of(mark, classes):
+    lane = lax.broadcasted_iota(jnp.int32, mark.shape, 1)
+    return jnp.where(lane < classes // 8, 0.0, mark)
+
+
+def pair_kernel(keep_ref, got_ref, hold_ref, tile_ref, code_ref, *, classes):
+    far = code_ref.shape[0] // 2
     base = 4 * far * classes
     tile = keep_ref[base : base + 8, :128] + got_ref[base : base + 8, :128]
-    for mask, code_ref in zip(near_masks, code_refs):
+    tile_ref[...] = tile
+    core = lax.axis_index("ex") % 2
+    for step in (1, 3, 0, 2):
         for j in range(far):
-            at = pl.ds(pl.multiple_of((j * 4 + near_id(mask)) * classes, classes), classes)
-            code_ref[j] = encode(keep_ref[at, :] + got_ref[at, :], tile)
+            block = j * 4 + near_id(step, core)
+            at = pl.ds(pl.multiple_of(block * classes, classes), classes)
+            value = keep_ref[at, :] + got_ref[at, :]
+            if step % 2:
+                code_ref[step // 2 * far + j] = encode(value, tile)
+            else:
+                hold_ref[step // 2 * far + j] = value
+
+
+def halve_kernel(hold_ref, tile_ref, got_ref, rest_ref, count_ref, code_ref, *, classes):
+    far = code_ref.shape[0]
+    mark = decode(got_ref[0], classes)[1]
+    tile = tile_ref[...] + counts_of(mark, classes)
+    count_ref[...] = tile
+    for j in range(far):
+        code_ref[j] = encode(hold_ref[far + j] + decode(got_ref[far + j], classes)[0], tile)
+        rest_ref[j] = hold_ref[j] + decode(got_ref[j], classes)[0]
+
+
+def near_kernel(hold_ref, tile_ref, got_ref, code_ref, *, classes):
+    for j in range(code_ref.shape[0]):
+        value, mark = decode(got_ref[j], classes)
+        code_ref[j] = encode(hold_ref[j] + value, tile_ref[...] + counts_of(mark, classes))
 
 
 def add_kernel(*refs, classes, last):
@@ -150,8 +179,7 @@
         if last:
             code_ref[j] = encode(value / jnp.sqrt(column(mark, classes, classes // 8)))
         else:
-            lane = lax.broadcasted_iota(jnp.int32, mark.shape, 1)
-            code_ref[j] = encode(value, jnp.where(lane < classes // 8, 0.0, mark))
+            code_ref[j] = encode(value, counts_of(mark, classes))
 
 
 def diagonal(block):
@@ -215,7 +243,8 @@
     far = jnp.zeros_like(pick)
     for b in range(3, bits):
         far = far + (((away >> b) & 1) << (bits - 1 - b))
-    near = ((away >> 2) & 1) + 2 * ((away >> 1) & 1)
+    by_y, by_z = (away >> 1) & 1, (away >> 2) & 1
+    near = jnp.where(device % 2 == 0, by_y + 2 * by_z, by_z + 2 * by_y)
     spot = (2 * near + (away & 1)) * (n_ex // 8) + far
     step = lax.broadcasted_iota(jnp.int32, pick.shape, 0)
     line = lax.broadcasted_iota(jnp.int32, (lines, classes), 0)
@@ -248,7 +277,7 @@
     width = half // code_ref.shape[0]
     here = pl.ds(pl.multiple_of(side * half, half), half)
     for k in range(4 * far):
-        block = k % far * 4 + near_id(near_masks[k // far])
+        block = k % far * 4 + near_id(k // far, side)
         target = decode(code_ref[k], classes)[0]
         target_ref[:, pl.ds(pl.multiple_of(target_at + block * width, width), width)] = target
         left_ref[:classes, pl.ds(pl.multiple_of(block * width, width), width)] = target.astype(bf16)
@@ -323,6 +352,10 @@
     def swap(x, mask):
         return lax.ppermute(x, "ex", [(d, d ^ mask) for d in range(n_ex)])
 
+    def cross(x, first):
+        masks = (2, 4) if first else (4, 2)
+        return lax.ppermute(x, "ex", [(d, d ^ masks[d % 2]) for d in range(n_ex)])
+
     def after(x, *others):
         return lax.optimization_barrier((x,) + others)[0]
 
@@ -354,14 +387,23 @@
 
     far_masks = [8 << b for b in range(n_ex.bit_length() - 4)]
     got = swap(send, 1)
-    codes = pl.pallas_call(
-        functools.partial(pair_kernel, classes=classes),
-        in_specs=[vmem] * 2,
-        out_specs=[vmem] * 4,
-        out_shape=[code] * 4,
-        compiler_params=limit,
-        name="pair_sums",
-    )(keep, got)
+    far = groups // 4
+
+    def call(kernel, name, outs, *args):
+        return pl.pallas_call(
+            functools.partial(kernel, classes=classes),
+            in_specs=[vmem] * len(args),
+            out_specs=[vmem] * len(outs),
+            out_shape=outs,
+            compiler_params=limit,
+            name=name,
+        )(*args)
+
+    def held_sums(count):
+        return [jax.ShapeDtypeStruct((count, classes, width), f32), jax.ShapeDtypeStruct((8, 128), f32)]
+
+    two = jax.ShapeDtypeStruct((2 * far,) + code.shape[1:], jnp.int16)
+    hold, tile, pair_code = call(pair_kernel, "pair_sums", held_sums(2 * far) + [two], keep, got)
     packed = pl.pallas_call(
         functools.partial(pack_kernel, steps=steps),
         in_specs=[vmem],
@@ -373,8 +415,11 @@
     for mask in reversed(far_masks):
         packed = jnp.concatenate([packed, swap(packed, mask)], axis=1)
 
-    near_codes = [swap(c, m) for c, m in zip(codes[1:], near_masks[1:])]
-    part_sum = add([codes[0], after(near_codes[0], packed)] + near_codes[1:], False)
+    got = cross(pair_code, True)
+    hold, tile, half_code = call(halve_kernel, "half_sums", held_sums(far) + [code], hold, tile, got)
+    got = cross(half_code, False)
+    given = swap(after(packed[1], half_code), 1)
+    (part_sum,) = call(near_kernel, "near_sums", [code], hold, tile, after(got, packed))
 
     def select(tail, *others):
         return pl.pallas_call(
@@ -386,31 +431,32 @@
             name="select_tails" if tail else "select_rows",
         )(after(pick_index, *others))
 
-    rest = select(True, codes[0])
-    near_sum = after(part_sum, rest)
+    rest = select(True, pair_code)
+    near_sum = after(part_sum, rest, given)
     more = swap(near_sum, far_masks[0])
     one = select(False, near_sum)
     part_sum = add([near_sum, more], len(far_masks) == 1)
     for mask in far_masks[1:]:
         part_sum = add([part_sum, swap(part_sum, mask)], mask == far_masks[-1])
-    given = swap(after(packed[1], near_sum), 1)
     near = jnp.concatenate([after(packed[0], one), given], axis=0)
-    parts = [near] + [swap(near, m) for m in near_masks[1:]]
-    own_parts = [part_sum] + [swap(part_sum, m) for m in near_masks[1:3]]
-    own_parts.append(swap(after(part_sum, parts[1]), near_masks[3]))
+    got = cross(part_sum, True)
+    pair = jnp.concatenate([part_sum, got], axis=0)
+    own_parts = [pair, cross(pair, False)]
+    lines = jnp.concatenate([near, after(cross(near, True), got)], axis=0)
+    parts = [lines, cross(lines, False)]
 
     x = pl.pallas_call(
         functools.partial(picked_kernel, steps=steps),
-        in_specs=[vmem] * 6,
+        in_specs=[vmem] * 4,
         out_specs=vmem,
         out_shape=jax.ShapeDtypeStruct((total, full // 2), bf16),
         scratch_shapes=[pltpu.VMEM((n_ex * 8, main), bf16)],
         compiler_params=limit,
         name="picked_rows",
-    )(one, rest, *parts)
+    )(after(one, own_parts[1]), rest, *parts)
 
     x_twin = swap(x, 1)
-    own_half = jnp.concatenate(after(own_parts, x), axis=0)
+    own_half = jnp.concatenate(own_parts, axis=0)
     twin_half = swap(own_half, 1)
     left = pltpu.VMEM((total + classes, full // 2), bf16)
     direct, gram, target = pl.pallas_call(

time: 45.2 us -> 47 us (1.040)
  waiting for transfers between devices: 13.2 us -> 18.2 us
  starting transfers between devices: 18.8 us -> 15.4 us
    ppermute x0 -> x6, waiting for transfers between devices: none -> 12.6 us  [cross(): return lax.ppermute(x, 'ex', [(d, d ^ masks[d % 2]) for d in range(n_ex)])]
    ppermute x15 -> x6, starting transfers between devices: 18.8 us -> 7.15 us  [swap(): return lax.ppermute(x, 'ex', [(d, d ^ mask) for d in range(n_ex)])]
    ppermute x0 -> x6, starting transfers between devices: none -> 8.28 us  [cross(): return lax.ppermute(x, 'ex', [(d, d ^ masks[d % 2]) for d in range(n_ex)])]
    ppermute x15 -> x6, waiting for transfers between devices: 13.2 us -> 5.56 us  [swap(): return lax.ppermute(x, 'ex', [(d, d ^ mask) for d in range(n_ex)])]
    pallas_call x1 -> x3, Pallas kernels: 0.18 us -> 0.71 us  [call(): pl.pallas_call(functools.partial(kernel, classes=classes), in_specs=[vmem...]
  transfers between devices with their start and end apart: 15 -> 12, of which waited for: 6 -> 5; matrix products, arithmetic and copies ran while one was open for 0% -> 0% of each run, Pallas kernels for 8% -> 7%
where the time goes in v18:
time: 47 us; the launch traced here: 46.9 us
  waiting for transfers between devices  18.2 us (39%)
  starting transfers between devices  15.4 us (33%)
  Pallas kernels  12.4 us (26%)
  between operations  0.8 us (2%)
    ppermute x6, waiting for transfers between devices, cross(): return lax.ppermute(x, 'ex', [(d, d ^ masks[d % 2]) for d in range(n_ex)])  12.6 us
    ppermute x6, starting transfers between devices, cross(): return lax.ppermute(x, 'ex', [(d, d ^ masks[d % 2]) for d in range(n_ex)])  8.28 us
    ppermute x6, starting transfers between devices, swap(): return lax.ppermute(x, 'ex', [(d, d ^ mask) for d in range(n_ex)])  7.15 us
    ppermute x6, waiting for transfers between devices, swap(): return lax.ppermute(x, 'ex', [(d, d ^ mask) for d in range(n_ex)])  5.56 us
    pallas_call x1, Pallas kernels, on_device(): pl.pallas_call(functools.partial(sums_kernel, n_ex=n_ex), in_specs=[hbm]...  5.02 us
    pallas_call x1, Pallas kernels, on_device(): pl.pallas_call(functools.partial(pursuit_kernel, steps=steps, scale=1.0 /...  3.19 us
    pallas_call x1, Pallas kernels, on_device(): pl.pallas_call(functools.partial(half_kernel, classes=classes), in_specs=...  2.06 us
  transfers between devices with their start and end apart: 12, of which 5 were waited for; matrix products, arithmetic and copies ran while one was open for 0% of the time, Pallas kernels for 7%

profile of v18, /device:TPU:0, one launch (start us, length us, event | category | flops | bytes accessed | tf_op | source)
XLA Modules:
  0.0 46.9 jit_solution(18424641575805966681)
XLA Ops:
  0.6 5.0 %class_sums.1 = (bf16[640,8192]{1,0:T(8,128)(2,1)S(1)}, f32[264,512]{1,0:T(8,128)S(1)}, f32[264,512]{1,0:T(8,128)S(1)}, f32[8,8192]{1,0:T(8,128)S(1)}) custom-call(s32[640]{0:T(1024)} %labels_ref.1, s32[3,32]{1,0:T(4,128)} %pick_ref.1, bf16[640,8192]{1,0:T(8,128)(2,1)} %feat_hbm.1), custom_call_target="tpu_custom_call" | custom-call | tf_op jit(solution)/shard_map/class_sums/pallas_call | solution.py:362
  5.7 0.5 %collective-permute-start = (f32[264,512]{1,0:T(8,128)S(1)}, f32[264,512]{1,0:T(8,128)S(1)}, u32[]{:S(2)}, u32[]{:S(2)}) collective-permute-start(f32[264,512]{1,0:T(8,128)S(1)} %get-tuple-element.25), channel_id=1, source_target_pairs={{0,1},{1,0},{2,3},{3,2},{4,5},{5,4},{6,7},{7,6},{8,9},{9,8},{10,11... | collective-permute-start | bytes 1622024 | tf_op jit(solution)/shard_map/ppermute | solution.py:353
  6.2 3.7 %collective-permute-start.3 = (bf16[2,8,3072]{2,1,0:T(8,128)(2,1)S(1)}, bf16[2,8,3072]{2,1,0:T(8,128)(2,1)S(1)}, u32[]{:S(2)}, u32[]{:S(2)}) collective-permute-start(bf16[2,8,3072]{2,1,0:T(8,128)(2,1)S(1)} %pack_rows.1), channel_id=1, source_target_pairs={{0,8},{1,9},{2,10},{3,11},{4,12},{5,13},{6,14},{7,15},{8,0},{9,1},... | collective-permute-start | bytes 294920 | tf_op jit(solution)/shard_map/ppermute | solution.py:353
  9.9 0.0 collective-permute-done.got_ref
  9.9 0.2 pair_sums.1
  10.1 1.6 %collective-permute-start.1 = (s16[4,136,128]{2,1,0:T(8,128)(2,1)S(1)}, s16[4,136,128]{2,1,0:T(8,128)(2,1)S(1)}, u32[]{:S(2)}, u32[]{:S(2)}) collective-permute-start(s16[4,136,128]{2,1,0:T(8,128)(2,1)S(1)} %get-tuple-element.28), channel_id=1, source_target_pairs={{0,2},{1,5},{2,0},{3,7},{4,6},{5,1},{6,4},{7,3},{8,10},{9,13},{10,... | collective-permute-start | bytes 417800 | tf_op jit(solution)/shard_map/ppermute | solution.py:357
  11.7 3.8 %collective-permute-done.3 = bf16[2,8,3072]{2,1,0:T(8,128)(2,1)S(1)} collective-permute-done((bf16[2,8,3072]{2,1,0:T(8,128)(2,1)S(1)}, bf16[2,8,3072]{2,1,0:T(8,128)(2,1)S(1)}, u32[]{:S(2)}, u32[]{:S(2)}) %collective-permute-start.3) | collective-permute-done | bytes 98336 | tf_op jit(solution)/shard_map/ppermute | solution.py:353
  15.5 0.0 collective-permute-done.1.got_ref
  15.5 0.3 half_sums.1
  15.8 0.1 collective-permute-start.4
  15.9 1.4 %collective-permute-start.2 = (s16[2,136,128]{2,1,0:T(8,128)(2,1)S(1)}, s16[2,136,128]{2,1,0:T(8,128)(2,1)S(1)}, u32[]{:S(2)}, u32[]{:S(2)}) collective-permute-start(s16[2,136,128]{2,1,0:T(8,128)(2,1)S(1)} %get-tuple-element.31), channel_id=1, source_target_pairs={{0,4},{1,3},{2,6},{3,1},{4,0},{5,7},{6,2},{7,5},{8,12},{9,11},{10,... | collective-permute-start | bytes 208904 | tf_op jit(solution)/shard_map/ppermute | solution.py:357
  17.2 0.3 select_tails.1.rest_ref
  17.6 2.7 %collective-permute-done.2.got_ref = s16[2,136,128]{2,1,0:T(8,128)(2,1)S(1)} collective-permute-done((s16[2,136,128]{2,1,0:T(8,128)(2,1)S(1)}, s16[2,136,128]{2,1,0:T(8,128)(2,1)S(1)}, u32[]{:S(2)}, u32[]{:S(2)}) %collective-permute-start.2) | collective-permute-done | bytes 69664 | tf_op jit(solution)/shard_map/ppermute | solution.py:357
  20.2 0.3 near_sums.1.refs_0_
  20.5 2.3 %collective-permute-start.5 = (s16[2,136,128]{2,1,0:T(8,128)(2,1)S(1)}, s16[2,136,128]{2,1,0:T(8,128)(2,1)S(1)}, u32[]{:S(2)}, u32[]{:S(2)}) collective-permute-start(s16[2,136,128]{2,1,0:T(8,128)(2,1)S(1)} %near_sums.1.refs_0_), channel_id=1, source_target_pairs={{0,8},{1,9},{2,10},{3,11},{4,12},{5,13},{6,14},{7,15},{8,0},{9,1},... | collective-permute-start | bytes 208904 | tf_op jit(solution)/shard_map/ppermute | solution.py:353
  22.7 0.3 select_rows.1.one_ref
  23.1 1.6 %collective-permute-start.8 = (bf16[32,3072]{1,0:T(8,128)(2,1)S(1)}, bf16[32,3072]{1,0:T(8,128)(2,1)S(1)}, u32[]{:S(2)}, u32[]{:S(2)}) collective-permute-start(bf16[32,3072]{1,0:T(8,128)(2,1)S(1)} %pad_maximum_fusion.1), channel_id=1, source_target_pairs={{0,2},{1,5},{2,0},{3,7},{4,6},{5,1},{6,4},{7,3},{8,10},{9,13},{10,... | collective-permute-start | bytes 589832 | tf_op jit(solution)/shard_map/ppermute | solution.py:357
  24.7 1.8 %collective-permute-done.5.refs_1_ = s16[2,136,128]{2,1,0:T(8,128)(2,1)S(1)} collective-permute-done((s16[2,136,128]{2,1,0:T(8,128)(2,1)S(1)}, s16[2,136,128]{2,1,0:T(8,128)(2,1)S(1)}, u32[]{:S(2)}, u32[]{:S(2)}) %collective-permute-start.5) | collective-permute-done | bytes 69664 | tf_op jit(solution)/shard_map/ppermute | solution.py:353
  26.5 0.3 add_sums.1
  26.8 0.0 copy-start.1
  26.8 1.6 %collective-permute-start.6 = (s16[2,136,128]{2,1,0:T(8,128)(2,1)S(1)}, s16[2,136,128]{2,1,0:T(8,128)(2,1)S(1)}, u32[]{:S(2)}, u32[]{:S(2)}) collective-permute-start(s16[2,136,128]{2,1,0:T(8,128)(2,1)S(1)} %add_sums.1), channel_id=1, source_target_pairs={{0,2},{1,5},{2,0},{3,7},{4,6},{5,1},{6,4},{7,3},{8,10},{9,13},{10,... | collective-permute-start | bytes 208904 | tf_op jit(solution)/shard_map/ppermute | solution.py:357
  28.4 2.8 %collective-permute-done.6 = s16[2,136,128]{2,1,0:T(8,128)(2,1)S(1)} collective-permute-done((s16[2,136,128]{2,1,0:T(8,128)(2,1)S(1)}, s16[2,136,128]{2,1,0:T(8,128)(2,1)S(1)}, u32[]{:S(2)}, u32[]{:S(2)}) %collective-permute-start.6) | collective-permute-done | bytes 69664 | tf_op jit(solution)/shard_map/ppermute | solution.py:357
  31.2 1.4 %collective-permute-start.9 = (bf16[64,3072]{1,0:T(8,128)(2,1)S(1)}, bf16[64,3072]{1,0:T(8,128)(2,1)S(1)}, u32[]{:S(2)}, u32[]{:S(2)}) collective-permute-start(bf16[64,3072]{1,0:T(8,128)(2,1)S(1)} %constant_dynamic-update-slice_fusion.refs_0_), channel_id=1, source_target_pairs={{0,4},{1,3},{2,6},{3,1},{4,0},{5,7},{6,2},{7,5},{8,12},{9,11},{10,... | collective-permute-start | bytes 1179656 | tf_op jit(solution)/shard_map/ppermute | solution.py:357
  32.6 0.7 %collective-permute-start.7 = (s16[4,136,128]{2,1,0:T(8,128)(2,1)S(1)}, s16[4,136,128]{2,1,0:T(8,128)(2,1)S(1)}, u32[]{:S(2)}, u32[]{:S(2)}) collective-permute-start(s16[4,136,128]{2,1,0:T(8,128)(2,1)S(1)} %pad_add_fusion.1), channel_id=1, source_target_pairs={{0,4},{1,3},{2,6},{3,1},{4,0},{5,7},{6,2},{7,5},{8,12},{9,11},{10,... | collective-permute-start | bytes 417800 | tf_op jit(solution)/shard_map/ppermute | solution.py:357
  33.3 7.2 %collective-permute-done.7 = s16[4,136,128]{2,1,0:T(8,128)(2,1)S(1)} collective-permute-done((s16[4,136,128]{2,1,0:T(8,128)(2,1)S(1)}, s16[4,136,128]{2,1,0:T(8,128)(2,1)S(1)}, u32[]{:S(2)}, u32[]{:S(2)}) %collective-permute-start.7) | collective-permute-done | bytes 139296 | tf_op jit(solution)/shard_map/ppermute | solution.py:357
  40.5 0.4 picked_rows.1.x_ref.x_own
  40.9 0.1 collective-permute-start.10
  41.0 0.6 %collective-permute-start.11 = (s16[8,136,128]{2,1,0:T(8,128)(2,1)S(1)}, s16[8,136,128]{2,1,0:T(8,128)(2,1)S(1)}, u32[]{:S(2)}, u32[]{:S(2)}) collective-permute-start(s16[8,136,128]{2,1,0:T(8,128)(2,1)S(1)} %pad_add_fusion.code_ref), channel_id=1, source_target_pairs={{0,1},{1,0},{2,3},{3,2},{4,5},{5,4},{6,7},{7,6},{8,9},{9,8},{10,11... | collective-permute-start | bytes 835592 | tf_op jit(solution)/shard_map/ppermute | solution.py:353
  41.6 2.1 %own_half_products.1 = (f32[96,640]{1,0:T(8,128)S(1)}, f32[128,96]{1,0:T(8,128)S(1)}, f32[32,4096]{1,0:T(8,128)S(1)}) custom-call(bf16[640,8192]{1,0:T(8,128)(2,1)S(1)} %get-tuple-element.23.feat_ref, s16[8,136,128]{2,1,0:T(8,128)(2,1)S(1)} %pad_add_fusion.code_ref, bf16[96,4096]{1,0:T(8,128)(2,1)S(1)} %picked_rows.1.x_ref.x_own), custom_call_target="tpu_custom_call" | custom-call | tf_op jit(solution)/shard_map/own_half_products/pallas_call | solution.py:462
  43.7 0.0 collective-permute-done.11.code_ref
  43.7 0.0 collective-permute-done.10.x_twin
  43.7 3.2 %pursuit.1 = (f32[3,640]{1,0:T(4,128)}, f32[32,8192]{1,0:T(8,128)}) custom-call(s32[640]{0:T(1024)S(1)} %copy-done.1, bf16[640,8192]{1,0:T(8,128)(2,1)S(1)} %get-tuple-element.23.feat_ref, bf16[96,4096]{1,0:T(8,128)(2,1)S(1)} %picked_rows.1.x_ref.x_own, bf16[96,4096]{1,0:T(8,128)(2,1)S(1)} %collective-permute-done.10.x_twin, ...), custom_call_target="tpu_custom_call" | custom-call | tf_op jit(solution)/shard_map/pursuit/pallas_call | solution.py:476
  (14 shorter events, 0.1 us)
Async XLA Ops:
  0.6 16.6 %copy-start = (s32[3,32]{1,0:T(4,128)S(1)}, s32[3,32]{1,0:T(4,128)}, u32[]{:S(2)}) copy-start(s32[3,32]{1,0:T(4,128)} %pick_ref.1) | copy-start | bytes 1156
  5.7 4.2 %collective-permute-start = (f32[264,512]{1,0:T(8,128)S(1)}, f32[264,512]{1,0:T(8,128)S(1)}, u32[]{:S(2)}, u32[]{:S(2)}) collective-permute-start(f32[264,512]{1,0:T(8,128)S(1)} %get-tuple-element.25), channel_id=1, source_target_pairs={{0,1},{1,0},{2,3},{3,2},{4,5},{5,4},{6,7},{7,6},{8,9},{9,8},{10,11... | collective-permute-start | bytes 1622024 | tf_op jit(solution)/shard_map/ppermute | solution.py:353
  6.2 9.2 %collective-permute-start.3 = (bf16[2,8,3072]{2,1,0:T(8,128)(2,1)S(1)}, bf16[2,8,3072]{2,1,0:T(8,128)(2,1)S(1)}, u32[]{:S(2)}, u32[]{:S(2)}) collective-permute-start(bf16[2,8,3072]{2,1,0:T(8,128)(2,1)S(1)} %pack_rows.1), channel_id=1, source_target_pairs={{0,8},{1,9},{2,10},{3,11},{4,12},{5,13},{6,14},{7,15},{8,0},{9,1},... | collective-permute-start | bytes 294920 | tf_op jit(solution)/shard_map/ppermute | solution.py:353
  10.1 5.4 %collective-permute-start.1 = (s16[4,136,128]{2,1,0:T(8,128)(2,1)S(1)}, s16[4,136,128]{2,1,0:T(8,128)(2,1)S(1)}, u32[]{:S(2)}, u32[]{:S(2)}) collective-permute-start(s16[4,136,128]{2,1,0:T(8,128)(2,1)S(1)} %get-tuple-element.28), channel_id=1, source_target_pairs={{0,2},{1,5},{2,0},{3,7},{4,6},{5,1},{6,4},{7,3},{8,10},{9,13},{10,... | collective-permute-start | bytes 417800 | tf_op jit(solution)/shard_map/ppermute | solution.py:357
  15.8 4.7 %collective-permute-start.4 = (bf16[16,3072]{1,0:T(8,128)(2,1)S(1)}, bf16[16,3072]{1,0:T(8,128)(2,1)S(1)}, u32[]{:S(2)}, u32[]{:S(2)}) collective-permute-start(bf16[16,3072]{1,0:T(8,128)(2,1)S(1)} %get-tuple-element.35), channel_id=1, source_target_pairs={{0,1},{1,0},{2,3},{3,2},{4,5},{5,4},{6,7},{7,6},{8,9},{9,8},{10,11... | collective-permute-start | bytes 294920 | tf_op jit(solution)/shard_map/ppermute | solution.py:353
  15.9 4.4 %collective-permute-start.2 = (s16[2,136,128]{2,1,0:T(8,128)(2,1)S(1)}, s16[2,136,128]{2,1,0:T(8,128)(2,1)S(1)}, u32[]{:S(2)}, u32[]{:S(2)}) collective-permute-start(s16[2,136,128]{2,1,0:T(8,128)(2,1)S(1)} %get-tuple-element.31), channel_id=1, source_target_pairs={{0,4},{1,3},{2,6},{3,1},{4,0},{5,7},{6,2},{7,5},{8,12},{9,11},{10,... | collective-permute-start | bytes 208904 | tf_op jit(solution)/shard_map/ppermute | solution.py:357
  20.5 6.0 %collective-permute-start.5 = (s16[2,136,128]{2,1,0:T(8,128)(2,1)S(1)}, s16[2,136,128]{2,1,0:T(8,128)(2,1)S(1)}, u32[]{:S(2)}, u32[]{:S(2)}) collective-permute-start(s16[2,136,128]{2,1,0:T(8,128)(2,1)S(1)} %near_sums.1.refs_0_), channel_id=1, source_target_pairs={{0,8},{1,9},{2,10},{3,11},{4,12},{5,13},{6,14},{7,15},{8,0},{9,1},... | collective-permute-start | bytes 208904 | tf_op jit(solution)/shard_map/ppermute | solution.py:353
  23.1 8.0 %collective-permute-start.8 = (bf16[32,3072]{1,0:T(8,128)(2,1)S(1)}, bf16[32,3072]{1,0:T(8,128)(2,1)S(1)}, u32[]{:S(2)}, u32[]{:S(2)}) collective-permute-start(bf16[32,3072]{1,0:T(8,128)(2,1)S(1)} %pad_maximum_fusion.1), channel_id=1, source_target_pairs={{0,2},{1,5},{2,0},{3,7},{4,6},{5,1},{6,4},{7,3},{8,10},{9,13},{10,... | collective-permute-start | bytes 589832 | tf_op jit(solution)/shard_map/ppermute | solution.py:357
  26.8 16.9 %copy-start.1 = (s32[640]{0:T(1024)S(1)}, s32[640]{0:T(1024)}, u32[]{:S(2)}) copy-start(s32[640]{0:T(1024)} %labels_ref.1) | copy-start | bytes 7684
  26.8 4.4 %collective-permute-start.6 = (s16[2,136,128]{2,1,0:T(8,128)(2,1)S(1)}, s16[2,136,128]{2,1,0:T(8,128)(2,1)S(1)}, u32[]{:S(2)}, u32[]{:S(2)}) collective-permute-start(s16[2,136,128]{2,1,0:T(8,128)(2,1)S(1)} %add_sums.1), channel_id=1, source_target_pairs={{0,2},{1,5},{2,0},{3,7},{4,6},{5,1},{6,4},{7,3},{8,10},{9,13},{10,... | collective-permute-start | bytes 208904 | tf_op jit(solution)/shard_map/ppermute | solution.py:357
  31.2 9.3 %collective-permute-start.9 = (bf16[64,3072]{1,0:T(8,128)(2,1)S(1)}, bf16[64,3072]{1,0:T(8,128)(2,1)S(1)}, u32[]{:S(2)}, u32[]{:S(2)}) collective-permute-start(bf16[64,3072]{1,0:T(8,128)(2,1)S(1)} %constant_dynamic-update-slice_fusion.refs_0_), channel_id=1, source_target_pairs={{0,4},{1,3},{2,6},{3,1},{4,0},{5,7},{6,2},{7,5},{8,12},{9,11},{10,... | collective-permute-start | bytes 1179656 | tf_op jit(solution)/shard_map/ppermute | solution.py:357
  32.6 7.9 %collective-permute-start.7 = (s16[4,136,128]{2,1,0:T(8,128)(2,1)S(1)}, s16[4,136,128]{2,1,0:T(8,128)(2,1)S(1)}, u32[]{:S(2)}, u32[]{:S(2)}) collective-permute-start(s16[4,136,128]{2,1,0:T(8,128)(2,1)S(1)} %pad_add_fusion.1), channel_id=1, source_target_pairs={{0,4},{1,3},{2,6},{3,1},{4,0},{5,7},{6,2},{7,5},{8,12},{9,11},{10,... | collective-permute-start | bytes 417800 | tf_op jit(solution)/shard_map/ppermute | solution.py:357
  40.9 2.8 %collective-permute-start.10 = (bf16[96,4096]{1,0:T(8,128)(2,1)S(1)}, bf16[96,4096]{1,0:T(8,128)(2,1)S(1)}, u32[]{:S(2)}, u32[]{:S(2)}) collective-permute-start(bf16[96,4096]{1,0:T(8,128)(2,1)S(1)} %picked_rows.1.x_ref.x_own), channel_id=1, source_target_pairs={{0,1},{1,0},{2,3},{3,2},{4,5},{5,4},{6,7},{7,6},{8,9},{9,8},{10,11... | collective-permute-start | bytes 2359304 | tf_op jit(solution)/shard_map/ppermute | solution.py:353
  41.0 2.6 %collective-permute-start.11 = (s16[8,136,128]{2,1,0:T(8,128)(2,1)S(1)}, s16[8,136,128]{2,1,0:T(8,128)(2,1)S(1)}, u32[]{:S(2)}, u32[]{:S(2)}) collective-permute-start(s16[8,136,128]{2,1,0:T(8,128)(2,1)S(1)} %pad_add_fusion.code_ref), channel_id=1, source_target_pairs={{0,1},{1,0},{2,3},{3,2},{4,5},{5,4},{6,7},{7,6},{8,9},{9,8},{10,11... | collective-permute-start | bytes 835592 | tf_op jit(solution)/shard_map/ppermute | solution.py:353

commit v19 on v18

--- a/solution.py
+++ b/solution.py
@@ -51,7 +51,7 @@
 
 
 def sums_kernel(
-    labels_hbm, pick_hbm, feat_hbm, feat_ref, send_ref, keep_ref, held, labels_ref, pick_ref, left, sems, *, n_ex
+    labels_hbm, pick_hbm, feat_hbm, feat_ref, send_ref, keep_ref, labels_ref, pick_ref, left, sems, *, n_ex
 ):
     rows, full = feat_ref.shape
     steps, classes = pick_ref.shape
@@ -108,20 +108,21 @@
         k = i % groups
         ref = send_ref if i < groups else keep_ref
         ref[k * classes : (k + 1) * classes, :] = both[:classes]
-        held[:, columns[i]] = both[classes : classes + 8]
-
-
-def pack_kernel(held, rows_ref, *, steps):
-    half = held.shape[1] // 2
+        ref[base + 8 + 8 * k : base + 16 + 8 * k, :] = both[classes : classes + 8]
+
+
+def pack_kernel(keep_ref, got_ref, rows_ref, *, steps, start):
+    lines, main = rows_ref.shape
     used = steps * slots
-    main = rows_ref.shape[2]
-    core = lax.axis_index("ex") % 2
-    for part, side in ((0, core), (1, 1 - core)):
-        h = held[:, pl.ds(pl.multiple_of(side * half, half), half)]
-        lines = [h[:used, :main]]
+    count = (keep_ref.shape[0] - start) // 8
+    halves = []
+    for ref in (keep_ref, got_ref):
+        halves.append(jnp.concatenate([ref[start + 8 * k : start + 8 * k + 8, :] for k in range(count)], axis=1))
+    out = [h[:used, :main] for h in halves]
+    for h in halves:
         for q in range(slots):
-            lines.append(jnp.concatenate([h[q * steps + u : q * steps + u + 1, main:] for u in range(steps)], axis=1))
-        rows_ref[part] = jnp.concatenate(lines, axis=0).astype(bf16)
+            out.append(jnp.concatenate([h[q * steps + u : q * steps + u + 1, main:] for u in range(steps)], axis=1))
+    rows_ref[...] = jnp.concatenate(out, axis=0).astype(bf16)
 
 
 def near_id(step, parity):
@@ -245,10 +246,16 @@
         far = far + (((away >> b) & 1) << (bits - 1 - b))
     by_y, by_z = (away >> 1) & 1, (away >> 2) & 1
     near = jnp.where(device % 2 == 0, by_y + 2 * by_z, by_z + 2 * by_y)
-    spot = (2 * near + (away & 1)) * (n_ex // 8) + far
+    others = n_ex // 8 - 1
+    spot = jnp.where(far == 0, near, 3 + near * others + far)
+    side = away & 1
+    used = steps * slots
     step = lax.broadcasted_iota(jnp.int32, pick.shape, 0)
     line = lax.broadcasted_iota(jnp.int32, (lines, classes), 0)
-    where = spot * 8 + (slots * steps + rank if tail else rank * steps + step)
+    if tail:
+        where = spot * 16 + 2 * used + side * slots + rank
+    else:
+        where = spot * 16 + side * used + rank * steps + step
     hits = [jnp.where(line == where[s : s + 1, :], 1.0, 0.0) for s in range(steps)]
     pad = jnp.zeros((lines, 128 - steps * classes), f32)
     one_ref[...] = jnp.transpose(jnp.concatenate(hits + [pad], axis=1))[: steps * classes].astype(bf16)
@@ -346,7 +353,7 @@
     vmem = pl.BlockSpec(memory_space=pltpu.VMEM)
     hbm = pl.BlockSpec(memory_space=pltpu.HBM)
     anywhere = pl.BlockSpec(memory_space=pl.ANY)
-    half = jax.ShapeDtypeStruct((groups * classes + 8, width), f32)
+    half = jax.ShapeDtypeStruct((groups * (classes + 8) + 8, width), f32)
     code = jax.ShapeDtypeStruct((groups // 4, classes * (width // 128) + 8, 128), jnp.int16)
 
     def swap(x, mask):
@@ -359,11 +366,11 @@
     def after(x, *others):
         return lax.optimization_barrier((x,) + others)[0]
 
-    feat, send, keep, held = pl.pallas_call(
+    feat, send, keep = pl.pallas_call(
         functools.partial(sums_kernel, n_ex=n_ex),
         in_specs=[hbm] * 3,
-        out_specs=[vmem] * 4,
-        out_shape=[pltpu.VMEM((rows, full), bf16), half, half, jax.ShapeDtypeStruct((8, full), f32)],
+        out_specs=[vmem] * 3,
+        out_shape=[pltpu.VMEM((rows, full), bf16), half, half],
         scratch_shapes=[
             pltpu.VMEM(labels.shape, jnp.int32),
             pltpu.VMEM(pick_index.shape, jnp.int32),
@@ -389,6 +396,8 @@
     got = swap(send, 1)
     far = groups // 4
 
+    weight = pl.CostEstimate(flops=10**10, bytes_accessed=10**8, transcendentals=0)
+
     def call(kernel, name, outs, *args):
         return pl.pallas_call(
             functools.partial(kernel, classes=classes),
@@ -396,6 +405,7 @@
             out_specs=[vmem] * len(outs),
             out_shape=outs,
             compiler_params=limit,
+            cost_estimate=weight,
             name=name,
         )(*args)
 
@@ -404,22 +414,24 @@
 
     two = jax.ShapeDtypeStruct((2 * far,) + code.shape[1:], jnp.int16)
     hold, tile, pair_code = call(pair_kernel, "pair_sums", held_sums(2 * far) + [two], keep, got)
-    packed = pl.pallas_call(
-        functools.partial(pack_kernel, steps=steps),
-        in_specs=[vmem],
+    here = pl.pallas_call(
+        functools.partial(pack_kernel, steps=steps, start=groups * classes + 8),
+        in_specs=[vmem] * 2,
         out_specs=vmem,
-        out_shape=jax.ShapeDtypeStruct((2, 8, main), bf16),
+        out_shape=jax.ShapeDtypeStruct((16, main), bf16),
         compiler_params=limit,
         name="pack_rows",
-    )(held)
+    )(keep, after(got, pair_code))
+    there = []
     for mask in reversed(far_masks):
-        packed = jnp.concatenate([packed, swap(packed, mask)], axis=1)
+        so_far = jnp.concatenate([here] + there, axis=0) if there else here
+        there.append(swap(so_far, mask))
 
     got = cross(pair_code, True)
     hold, tile, half_code = call(halve_kernel, "half_sums", held_sums(far) + [code], hold, tile, got)
+    here_next = cross(after(here, half_code), True)
     got = cross(half_code, False)
-    given = swap(after(packed[1], half_code), 1)
-    (part_sum,) = call(near_kernel, "near_sums", [code], hold, tile, after(got, packed))
+    (part_sum,) = call(near_kernel, "near_sums", [code], hold, tile, after(got, there))
 
     def select(tail, *others):
         return pl.pallas_call(
@@ -432,22 +444,24 @@
         )(after(pick_index, *others))
 
     rest = select(True, pair_code)
-    near_sum = after(part_sum, rest, given)
+    one = select(False, half_code)
+    near_sum = after(part_sum, rest, one)
     more = swap(near_sum, far_masks[0])
-    one = select(False, near_sum)
+    here_all = jnp.concatenate([after(here, near_sum), here_next], axis=0)
+    here_far = cross(here_all, False)
     part_sum = add([near_sum, more], len(far_masks) == 1)
     for mask in far_masks[1:]:
         part_sum = add([part_sum, swap(part_sum, mask)], mask == far_masks[-1])
-    near = jnp.concatenate([after(packed[0], one), given], axis=0)
+    there = after(jnp.concatenate(there, axis=0) if len(there) > 1 else there[0], more)
     got = cross(part_sum, True)
     pair = jnp.concatenate([part_sum, got], axis=0)
     own_parts = [pair, cross(pair, False)]
-    lines = jnp.concatenate([near, after(cross(near, True), got)], axis=0)
-    parts = [lines, cross(lines, False)]
+    there_all = jnp.concatenate([there, cross(there, True)], axis=0)
+    parts = [here_all, here_far, there_all, cross(there_all, False)]
 
     x = pl.pallas_call(
         functools.partial(picked_kernel, steps=steps),
-        in_specs=[vmem] * 4,
+        in_specs=[vmem] * 6,
         out_specs=vmem,
         out_shape=jax.ShapeDtypeStruct((total, full // 2), bf16),
         scratch_shapes=[pltpu.VMEM((n_ex * 8, main), bf16)],

time: 47 us -> 45.8 us (0.974)
  waiting for transfers between devices: 18.2 us -> 15.7 us
  starting transfers between devices: 15.4 us -> 16.7 us
    ppermute x6 -> x8, starting transfers between devices: 8.28 us -> 11.2 us  [cross(): return lax.ppermute(x, 'ex', [(d, d ^ masks[d % 2]) for d in range(n_ex)])]
    ppermute x6 -> x5, starting transfers between devices: 7.15 us -> 5.5 us  [swap(): return lax.ppermute(x, 'ex', [(d, d ^ mask) for d in range(n_ex)])]
    ppermute x6 -> x8, waiting for transfers between devices: 12.6 us -> 11.1 us  [cross(): return lax.ppermute(x, 'ex', [(d, d ^ masks[d % 2]) for d in range(n_ex)])]
    ppermute x6 -> x5, waiting for transfers between devices: 5.56 us -> 4.57 us  [swap(): return lax.ppermute(x, 'ex', [(d, d ^ mask) for d in range(n_ex)])]
  transfers between devices with their start and end apart: 12 -> 13, of which waited for: 5 -> 8; matrix products, arithmetic and copies ran while one was open for 0% -> 0% of each run, Pallas kernels for 7% -> 8%
where the time goes in v19:
time: 45.8 us; the launch traced here: 45.6 us
  starting transfers between devices  16.7 us (36%)
  waiting for transfers between devices  15.7 us (34%)
  Pallas kernels  12.4 us (27%)
  between operations  0.77 us (2%)
    ppermute x8, starting transfers between devices, cross(): return lax.ppermute(x, 'ex', [(d, d ^ masks[d % 2]) for d in range(n_ex)])  11.2 us
    ppermute x8, waiting for transfers between devices, cross(): return lax.ppermute(x, 'ex', [(d, d ^ masks[d % 2]) for d in range(n_ex)])  11.1 us
    ppermute x5, starting transfers between devices, swap(): return lax.ppermute(x, 'ex', [(d, d ^ mask) for d in range(n_ex)])  5.5 us
    pallas_call x1, Pallas kernels, on_device(): pl.pallas_call(functools.partial(sums_kernel, n_ex=n_ex), in_specs=[hbm]...  5.02 us
    ppermute x5, waiting for transfers between devices, swap(): return lax.ppermute(x, 'ex', [(d, d ^ mask) for d in range(n_ex)])  4.57 us
    pallas_call x1, Pallas kernels, on_device(): pl.pallas_call(functools.partial(pursuit_kernel, steps=steps, scale=1.0 /...  3.19 us
    pallas_call x1, Pallas kernels, on_device(): pl.pallas_call(functools.partial(half_kernel, classes=classes), in_specs=...  2.06 us
  transfers between devices with their start and end apart: 13, of which 8 were waited for; matrix products, arithmetic and copies ran while one was open for 0% of the time, Pallas kernels for 8%

profile of v19, /device:TPU:0, one launch (start us, length us, event | category | flops | bytes accessed | tf_op | source)
XLA Modules:
  0.0 45.6 jit_solution(2580723286135247937)
XLA Ops:
  0.6 5.0 %class_sums.1 = (bf16[640,8192]{1,0:T(8,128)(2,1)S(1)}, f32[328,512]{1,0:T(8,128)S(1)}, f32[328,512]{1,0:T(8,128)S(1)}) custom-call(s32[640]{0:T(1024)} %labels_ref.1, s32[3,32]{1,0:T(4,128)} %pick_ref.1, bf16[640,8192]{1,0:T(8,128)(2,1)} %feat_hbm.1), custom_call_target="tpu_custom_call" | custom-call | tf_op jit(solution)/shard_map/class_sums/pallas_call | solution.py:369
  5.7 0.5 %collective-permute-start = (f32[328,512]{1,0:T(8,128)S(1)}, f32[328,512]{1,0:T(8,128)S(1)}, u32[]{:S(2)}, u32[]{:S(2)}) collective-permute-start(f32[328,512]{1,0:T(8,128)S(1)} %get-tuple-element.25), channel_id=1, source_target_pairs={{0,1},{1,0},{2,3},{3,2},{4,5},{5,4},{6,7},{7,6},{8,9},{9,8},{10,11... | collective-permute-start | bytes 2015240 | tf_op jit(solution)/shard_map/ppermute | solution.py:360
  6.2 1.7 %collective-permute-done.got_ref = f32[328,512]{1,0:T(8,128)S(1)} collective-permute-done((f32[328,512]{1,0:T(8,128)S(1)}, f32[328,512]{1,0:T(8,128)S(1)}, u32[]{:S(2)}, u32[]{:S(2)}) %collective-permute-start) | collective-permute-done | bytes 671776 | tf_op jit(solution)/shard_map/ppermute | solution.py:360
  7.9 0.2 pair_sums.1
  8.1 3.0 %collective-permute-start.1 = (s16[4,136,128]{2,1,0:T(8,128)(2,1)S(1)}, s16[4,136,128]{2,1,0:T(8,128)(2,1)S(1)}, u32[]{:S(2)}, u32[]{:S(2)}) collective-permute-start(s16[4,136,128]{2,1,0:T(8,128)(2,1)S(1)} %get-tuple-element.28), channel_id=1, source_target_pairs={{0,2},{1,5},{2,0},{3,7},{4,6},{5,1},{6,4},{7,3},{8,10},{9,13},{10,... | collective-permute-start | bytes 417800 | tf_op jit(solution)/shard_map/ppermute | solution.py:364
  11.1 2.7 %collective-permute-start.3 = (bf16[16,3072]{1,0:T(8,128)(2,1)S(1)}, bf16[16,3072]{1,0:T(8,128)(2,1)S(1)}, u32[]{:S(2)}, u32[]{:S(2)}) collective-permute-start(bf16[16,3072]{1,0:T(8,128)(2,1)S(1)} %pack_rows.1), channel_id=1, source_target_pairs={{0,8},{1,9},{2,10},{3,11},{4,12},{5,13},{6,14},{7,15},{8,0},{9,1},... | collective-permute-start | bytes 294920 | tf_op jit(solution)/shard_map/ppermute | solution.py:360
  13.8 0.3 collective-permute-done.1.got_ref
  14.1 0.3 half_sums.1
  14.4 2.1 %collective-permute-start.2 = (s16[2,136,128]{2,1,0:T(8,128)(2,1)S(1)}, s16[2,136,128]{2,1,0:T(8,128)(2,1)S(1)}, u32[]{:S(2)}, u32[]{:S(2)}) collective-permute-start(s16[2,136,128]{2,1,0:T(8,128)(2,1)S(1)} %get-tuple-element.29), channel_id=1, source_target_pairs={{0,4},{1,3},{2,6},{3,1},{4,0},{5,7},{6,2},{7,5},{8,12},{9,11},{10,... | collective-permute-start | bytes 208904 | tf_op jit(solution)/shard_map/ppermute | solution.py:364
  16.5 0.3 select_tails.1.rest_ref
  16.9 0.3 select_rows.1.one_ref
  17.2 1.6 %collective-permute-start.7 = (bf16[16,3072]{1,0:T(8,128)(2,1)S(1)}, bf16[16,3072]{1,0:T(8,128)(2,1)S(1)}, u32[]{:S(2)}, u32[]{:S(2)}) collective-permute-start(bf16[16,3072]{1,0:T(8,128)(2,1)S(1)} %pack_rows.1), channel_id=1, source_target_pairs={{0,2},{1,5},{2,0},{3,7},{4,6},{5,1},{6,4},{7,3},{8,10},{9,13},{10,... | collective-permute-start | bytes 294920 | tf_op jit(solution)/shard_map/ppermute | solution.py:364
  18.8 0.1 collective-permute-done.3
  18.9 1.3 %collective-permute-done.2.got_ref = s16[2,136,128]{2,1,0:T(8,128)(2,1)S(1)} collective-permute-done((s16[2,136,128]{2,1,0:T(8,128)(2,1)S(1)}, s16[2,136,128]{2,1,0:T(8,128)(2,1)S(1)}, u32[]{:S(2)}, u32[]{:S(2)}) %collective-permute-start.2) | collective-permute-done | bytes 69664 | tf_op jit(solution)/shard_map/ppermute | solution.py:364
  20.2 0.3 near_sums.1.refs_0_
  20.5 1.7 %collective-permute-start.4 = (s16[2,136,128]{2,1,0:T(8,128)(2,1)S(1)}, s16[2,136,128]{2,1,0:T(8,128)(2,1)S(1)}, u32[]{:S(2)}, u32[]{:S(2)}) collective-permute-start(s16[2,136,128]{2,1,0:T(8,128)(2,1)S(1)} %near_sums.1.refs_0_), channel_id=1, source_target_pairs={{0,8},{1,9},{2,10},{3,11},{4,12},{5,13},{6,14},{7,15},{8,0},{9,1},... | collective-permute-start | bytes 208904 | tf_op jit(solution)/shard_map/ppermute | solution.py:360
  22.2 1.6 %collective-permute-start.8 = (bf16[32,3072]{1,0:T(8,128)(2,1)S(1)}, bf16[32,3072]{1,0:T(8,128)(2,1)S(1)}, u32[]{:S(2)}, u32[]{:S(2)}) collective-permute-start(bf16[32,3072]{1,0:T(8,128)(2,1)S(1)} %constant_dynamic-update-slice_fusion.refs_0_), channel_id=1, source_target_pairs={{0,4},{1,3},{2,6},{3,1},{4,0},{5,7},{6,2},{7,5},{8,12},{9,11},{10,... | collective-permute-start | bytes 589832 | tf_op jit(solution)/shard_map/ppermute | solution.py:364
  23.8 2.8 %collective-permute-done.4.refs_1_ = s16[2,136,128]{2,1,0:T(8,128)(2,1)S(1)} collective-permute-done((s16[2,136,128]{2,1,0:T(8,128)(2,1)S(1)}, s16[2,136,128]{2,1,0:T(8,128)(2,1)S(1)}, u32[]{:S(2)}, u32[]{:S(2)}) %collective-permute-start.4) | collective-permute-done | bytes 69664 | tf_op jit(solution)/shard_map/ppermute | solution.py:360
  26.6 1.4 %collective-permute-start.9 = (bf16[16,3072]{1,0:T(8,128)(2,1)S(1)}, bf16[16,3072]{1,0:T(8,128)(2,1)S(1)}, u32[]{:S(2)}, u32[]{:S(2)}) collective-permute-start(bf16[16,3072]{1,0:T(8,128)(2,1)S(1)} %collective-permute-done.3), channel_id=1, source_target_pairs={{0,2},{1,5},{2,0},{3,7},{4,6},{5,1},{6,4},{7,3},{8,10},{9,13},{10,... | collective-permute-start | bytes 294920 | tf_op jit(solution)/shard_map/ppermute | solution.py:364
  28.0 0.3 add_sums.1
  28.3 0.7 %collective-permute-start.5 = (s16[2,136,128]{2,1,0:T(8,128)(2,1)S(1)}, s16[2,136,128]{2,1,0:T(8,128)(2,1)S(1)}, u32[]{:S(2)}, u32[]{:S(2)}) collective-permute-start(s16[2,136,128]{2,1,0:T(8,128)(2,1)S(1)} %add_sums.1), channel_id=1, source_target_pairs={{0,2},{1,5},{2,0},{3,7},{4,6},{5,1},{6,4},{7,3},{8,10},{9,13},{10,... | collective-permute-start | bytes 208904 | tf_op jit(solution)/shard_map/ppermute | solution.py:364
  29.0 3.0 %collective-permute-done.9 = bf16[16,3072]{1,0:T(8,128)(2,1)S(1)} collective-permute-done((bf16[16,3072]{1,0:T(8,128)(2,1)S(1)}, bf16[16,3072]{1,0:T(8,128)(2,1)S(1)}, u32[]{:S(2)}, u32[]{:S(2)}) %collective-permute-start.9) | collective-permute-done | bytes 98336 | tf_op jit(solution)/shard_map/ppermute | solution.py:364
  32.0 0.1 collective-permute-start.10
  32.1 1.4 %collective-permute-done.5 = s16[2,136,128]{2,1,0:T(8,128)(2,1)S(1)} collective-permute-done((s16[2,136,128]{2,1,0:T(8,128)(2,1)S(1)}, s16[2,136,128]{2,1,0:T(8,128)(2,1)S(1)}, u32[]{:S(2)}, u32[]{:S(2)}) %collective-permute-start.5) | collective-permute-done | bytes 69664 | tf_op jit(solution)/shard_map/ppermute | solution.py:364
  33.5 0.7 %collective-permute-start.6 = (s16[4,136,128]{2,1,0:T(8,128)(2,1)S(1)}, s16[4,136,128]{2,1,0:T(8,128)(2,1)S(1)}, u32[]{:S(2)}, u32[]{:S(2)}) collective-permute-start(s16[4,136,128]{2,1,0:T(8,128)(2,1)S(1)} %pad_add_fusion.1), channel_id=1, source_target_pairs={{0,4},{1,3},{2,6},{3,1},{4,0},{5,7},{6,2},{7,5},{8,12},{9,11},{10,... | collective-permute-start | bytes 417800 | tf_op jit(solution)/shard_map/ppermute | solution.py:364
  34.2 5.1 %collective-permute-done.6 = s16[4,136,128]{2,1,0:T(8,128)(2,1)S(1)} collective-permute-done((s16[4,136,128]{2,1,0:T(8,128)(2,1)S(1)}, s16[4,136,128]{2,1,0:T(8,128)(2,1)S(1)}, u32[]{:S(2)}, u32[]{:S(2)}) %collective-permute-start.6) | collective-permute-done | bytes 139296 | tf_op jit(solution)/shard_map/ppermute | solution.py:364
  39.2 0.4 picked_rows.1.x_ref.x_own
  39.6 0.1 collective-permute-start.11
  39.8 0.6 %collective-permute-start.12 = (s16[8,136,128]{2,1,0:T(8,128)(2,1)S(1)}, s16[8,136,128]{2,1,0:T(8,128)(2,1)S(1)}, u32[]{:S(2)}, u32[]{:S(2)}) collective-permute-start(s16[8,136,128]{2,1,0:T(8,128)(2,1)S(1)} %pad_add_fusion.code_ref), channel_id=1, source_target_pairs={{0,1},{1,0},{2,3},{3,2},{4,5},{5,4},{6,7},{7,6},{8,9},{9,8},{10,11... | collective-permute-start | bytes 835592 | tf_op jit(solution)/shard_map/ppermute | solution.py:360
  40.3 2.1 %own_half_products.1 = (f32[96,640]{1,0:T(8,128)S(1)}, f32[128,96]{1,0:T(8,128)S(1)}, f32[32,4096]{1,0:T(8,128)S(1)}) custom-call(bf16[640,8192]{1,0:T(8,128)(2,1)S(1)} %get-tuple-element.23.feat_ref, s16[8,136,128]{2,1,0:T(8,128)(2,1)S(1)} %pad_add_fusion.code_ref, bf16[96,4096]{1,0:T(8,128)(2,1)S(1)} %picked_rows.1.x_ref.x_own), custom_call_target="tpu_custom_call" | custom-call | tf_op jit(solution)/shard_map/own_half_products/pallas_call | solution.py:476
  42.4 0.0 collective-permute-done.12.code_ref
  42.4 3.2 %pursuit.1 = (f32[3,640]{1,0:T(4,128)}, f32[32,8192]{1,0:T(8,128)}) custom-call(s32[640]{0:T(1024)S(1)} %copy-done.1, bf16[640,8192]{1,0:T(8,128)(2,1)S(1)} %get-tuple-element.23.feat_ref, bf16[96,4096]{1,0:T(8,128)(2,1)S(1)} %picked_rows.1.x_ref.x_own, bf16[96,4096]{1,0:T(8,128)(2,1)S(1)} %collective-permute-done.11.x_twin, ...), custom_call_target="tpu_custom_call" | custom-call | tf_op jit(solution)/shard_map/pursuit/pallas_call | solution.py:490
  (15 shorter events, 0.1 us)
Async XLA Ops:
  5.7 2.3 %collective-permute-start = (f32[328,512]{1,0:T(8,128)S(1)}, f32[328,512]{1,0:T(8,128)S(1)}, u32[]{:S(2)}, u32[]{:S(2)}) collective-permute-start(f32[328,512]{1,0:T(8,128)S(1)} %get-tuple-element.25), channel_id=1, source_target_pairs={{0,1},{1,0},{2,3},{3,2},{4,5},{5,4},{6,7},{7,6},{8,9},{9,8},{10,11... | collective-permute-start | bytes 2015240 | tf_op jit(solution)/shard_map/ppermute | solution.py:360
  8.1 6.0 %collective-permute-start.1 = (s16[4,136,128]{2,1,0:T(8,128)(2,1)S(1)}, s16[4,136,128]{2,1,0:T(8,128)(2,1)S(1)}, u32[]{:S(2)}, u32[]{:S(2)}) collective-permute-start(s16[4,136,128]{2,1,0:T(8,128)(2,1)S(1)} %get-tuple-element.28), channel_id=1, source_target_pairs={{0,2},{1,5},{2,0},{3,7},{4,6},{5,1},{6,4},{7,3},{8,10},{9,13},{10,... | collective-permute-start | bytes 417800 | tf_op jit(solution)/shard_map/ppermute | solution.py:364
  11.1 7.8 %collective-permute-start.3 = (bf16[16,3072]{1,0:T(8,128)(2,1)S(1)}, bf16[16,3072]{1,0:T(8,128)(2,1)S(1)}, u32[]{:S(2)}, u32[]{:S(2)}) collective-permute-start(bf16[16,3072]{1,0:T(8,128)(2,1)S(1)} %pack_rows.1), channel_id=1, source_target_pairs={{0,8},{1,9},{2,10},{3,11},{4,12},{5,13},{6,14},{7,15},{8,0},{9,1},... | collective-permute-start | bytes 294920 | tf_op jit(solution)/shard_map/ppermute | solution.py:360
  14.1 2.4 %copy-start = (s32[3,32]{1,0:T(4,128)S(1)}, s32[3,32]{1,0:T(4,128)}, u32[]{:S(2)}) copy-start(s32[3,32]{1,0:T(4,128)} %pick_ref.1) | copy-start | bytes 1156
  14.4 5.8 %collective-permute-start.2 = (s16[2,136,128]{2,1,0:T(8,128)(2,1)S(1)}, s16[2,136,128]{2,1,0:T(8,128)(2,1)S(1)}, u32[]{:S(2)}, u32[]{:S(2)}) collective-permute-start(s16[2,136,128]{2,1,0:T(8,128)(2,1)S(1)} %get-tuple-element.29), channel_id=1, source_target_pairs={{0,4},{1,3},{2,6},{3,1},{4,0},{5,7},{6,2},{7,5},{8,12},{9,11},{10,... | collective-permute-start | bytes 208904 | tf_op jit(solution)/shard_map/ppermute | solution.py:364
  17.2 5.0 %collective-permute-start.7 = (bf16[16,3072]{1,0:T(8,128)(2,1)S(1)}, bf16[16,3072]{1,0:T(8,128)(2,1)S(1)}, u32[]{:S(2)}, u32[]{:S(2)}) collective-permute-start(bf16[16,3072]{1,0:T(8,128)(2,1)S(1)} %pack_rows.1), channel_id=1, source_target_pairs={{0,2},{1,5},{2,0},{3,7},{4,6},{5,1},{6,4},{7,3},{8,10},{9,13},{10,... | collective-permute-start | bytes 294920 | tf_op jit(solution)/shard_map/ppermute | solution.py:364
  20.5 6.1 %collective-permute-start.4 = (s16[2,136,128]{2,1,0:T(8,128)(2,1)S(1)}, s16[2,136,128]{2,1,0:T(8,128)(2,1)S(1)}, u32[]{:S(2)}, u32[]{:S(2)}) collective-permute-start(s16[2,136,128]{2,1,0:T(8,128)(2,1)S(1)} %near_sums.1.refs_0_), channel_id=1, source_target_pairs={{0,8},{1,9},{2,10},{3,11},{4,12},{5,13},{6,14},{7,15},{8,0},{9,1},... | collective-permute-start | bytes 208904 | tf_op jit(solution)/shard_map/ppermute | solution.py:360
  22.2 17.0 %collective-permute-start.8 = (bf16[32,3072]{1,0:T(8,128)(2,1)S(1)}, bf16[32,3072]{1,0:T(8,128)(2,1)S(1)}, u32[]{:S(2)}, u32[]{:S(2)}) collective-permute-start(bf16[32,3072]{1,0:T(8,128)(2,1)S(1)} %constant_dynamic-update-slice_fusion.refs_0_), channel_id=1, source_target_pairs={{0,4},{1,3},{2,6},{3,1},{4,0},{5,7},{6,2},{7,5},{8,12},{9,11},{10,... | collective-permute-start | bytes 589832 | tf_op jit(solution)/shard_map/ppermute | solution.py:364
  26.6 5.4 %collective-permute-start.9 = (bf16[16,3072]{1,0:T(8,128)(2,1)S(1)}, bf16[16,3072]{1,0:T(8,128)(2,1)S(1)}, u32[]{:S(2)}, u32[]{:S(2)}) collective-permute-start(bf16[16,3072]{1,0:T(8,128)(2,1)S(1)} %collective-permute-done.3), channel_id=1, source_target_pairs={{0,2},{1,5},{2,0},{3,7},{4,6},{5,1},{6,4},{7,3},{8,10},{9,13},{10,... | collective-permute-start | bytes 294920 | tf_op jit(solution)/shard_map/ppermute | solution.py:364
  28.3 14.1 %copy-start.1 = (s32[640]{0:T(1024)S(1)}, s32[640]{0:T(1024)}, u32[]{:S(2)}) copy-start(s32[640]{0:T(1024)} %labels_ref.1) | copy-start | bytes 7684
  28.3 5.2 %collective-permute-start.5 = (s16[2,136,128]{2,1,0:T(8,128)(2,1)S(1)}, s16[2,136,128]{2,1,0:T(8,128)(2,1)S(1)}, u32[]{:S(2)}, u32[]{:S(2)}) collective-permute-start(s16[2,136,128]{2,1,0:T(8,128)(2,1)S(1)} %add_sums.1), channel_id=1, source_target_pairs={{0,2},{1,5},{2,0},{3,7},{4,6},{5,1},{6,4},{7,3},{8,10},{9,13},{10,... | collective-permute-start | bytes 208904 | tf_op jit(solution)/shard_map/ppermute | solution.py:364
  32.0 7.2 %collective-permute-start.10 = (bf16[32,3072]{1,0:T(8,128)(2,1)S(1)}, bf16[32,3072]{1,0:T(8,128)(2,1)S(1)}, u32[]{:S(2)}, u32[]{:S(2)}) collective-permute-start(bf16[32,3072]{1,0:T(8,128)(2,1)S(1)} %constant_dynamic-update-slice_fusion.2.refs_2_), channel_id=1, source_target_pairs={{0,4},{1,3},{2,6},{3,1},{4,0},{5,7},{6,2},{7,5},{8,12},{9,11},{10,... | collective-permute-start | bytes 589832 | tf_op jit(solution)/shard_map/ppermute | solution.py:364
  33.5 5.7 %collective-permute-start.6 = (s16[4,136,128]{2,1,0:T(8,128)(2,1)S(1)}, s16[4,136,128]{2,1,0:T(8,128)(2,1)S(1)}, u32[]{:S(2)}, u32[]{:S(2)}) collective-permute-start(s16[4,136,128]{2,1,0:T(8,128)(2,1)S(1)} %pad_add_fusion.1), channel_id=1, source_target_pairs={{0,4},{1,3},{2,6},{3,1},{4,0},{5,7},{6,2},{7,5},{8,12},{9,11},{10,... | collective-permute-start | bytes 417800 | tf_op jit(solution)/shard_map/ppermute | solution.py:364
  39.6 2.8 %collective-permute-start.11 = (bf16[96,4096]{1,0:T(8,128)(2,1)S(1)}, bf16[96,4096]{1,0:T(8,128)(2,1)S(1)}, u32[]{:S(2)}, u32[]{:S(2)}) collective-permute-start(bf16[96,4096]{1,0:T(8,128)(2,1)S(1)} %picked_rows.1.x_ref.x_own), channel_id=1, source_target_pairs={{0,1},{1,0},{2,3},{3,2},{4,5},{5,4},{6,7},{7,6},{8,9},{9,8},{10,11... | collective-permute-start | bytes 2359304 | tf_op jit(solution)/shard_map/ppermute | solution.py:360
  39.8 2.6 %collective-permute-start.12 = (s16[8,136,128]{2,1,0:T(8,128)(2,1)S(1)}, s16[8,136,128]{2,1,0:T(8,128)(2,1)S(1)}, u32[]{:S(2)}, u32[]{:S(2)}) collective-permute-start(s16[8,136,128]{2,1,0:T(8,128)(2,1)S(1)} %pad_add_fusion.code_ref), channel_id=1, source_target_pairs={{0,1},{1,0},{2,3},{3,2},{4,5},{5,4},{6,7},{7,6},{8,9},{9,8},{10,11... | collective-permute-start | bytes 835592 | tf_op jit(solution)/shard_map/ppermute | solution.py:360

commit v20 on v12

--- a/solution.py
+++ b/solution.py
@@ -320,6 +320,10 @@
     half = jax.ShapeDtypeStruct((groups * classes + 8, width), f32)
     code = jax.ShapeDtypeStruct((groups // 4, classes * (width // 128) + 8, 128), jnp.int16)
 
+    def near_swaps(x):
+        diagonal_part, by_y = swap(x[3], 6), swap(x[2], 2)
+        return [swap(x[1], 4), by_y, diagonal_part]
+
     def swap(x, mask):
         return lax.ppermute(x, "ex", [(d, d ^ mask) for d in range(n_ex)])
 
@@ -372,8 +376,8 @@
     for mask in reversed(far_masks):
         packed = jnp.concatenate([packed, swap(packed, mask)], axis=1)
 
-    near_codes = [swap(c, m) for c, m in zip(codes[1:], near_masks[1:])]
-    part_sum = add([codes[0], after(near_codes[0], packed)] + near_codes[1:], False)
+    near_codes = near_swaps(codes)
+    part_sum = add([codes[0], after(near_codes[2], packed), near_codes[1], near_codes[0]], False)
 
     def select(tail, *others):
         return pl.pallas_call(
@@ -393,9 +397,8 @@
         more = swap(part_sum, mask)
         part_sum = add([part_sum, more], mask == far_masks[-1])
     near = jnp.concatenate([after(packed[0], more), given], axis=0)
-    parts = [near] + [swap(near, m) for m in near_masks[1:]]
-    own_parts = [part_sum] + [swap(part_sum, m) for m in near_masks[1:3]]
-    own_parts.append(swap(after(part_sum, parts[1]), near_masks[3]))
+    parts = [near] + near_swaps([near] * 4)
+    own_parts = [part_sum] + near_swaps([None, after(part_sum, parts[1]), part_sum, part_sum])
 
     x = pl.pallas_call(
         functools.partial(picked_kernel, steps=steps),

time: 43.6 us -> 43.8 us (level)
  starting transfers between devices: 14.3 us -> 15.4 us
  waiting for transfers between devices: 16.2 us -> 15.3 us
    ppermute x15, starting transfers between devices: 14.3 us -> 15.4 us  [swap(): return lax.ppermute(x, 'ex', [(d, d ^ mask) for d in range(n_ex)])]
    ppermute x15, waiting for transfers between devices: 16.2 us -> 15.3 us  [swap(): return lax.ppermute(x, 'ex', [(d, d ^ mask) for d in range(n_ex)])]
  transfers between devices with their start and end apart: 15 -> 15, of which waited for: 9 -> 8; matrix products, arithmetic and copies ran while one was open for 0% -> 0% of each run, Pallas kernels for 9% -> 9%
where the time goes in v20:
time: 43.8 us; the launch traced here: 43.7 us
  starting transfers between devices  15.4 us (35%)
  waiting for transfers between devices  15.3 us (35%)
  Pallas kernels  12.1 us (28%)
  between operations  0.8 us (2%)
    ppermute x15, starting transfers between devices, swap(): return lax.ppermute(x, 'ex', [(d, d ^ mask) for d in range(n_ex)])  15.4 us
    ppermute x15, waiting for transfers between devices, swap(): return lax.ppermute(x, 'ex', [(d, d ^ mask) for d in range(n_ex)])  15.3 us
    pallas_call x1, Pallas kernels, on_device(): pl.pallas_call(functools.partial(sums_kernel, n_ex=n_ex), in_specs=[hbm]...  5.02 us
    pallas_call x1, Pallas kernels, on_device(): pl.pallas_call(functools.partial(pursuit_kernel, steps=steps, scale=1.0 /...  3.19 us
    pallas_call x1, Pallas kernels, on_device(): pl.pallas_call(functools.partial(half_kernel, classes=classes), in_specs=...  2.06 us
  transfers between devices with their start and end apart: 15, of which 8 were waited for; matrix products, arithmetic and copies ran while one was open for 0% of the time, Pallas kernels for 9%

profile of v20, /device:TPU:0, one launch (start us, length us, event | category | flops | bytes accessed | tf_op | source)
XLA Modules:
  0.0 43.7 jit_solution(3709809423959005196)
XLA Ops:
  0.6 5.0 %class_sums.1 = (bf16[640,8192]{1,0:T(8,128)(2,1)S(1)}, f32[264,512]{1,0:T(8,128)S(1)}, f32[264,512]{1,0:T(8,128)S(1)}, f32[8,8192]{1,0:T(8,128)S(1)}) custom-call(s32[640]{0:T(1024)} %labels_ref.1, s32[3,32]{1,0:T(4,128)} %pick_ref.1, bf16[640,8192]{1,0:T(8,128)(2,1)} %feat_hbm.1), custom_call_target="tpu_custom_call" | custom-call | tf_op jit(solution)/shard_map/class_sums/pallas_call | solution.py:333
  5.7 0.5 %collective-permute-start = (f32[264,512]{1,0:T(8,128)S(1)}, f32[264,512]{1,0:T(8,128)S(1)}, u32[]{:S(2)}, u32[]{:S(2)}) collective-permute-start(f32[264,512]{1,0:T(8,128)S(1)} %get-tuple-element.25), channel_id=1, source_target_pairs={{0,1},{1,0},{2,3},{3,2},{4,5},{5,4},{6,7},{7,6},{8,9},{9,8},{10,11... | collective-permute-start | bytes 1622024 | tf_op jit(solution)/shard_map/ppermute | solution.py:328
  6.2 3.7 %collective-permute-start.1 = (bf16[2,8,3072]{2,1,0:T(8,128)(2,1)S(1)}, bf16[2,8,3072]{2,1,0:T(8,128)(2,1)S(1)}, u32[]{:S(2)}, u32[]{:S(2)}) collective-permute-start(bf16[2,8,3072]{2,1,0:T(8,128)(2,1)S(1)} %pack_rows.1), channel_id=1, source_target_pairs={{0,8},{1,9},{2,10},{3,11},{4,12},{5,13},{6,14},{7,15},{8,0},{9,1},... | collective-permute-start | bytes 294920 | tf_op jit(solution)/shard_map/ppermute | solution.py:328
  9.9 0.2 pair_sums.1
  10.1 2.6 %collective-permute-start.2 = (s16[2,136,128]{2,1,0:T(8,128)(2,1)S(1)}, s16[2,136,128]{2,1,0:T(8,128)(2,1)S(1)}, u32[]{:S(2)}, u32[]{:S(2)}) collective-permute-start(s16[2,136,128]{2,1,0:T(8,128)(2,1)S(1)} %get-tuple-element.29), channel_id=1, source_target_pairs={{0,6},{1,7},{2,4},{3,5},{4,2},{5,3},{6,0},{7,1},{8,14},{9,15},{10,... | collective-permute-start | bytes 208904 | tf_op jit(solution)/shard_map/ppermute | solution.py:328
  12.7 0.5 %collective-permute-start.3 = (s16[2,136,128]{2,1,0:T(8,128)(2,1)S(1)}, s16[2,136,128]{2,1,0:T(8,128)(2,1)S(1)}, u32[]{:S(2)}, u32[]{:S(2)}) collective-permute-start(s16[2,136,128]{2,1,0:T(8,128)(2,1)S(1)} %get-tuple-element.31), channel_id=1, source_target_pairs={{0,2},{1,3},{2,0},{3,1},{4,6},{5,7},{6,4},{7,5},{8,10},{9,11},{10,... | collective-permute-start | bytes 208904 | tf_op jit(solution)/shard_map/ppermute | solution.py:328
  13.2 0.5 %collective-permute-start.4 = (s16[2,136,128]{2,1,0:T(8,128)(2,1)S(1)}, s16[2,136,128]{2,1,0:T(8,128)(2,1)S(1)}, u32[]{:S(2)}, u32[]{:S(2)}) collective-permute-start(s16[2,136,128]{2,1,0:T(8,128)(2,1)S(1)} %get-tuple-element.32), channel_id=1, source_target_pairs={{0,4},{1,5},{2,6},{3,7},{4,0},{5,1},{6,2},{7,3},{8,12},{9,13},{10,... | collective-permute-start | bytes 208904 | tf_op jit(solution)/shard_map/ppermute | solution.py:328
  13.7 0.3 select_tails.1.rest_ref
  14.0 0.3 select_rows.1.one_ref
  14.4 1.2 %collective-permute-done.2.refs_1_ = s16[2,136,128]{2,1,0:T(8,128)(2,1)S(1)} collective-permute-done((s16[2,136,128]{2,1,0:T(8,128)(2,1)S(1)}, s16[2,136,128]{2,1,0:T(8,128)(2,1)S(1)}, u32[]{:S(2)}, u32[]{:S(2)}) %collective-permute-start.2) | collective-permute-done | bytes 69664 | tf_op jit(solution)/shard_map/ppermute | solution.py:328
  15.6 1.4 %collective-permute-done.3.refs_2_ = s16[2,136,128]{2,1,0:T(8,128)(2,1)S(1)} collective-permute-done((s16[2,136,128]{2,1,0:T(8,128)(2,1)S(1)}, s16[2,136,128]{2,1,0:T(8,128)(2,1)S(1)}, u32[]{:S(2)}, u32[]{:S(2)}) %collective-permute-start.3) | collective-permute-done | bytes 69664 | tf_op jit(solution)/shard_map/ppermute | solution.py:328
  17.0 0.8 %collective-permute-done.4.refs_3_ = s16[2,136,128]{2,1,0:T(8,128)(2,1)S(1)} collective-permute-done((s16[2,136,128]{2,1,0:T(8,128)(2,1)S(1)}, s16[2,136,128]{2,1,0:T(8,128)(2,1)S(1)}, u32[]{:S(2)}, u32[]{:S(2)}) %collective-permute-start.4) | collective-permute-done | bytes 69664 | tf_op jit(solution)/shard_map/ppermute | solution.py:328
  17.9 0.3 add_sums.2.refs_0_
  18.1 2.0 %collective-permute-start.5 = (s16[2,136,128]{2,1,0:T(8,128)(2,1)S(1)}, s16[2,136,128]{2,1,0:T(8,128)(2,1)S(1)}, u32[]{:S(2)}, u32[]{:S(2)}) collective-permute-start(s16[2,136,128]{2,1,0:T(8,128)(2,1)S(1)} %add_sums.2.refs_0_), channel_id=1, source_target_pairs={{0,8},{1,9},{2,10},{3,11},{4,12},{5,13},{6,14},{7,15},{8,0},{9,1},... | collective-permute-start | bytes 208904 | tf_op jit(solution)/shard_map/ppermute | solution.py:328
  20.1 0.1 collective-permute-start.6
  20.2 4.6 %collective-permute-done.5.refs_1_ = s16[2,136,128]{2,1,0:T(8,128)(2,1)S(1)} collective-permute-done((s16[2,136,128]{2,1,0:T(8,128)(2,1)S(1)}, s16[2,136,128]{2,1,0:T(8,128)(2,1)S(1)}, u32[]{:S(2)}, u32[]{:S(2)}) %collective-permute-start.5) | collective-permute-done | bytes 69664 | tf_op jit(solution)/shard_map/ppermute | solution.py:328
  24.9 0.1 collective-permute-start.7
  25.0 2.0 %collective-permute-start.9 = (bf16[32,3072]{1,0:T(8,128)(2,1)S(1)}, bf16[32,3072]{1,0:T(8,128)(2,1)S(1)}, u32[]{:S(2)}, u32[]{:S(2)}) collective-permute-start(bf16[32,3072]{1,0:T(8,128)(2,1)S(1)} %constant_dynamic-update-slice_fusion.refs_0_), channel_id=1, source_target_pairs={{0,6},{1,7},{2,4},{3,5},{4,2},{5,3},{6,0},{7,1},{8,14},{9,15},{10,... | collective-permute-start | bytes 589832 | tf_op jit(solution)/shard_map/ppermute | solution.py:328
  26.9 1.5 %collective-permute-start.8 = (bf16[32,3072]{1,0:T(8,128)(2,1)S(1)}, bf16[32,3072]{1,0:T(8,128)(2,1)S(1)}, u32[]{:S(2)}, u32[]{:S(2)}) collective-permute-start(bf16[32,3072]{1,0:T(8,128)(2,1)S(1)} %constant_dynamic-update-slice_fusion.refs_0_), channel_id=1, source_target_pairs={{0,2},{1,3},{2,0},{3,1},{4,6},{5,7},{6,4},{7,5},{8,10},{9,11},{10,... | collective-permute-start | bytes 589832 | tf_op jit(solution)/shard_map/ppermute | solution.py:328
  28.4 0.3 add_sums.3
  28.7 0.1 collective-permute-start.13
  28.8 1.5 %collective-permute-start.12 = (s16[2,136,128]{2,1,0:T(8,128)(2,1)S(1)}, s16[2,136,128]{2,1,0:T(8,128)(2,1)S(1)}, u32[]{:S(2)}, u32[]{:S(2)}) collective-permute-start(s16[2,136,128]{2,1,0:T(8,128)(2,1)S(1)} %add_sums.3), channel_id=1, source_target_pairs={{0,2},{1,3},{2,0},{3,1},{4,6},{5,7},{6,4},{7,5},{8,10},{9,11},{10,... | collective-permute-start | bytes 208904 | tf_op jit(solution)/shard_map/ppermute | solution.py:328
  30.3 2.5 %collective-permute-done.7.refs_1_ = bf16[32,3072]{1,0:T(8,128)(2,1)S(1)} collective-permute-done((bf16[32,3072]{1,0:T(8,128)(2,1)S(1)}, bf16[32,3072]{1,0:T(8,128)(2,1)S(1)}, u32[]{:S(2)}, u32[]{:S(2)}) %collective-permute-start.7) | collective-permute-done | bytes 196640 | tf_op jit(solution)/shard_map/ppermute | solution.py:328
  32.8 0.0 collective-permute-start.11
  32.8 2.5 %collective-permute-done.9.refs_3_ = bf16[32,3072]{1,0:T(8,128)(2,1)S(1)} collective-permute-done((bf16[32,3072]{1,0:T(8,128)(2,1)S(1)}, bf16[32,3072]{1,0:T(8,128)(2,1)S(1)}, u32[]{:S(2)}, u32[]{:S(2)}) %collective-permute-start.9) | collective-permute-done | bytes 196640 | tf_op jit(solution)/shard_map/ppermute | solution.py:328
  35.3 1.9 %collective-permute-done.8.refs_2_ = bf16[32,3072]{1,0:T(8,128)(2,1)S(1)} collective-permute-done((bf16[32,3072]{1,0:T(8,128)(2,1)S(1)}, bf16[32,3072]{1,0:T(8,128)(2,1)S(1)}, u32[]{:S(2)}, u32[]{:S(2)}) %collective-permute-start.8) | collective-permute-done | bytes 196640 | tf_op jit(solution)/shard_map/ppermute | solution.py:328
  37.2 0.4 picked_rows.1.x_ref.x_own
  37.6 0.1 collective-permute-start.10
  37.7 0.2 collective-permute-done.12
  38.1 0.3 collective-permute-start.14
  38.4 2.1 %own_half_products.1 = (f32[96,640]{1,0:T(8,128)S(1)}, f32[128,96]{1,0:T(8,128)S(1)}, f32[32,4096]{1,0:T(8,128)S(1)}) custom-call(bf16[640,8192]{1,0:T(8,128)(2,1)S(1)} %get-tuple-element.23.feat_ref, s16[8,136,128]{2,1,0:T(8,128)(2,1)S(1)} %constant_dynamic-update-slice_fusion.2.code_ref, bf16[96,4096]{1,0:T(8,128)(2,1)S(1)} %picked_rows.1.x_ref.x_own), custom_call_target="tpu_custom_call" | custom-call | tf_op jit(solution)/shard_map/own_half_products/pallas_call | solution.py:417
  40.5 3.2 %pursuit.1 = (f32[3,640]{1,0:T(4,128)}, f32[32,8192]{1,0:T(8,128)}) custom-call(s32[640]{0:T(1024)S(1)} %copy-done.1, bf16[640,8192]{1,0:T(8,128)(2,1)S(1)} %get-tuple-element.23.feat_ref, bf16[96,4096]{1,0:T(8,128)(2,1)S(1)} %picked_rows.1.x_ref.x_own, bf16[96,4096]{1,0:T(8,128)(2,1)S(1)} %collective-permute-done.10.x_twin, ...), custom_call_target="tpu_custom_call" | custom-call | tf_op jit(solution)/shard_map/pursuit/pallas_call | solution.py:431
  (19 shorter events, 0.1 us)
Async XLA Ops:
  0.6 13.0 %copy-start = (s32[3,32]{1,0:T(4,128)S(1)}, s32[3,32]{1,0:T(4,128)}, u32[]{:S(2)}) copy-start(s32[3,32]{1,0:T(4,128)} %pick_ref.1) | copy-start | bytes 1156
  5.7 34.8 %copy-start.1 = (s32[640]{0:T(1024)S(1)}, s32[640]{0:T(1024)}, u32[]{:S(2)}) copy-start(s32[640]{0:T(1024)} %labels_ref.1) | copy-start | bytes 7684
  5.7 4.2 %collective-permute-start = (f32[264,512]{1,0:T(8,128)S(1)}, f32[264,512]{1,0:T(8,128)S(1)}, u32[]{:S(2)}, u32[]{:S(2)}) collective-permute-start(f32[264,512]{1,0:T(8,128)S(1)} %get-tuple-element.25), channel_id=1, source_target_pairs={{0,1},{1,0},{2,3},{3,2},{4,5},{5,4},{6,7},{7,6},{8,9},{9,8},{10,11... | collective-permute-start | bytes 1622024 | tf_op jit(solution)/shard_map/ppermute | solution.py:328
  6.2 13.9 %collective-permute-start.1 = (bf16[2,8,3072]{2,1,0:T(8,128)(2,1)S(1)}, bf16[2,8,3072]{2,1,0:T(8,128)(2,1)S(1)}, u32[]{:S(2)}, u32[]{:S(2)}) collective-permute-start(bf16[2,8,3072]{2,1,0:T(8,128)(2,1)S(1)} %pack_rows.1), channel_id=1, source_target_pairs={{0,8},{1,9},{2,10},{3,11},{4,12},{5,13},{6,14},{7,15},{8,0},{9,1},... | collective-permute-start | bytes 294920 | tf_op jit(solution)/shard_map/ppermute | solution.py:328
  10.1 5.5 %collective-permute-start.2 = (s16[2,136,128]{2,1,0:T(8,128)(2,1)S(1)}, s16[2,136,128]{2,1,0:T(8,128)(2,1)S(1)}, u32[]{:S(2)}, u32[]{:S(2)}) collective-permute-start(s16[2,136,128]{2,1,0:T(8,128)(2,1)S(1)} %get-tuple-element.29), channel_id=1, source_target_pairs={{0,6},{1,7},{2,4},{3,5},{4,2},{5,3},{6,0},{7,1},{8,14},{9,15},{10,... | collective-permute-start | bytes 208904 | tf_op jit(solution)/shard_map/ppermute | solution.py:328
  12.7 4.3 %collective-permute-start.3 = (s16[2,136,128]{2,1,0:T(8,128)(2,1)S(1)}, s16[2,136,128]{2,1,0:T(8,128)(2,1)S(1)}, u32[]{:S(2)}, u32[]{:S(2)}) collective-permute-start(s16[2,136,128]{2,1,0:T(8,128)(2,1)S(1)} %get-tuple-element.31), channel_id=1, source_target_pairs={{0,2},{1,3},{2,0},{3,1},{4,6},{5,7},{6,4},{7,5},{8,10},{9,11},{10,... | collective-permute-start | bytes 208904 | tf_op jit(solution)/shard_map/ppermute | solution.py:328
  13.2 4.6 %collective-permute-start.4 = (s16[2,136,128]{2,1,0:T(8,128)(2,1)S(1)}, s16[2,136,128]{2,1,0:T(8,128)(2,1)S(1)}, u32[]{:S(2)}, u32[]{:S(2)}) collective-permute-start(s16[2,136,128]{2,1,0:T(8,128)(2,1)S(1)} %get-tuple-element.32), channel_id=1, source_target_pairs={{0,4},{1,5},{2,6},{3,7},{4,0},{5,1},{6,2},{7,3},{8,12},{9,13},{10,... | collective-permute-start | bytes 208904 | tf_op jit(solution)/shard_map/ppermute | solution.py:328
  18.1 6.7 %collective-permute-start.5 = (s16[2,136,128]{2,1,0:T(8,128)(2,1)S(1)}, s16[2,136,128]{2,1,0:T(8,128)(2,1)S(1)}, u32[]{:S(2)}, u32[]{:S(2)}) collective-permute-start(s16[2,136,128]{2,1,0:T(8,128)(2,1)S(1)} %add_sums.2.refs_0_), channel_id=1, source_target_pairs={{0,8},{1,9},{2,10},{3,11},{4,12},{5,13},{6,14},{7,15},{8,0},{9,1},... | collective-permute-start | bytes 208904 | tf_op jit(solution)/shard_map/ppermute | solution.py:328
  20.1 4.7 %collective-permute-start.6 = (bf16[16,3072]{1,0:T(8,128)(2,1)S(1)}, bf16[16,3072]{1,0:T(8,128)(2,1)S(1)}, u32[]{:S(2)}, u32[]{:S(2)}) collective-permute-start(bf16[16,3072]{1,0:T(8,128)(2,1)S(1)} %get-tuple-element.35), channel_id=1, source_target_pairs={{0,1},{1,0},{2,3},{3,2},{4,5},{5,4},{6,7},{7,6},{8,9},{9,8},{10,11... | collective-permute-start | bytes 294920 | tf_op jit(solution)/shard_map/ppermute | solution.py:328
  24.9 7.9 %collective-permute-start.7 = (bf16[32,3072]{1,0:T(8,128)(2,1)S(1)}, bf16[32,3072]{1,0:T(8,128)(2,1)S(1)}, u32[]{:S(2)}, u32[]{:S(2)}) collective-permute-start(bf16[32,3072]{1,0:T(8,128)(2,1)S(1)} %constant_dynamic-update-slice_fusion.refs_0_), channel_id=1, source_target_pairs={{0,4},{1,5},{2,6},{3,7},{4,0},{5,1},{6,2},{7,3},{8,12},{9,13},{10,... | collective-permute-start | bytes 589832 | tf_op jit(solution)/shard_map/ppermute | solution.py:328
  25.0 10.4 %collective-permute-start.9 = (bf16[32,3072]{1,0:T(8,128)(2,1)S(1)}, bf16[32,3072]{1,0:T(8,128)(2,1)S(1)}, u32[]{:S(2)}, u32[]{:S(2)}) collective-permute-start(bf16[32,3072]{1,0:T(8,128)(2,1)S(1)} %constant_dynamic-update-slice_fusion.refs_0_), channel_id=1, source_target_pairs={{0,6},{1,7},{2,4},{3,5},{4,2},{5,3},{6,0},{7,1},{8,14},{9,15},{10,... | collective-permute-start | bytes 589832 | tf_op jit(solution)/shard_map/ppermute | solution.py:328
  26.9 10.3 %collective-permute-start.8 = (bf16[32,3072]{1,0:T(8,128)(2,1)S(1)}, bf16[32,3072]{1,0:T(8,128)(2,1)S(1)}, u32[]{:S(2)}, u32[]{:S(2)}) collective-permute-start(bf16[32,3072]{1,0:T(8,128)(2,1)S(1)} %constant_dynamic-update-slice_fusion.refs_0_), channel_id=1, source_target_pairs={{0,2},{1,3},{2,0},{3,1},{4,6},{5,7},{6,4},{7,5},{8,10},{9,11},{10,... | collective-permute-start | bytes 589832 | tf_op jit(solution)/shard_map/ppermute | solution.py:328
  28.7 9.0 %collective-permute-start.13 = (s16[2,136,128]{2,1,0:T(8,128)(2,1)S(1)}, s16[2,136,128]{2,1,0:T(8,128)(2,1)S(1)}, u32[]{:S(2)}, u32[]{:S(2)}) collective-permute-start(s16[2,136,128]{2,1,0:T(8,128)(2,1)S(1)} %add_sums.3), channel_id=1, source_target_pairs={{0,6},{1,7},{2,4},{3,5},{4,2},{5,3},{6,0},{7,1},{8,14},{9,15},{10,... | collective-permute-start | bytes 208904 | tf_op jit(solution)/shard_map/ppermute | solution.py:328
  28.8 9.1 %collective-permute-start.12 = (s16[2,136,128]{2,1,0:T(8,128)(2,1)S(1)}, s16[2,136,128]{2,1,0:T(8,128)(2,1)S(1)}, u32[]{:S(2)}, u32[]{:S(2)}) collective-permute-start(s16[2,136,128]{2,1,0:T(8,128)(2,1)S(1)} %add_sums.3), channel_id=1, source_target_pairs={{0,2},{1,3},{2,0},{3,1},{4,6},{5,7},{6,4},{7,5},{8,10},{9,11},{10,... | collective-permute-start | bytes 208904 | tf_op jit(solution)/shard_map/ppermute | solution.py:328
  32.8 5.2 %collective-permute-start.11 = (s16[2,136,128]{2,1,0:T(8,128)(2,1)S(1)}, s16[2,136,128]{2,1,0:T(8,128)(2,1)S(1)}, u32[]{:S(2)}, u32[]{:S(2)}) collective-permute-start(s16[2,136,128]{2,1,0:T(8,128)(2,1)S(1)} %add_sums.3), channel_id=1, source_target_pairs={{0,4},{1,5},{2,6},{3,7},{4,0},{5,1},{6,2},{7,3},{8,12},{9,13},{10,... | collective-permute-start | bytes 208904 | tf_op jit(solution)/shard_map/ppermute | solution.py:328
  37.6 2.8 %collective-permute-start.10 = (bf16[96,4096]{1,0:T(8,128)(2,1)S(1)}, bf16[96,4096]{1,0:T(8,128)(2,1)S(1)}, u32[]{:S(2)}, u32[]{:S(2)}) collective-permute-start(bf16[96,4096]{1,0:T(8,128)(2,1)S(1)} %picked_rows.1.x_ref.x_own), channel_id=1, source_target_pairs={{0,1},{1,0},{2,3},{3,2},{4,5},{5,4},{6,7},{7,6},{8,9},{9,8},{10,11... | collective-permute-start | bytes 2359304 | tf_op jit(solution)/shard_map/ppermute | solution.py:328
  38.1 2.4 %collective-permute-start.14 = (s16[8,136,128]{2,1,0:T(8,128)(2,1)S(1)}, s16[8,136,128]{2,1,0:T(8,128)(2,1)S(1)}, u32[]{:S(2)}, u32[]{:S(2)}) collective-permute-start(s16[8,136,128]{2,1,0:T(8,128)(2,1)S(1)} %constant_dynamic-update-slice_fusion.2.code_ref), channel_id=1, source_target_pairs={{0,1},{1,0},{2,3},{3,2},{4,5},{5,4},{6,7},{7,6},{8,9},{9,8},{10,11... | collective-permute-start | bytes 835592 | tf_op jit(solution)/shard_map/ppermute | solution.py:328

commit v21 on v20

--- a/solution.py
+++ b/solution.py
@@ -10,7 +10,6 @@
 
 ridge = 1.0
 slots = 2
-near_masks = (0, 4, 2, 6)
 f32 = jnp.float32
 bf16 = jnp.bfloat16
 
@@ -125,17 +124,20 @@
         rows_ref[part] = jnp.concatenate(lines, axis=0).astype(bf16)
 
 
-def near_id(mask):
-    return (lax.axis_index("ex") // 2 % 4) ^ (mask // 2)
+def near_id(step, parity):
+    first = 1 + parity
+    flip = (step % 2) * first + (step // 2) * (3 - first)
+    return (lax.axis_index("ex") // 2 % 4) ^ flip
 
 
 def pair_kernel(keep_ref, got_ref, *code_refs, classes):
     far = code_refs[0].shape[0]
     base = 4 * far * classes
     tile = keep_ref[base : base + 8, :128] + got_ref[base : base + 8, :128]
-    for mask, code_ref in zip(near_masks, code_refs):
+    core = lax.axis_index("ex") % 2
+    for step, code_ref in enumerate(code_refs):
         for j in range(far):
-            at = pl.ds(pl.multiple_of((j * 4 + near_id(mask)) * classes, classes), classes)
+            at = pl.ds(pl.multiple_of((j * 4 + near_id(step, core)) * classes, classes), classes)
             code_ref[j] = encode(keep_ref[at, :] + got_ref[at, :], tile)
 
 
@@ -215,7 +217,8 @@
     far = jnp.zeros_like(pick)
     for b in range(3, bits):
         far = far + (((away >> b) & 1) << (bits - 1 - b))
-    near = ((away >> 2) & 1) + 2 * ((away >> 1) & 1)
+    by_y, by_z = (away >> 1) & 1, (away >> 2) & 1
+    near = jnp.where(device % 2 == 0, by_y + 2 * by_z, by_z + 2 * by_y)
     spot = (2 * near + (away & 1)) * (n_ex // 8) + far
     step = lax.broadcasted_iota(jnp.int32, pick.shape, 0)
     line = lax.broadcasted_iota(jnp.int32, (lines, classes), 0)
@@ -248,7 +251,7 @@
     width = half // code_ref.shape[0]
     here = pl.ds(pl.multiple_of(side * half, half), half)
     for k in range(4 * far):
-        block = k % far * 4 + near_id(near_masks[k // far])
+        block = k % far * 4 + near_id(k // far, side)
         target = decode(code_ref[k], classes)[0]
         target_ref[:, pl.ds(pl.multiple_of(target_at + block * width, width), width)] = target
         left_ref[:classes, pl.ds(pl.multiple_of(block * width, width), width)] = target.astype(bf16)
@@ -321,8 +324,12 @@
     code = jax.ShapeDtypeStruct((groups // 4, classes * (width // 128) + 8, 128), jnp.int16)
 
     def near_swaps(x):
-        diagonal_part, by_y = swap(x[3], 6), swap(x[2], 2)
-        return [swap(x[1], 4), by_y, diagonal_part]
+        diagonal_part, second = swap(x[3], 6), cross(x[2], False)
+        return [cross(x[1], True), second, diagonal_part]
+
+    def cross(x, first):
+        masks = (2, 4) if first else (4, 2)
+        return lax.ppermute(x, "ex", [(d, d ^ masks[d % 2]) for d in range(n_ex)])
 
     def swap(x, mask):
         return lax.ppermute(x, "ex", [(d, d ^ mask) for d in range(n_ex)])

time: 43.8 us -> 47.3 us (1.080)
  waiting for transfers between devices: 15.3 us -> 17.1 us
  starting transfers between devices: 15.4 us -> 16.9 us
    ppermute x0 -> x6, waiting for transfers between devices: none -> 11.2 us  [cross(): return lax.ppermute(x, 'ex', [(d, d ^ masks[d % 2]) for d in range(n_ex)])]
    ppermute x15 -> x9, waiting for transfers between devices: 15.3 us -> 5.86 us  [swap(): return lax.ppermute(x, 'ex', [(d, d ^ mask) for d in range(n_ex)])]
    ppermute x0 -> x6, starting transfers between devices: none -> 6.96 us  [cross(): return lax.ppermute(x, 'ex', [(d, d ^ masks[d % 2]) for d in range(n_ex)])]
    ppermute x15 -> x9, starting transfers between devices: 15.4 us -> 9.99 us  [swap(): return lax.ppermute(x, 'ex', [(d, d ^ mask) for d in range(n_ex)])]
  transfers between devices with their start and end apart: 15 -> 15, of which waited for: 8 -> 5; matrix products, arithmetic and copies ran while one was open for 0% -> 0% of each run, Pallas kernels for 9% -> 8%
where the time goes in v21:
time: 47.3 us; the launch traced here: 47.1 us
  waiting for transfers between devices  17.1 us (36%)
  starting transfers between devices  16.9 us (36%)
  Pallas kernels  12.1 us (26%)
  between operations  0.81 us (2%)
    ppermute x6, waiting for transfers between devices, cross(): return lax.ppermute(x, 'ex', [(d, d ^ masks[d % 2]) for d in range(n_ex)])  11.2 us
    ppermute x9, starting transfers between devices, swap(): return lax.ppermute(x, 'ex', [(d, d ^ mask) for d in range(n_ex)])  9.99 us
    ppermute x6, starting transfers between devices, cross(): return lax.ppermute(x, 'ex', [(d, d ^ masks[d % 2]) for d in range(n_ex)])  6.96 us
    ppermute x9, waiting for transfers between devices, swap(): return lax.ppermute(x, 'ex', [(d, d ^ mask) for d in range(n_ex)])  5.86 us
    pallas_call x1, Pallas kernels, on_device(): pl.pallas_call(functools.partial(sums_kernel, n_ex=n_ex), in_specs=[hbm]...  5.02 us
    pallas_call x1, Pallas kernels, on_device(): pl.pallas_call(functools.partial(pursuit_kernel, steps=steps, scale=1.0 /...  3.19 us
    pallas_call x1, Pallas kernels, on_device(): pl.pallas_call(functools.partial(half_kernel, classes=classes), in_specs=...  2.06 us
  transfers between devices with their start and end apart: 15, of which 5 were waited for; matrix products, arithmetic and copies ran while one was open for 0% of the time, Pallas kernels for 8%

profile of v21, /device:TPU:0, one launch (start us, length us, event | category | flops | bytes accessed | tf_op | source)
XLA Modules:
  0.0 47.1 jit_solution(12591148146339933199)
XLA Ops:
  0.6 5.0 %class_sums.1 = (bf16[640,8192]{1,0:T(8,128)(2,1)S(1)}, f32[264,512]{1,0:T(8,128)S(1)}, f32[264,512]{1,0:T(8,128)S(1)}, f32[8,8192]{1,0:T(8,128)S(1)}) custom-call(s32[640]{0:T(1024)} %labels_ref.1, s32[3,32]{1,0:T(4,128)} %pick_ref.1, bf16[640,8192]{1,0:T(8,128)(2,1)} %feat_hbm.1), custom_call_target="tpu_custom_call" | custom-call | tf_op jit(solution)/shard_map/class_sums/pallas_call | solution.py:340
  5.7 0.0 copy-start.1
  5.7 0.5 %collective-permute-start = (f32[264,512]{1,0:T(8,128)S(1)}, f32[264,512]{1,0:T(8,128)S(1)}, u32[]{:S(2)}, u32[]{:S(2)}) collective-permute-start(f32[264,512]{1,0:T(8,128)S(1)} %get-tuple-element.25), channel_id=1, source_target_pairs={{0,1},{1,0},{2,3},{3,2},{4,5},{5,4},{6,7},{7,6},{8,9},{9,8},{10,11... | collective-permute-start | bytes 1622024 | tf_op jit(solution)/shard_map/ppermute | solution.py:335
  6.2 3.7 %collective-permute-start.1 = (bf16[2,8,3072]{2,1,0:T(8,128)(2,1)S(1)}, bf16[2,8,3072]{2,1,0:T(8,128)(2,1)S(1)}, u32[]{:S(2)}, u32[]{:S(2)}) collective-permute-start(bf16[2,8,3072]{2,1,0:T(8,128)(2,1)S(1)} %pack_rows.1), channel_id=1, source_target_pairs={{0,8},{1,9},{2,10},{3,11},{4,12},{5,13},{6,14},{7,15},{8,0},{9,1},... | collective-permute-start | bytes 294920 | tf_op jit(solution)/shard_map/ppermute | solution.py:335
  9.9 0.0 collective-permute-done.got_ref
  9.9 0.2 pair_sums.1
  10.1 2.6 %collective-permute-start.2 = (s16[2,136,128]{2,1,0:T(8,128)(2,1)S(1)}, s16[2,136,128]{2,1,0:T(8,128)(2,1)S(1)}, u32[]{:S(2)}, u32[]{:S(2)}) collective-permute-start(s16[2,136,128]{2,1,0:T(8,128)(2,1)S(1)} %get-tuple-element.29), channel_id=1, source_target_pairs={{0,6},{1,7},{2,4},{3,5},{4,2},{5,3},{6,0},{7,1},{8,14},{9,15},{10,... | collective-permute-start | bytes 208904 | tf_op jit(solution)/shard_map/ppermute | solution.py:335
  12.7 0.4 collective-permute-start.3
  13.2 0.5 %collective-permute-start.4 = (s16[2,136,128]{2,1,0:T(8,128)(2,1)S(1)}, s16[2,136,128]{2,1,0:T(8,128)(2,1)S(1)}, u32[]{:S(2)}, u32[]{:S(2)}) collective-permute-start(s16[2,136,128]{2,1,0:T(8,128)(2,1)S(1)} %get-tuple-element.32), channel_id=1, source_target_pairs={{0,2},{1,5},{2,0},{3,7},{4,6},{5,1},{6,4},{7,3},{8,10},{9,13},{10,... | collective-permute-start | bytes 208904 | tf_op jit(solution)/shard_map/ppermute | solution.py:332
  13.7 0.3 select_tails.1.rest_ref
  14.0 0.3 select_rows.1.one_ref
  14.4 1.2 %collective-permute-done.2.refs_1_ = s16[2,136,128]{2,1,0:T(8,128)(2,1)S(1)} collective-permute-done((s16[2,136,128]{2,1,0:T(8,128)(2,1)S(1)}, s16[2,136,128]{2,1,0:T(8,128)(2,1)S(1)}, u32[]{:S(2)}, u32[]{:S(2)}) %collective-permute-start.2) | collective-permute-done | bytes 69664 | tf_op jit(solution)/shard_map/ppermute | solution.py:335
  15.6 2.3 %collective-permute-done.3.refs_2_ = s16[2,136,128]{2,1,0:T(8,128)(2,1)S(1)} collective-permute-done((s16[2,136,128]{2,1,0:T(8,128)(2,1)S(1)}, s16[2,136,128]{2,1,0:T(8,128)(2,1)S(1)}, u32[]{:S(2)}, u32[]{:S(2)}) %collective-permute-start.3) | collective-permute-done | bytes 69664 | tf_op jit(solution)/shard_map/ppermute | solution.py:332
  17.9 0.0 collective-permute-done.4.refs_3_
  17.9 0.3 add_sums.2.refs_0_
  18.1 2.0 %collective-permute-start.5 = (s16[2,136,128]{2,1,0:T(8,128)(2,1)S(1)}, s16[2,136,128]{2,1,0:T(8,128)(2,1)S(1)}, u32[]{:S(2)}, u32[]{:S(2)}) collective-permute-start(s16[2,136,128]{2,1,0:T(8,128)(2,1)S(1)} %add_sums.2.refs_0_), channel_id=1, source_target_pairs={{0,8},{1,9},{2,10},{3,11},{4,12},{5,13},{6,14},{7,15},{8,0},{9,1},... | collective-permute-start | bytes 208904 | tf_op jit(solution)/shard_map/ppermute | solution.py:335
  20.1 0.1 collective-permute-start.6
  20.2 4.6 %collective-permute-done.5.refs_1_ = s16[2,136,128]{2,1,0:T(8,128)(2,1)S(1)} collective-permute-done((s16[2,136,128]{2,1,0:T(8,128)(2,1)S(1)}, s16[2,136,128]{2,1,0:T(8,128)(2,1)S(1)}, u32[]{:S(2)}, u32[]{:S(2)}) %collective-permute-start.5) | collective-permute-done | bytes 69664 | tf_op jit(solution)/shard_map/ppermute | solution.py:335
  24.9 0.7 %collective-permute-start.7 = (bf16[32,3072]{1,0:T(8,128)(2,1)S(1)}, bf16[32,3072]{1,0:T(8,128)(2,1)S(1)}, u32[]{:S(2)}, u32[]{:S(2)}) collective-permute-start(bf16[32,3072]{1,0:T(8,128)(2,1)S(1)} %constant_dynamic-update-slice_fusion.refs_0_), channel_id=1, source_target_pairs={{0,2},{1,5},{2,0},{3,7},{4,6},{5,1},{6,4},{7,3},{8,10},{9,13},{10,... | collective-permute-start | bytes 589832 | tf_op jit(solution)/shard_map/ppermute | solution.py:332
  25.6 0.9 %collective-permute-start.9 = (bf16[32,3072]{1,0:T(8,128)(2,1)S(1)}, bf16[32,3072]{1,0:T(8,128)(2,1)S(1)}, u32[]{:S(2)}, u32[]{:S(2)}) collective-permute-start(bf16[32,3072]{1,0:T(8,128)(2,1)S(1)} %constant_dynamic-update-slice_fusion.refs_0_), channel_id=1, source_target_pairs={{0,6},{1,7},{2,4},{3,5},{4,2},{5,3},{6,0},{7,1},{8,14},{9,15},{10,... | collective-permute-start | bytes 589832 | tf_op jit(solution)/shard_map/ppermute | solution.py:335
  26.4 2.0 %collective-permute-start.8 = (bf16[32,3072]{1,0:T(8,128)(2,1)S(1)}, bf16[32,3072]{1,0:T(8,128)(2,1)S(1)}, u32[]{:S(2)}, u32[]{:S(2)}) collective-permute-start(bf16[32,3072]{1,0:T(8,128)(2,1)S(1)} %constant_dynamic-update-slice_fusion.refs_0_), channel_id=1, source_target_pairs={{0,4},{1,3},{2,6},{3,1},{4,0},{5,7},{6,2},{7,5},{8,12},{9,11},{10,... | collective-permute-start | bytes 589832 | tf_op jit(solution)/shard_map/ppermute | solution.py:332
  28.4 0.3 add_sums.3
  28.7 0.2 collective-permute-start.13
  28.8 2.0 %collective-permute-start.12 = (s16[2,136,128]{2,1,0:T(8,128)(2,1)S(1)}, s16[2,136,128]{2,1,0:T(8,128)(2,1)S(1)}, u32[]{:S(2)}, u32[]{:S(2)}) collective-permute-start(s16[2,136,128]{2,1,0:T(8,128)(2,1)S(1)} %add_sums.3), channel_id=1, source_target_pairs={{0,4},{1,3},{2,6},{3,1},{4,0},{5,7},{6,2},{7,5},{8,12},{9,11},{10,... | collective-permute-start | bytes 208904 | tf_op jit(solution)/shard_map/ppermute | solution.py:332
  30.9 6.5 %collective-permute-done.7.refs_1_ = bf16[32,3072]{1,0:T(8,128)(2,1)S(1)} collective-permute-done((bf16[32,3072]{1,0:T(8,128)(2,1)S(1)}, bf16[32,3072]{1,0:T(8,128)(2,1)S(1)}, u32[]{:S(2)}, u32[]{:S(2)}) %collective-permute-start.7) | collective-permute-done | bytes 196640 | tf_op jit(solution)/shard_map/ppermute | solution.py:332
  37.3 1.3 %collective-permute-start.11 = (s16[2,136,128]{2,1,0:T(8,128)(2,1)S(1)}, s16[2,136,128]{2,1,0:T(8,128)(2,1)S(1)}, u32[]{:S(2)}, u32[]{:S(2)}) collective-permute-start(s16[2,136,128]{2,1,0:T(8,128)(2,1)S(1)} %add_sums.3), channel_id=1, source_target_pairs={{0,2},{1,5},{2,0},{3,7},{4,6},{5,1},{6,4},{7,3},{8,10},{9,13},{10,... | collective-permute-start | bytes 208904 | tf_op jit(solution)/shard_map/ppermute | solution.py:332
  38.6 0.4 picked_rows.1.x_ref.x_own
  39.0 0.1 collective-permute-start.10
  39.1 2.5 %collective-permute-done.11 = s16[2,136,128]{2,1,0:T(8,128)(2,1)S(1)} collective-permute-done((s16[2,136,128]{2,1,0:T(8,128)(2,1)S(1)}, s16[2,136,128]{2,1,0:T(8,128)(2,1)S(1)}, u32[]{:S(2)}, u32[]{:S(2)}) %collective-permute-start.11) | collective-permute-done | bytes 69664 | tf_op jit(solution)/shard_map/ppermute | solution.py:332
  41.7 0.1 collective-permute-start.14
  41.8 2.1 %own_half_products.1 = (f32[96,640]{1,0:T(8,128)S(1)}, f32[128,96]{1,0:T(8,128)S(1)}, f32[32,4096]{1,0:T(8,128)S(1)}) custom-call(bf16[640,8192]{1,0:T(8,128)(2,1)S(1)} %get-tuple-element.23.feat_ref, s16[8,136,128]{2,1,0:T(8,128)(2,1)S(1)} %constant_dynamic-update-slice_fusion.2.code_ref, bf16[96,4096]{1,0:T(8,128)(2,1)S(1)} %picked_rows.1.x_ref.x_own), custom_call_target="tpu_custom_call" | custom-call | tf_op jit(solution)/shard_map/own_half_products/pallas_call | solution.py:424
  43.9 3.2 %pursuit.1 = (f32[3,640]{1,0:T(4,128)}, f32[32,8192]{1,0:T(8,128)}) custom-call(s32[640]{0:T(1024)S(1)} %copy-done.1, bf16[640,8192]{1,0:T(8,128)(2,1)S(1)} %get-tuple-element.23.feat_ref, bf16[96,4096]{1,0:T(8,128)(2,1)S(1)} %picked_rows.1.x_ref.x_own, bf16[96,4096]{1,0:T(8,128)(2,1)S(1)} %collective-permute-done.10.x_twin, ...), custom_call_target="tpu_custom_call" | custom-call | tf_op jit(solution)/shard_map/pursuit/pallas_call | solution.py:438
  (19 shorter events, 0.1 us)
Async XLA Ops:
  0.6 13.0 %copy-start = (s32[3,32]{1,0:T(4,128)S(1)}, s32[3,32]{1,0:T(4,128)}, u32[]{:S(2)}) copy-start(s32[3,32]{1,0:T(4,128)} %pick_ref.1) | copy-start | bytes 1156
  5.7 38.2 %copy-start.1 = (s32[640]{0:T(1024)S(1)}, s32[640]{0:T(1024)}, u32[]{:S(2)}) copy-start(s32[640]{0:T(1024)} %labels_ref.1) | copy-start | bytes 7684
  5.7 4.2 %collective-permute-start = (f32[264,512]{1,0:T(8,128)S(1)}, f32[264,512]{1,0:T(8,128)S(1)}, u32[]{:S(2)}, u32[]{:S(2)}) collective-permute-start(f32[264,512]{1,0:T(8,128)S(1)} %get-tuple-element.25), channel_id=1, source_target_pairs={{0,1},{1,0},{2,3},{3,2},{4,5},{5,4},{6,7},{7,6},{8,9},{9,8},{10,11... | collective-permute-start | bytes 1622024 | tf_op jit(solution)/shard_map/ppermute | solution.py:335
  6.2 13.9 %collective-permute-start.1 = (bf16[2,8,3072]{2,1,0:T(8,128)(2,1)S(1)}, bf16[2,8,3072]{2,1,0:T(8,128)(2,1)S(1)}, u32[]{:S(2)}, u32[]{:S(2)}) collective-permute-start(bf16[2,8,3072]{2,1,0:T(8,128)(2,1)S(1)} %pack_rows.1), channel_id=1, source_target_pairs={{0,8},{1,9},{2,10},{3,11},{4,12},{5,13},{6,14},{7,15},{8,0},{9,1},... | collective-permute-start | bytes 294920 | tf_op jit(solution)/shard_map/ppermute | solution.py:335
  10.1 5.5 %collective-permute-start.2 = (s16[2,136,128]{2,1,0:T(8,128)(2,1)S(1)}, s16[2,136,128]{2,1,0:T(8,128)(2,1)S(1)}, u32[]{:S(2)}, u32[]{:S(2)}) collective-permute-start(s16[2,136,128]{2,1,0:T(8,128)(2,1)S(1)} %get-tuple-element.29), channel_id=1, source_target_pairs={{0,6},{1,7},{2,4},{3,5},{4,2},{5,3},{6,0},{7,1},{8,14},{9,15},{10,... | collective-permute-start | bytes 208904 | tf_op jit(solution)/shard_map/ppermute | solution.py:335
  12.7 5.1 %collective-permute-start.3 = (s16[2,136,128]{2,1,0:T(8,128)(2,1)S(1)}, s16[2,136,128]{2,1,0:T(8,128)(2,1)S(1)}, u32[]{:S(2)}, u32[]{:S(2)}) collective-permute-start(s16[2,136,128]{2,1,0:T(8,128)(2,1)S(1)} %get-tuple-element.31), channel_id=1, source_target_pairs={{0,4},{1,3},{2,6},{3,1},{4,0},{5,7},{6,2},{7,5},{8,12},{9,11},{10,... | collective-permute-start | bytes 208904 | tf_op jit(solution)/shard_map/ppermute | solution.py:332
  13.2 4.7 %collective-permute-start.4 = (s16[2,136,128]{2,1,0:T(8,128)(2,1)S(1)}, s16[2,136,128]{2,1,0:T(8,128)(2,1)S(1)}, u32[]{:S(2)}, u32[]{:S(2)}) collective-permute-start(s16[2,136,128]{2,1,0:T(8,128)(2,1)S(1)} %get-tuple-element.32), channel_id=1, source_target_pairs={{0,2},{1,5},{2,0},{3,7},{4,6},{5,1},{6,4},{7,3},{8,10},{9,13},{10,... | collective-permute-start | bytes 208904 | tf_op jit(solution)/shard_map/ppermute | solution.py:332
  18.1 6.7 %collective-permute-start.5 = (s16[2,136,128]{2,1,0:T(8,128)(2,1)S(1)}, s16[2,136,128]{2,1,0:T(8,128)(2,1)S(1)}, u32[]{:S(2)}, u32[]{:S(2)}) collective-permute-start(s16[2,136,128]{2,1,0:T(8,128)(2,1)S(1)} %add_sums.2.refs_0_), channel_id=1, source_target_pairs={{0,8},{1,9},{2,10},{3,11},{4,12},{5,13},{6,14},{7,15},{8,0},{9,1},... | collective-permute-start | bytes 208904 | tf_op jit(solution)/shard_map/ppermute | solution.py:335
  20.1 4.7 %collective-permute-start.6 = (bf16[16,3072]{1,0:T(8,128)(2,1)S(1)}, bf16[16,3072]{1,0:T(8,128)(2,1)S(1)}, u32[]{:S(2)}, u32[]{:S(2)}) collective-permute-start(bf16[16,3072]{1,0:T(8,128)(2,1)S(1)} %get-tuple-element.35), channel_id=1, source_target_pairs={{0,1},{1,0},{2,3},{3,2},{4,5},{5,4},{6,7},{7,6},{8,9},{9,8},{10,11... | collective-permute-start | bytes 294920 | tf_op jit(solution)/shard_map/ppermute | solution.py:335
  24.9 12.5 %collective-permute-start.7 = (bf16[32,3072]{1,0:T(8,128)(2,1)S(1)}, bf16[32,3072]{1,0:T(8,128)(2,1)S(1)}, u32[]{:S(2)}, u32[]{:S(2)}) collective-permute-start(bf16[32,3072]{1,0:T(8,128)(2,1)S(1)} %constant_dynamic-update-slice_fusion.refs_0_), channel_id=1, source_target_pairs={{0,2},{1,5},{2,0},{3,7},{4,6},{5,1},{6,4},{7,3},{8,10},{9,13},{10,... | collective-permute-start | bytes 589832 | tf_op jit(solution)/shard_map/ppermute | solution.py:332
  25.6 13.1 %collective-permute-start.9 = (bf16[32,3072]{1,0:T(8,128)(2,1)S(1)}, bf16[32,3072]{1,0:T(8,128)(2,1)S(1)}, u32[]{:S(2)}, u32[]{:S(2)}) collective-permute-start(bf16[32,3072]{1,0:T(8,128)(2,1)S(1)} %constant_dynamic-update-slice_fusion.refs_0_), channel_id=1, source_target_pairs={{0,6},{1,7},{2,4},{3,5},{4,2},{5,3},{6,0},{7,1},{8,14},{9,15},{10,... | collective-permute-start | bytes 589832 | tf_op jit(solution)/shard_map/ppermute | solution.py:335
  26.4 12.2 %collective-permute-start.8 = (bf16[32,3072]{1,0:T(8,128)(2,1)S(1)}, bf16[32,3072]{1,0:T(8,128)(2,1)S(1)}, u32[]{:S(2)}, u32[]{:S(2)}) collective-permute-start(bf16[32,3072]{1,0:T(8,128)(2,1)S(1)} %constant_dynamic-update-slice_fusion.refs_0_), channel_id=1, source_target_pairs={{0,4},{1,3},{2,6},{3,1},{4,0},{5,7},{6,2},{7,5},{8,12},{9,11},{10,... | collective-permute-start | bytes 589832 | tf_op jit(solution)/shard_map/ppermute | solution.py:332
  28.7 10.4 %collective-permute-start.13 = (s16[2,136,128]{2,1,0:T(8,128)(2,1)S(1)}, s16[2,136,128]{2,1,0:T(8,128)(2,1)S(1)}, u32[]{:S(2)}, u32[]{:S(2)}) collective-permute-start(s16[2,136,128]{2,1,0:T(8,128)(2,1)S(1)} %add_sums.3), channel_id=1, source_target_pairs={{0,6},{1,7},{2,4},{3,5},{4,2},{5,3},{6,0},{7,1},{8,14},{9,15},{10,... | collective-permute-start | bytes 208904 | tf_op jit(solution)/shard_map/ppermute | solution.py:335
  28.8 10.3 %collective-permute-start.12 = (s16[2,136,128]{2,1,0:T(8,128)(2,1)S(1)}, s16[2,136,128]{2,1,0:T(8,128)(2,1)S(1)}, u32[]{:S(2)}, u32[]{:S(2)}) collective-permute-start(s16[2,136,128]{2,1,0:T(8,128)(2,1)S(1)} %add_sums.3), channel_id=1, source_target_pairs={{0,4},{1,3},{2,6},{3,1},{4,0},{5,7},{6,2},{7,5},{8,12},{9,11},{10,... | collective-permute-start | bytes 208904 | tf_op jit(solution)/shard_map/ppermute | solution.py:332
  37.3 4.3 %collective-permute-start.11 = (s16[2,136,128]{2,1,0:T(8,128)(2,1)S(1)}, s16[2,136,128]{2,1,0:T(8,128)(2,1)S(1)}, u32[]{:S(2)}, u32[]{:S(2)}) collective-permute-start(s16[2,136,128]{2,1,0:T(8,128)(2,1)S(1)} %add_sums.3), channel_id=1, source_target_pairs={{0,2},{1,5},{2,0},{3,7},{4,6},{5,1},{6,4},{7,3},{8,10},{9,13},{10,... | collective-permute-start | bytes 208904 | tf_op jit(solution)/shard_map/ppermute | solution.py:332
  39.0 4.8 %collective-permute-start.10 = (bf16[96,4096]{1,0:T(8,128)(2,1)S(1)}, bf16[96,4096]{1,0:T(8,128)(2,1)S(1)}, u32[]{:S(2)}, u32[]{:S(2)}) collective-permute-start(bf16[96,4096]{1,0:T(8,128)(2,1)S(1)} %picked_rows.1.x_ref.x_own), channel_id=1, source_target_pairs={{0,1},{1,0},{2,3},{3,2},{4,5},{5,4},{6,7},{7,6},{8,9},{9,8},{10,11... | collective-permute-start | bytes 2359304 | tf_op jit(solution)/shard_map/ppermute | solution.py:335
  41.7 2.2 %collective-permute-start.14 = (s16[8,136,128]{2,1,0:T(8,128)(2,1)S(1)}, s16[8,136,128]{2,1,0:T(8,128)(2,1)S(1)}, u32[]{:S(2)}, u32[]{:S(2)}) collective-permute-start(s16[8,136,128]{2,1,0:T(8,128)(2,1)S(1)} %constant_dynamic-update-slice_fusion.2.code_ref), channel_id=1, source_target_pairs={{0,1},{1,0},{2,3},{3,2},{4,5},{5,4},{6,7},{7,6},{8,9},{9,8},{10,11... | collective-permute-start | bytes 835592 | tf_op jit(solution)/shard_map/ppermute | solution.py:335

commit v22 on v12

--- a/solution.py
+++ b/solution.py
@@ -242,24 +242,35 @@
         x_ref[at, main:] = rest.astype(bf16)
 
 
-def half_target(side, code_ref, x_ref, target_ref, target_at, left_ref, *, classes):
+def prepare(j, side, code_ref, x_ref, target_ref, target_at, left_ref, *, classes):
+    far = code_ref.shape[0] // 4
+    width = left_ref.shape[1] // code_ref.shape[0]
+    for k, mask in enumerate(near_masks):
+        block = j * 4 + near_id(mask)
+        target = decode(code_ref[k * far + j], classes)[0]
+        target_ref[:, pl.ds(pl.multiple_of(target_at + block * width, width), width)] = target
+        left_ref[:classes, pl.ds(pl.multiple_of(block * width, width), width)] = target.astype(bf16)
+    cols = slice(j * 4 * width, (j + 1) * 4 * width)
+    left_ref[classes:, cols] = x_ref[:, cols]
+    return cols
+
+
+def half_kernel(feat_ref, code_ref, x_ref, direct_ref, gram_ref, target_ref, left_ref, *, classes):
+    core = lax.axis_index("ex") % 2
     half = left_ref.shape[1]
     far = code_ref.shape[0] // 4
-    width = half // code_ref.shape[0]
-    here = pl.ds(pl.multiple_of(side * half, half), half)
-    for k in range(4 * far):
-        block = k % far * 4 + near_id(near_masks[k // far])
-        target = decode(code_ref[k], classes)[0]
-        target_ref[:, pl.ds(pl.multiple_of(target_at + block * width, width), width)] = target
-        left_ref[:classes, pl.ds(pl.multiple_of(block * width, width), width)] = target.astype(bf16)
-    left_ref[classes:, :] = x_ref[...]
-    return nt_dot(left_ref[...], x_ref[...]), here
-
-
-def half_kernel(feat_ref, code_ref, x_ref, direct_ref, gram_ref, target_ref, left_ref, *, classes):
-    core = lax.axis_index("ex") % 2
-    gram_ref[...], here = half_target(core, code_ref, x_ref, target_ref, 0, left_ref, classes=classes)
-    direct_ref[...] = nt_dot(left_ref[: direct_ref.shape[0], :], feat_ref[:, here])
+    gram = direct = 0.0
+    cols = prepare(0, core, code_ref, x_ref, target_ref, 0, left_ref, classes=classes)
+    for j in range(far):
+        now = cols
+        if j + 1 < far:
+            cols = prepare(j + 1, core, code_ref, x_ref, target_ref, 0, left_ref, classes=classes)
+        span = half // far
+        here = pl.ds(pl.multiple_of(core * half + j * span, span), span)
+        direct = direct + nt_dot(left_ref[: direct_ref.shape[0], now], feat_ref[:, here])
+        gram = gram + nt_dot(left_ref[:, now], x_ref[:, now])
+    direct_ref[...] = direct
+    gram_ref[...] = gram
 
 
 def pursuit_kernel(
@@ -269,8 +280,10 @@
     classes, full = resid_ref.shape
     half = full // 2
     core = lax.axis_index("ex") % 2
-    gram, other = half_target(1 - core, code_ref, x_twin, resid_ref, (1 - core) * half, left_ref, classes=classes)
-    gram = gram + gram_own[...]
+    gram = gram_own[...]
+    for j in range(code_ref.shape[0] // 4):
+        cols = prepare(j, 1 - core, code_ref, x_twin, resid_ref, (1 - core) * half, left_ref, classes=classes)
+        gram = gram + nt_dot(left_ref[:, cols], x_twin[:, cols])
     blocks = [
         [
             diagonal(gram[(a + 1) * classes : (a + 2) * classes, b * classes : (b + 1) * classes])
@@ -283,6 +296,7 @@
     weights = solve_all(factor_all(blocks), rhs)
     last = weights[steps - 1]
     copies = []
+    direct = direct_own[...]
     span = half // 2
     for x_ref, side in ((x_own, core), (x_twin, 1 - core)):
         for q in range(2):
@@ -294,8 +308,11 @@
             resid_ref[:, here] = value
             copies.append(pltpu.make_async_copy(resid_ref.at[:, here], resid_hbm.at[:, here], sems.at[len(copies)]))
             copies[-1].start()
-
-    direct = direct_own[...] + nt_dot(left_ref[: direct_own.shape[0], :], feat_ref[:, other])
+            step = half // 4
+            at = (len(copies) - 1) * step
+            other = pl.ds(pl.multiple_of((1 - core) * half + at, step), step)
+            direct = direct + nt_dot(left_ref[: direct.shape[0], at : at + step], feat_ref[:, other])
+
     member = lax.broadcasted_iota(jnp.int32, (classes, direct.shape[1]), 0) == labels_ref[...].reshape(1, direct.shape[1])
     for s in range(steps):
         value = direct[:classes]

time: 43.6 us -> 44.2 us (1.014)
  Pallas kernels: 12.1 us -> 12.7 us
    pallas_call x1, Pallas kernels: 3.19 us -> 3.71 us  [on_device(): pl.pallas_call(functools.partial(pursuit_kernel, steps=steps, scale=1.0 /...]
where the time goes in v22:
time: 44.2 us; the launch traced here: 44.1 us
  waiting for transfers between devices  16.2 us (37%)
  starting transfers between devices  14.3 us (32%)
  Pallas kernels  12.7 us (29%)
  between operations  0.79 us (2%)
    ppermute x15, waiting for transfers between devices, swap(): return lax.ppermute(x, 'ex', [(d, d ^ mask) for d in range(n_ex)])  16.2 us
    ppermute x15, starting transfers between devices, swap(): return lax.ppermute(x, 'ex', [(d, d ^ mask) for d in range(n_ex)])  14.3 us
    pallas_call x1, Pallas kernels, on_device(): pl.pallas_call(functools.partial(sums_kernel, n_ex=n_ex), in_specs=[hbm]...  5.02 us
    pallas_call x1, Pallas kernels, on_device(): pl.pallas_call(functools.partial(pursuit_kernel, steps=steps, scale=1.0 /...  3.71 us
    pallas_call x1, Pallas kernels, on_device(): pl.pallas_call(functools.partial(half_kernel, classes=classes), in_specs=...  2.14 us
  transfers between devices with their start and end apart: 15, of which 9 were waited for; matrix products, arithmetic and copies ran while one was open for 0% of the time, Pallas kernels for 9%

profile of v22, /device:TPU:0, one launch (start us, length us, event | category | flops | bytes accessed | tf_op | source)
XLA Modules:
  0.0 44.1 jit_solution(178585609579530952)
XLA Ops:
  0.6 5.0 %class_sums.1 = (bf16[640,8192]{1,0:T(8,128)(2,1)S(1)}, f32[264,512]{1,0:T(8,128)S(1)}, f32[264,512]{1,0:T(8,128)S(1)}, f32[8,8192]{1,0:T(8,128)S(1)}) custom-call(s32[640]{0:T(1024)} %labels_ref.1, s32[3,32]{1,0:T(4,128)} %pick_ref.1, bf16[640,8192]{1,0:T(8,128)(2,1)} %feat_hbm.1), custom_call_target="tpu_custom_call" | custom-call | tf_op jit(solution)/shard_map/class_sums/pallas_call | solution.py:346
  5.7 0.5 %collective-permute-start = (f32[264,512]{1,0:T(8,128)S(1)}, f32[264,512]{1,0:T(8,128)S(1)}, u32[]{:S(2)}, u32[]{:S(2)}) collective-permute-start(f32[264,512]{1,0:T(8,128)S(1)} %get-tuple-element.25), channel_id=1, source_target_pairs={{0,1},{1,0},{2,3},{3,2},{4,5},{5,4},{6,7},{7,6},{8,9},{9,8},{10,11... | collective-permute-start | bytes 1622024 | tf_op jit(solution)/shard_map/ppermute | solution.py:341
  6.2 3.7 %collective-permute-start.1 = (bf16[2,8,3072]{2,1,0:T(8,128)(2,1)S(1)}, bf16[2,8,3072]{2,1,0:T(8,128)(2,1)S(1)}, u32[]{:S(2)}, u32[]{:S(2)}) collective-permute-start(bf16[2,8,3072]{2,1,0:T(8,128)(2,1)S(1)} %pack_rows.1), channel_id=1, source_target_pairs={{0,8},{1,9},{2,10},{3,11},{4,12},{5,13},{6,14},{7,15},{8,0},{9,1},... | collective-permute-start | bytes 294920 | tf_op jit(solution)/shard_map/ppermute | solution.py:341
  9.9 0.2 pair_sums.1
  10.1 1.6 %collective-permute-start.2 = (s16[2,136,128]{2,1,0:T(8,128)(2,1)S(1)}, s16[2,136,128]{2,1,0:T(8,128)(2,1)S(1)}, u32[]{:S(2)}, u32[]{:S(2)}) collective-permute-start(s16[2,136,128]{2,1,0:T(8,128)(2,1)S(1)} %get-tuple-element.29), channel_id=1, source_target_pairs={{0,4},{1,5},{2,6},{3,7},{4,0},{5,1},{6,2},{7,3},{8,12},{9,13},{10,... | collective-permute-start | bytes 208904 | tf_op jit(solution)/shard_map/ppermute | solution.py:341
  11.8 1.5 %collective-permute-start.3 = (s16[2,136,128]{2,1,0:T(8,128)(2,1)S(1)}, s16[2,136,128]{2,1,0:T(8,128)(2,1)S(1)}, u32[]{:S(2)}, u32[]{:S(2)}) collective-permute-start(s16[2,136,128]{2,1,0:T(8,128)(2,1)S(1)} %get-tuple-element.31), channel_id=1, source_target_pairs={{0,2},{1,3},{2,0},{3,1},{4,6},{5,7},{6,4},{7,5},{8,10},{9,11},{10,... | collective-permute-start | bytes 208904 | tf_op jit(solution)/shard_map/ppermute | solution.py:341
  13.3 0.4 collective-permute-start.4
  13.7 0.3 select_tails.1.rest_ref
  14.0 0.3 select_rows.1.one_ref
  14.4 0.3 collective-permute-done.2.refs_1_
  14.7 1.4 %collective-permute-done.3.refs_2_ = s16[2,136,128]{2,1,0:T(8,128)(2,1)S(1)} collective-permute-done((s16[2,136,128]{2,1,0:T(8,128)(2,1)S(1)}, s16[2,136,128]{2,1,0:T(8,128)(2,1)S(1)}, u32[]{:S(2)}, u32[]{:S(2)}) %collective-permute-start.3) | collective-permute-done | bytes 69664 | tf_op jit(solution)/shard_map/ppermute | solution.py:341
  16.1 2.4 %collective-permute-done.4.refs_3_ = s16[2,136,128]{2,1,0:T(8,128)(2,1)S(1)} collective-permute-done((s16[2,136,128]{2,1,0:T(8,128)(2,1)S(1)}, s16[2,136,128]{2,1,0:T(8,128)(2,1)S(1)}, u32[]{:S(2)}, u32[]{:S(2)}) %collective-permute-start.4) | collective-permute-done | bytes 69664 | tf_op jit(solution)/shard_map/ppermute | solution.py:341
  18.5 0.3 add_sums.2.refs_0_
  18.8 1.9 %collective-permute-start.5 = (s16[2,136,128]{2,1,0:T(8,128)(2,1)S(1)}, s16[2,136,128]{2,1,0:T(8,128)(2,1)S(1)}, u32[]{:S(2)}, u32[]{:S(2)}) collective-permute-start(s16[2,136,128]{2,1,0:T(8,128)(2,1)S(1)} %add_sums.2.refs_0_), channel_id=1, source_target_pairs={{0,8},{1,9},{2,10},{3,11},{4,12},{5,13},{6,14},{7,15},{8,0},{9,1},... | collective-permute-start | bytes 208904 | tf_op jit(solution)/shard_map/ppermute | solution.py:341
  20.6 0.1 collective-permute-start.6
  20.7 4.1 %collective-permute-done.5.refs_1_ = s16[2,136,128]{2,1,0:T(8,128)(2,1)S(1)} collective-permute-done((s16[2,136,128]{2,1,0:T(8,128)(2,1)S(1)}, s16[2,136,128]{2,1,0:T(8,128)(2,1)S(1)}, u32[]{:S(2)}, u32[]{:S(2)}) %collective-permute-start.5) | collective-permute-done | bytes 69664 | tf_op jit(solution)/shard_map/ppermute | solution.py:341
  24.9 0.1 collective-permute-start.7
  25.1 1.9 %collective-permute-start.9 = (bf16[32,3072]{1,0:T(8,128)(2,1)S(1)}, bf16[32,3072]{1,0:T(8,128)(2,1)S(1)}, u32[]{:S(2)}, u32[]{:S(2)}) collective-permute-start(bf16[32,3072]{1,0:T(8,128)(2,1)S(1)} %constant_dynamic-update-slice_fusion.refs_0_), channel_id=1, source_target_pairs={{0,6},{1,7},{2,4},{3,5},{4,2},{5,3},{6,0},{7,1},{8,14},{9,15},{10,... | collective-permute-start | bytes 589832 | tf_op jit(solution)/shard_map/ppermute | solution.py:341
  26.9 1.5 %collective-permute-start.8 = (bf16[32,3072]{1,0:T(8,128)(2,1)S(1)}, bf16[32,3072]{1,0:T(8,128)(2,1)S(1)}, u32[]{:S(2)}, u32[]{:S(2)}) collective-permute-start(bf16[32,3072]{1,0:T(8,128)(2,1)S(1)} %constant_dynamic-update-slice_fusion.refs_0_), channel_id=1, source_target_pairs={{0,2},{1,3},{2,0},{3,1},{4,6},{5,7},{6,4},{7,5},{8,10},{9,11},{10,... | collective-permute-start | bytes 589832 | tf_op jit(solution)/shard_map/ppermute | solution.py:341
  28.5 0.3 add_sums.3
  28.7 0.6 %collective-permute-start.12 = (s16[2,136,128]{2,1,0:T(8,128)(2,1)S(1)}, s16[2,136,128]{2,1,0:T(8,128)(2,1)S(1)}, u32[]{:S(2)}, u32[]{:S(2)}) collective-permute-start(s16[2,136,128]{2,1,0:T(8,128)(2,1)S(1)} %add_sums.3), channel_id=1, source_target_pairs={{0,2},{1,3},{2,0},{3,1},{4,6},{5,7},{6,4},{7,5},{8,10},{9,11},{10,... | collective-permute-start | bytes 208904 | tf_op jit(solution)/shard_map/ppermute | solution.py:341
  29.3 0.2 collective-permute-start.11
  29.5 3.3 %collective-permute-done.7.refs_1_ = bf16[32,3072]{1,0:T(8,128)(2,1)S(1)} collective-permute-done((bf16[32,3072]{1,0:T(8,128)(2,1)S(1)}, bf16[32,3072]{1,0:T(8,128)(2,1)S(1)}, u32[]{:S(2)}, u32[]{:S(2)}) %collective-permute-start.7) | collective-permute-done | bytes 196640 | tf_op jit(solution)/shard_map/ppermute | solution.py:341
  32.8 0.1 collective-permute-start.13
  32.9 2.5 %collective-permute-done.9.refs_3_ = bf16[32,3072]{1,0:T(8,128)(2,1)S(1)} collective-permute-done((bf16[32,3072]{1,0:T(8,128)(2,1)S(1)}, bf16[32,3072]{1,0:T(8,128)(2,1)S(1)}, u32[]{:S(2)}, u32[]{:S(2)}) %collective-permute-start.9) | collective-permute-done | bytes 196640 | tf_op jit(solution)/shard_map/ppermute | solution.py:341
  35.4 1.1 %collective-permute-done.8.refs_2_ = bf16[32,3072]{1,0:T(8,128)(2,1)S(1)} collective-permute-done((bf16[32,3072]{1,0:T(8,128)(2,1)S(1)}, bf16[32,3072]{1,0:T(8,128)(2,1)S(1)}, u32[]{:S(2)}, u32[]{:S(2)}) %collective-permute-start.8) | collective-permute-done | bytes 196640 | tf_op jit(solution)/shard_map/ppermute | solution.py:341
  36.5 0.4 picked_rows.1.x_ref.x_own
  37.0 0.3 collective-permute-done.12
  37.2 0.8 %collective-permute-done.13 = s16[2,136,128]{2,1,0:T(8,128)(2,1)S(1)} collective-permute-done((s16[2,136,128]{2,1,0:T(8,128)(2,1)S(1)}, s16[2,136,128]{2,1,0:T(8,128)(2,1)S(1)}, u32[]{:S(2)}, u32[]{:S(2)}) %collective-permute-start.13) | collective-permute-done | bytes 69664 | tf_op jit(solution)/shard_map/ppermute | solution.py:341
  38.1 0.1 collective-permute-start.14
  38.2 2.1 %own_half_products.1 = (f32[96,640]{1,0:T(8,128)S(1)}, f32[128,96]{1,0:T(8,128)S(1)}, f32[32,4096]{1,0:T(8,128)S(1)}) custom-call(bf16[640,8192]{1,0:T(8,128)(2,1)S(1)} %get-tuple-element.23.feat_ref, s16[8,136,128]{2,1,0:T(8,128)(2,1)S(1)} %constant_dynamic-update-slice_fusion.2.code_ref, bf16[96,4096]{1,0:T(8,128)(2,1)S(1)} %picked_rows.1.x_ref.x_own), custom_call_target="tpu_custom_call" | custom-call | tf_op jit(solution)/shard_map/own_half_products/pallas_call | solution.py:431
  40.3 3.7 %pursuit.1 = (f32[3,640]{1,0:T(4,128)}, f32[32,8192]{1,0:T(8,128)}) custom-call(s32[640]{0:T(1024)S(1)} %copy-done.1, bf16[640,8192]{1,0:T(8,128)(2,1)S(1)} %get-tuple-element.23.feat_ref, bf16[96,4096]{1,0:T(8,128)(2,1)S(1)} %picked_rows.1.x_ref.x_own, bf16[96,4096]{1,0:T(8,128)(2,1)S(1)} %collective-permute-done.10.x_twin, ...), custom_call_target="tpu_custom_call" | custom-call | tf_op jit(solution)/shard_map/pursuit/pallas_call | solution.py:445
  (19 shorter events, 0.2 us)
Async XLA Ops:
  0.6 13.0 %copy-start = (s32[3,32]{1,0:T(4,128)S(1)}, s32[3,32]{1,0:T(4,128)}, u32[]{:S(2)}) copy-start(s32[3,32]{1,0:T(4,128)} %pick_ref.1) | copy-start | bytes 1156
  5.7 34.7 %copy-start.1 = (s32[640]{0:T(1024)S(1)}, s32[640]{0:T(1024)}, u32[]{:S(2)}) copy-start(s32[640]{0:T(1024)} %labels_ref.1) | copy-start | bytes 7684
  5.7 4.2 %collective-permute-start = (f32[264,512]{1,0:T(8,128)S(1)}, f32[264,512]{1,0:T(8,128)S(1)}, u32[]{:S(2)}, u32[]{:S(2)}) collective-permute-start(f32[264,512]{1,0:T(8,128)S(1)} %get-tuple-element.25), channel_id=1, source_target_pairs={{0,1},{1,0},{2,3},{3,2},{4,5},{5,4},{6,7},{7,6},{8,9},{9,8},{10,11... | collective-permute-start | bytes 1622024 | tf_op jit(solution)/shard_map/ppermute | solution.py:341
  6.2 14.4 %collective-permute-start.1 = (bf16[2,8,3072]{2,1,0:T(8,128)(2,1)S(1)}, bf16[2,8,3072]{2,1,0:T(8,128)(2,1)S(1)}, u32[]{:S(2)}, u32[]{:S(2)}) collective-permute-start(bf16[2,8,3072]{2,1,0:T(8,128)(2,1)S(1)} %pack_rows.1), channel_id=1, source_target_pairs={{0,8},{1,9},{2,10},{3,11},{4,12},{5,13},{6,14},{7,15},{8,0},{9,1},... | collective-permute-start | bytes 294920 | tf_op jit(solution)/shard_map/ppermute | solution.py:341
  10.1 4.6 %collective-permute-start.2 = (s16[2,136,128]{2,1,0:T(8,128)(2,1)S(1)}, s16[2,136,128]{2,1,0:T(8,128)(2,1)S(1)}, u32[]{:S(2)}, u32[]{:S(2)}) collective-permute-start(s16[2,136,128]{2,1,0:T(8,128)(2,1)S(1)} %get-tuple-element.29), channel_id=1, source_target_pairs={{0,4},{1,5},{2,6},{3,7},{4,0},{5,1},{6,2},{7,3},{8,12},{9,13},{10,... | collective-permute-start | bytes 208904 | tf_op jit(solution)/shard_map/ppermute | solution.py:341
  11.8 4.3 %collective-permute-start.3 = (s16[2,136,128]{2,1,0:T(8,128)(2,1)S(1)}, s16[2,136,128]{2,1,0:T(8,128)(2,1)S(1)}, u32[]{:S(2)}, u32[]{:S(2)}) collective-permute-start(s16[2,136,128]{2,1,0:T(8,128)(2,1)S(1)} %get-tuple-element.31), channel_id=1, source_target_pairs={{0,2},{1,3},{2,0},{3,1},{4,6},{5,7},{6,4},{7,5},{8,10},{9,11},{10,... | collective-permute-start | bytes 208904 | tf_op jit(solution)/shard_map/ppermute | solution.py:341
  13.3 5.2 %collective-permute-start.4 = (s16[2,136,128]{2,1,0:T(8,128)(2,1)S(1)}, s16[2,136,128]{2,1,0:T(8,128)(2,1)S(1)}, u32[]{:S(2)}, u32[]{:S(2)}) collective-permute-start(s16[2,136,128]{2,1,0:T(8,128)(2,1)S(1)} %get-tuple-element.32), channel_id=1, source_target_pairs={{0,6},{1,7},{2,4},{3,5},{4,2},{5,3},{6,0},{7,1},{8,14},{9,15},{10,... | collective-permute-start | bytes 208904 | tf_op jit(solution)/shard_map/ppermute | solution.py:341
  18.8 6.1 %collective-permute-start.5 = (s16[2,136,128]{2,1,0:T(8,128)(2,1)S(1)}, s16[2,136,128]{2,1,0:T(8,128)(2,1)S(1)}, u32[]{:S(2)}, u32[]{:S(2)}) collective-permute-start(s16[2,136,128]{2,1,0:T(8,128)(2,1)S(1)} %add_sums.2.refs_0_), channel_id=1, source_target_pairs={{0,8},{1,9},{2,10},{3,11},{4,12},{5,13},{6,14},{7,15},{8,0},{9,1},... | collective-permute-start | bytes 208904 | tf_op jit(solution)/shard_map/ppermute | solution.py:341
  20.6 4.2 %collective-permute-start.6 = (bf16[16,3072]{1,0:T(8,128)(2,1)S(1)}, bf16[16,3072]{1,0:T(8,128)(2,1)S(1)}, u32[]{:S(2)}, u32[]{:S(2)}) collective-permute-start(bf16[16,3072]{1,0:T(8,128)(2,1)S(1)} %get-tuple-element.35), channel_id=1, source_target_pairs={{0,1},{1,0},{2,3},{3,2},{4,5},{5,4},{6,7},{7,6},{8,9},{9,8},{10,11... | collective-permute-start | bytes 294920 | tf_op jit(solution)/shard_map/ppermute | solution.py:341
  24.9 7.9 %collective-permute-start.7 = (bf16[32,3072]{1,0:T(8,128)(2,1)S(1)}, bf16[32,3072]{1,0:T(8,128)(2,1)S(1)}, u32[]{:S(2)}, u32[]{:S(2)}) collective-permute-start(bf16[32,3072]{1,0:T(8,128)(2,1)S(1)} %constant_dynamic-update-slice_fusion.refs_0_), channel_id=1, source_target_pairs={{0,4},{1,5},{2,6},{3,7},{4,0},{5,1},{6,2},{7,3},{8,12},{9,13},{10,... | collective-permute-start | bytes 589832 | tf_op jit(solution)/shard_map/ppermute | solution.py:341
  25.1 10.4 %collective-permute-start.9 = (bf16[32,3072]{1,0:T(8,128)(2,1)S(1)}, bf16[32,3072]{1,0:T(8,128)(2,1)S(1)}, u32[]{:S(2)}, u32[]{:S(2)}) collective-permute-start(bf16[32,3072]{1,0:T(8,128)(2,1)S(1)} %constant_dynamic-update-slice_fusion.refs_0_), channel_id=1, source_target_pairs={{0,6},{1,7},{2,4},{3,5},{4,2},{5,3},{6,0},{7,1},{8,14},{9,15},{10,... | collective-permute-start | bytes 589832 | tf_op jit(solution)/shard_map/ppermute | solution.py:341
  26.9 9.5 %collective-permute-start.8 = (bf16[32,3072]{1,0:T(8,128)(2,1)S(1)}, bf16[32,3072]{1,0:T(8,128)(2,1)S(1)}, u32[]{:S(2)}, u32[]{:S(2)}) collective-permute-start(bf16[32,3072]{1,0:T(8,128)(2,1)S(1)} %constant_dynamic-update-slice_fusion.refs_0_), channel_id=1, source_target_pairs={{0,2},{1,3},{2,0},{3,1},{4,6},{5,7},{6,4},{7,5},{8,10},{9,11},{10,... | collective-permute-start | bytes 589832 | tf_op jit(solution)/shard_map/ppermute | solution.py:341
  28.7 8.5 %collective-permute-start.12 = (s16[2,136,128]{2,1,0:T(8,128)(2,1)S(1)}, s16[2,136,128]{2,1,0:T(8,128)(2,1)S(1)}, u32[]{:S(2)}, u32[]{:S(2)}) collective-permute-start(s16[2,136,128]{2,1,0:T(8,128)(2,1)S(1)} %add_sums.3), channel_id=1, source_target_pairs={{0,2},{1,3},{2,0},{3,1},{4,6},{5,7},{6,4},{7,5},{8,10},{9,11},{10,... | collective-permute-start | bytes 208904 | tf_op jit(solution)/shard_map/ppermute | solution.py:341
  29.3 7.9 %collective-permute-start.11 = (s16[2,136,128]{2,1,0:T(8,128)(2,1)S(1)}, s16[2,136,128]{2,1,0:T(8,128)(2,1)S(1)}, u32[]{:S(2)}, u32[]{:S(2)}) collective-permute-start(s16[2,136,128]{2,1,0:T(8,128)(2,1)S(1)} %add_sums.3), channel_id=1, source_target_pairs={{0,4},{1,5},{2,6},{3,7},{4,0},{5,1},{6,2},{7,3},{8,12},{9,13},{10,... | collective-permute-start | bytes 208904 | tf_op jit(solution)/shard_map/ppermute | solution.py:341
  32.8 5.2 %collective-permute-start.13 = (s16[2,136,128]{2,1,0:T(8,128)(2,1)S(1)}, s16[2,136,128]{2,1,0:T(8,128)(2,1)S(1)}, u32[]{:S(2)}, u32[]{:S(2)}) collective-permute-start(s16[2,136,128]{2,1,0:T(8,128)(2,1)S(1)} %add_sums.3), channel_id=1, source_target_pairs={{0,6},{1,7},{2,4},{3,5},{4,2},{5,3},{6,0},{7,1},{8,14},{9,15},{10,... | collective-permute-start | bytes 208904 | tf_op jit(solution)/shard_map/ppermute | solution.py:341
  36.9 3.4 %collective-permute-start.10 = (bf16[96,4096]{1,0:T(8,128)(2,1)S(1)}, bf16[96,4096]{1,0:T(8,128)(2,1)S(1)}, u32[]{:S(2)}, u32[]{:S(2)}) collective-permute-start(bf16[96,4096]{1,0:T(8,128)(2,1)S(1)} %picked_rows.1.x_ref.x_own), channel_id=1, source_target_pairs={{0,1},{1,0},{2,3},{3,2},{4,5},{5,4},{6,7},{7,6},{8,9},{9,8},{10,11... | collective-permute-start | bytes 2359304 | tf_op jit(solution)/shard_map/ppermute | solution.py:341
  38.1 2.2 %collective-permute-start.14 = (s16[8,136,128]{2,1,0:T(8,128)(2,1)S(1)}, s16[8,136,128]{2,1,0:T(8,128)(2,1)S(1)}, u32[]{:S(2)}, u32[]{:S(2)}) collective-permute-start(s16[8,136,128]{2,1,0:T(8,128)(2,1)S(1)} %constant_dynamic-update-slice_fusion.2.code_ref), channel_id=1, source_target_pairs={{0,1},{1,0},{2,3},{3,2},{4,5},{5,4},{6,7},{7,6},{8,9},{9,8},{10,11... | collective-permute-start | bytes 835592 | tf_op jit(solution)/shard_map/ppermute | solution.py:341

commit v23 on v20

--- a/solution.py
+++ b/solution.py
@@ -215,7 +215,8 @@
     far = jnp.zeros_like(pick)
     for b in range(3, bits):
         far = far + (((away >> b) & 1) << (bits - 1 - b))
-    near = ((away >> 2) & 1) + 2 * ((away >> 1) & 1)
+    by_y, by_z = (away >> 1) & 1, (away >> 2) & 1
+    near = 3 * by_z + 2 * by_y - 4 * by_z * by_y
     spot = (2 * near + (away & 1)) * (n_ex // 8) + far
     step = lax.broadcasted_iota(jnp.int32, pick.shape, 0)
     line = lax.broadcasted_iota(jnp.int32, (lines, classes), 0)
@@ -398,7 +399,7 @@
         part_sum = add([part_sum, more], mask == far_masks[-1])
     near = jnp.concatenate([after(packed[0], more), given], axis=0)
     parts = [near] + near_swaps([near] * 4)
-    own_parts = [part_sum] + near_swaps([None, after(part_sum, parts[1]), part_sum, part_sum])
+    own_parts = [part_sum] + near_swaps([None, after(part_sum, parts[3]), part_sum, part_sum])
 
     x = pl.pallas_call(
         functools.partial(picked_kernel, steps=steps),
@@ -408,7 +409,7 @@
         scratch_shapes=[pltpu.VMEM((n_ex * 8, main), bf16)],
         compiler_params=limit,
         name="picked_rows",
-    )(one, rest, *parts)
+    )(one, rest, parts[0], *parts[:0:-1])
 
     x_twin = swap(x, 1)
     own_half = jnp.concatenate(after(own_parts, x), axis=0)

time: 43.8 us -> 43.2 us (0.986)
  waiting for transfers between devices: 15.3 us -> 14.4 us
    ppermute x15, waiting for transfers between devices: 15.3 us -> 14.4 us  [swap(): return lax.ppermute(x, 'ex', [(d, d ^ mask) for d in range(n_ex)])]
  transfers between devices with their start and end apart: 15 -> 15, of which waited for: 8 -> 10; matrix products, arithmetic and copies ran while one was open for 0% -> 0% of each run, Pallas kernels for 9% -> 9%
where the time goes in v23:
time: 43.2 us; the launch traced here: 42.9 us
  starting transfers between devices  15.6 us (36%)
  waiting for transfers between devices  14.4 us (33%)
  Pallas kernels  12.1 us (28%)
  between operations  0.79 us (2%)
    ppermute x15, starting transfers between devices, swap(): return lax.ppermute(x, 'ex', [(d, d ^ mask) for d in range(n_ex)])  15.6 us
    ppermute x15, waiting for transfers between devices, swap(): return lax.ppermute(x, 'ex', [(d, d ^ mask) for d in range(n_ex)])  14.4 us
    pallas_call x1, Pallas kernels, on_device(): pl.pallas_call(functools.partial(sums_kernel, n_ex=n_ex), in_specs=[hbm]...  5.02 us
    pallas_call x1, Pallas kernels, on_device(): pl.pallas_call(functools.partial(pursuit_kernel, steps=steps, scale=1.0 /...  3.19 us
    pallas_call x1, Pallas kernels, on_device(): pl.pallas_call(functools.partial(half_kernel, classes=classes), in_specs=...  2.06 us
  transfers between devices with their start and end apart: 15, of which 10 were waited for; matrix products, arithmetic and copies ran while one was open for 0% of the time, Pallas kernels for 9%

profile of v23, /device:TPU:0, one launch (start us, length us, event | category | flops | bytes accessed | tf_op | source)
XLA Modules:
  0.0 42.9 jit_solution(8231150085684585585)
XLA Ops:
  0.6 5.0 %class_sums.1 = (bf16[640,8192]{1,0:T(8,128)(2,1)S(1)}, f32[264,512]{1,0:T(8,128)S(1)}, f32[264,512]{1,0:T(8,128)S(1)}, f32[8,8192]{1,0:T(8,128)S(1)}) custom-call(s32[640]{0:T(1024)} %labels_ref.1, s32[3,32]{1,0:T(4,128)} %pick_ref.1, bf16[640,8192]{1,0:T(8,128)(2,1)} %feat_hbm.1), custom_call_target="tpu_custom_call" | custom-call | tf_op jit(solution)/shard_map/class_sums/pallas_call | solution.py:334
  5.7 0.5 %collective-permute-start = (f32[264,512]{1,0:T(8,128)S(1)}, f32[264,512]{1,0:T(8,128)S(1)}, u32[]{:S(2)}, u32[]{:S(2)}) collective-permute-start(f32[264,512]{1,0:T(8,128)S(1)} %get-tuple-element.25), channel_id=1, source_target_pairs={{0,1},{1,0},{2,3},{3,2},{4,5},{5,4},{6,7},{7,6},{8,9},{9,8},{10,11... | collective-permute-start | bytes 1622024 | tf_op jit(solution)/shard_map/ppermute | solution.py:329
  6.2 3.7 %collective-permute-start.1 = (bf16[2,8,3072]{2,1,0:T(8,128)(2,1)S(1)}, bf16[2,8,3072]{2,1,0:T(8,128)(2,1)S(1)}, u32[]{:S(2)}, u32[]{:S(2)}) collective-permute-start(bf16[2,8,3072]{2,1,0:T(8,128)(2,1)S(1)} %pack_rows.1), channel_id=1, source_target_pairs={{0,8},{1,9},{2,10},{3,11},{4,12},{5,13},{6,14},{7,15},{8,0},{9,1},... | collective-permute-start | bytes 294920 | tf_op jit(solution)/shard_map/ppermute | solution.py:329
  9.9 0.2 pair_sums.1
  10.1 2.6 %collective-permute-start.2 = (s16[2,136,128]{2,1,0:T(8,128)(2,1)S(1)}, s16[2,136,128]{2,1,0:T(8,128)(2,1)S(1)}, u32[]{:S(2)}, u32[]{:S(2)}) collective-permute-start(s16[2,136,128]{2,1,0:T(8,128)(2,1)S(1)} %get-tuple-element.29), channel_id=1, source_target_pairs={{0,6},{1,7},{2,4},{3,5},{4,2},{5,3},{6,0},{7,1},{8,14},{9,15},{10,... | collective-permute-start | bytes 208904 | tf_op jit(solution)/shard_map/ppermute | solution.py:329
  12.7 0.5 %collective-permute-start.3 = (s16[2,136,128]{2,1,0:T(8,128)(2,1)S(1)}, s16[2,136,128]{2,1,0:T(8,128)(2,1)S(1)}, u32[]{:S(2)}, u32[]{:S(2)}) collective-permute-start(s16[2,136,128]{2,1,0:T(8,128)(2,1)S(1)} %get-tuple-element.31), channel_id=1, source_target_pairs={{0,2},{1,3},{2,0},{3,1},{4,6},{5,7},{6,4},{7,5},{8,10},{9,11},{10,... | collective-permute-start | bytes 208904 | tf_op jit(solution)/shard_map/ppermute | solution.py:329
  13.2 0.5 %collective-permute-start.4 = (s16[2,136,128]{2,1,0:T(8,128)(2,1)S(1)}, s16[2,136,128]{2,1,0:T(8,128)(2,1)S(1)}, u32[]{:S(2)}, u32[]{:S(2)}) collective-permute-start(s16[2,136,128]{2,1,0:T(8,128)(2,1)S(1)} %get-tuple-element.32), channel_id=1, source_target_pairs={{0,4},{1,5},{2,6},{3,7},{4,0},{5,1},{6,2},{7,3},{8,12},{9,13},{10,... | collective-permute-start | bytes 208904 | tf_op jit(solution)/shard_map/ppermute | solution.py:329
  13.7 0.3 select_tails.1.rest_ref
  14.0 0.3 select_rows.1.one_ref
  14.4 1.2 %collective-permute-done.2.refs_1_ = s16[2,136,128]{2,1,0:T(8,128)(2,1)S(1)} collective-permute-done((s16[2,136,128]{2,1,0:T(8,128)(2,1)S(1)}, s16[2,136,128]{2,1,0:T(8,128)(2,1)S(1)}, u32[]{:S(2)}, u32[]{:S(2)}) %collective-permute-start.2) | collective-permute-done | bytes 69664 | tf_op jit(solution)/shard_map/ppermute | solution.py:329
  15.6 1.4 %collective-permute-done.3.refs_2_ = s16[2,136,128]{2,1,0:T(8,128)(2,1)S(1)} collective-permute-done((s16[2,136,128]{2,1,0:T(8,128)(2,1)S(1)}, s16[2,136,128]{2,1,0:T(8,128)(2,1)S(1)}, u32[]{:S(2)}, u32[]{:S(2)}) %collective-permute-start.3) | collective-permute-done | bytes 69664 | tf_op jit(solution)/shard_map/ppermute | solution.py:329
  17.0 0.8 %collective-permute-done.4.refs_3_ = s16[2,136,128]{2,1,0:T(8,128)(2,1)S(1)} collective-permute-done((s16[2,136,128]{2,1,0:T(8,128)(2,1)S(1)}, s16[2,136,128]{2,1,0:T(8,128)(2,1)S(1)}, u32[]{:S(2)}, u32[]{:S(2)}) %collective-permute-start.4) | collective-permute-done | bytes 69664 | tf_op jit(solution)/shard_map/ppermute | solution.py:329
  17.9 0.3 add_sums.2.refs_0_
  18.1 2.0 %collective-permute-start.5 = (s16[2,136,128]{2,1,0:T(8,128)(2,1)S(1)}, s16[2,136,128]{2,1,0:T(8,128)(2,1)S(1)}, u32[]{:S(2)}, u32[]{:S(2)}) collective-permute-start(s16[2,136,128]{2,1,0:T(8,128)(2,1)S(1)} %add_sums.2.refs_0_), channel_id=1, source_target_pairs={{0,8},{1,9},{2,10},{3,11},{4,12},{5,13},{6,14},{7,15},{8,0},{9,1},... | collective-permute-start | bytes 208904 | tf_op jit(solution)/shard_map/ppermute | solution.py:329
  20.1 0.1 collective-permute-start.6
  20.2 4.6 %collective-permute-done.5.refs_1_ = s16[2,136,128]{2,1,0:T(8,128)(2,1)S(1)} collective-permute-done((s16[2,136,128]{2,1,0:T(8,128)(2,1)S(1)}, s16[2,136,128]{2,1,0:T(8,128)(2,1)S(1)}, u32[]{:S(2)}, u32[]{:S(2)}) %collective-permute-start.5) | collective-permute-done | bytes 69664 | tf_op jit(solution)/shard_map/ppermute | solution.py:329
  24.9 0.1 collective-permute-start.7
  25.0 1.9 %collective-permute-start.9 = (bf16[32,3072]{1,0:T(8,128)(2,1)S(1)}, bf16[32,3072]{1,0:T(8,128)(2,1)S(1)}, u32[]{:S(2)}, u32[]{:S(2)}) collective-permute-start(bf16[32,3072]{1,0:T(8,128)(2,1)S(1)} %constant_dynamic-update-slice_fusion.refs_0_), channel_id=1, source_target_pairs={{0,4},{1,5},{2,6},{3,7},{4,0},{5,1},{6,2},{7,3},{8,12},{9,13},{10,... | collective-permute-start | bytes 589832 | tf_op jit(solution)/shard_map/ppermute | solution.py:329
  26.9 1.5 %collective-permute-start.8 = (bf16[32,3072]{1,0:T(8,128)(2,1)S(1)}, bf16[32,3072]{1,0:T(8,128)(2,1)S(1)}, u32[]{:S(2)}, u32[]{:S(2)}) collective-permute-start(bf16[32,3072]{1,0:T(8,128)(2,1)S(1)} %constant_dynamic-update-slice_fusion.refs_0_), channel_id=1, source_target_pairs={{0,2},{1,3},{2,0},{3,1},{4,6},{5,7},{6,4},{7,5},{8,10},{9,11},{10,... | collective-permute-start | bytes 589832 | tf_op jit(solution)/shard_map/ppermute | solution.py:329
  28.4 0.3 add_sums.3
  28.7 0.1 collective-permute-start.13
  28.8 1.4 %collective-permute-start.12 = (s16[2,136,128]{2,1,0:T(8,128)(2,1)S(1)}, s16[2,136,128]{2,1,0:T(8,128)(2,1)S(1)}, u32[]{:S(2)}, u32[]{:S(2)}) collective-permute-start(s16[2,136,128]{2,1,0:T(8,128)(2,1)S(1)} %add_sums.3), channel_id=1, source_target_pairs={{0,2},{1,3},{2,0},{3,1},{4,6},{5,7},{6,4},{7,5},{8,10},{9,11},{10,... | collective-permute-start | bytes 208904 | tf_op jit(solution)/shard_map/ppermute | solution.py:329
  30.3 2.9 %collective-permute-done.7.refs_1_ = bf16[32,3072]{1,0:T(8,128)(2,1)S(1)} collective-permute-done((bf16[32,3072]{1,0:T(8,128)(2,1)S(1)}, bf16[32,3072]{1,0:T(8,128)(2,1)S(1)}, u32[]{:S(2)}, u32[]{:S(2)}) %collective-permute-start.7) | collective-permute-done | bytes 196640 | tf_op jit(solution)/shard_map/ppermute | solution.py:329
  33.2 0.5 %collective-permute-start.11 = (s16[2,136,128]{2,1,0:T(8,128)(2,1)S(1)}, s16[2,136,128]{2,1,0:T(8,128)(2,1)S(1)}, u32[]{:S(2)}, u32[]{:S(2)}) collective-permute-start(s16[2,136,128]{2,1,0:T(8,128)(2,1)S(1)} %add_sums.3), channel_id=1, source_target_pairs={{0,4},{1,5},{2,6},{3,7},{4,0},{5,1},{6,2},{7,3},{8,12},{9,13},{10,... | collective-permute-start | bytes 208904 | tf_op jit(solution)/shard_map/ppermute | solution.py:329
  33.7 1.2 %collective-permute-done.9.refs_3_ = bf16[32,3072]{1,0:T(8,128)(2,1)S(1)} collective-permute-done((bf16[32,3072]{1,0:T(8,128)(2,1)S(1)}, bf16[32,3072]{1,0:T(8,128)(2,1)S(1)}, u32[]{:S(2)}, u32[]{:S(2)}) %collective-permute-start.9) | collective-permute-done | bytes 196640 | tf_op jit(solution)/shard_map/ppermute | solution.py:329
  35.0 0.2 collective-permute-done.8.refs_2_
  35.2 0.4 picked_rows.1.x_ref.x_own
  35.7 0.4 collective-permute-done.13
  36.1 0.6 %collective-permute-done.12 = s16[2,136,128]{2,1,0:T(8,128)(2,1)S(1)} collective-permute-done((s16[2,136,128]{2,1,0:T(8,128)(2,1)S(1)}, s16[2,136,128]{2,1,0:T(8,128)(2,1)S(1)}, u32[]{:S(2)}, u32[]{:S(2)}) %collective-permute-start.12) | collective-permute-done | bytes 69664 | tf_op jit(solution)/shard_map/ppermute | solution.py:329
  36.7 0.8 %collective-permute-done.11 = s16[2,136,128]{2,1,0:T(8,128)(2,1)S(1)} collective-permute-done((s16[2,136,128]{2,1,0:T(8,128)(2,1)S(1)}, s16[2,136,128]{2,1,0:T(8,128)(2,1)S(1)}, u32[]{:S(2)}, u32[]{:S(2)}) %collective-permute-start.11) | collective-permute-done | bytes 69664 | tf_op jit(solution)/shard_map/ppermute | solution.py:329
  37.7 2.1 %own_half_products.1 = (f32[96,640]{1,0:T(8,128)S(1)}, f32[128,96]{1,0:T(8,128)S(1)}, f32[32,4096]{1,0:T(8,128)S(1)}) custom-call(bf16[640,8192]{1,0:T(8,128)(2,1)S(1)} %get-tuple-element.23.feat_ref, s16[8,136,128]{2,1,0:T(8,128)(2,1)S(1)} %constant_dynamic-update-slice_fusion.2.code_ref, bf16[96,4096]{1,0:T(8,128)(2,1)S(1)} %picked_rows.1.x_ref.x_own), custom_call_target="tpu_custom_call" | custom-call | tf_op jit(solution)/shard_map/own_half_products/pallas_call | solution.py:418
  39.8 3.2 %pursuit.1 = (f32[3,640]{1,0:T(4,128)}, f32[32,8192]{1,0:T(8,128)}) custom-call(s32[640]{0:T(1024)S(1)} %copy-done.1, bf16[640,8192]{1,0:T(8,128)(2,1)S(1)} %get-tuple-element.23.feat_ref, bf16[96,4096]{1,0:T(8,128)(2,1)S(1)} %picked_rows.1.x_ref.x_own, bf16[96,4096]{1,0:T(8,128)(2,1)S(1)} %collective-permute-done.10.x_twin, ...), custom_call_target="tpu_custom_call" | custom-call | tf_op jit(solution)/shard_map/pursuit/pallas_call | solution.py:432
  (19 shorter events, 0.3 us)
Async XLA Ops:
  0.6 13.0 %copy-start = (s32[3,32]{1,0:T(4,128)S(1)}, s32[3,32]{1,0:T(4,128)}, u32[]{:S(2)}) copy-start(s32[3,32]{1,0:T(4,128)} %pick_ref.1) | copy-start | bytes 1156
  5.7 34.1 %copy-start.1 = (s32[640]{0:T(1024)S(1)}, s32[640]{0:T(1024)}, u32[]{:S(2)}) copy-start(s32[640]{0:T(1024)} %labels_ref.1) | copy-start | bytes 7684
  5.7 4.2 %collective-permute-start = (f32[264,512]{1,0:T(8,128)S(1)}, f32[264,512]{1,0:T(8,128)S(1)}, u32[]{:S(2)}, u32[]{:S(2)}) collective-permute-start(f32[264,512]{1,0:T(8,128)S(1)} %get-tuple-element.25), channel_id=1, source_target_pairs={{0,1},{1,0},{2,3},{3,2},{4,5},{5,4},{6,7},{7,6},{8,9},{9,8},{10,11... | collective-permute-start | bytes 1622024 | tf_op jit(solution)/shard_map/ppermute | solution.py:329
  6.2 13.9 %collective-permute-start.1 = (bf16[2,8,3072]{2,1,0:T(8,128)(2,1)S(1)}, bf16[2,8,3072]{2,1,0:T(8,128)(2,1)S(1)}, u32[]{:S(2)}, u32[]{:S(2)}) collective-permute-start(bf16[2,8,3072]{2,1,0:T(8,128)(2,1)S(1)} %pack_rows.1), channel_id=1, source_target_pairs={{0,8},{1,9},{2,10},{3,11},{4,12},{5,13},{6,14},{7,15},{8,0},{9,1},... | collective-permute-start | bytes 294920 | tf_op jit(solution)/shard_map/ppermute | solution.py:329
  10.1 5.5 %collective-permute-start.2 = (s16[2,136,128]{2,1,0:T(8,128)(2,1)S(1)}, s16[2,136,128]{2,1,0:T(8,128)(2,1)S(1)}, u32[]{:S(2)}, u32[]{:S(2)}) collective-permute-start(s16[2,136,128]{2,1,0:T(8,128)(2,1)S(1)} %get-tuple-element.29), channel_id=1, source_target_pairs={{0,6},{1,7},{2,4},{3,5},{4,2},{5,3},{6,0},{7,1},{8,14},{9,15},{10,... | collective-permute-start | bytes 208904 | tf_op jit(solution)/shard_map/ppermute | solution.py:329
  12.7 4.3 %collective-permute-start.3 = (s16[2,136,128]{2,1,0:T(8,128)(2,1)S(1)}, s16[2,136,128]{2,1,0:T(8,128)(2,1)S(1)}, u32[]{:S(2)}, u32[]{:S(2)}) collective-permute-start(s16[2,136,128]{2,1,0:T(8,128)(2,1)S(1)} %get-tuple-element.31), channel_id=1, source_target_pairs={{0,2},{1,3},{2,0},{3,1},{4,6},{5,7},{6,4},{7,5},{8,10},{9,11},{10,... | collective-permute-start | bytes 208904 | tf_op jit(solution)/shard_map/ppermute | solution.py:329
  13.2 4.6 %collective-permute-start.4 = (s16[2,136,128]{2,1,0:T(8,128)(2,1)S(1)}, s16[2,136,128]{2,1,0:T(8,128)(2,1)S(1)}, u32[]{:S(2)}, u32[]{:S(2)}) collective-permute-start(s16[2,136,128]{2,1,0:T(8,128)(2,1)S(1)} %get-tuple-element.32), channel_id=1, source_target_pairs={{0,4},{1,5},{2,6},{3,7},{4,0},{5,1},{6,2},{7,3},{8,12},{9,13},{10,... | collective-permute-start | bytes 208904 | tf_op jit(solution)/shard_map/ppermute | solution.py:329
  18.1 6.7 %collective-permute-start.5 = (s16[2,136,128]{2,1,0:T(8,128)(2,1)S(1)}, s16[2,136,128]{2,1,0:T(8,128)(2,1)S(1)}, u32[]{:S(2)}, u32[]{:S(2)}) collective-permute-start(s16[2,136,128]{2,1,0:T(8,128)(2,1)S(1)} %add_sums.2.refs_0_), channel_id=1, source_target_pairs={{0,8},{1,9},{2,10},{3,11},{4,12},{5,13},{6,14},{7,15},{8,0},{9,1},... | collective-permute-start | bytes 208904 | tf_op jit(solution)/shard_map/ppermute | solution.py:329
  20.1 4.7 %collective-permute-start.6 = (bf16[16,3072]{1,0:T(8,128)(2,1)S(1)}, bf16[16,3072]{1,0:T(8,128)(2,1)S(1)}, u32[]{:S(2)}, u32[]{:S(2)}) collective-permute-start(bf16[16,3072]{1,0:T(8,128)(2,1)S(1)} %get-tuple-element.35), channel_id=1, source_target_pairs={{0,1},{1,0},{2,3},{3,2},{4,5},{5,4},{6,7},{7,6},{8,9},{9,8},{10,11... | collective-permute-start | bytes 294920 | tf_op jit(solution)/shard_map/ppermute | solution.py:329
  24.9 8.4 %collective-permute-start.7 = (bf16[32,3072]{1,0:T(8,128)(2,1)S(1)}, bf16[32,3072]{1,0:T(8,128)(2,1)S(1)}, u32[]{:S(2)}, u32[]{:S(2)}) collective-permute-start(bf16[32,3072]{1,0:T(8,128)(2,1)S(1)} %constant_dynamic-update-slice_fusion.refs_0_), channel_id=1, source_target_pairs={{0,6},{1,7},{2,4},{3,5},{4,2},{5,3},{6,0},{7,1},{8,14},{9,15},{10,... | collective-permute-start | bytes 589832 | tf_op jit(solution)/shard_map/ppermute | solution.py:329
  25.0 10.0 %collective-permute-start.9 = (bf16[32,3072]{1,0:T(8,128)(2,1)S(1)}, bf16[32,3072]{1,0:T(8,128)(2,1)S(1)}, u32[]{:S(2)}, u32[]{:S(2)}) collective-permute-start(bf16[32,3072]{1,0:T(8,128)(2,1)S(1)} %constant_dynamic-update-slice_fusion.refs_0_), channel_id=1, source_target_pairs={{0,4},{1,5},{2,6},{3,7},{4,0},{5,1},{6,2},{7,3},{8,12},{9,13},{10,... | collective-permute-start | bytes 589832 | tf_op jit(solution)/shard_map/ppermute | solution.py:329
  26.9 8.3 %collective-permute-start.8 = (bf16[32,3072]{1,0:T(8,128)(2,1)S(1)}, bf16[32,3072]{1,0:T(8,128)(2,1)S(1)}, u32[]{:S(2)}, u32[]{:S(2)}) collective-permute-start(bf16[32,3072]{1,0:T(8,128)(2,1)S(1)} %constant_dynamic-update-slice_fusion.refs_0_), channel_id=1, source_target_pairs={{0,2},{1,3},{2,0},{3,1},{4,6},{5,7},{6,4},{7,5},{8,10},{9,11},{10,... | collective-permute-start | bytes 589832 | tf_op jit(solution)/shard_map/ppermute | solution.py:329
  28.7 7.4 %collective-permute-start.13 = (s16[2,136,128]{2,1,0:T(8,128)(2,1)S(1)}, s16[2,136,128]{2,1,0:T(8,128)(2,1)S(1)}, u32[]{:S(2)}, u32[]{:S(2)}) collective-permute-start(s16[2,136,128]{2,1,0:T(8,128)(2,1)S(1)} %add_sums.3), channel_id=1, source_target_pairs={{0,6},{1,7},{2,4},{3,5},{4,2},{5,3},{6,0},{7,1},{8,14},{9,15},{10,... | collective-permute-start | bytes 208904 | tf_op jit(solution)/shard_map/ppermute | solution.py:329
  28.8 7.9 %collective-permute-start.12 = (s16[2,136,128]{2,1,0:T(8,128)(2,1)S(1)}, s16[2,136,128]{2,1,0:T(8,128)(2,1)S(1)}, u32[]{:S(2)}, u32[]{:S(2)}) collective-permute-start(s16[2,136,128]{2,1,0:T(8,128)(2,1)S(1)} %add_sums.3), channel_id=1, source_target_pairs={{0,2},{1,3},{2,0},{3,1},{4,6},{5,7},{6,4},{7,5},{8,10},{9,11},{10,... | collective-permute-start | bytes 208904 | tf_op jit(solution)/shard_map/ppermute | solution.py:329
  33.2 4.3 %collective-permute-start.11 = (s16[2,136,128]{2,1,0:T(8,128)(2,1)S(1)}, s16[2,136,128]{2,1,0:T(8,128)(2,1)S(1)}, u32[]{:S(2)}, u32[]{:S(2)}) collective-permute-start(s16[2,136,128]{2,1,0:T(8,128)(2,1)S(1)} %add_sums.3), channel_id=1, source_target_pairs={{0,4},{1,5},{2,6},{3,7},{4,0},{5,1},{6,2},{7,3},{8,12},{9,13},{10,... | collective-permute-start | bytes 208904 | tf_op jit(solution)/shard_map/ppermute | solution.py:329
  35.6 4.1 %collective-permute-start.10 = (bf16[96,4096]{1,0:T(8,128)(2,1)S(1)}, bf16[96,4096]{1,0:T(8,128)(2,1)S(1)}, u32[]{:S(2)}, u32[]{:S(2)}) collective-permute-start(bf16[96,4096]{1,0:T(8,128)(2,1)S(1)} %picked_rows.1.x_ref.x_own), channel_id=1, source_target_pairs={{0,1},{1,0},{2,3},{3,2},{4,5},{5,4},{6,7},{7,6},{8,9},{9,8},{10,11... | collective-permute-start | bytes 2359304 | tf_op jit(solution)/shard_map/ppermute | solution.py:329
  37.6 2.1 %collective-permute-start.14 = (s16[8,136,128]{2,1,0:T(8,128)(2,1)S(1)}, s16[8,136,128]{2,1,0:T(8,128)(2,1)S(1)}, u32[]{:S(2)}, u32[]{:S(2)}) collective-permute-start(s16[8,136,128]{2,1,0:T(8,128)(2,1)S(1)} %constant_dynamic-update-slice_fusion.2.code_ref), channel_id=1, source_target_pairs={{0,1},{1,0},{2,3},{3,2},{4,5},{5,4},{6,7},{7,6},{8,9},{9,8},{10,11... | collective-permute-start | bytes 835592 | tf_op jit(solution)/shard_map/ppermute | solution.py:329

commit v24 on v23

--- a/solution.py
+++ b/solution.py
@@ -11,6 +11,7 @@
 ridge = 1.0
 slots = 2
 near_masks = (0, 4, 2, 6)
+gather_masks = (0, 2, 4, 6)
 f32 = jnp.float32
 bf16 = jnp.bfloat16
 
@@ -249,7 +250,7 @@
     width = half // code_ref.shape[0]
     here = pl.ds(pl.multiple_of(side * half, half), half)
     for k in range(4 * far):
-        block = k % far * 4 + near_id(near_masks[k // far])
+        block = k % far * 4 + near_id(gather_masks[k // far])
         target = decode(code_ref[k], classes)[0]
         target_ref[:, pl.ds(pl.multiple_of(target_at + block * width, width), width)] = target
         left_ref[:classes, pl.ds(pl.multiple_of(block * width, width), width)] = target.astype(bf16)
@@ -399,7 +400,8 @@
         part_sum = add([part_sum, more], mask == far_masks[-1])
     near = jnp.concatenate([after(packed[0], more), given], axis=0)
     parts = [near] + near_swaps([near] * 4)
-    own_parts = [part_sum] + near_swaps([None, after(part_sum, parts[3]), part_sum, part_sum])
+    pair = jnp.concatenate([after(part_sum, parts[3]), swap(part_sum, 2)], axis=0)
+    own_parts = [pair, swap(pair, 4)]
 
     x = pl.pallas_call(
         functools.partial(picked_kernel, steps=steps),
@@ -409,10 +411,10 @@
         scratch_shapes=[pltpu.VMEM((n_ex * 8, main), bf16)],
         compiler_params=limit,
         name="picked_rows",
-    )(one, rest, parts[0], *parts[:0:-1])
+    )(after(one, own_parts[1]), rest, parts[0], *parts[:0:-1])
 
     x_twin = swap(x, 1)
-    own_half = jnp.concatenate(after(own_parts, x), axis=0)
+    own_half = jnp.concatenate(own_parts, axis=0)
     twin_half = swap(own_half, 1)
     left = pltpu.VMEM((total + classes, full // 2), bf16)
     direct, gram, target = pl.pallas_call(

time: 43.2 us -> 44.2 us (1.023)
  waiting for transfers between devices: 14.4 us -> 15.2 us
    ppermute x15 -> x14, waiting for transfers between devices: 14.4 us -> 15.2 us  [swap(): return lax.ppermute(x, 'ex', [(d, d ^ mask) for d in range(n_ex)])]
    ppermute x15 -> x14, starting transfers between devices: 15.6 us -> 15.9 us  [swap(): return lax.ppermute(x, 'ex', [(d, d ^ mask) for d in range(n_ex)])]
  transfers between devices with their start and end apart: 15 -> 14, of which waited for: 10 -> 7; matrix products, arithmetic and copies ran while one was open for 0% -> 0% of each run, Pallas kernels for 9% -> 8%
where the time goes in v24:
time: 44.2 us; the launch traced here: 44.1 us
  starting transfers between devices  15.9 us (36%)
  waiting for transfers between devices  15.2 us (34%)
  Pallas kernels  12.1 us (27%)
  between operations  0.8 us (2%)
    ppermute x14, starting transfers between devices, swap(): return lax.ppermute(x, 'ex', [(d, d ^ mask) for d in range(n_ex)])  15.9 us
    ppermute x14, waiting for transfers between devices, swap(): return lax.ppermute(x, 'ex', [(d, d ^ mask) for d in range(n_ex)])  15.2 us
    pallas_call x1, Pallas kernels, on_device(): pl.pallas_call(functools.partial(sums_kernel, n_ex=n_ex), in_specs=[hbm]...  5.02 us
    pallas_call x1, Pallas kernels, on_device(): pl.pallas_call(functools.partial(pursuit_kernel, steps=steps, scale=1.0 /...  3.19 us
    pallas_call x1, Pallas kernels, on_device(): pl.pallas_call(functools.partial(half_kernel, classes=classes), in_specs=...  2.06 us
  transfers between devices with their start and end apart: 14, of which 7 were waited for; matrix products, arithmetic and copies ran while one was open for 0% of the time, Pallas kernels for 8%

profile of v24, /device:TPU:0, one launch (start us, length us, event | category | flops | bytes accessed | tf_op | source)
XLA Modules:
  0.0 44.1 jit_solution(17994931105001941438)
XLA Ops:
  0.6 5.0 %class_sums.1 = (bf16[640,8192]{1,0:T(8,128)(2,1)S(1)}, f32[264,512]{1,0:T(8,128)S(1)}, f32[264,512]{1,0:T(8,128)S(1)}, f32[8,8192]{1,0:T(8,128)S(1)}) custom-call(s32[640]{0:T(1024)} %labels_ref.1, s32[3,32]{1,0:T(4,128)} %pick_ref.1, bf16[640,8192]{1,0:T(8,128)(2,1)} %feat_hbm.1), custom_call_target="tpu_custom_call" | custom-call | tf_op jit(solution)/shard_map/class_sums/pallas_call | solution.py:335
  5.7 0.0 copy-start.1
  5.7 0.5 %collective-permute-start = (f32[264,512]{1,0:T(8,128)S(1)}, f32[264,512]{1,0:T(8,128)S(1)}, u32[]{:S(2)}, u32[]{:S(2)}) collective-permute-start(f32[264,512]{1,0:T(8,128)S(1)} %get-tuple-element.22), channel_id=1, source_target_pairs={{0,1},{1,0},{2,3},{3,2},{4,5},{5,4},{6,7},{7,6},{8,9},{9,8},{10,11... | collective-permute-start | bytes 1622024 | tf_op jit(solution)/shard_map/ppermute | solution.py:330
  6.2 3.7 %collective-permute-start.2 = (bf16[2,8,3072]{2,1,0:T(8,128)(2,1)S(1)}, bf16[2,8,3072]{2,1,0:T(8,128)(2,1)S(1)}, u32[]{:S(2)}, u32[]{:S(2)}) collective-permute-start(bf16[2,8,3072]{2,1,0:T(8,128)(2,1)S(1)} %pack_rows.1), channel_id=1, source_target_pairs={{0,8},{1,9},{2,10},{3,11},{4,12},{5,13},{6,14},{7,15},{8,0},{9,1},... | collective-permute-start | bytes 294920 | tf_op jit(solution)/shard_map/ppermute | solution.py:330
  9.9 0.2 pair_sums.1
  10.1 2.6 %collective-permute-start.1 = (s16[2,136,128]{2,1,0:T(8,128)(2,1)S(1)}, s16[2,136,128]{2,1,0:T(8,128)(2,1)S(1)}, u32[]{:S(2)}, u32[]{:S(2)}) collective-permute-start(s16[2,136,128]{2,1,0:T(8,128)(2,1)S(1)} %get-tuple-element.25), channel_id=1, source_target_pairs={{0,6},{1,7},{2,4},{3,5},{4,2},{5,3},{6,0},{7,1},{8,14},{9,15},{10,... | collective-permute-start | bytes 208904 | tf_op jit(solution)/shard_map/ppermute | solution.py:330
  12.7 0.5 %collective-permute-start.3 = (s16[2,136,128]{2,1,0:T(8,128)(2,1)S(1)}, s16[2,136,128]{2,1,0:T(8,128)(2,1)S(1)}, u32[]{:S(2)}, u32[]{:S(2)}) collective-permute-start(s16[2,136,128]{2,1,0:T(8,128)(2,1)S(1)} %get-tuple-element.28), channel_id=1, source_target_pairs={{0,2},{1,3},{2,0},{3,1},{4,6},{5,7},{6,4},{7,5},{8,10},{9,11},{10,... | collective-permute-start | bytes 208904 | tf_op jit(solution)/shard_map/ppermute | solution.py:330
  13.2 0.5 %collective-permute-start.4 = (s16[2,136,128]{2,1,0:T(8,128)(2,1)S(1)}, s16[2,136,128]{2,1,0:T(8,128)(2,1)S(1)}, u32[]{:S(2)}, u32[]{:S(2)}) collective-permute-start(s16[2,136,128]{2,1,0:T(8,128)(2,1)S(1)} %get-tuple-element.29), channel_id=1, source_target_pairs={{0,4},{1,5},{2,6},{3,7},{4,0},{5,1},{6,2},{7,3},{8,12},{9,13},{10,... | collective-permute-start | bytes 208904 | tf_op jit(solution)/shard_map/ppermute | solution.py:330
  13.7 0.3 select_tails.1.rest_ref
  14.0 0.3 select_rows.1.one_ref
  14.4 1.2 %collective-permute-done.1.refs_1_ = s16[2,136,128]{2,1,0:T(8,128)(2,1)S(1)} collective-permute-done((s16[2,136,128]{2,1,0:T(8,128)(2,1)S(1)}, s16[2,136,128]{2,1,0:T(8,128)(2,1)S(1)}, u32[]{:S(2)}, u32[]{:S(2)}) %collective-permute-start.1) | collective-permute-done | bytes 69664 | tf_op jit(solution)/shard_map/ppermute | solution.py:330
  15.6 1.4 %collective-permute-done.3.refs_2_ = s16[2,136,128]{2,1,0:T(8,128)(2,1)S(1)} collective-permute-done((s16[2,136,128]{2,1,0:T(8,128)(2,1)S(1)}, s16[2,136,128]{2,1,0:T(8,128)(2,1)S(1)}, u32[]{:S(2)}, u32[]{:S(2)}) %collective-permute-start.3) | collective-permute-done | bytes 69664 | tf_op jit(solution)/shard_map/ppermute | solution.py:330
  17.0 0.8 %collective-permute-done.4.refs_3_ = s16[2,136,128]{2,1,0:T(8,128)(2,1)S(1)} collective-permute-done((s16[2,136,128]{2,1,0:T(8,128)(2,1)S(1)}, s16[2,136,128]{2,1,0:T(8,128)(2,1)S(1)}, u32[]{:S(2)}, u32[]{:S(2)}) %collective-permute-start.4) | collective-permute-done | bytes 69664 | tf_op jit(solution)/shard_map/ppermute | solution.py:330
  17.9 0.3 add_sums.2.refs_0_
  18.1 2.0 %collective-permute-start.5 = (s16[2,136,128]{2,1,0:T(8,128)(2,1)S(1)}, s16[2,136,128]{2,1,0:T(8,128)(2,1)S(1)}, u32[]{:S(2)}, u32[]{:S(2)}) collective-permute-start(s16[2,136,128]{2,1,0:T(8,128)(2,1)S(1)} %add_sums.2.refs_0_), channel_id=1, source_target_pairs={{0,8},{1,9},{2,10},{3,11},{4,12},{5,13},{6,14},{7,15},{8,0},{9,1},... | collective-permute-start | bytes 208904 | tf_op jit(solution)/shard_map/ppermute | solution.py:330
  20.1 0.0 collective-permute-done.2
  20.1 0.1 collective-permute-start.6
  20.2 4.6 %collective-permute-done.5.refs_1_ = s16[2,136,128]{2,1,0:T(8,128)(2,1)S(1)} collective-permute-done((s16[2,136,128]{2,1,0:T(8,128)(2,1)S(1)}, s16[2,136,128]{2,1,0:T(8,128)(2,1)S(1)}, u32[]{:S(2)}, u32[]{:S(2)}) %collective-permute-start.5) | collective-permute-done | bytes 69664 | tf_op jit(solution)/shard_map/ppermute | solution.py:330
  24.9 0.1 collective-permute-start.7
  25.0 0.3 add_sums.3
  25.3 1.5 %collective-permute-start.8 = (s16[2,136,128]{2,1,0:T(8,128)(2,1)S(1)}, s16[2,136,128]{2,1,0:T(8,128)(2,1)S(1)}, u32[]{:S(2)}, u32[]{:S(2)}) collective-permute-start(s16[2,136,128]{2,1,0:T(8,128)(2,1)S(1)} %add_sums.3), channel_id=1, source_target_pairs={{0,2},{1,3},{2,0},{3,1},{4,6},{5,7},{6,4},{7,5},{8,10},{9,11},{10,... | collective-permute-start | bytes 208904 | tf_op jit(solution)/shard_map/ppermute | solution.py:330
  26.8 2.0 %collective-permute-start.11 = (bf16[32,3072]{1,0:T(8,128)(2,1)S(1)}, bf16[32,3072]{1,0:T(8,128)(2,1)S(1)}, u32[]{:S(2)}, u32[]{:S(2)}) collective-permute-start(bf16[32,3072]{1,0:T(8,128)(2,1)S(1)} %constant_dynamic-update-slice_fusion.refs_0_), channel_id=1, source_target_pairs={{0,4},{1,5},{2,6},{3,7},{4,0},{5,1},{6,2},{7,3},{8,12},{9,13},{10,... | collective-permute-start | bytes 589832 | tf_op jit(solution)/shard_map/ppermute | solution.py:330
  28.8 0.6 %collective-permute-start.10 = (bf16[32,3072]{1,0:T(8,128)(2,1)S(1)}, bf16[32,3072]{1,0:T(8,128)(2,1)S(1)}, u32[]{:S(2)}, u32[]{:S(2)}) collective-permute-start(bf16[32,3072]{1,0:T(8,128)(2,1)S(1)} %constant_dynamic-update-slice_fusion.refs_0_), channel_id=1, source_target_pairs={{0,2},{1,3},{2,0},{3,1},{4,6},{5,7},{6,4},{7,5},{8,10},{9,11},{10,... | collective-permute-start | bytes 589832 | tf_op jit(solution)/shard_map/ppermute | solution.py:330
  29.3 3.2 %collective-permute-done.7.refs_1_ = bf16[32,3072]{1,0:T(8,128)(2,1)S(1)} collective-permute-done((bf16[32,3072]{1,0:T(8,128)(2,1)S(1)}, bf16[32,3072]{1,0:T(8,128)(2,1)S(1)}, u32[]{:S(2)}, u32[]{:S(2)}) %collective-permute-start.7) | collective-permute-done | bytes 196640 | tf_op jit(solution)/shard_map/ppermute | solution.py:330
  32.5 0.1 collective-permute-done.8
  32.6 1.3 %collective-permute-start.9 = (s16[4,136,128]{2,1,0:T(8,128)(2,1)S(1)}, s16[4,136,128]{2,1,0:T(8,128)(2,1)S(1)}, u32[]{:S(2)}, u32[]{:S(2)}) collective-permute-start(s16[4,136,128]{2,1,0:T(8,128)(2,1)S(1)} %pad_add_fusion), channel_id=1, source_target_pairs={{0,4},{1,5},{2,6},{3,7},{4,0},{5,1},{6,2},{7,3},{8,12},{9,13},{10,... | collective-permute-start | bytes 417800 | tf_op jit(solution)/shard_map/ppermute | solution.py:330
  33.9 3.8 %collective-permute-done.9 = s16[4,136,128]{2,1,0:T(8,128)(2,1)S(1)} collective-permute-done((s16[4,136,128]{2,1,0:T(8,128)(2,1)S(1)}, s16[4,136,128]{2,1,0:T(8,128)(2,1)S(1)}, u32[]{:S(2)}, u32[]{:S(2)}) %collective-permute-start.9) | collective-permute-done | bytes 139296 | tf_op jit(solution)/shard_map/ppermute | solution.py:330
  37.7 0.4 picked_rows.1.x_ref.x_own
  38.1 0.1 collective-permute-start.12
  38.3 0.5 %collective-permute-start.13 = (s16[8,136,128]{2,1,0:T(8,128)(2,1)S(1)}, s16[8,136,128]{2,1,0:T(8,128)(2,1)S(1)}, u32[]{:S(2)}, u32[]{:S(2)}) collective-permute-start(s16[8,136,128]{2,1,0:T(8,128)(2,1)S(1)} %constant_dynamic-update-slice_fusion.2.code_ref), channel_id=1, source_target_pairs={{0,1},{1,0},{2,3},{3,2},{4,5},{5,4},{6,7},{7,6},{8,9},{9,8},{10,11... | collective-permute-start | bytes 835592 | tf_op jit(solution)/shard_map/ppermute | solution.py:330
  38.8 2.1 %own_half_products.1 = (f32[96,640]{1,0:T(8,128)S(1)}, f32[128,96]{1,0:T(8,128)S(1)}, f32[32,4096]{1,0:T(8,128)S(1)}) custom-call(bf16[640,8192]{1,0:T(8,128)(2,1)S(1)} %get-tuple-element.20.feat_ref, s16[8,136,128]{2,1,0:T(8,128)(2,1)S(1)} %constant_dynamic-update-slice_fusion.2.code_ref, bf16[96,4096]{1,0:T(8,128)(2,1)S(1)} %picked_rows.1.x_ref.x_own), custom_call_target="tpu_custom_call" | custom-call | tf_op jit(solution)/shard_map/own_half_products/pallas_call | solution.py:420
  40.9 3.2 %pursuit.1 = (f32[3,640]{1,0:T(4,128)}, f32[32,8192]{1,0:T(8,128)}) custom-call(s32[640]{0:T(1024)S(1)} %copy-done.1, bf16[640,8192]{1,0:T(8,128)(2,1)S(1)} %get-tuple-element.20.feat_ref, bf16[96,4096]{1,0:T(8,128)(2,1)S(1)} %picked_rows.1.x_ref.x_own, bf16[96,4096]{1,0:T(8,128)(2,1)S(1)} %collective-permute-done.12.x_twin, ...), custom_call_target="tpu_custom_call" | custom-call | tf_op jit(solution)/shard_map/pursuit/pallas_call | solution.py:434
  (17 shorter events, 0.1 us)
Async XLA Ops:
  0.6 13.0 %copy-start = (s32[3,32]{1,0:T(4,128)S(1)}, s32[3,32]{1,0:T(4,128)}, u32[]{:S(2)}) copy-start(s32[3,32]{1,0:T(4,128)} %pick_ref.1) | copy-start | bytes 1156
  5.7 35.2 %copy-start.1 = (s32[640]{0:T(1024)S(1)}, s32[640]{0:T(1024)}, u32[]{:S(2)}) copy-start(s32[640]{0:T(1024)} %labels_ref.1) | copy-start | bytes 7684
  5.7 4.2 %collective-permute-start = (f32[264,512]{1,0:T(8,128)S(1)}, f32[264,512]{1,0:T(8,128)S(1)}, u32[]{:S(2)}, u32[]{:S(2)}) collective-permute-start(f32[264,512]{1,0:T(8,128)S(1)} %get-tuple-element.22), channel_id=1, source_target_pairs={{0,1},{1,0},{2,3},{3,2},{4,5},{5,4},{6,7},{7,6},{8,9},{9,8},{10,11... | collective-permute-start | bytes 1622024 | tf_op jit(solution)/shard_map/ppermute | solution.py:330
  6.2 13.9 %collective-permute-start.2 = (bf16[2,8,3072]{2,1,0:T(8,128)(2,1)S(1)}, bf16[2,8,3072]{2,1,0:T(8,128)(2,1)S(1)}, u32[]{:S(2)}, u32[]{:S(2)}) collective-permute-start(bf16[2,8,3072]{2,1,0:T(8,128)(2,1)S(1)} %pack_rows.1), channel_id=1, source_target_pairs={{0,8},{1,9},{2,10},{3,11},{4,12},{5,13},{6,14},{7,15},{8,0},{9,1},... | collective-permute-start | bytes 294920 | tf_op jit(solution)/shard_map/ppermute | solution.py:330
  10.1 5.5 %collective-permute-start.1 = (s16[2,136,128]{2,1,0:T(8,128)(2,1)S(1)}, s16[2,136,128]{2,1,0:T(8,128)(2,1)S(1)}, u32[]{:S(2)}, u32[]{:S(2)}) collective-permute-start(s16[2,136,128]{2,1,0:T(8,128)(2,1)S(1)} %get-tuple-element.25), channel_id=1, source_target_pairs={{0,6},{1,7},{2,4},{3,5},{4,2},{5,3},{6,0},{7,1},{8,14},{9,15},{10,... | collective-permute-start | bytes 208904 | tf_op jit(solution)/shard_map/ppermute | solution.py:330
  12.7 4.3 %collective-permute-start.3 = (s16[2,136,128]{2,1,0:T(8,128)(2,1)S(1)}, s16[2,136,128]{2,1,0:T(8,128)(2,1)S(1)}, u32[]{:S(2)}, u32[]{:S(2)}) collective-permute-start(s16[2,136,128]{2,1,0:T(8,128)(2,1)S(1)} %get-tuple-element.28), channel_id=1, source_target_pairs={{0,2},{1,3},{2,0},{3,1},{4,6},{5,7},{6,4},{7,5},{8,10},{9,11},{10,... | collective-permute-start | bytes 208904 | tf_op jit(solution)/shard_map/ppermute | solution.py:330
  13.2 4.6 %collective-permute-start.4 = (s16[2,136,128]{2,1,0:T(8,128)(2,1)S(1)}, s16[2,136,128]{2,1,0:T(8,128)(2,1)S(1)}, u32[]{:S(2)}, u32[]{:S(2)}) collective-permute-start(s16[2,136,128]{2,1,0:T(8,128)(2,1)S(1)} %get-tuple-element.29), channel_id=1, source_target_pairs={{0,4},{1,5},{2,6},{3,7},{4,0},{5,1},{6,2},{7,3},{8,12},{9,13},{10,... | collective-permute-start | bytes 208904 | tf_op jit(solution)/shard_map/ppermute | solution.py:330
  18.1 6.7 %collective-permute-start.5 = (s16[2,136,128]{2,1,0:T(8,128)(2,1)S(1)}, s16[2,136,128]{2,1,0:T(8,128)(2,1)S(1)}, u32[]{:S(2)}, u32[]{:S(2)}) collective-permute-start(s16[2,136,128]{2,1,0:T(8,128)(2,1)S(1)} %add_sums.2.refs_0_), channel_id=1, source_target_pairs={{0,8},{1,9},{2,10},{3,11},{4,12},{5,13},{6,14},{7,15},{8,0},{9,1},... | collective-permute-start | bytes 208904 | tf_op jit(solution)/shard_map/ppermute | solution.py:330
  20.1 4.7 %collective-permute-start.6 = (bf16[16,3072]{1,0:T(8,128)(2,1)S(1)}, bf16[16,3072]{1,0:T(8,128)(2,1)S(1)}, u32[]{:S(2)}, u32[]{:S(2)}) collective-permute-start(bf16[16,3072]{1,0:T(8,128)(2,1)S(1)} %get-tuple-element.32), channel_id=1, source_target_pairs={{0,1},{1,0},{2,3},{3,2},{4,5},{5,4},{6,7},{7,6},{8,9},{9,8},{10,11... | collective-permute-start | bytes 294920 | tf_op jit(solution)/shard_map/ppermute | solution.py:330
  24.9 7.6 %collective-permute-start.7 = (bf16[32,3072]{1,0:T(8,128)(2,1)S(1)}, bf16[32,3072]{1,0:T(8,128)(2,1)S(1)}, u32[]{:S(2)}, u32[]{:S(2)}) collective-permute-start(bf16[32,3072]{1,0:T(8,128)(2,1)S(1)} %constant_dynamic-update-slice_fusion.refs_0_), channel_id=1, source_target_pairs={{0,6},{1,7},{2,4},{3,5},{4,2},{5,3},{6,0},{7,1},{8,14},{9,15},{10,... | collective-permute-start | bytes 589832 | tf_op jit(solution)/shard_map/ppermute | solution.py:330
  25.3 7.3 %collective-permute-start.8 = (s16[2,136,128]{2,1,0:T(8,128)(2,1)S(1)}, s16[2,136,128]{2,1,0:T(8,128)(2,1)S(1)}, u32[]{:S(2)}, u32[]{:S(2)}) collective-permute-start(s16[2,136,128]{2,1,0:T(8,128)(2,1)S(1)} %add_sums.3), channel_id=1, source_target_pairs={{0,2},{1,3},{2,0},{3,1},{4,6},{5,7},{6,4},{7,5},{8,10},{9,11},{10,... | collective-permute-start | bytes 208904 | tf_op jit(solution)/shard_map/ppermute | solution.py:330
  26.8 10.9 %collective-permute-start.11 = (bf16[32,3072]{1,0:T(8,128)(2,1)S(1)}, bf16[32,3072]{1,0:T(8,128)(2,1)S(1)}, u32[]{:S(2)}, u32[]{:S(2)}) collective-permute-start(bf16[32,3072]{1,0:T(8,128)(2,1)S(1)} %constant_dynamic-update-slice_fusion.refs_0_), channel_id=1, source_target_pairs={{0,4},{1,5},{2,6},{3,7},{4,0},{5,1},{6,2},{7,3},{8,12},{9,13},{10,... | collective-permute-start | bytes 589832 | tf_op jit(solution)/shard_map/ppermute | solution.py:330
  28.8 9.0 %collective-permute-start.10 = (bf16[32,3072]{1,0:T(8,128)(2,1)S(1)}, bf16[32,3072]{1,0:T(8,128)(2,1)S(1)}, u32[]{:S(2)}, u32[]{:S(2)}) collective-permute-start(bf16[32,3072]{1,0:T(8,128)(2,1)S(1)} %constant_dynamic-update-slice_fusion.refs_0_), channel_id=1, source_target_pairs={{0,2},{1,3},{2,0},{3,1},{4,6},{5,7},{6,4},{7,5},{8,10},{9,11},{10,... | collective-permute-start | bytes 589832 | tf_op jit(solution)/shard_map/ppermute | solution.py:330
  32.6 5.1 %collective-permute-start.9 = (s16[4,136,128]{2,1,0:T(8,128)(2,1)S(1)}, s16[4,136,128]{2,1,0:T(8,128)(2,1)S(1)}, u32[]{:S(2)}, u32[]{:S(2)}) collective-permute-start(s16[4,136,128]{2,1,0:T(8,128)(2,1)S(1)} %pad_add_fusion), channel_id=1, source_target_pairs={{0,4},{1,5},{2,6},{3,7},{4,0},{5,1},{6,2},{7,3},{8,12},{9,13},{10,... | collective-permute-start | bytes 417800 | tf_op jit(solution)/shard_map/ppermute | solution.py:330
  38.1 2.8 %collective-permute-start.12 = (bf16[96,4096]{1,0:T(8,128)(2,1)S(1)}, bf16[96,4096]{1,0:T(8,128)(2,1)S(1)}, u32[]{:S(2)}, u32[]{:S(2)}) collective-permute-start(bf16[96,4096]{1,0:T(8,128)(2,1)S(1)} %picked_rows.1.x_ref.x_own), channel_id=1, source_target_pairs={{0,1},{1,0},{2,3},{3,2},{4,5},{5,4},{6,7},{7,6},{8,9},{9,8},{10,11... | collective-permute-start | bytes 2359304 | tf_op jit(solution)/shard_map/ppermute | solution.py:330
  38.3 2.6 %collective-permute-start.13 = (s16[8,136,128]{2,1,0:T(8,128)(2,1)S(1)}, s16[8,136,128]{2,1,0:T(8,128)(2,1)S(1)}, u32[]{:S(2)}, u32[]{:S(2)}) collective-permute-start(s16[8,136,128]{2,1,0:T(8,128)(2,1)S(1)} %constant_dynamic-update-slice_fusion.2.code_ref), channel_id=1, source_target_pairs={{0,1},{1,0},{2,3},{3,2},{4,5},{5,4},{6,7},{7,6},{8,9},{9,8},{10,11... | collective-permute-start | bytes 835592 | tf_op jit(solution)/shard_map/ppermute | solution.py:330

commit v25 on v23

--- a/solution.py
+++ b/solution.py
@@ -216,7 +216,7 @@
     for b in range(3, bits):
         far = far + (((away >> b) & 1) << (bits - 1 - b))
     by_y, by_z = (away >> 1) & 1, (away >> 2) & 1
-    near = 3 * by_z + 2 * by_y - 4 * by_z * by_y
+    near = 3 * by_y + 2 * by_z - 4 * by_z * by_y
     spot = (2 * near + (away & 1)) * (n_ex // 8) + far
     step = lax.broadcasted_iota(jnp.int32, pick.shape, 0)
     line = lax.broadcasted_iota(jnp.int32, (lines, classes), 0)
@@ -409,7 +409,7 @@
         scratch_shapes=[pltpu.VMEM((n_ex * 8, main), bf16)],
         compiler_params=limit,
         name="picked_rows",
-    )(one, rest, parts[0], *parts[:0:-1])
+    )(one, rest, parts[0], parts[3], parts[1], parts[2])
 
     x_twin = swap(x, 1)
     own_half = jnp.concatenate(after(own_parts, x), axis=0)

time: 43.2 us -> 43.4 us (level)
  waiting for transfers between devices: 14.4 us -> 14.9 us
    ppermute x15, waiting for transfers between devices: 14.4 us -> 14.9 us  [swap(): return lax.ppermute(x, 'ex', [(d, d ^ mask) for d in range(n_ex)])]
where the time goes in v25:
time: 43.4 us; the launch traced here: 43.2 us
  starting transfers between devices  15.3 us (35%)
  waiting for transfers between devices  14.9 us (34%)
  Pallas kernels  12.1 us (28%)
  between operations  0.8 us (2%)
    ppermute x15, starting transfers between devices, swap(): return lax.ppermute(x, 'ex', [(d, d ^ mask) for d in range(n_ex)])  15.3 us
    ppermute x15, waiting for transfers between devices, swap(): return lax.ppermute(x, 'ex', [(d, d ^ mask) for d in range(n_ex)])  14.9 us
    pallas_call x1, Pallas kernels, on_device(): pl.pallas_call(functools.partial(sums_kernel, n_ex=n_ex), in_specs=[hbm]...  5.02 us
    pallas_call x1, Pallas kernels, on_device(): pl.pallas_call(functools.partial(pursuit_kernel, steps=steps, scale=1.0 /...  3.19 us
    pallas_call x1, Pallas kernels, on_device(): pl.pallas_call(functools.partial(half_kernel, classes=classes), in_specs=...  2.06 us
  transfers between devices with their start and end apart: 15, of which 10 were waited for; matrix products, arithmetic and copies ran while one was open for 0% of the time, Pallas kernels for 9%

profile of v25, /device:TPU:0, one launch (start us, length us, event | category | flops | bytes accessed | tf_op | source)
XLA Modules:
  0.0 43.2 jit_solution(6993691401113337998)
XLA Ops:
  0.6 5.0 %class_sums.1 = (bf16[640,8192]{1,0:T(8,128)(2,1)S(1)}, f32[264,512]{1,0:T(8,128)S(1)}, f32[264,512]{1,0:T(8,128)S(1)}, f32[8,8192]{1,0:T(8,128)S(1)}) custom-call(s32[640]{0:T(1024)} %labels_ref.1, s32[3,32]{1,0:T(4,128)} %pick_ref.1, bf16[640,8192]{1,0:T(8,128)(2,1)} %feat_hbm.1), custom_call_target="tpu_custom_call" | custom-call | tf_op jit(solution)/shard_map/class_sums/pallas_call | solution.py:334
  5.7 0.5 %collective-permute-start = (f32[264,512]{1,0:T(8,128)S(1)}, f32[264,512]{1,0:T(8,128)S(1)}, u32[]{:S(2)}, u32[]{:S(2)}) collective-permute-start(f32[264,512]{1,0:T(8,128)S(1)} %get-tuple-element.25), channel_id=1, source_target_pairs={{0,1},{1,0},{2,3},{3,2},{4,5},{5,4},{6,7},{7,6},{8,9},{9,8},{10,11... | collective-permute-start | bytes 1622024 | tf_op jit(solution)/shard_map/ppermute | solution.py:329
  6.2 3.7 %collective-permute-start.1 = (bf16[2,8,3072]{2,1,0:T(8,128)(2,1)S(1)}, bf16[2,8,3072]{2,1,0:T(8,128)(2,1)S(1)}, u32[]{:S(2)}, u32[]{:S(2)}) collective-permute-start(bf16[2,8,3072]{2,1,0:T(8,128)(2,1)S(1)} %pack_rows.1), channel_id=1, source_target_pairs={{0,8},{1,9},{2,10},{3,11},{4,12},{5,13},{6,14},{7,15},{8,0},{9,1},... | collective-permute-start | bytes 294920 | tf_op jit(solution)/shard_map/ppermute | solution.py:329
  9.9 0.2 pair_sums.1
  10.1 2.6 %collective-permute-start.2 = (s16[2,136,128]{2,1,0:T(8,128)(2,1)S(1)}, s16[2,136,128]{2,1,0:T(8,128)(2,1)S(1)}, u32[]{:S(2)}, u32[]{:S(2)}) collective-permute-start(s16[2,136,128]{2,1,0:T(8,128)(2,1)S(1)} %get-tuple-element.29), channel_id=1, source_target_pairs={{0,6},{1,7},{2,4},{3,5},{4,2},{5,3},{6,0},{7,1},{8,14},{9,15},{10,... | collective-permute-start | bytes 208904 | tf_op jit(solution)/shard_map/ppermute | solution.py:329
  12.7 0.5 %collective-permute-start.3 = (s16[2,136,128]{2,1,0:T(8,128)(2,1)S(1)}, s16[2,136,128]{2,1,0:T(8,128)(2,1)S(1)}, u32[]{:S(2)}, u32[]{:S(2)}) collective-permute-start(s16[2,136,128]{2,1,0:T(8,128)(2,1)S(1)} %get-tuple-element.31), channel_id=1, source_target_pairs={{0,2},{1,3},{2,0},{3,1},{4,6},{5,7},{6,4},{7,5},{8,10},{9,11},{10,... | collective-permute-start | bytes 208904 | tf_op jit(solution)/shard_map/ppermute | solution.py:329
  13.2 0.5 %collective-permute-start.4 = (s16[2,136,128]{2,1,0:T(8,128)(2,1)S(1)}, s16[2,136,128]{2,1,0:T(8,128)(2,1)S(1)}, u32[]{:S(2)}, u32[]{:S(2)}) collective-permute-start(s16[2,136,128]{2,1,0:T(8,128)(2,1)S(1)} %get-tuple-element.32), channel_id=1, source_target_pairs={{0,4},{1,5},{2,6},{3,7},{4,0},{5,1},{6,2},{7,3},{8,12},{9,13},{10,... | collective-permute-start | bytes 208904 | tf_op jit(solution)/shard_map/ppermute | solution.py:329
  13.7 0.3 select_tails.1.rest_ref
  14.0 0.3 select_rows.1.one_ref
  14.4 1.2 %collective-permute-done.2.refs_1_ = s16[2,136,128]{2,1,0:T(8,128)(2,1)S(1)} collective-permute-done((s16[2,136,128]{2,1,0:T(8,128)(2,1)S(1)}, s16[2,136,128]{2,1,0:T(8,128)(2,1)S(1)}, u32[]{:S(2)}, u32[]{:S(2)}) %collective-permute-start.2) | collective-permute-done | bytes 69664 | tf_op jit(solution)/shard_map/ppermute | solution.py:329
  15.6 1.4 %collective-permute-done.3.refs_2_ = s16[2,136,128]{2,1,0:T(8,128)(2,1)S(1)} collective-permute-done((s16[2,136,128]{2,1,0:T(8,128)(2,1)S(1)}, s16[2,136,128]{2,1,0:T(8,128)(2,1)S(1)}, u32[]{:S(2)}, u32[]{:S(2)}) %collective-permute-start.3) | collective-permute-done | bytes 69664 | tf_op jit(solution)/shard_map/ppermute | solution.py:329
  17.0 0.8 %collective-permute-done.4.refs_3_ = s16[2,136,128]{2,1,0:T(8,128)(2,1)S(1)} collective-permute-done((s16[2,136,128]{2,1,0:T(8,128)(2,1)S(1)}, s16[2,136,128]{2,1,0:T(8,128)(2,1)S(1)}, u32[]{:S(2)}, u32[]{:S(2)}) %collective-permute-start.4) | collective-permute-done | bytes 69664 | tf_op jit(solution)/shard_map/ppermute | solution.py:329
  17.9 0.3 add_sums.2.refs_0_
  18.1 2.0 %collective-permute-start.5 = (s16[2,136,128]{2,1,0:T(8,128)(2,1)S(1)}, s16[2,136,128]{2,1,0:T(8,128)(2,1)S(1)}, u32[]{:S(2)}, u32[]{:S(2)}) collective-permute-start(s16[2,136,128]{2,1,0:T(8,128)(2,1)S(1)} %add_sums.2.refs_0_), channel_id=1, source_target_pairs={{0,8},{1,9},{2,10},{3,11},{4,12},{5,13},{6,14},{7,15},{8,0},{9,1},... | collective-permute-start | bytes 208904 | tf_op jit(solution)/shard_map/ppermute | solution.py:329
  20.1 0.1 collective-permute-start.6
  20.2 4.6 %collective-permute-done.5.refs_1_ = s16[2,136,128]{2,1,0:T(8,128)(2,1)S(1)} collective-permute-done((s16[2,136,128]{2,1,0:T(8,128)(2,1)S(1)}, s16[2,136,128]{2,1,0:T(8,128)(2,1)S(1)}, u32[]{:S(2)}, u32[]{:S(2)}) %collective-permute-start.5) | collective-permute-done | bytes 69664 | tf_op jit(solution)/shard_map/ppermute | solution.py:329
  24.9 0.1 collective-permute-start.7
  25.0 1.4 %collective-permute-start.9 = (bf16[32,3072]{1,0:T(8,128)(2,1)S(1)}, bf16[32,3072]{1,0:T(8,128)(2,1)S(1)}, u32[]{:S(2)}, u32[]{:S(2)}) collective-permute-start(bf16[32,3072]{1,0:T(8,128)(2,1)S(1)} %constant_dynamic-update-slice_fusion.refs_0_), channel_id=1, source_target_pairs={{0,2},{1,3},{2,0},{3,1},{4,6},{5,7},{6,4},{7,5},{8,10},{9,11},{10,... | collective-permute-start | bytes 589832 | tf_op jit(solution)/shard_map/ppermute | solution.py:329
  26.4 2.0 %collective-permute-start.8 = (bf16[32,3072]{1,0:T(8,128)(2,1)S(1)}, bf16[32,3072]{1,0:T(8,128)(2,1)S(1)}, u32[]{:S(2)}, u32[]{:S(2)}) collective-permute-start(bf16[32,3072]{1,0:T(8,128)(2,1)S(1)} %constant_dynamic-update-slice_fusion.refs_0_), channel_id=1, source_target_pairs={{0,4},{1,5},{2,6},{3,7},{4,0},{5,1},{6,2},{7,3},{8,12},{9,13},{10,... | collective-permute-start | bytes 589832 | tf_op jit(solution)/shard_map/ppermute | solution.py:329
  28.4 0.3 add_sums.3
  28.7 0.1 collective-permute-start.13
  28.8 1.4 %collective-permute-start.12 = (s16[2,136,128]{2,1,0:T(8,128)(2,1)S(1)}, s16[2,136,128]{2,1,0:T(8,128)(2,1)S(1)}, u32[]{:S(2)}, u32[]{:S(2)}) collective-permute-start(s16[2,136,128]{2,1,0:T(8,128)(2,1)S(1)} %add_sums.3), channel_id=1, source_target_pairs={{0,2},{1,3},{2,0},{3,1},{4,6},{5,7},{6,4},{7,5},{8,10},{9,11},{10,... | collective-permute-start | bytes 208904 | tf_op jit(solution)/shard_map/ppermute | solution.py:329
  30.3 3.2 %collective-permute-done.7.refs_1_ = bf16[32,3072]{1,0:T(8,128)(2,1)S(1)} collective-permute-done((bf16[32,3072]{1,0:T(8,128)(2,1)S(1)}, bf16[32,3072]{1,0:T(8,128)(2,1)S(1)}, u32[]{:S(2)}, u32[]{:S(2)}) %collective-permute-start.7) | collective-permute-done | bytes 196640 | tf_op jit(solution)/shard_map/ppermute | solution.py:329
  33.5 0.3 collective-permute-start.11
  33.7 1.5 %collective-permute-done.9.refs_3_ = bf16[32,3072]{1,0:T(8,128)(2,1)S(1)} collective-permute-done((bf16[32,3072]{1,0:T(8,128)(2,1)S(1)}, bf16[32,3072]{1,0:T(8,128)(2,1)S(1)}, u32[]{:S(2)}, u32[]{:S(2)}) %collective-permute-start.9) | collective-permute-done | bytes 196640 | tf_op jit(solution)/shard_map/ppermute | solution.py:329
  35.2 0.3 collective-permute-done.8.refs_2_
  35.5 0.4 picked_rows.1.x_ref.x_own
  36.0 0.4 collective-permute-done.13
  36.4 0.3 collective-permute-done.12
  36.7 1.1 %collective-permute-done.11 = s16[2,136,128]{2,1,0:T(8,128)(2,1)S(1)} collective-permute-done((s16[2,136,128]{2,1,0:T(8,128)(2,1)S(1)}, s16[2,136,128]{2,1,0:T(8,128)(2,1)S(1)}, u32[]{:S(2)}, u32[]{:S(2)}) %collective-permute-start.11) | collective-permute-done | bytes 69664 | tf_op jit(solution)/shard_map/ppermute | solution.py:329
  37.9 2.1 %own_half_products.1 = (f32[96,640]{1,0:T(8,128)S(1)}, f32[128,96]{1,0:T(8,128)S(1)}, f32[32,4096]{1,0:T(8,128)S(1)}) custom-call(bf16[640,8192]{1,0:T(8,128)(2,1)S(1)} %get-tuple-element.23.feat_ref, s16[8,136,128]{2,1,0:T(8,128)(2,1)S(1)} %constant_dynamic-update-slice_fusion.2.code_ref, bf16[96,4096]{1,0:T(8,128)(2,1)S(1)} %picked_rows.1.x_ref.x_own), custom_call_target="tpu_custom_call" | custom-call | tf_op jit(solution)/shard_map/own_half_products/pallas_call | solution.py:418
  40.0 3.2 %pursuit.1 = (f32[3,640]{1,0:T(4,128)}, f32[32,8192]{1,0:T(8,128)}) custom-call(s32[640]{0:T(1024)S(1)} %copy-done.1, bf16[640,8192]{1,0:T(8,128)(2,1)S(1)} %get-tuple-element.23.feat_ref, bf16[96,4096]{1,0:T(8,128)(2,1)S(1)} %picked_rows.1.x_ref.x_own, bf16[96,4096]{1,0:T(8,128)(2,1)S(1)} %collective-permute-done.10.x_twin, ...), custom_call_target="tpu_custom_call" | custom-call | tf_op jit(solution)/shard_map/pursuit/pallas_call | solution.py:432
  (19 shorter events, 0.3 us)
Async XLA Ops:
  0.6 13.0 %copy-start = (s32[3,32]{1,0:T(4,128)S(1)}, s32[3,32]{1,0:T(4,128)}, u32[]{:S(2)}) copy-start(s32[3,32]{1,0:T(4,128)} %pick_ref.1) | copy-start | bytes 1156
  5.7 34.3 %copy-start.1 = (s32[640]{0:T(1024)S(1)}, s32[640]{0:T(1024)}, u32[]{:S(2)}) copy-start(s32[640]{0:T(1024)} %labels_ref.1) | copy-start | bytes 7684
  5.7 4.2 %collective-permute-start = (f32[264,512]{1,0:T(8,128)S(1)}, f32[264,512]{1,0:T(8,128)S(1)}, u32[]{:S(2)}, u32[]{:S(2)}) collective-permute-start(f32[264,512]{1,0:T(8,128)S(1)} %get-tuple-element.25), channel_id=1, source_target_pairs={{0,1},{1,0},{2,3},{3,2},{4,5},{5,4},{6,7},{7,6},{8,9},{9,8},{10,11... | collective-permute-start | bytes 1622024 | tf_op jit(solution)/shard_map/ppermute | solution.py:329
  6.2 13.9 %collective-permute-start.1 = (bf16[2,8,3072]{2,1,0:T(8,128)(2,1)S(1)}, bf16[2,8,3072]{2,1,0:T(8,128)(2,1)S(1)}, u32[]{:S(2)}, u32[]{:S(2)}) collective-permute-start(bf16[2,8,3072]{2,1,0:T(8,128)(2,1)S(1)} %pack_rows.1), channel_id=1, source_target_pairs={{0,8},{1,9},{2,10},{3,11},{4,12},{5,13},{6,14},{7,15},{8,0},{9,1},... | collective-permute-start | bytes 294920 | tf_op jit(solution)/shard_map/ppermute | solution.py:329
  10.1 5.5 %collective-permute-start.2 = (s16[2,136,128]{2,1,0:T(8,128)(2,1)S(1)}, s16[2,136,128]{2,1,0:T(8,128)(2,1)S(1)}, u32[]{:S(2)}, u32[]{:S(2)}) collective-permute-start(s16[2,136,128]{2,1,0:T(8,128)(2,1)S(1)} %get-tuple-element.29), channel_id=1, source_target_pairs={{0,6},{1,7},{2,4},{3,5},{4,2},{5,3},{6,0},{7,1},{8,14},{9,15},{10,... | collective-permute-start | bytes 208904 | tf_op jit(solution)/shard_map/ppermute | solution.py:329
  12.7 4.3 %collective-permute-start.3 = (s16[2,136,128]{2,1,0:T(8,128)(2,1)S(1)}, s16[2,136,128]{2,1,0:T(8,128)(2,1)S(1)}, u32[]{:S(2)}, u32[]{:S(2)}) collective-permute-start(s16[2,136,128]{2,1,0:T(8,128)(2,1)S(1)} %get-tuple-element.31), channel_id=1, source_target_pairs={{0,2},{1,3},{2,0},{3,1},{4,6},{5,7},{6,4},{7,5},{8,10},{9,11},{10,... | collective-permute-start | bytes 208904 | tf_op jit(solution)/shard_map/ppermute | solution.py:329
  13.2 4.6 %collective-permute-start.4 = (s16[2,136,128]{2,1,0:T(8,128)(2,1)S(1)}, s16[2,136,128]{2,1,0:T(8,128)(2,1)S(1)}, u32[]{:S(2)}, u32[]{:S(2)}) collective-permute-start(s16[2,136,128]{2,1,0:T(8,128)(2,1)S(1)} %get-tuple-element.32), channel_id=1, source_target_pairs={{0,4},{1,5},{2,6},{3,7},{4,0},{5,1},{6,2},{7,3},{8,12},{9,13},{10,... | collective-permute-start | bytes 208904 | tf_op jit(solution)/shard_map/ppermute | solution.py:329
  18.1 6.7 %collective-permute-start.5 = (s16[2,136,128]{2,1,0:T(8,128)(2,1)S(1)}, s16[2,136,128]{2,1,0:T(8,128)(2,1)S(1)}, u32[]{:S(2)}, u32[]{:S(2)}) collective-permute-start(s16[2,136,128]{2,1,0:T(8,128)(2,1)S(1)} %add_sums.2.refs_0_), channel_id=1, source_target_pairs={{0,8},{1,9},{2,10},{3,11},{4,12},{5,13},{6,14},{7,15},{8,0},{9,1},... | collective-permute-start | bytes 208904 | tf_op jit(solution)/shard_map/ppermute | solution.py:329
  20.1 4.7 %collective-permute-start.6 = (bf16[16,3072]{1,0:T(8,128)(2,1)S(1)}, bf16[16,3072]{1,0:T(8,128)(2,1)S(1)}, u32[]{:S(2)}, u32[]{:S(2)}) collective-permute-start(bf16[16,3072]{1,0:T(8,128)(2,1)S(1)} %get-tuple-element.35), channel_id=1, source_target_pairs={{0,1},{1,0},{2,3},{3,2},{4,5},{5,4},{6,7},{7,6},{8,9},{9,8},{10,11... | collective-permute-start | bytes 294920 | tf_op jit(solution)/shard_map/ppermute | solution.py:329
  24.9 8.6 %collective-permute-start.7 = (bf16[32,3072]{1,0:T(8,128)(2,1)S(1)}, bf16[32,3072]{1,0:T(8,128)(2,1)S(1)}, u32[]{:S(2)}, u32[]{:S(2)}) collective-permute-start(bf16[32,3072]{1,0:T(8,128)(2,1)S(1)} %constant_dynamic-update-slice_fusion.refs_0_), channel_id=1, source_target_pairs={{0,6},{1,7},{2,4},{3,5},{4,2},{5,3},{6,0},{7,1},{8,14},{9,15},{10,... | collective-permute-start | bytes 589832 | tf_op jit(solution)/shard_map/ppermute | solution.py:329
  25.0 10.2 %collective-permute-start.9 = (bf16[32,3072]{1,0:T(8,128)(2,1)S(1)}, bf16[32,3072]{1,0:T(8,128)(2,1)S(1)}, u32[]{:S(2)}, u32[]{:S(2)}) collective-permute-start(bf16[32,3072]{1,0:T(8,128)(2,1)S(1)} %constant_dynamic-update-slice_fusion.refs_0_), channel_id=1, source_target_pairs={{0,2},{1,3},{2,0},{3,1},{4,6},{5,7},{6,4},{7,5},{8,10},{9,11},{10,... | collective-permute-start | bytes 589832 | tf_op jit(solution)/shard_map/ppermute | solution.py:329
  26.4 9.0 %collective-permute-start.8 = (bf16[32,3072]{1,0:T(8,128)(2,1)S(1)}, bf16[32,3072]{1,0:T(8,128)(2,1)S(1)}, u32[]{:S(2)}, u32[]{:S(2)}) collective-permute-start(bf16[32,3072]{1,0:T(8,128)(2,1)S(1)} %constant_dynamic-update-slice_fusion.refs_0_), channel_id=1, source_target_pairs={{0,4},{1,5},{2,6},{3,7},{4,0},{5,1},{6,2},{7,3},{8,12},{9,13},{10,... | collective-permute-start | bytes 589832 | tf_op jit(solution)/shard_map/ppermute | solution.py:329
  28.7 7.7 %collective-permute-start.13 = (s16[2,136,128]{2,1,0:T(8,128)(2,1)S(1)}, s16[2,136,128]{2,1,0:T(8,128)(2,1)S(1)}, u32[]{:S(2)}, u32[]{:S(2)}) collective-permute-start(s16[2,136,128]{2,1,0:T(8,128)(2,1)S(1)} %add_sums.3), channel_id=1, source_target_pairs={{0,6},{1,7},{2,4},{3,5},{4,2},{5,3},{6,0},{7,1},{8,14},{9,15},{10,... | collective-permute-start | bytes 208904 | tf_op jit(solution)/shard_map/ppermute | solution.py:329
  28.8 7.9 %collective-permute-start.12 = (s16[2,136,128]{2,1,0:T(8,128)(2,1)S(1)}, s16[2,136,128]{2,1,0:T(8,128)(2,1)S(1)}, u32[]{:S(2)}, u32[]{:S(2)}) collective-permute-start(s16[2,136,128]{2,1,0:T(8,128)(2,1)S(1)} %add_sums.3), channel_id=1, source_target_pairs={{0,2},{1,3},{2,0},{3,1},{4,6},{5,7},{6,4},{7,5},{8,10},{9,11},{10,... | collective-permute-start | bytes 208904 | tf_op jit(solution)/shard_map/ppermute | solution.py:329
  33.5 4.3 %collective-permute-start.11 = (s16[2,136,128]{2,1,0:T(8,128)(2,1)S(1)}, s16[2,136,128]{2,1,0:T(8,128)(2,1)S(1)}, u32[]{:S(2)}, u32[]{:S(2)}) collective-permute-start(s16[2,136,128]{2,1,0:T(8,128)(2,1)S(1)} %add_sums.3), channel_id=1, source_target_pairs={{0,4},{1,5},{2,6},{3,7},{4,0},{5,1},{6,2},{7,3},{8,12},{9,13},{10,... | collective-permute-start | bytes 208904 | tf_op jit(solution)/shard_map/ppermute | solution.py:329
  35.9 4.1 %collective-permute-start.10 = (bf16[96,4096]{1,0:T(8,128)(2,1)S(1)}, bf16[96,4096]{1,0:T(8,128)(2,1)S(1)}, u32[]{:S(2)}, u32[]{:S(2)}) collective-permute-start(bf16[96,4096]{1,0:T(8,128)(2,1)S(1)} %picked_rows.1.x_ref.x_own), channel_id=1, source_target_pairs={{0,1},{1,0},{2,3},{3,2},{4,5},{5,4},{6,7},{7,6},{8,9},{9,8},{10,11... | collective-permute-start | bytes 2359304 | tf_op jit(solution)/shard_map/ppermute | solution.py:329
  37.8 2.1 %collective-permute-start.14 = (s16[8,136,128]{2,1,0:T(8,128)(2,1)S(1)}, s16[8,136,128]{2,1,0:T(8,128)(2,1)S(1)}, u32[]{:S(2)}, u32[]{:S(2)}) collective-permute-start(s16[8,136,128]{2,1,0:T(8,128)(2,1)S(1)} %constant_dynamic-update-slice_fusion.2.code_ref), channel_id=1, source_target_pairs={{0,1},{1,0},{2,3},{3,2},{4,5},{5,4},{6,7},{7,6},{8,9},{9,8},{10,11... | collective-permute-start | bytes 835592 | tf_op jit(solution)/shard_map/ppermute | solution.py:329

commit v26 on v14

--- a/solution.py
+++ b/solution.py
@@ -215,7 +215,8 @@
     far = jnp.zeros_like(pick)
     for b in range(3, bits):
         far = far + (((away >> b) & 1) << (bits - 1 - b))
-    near = ((away >> 2) & 1) + 2 * ((away >> 1) & 1)
+    by_y, by_z = (away >> 1) & 1, (away >> 2) & 1
+    near = 3 * by_z + 2 * by_y - 4 * by_z * by_y
     spot = (2 * near + (away & 1)) * (n_ex // 8) + far
     step = lax.broadcasted_iota(jnp.int32, pick.shape, 0)
     line = lax.broadcasted_iota(jnp.int32, (lines, classes), 0)
@@ -320,6 +321,10 @@
     half = jax.ShapeDtypeStruct((groups * classes + 8, width), f32)
     code = jax.ShapeDtypeStruct((groups // 4, classes * (width // 128) + 8, 128), jnp.int16)
 
+    def near_swaps(x):
+        diagonal_part, by_y = swap(x[3], 6), swap(x[2], 2)
+        return [swap(x[1], 4), by_y, diagonal_part]
+
     def swap(x, mask):
         return lax.ppermute(x, "ex", [(d, d ^ mask) for d in range(n_ex)])
 
@@ -373,8 +378,8 @@
     for mask in reversed(far_masks):
         packed = jnp.concatenate([packed, swap(packed, mask)], axis=1)
 
-    near_codes = [swap(c, m) for c, m in zip(codes[1:], near_masks[1:])]
-    part_sum = add([codes[0], after(near_codes[0], packed)] + near_codes[1:], False)
+    near_codes = near_swaps(codes)
+    part_sum = add([codes[0], after(near_codes[2], packed), near_codes[1], near_codes[0]], False)
 
     def select(tail, *others):
         return pl.pallas_call(
@@ -395,9 +400,8 @@
         part_sum = add([part_sum, swap(part_sum, mask)], mask == far_masks[-1])
     given = swap(after(packed[1], near_sum), 1)
     near = jnp.concatenate([after(packed[0], one), given], axis=0)
-    parts = [near] + [swap(near, m) for m in near_masks[1:]]
-    own_parts = [part_sum] + [swap(part_sum, m) for m in near_masks[1:3]]
-    own_parts.append(swap(after(part_sum, parts[1]), near_masks[3]))
+    parts = [near] + near_swaps([near] * 4)
+    own_parts = [part_sum] + near_swaps([None, after(part_sum, parts[1]), part_sum, part_sum])
 
     x = pl.pallas_call(
         functools.partial(picked_kernel, steps=steps),
@@ -407,7 +411,7 @@
         scratch_shapes=[pltpu.VMEM((n_ex * 8, main), bf16)],
         compiler_params=limit,
         name="picked_rows",
-    )(one, rest, *parts)
+    )(one, rest, parts[0], *parts[:0:-1])
 
     x_twin = swap(x, 1)
     own_half = jnp.concatenate(after(own_parts, x), axis=0)

time: 45.2 us -> 44 us (0.973)
  waiting for transfers between devices: 13.2 us -> 11.1 us
  starting transfers between devices: 18.8 us -> 19.8 us
    ppermute x15, waiting for transfers between devices: 13.2 us -> 11.1 us  [swap(): return lax.ppermute(x, 'ex', [(d, d ^ mask) for d in range(n_ex)])]
    ppermute x15, starting transfers between devices: 18.8 us -> 19.8 us  [swap(): return lax.ppermute(x, 'ex', [(d, d ^ mask) for d in range(n_ex)])]
  transfers between devices with their start and end apart: 15 -> 15, of which waited for: 6 -> 7; matrix products, arithmetic and copies ran while one was open for 0% -> 0% of each run, Pallas kernels for 8% -> 8%
where the time goes in v26:
time: 44 us; the launch traced here: 43.9 us
  starting transfers between devices  19.8 us (45%)
  Pallas kernels  12.1 us (28%)
  waiting for transfers between devices  11.1 us (25%)
  between operations  0.81 us (2%)
    ppermute x15, starting transfers between devices, swap(): return lax.ppermute(x, 'ex', [(d, d ^ mask) for d in range(n_ex)])  19.8 us
    ppermute x15, waiting for transfers between devices, swap(): return lax.ppermute(x, 'ex', [(d, d ^ mask) for d in range(n_ex)])  11.1 us
    pallas_call x1, Pallas kernels, on_device(): pl.pallas_call(functools.partial(sums_kernel, n_ex=n_ex), in_specs=[hbm]...  5.02 us
    pallas_call x1, Pallas kernels, on_device(): pl.pallas_call(functools.partial(pursuit_kernel, steps=steps, scale=1.0 /...  3.19 us
    pallas_call x1, Pallas kernels, on_device(): pl.pallas_call(functools.partial(half_kernel, classes=classes), in_specs=...  2.06 us
  transfers between devices with their start and end apart: 15, of which 7 were waited for; matrix products, arithmetic and copies ran while one was open for 0% of the time, Pallas kernels for 8%

profile of v26, /device:TPU:0, one launch (start us, length us, event | category | flops | bytes accessed | tf_op | source)
XLA Modules:
  0.0 43.9 jit_solution(15402738615255007956)
XLA Ops:
  0.6 5.0 %class_sums.1 = (bf16[640,8192]{1,0:T(8,128)(2,1)S(1)}, f32[264,512]{1,0:T(8,128)S(1)}, f32[264,512]{1,0:T(8,128)S(1)}, f32[8,8192]{1,0:T(8,128)S(1)}) custom-call(s32[640]{0:T(1024)} %labels_ref.1, s32[3,32]{1,0:T(4,128)} %pick_ref.1, bf16[640,8192]{1,0:T(8,128)(2,1)} %feat_hbm.1), custom_call_target="tpu_custom_call" | custom-call | tf_op jit(solution)/shard_map/class_sums/pallas_call | solution.py:334
  5.7 0.5 %collective-permute-start = (f32[264,512]{1,0:T(8,128)S(1)}, f32[264,512]{1,0:T(8,128)S(1)}, u32[]{:S(2)}, u32[]{:S(2)}) collective-permute-start(f32[264,512]{1,0:T(8,128)S(1)} %get-tuple-element.26), channel_id=1, source_target_pairs={{0,1},{1,0},{2,3},{3,2},{4,5},{5,4},{6,7},{7,6},{8,9},{9,8},{10,11... | collective-permute-start | bytes 1622024 | tf_op jit(solution)/shard_map/ppermute | solution.py:329
  6.2 3.7 %collective-permute-start.2 = (bf16[2,8,3072]{2,1,0:T(8,128)(2,1)S(1)}, bf16[2,8,3072]{2,1,0:T(8,128)(2,1)S(1)}, u32[]{:S(2)}, u32[]{:S(2)}) collective-permute-start(bf16[2,8,3072]{2,1,0:T(8,128)(2,1)S(1)} %pack_rows.1), channel_id=1, source_target_pairs={{0,8},{1,9},{2,10},{3,11},{4,12},{5,13},{6,14},{7,15},{8,0},{9,1},... | collective-permute-start | bytes 294920 | tf_op jit(solution)/shard_map/ppermute | solution.py:329
  9.9 0.2 pair_sums.1
  10.1 2.6 %collective-permute-start.1 = (s16[2,136,128]{2,1,0:T(8,128)(2,1)S(1)}, s16[2,136,128]{2,1,0:T(8,128)(2,1)S(1)}, u32[]{:S(2)}, u32[]{:S(2)}) collective-permute-start(s16[2,136,128]{2,1,0:T(8,128)(2,1)S(1)} %get-tuple-element.28), channel_id=1, source_target_pairs={{0,6},{1,7},{2,4},{3,5},{4,2},{5,3},{6,0},{7,1},{8,14},{9,15},{10,... | collective-permute-start | bytes 208904 | tf_op jit(solution)/shard_map/ppermute | solution.py:329
  12.7 0.5 %collective-permute-start.3 = (s16[2,136,128]{2,1,0:T(8,128)(2,1)S(1)}, s16[2,136,128]{2,1,0:T(8,128)(2,1)S(1)}, u32[]{:S(2)}, u32[]{:S(2)}) collective-permute-start(s16[2,136,128]{2,1,0:T(8,128)(2,1)S(1)} %get-tuple-element.31), channel_id=1, source_target_pairs={{0,2},{1,3},{2,0},{3,1},{4,6},{5,7},{6,4},{7,5},{8,10},{9,11},{10,... | collective-permute-start | bytes 208904 | tf_op jit(solution)/shard_map/ppermute | solution.py:329
  13.2 0.5 %collective-permute-start.4 = (s16[2,136,128]{2,1,0:T(8,128)(2,1)S(1)}, s16[2,136,128]{2,1,0:T(8,128)(2,1)S(1)}, u32[]{:S(2)}, u32[]{:S(2)}) collective-permute-start(s16[2,136,128]{2,1,0:T(8,128)(2,1)S(1)} %get-tuple-element.32), channel_id=1, source_target_pairs={{0,4},{1,5},{2,6},{3,7},{4,0},{5,1},{6,2},{7,3},{8,12},{9,13},{10,... | collective-permute-start | bytes 208904 | tf_op jit(solution)/shard_map/ppermute | solution.py:329
  13.7 1.9 %collective-permute-done.2 = bf16[2,8,3072]{2,1,0:T(8,128)(2,1)S(1)} collective-permute-done((bf16[2,8,3072]{2,1,0:T(8,128)(2,1)S(1)}, bf16[2,8,3072]{2,1,0:T(8,128)(2,1)S(1)}, u32[]{:S(2)}, u32[]{:S(2)}) %collective-permute-start.2) | collective-permute-done | bytes 98336 | tf_op jit(solution)/shard_map/ppermute | solution.py:329
  15.6 0.3 select_tails.1.rest_ref
  15.9 1.1 %collective-permute-done.3.refs_2_ = s16[2,136,128]{2,1,0:T(8,128)(2,1)S(1)} collective-permute-done((s16[2,136,128]{2,1,0:T(8,128)(2,1)S(1)}, s16[2,136,128]{2,1,0:T(8,128)(2,1)S(1)}, u32[]{:S(2)}, u32[]{:S(2)}) %collective-permute-start.3) | collective-permute-done | bytes 69664 | tf_op jit(solution)/shard_map/ppermute | solution.py:329
  17.0 0.8 %collective-permute-done.4.refs_3_ = s16[2,136,128]{2,1,0:T(8,128)(2,1)S(1)} collective-permute-done((s16[2,136,128]{2,1,0:T(8,128)(2,1)S(1)}, s16[2,136,128]{2,1,0:T(8,128)(2,1)S(1)}, u32[]{:S(2)}, u32[]{:S(2)}) %collective-permute-start.4) | collective-permute-done | bytes 69664 | tf_op jit(solution)/shard_map/ppermute | solution.py:329
  17.8 0.3 add_sums.2.refs_0_
  18.1 2.0 %collective-permute-start.10 = (s16[2,136,128]{2,1,0:T(8,128)(2,1)S(1)}, s16[2,136,128]{2,1,0:T(8,128)(2,1)S(1)}, u32[]{:S(2)}, u32[]{:S(2)}) collective-permute-start(s16[2,136,128]{2,1,0:T(8,128)(2,1)S(1)} %add_sums.2.refs_0_), channel_id=1, source_target_pairs={{0,8},{1,9},{2,10},{3,11},{4,12},{5,13},{6,14},{7,15},{8,0},{9,1},... | collective-permute-start | bytes 208904 | tf_op jit(solution)/shard_map/ppermute | solution.py:329
  20.1 0.3 select_rows.1.one_ref
  20.4 0.1 collective-permute-start.5
  20.5 1.3 %collective-permute-done.5 = bf16[16,3072]{1,0:T(8,128)(2,1)S(1)} collective-permute-done((bf16[16,3072]{1,0:T(8,128)(2,1)S(1)}, bf16[16,3072]{1,0:T(8,128)(2,1)S(1)}, u32[]{:S(2)}, u32[]{:S(2)}) %collective-permute-start.5) | collective-permute-done | bytes 98336 | tf_op jit(solution)/shard_map/ppermute | solution.py:329
  21.8 2.5 %collective-permute-start.8 = (bf16[32,3072]{1,0:T(8,128)(2,1)S(1)}, bf16[32,3072]{1,0:T(8,128)(2,1)S(1)}, u32[]{:S(2)}, u32[]{:S(2)}) collective-permute-start(bf16[32,3072]{1,0:T(8,128)(2,1)S(1)} %constant_dynamic-update-slice_fusion.refs_0_), channel_id=1, source_target_pairs={{0,4},{1,5},{2,6},{3,7},{4,0},{5,1},{6,2},{7,3},{8,12},{9,13},{10,... | collective-permute-start | bytes 589832 | tf_op jit(solution)/shard_map/ppermute | solution.py:329
  24.3 0.6 %collective-permute-start.7 = (bf16[32,3072]{1,0:T(8,128)(2,1)S(1)}, bf16[32,3072]{1,0:T(8,128)(2,1)S(1)}, u32[]{:S(2)}, u32[]{:S(2)}) collective-permute-start(bf16[32,3072]{1,0:T(8,128)(2,1)S(1)} %constant_dynamic-update-slice_fusion.refs_0_), channel_id=1, source_target_pairs={{0,2},{1,3},{2,0},{3,1},{4,6},{5,7},{6,4},{7,5},{8,10},{9,11},{10,... | collective-permute-start | bytes 589832 | tf_op jit(solution)/shard_map/ppermute | solution.py:329
  24.9 0.9 %collective-permute-start.6 = (bf16[32,3072]{1,0:T(8,128)(2,1)S(1)}, bf16[32,3072]{1,0:T(8,128)(2,1)S(1)}, u32[]{:S(2)}, u32[]{:S(2)}) collective-permute-start(bf16[32,3072]{1,0:T(8,128)(2,1)S(1)} %constant_dynamic-update-slice_fusion.refs_0_), channel_id=1, source_target_pairs={{0,6},{1,7},{2,4},{3,5},{4,2},{5,3},{6,0},{7,1},{8,14},{9,15},{10,... | collective-permute-start | bytes 589832 | tf_op jit(solution)/shard_map/ppermute | solution.py:329
  25.9 0.3 add_sums.3
  26.2 0.0 copy-start.1
  26.2 2.0 %collective-permute-start.13 = (s16[2,136,128]{2,1,0:T(8,128)(2,1)S(1)}, s16[2,136,128]{2,1,0:T(8,128)(2,1)S(1)}, u32[]{:S(2)}, u32[]{:S(2)}) collective-permute-start(s16[2,136,128]{2,1,0:T(8,128)(2,1)S(1)} %add_sums.3), channel_id=1, source_target_pairs={{0,6},{1,7},{2,4},{3,5},{4,2},{5,3},{6,0},{7,1},{8,14},{9,15},{10,... | collective-permute-start | bytes 208904 | tf_op jit(solution)/shard_map/ppermute | solution.py:329
  28.2 1.4 %collective-permute-start.12 = (s16[2,136,128]{2,1,0:T(8,128)(2,1)S(1)}, s16[2,136,128]{2,1,0:T(8,128)(2,1)S(1)}, u32[]{:S(2)}, u32[]{:S(2)}) collective-permute-start(s16[2,136,128]{2,1,0:T(8,128)(2,1)S(1)} %add_sums.3), channel_id=1, source_target_pairs={{0,2},{1,3},{2,0},{3,1},{4,6},{5,7},{6,4},{7,5},{8,10},{9,11},{10,... | collective-permute-start | bytes 208904 | tf_op jit(solution)/shard_map/ppermute | solution.py:329
  29.7 0.4 collective-permute-done.8.refs_3_
  30.0 2.1 %collective-permute-start.11 = (s16[2,136,128]{2,1,0:T(8,128)(2,1)S(1)}, s16[2,136,128]{2,1,0:T(8,128)(2,1)S(1)}, u32[]{:S(2)}, u32[]{:S(2)}) collective-permute-start(s16[2,136,128]{2,1,0:T(8,128)(2,1)S(1)} %add_sums.3), channel_id=1, source_target_pairs={{0,4},{1,5},{2,6},{3,7},{4,0},{5,1},{6,2},{7,3},{8,12},{9,13},{10,... | collective-permute-start | bytes 208904 | tf_op jit(solution)/shard_map/ppermute | solution.py:329
  32.1 5.3 %collective-permute-done.7.refs_2_ = bf16[32,3072]{1,0:T(8,128)(2,1)S(1)} collective-permute-done((bf16[32,3072]{1,0:T(8,128)(2,1)S(1)}, bf16[32,3072]{1,0:T(8,128)(2,1)S(1)}, u32[]{:S(2)}, u32[]{:S(2)}) %collective-permute-start.7) | collective-permute-done | bytes 196640 | tf_op jit(solution)/shard_map/ppermute | solution.py:329
  37.4 0.4 picked_rows.1.x_ref.x_own
  37.8 0.1 collective-permute-start.9
  37.9 0.2 collective-permute-done.12
  38.3 0.3 collective-permute-start.14
  38.6 2.1 %own_half_products.1 = (f32[96,640]{1,0:T(8,128)S(1)}, f32[128,96]{1,0:T(8,128)S(1)}, f32[32,4096]{1,0:T(8,128)S(1)}) custom-call(bf16[640,8192]{1,0:T(8,128)(2,1)S(1)} %get-tuple-element.24.feat_ref, s16[8,136,128]{2,1,0:T(8,128)(2,1)S(1)} %constant_dynamic-update-slice_fusion.2.code_ref, bf16[96,4096]{1,0:T(8,128)(2,1)S(1)} %picked_rows.1.x_ref.x_own), custom_call_target="tpu_custom_call" | custom-call | tf_op jit(solution)/shard_map/own_half_products/pallas_call | solution.py:420
  40.7 3.2 %pursuit.1 = (f32[3,640]{1,0:T(4,128)}, f32[32,8192]{1,0:T(8,128)}) custom-call(s32[640]{0:T(1024)S(1)} %copy-done.1, bf16[640,8192]{1,0:T(8,128)(2,1)S(1)} %get-tuple-element.24.feat_ref, bf16[96,4096]{1,0:T(8,128)(2,1)S(1)} %picked_rows.1.x_ref.x_own, bf16[96,4096]{1,0:T(8,128)(2,1)S(1)} %collective-permute-done.9.x_twin, ...), custom_call_target="tpu_custom_call" | custom-call | tf_op jit(solution)/shard_map/pursuit/pallas_call | solution.py:434
  (19 shorter events, 0.1 us)
Async XLA Ops:
  0.6 14.9 %copy-start = (s32[3,32]{1,0:T(4,128)S(1)}, s32[3,32]{1,0:T(4,128)}, u32[]{:S(2)}) copy-start(s32[3,32]{1,0:T(4,128)} %pick_ref.1) | copy-start | bytes 1156
  5.7 4.2 %collective-permute-start = (f32[264,512]{1,0:T(8,128)S(1)}, f32[264,512]{1,0:T(8,128)S(1)}, u32[]{:S(2)}, u32[]{:S(2)}) collective-permute-start(f32[264,512]{1,0:T(8,128)S(1)} %get-tuple-element.26), channel_id=1, source_target_pairs={{0,1},{1,0},{2,3},{3,2},{4,5},{5,4},{6,7},{7,6},{8,9},{9,8},{10,11... | collective-permute-start | bytes 1622024 | tf_op jit(solution)/shard_map/ppermute | solution.py:329
  6.2 9.3 %collective-permute-start.2 = (bf16[2,8,3072]{2,1,0:T(8,128)(2,1)S(1)}, bf16[2,8,3072]{2,1,0:T(8,128)(2,1)S(1)}, u32[]{:S(2)}, u32[]{:S(2)}) collective-permute-start(bf16[2,8,3072]{2,1,0:T(8,128)(2,1)S(1)} %pack_rows.1), channel_id=1, source_target_pairs={{0,8},{1,9},{2,10},{3,11},{4,12},{5,13},{6,14},{7,15},{8,0},{9,1},... | collective-permute-start | bytes 294920 | tf_op jit(solution)/shard_map/ppermute | solution.py:329
  10.1 5.8 %collective-permute-start.1 = (s16[2,136,128]{2,1,0:T(8,128)(2,1)S(1)}, s16[2,136,128]{2,1,0:T(8,128)(2,1)S(1)}, u32[]{:S(2)}, u32[]{:S(2)}) collective-permute-start(s16[2,136,128]{2,1,0:T(8,128)(2,1)S(1)} %get-tuple-element.28), channel_id=1, source_target_pairs={{0,6},{1,7},{2,4},{3,5},{4,2},{5,3},{6,0},{7,1},{8,14},{9,15},{10,... | collective-permute-start | bytes 208904 | tf_op jit(solution)/shard_map/ppermute | solution.py:329
  12.7 4.3 %collective-permute-start.3 = (s16[2,136,128]{2,1,0:T(8,128)(2,1)S(1)}, s16[2,136,128]{2,1,0:T(8,128)(2,1)S(1)}, u32[]{:S(2)}, u32[]{:S(2)}) collective-permute-start(s16[2,136,128]{2,1,0:T(8,128)(2,1)S(1)} %get-tuple-element.31), channel_id=1, source_target_pairs={{0,2},{1,3},{2,0},{3,1},{4,6},{5,7},{6,4},{7,5},{8,10},{9,11},{10,... | collective-permute-start | bytes 208904 | tf_op jit(solution)/shard_map/ppermute | solution.py:329
  13.2 4.6 %collective-permute-start.4 = (s16[2,136,128]{2,1,0:T(8,128)(2,1)S(1)}, s16[2,136,128]{2,1,0:T(8,128)(2,1)S(1)}, u32[]{:S(2)}, u32[]{:S(2)}) collective-permute-start(s16[2,136,128]{2,1,0:T(8,128)(2,1)S(1)} %get-tuple-element.32), channel_id=1, source_target_pairs={{0,4},{1,5},{2,6},{3,7},{4,0},{5,1},{6,2},{7,3},{8,12},{9,13},{10,... | collective-permute-start | bytes 208904 | tf_op jit(solution)/shard_map/ppermute | solution.py:329
  18.1 7.8 %collective-permute-start.10 = (s16[2,136,128]{2,1,0:T(8,128)(2,1)S(1)}, s16[2,136,128]{2,1,0:T(8,128)(2,1)S(1)}, u32[]{:S(2)}, u32[]{:S(2)}) collective-permute-start(s16[2,136,128]{2,1,0:T(8,128)(2,1)S(1)} %add_sums.2.refs_0_), channel_id=1, source_target_pairs={{0,8},{1,9},{2,10},{3,11},{4,12},{5,13},{6,14},{7,15},{8,0},{9,1},... | collective-permute-start | bytes 208904 | tf_op jit(solution)/shard_map/ppermute | solution.py:329
  20.4 1.4 %collective-permute-start.5 = (bf16[16,3072]{1,0:T(8,128)(2,1)S(1)}, bf16[16,3072]{1,0:T(8,128)(2,1)S(1)}, u32[]{:S(2)}, u32[]{:S(2)}) collective-permute-start(bf16[16,3072]{1,0:T(8,128)(2,1)S(1)} %get-tuple-element.37), channel_id=1, source_target_pairs={{0,1},{1,0},{2,3},{3,2},{4,5},{5,4},{6,7},{7,6},{8,9},{9,8},{10,11... | collective-permute-start | bytes 294920 | tf_op jit(solution)/shard_map/ppermute | solution.py:329
  21.8 8.2 %collective-permute-start.8 = (bf16[32,3072]{1,0:T(8,128)(2,1)S(1)}, bf16[32,3072]{1,0:T(8,128)(2,1)S(1)}, u32[]{:S(2)}, u32[]{:S(2)}) collective-permute-start(bf16[32,3072]{1,0:T(8,128)(2,1)S(1)} %constant_dynamic-update-slice_fusion.refs_0_), channel_id=1, source_target_pairs={{0,4},{1,5},{2,6},{3,7},{4,0},{5,1},{6,2},{7,3},{8,12},{9,13},{10,... | collective-permute-start | bytes 589832 | tf_op jit(solution)/shard_map/ppermute | solution.py:329
  24.3 13.1 %collective-permute-start.7 = (bf16[32,3072]{1,0:T(8,128)(2,1)S(1)}, bf16[32,3072]{1,0:T(8,128)(2,1)S(1)}, u32[]{:S(2)}, u32[]{:S(2)}) collective-permute-start(bf16[32,3072]{1,0:T(8,128)(2,1)S(1)} %constant_dynamic-update-slice_fusion.refs_0_), channel_id=1, source_target_pairs={{0,2},{1,3},{2,0},{3,1},{4,6},{5,7},{6,4},{7,5},{8,10},{9,11},{10,... | collective-permute-start | bytes 589832 | tf_op jit(solution)/shard_map/ppermute | solution.py:329
  24.9 12.5 %collective-permute-start.6 = (bf16[32,3072]{1,0:T(8,128)(2,1)S(1)}, bf16[32,3072]{1,0:T(8,128)(2,1)S(1)}, u32[]{:S(2)}, u32[]{:S(2)}) collective-permute-start(bf16[32,3072]{1,0:T(8,128)(2,1)S(1)} %constant_dynamic-update-slice_fusion.refs_0_), channel_id=1, source_target_pairs={{0,6},{1,7},{2,4},{3,5},{4,2},{5,3},{6,0},{7,1},{8,14},{9,15},{10,... | collective-permute-start | bytes 589832 | tf_op jit(solution)/shard_map/ppermute | solution.py:329
  26.2 14.5 %copy-start.1 = (s32[640]{0:T(1024)S(1)}, s32[640]{0:T(1024)}, u32[]{:S(2)}) copy-start(s32[640]{0:T(1024)} %labels_ref.1) | copy-start | bytes 7684
  26.2 11.7 %collective-permute-start.13 = (s16[2,136,128]{2,1,0:T(8,128)(2,1)S(1)}, s16[2,136,128]{2,1,0:T(8,128)(2,1)S(1)}, u32[]{:S(2)}, u32[]{:S(2)}) collective-permute-start(s16[2,136,128]{2,1,0:T(8,128)(2,1)S(1)} %add_sums.3), channel_id=1, source_target_pairs={{0,6},{1,7},{2,4},{3,5},{4,2},{5,3},{6,0},{7,1},{8,14},{9,15},{10,... | collective-permute-start | bytes 208904 | tf_op jit(solution)/shard_map/ppermute | solution.py:329
  28.2 9.9 %collective-permute-start.12 = (s16[2,136,128]{2,1,0:T(8,128)(2,1)S(1)}, s16[2,136,128]{2,1,0:T(8,128)(2,1)S(1)}, u32[]{:S(2)}, u32[]{:S(2)}) collective-permute-start(s16[2,136,128]{2,1,0:T(8,128)(2,1)S(1)} %add_sums.3), channel_id=1, source_target_pairs={{0,2},{1,3},{2,0},{3,1},{4,6},{5,7},{6,4},{7,5},{8,10},{9,11},{10,... | collective-permute-start | bytes 208904 | tf_op jit(solution)/shard_map/ppermute | solution.py:329
  30.0 8.1 %collective-permute-start.11 = (s16[2,136,128]{2,1,0:T(8,128)(2,1)S(1)}, s16[2,136,128]{2,1,0:T(8,128)(2,1)S(1)}, u32[]{:S(2)}, u32[]{:S(2)}) collective-permute-start(s16[2,136,128]{2,1,0:T(8,128)(2,1)S(1)} %add_sums.3), channel_id=1, source_target_pairs={{0,4},{1,5},{2,6},{3,7},{4,0},{5,1},{6,2},{7,3},{8,12},{9,13},{10,... | collective-permute-start | bytes 208904 | tf_op jit(solution)/shard_map/ppermute | solution.py:329
  37.8 2.8 %collective-permute-start.9 = (bf16[96,4096]{1,0:T(8,128)(2,1)S(1)}, bf16[96,4096]{1,0:T(8,128)(2,1)S(1)}, u32[]{:S(2)}, u32[]{:S(2)}) collective-permute-start(bf16[96,4096]{1,0:T(8,128)(2,1)S(1)} %picked_rows.1.x_ref.x_own), channel_id=1, source_target_pairs={{0,1},{1,0},{2,3},{3,2},{4,5},{5,4},{6,7},{7,6},{8,9},{9,8},{10,11... | collective-permute-start | bytes 2359304 | tf_op jit(solution)/shard_map/ppermute | solution.py:329
  38.3 2.4 %collective-permute-start.14 = (s16[8,136,128]{2,1,0:T(8,128)(2,1)S(1)}, s16[8,136,128]{2,1,0:T(8,128)(2,1)S(1)}, u32[]{:S(2)}, u32[]{:S(2)}) collective-permute-start(s16[8,136,128]{2,1,0:T(8,128)(2,1)S(1)} %constant_dynamic-update-slice_fusion.2.code_ref), channel_id=1, source_target_pairs={{0,1},{1,0},{2,3},{3,2},{4,5},{5,4},{6,7},{7,6},{8,9},{9,8},{10,11... | collective-permute-start | bytes 835592 | tf_op jit(solution)/shard_map/ppermute | solution.py:329

commit v27 on v25

--- a/solution.py
+++ b/solution.py
@@ -399,7 +399,7 @@
         part_sum = add([part_sum, more], mask == far_masks[-1])
     near = jnp.concatenate([after(packed[0], more), given], axis=0)
     parts = [near] + near_swaps([near] * 4)
-    own_parts = [part_sum] + near_swaps([None, after(part_sum, parts[3]), part_sum, part_sum])
+    own_parts = [part_sum] + near_swaps([None, part_sum, after(part_sum, parts[3]), part_sum])
 
     x = pl.pallas_call(
         functools.partial(picked_kernel, steps=steps),

time: 43.4 us -> 43.4 us (level)
  waiting for transfers between devices: 14.9 us -> 13.9 us
  starting transfers between devices: 15.3 us -> 16.2 us
    ppermute x15, waiting for transfers between devices: 14.9 us -> 13.9 us  [swap(): return lax.ppermute(x, 'ex', [(d, d ^ mask) for d in range(n_ex)])]
    ppermute x15, starting transfers between devices: 15.3 us -> 16.2 us  [swap(): return lax.ppermute(x, 'ex', [(d, d ^ mask) for d in range(n_ex)])]
where the time goes in v27:
time: 43.4 us; the launch traced here: 43.2 us
  starting transfers between devices  16.2 us (37%)
  waiting for transfers between devices  13.9 us (32%)
  Pallas kernels  12.1 us (28%)
  between operations  0.8 us (2%)
    ppermute x15, starting transfers between devices, swap(): return lax.ppermute(x, 'ex', [(d, d ^ mask) for d in range(n_ex)])  16.2 us
    ppermute x15, waiting for transfers between devices, swap(): return lax.ppermute(x, 'ex', [(d, d ^ mask) for d in range(n_ex)])  13.9 us
    pallas_call x1, Pallas kernels, on_device(): pl.pallas_call(functools.partial(sums_kernel, n_ex=n_ex), in_specs=[hbm]...  5.02 us
    pallas_call x1, Pallas kernels, on_device(): pl.pallas_call(functools.partial(pursuit_kernel, steps=steps, scale=1.0 /...  3.19 us
    pallas_call x1, Pallas kernels, on_device(): pl.pallas_call(functools.partial(half_kernel, classes=classes), in_specs=...  2.06 us
  transfers between devices with their start and end apart: 15, of which 10 were waited for; matrix products, arithmetic and copies ran while one was open for 0% of the time, Pallas kernels for 9%

profile of v27, /device:TPU:0, one launch (start us, length us, event | category | flops | bytes accessed | tf_op | source)
XLA Modules:
  0.0 43.2 jit_solution(4309419041062967816)
XLA Ops:
  0.6 5.0 %class_sums.1 = (bf16[640,8192]{1,0:T(8,128)(2,1)S(1)}, f32[264,512]{1,0:T(8,128)S(1)}, f32[264,512]{1,0:T(8,128)S(1)}, f32[8,8192]{1,0:T(8,128)S(1)}) custom-call(s32[640]{0:T(1024)} %labels_ref.1, s32[3,32]{1,0:T(4,128)} %pick_ref.1, bf16[640,8192]{1,0:T(8,128)(2,1)} %feat_hbm.1), custom_call_target="tpu_custom_call" | custom-call | tf_op jit(solution)/shard_map/class_sums/pallas_call | solution.py:334
  5.7 0.5 %collective-permute-start = (f32[264,512]{1,0:T(8,128)S(1)}, f32[264,512]{1,0:T(8,128)S(1)}, u32[]{:S(2)}, u32[]{:S(2)}) collective-permute-start(f32[264,512]{1,0:T(8,128)S(1)} %get-tuple-element.25), channel_id=1, source_target_pairs={{0,1},{1,0},{2,3},{3,2},{4,5},{5,4},{6,7},{7,6},{8,9},{9,8},{10,11... | collective-permute-start | bytes 1622024 | tf_op jit(solution)/shard_map/ppermute | solution.py:329
  6.2 3.7 %collective-permute-start.1 = (bf16[2,8,3072]{2,1,0:T(8,128)(2,1)S(1)}, bf16[2,8,3072]{2,1,0:T(8,128)(2,1)S(1)}, u32[]{:S(2)}, u32[]{:S(2)}) collective-permute-start(bf16[2,8,3072]{2,1,0:T(8,128)(2,1)S(1)} %pack_rows.1), channel_id=1, source_target_pairs={{0,8},{1,9},{2,10},{3,11},{4,12},{5,13},{6,14},{7,15},{8,0},{9,1},... | collective-permute-start | bytes 294920 | tf_op jit(solution)/shard_map/ppermute | solution.py:329
  9.9 0.2 pair_sums.1
  10.1 2.6 %collective-permute-start.2 = (s16[2,136,128]{2,1,0:T(8,128)(2,1)S(1)}, s16[2,136,128]{2,1,0:T(8,128)(2,1)S(1)}, u32[]{:S(2)}, u32[]{:S(2)}) collective-permute-start(s16[2,136,128]{2,1,0:T(8,128)(2,1)S(1)} %get-tuple-element.29), channel_id=1, source_target_pairs={{0,6},{1,7},{2,4},{3,5},{4,2},{5,3},{6,0},{7,1},{8,14},{9,15},{10,... | collective-permute-start | bytes 208904 | tf_op jit(solution)/shard_map/ppermute | solution.py:329
  12.7 0.5 %collective-permute-start.3 = (s16[2,136,128]{2,1,0:T(8,128)(2,1)S(1)}, s16[2,136,128]{2,1,0:T(8,128)(2,1)S(1)}, u32[]{:S(2)}, u32[]{:S(2)}) collective-permute-start(s16[2,136,128]{2,1,0:T(8,128)(2,1)S(1)} %get-tuple-element.31), channel_id=1, source_target_pairs={{0,2},{1,3},{2,0},{3,1},{4,6},{5,7},{6,4},{7,5},{8,10},{9,11},{10,... | collective-permute-start | bytes 208904 | tf_op jit(solution)/shard_map/ppermute | solution.py:329
  13.2 0.5 %collective-permute-start.4 = (s16[2,136,128]{2,1,0:T(8,128)(2,1)S(1)}, s16[2,136,128]{2,1,0:T(8,128)(2,1)S(1)}, u32[]{:S(2)}, u32[]{:S(2)}) collective-permute-start(s16[2,136,128]{2,1,0:T(8,128)(2,1)S(1)} %get-tuple-element.32), channel_id=1, source_target_pairs={{0,4},{1,5},{2,6},{3,7},{4,0},{5,1},{6,2},{7,3},{8,12},{9,13},{10,... | collective-permute-start | bytes 208904 | tf_op jit(solution)/shard_map/ppermute | solution.py:329
  13.7 0.3 select_tails.1.rest_ref
  14.0 0.3 select_rows.1.one_ref
  14.4 1.2 %collective-permute-done.2.refs_1_ = s16[2,136,128]{2,1,0:T(8,128)(2,1)S(1)} collective-permute-done((s16[2,136,128]{2,1,0:T(8,128)(2,1)S(1)}, s16[2,136,128]{2,1,0:T(8,128)(2,1)S(1)}, u32[]{:S(2)}, u32[]{:S(2)}) %collective-permute-start.2) | collective-permute-done | bytes 69664 | tf_op jit(solution)/shard_map/ppermute | solution.py:329
  15.6 1.4 %collective-permute-done.3.refs_2_ = s16[2,136,128]{2,1,0:T(8,128)(2,1)S(1)} collective-permute-done((s16[2,136,128]{2,1,0:T(8,128)(2,1)S(1)}, s16[2,136,128]{2,1,0:T(8,128)(2,1)S(1)}, u32[]{:S(2)}, u32[]{:S(2)}) %collective-permute-start.3) | collective-permute-done | bytes 69664 | tf_op jit(solution)/shard_map/ppermute | solution.py:329
  17.0 0.8 %collective-permute-done.4.refs_3_ = s16[2,136,128]{2,1,0:T(8,128)(2,1)S(1)} collective-permute-done((s16[2,136,128]{2,1,0:T(8,128)(2,1)S(1)}, s16[2,136,128]{2,1,0:T(8,128)(2,1)S(1)}, u32[]{:S(2)}, u32[]{:S(2)}) %collective-permute-start.4) | collective-permute-done | bytes 69664 | tf_op jit(solution)/shard_map/ppermute | solution.py:329
  17.9 0.3 add_sums.2.refs_0_
  18.1 2.0 %collective-permute-start.5 = (s16[2,136,128]{2,1,0:T(8,128)(2,1)S(1)}, s16[2,136,128]{2,1,0:T(8,128)(2,1)S(1)}, u32[]{:S(2)}, u32[]{:S(2)}) collective-permute-start(s16[2,136,128]{2,1,0:T(8,128)(2,1)S(1)} %add_sums.2.refs_0_), channel_id=1, source_target_pairs={{0,8},{1,9},{2,10},{3,11},{4,12},{5,13},{6,14},{7,15},{8,0},{9,1},... | collective-permute-start | bytes 208904 | tf_op jit(solution)/shard_map/ppermute | solution.py:329
  20.1 0.1 collective-permute-start.6
  20.2 4.6 %collective-permute-done.5.refs_1_ = s16[2,136,128]{2,1,0:T(8,128)(2,1)S(1)} collective-permute-done((s16[2,136,128]{2,1,0:T(8,128)(2,1)S(1)}, s16[2,136,128]{2,1,0:T(8,128)(2,1)S(1)}, u32[]{:S(2)}, u32[]{:S(2)}) %collective-permute-start.5) | collective-permute-done | bytes 69664 | tf_op jit(solution)/shard_map/ppermute | solution.py:329
  24.9 0.1 collective-permute-start.7
  25.0 1.4 %collective-permute-start.9 = (bf16[32,3072]{1,0:T(8,128)(2,1)S(1)}, bf16[32,3072]{1,0:T(8,128)(2,1)S(1)}, u32[]{:S(2)}, u32[]{:S(2)}) collective-permute-start(bf16[32,3072]{1,0:T(8,128)(2,1)S(1)} %constant_dynamic-update-slice_fusion.refs_0_), channel_id=1, source_target_pairs={{0,2},{1,3},{2,0},{3,1},{4,6},{5,7},{6,4},{7,5},{8,10},{9,11},{10,... | collective-permute-start | bytes 589832 | tf_op jit(solution)/shard_map/ppermute | solution.py:329
  26.4 2.0 %collective-permute-start.8 = (bf16[32,3072]{1,0:T(8,128)(2,1)S(1)}, bf16[32,3072]{1,0:T(8,128)(2,1)S(1)}, u32[]{:S(2)}, u32[]{:S(2)}) collective-permute-start(bf16[32,3072]{1,0:T(8,128)(2,1)S(1)} %constant_dynamic-update-slice_fusion.refs_0_), channel_id=1, source_target_pairs={{0,4},{1,5},{2,6},{3,7},{4,0},{5,1},{6,2},{7,3},{8,12},{9,13},{10,... | collective-permute-start | bytes 589832 | tf_op jit(solution)/shard_map/ppermute | solution.py:329
  28.4 0.3 add_sums.3
  28.7 0.1 collective-permute-start.13
  28.8 1.9 %collective-permute-start.11 = (s16[2,136,128]{2,1,0:T(8,128)(2,1)S(1)}, s16[2,136,128]{2,1,0:T(8,128)(2,1)S(1)}, u32[]{:S(2)}, u32[]{:S(2)}) collective-permute-start(s16[2,136,128]{2,1,0:T(8,128)(2,1)S(1)} %add_sums.3), channel_id=1, source_target_pairs={{0,4},{1,5},{2,6},{3,7},{4,0},{5,1},{6,2},{7,3},{8,12},{9,13},{10,... | collective-permute-start | bytes 208904 | tf_op jit(solution)/shard_map/ppermute | solution.py:329
  30.8 2.7 %collective-permute-done.7.refs_1_ = bf16[32,3072]{1,0:T(8,128)(2,1)S(1)} collective-permute-done((bf16[32,3072]{1,0:T(8,128)(2,1)S(1)}, bf16[32,3072]{1,0:T(8,128)(2,1)S(1)}, u32[]{:S(2)}, u32[]{:S(2)}) %collective-permute-start.7) | collective-permute-done | bytes 196640 | tf_op jit(solution)/shard_map/ppermute | solution.py:329
  33.5 0.7 %collective-permute-start.12 = (s16[2,136,128]{2,1,0:T(8,128)(2,1)S(1)}, s16[2,136,128]{2,1,0:T(8,128)(2,1)S(1)}, u32[]{:S(2)}, u32[]{:S(2)}) collective-permute-start(s16[2,136,128]{2,1,0:T(8,128)(2,1)S(1)} %add_sums.3), channel_id=1, source_target_pairs={{0,2},{1,3},{2,0},{3,1},{4,6},{5,7},{6,4},{7,5},{8,10},{9,11},{10,... | collective-permute-start | bytes 208904 | tf_op jit(solution)/shard_map/ppermute | solution.py:329
  34.1 1.1 %collective-permute-done.9.refs_3_ = bf16[32,3072]{1,0:T(8,128)(2,1)S(1)} collective-permute-done((bf16[32,3072]{1,0:T(8,128)(2,1)S(1)}, bf16[32,3072]{1,0:T(8,128)(2,1)S(1)}, u32[]{:S(2)}, u32[]{:S(2)}) %collective-permute-start.9) | collective-permute-done | bytes 196640 | tf_op jit(solution)/shard_map/ppermute | solution.py:329
  35.2 0.3 collective-permute-done.8.refs_2_
  35.5 0.4 picked_rows.1.x_ref.x_own
  36.0 0.3 collective-permute-done.13
  36.3 0.7 %collective-permute-done.11 = s16[2,136,128]{2,1,0:T(8,128)(2,1)S(1)} collective-permute-done((s16[2,136,128]{2,1,0:T(8,128)(2,1)S(1)}, s16[2,136,128]{2,1,0:T(8,128)(2,1)S(1)}, u32[]{:S(2)}, u32[]{:S(2)}) %collective-permute-start.11) | collective-permute-done | bytes 69664 | tf_op jit(solution)/shard_map/ppermute | solution.py:329
  37.0 0.8 %collective-permute-done.12 = s16[2,136,128]{2,1,0:T(8,128)(2,1)S(1)} collective-permute-done((s16[2,136,128]{2,1,0:T(8,128)(2,1)S(1)}, s16[2,136,128]{2,1,0:T(8,128)(2,1)S(1)}, u32[]{:S(2)}, u32[]{:S(2)}) %collective-permute-start.12) | collective-permute-done | bytes 69664 | tf_op jit(solution)/shard_map/ppermute | solution.py:329
  37.9 2.1 %own_half_products.1 = (f32[96,640]{1,0:T(8,128)S(1)}, f32[128,96]{1,0:T(8,128)S(1)}, f32[32,4096]{1,0:T(8,128)S(1)}) custom-call(bf16[640,8192]{1,0:T(8,128)(2,1)S(1)} %get-tuple-element.23.feat_ref, s16[8,136,128]{2,1,0:T(8,128)(2,1)S(1)} %constant_dynamic-update-slice_fusion.2.code_ref, bf16[96,4096]{1,0:T(8,128)(2,1)S(1)} %picked_rows.1.x_ref.x_own), custom_call_target="tpu_custom_call" | custom-call | tf_op jit(solution)/shard_map/own_half_products/pallas_call | solution.py:418
  40.0 3.2 %pursuit.1 = (f32[3,640]{1,0:T(4,128)}, f32[32,8192]{1,0:T(8,128)}) custom-call(s32[640]{0:T(1024)S(1)} %copy-done.1, bf16[640,8192]{1,0:T(8,128)(2,1)S(1)} %get-tuple-element.23.feat_ref, bf16[96,4096]{1,0:T(8,128)(2,1)S(1)} %picked_rows.1.x_ref.x_own, bf16[96,4096]{1,0:T(8,128)(2,1)S(1)} %collective-permute-done.10.x_twin, ...), custom_call_target="tpu_custom_call" | custom-call | tf_op jit(solution)/shard_map/pursuit/pallas_call | solution.py:432
  (19 shorter events, 0.3 us)
Async XLA Ops:
  0.6 13.0 %copy-start = (s32[3,32]{1,0:T(4,128)S(1)}, s32[3,32]{1,0:T(4,128)}, u32[]{:S(2)}) copy-start(s32[3,32]{1,0:T(4,128)} %pick_ref.1) | copy-start | bytes 1156
  5.7 34.3 %copy-start.1 = (s32[640]{0:T(1024)S(1)}, s32[640]{0:T(1024)}, u32[]{:S(2)}) copy-start(s32[640]{0:T(1024)} %labels_ref.1) | copy-start | bytes 7684
  5.7 4.2 %collective-permute-start = (f32[264,512]{1,0:T(8,128)S(1)}, f32[264,512]{1,0:T(8,128)S(1)}, u32[]{:S(2)}, u32[]{:S(2)}) collective-permute-start(f32[264,512]{1,0:T(8,128)S(1)} %get-tuple-element.25), channel_id=1, source_target_pairs={{0,1},{1,0},{2,3},{3,2},{4,5},{5,4},{6,7},{7,6},{8,9},{9,8},{10,11... | collective-permute-start | bytes 1622024 | tf_op jit(solution)/shard_map/ppermute | solution.py:329
  6.2 13.9 %collective-permute-start.1 = (bf16[2,8,3072]{2,1,0:T(8,128)(2,1)S(1)}, bf16[2,8,3072]{2,1,0:T(8,128)(2,1)S(1)}, u32[]{:S(2)}, u32[]{:S(2)}) collective-permute-start(bf16[2,8,3072]{2,1,0:T(8,128)(2,1)S(1)} %pack_rows.1), channel_id=1, source_target_pairs={{0,8},{1,9},{2,10},{3,11},{4,12},{5,13},{6,14},{7,15},{8,0},{9,1},... | collective-permute-start | bytes 294920 | tf_op jit(solution)/shard_map/ppermute | solution.py:329
  10.1 5.5 %collective-permute-start.2 = (s16[2,136,128]{2,1,0:T(8,128)(2,1)S(1)}, s16[2,136,128]{2,1,0:T(8,128)(2,1)S(1)}, u32[]{:S(2)}, u32[]{:S(2)}) collective-permute-start(s16[2,136,128]{2,1,0:T(8,128)(2,1)S(1)} %get-tuple-element.29), channel_id=1, source_target_pairs={{0,6},{1,7},{2,4},{3,5},{4,2},{5,3},{6,0},{7,1},{8,14},{9,15},{10,... | collective-permute-start | bytes 208904 | tf_op jit(solution)/shard_map/ppermute | solution.py:329
  12.7 4.3 %collective-permute-start.3 = (s16[2,136,128]{2,1,0:T(8,128)(2,1)S(1)}, s16[2,136,128]{2,1,0:T(8,128)(2,1)S(1)}, u32[]{:S(2)}, u32[]{:S(2)}) collective-permute-start(s16[2,136,128]{2,1,0:T(8,128)(2,1)S(1)} %get-tuple-element.31), channel_id=1, source_target_pairs={{0,2},{1,3},{2,0},{3,1},{4,6},{5,7},{6,4},{7,5},{8,10},{9,11},{10,... | collective-permute-start | bytes 208904 | tf_op jit(solution)/shard_map/ppermute | solution.py:329
  13.2 4.6 %collective-permute-start.4 = (s16[2,136,128]{2,1,0:T(8,128)(2,1)S(1)}, s16[2,136,128]{2,1,0:T(8,128)(2,1)S(1)}, u32[]{:S(2)}, u32[]{:S(2)}) collective-permute-start(s16[2,136,128]{2,1,0:T(8,128)(2,1)S(1)} %get-tuple-element.32), channel_id=1, source_target_pairs={{0,4},{1,5},{2,6},{3,7},{4,0},{5,1},{6,2},{7,3},{8,12},{9,13},{10,... | collective-permute-start | bytes 208904 | tf_op jit(solution)/shard_map/ppermute | solution.py:329
  18.1 6.7 %collective-permute-start.5 = (s16[2,136,128]{2,1,0:T(8,128)(2,1)S(1)}, s16[2,136,128]{2,1,0:T(8,128)(2,1)S(1)}, u32[]{:S(2)}, u32[]{:S(2)}) collective-permute-start(s16[2,136,128]{2,1,0:T(8,128)(2,1)S(1)} %add_sums.2.refs_0_), channel_id=1, source_target_pairs={{0,8},{1,9},{2,10},{3,11},{4,12},{5,13},{6,14},{7,15},{8,0},{9,1},... | collective-permute-start | bytes 208904 | tf_op jit(solution)/shard_map/ppermute | solution.py:329
  20.1 4.7 %collective-permute-start.6 = (bf16[16,3072]{1,0:T(8,128)(2,1)S(1)}, bf16[16,3072]{1,0:T(8,128)(2,1)S(1)}, u32[]{:S(2)}, u32[]{:S(2)}) collective-permute-start(bf16[16,3072]{1,0:T(8,128)(2,1)S(1)} %get-tuple-element.35), channel_id=1, source_target_pairs={{0,1},{1,0},{2,3},{3,2},{4,5},{5,4},{6,7},{7,6},{8,9},{9,8},{10,11... | collective-permute-start | bytes 294920 | tf_op jit(solution)/shard_map/ppermute | solution.py:329
  24.9 8.6 %collective-permute-start.7 = (bf16[32,3072]{1,0:T(8,128)(2,1)S(1)}, bf16[32,3072]{1,0:T(8,128)(2,1)S(1)}, u32[]{:S(2)}, u32[]{:S(2)}) collective-permute-start(bf16[32,3072]{1,0:T(8,128)(2,1)S(1)} %constant_dynamic-update-slice_fusion.refs_0_), channel_id=1, source_target_pairs={{0,6},{1,7},{2,4},{3,5},{4,2},{5,3},{6,0},{7,1},{8,14},{9,15},{10,... | collective-permute-start | bytes 589832 | tf_op jit(solution)/shard_map/ppermute | solution.py:329
  25.0 10.2 %collective-permute-start.9 = (bf16[32,3072]{1,0:T(8,128)(2,1)S(1)}, bf16[32,3072]{1,0:T(8,128)(2,1)S(1)}, u32[]{:S(2)}, u32[]{:S(2)}) collective-permute-start(bf16[32,3072]{1,0:T(8,128)(2,1)S(1)} %constant_dynamic-update-slice_fusion.refs_0_), channel_id=1, source_target_pairs={{0,2},{1,3},{2,0},{3,1},{4,6},{5,7},{6,4},{7,5},{8,10},{9,11},{10,... | collective-permute-start | bytes 589832 | tf_op jit(solution)/shard_map/ppermute | solution.py:329
  26.4 9.0 %collective-permute-start.8 = (bf16[32,3072]{1,0:T(8,128)(2,1)S(1)}, bf16[32,3072]{1,0:T(8,128)(2,1)S(1)}, u32[]{:S(2)}, u32[]{:S(2)}) collective-permute-start(bf16[32,3072]{1,0:T(8,128)(2,1)S(1)} %constant_dynamic-update-slice_fusion.refs_0_), channel_id=1, source_target_pairs={{0,4},{1,5},{2,6},{3,7},{4,0},{5,1},{6,2},{7,3},{8,12},{9,13},{10,... | collective-permute-start | bytes 589832 | tf_op jit(solution)/shard_map/ppermute | solution.py:329
  28.7 7.6 %collective-permute-start.13 = (s16[2,136,128]{2,1,0:T(8,128)(2,1)S(1)}, s16[2,136,128]{2,1,0:T(8,128)(2,1)S(1)}, u32[]{:S(2)}, u32[]{:S(2)}) collective-permute-start(s16[2,136,128]{2,1,0:T(8,128)(2,1)S(1)} %add_sums.3), channel_id=1, source_target_pairs={{0,6},{1,7},{2,4},{3,5},{4,2},{5,3},{6,0},{7,1},{8,14},{9,15},{10,... | collective-permute-start | bytes 208904 | tf_op jit(solution)/shard_map/ppermute | solution.py:329
  28.8 8.1 %collective-permute-start.11 = (s16[2,136,128]{2,1,0:T(8,128)(2,1)S(1)}, s16[2,136,128]{2,1,0:T(8,128)(2,1)S(1)}, u32[]{:S(2)}, u32[]{:S(2)}) collective-permute-start(s16[2,136,128]{2,1,0:T(8,128)(2,1)S(1)} %add_sums.3), channel_id=1, source_target_pairs={{0,4},{1,5},{2,6},{3,7},{4,0},{5,1},{6,2},{7,3},{8,12},{9,13},{10,... | collective-permute-start | bytes 208904 | tf_op jit(solution)/shard_map/ppermute | solution.py:329
  33.5 4.3 %collective-permute-start.12 = (s16[2,136,128]{2,1,0:T(8,128)(2,1)S(1)}, s16[2,136,128]{2,1,0:T(8,128)(2,1)S(1)}, u32[]{:S(2)}, u32[]{:S(2)}) collective-permute-start(s16[2,136,128]{2,1,0:T(8,128)(2,1)S(1)} %add_sums.3), channel_id=1, source_target_pairs={{0,2},{1,3},{2,0},{3,1},{4,6},{5,7},{6,4},{7,5},{8,10},{9,11},{10,... | collective-permute-start | bytes 208904 | tf_op jit(solution)/shard_map/ppermute | solution.py:329
  35.9 4.1 %collective-permute-start.10 = (bf16[96,4096]{1,0:T(8,128)(2,1)S(1)}, bf16[96,4096]{1,0:T(8,128)(2,1)S(1)}, u32[]{:S(2)}, u32[]{:S(2)}) collective-permute-start(bf16[96,4096]{1,0:T(8,128)(2,1)S(1)} %picked_rows.1.x_ref.x_own), channel_id=1, source_target_pairs={{0,1},{1,0},{2,3},{3,2},{4,5},{5,4},{6,7},{7,6},{8,9},{9,8},{10,11... | collective-permute-start | bytes 2359304 | tf_op jit(solution)/shard_map/ppermute | solution.py:329
  37.8 2.1 %collective-permute-start.14 = (s16[8,136,128]{2,1,0:T(8,128)(2,1)S(1)}, s16[8,136,128]{2,1,0:T(8,128)(2,1)S(1)}, u32[]{:S(2)}, u32[]{:S(2)}) collective-permute-start(s16[8,136,128]{2,1,0:T(8,128)(2,1)S(1)} %constant_dynamic-update-slice_fusion.2.code_ref), channel_id=1, source_target_pairs={{0,1},{1,0},{2,3},{3,2},{4,5},{5,4},{6,7},{7,6},{8,9},{9,8},{10,11... | collective-permute-start | bytes 835592 | tf_op jit(solution)/shard_map/ppermute | solution.py:329

commit v28 on v23

--- a/solution.py
+++ b/solution.py
@@ -284,9 +284,9 @@
     weights = solve_all(factor_all(blocks), rhs)
     last = weights[steps - 1]
     copies = []
-    span = half // 2
+    span = half
     for x_ref, side in ((x_own, core), (x_twin, 1 - core)):
-        for q in range(2):
+        for q in range(1):
             there = slice(q * span, (q + 1) * span)
             here = pl.ds(pl.multiple_of(side * half + q * span, span), span)
             value = target_own[:, there] if x_ref is x_own else resid_ref[:, here]

time: 43.2 us -> 43.3 us (level)
  no operation moved by 1% of the time
where the time goes in v28:
time: 43.3 us; the launch traced here: 43 us
  starting transfers between devices  15.6 us (36%)
  waiting for transfers between devices  14.4 us (33%)
  Pallas kernels  12.2 us (28%)
  between operations  0.79 us (2%)
    ppermute x15, starting transfers between devices, swap(): return lax.ppermute(x, 'ex', [(d, d ^ mask) for d in range(n_ex)])  15.6 us
    ppermute x15, waiting for transfers between devices, swap(): return lax.ppermute(x, 'ex', [(d, d ^ mask) for d in range(n_ex)])  14.4 us
    pallas_call x1, Pallas kernels, on_device(): pl.pallas_call(functools.partial(sums_kernel, n_ex=n_ex), in_specs=[hbm]...  5.02 us
    pallas_call x1, Pallas kernels, on_device(): pl.pallas_call(functools.partial(pursuit_kernel, steps=steps, scale=1.0 /...  3.26 us
    pallas_call x1, Pallas kernels, on_device(): pl.pallas_call(functools.partial(half_kernel, classes=classes), in_specs=...  2.06 us
  transfers between devices with their start and end apart: 15, of which 10 were waited for; matrix products, arithmetic and copies ran while one was open for 0% of the time, Pallas kernels for 9%

profile of v28, /device:TPU:0, one launch (start us, length us, event | category | flops | bytes accessed | tf_op | source)
XLA Modules:
  0.0 43.0 jit_solution(7397073176200868406)
XLA Ops:
  0.6 5.0 %class_sums.1 = (bf16[640,8192]{1,0:T(8,128)(2,1)S(1)}, f32[264,512]{1,0:T(8,128)S(1)}, f32[264,512]{1,0:T(8,128)S(1)}, f32[8,8192]{1,0:T(8,128)S(1)}) custom-call(s32[640]{0:T(1024)} %labels_ref.1, s32[3,32]{1,0:T(4,128)} %pick_ref.1, bf16[640,8192]{1,0:T(8,128)(2,1)} %feat_hbm.1), custom_call_target="tpu_custom_call" | custom-call | tf_op jit(solution)/shard_map/class_sums/pallas_call | solution.py:334
  5.7 0.5 %collective-permute-start = (f32[264,512]{1,0:T(8,128)S(1)}, f32[264,512]{1,0:T(8,128)S(1)}, u32[]{:S(2)}, u32[]{:S(2)}) collective-permute-start(f32[264,512]{1,0:T(8,128)S(1)} %get-tuple-element.25), channel_id=1, source_target_pairs={{0,1},{1,0},{2,3},{3,2},{4,5},{5,4},{6,7},{7,6},{8,9},{9,8},{10,11... | collective-permute-start | bytes 1622024 | tf_op jit(solution)/shard_map/ppermute | solution.py:329
  6.2 3.7 %collective-permute-start.1 = (bf16[2,8,3072]{2,1,0:T(8,128)(2,1)S(1)}, bf16[2,8,3072]{2,1,0:T(8,128)(2,1)S(1)}, u32[]{:S(2)}, u32[]{:S(2)}) collective-permute-start(bf16[2,8,3072]{2,1,0:T(8,128)(2,1)S(1)} %pack_rows.1), channel_id=1, source_target_pairs={{0,8},{1,9},{2,10},{3,11},{4,12},{5,13},{6,14},{7,15},{8,0},{9,1},... | collective-permute-start | bytes 294920 | tf_op jit(solution)/shard_map/ppermute | solution.py:329
  9.9 0.2 pair_sums.1
  10.1 2.6 %collective-permute-start.2 = (s16[2,136,128]{2,1,0:T(8,128)(2,1)S(1)}, s16[2,136,128]{2,1,0:T(8,128)(2,1)S(1)}, u32[]{:S(2)}, u32[]{:S(2)}) collective-permute-start(s16[2,136,128]{2,1,0:T(8,128)(2,1)S(1)} %get-tuple-element.29), channel_id=1, source_target_pairs={{0,6},{1,7},{2,4},{3,5},{4,2},{5,3},{6,0},{7,1},{8,14},{9,15},{10,... | collective-permute-start | bytes 208904 | tf_op jit(solution)/shard_map/ppermute | solution.py:329
  12.7 0.5 %collective-permute-start.3 = (s16[2,136,128]{2,1,0:T(8,128)(2,1)S(1)}, s16[2,136,128]{2,1,0:T(8,128)(2,1)S(1)}, u32[]{:S(2)}, u32[]{:S(2)}) collective-permute-start(s16[2,136,128]{2,1,0:T(8,128)(2,1)S(1)} %get-tuple-element.31), channel_id=1, source_target_pairs={{0,2},{1,3},{2,0},{3,1},{4,6},{5,7},{6,4},{7,5},{8,10},{9,11},{10,... | collective-permute-start | bytes 208904 | tf_op jit(solution)/shard_map/ppermute | solution.py:329
  13.2 0.5 %collective-permute-start.4 = (s16[2,136,128]{2,1,0:T(8,128)(2,1)S(1)}, s16[2,136,128]{2,1,0:T(8,128)(2,1)S(1)}, u32[]{:S(2)}, u32[]{:S(2)}) collective-permute-start(s16[2,136,128]{2,1,0:T(8,128)(2,1)S(1)} %get-tuple-element.32), channel_id=1, source_target_pairs={{0,4},{1,5},{2,6},{3,7},{4,0},{5,1},{6,2},{7,3},{8,12},{9,13},{10,... | collective-permute-start | bytes 208904 | tf_op jit(solution)/shard_map/ppermute | solution.py:329
  13.7 0.3 select_tails.1.rest_ref
  14.0 0.3 select_rows.1.one_ref
  14.4 1.2 %collective-permute-done.2.refs_1_ = s16[2,136,128]{2,1,0:T(8,128)(2,1)S(1)} collective-permute-done((s16[2,136,128]{2,1,0:T(8,128)(2,1)S(1)}, s16[2,136,128]{2,1,0:T(8,128)(2,1)S(1)}, u32[]{:S(2)}, u32[]{:S(2)}) %collective-permute-start.2) | collective-permute-done | bytes 69664 | tf_op jit(solution)/shard_map/ppermute | solution.py:329
  15.6 1.4 %collective-permute-done.3.refs_2_ = s16[2,136,128]{2,1,0:T(8,128)(2,1)S(1)} collective-permute-done((s16[2,136,128]{2,1,0:T(8,128)(2,1)S(1)}, s16[2,136,128]{2,1,0:T(8,128)(2,1)S(1)}, u32[]{:S(2)}, u32[]{:S(2)}) %collective-permute-start.3) | collective-permute-done | bytes 69664 | tf_op jit(solution)/shard_map/ppermute | solution.py:329
  17.0 0.8 %collective-permute-done.4.refs_3_ = s16[2,136,128]{2,1,0:T(8,128)(2,1)S(1)} collective-permute-done((s16[2,136,128]{2,1,0:T(8,128)(2,1)S(1)}, s16[2,136,128]{2,1,0:T(8,128)(2,1)S(1)}, u32[]{:S(2)}, u32[]{:S(2)}) %collective-permute-start.4) | collective-permute-done | bytes 69664 | tf_op jit(solution)/shard_map/ppermute | solution.py:329
  17.9 0.3 add_sums.2.refs_0_
  18.1 2.0 %collective-permute-start.5 = (s16[2,136,128]{2,1,0:T(8,128)(2,1)S(1)}, s16[2,136,128]{2,1,0:T(8,128)(2,1)S(1)}, u32[]{:S(2)}, u32[]{:S(2)}) collective-permute-start(s16[2,136,128]{2,1,0:T(8,128)(2,1)S(1)} %add_sums.2.refs_0_), channel_id=1, source_target_pairs={{0,8},{1,9},{2,10},{3,11},{4,12},{5,13},{6,14},{7,15},{8,0},{9,1},... | collective-permute-start | bytes 208904 | tf_op jit(solution)/shard_map/ppermute | solution.py:329
  20.1 0.1 collective-permute-start.6
  20.2 4.6 %collective-permute-done.5.refs_1_ = s16[2,136,128]{2,1,0:T(8,128)(2,1)S(1)} collective-permute-done((s16[2,136,128]{2,1,0:T(8,128)(2,1)S(1)}, s16[2,136,128]{2,1,0:T(8,128)(2,1)S(1)}, u32[]{:S(2)}, u32[]{:S(2)}) %collective-permute-start.5) | collective-permute-done | bytes 69664 | tf_op jit(solution)/shard_map/ppermute | solution.py:329
  24.9 0.1 collective-permute-start.7
  25.0 1.9 %collective-permute-start.9 = (bf16[32,3072]{1,0:T(8,128)(2,1)S(1)}, bf16[32,3072]{1,0:T(8,128)(2,1)S(1)}, u32[]{:S(2)}, u32[]{:S(2)}) collective-permute-start(bf16[32,3072]{1,0:T(8,128)(2,1)S(1)} %constant_dynamic-update-slice_fusion.refs_0_), channel_id=1, source_target_pairs={{0,4},{1,5},{2,6},{3,7},{4,0},{5,1},{6,2},{7,3},{8,12},{9,13},{10,... | collective-permute-start | bytes 589832 | tf_op jit(solution)/shard_map/ppermute | solution.py:329
  26.9 1.5 %collective-permute-start.8 = (bf16[32,3072]{1,0:T(8,128)(2,1)S(1)}, bf16[32,3072]{1,0:T(8,128)(2,1)S(1)}, u32[]{:S(2)}, u32[]{:S(2)}) collective-permute-start(bf16[32,3072]{1,0:T(8,128)(2,1)S(1)} %constant_dynamic-update-slice_fusion.refs_0_), channel_id=1, source_target_pairs={{0,2},{1,3},{2,0},{3,1},{4,6},{5,7},{6,4},{7,5},{8,10},{9,11},{10,... | collective-permute-start | bytes 589832 | tf_op jit(solution)/shard_map/ppermute | solution.py:329
  28.4 0.3 add_sums.3
  28.7 0.1 collective-permute-start.13
  28.8 1.4 %collective-permute-start.12 = (s16[2,136,128]{2,1,0:T(8,128)(2,1)S(1)}, s16[2,136,128]{2,1,0:T(8,128)(2,1)S(1)}, u32[]{:S(2)}, u32[]{:S(2)}) collective-permute-start(s16[2,136,128]{2,1,0:T(8,128)(2,1)S(1)} %add_sums.3), channel_id=1, source_target_pairs={{0,2},{1,3},{2,0},{3,1},{4,6},{5,7},{6,4},{7,5},{8,10},{9,11},{10,... | collective-permute-start | bytes 208904 | tf_op jit(solution)/shard_map/ppermute | solution.py:329
  30.3 2.9 %collective-permute-done.7.refs_1_ = bf16[32,3072]{1,0:T(8,128)(2,1)S(1)} collective-permute-done((bf16[32,3072]{1,0:T(8,128)(2,1)S(1)}, bf16[32,3072]{1,0:T(8,128)(2,1)S(1)}, u32[]{:S(2)}, u32[]{:S(2)}) %collective-permute-start.7) | collective-permute-done | bytes 196640 | tf_op jit(solution)/shard_map/ppermute | solution.py:329
  33.2 0.5 %collective-permute-start.11 = (s16[2,136,128]{2,1,0:T(8,128)(2,1)S(1)}, s16[2,136,128]{2,1,0:T(8,128)(2,1)S(1)}, u32[]{:S(2)}, u32[]{:S(2)}) collective-permute-start(s16[2,136,128]{2,1,0:T(8,128)(2,1)S(1)} %add_sums.3), channel_id=1, source_target_pairs={{0,4},{1,5},{2,6},{3,7},{4,0},{5,1},{6,2},{7,3},{8,12},{9,13},{10,... | collective-permute-start | bytes 208904 | tf_op jit(solution)/shard_map/ppermute | solution.py:329
  33.7 1.2 %collective-permute-done.9.refs_3_ = bf16[32,3072]{1,0:T(8,128)(2,1)S(1)} collective-permute-done((bf16[32,3072]{1,0:T(8,128)(2,1)S(1)}, bf16[32,3072]{1,0:T(8,128)(2,1)S(1)}, u32[]{:S(2)}, u32[]{:S(2)}) %collective-permute-start.9) | collective-permute-done | bytes 196640 | tf_op jit(solution)/shard_map/ppermute | solution.py:329
  35.0 0.2 collective-permute-done.8.refs_2_
  35.2 0.4 picked_rows.1.x_ref.x_own
  35.7 0.4 collective-permute-done.13
  36.1 0.6 %collective-permute-done.12 = s16[2,136,128]{2,1,0:T(8,128)(2,1)S(1)} collective-permute-done((s16[2,136,128]{2,1,0:T(8,128)(2,1)S(1)}, s16[2,136,128]{2,1,0:T(8,128)(2,1)S(1)}, u32[]{:S(2)}, u32[]{:S(2)}) %collective-permute-start.12) | collective-permute-done | bytes 69664 | tf_op jit(solution)/shard_map/ppermute | solution.py:329
  36.7 0.8 %collective-permute-done.11 = s16[2,136,128]{2,1,0:T(8,128)(2,1)S(1)} collective-permute-done((s16[2,136,128]{2,1,0:T(8,128)(2,1)S(1)}, s16[2,136,128]{2,1,0:T(8,128)(2,1)S(1)}, u32[]{:S(2)}, u32[]{:S(2)}) %collective-permute-start.11) | collective-permute-done | bytes 69664 | tf_op jit(solution)/shard_map/ppermute | solution.py:329
  37.7 2.1 %own_half_products.1 = (f32[96,640]{1,0:T(8,128)S(1)}, f32[128,96]{1,0:T(8,128)S(1)}, f32[32,4096]{1,0:T(8,128)S(1)}) custom-call(bf16[640,8192]{1,0:T(8,128)(2,1)S(1)} %get-tuple-element.23.feat_ref, s16[8,136,128]{2,1,0:T(8,128)(2,1)S(1)} %constant_dynamic-update-slice_fusion.2.code_ref, bf16[96,4096]{1,0:T(8,128)(2,1)S(1)} %picked_rows.1.x_ref.x_own), custom_call_target="tpu_custom_call" | custom-call | tf_op jit(solution)/shard_map/own_half_products/pallas_call | solution.py:418
  39.8 3.3 %pursuit.1 = (f32[3,640]{1,0:T(4,128)}, f32[32,8192]{1,0:T(8,128)}) custom-call(s32[640]{0:T(1024)S(1)} %copy-done.1, bf16[640,8192]{1,0:T(8,128)(2,1)S(1)} %get-tuple-element.23.feat_ref, bf16[96,4096]{1,0:T(8,128)(2,1)S(1)} %picked_rows.1.x_ref.x_own, bf16[96,4096]{1,0:T(8,128)(2,1)S(1)} %collective-permute-done.10.x_twin, ...), custom_call_target="tpu_custom_call" | custom-call | tf_op jit(solution)/shard_map/pursuit/pallas_call | solution.py:432
  (19 shorter events, 0.3 us)
Async XLA Ops:
  0.6 13.0 %copy-start = (s32[3,32]{1,0:T(4,128)S(1)}, s32[3,32]{1,0:T(4,128)}, u32[]{:S(2)}) copy-start(s32[3,32]{1,0:T(4,128)} %pick_ref.1) | copy-start | bytes 1156
  5.7 34.1 %copy-start.1 = (s32[640]{0:T(1024)S(1)}, s32[640]{0:T(1024)}, u32[]{:S(2)}) copy-start(s32[640]{0:T(1024)} %labels_ref.1) | copy-start | bytes 7684
  5.7 4.2 %collective-permute-start = (f32[264,512]{1,0:T(8,128)S(1)}, f32[264,512]{1,0:T(8,128)S(1)}, u32[]{:S(2)}, u32[]{:S(2)}) collective-permute-start(f32[264,512]{1,0:T(8,128)S(1)} %get-tuple-element.25), channel_id=1, source_target_pairs={{0,1},{1,0},{2,3},{3,2},{4,5},{5,4},{6,7},{7,6},{8,9},{9,8},{10,11... | collective-permute-start | bytes 1622024 | tf_op jit(solution)/shard_map/ppermute | solution.py:329
  6.2 13.9 %collective-permute-start.1 = (bf16[2,8,3072]{2,1,0:T(8,128)(2,1)S(1)}, bf16[2,8,3072]{2,1,0:T(8,128)(2,1)S(1)}, u32[]{:S(2)}, u32[]{:S(2)}) collective-permute-start(bf16[2,8,3072]{2,1,0:T(8,128)(2,1)S(1)} %pack_rows.1), channel_id=1, source_target_pairs={{0,8},{1,9},{2,10},{3,11},{4,12},{5,13},{6,14},{7,15},{8,0},{9,1},... | collective-permute-start | bytes 294920 | tf_op jit(solution)/shard_map/ppermute | solution.py:329
  10.1 5.5 %collective-permute-start.2 = (s16[2,136,128]{2,1,0:T(8,128)(2,1)S(1)}, s16[2,136,128]{2,1,0:T(8,128)(2,1)S(1)}, u32[]{:S(2)}, u32[]{:S(2)}) collective-permute-start(s16[2,136,128]{2,1,0:T(8,128)(2,1)S(1)} %get-tuple-element.29), channel_id=1, source_target_pairs={{0,6},{1,7},{2,4},{3,5},{4,2},{5,3},{6,0},{7,1},{8,14},{9,15},{10,... | collective-permute-start | bytes 208904 | tf_op jit(solution)/shard_map/ppermute | solution.py:329
  12.7 4.3 %collective-permute-start.3 = (s16[2,136,128]{2,1,0:T(8,128)(2,1)S(1)}, s16[2,136,128]{2,1,0:T(8,128)(2,1)S(1)}, u32[]{:S(2)}, u32[]{:S(2)}) collective-permute-start(s16[2,136,128]{2,1,0:T(8,128)(2,1)S(1)} %get-tuple-element.31), channel_id=1, source_target_pairs={{0,2},{1,3},{2,0},{3,1},{4,6},{5,7},{6,4},{7,5},{8,10},{9,11},{10,... | collective-permute-start | bytes 208904 | tf_op jit(solution)/shard_map/ppermute | solution.py:329
  13.2 4.6 %collective-permute-start.4 = (s16[2,136,128]{2,1,0:T(8,128)(2,1)S(1)}, s16[2,136,128]{2,1,0:T(8,128)(2,1)S(1)}, u32[]{:S(2)}, u32[]{:S(2)}) collective-permute-start(s16[2,136,128]{2,1,0:T(8,128)(2,1)S(1)} %get-tuple-element.32), channel_id=1, source_target_pairs={{0,4},{1,5},{2,6},{3,7},{4,0},{5,1},{6,2},{7,3},{8,12},{9,13},{10,... | collective-permute-start | bytes 208904 | tf_op jit(solution)/shard_map/ppermute | solution.py:329
  18.1 6.7 %collective-permute-start.5 = (s16[2,136,128]{2,1,0:T(8,128)(2,1)S(1)}, s16[2,136,128]{2,1,0:T(8,128)(2,1)S(1)}, u32[]{:S(2)}, u32[]{:S(2)}) collective-permute-start(s16[2,136,128]{2,1,0:T(8,128)(2,1)S(1)} %add_sums.2.refs_0_), channel_id=1, source_target_pairs={{0,8},{1,9},{2,10},{3,11},{4,12},{5,13},{6,14},{7,15},{8,0},{9,1},... | collective-permute-start | bytes 208904 | tf_op jit(solution)/shard_map/ppermute | solution.py:329
  20.1 4.7 %collective-permute-start.6 = (bf16[16,3072]{1,0:T(8,128)(2,1)S(1)}, bf16[16,3072]{1,0:T(8,128)(2,1)S(1)}, u32[]{:S(2)}, u32[]{:S(2)}) collective-permute-start(bf16[16,3072]{1,0:T(8,128)(2,1)S(1)} %get-tuple-element.35), channel_id=1, source_target_pairs={{0,1},{1,0},{2,3},{3,2},{4,5},{5,4},{6,7},{7,6},{8,9},{9,8},{10,11... | collective-permute-start | bytes 294920 | tf_op jit(solution)/shard_map/ppermute | solution.py:329
  24.9 8.4 %collective-permute-start.7 = (bf16[32,3072]{1,0:T(8,128)(2,1)S(1)}, bf16[32,3072]{1,0:T(8,128)(2,1)S(1)}, u32[]{:S(2)}, u32[]{:S(2)}) collective-permute-start(bf16[32,3072]{1,0:T(8,128)(2,1)S(1)} %constant_dynamic-update-slice_fusion.refs_0_), channel_id=1, source_target_pairs={{0,6},{1,7},{2,4},{3,5},{4,2},{5,3},{6,0},{7,1},{8,14},{9,15},{10,... | collective-permute-start | bytes 589832 | tf_op jit(solution)/shard_map/ppermute | solution.py:329
  25.0 10.0 %collective-permute-start.9 = (bf16[32,3072]{1,0:T(8,128)(2,1)S(1)}, bf16[32,3072]{1,0:T(8,128)(2,1)S(1)}, u32[]{:S(2)}, u32[]{:S(2)}) collective-permute-start(bf16[32,3072]{1,0:T(8,128)(2,1)S(1)} %constant_dynamic-update-slice_fusion.refs_0_), channel_id=1, source_target_pairs={{0,4},{1,5},{2,6},{3,7},{4,0},{5,1},{6,2},{7,3},{8,12},{9,13},{10,... | collective-permute-start | bytes 589832 | tf_op jit(solution)/shard_map/ppermute | solution.py:329
  26.9 8.3 %collective-permute-start.8 = (bf16[32,3072]{1,0:T(8,128)(2,1)S(1)}, bf16[32,3072]{1,0:T(8,128)(2,1)S(1)}, u32[]{:S(2)}, u32[]{:S(2)}) collective-permute-start(bf16[32,3072]{1,0:T(8,128)(2,1)S(1)} %constant_dynamic-update-slice_fusion.refs_0_), channel_id=1, source_target_pairs={{0,2},{1,3},{2,0},{3,1},{4,6},{5,7},{6,4},{7,5},{8,10},{9,11},{10,... | collective-permute-start | bytes 589832 | tf_op jit(solution)/shard_map/ppermute | solution.py:329
  28.7 7.4 %collective-permute-start.13 = (s16[2,136,128]{2,1,0:T(8,128)(2,1)S(1)}, s16[2,136,128]{2,1,0:T(8,128)(2,1)S(1)}, u32[]{:S(2)}, u32[]{:S(2)}) collective-permute-start(s16[2,136,128]{2,1,0:T(8,128)(2,1)S(1)} %add_sums.3), channel_id=1, source_target_pairs={{0,6},{1,7},{2,4},{3,5},{4,2},{5,3},{6,0},{7,1},{8,14},{9,15},{10,... | collective-permute-start | bytes 208904 | tf_op jit(solution)/shard_map/ppermute | solution.py:329
  28.8 7.9 %collective-permute-start.12 = (s16[2,136,128]{2,1,0:T(8,128)(2,1)S(1)}, s16[2,136,128]{2,1,0:T(8,128)(2,1)S(1)}, u32[]{:S(2)}, u32[]{:S(2)}) collective-permute-start(s16[2,136,128]{2,1,0:T(8,128)(2,1)S(1)} %add_sums.3), channel_id=1, source_target_pairs={{0,2},{1,3},{2,0},{3,1},{4,6},{5,7},{6,4},{7,5},{8,10},{9,11},{10,... | collective-permute-start | bytes 208904 | tf_op jit(solution)/shard_map/ppermute | solution.py:329
  33.2 4.3 %collective-permute-start.11 = (s16[2,136,128]{2,1,0:T(8,128)(2,1)S(1)}, s16[2,136,128]{2,1,0:T(8,128)(2,1)S(1)}, u32[]{:S(2)}, u32[]{:S(2)}) collective-permute-start(s16[2,136,128]{2,1,0:T(8,128)(2,1)S(1)} %add_sums.3), channel_id=1, source_target_pairs={{0,4},{1,5},{2,6},{3,7},{4,0},{5,1},{6,2},{7,3},{8,12},{9,13},{10,... | collective-permute-start | bytes 208904 | tf_op jit(solution)/shard_map/ppermute | solution.py:329
  35.6 4.1 %collective-permute-start.10 = (bf16[96,4096]{1,0:T(8,128)(2,1)S(1)}, bf16[96,4096]{1,0:T(8,128)(2,1)S(1)}, u32[]{:S(2)}, u32[]{:S(2)}) collective-permute-start(bf16[96,4096]{1,0:T(8,128)(2,1)S(1)} %picked_rows.1.x_ref.x_own), channel_id=1, source_target_pairs={{0,1},{1,0},{2,3},{3,2},{4,5},{5,4},{6,7},{7,6},{8,9},{9,8},{10,11... | collective-permute-start | bytes 2359304 | tf_op jit(solution)/shard_map/ppermute | solution.py:329
  37.6 2.1 %collective-permute-start.14 = (s16[8,136,128]{2,1,0:T(8,128)(2,1)S(1)}, s16[8,136,128]{2,1,0:T(8,128)(2,1)S(1)}, u32[]{:S(2)}, u32[]{:S(2)}) collective-permute-start(s16[8,136,128]{2,1,0:T(8,128)(2,1)S(1)} %constant_dynamic-update-slice_fusion.2.code_ref), channel_id=1, source_target_pairs={{0,1},{1,0},{2,3},{3,2},{4,5},{5,4},{6,7},{7,6},{8,9},{9,8},{10,11... | collective-permute-start | bytes 835592 | tf_op jit(solution)/shard_map/ppermute | solution.py:329
